TPU v7x, 32 devices: a whole 2x2x4 slice. The times are simulated.
32 devices in a mesh: seq: 16 (over z, x, core), tp: 2 (over y).
Axes of the slice: x: 2, y: 2, z: 4, core: 2. Of those that a mesh axis runs over, the one named last changes fastest.
Arguments:
- features: bfloat16 [2048, 8192], P('seq', 'tp'), may hold values from -6 to 6
- in_proj: bfloat16 [3, 8192, 1024], P(None, 'seq', 'tp'), may hold values from -0.0625 to 0.0625
- short_taps: float32 [3, 3, 1024], P(None, None, 'tp'), may hold values from -3 to 3
- long_filter: float32 [2048, 1024], P('seq', 'tp'), may hold values from -1.8 to 1.8
- skip_gain: float32 [1024], P('tp'), may hold values from -4 to 4
- out_proj: bfloat16 [1024, 8192], P('tp', 'seq'), may hold values from -0.1875 to 0.1875
Outputs:
- mixed: bfloat16 [2048, 8192], P('seq', 'tp')
All inputs are finite; a program needn't handle non-finite values.
Results may differ from a plain program's by a relative error of at most 0.007.
Values may be sent and summed in bfloat16 or wider, within the bound.
No kernel may reach another device: no remote copies, remote signals or barrier semaphores. Data moves between devices by JAX's collectives and lax.ppermute only.
A program may use at most 128 MiB of HBM per device.

v0:
```python
import functools
import math

import jax
import jax.numpy as jnp
import numpy as np
from jax import lax
from jax.experimental import pallas as pl
from jax.experimental.pallas import tpu as pltpu
from jax.sharding import PartitionSpec as P

HIGHEST = lax.Precision.HIGHEST
UNROLL = 16


def outer_factor(seq_parts):
    outer = 1
    while 4 * outer * outer <= seq_parts and seq_parts % (2 * outer) == 0:
        outer *= 2
    return outer


def match_rounds(edges, nodes, degree):
    left = list(edges)
    rounds = []
    for _ in range(degree):
        by_source = {}
        for edge in left:
            by_source.setdefault(edge[0], []).append(edge)
        taken = {}

        def place(source, seen):
            for edge in by_source[source]:
                target = edge[1]
                if target in seen:
                    continue
                seen.add(target)
                if target not in taken or place(taken[target][0], seen):
                    taken[target] = edge
                    return True
            return False

        for source in range(nodes):
            place(source, set())
        chosen = sorted(taken.values())
        rounds.append(chosen)
        for edge in chosen:
            left.remove(edge)
    return rounds


def feature_routes(outer, tp_parts):
    groups = max(1, outer // tp_parts)
    shares = max(1, tp_parts // outer)
    edges = []
    for src_outer in range(outer):
        for src_tp in range(tp_parts):
            for group in range(groups):
                for dst_tp in range(tp_parts):
                    dst_outer = src_tp * groups + group if groups > 1 else src_tp // shares
                    slot = src_outer * shares + (src_tp % shares)
                    edges.append(
                        (
                            src_outer * tp_parts + src_tp,
                            dst_outer * tp_parts + dst_tp,
                            group * tp_parts + dst_tp,
                            slot,
                        )
                    )
    return match_rounds(edges, outer * tp_parts, groups * tp_parts)


def spread_features(features, outer, inner_parts, tp_parts):
    rows, cols = features.shape
    groups = max(1, outer // tp_parts)
    shares = max(1, tp_parts // outer)
    width = cols // (groups * tp_parts)
    node = (lax.axis_index("seq") // inner_parts) * tp_parts + lax.axis_index("tp")
    buffer = jnp.zeros((outer * shares, rows, width), features.dtype)
    for chosen in feature_routes(outer, tp_parts):
        send = np.zeros(outer * tp_parts, np.int32)
        fill = np.zeros(outer * tp_parts, np.int32)
        pairs = []
        for source, target, block, slot in chosen:
            send[source] = block
            fill[target] = slot
            for inner in range(inner_parts):
                pairs.append(
                    (
                        ((source // tp_parts) * inner_parts + inner) * tp_parts + source % tp_parts,
                        ((target // tp_parts) * inner_parts + inner) * tp_parts + target % tp_parts,
                    )
                )
        piece = lax.dynamic_slice_in_dim(features, jnp.asarray(send)[node] * width, width, axis=1)
        piece = lax.ppermute(piece, ("seq", "tp"), pairs)
        buffer = lax.dynamic_update_slice_in_dim(buffer, piece[None], jnp.asarray(fill)[node], axis=0)
    return buffer.reshape(outer, shares, rows, width)


def share_over_tp(part, tp_parts):
    pieces = [part]
    for step in range(1, tp_parts):
        pairs = [(i, (i + step) % tp_parts) for i in range(tp_parts)]
        pieces.append(lax.ppermute(part, "tp", pairs))
    return pieces


def project_kernel(place_ref, *refs):
    *share_refs, weight_ref, out_ref = refs
    tp_parts = len(share_refs)
    outer, shares, rows, width = share_refs[0].shape
    seq_parts, _, chans, count = out_ref.shape
    sums = jnp.zeros((count, seq_parts * chans), jnp.float32)
    for step, share_ref in enumerate(share_refs):
        which = lax.rem(place_ref[0] - step + tp_parts, tp_parts)
        for share in range(shares):
            sums = sums + jnp.dot(
                share_ref[:, share].reshape(count, width),
                weight_ref[0, share, which],
                preferred_element_type=jnp.float32,
            )
    turned = sums.T.astype(out_ref.dtype)
    for seq in range(seq_parts):
        out_ref[seq, 0] = turned[seq * chans : (seq + 1) * chans]


def project_in(pieces, weight, seq_parts):
    tp_parts = len(pieces)
    outer, shares, rows, width = pieces[0].shape
    streams, _, chan_tp = weight.shape
    weight = weight.reshape(streams, shares, tp_parts, width, chan_tp)
    chans = chan_tp // seq_parts
    count = outer * rows
    place = lax.axis_index("tp").astype(jnp.int32)[None]
    whole = pl.BlockSpec((outer, shares, rows, width), lambda i, place: (0, 0, 0, 0))
    return pl.pallas_call(
        project_kernel,
        grid_spec=pltpu.PrefetchScalarGridSpec(
            num_scalar_prefetch=1,
            grid=(streams,),
            in_specs=[whole] * tp_parts
            + [
                pl.BlockSpec(
                    (1, shares, tp_parts, width, chan_tp), lambda i, place: (i, 0, 0, 0, 0)
                )
            ],
            out_specs=pl.BlockSpec((seq_parts, 1, chans, count), lambda i, place: (0, i, 0, 0)),
        ),
        out_shape=jax.ShapeDtypeStruct((seq_parts, streams, chans, count), jnp.bfloat16),
        compiler_params=pltpu.CompilerParams(vmem_limit_bytes=56 * 2**20),
        cost_estimate=pl.CostEstimate(
            flops=2 * count * weight.size,
            bytes_accessed=2 * (weight.size + tp_parts * pieces[0].size) + 2 * streams * count * chan_tp,
            transcendentals=0,
        ),
    )(place, *pieces, weight)


def tables(block):
    place = np.arange(block)
    angle = 2.0 * math.pi * np.outer(place, place + 0.5) / (2 * block)
    forward = np.concatenate([np.cos(angle), -np.sin(angle)], 1)
    place = np.arange(2 * block)
    angle = 2.0 * math.pi * np.outer(np.arange(block) + 0.5, place) / (2 * block)
    backward = np.concatenate([np.cos(angle), -np.sin(angle)], 0) / block
    return forward.astype(np.float32), backward.astype(np.float32)


def each(count, body):
    if isinstance(count, int) and count <= UNROLL:
        for index in range(count):
            body(index)
    else:
        lax.fori_loop(0, count, lambda index, carry: (body(index), carry)[1], 0)


def total(count, term, zero):
    if isinstance(count, int) and count <= UNROLL:
        result = zero
        for index in range(count):
            result = jax.tree.map(jnp.add, result, term(index))
        return result
    return lax.fori_loop(
        0, count, lambda index, sums: jax.tree.map(jnp.add, sums, term(index)), zero
    )


def conv_kernel(
    outer, parts_ref, filter_ref, taps_ref, skip_ref, fwd_ref, bwd_ref, out_ref,
    proj, query, inner, spec, filter_spec, product, back
):
    blocks, streams, chans, _ = parts_ref.shape
    rows = filter_ref.shape[2]
    inner_parts = blocks // outer
    taps_count = taps_ref.shape[1]
    lane = lax.broadcasted_iota(jnp.int32, (chans, rows), 1)

    def add_up(index, stream, slot):
        sums = jnp.zeros((chans, rows), jnp.float32)
        column = pl.ds(pl.multiple_of(slot * rows, rows), rows)
        for part in range(outer):
            sums = sums + parts_ref[part * inner_parts + index % inner_parts, stream, :, column].astype(jnp.float32)
        return sums

    for stream in range(streams):
        proj[0, stream] = jnp.zeros((chans, rows), jnp.float32)

    def first(index):
        filtered = []
        for stream in range(streams):
            proj[index + 1, stream] = add_up(index, stream, index // inner_parts)
        for stream in range(streams):
            now, past = proj[index + 1, stream], proj[index, stream]
            value = taps_ref[stream, 0] * now
            for offset in range(1, taps_count):
                moved = jnp.where(
                    lane < offset, pltpu.roll(past, offset, 1), pltpu.roll(now, offset, 1)
                )
                value = value + taps_ref[stream, offset] * moved
            filtered.append(value)
        query[index] = filtered[0]
        inner[index] = filtered[1] * filtered[2]

    each(blocks, first)

    def apply(source, table_ref, target):
        if chans % 8 == 0:
            flat = source[...].reshape(blocks * chans, source.shape[2])
            done = jnp.dot(flat, table_ref[...], precision=HIGHEST, preferred_element_type=jnp.float32)
            target[...] = done.reshape(target.shape)
        else:

            def one(index):
                target[index] = jnp.dot(
                    source[index], table_ref[...], precision=HIGHEST, preferred_element_type=jnp.float32
                )

            each(blocks, one)

    apply(filter_ref, fwd_ref, filter_spec)
    apply(inner, fwd_ref, spec)

    def multiply(index):
        def term(step):
            left, right = spec[step], filter_spec[index - step]
            left_real, left_imag = left[:, :rows], left[:, rows:]
            right_real, right_imag = right[:, :rows], right[:, rows:]
            return (
                left_real * right_real - left_imag * right_imag,
                left_real * right_imag + left_imag * right_real,
            )

        zero = jnp.zeros((chans, rows), jnp.float32)
        real, imag = total(index + 1, term, (zero, zero))
        product[index, :, :rows] = real
        product[index, :, rows:] = imag

    each(blocks, multiply)
    apply(product, bwd_ref, back)

    def last(index, carried):
        long_mix = back[index, :, :rows] + carried
        gated = query[index] * (long_mix + skip_ref[...] * inner[index])
        out_ref[index] = gated.astype(out_ref.dtype)

    last(0, jnp.zeros((chans, rows), jnp.float32))
    each(blocks - 1, lambda index: last(index + 1, back[index, :, rows:]))


def convolve(parts, filter_blocks, taps, skip, outer):
    blocks, streams, chans, _ = parts.shape
    rows = filter_blocks.shape[2]
    forward, backward = tables(rows)
    wide = (blocks, chans, 2 * rows)
    narrow = (blocks, chans, rows)
    vmem = pl.BlockSpec(memory_space=pltpu.VMEM)
    return pl.pallas_call(
        functools.partial(conv_kernel, outer),
        out_shape=jax.ShapeDtypeStruct(narrow, jnp.bfloat16),
        in_specs=[vmem] * 6,
        out_specs=vmem,
        scratch_shapes=[
            pltpu.VMEM((blocks + 1, streams, chans, rows), jnp.float32),
            pltpu.VMEM(narrow, jnp.float32),
            pltpu.VMEM(narrow, jnp.float32),
            pltpu.VMEM(wide, jnp.float32),
            pltpu.VMEM(wide, jnp.float32),
            pltpu.VMEM(wide, jnp.float32),
            pltpu.VMEM(wide, jnp.float32),
        ],
        compiler_params=pltpu.CompilerParams(vmem_limit_bytes=40 * 2**20),
        cost_estimate=pl.CostEstimate(flops=10**9, bytes_accessed=4 * 2**20, transcendentals=0),
    )(parts, filter_blocks, taps, skip, jnp.asarray(forward), jnp.asarray(backward))


def lay_out(out_proj, seq_parts, tp_parts):
    ranges = seq_parts // tp_parts
    pairs = []
    for seq in range(seq_parts):
        for tp in range(tp_parts):
            target = (tp * ranges + seq % ranges) * tp_parts + seq // ranges
            pairs.append((seq * tp_parts + tp, target))
    return lax.ppermute(out_proj, ("seq", "tp"), pairs)


def out_kernel(gated_ref, weight_ref, out_ref):
    shares, _, depth, _ = weight_ref.shape
    sums = jnp.zeros(out_ref.shape, jnp.float32)
    for share in range(shares):
        left = gated_ref[:, share * depth : (share + 1) * depth]
        sums = sums + jnp.dot(left, weight_ref[share, 0], preferred_element_type=jnp.float32)
    out_ref[...] = sums.astype(out_ref.dtype)


def project_out(gated, weight):
    rows, depth_all = gated.shape
    shares, ranges, depth, width = weight.shape
    columns = ranges * width
    return pl.pallas_call(
        out_kernel,
        grid=(ranges,),
        out_shape=jax.ShapeDtypeStruct((rows, columns), jnp.bfloat16),
        in_specs=[
            pl.BlockSpec((rows, depth_all), lambda r: (0, 0)),
            pl.BlockSpec((shares, 1, depth, width), lambda r: (0, r, 0, 0)),
        ],
        out_specs=pl.BlockSpec((rows, width), lambda r: (0, r)),
        compiler_params=pltpu.CompilerParams(vmem_limit_bytes=56 * 2**20),
        cost_estimate=pl.CostEstimate(
            flops=2 * rows * depth_all * columns,
            bytes_accessed=2 * (weight.size + gated.size + rows * columns),
            transcendentals=0,
        ),
    )(gated, weight)


def per_device(features, in_proj, short_taps, long_filter, skip_gain, out_proj):
    rows = features.shape[0]
    seq_parts = lax.axis_size("seq")
    tp_parts = lax.axis_size("tp")
    outer = outer_factor(seq_parts)
    inner_parts = seq_parts // outer
    streams, _, chan_tp = in_proj.shape
    chans = chan_tp // seq_parts
    position = lax.axis_index("seq")

    inner_groups = [[a * inner_parts + b for b in range(inner_parts)] for a in range(outer)]
    weight = lax.all_gather(in_proj, "seq", axis=1, tiled=True, axis_index_groups=inner_groups)

    part = spread_features(features, outer, inner_parts, tp_parts)
    part, out_proj, long_filter = lax.optimization_barrier((part, out_proj, long_filter))
    pieces = share_over_tp(part, tp_parts)
    out_block = lay_out(out_proj, seq_parts, tp_parts)
    filter_blocks = lax.all_to_all(
        long_filter.T.reshape(seq_parts, chans, rows), "seq", split_axis=0, concat_axis=0, tiled=True
    )
    pieces, weight, out_block, filter_blocks = lax.optimization_barrier(
        (pieces, weight, out_block, filter_blocks)
    )
    out_weight = lax.all_gather(out_block, "seq")
    out_weight = out_weight.reshape((tp_parts, seq_parts // tp_parts) + out_proj.shape)

    taps = lax.dynamic_slice_in_dim(short_taps, position * chans, chans, axis=2)
    taps = jnp.broadcast_to(taps[..., None], taps.shape + (rows,))
    skip = lax.dynamic_slice_in_dim(skip_gain, position * chans, chans, axis=0)
    skip = jnp.broadcast_to(skip[:, None], (chans, rows))

    partial = project_in(pieces, weight, seq_parts)
    parts = lax.all_to_all(partial, "seq", split_axis=0, concat_axis=0, tiled=True)

    gated = convolve(parts, filter_blocks, taps, skip, outer)
    gated = jnp.broadcast_to(gated[None], (tp_parts,) + gated.shape).reshape(-1, chans, rows)
    gated = lax.all_to_all(gated, ("tp", "seq"), split_axis=0, concat_axis=0, tiled=True)
    gated = gated.reshape(tp_parts * chan_tp, rows).T
    return project_out(gated, out_weight)


def solution(mesh):
    return jax.shard_map(
        per_device,
        mesh=mesh,
        in_specs=(
            P("seq", "tp"),
            P(None, "seq", "tp"),
            P(None, None, "tp"),
            P("seq", "tp"),
            P("tp"),
            P("tp", "seq"),
        ),
        out_specs=P("seq", "tp"),
        check_vma=False,
    )
```

profile of v0, /device:TPU:0, one launch (start us, length us, event | category | flops | bytes accessed | tf_op | source)
XLA Modules:
  0.0 217.8 jit_solution(5258277893568747744)
XLA Ops:
  6.7 0.7 all-gather.4.cloned.1.call-update
  8.7 0.6 dynamic_slice.45
  9.9 0.6 dynamic_slice.48
  12.6 5.9 %collective-permute-start = (bf16[128,1024]{1,0:T(8,128)(2,1)S(1)}, bf16[128,1024]{1,0:T(8,128)(2,1)S(1)}, u32[]{:S(2)}, u32[]{:S(2)}) collective-permute-start(bf16[128,1024]{1,0:T(8,128)(2,1)S(1)} %get-tuple-element.23), channel_id=1, source_target_pairs={{0,9},{2,11},{4,13},{6,15},{1,25},{3,27},{5,29},{7,31},{8,8},{10,1... | collective-permute-start | bytes 786440 | tf_op jit(solution)/shard_map/ppermute | solution.py:95
  18.5 2.6 %collective-permute-start.2 = (bf16[128,1024]{1,0:T(8,128)(2,1)S(1)}, bf16[128,1024]{1,0:T(8,128)(2,1)S(1)}, u32[]{:S(2)}, u32[]{:S(2)}) collective-permute-start(bf16[128,1024]{1,0:T(8,128)(2,1)S(1)} %get-tuple-element.24), channel_id=1, source_target_pairs={{0,1},{2,3},{4,5},{6,7},{1,17},{3,19},{5,21},{7,23},{8,9},{10,11},... | collective-permute-start | bytes 786440 | tf_op jit(solution)/shard_map/ppermute | solution.py:95
  21.2 0.7 collective-permute-start.3
  21.9 0.6 dynamic_slice.44
  23.8 0.7 dynamic_slice.47
  25.8 0.6 dynamic_slice.50
  27.7 0.7 dynamic_slice.53
  32.4 4.9 %collective-permute-done.1 = bf16[128,1024]{1,0:T(8,128)(2,1)S(1)} collective-permute-done((bf16[128,1024]{1,0:T(8,128)(2,1)S(1)}, bf16[128,1024]{1,0:T(8,128)(2,1)S(1)}, u32[]{:S(2)}, u32[]{:S(2)}) %collective-permute-start.1) | collective-permute-done | bytes 262176 | tf_op jit(solution)/shard_map/ppermute | solution.py:95
  37.3 22.4 %collective-permute-done.2 = bf16[128,1024]{1,0:T(8,128)(2,1)S(1)} collective-permute-done((bf16[128,1024]{1,0:T(8,128)(2,1)S(1)}, bf16[128,1024]{1,0:T(8,128)(2,1)S(1)}, u32[]{:S(2)}, u32[]{:S(2)}) %collective-permute-start.2) | collective-permute-done | bytes 262176 | tf_op jit(solution)/shard_map/ppermute | solution.py:95
  59.9 1.7 collective-permute-start.5
  61.7 36.3 %all_to_all.15.filter_ref = f32[16,32,128]{2,1,0:T(8,128)S(1)} all-to-all(f32[16,32,128]{2,1,0:T(8,128)S(1)} %bitcast.28), channel_id=1, replica_groups=mesh['seq'=16,'tp'=2] {'seq'}, dimensions={0} | all-to-all | bytes 524288 | tf_op jit(solution)/shard_map/all_to_all | solution.py:354
  98.1 0.8 copy-done.5
  98.9 7.5 %shard_map.154 = bf16[16,3,32,512]{3,2,1,0:T(8,128)(2,1)} custom-call(s32[1]{0:T(128)} %bitcast.place_ref, bf16[4,1,128,1024]{3,2,1,0:T(8,128)(2,1)} %copy-done.4, bf16[4,1,128,1024]{3,2,1,0:T(8,128)(2,1)} %collective-permute-done.4.refs_1_, bf16[3,1,2,1024,512]{4,3,2,1,0:T(8,128)(2,1)} %bitcast.30), custom_call_target="tpu_custom_call" | custom-call | flops 3221225472 | bytes 9961472 | tf_op jit(solution)/shard_map/pallas_call | solution.py:136
  106.3 5.8 %all-to-all-start.1 = ((bf16[16,3,32,512]{3,2,1,0:T(8,128)(2,1)}), bf16[16,3,32,512]{3,2,1,0:T(8,128)(2,1)S(1)}, u32[]{:S(2)}, u32[]{:S(2)}) async-start(bf16[16,3,32,512]{3,2,1,0:T(8,128)(2,1)} %shard_map.154), calls=%async_computation.1 | async-start | bytes 3145728 | tf_op jit(solution)/shard_map/all_to_all | solution.py:369
  112.2 0.8 dynamic_slice.55
  113.0 43.3 %all-to-all-done.1.parts_ref = bf16[16,3,32,512]{3,2,1,0:T(8,128)(2,1)S(1)} async-done(((bf16[16,3,32,512]{3,2,1,0:T(8,128)(2,1)}), bf16[16,3,32,512]{3,2,1,0:T(8,128)(2,1)S(1)}, u32[]{:S(2)}, u32[]{:S(2)}) %all-to-all-start.1) | async-done | bytes 1572896 | tf_op jit(solution)/shard_map/all_to_all | solution.py:369
  156.5 2.9 %shard_map.155 = bf16[16,32,128]{2,1,0:T(8,128)(2,1)S(1)} custom-call(bf16[16,3,32,512]{3,2,1,0:T(8,128)(2,1)S(1)} %all-to-all-done.1.parts_ref, f32[16,32,128]{2,1,0:T(8,128)S(1)} %all_to_all.15.filter_ref, f32[3,3,32,128]{3,2,1,0:T(8,128)S(1)} %broadcast_in_dim.9.taps_ref, f32[32,128]{1,0:T(8,128)S(1)} %broadcast_in_dim.10.skip_ref, ...), custom_call_target="tpu_custom_call" | custom-call | flops 1000000000 | bytes 4194304 | tf_op jit(solution)/shard_map/pallas_call | solution.py:277
  159.4 35.2 %all_to_all.16 = bf16[32,32,128]{2,1,0:T(8,128)(2,1)S(1)} all-to-all(bf16[32,32,128]{2,1,0:T(8,128)(2,1)S(1)} %bitcast.26), channel_id=1, replica_groups=mesh['seq'=16,'tp'=2] {'tp','seq'}, dimensions={0} | all-to-all | bytes 524288 | tf_op jit(solution)/shard_map/all_to_all | solution.py:373
  194.7 0.9 copy.20
  195.5 7.6 %all-gather.6.cloned.1.call-done = bf16[8192,512]{1,0:T(8,128)(2,1)} async-done(((bf16[512,512]{1,0:T(8,128)(2,1)}), bf16[8192,512]{1,0:T(8,128)(2,1)}) %all-gather.6.cloned.1.call-update) | async-done | bytes 8388624 | tf_op jit(solution)/shard_map/all_gather | solution.py:360
  203.1 7.9 %shard_map.156 = bf16[128,4096]{1,0:T(8,128)(2,1)} custom-call(bf16[128,1024]{1,0:T(8,128)(2,1)} %bitcast.25, bf16[2,8,512,512]{3,2,1,0:T(8,128)(2,1)} %bitcast.24), custom_call_target="tpu_custom_call" | custom-call | flops 1073741824 | bytes 9699328 | tf_op jit(solution)/shard_map/pallas_call | solution.py:319
  (52 shorter events, 2.2 us)
Async XLA Ops:
  6.5 106.4 %copy-start = (f32[3,3,512]{2,1,0:T(4,128)S(1)}, f32[3,3,512]{2,1,0:T(4,128)}, u32[]{:S(2)}) copy-start(f32[3,3,512]{2,1,0:T(4,128)} %param.18) | copy-start | bytes 55300
  6.5 0.9 copy-start.14
  6.5 2.1 copy-start.13
  6.5 3.4 %copy-start.12 = (s32[8]{0:T(128)S(1)}, s32[8]{0:T(128)}, u32[]{:S(2)}) copy-start(s32[8]{0:T(128)} %constant.71.clone) | copy-start | bytes 100
  6.5 4.6 %copy-start.11 = (s32[8]{0:T(128)S(1)}, s32[8]{0:T(128)}, u32[]{:S(2)}) copy-start(s32[8]{0:T(128)} %constant.73.clone) | copy-start | bytes 100
  6.6 15.3 %copy-start.10 = (s32[8]{0:T(128)S(1)}, s32[8]{0:T(128)}, u32[]{:S(2)}) copy-start(s32[8]{0:T(128)} %constant.68.clone) | copy-start | bytes 100
  6.6 17.2 %copy-start.9 = (s32[8]{0:T(128)S(1)}, s32[8]{0:T(128)}, u32[]{:S(2)}) copy-start(s32[8]{0:T(128)} %constant.70.clone) | copy-start | bytes 100
  6.6 19.2 %copy-start.8 = (s32[8]{0:T(128)S(1)}, s32[8]{0:T(128)}, u32[]{:S(2)}) copy-start(s32[8]{0:T(128)} %constant.72.clone) | copy-start | bytes 100
  6.6 21.1 %copy-start.7 = (s32[8]{0:T(128)S(1)}, s32[8]{0:T(128)}, u32[]{:S(2)}) copy-start(s32[8]{0:T(128)} %constant.74.clone) | copy-start | bytes 100
  6.6 5.8 %copy-start.3 = (bf16[128,4096]{1,0:T(8,128)(2,1)S(1)}, bf16[128,4096]{1,0:T(8,128)(2,1)}, u32[]{:S(2)}) copy-start(bf16[128,4096]{1,0:T(8,128)(2,1)} %param.16) | copy-start | bytes 3145732
  6.6 91.5 %all-gather.4.cloned.1.call-start = ((), (), s32[]{:S(2)}) async-start(), calls=%async_computation.3 | async-start | bytes 7864320 | tf_op jit(solution)/shard_map/all_gather | solution.py:348
  7.3 195.8 %all-gather.6.cloned.1.call-start = ((), (), s32[]{:S(2)}) async-start(), calls=%async_computation.4 | async-start | bytes 8912896 | tf_op jit(solution)/shard_map/all_gather | solution.py:360
  12.6 19.6 %collective-permute-start = (bf16[128,1024]{1,0:T(8,128)(2,1)S(1)}, bf16[128,1024]{1,0:T(8,128)(2,1)S(1)}, u32[]{:S(2)}, u32[]{:S(2)}) collective-permute-start(bf16[128,1024]{1,0:T(8,128)(2,1)S(1)} %get-tuple-element.23), channel_id=1, source_target_pairs={{0,9},{2,11},{4,13},{6,15},{1,25},{3,27},{5,29},{7,31},{8,8},{10,1... | collective-permute-start | bytes 786440 | tf_op jit(solution)/shard_map/ppermute | solution.py:95
  18.5 18.8 %collective-permute-start.1 = (bf16[128,1024]{1,0:T(8,128)(2,1)S(1)}, bf16[128,1024]{1,0:T(8,128)(2,1)S(1)}, u32[]{:S(2)}, u32[]{:S(2)}) collective-permute-start(bf16[128,1024]{1,0:T(8,128)(2,1)S(1)} %get-tuple-element.22), channel_id=1, source_target_pairs={{0,8},{2,10},{4,12},{6,14},{1,24},{3,26},{5,28},{7,30},{8,0},{10,2... | collective-permute-start | bytes 786440 | tf_op jit(solution)/shard_map/ppermute | solution.py:95
  18.5 41.2 %collective-permute-start.2 = (bf16[128,1024]{1,0:T(8,128)(2,1)S(1)}, bf16[128,1024]{1,0:T(8,128)(2,1)S(1)}, u32[]{:S(2)}, u32[]{:S(2)}) collective-permute-start(bf16[128,1024]{1,0:T(8,128)(2,1)S(1)} %get-tuple-element.24), channel_id=1, source_target_pairs={{0,1},{2,3},{4,5},{6,7},{1,17},{3,19},{5,21},{7,23},{8,9},{10,11},... | collective-permute-start | bytes 786440 | tf_op jit(solution)/shard_map/ppermute | solution.py:95
  21.2 38.6 %collective-permute-start.3 = (bf16[128,1024]{1,0:T(8,128)(2,1)S(1)}, bf16[128,1024]{1,0:T(8,128)(2,1)S(1)}, u32[]{:S(2)}, u32[]{:S(2)}) collective-permute-start(bf16[128,1024]{1,0:T(8,128)(2,1)S(1)} %get-tuple-element.21), channel_id=1, source_target_pairs={{0,0},{2,2},{4,4},{6,6},{1,16},{3,18},{5,20},{7,22},{8,1},{10,3},{... | collective-permute-start | bytes 786440 | tf_op jit(solution)/shard_map/ppermute | solution.py:95
  32.2 29.4 %copy-start.6 = (f32[128,512]{1,0:T(8,128)S(1)}, f32[128,512]{1,0:T(8,128)}, u32[]{:S(2)}) copy-start(f32[128,512]{1,0:T(8,128)} %param.19) | copy-start | bytes 786436
  59.8 39.1 %copy-start.4 = (bf16[4,1,128,1024]{3,2,1,0:T(8,128)(2,1)}, bf16[4,1,128,1024]{3,2,1,0:T(8,128)(2,1)S(1)}, u32[]{:S(2)}) copy-start(bf16[4,1,128,1024]{3,2,1,0:T(8,128)(2,1)S(1)} %bitcast_dynamic-update-slice_fusion.refs_0_) | copy-start | bytes 3145732
  59.8 38.3 %collective-permute-start.4 = (bf16[4,1,128,1024]{3,2,1,0:T(8,128)(2,1)S(1)}, bf16[4,1,128,1024]{3,2,1,0:T(8,128)(2,1)}, u32[]{:S(2)}, u32[]{:S(2)}) collective-permute-start(bf16[4,1,128,1024]{3,2,1,0:T(8,128)(2,1)S(1)} %bitcast_dynamic-update-slice_fusion.refs_0_), channel_id=1, source_target_pairs={{0,1},{1,0},{2,3},{3,2},{4,5},{5,4},{6,7},{7,6},{8,9},{9,8},{10,11... | collective-permute-start | bytes 3145736 | tf_op jit(solution)/shard_map/ppermute | solution.py:104
  59.9 38.2 %collective-permute-start.5 = (bf16[512,512]{1,0:T(8,128)(2,1)}, bf16[512,512]{1,0:T(8,128)(2,1)S(1)}, u32[]{:S(2)}, u32[]{:S(2)}) collective-permute-start(bf16[512,512]{1,0:T(8,128)(2,1)} %param.21), channel_id=1, source_target_pairs={{0,0},{1,16},{2,2},{3,18},{4,4},{5,20},{6,6},{7,22},{8,8},{9,24},{... | collective-permute-start | bytes 1572872 | tf_op jit(solution)/shard_map/ppermute | solution.py:303
  98.0 0.8 copy-start.5
  106.3 50.2 %copy-start.1 = (f32[256,256]{1,0:T(8,128)S(1)}, f32[256,256]{1,0:T(8,128)}, u32[]{:S(2)}) copy-start(f32[256,256]{1,0:T(8,128)} %constant.76.clone.bwd_ref) | copy-start | bytes 786436
  106.3 50.2 %copy-start.2 = (f32[128,256]{1,0:T(8,128)S(1)}, f32[128,256]{1,0:T(8,128)}, u32[]{:S(2)}) copy-start(f32[128,256]{1,0:T(8,128)} %constant.75.clone.fwd_ref) | copy-start | bytes 393220
  106.3 50.0 %all-to-all-start.1 = ((bf16[16,3,32,512]{3,2,1,0:T(8,128)(2,1)}), bf16[16,3,32,512]{3,2,1,0:T(8,128)(2,1)S(1)}, u32[]{:S(2)}, u32[]{:S(2)}) async-start(bf16[16,3,32,512]{3,2,1,0:T(8,128)(2,1)} %shard_map.154), calls=%async_computation.1 | async-start | bytes 3145728 | tf_op jit(solution)/shard_map/all_to_all | solution.py:369
Sparse Core Ops, SparseCore 0:
  9.0 49.0 all-gather.3
  99.0 104.0 all-gather.5
where the time goes:
time: 219 us; the launch traced here: 218 us
  waiting for transfers between devices  78.9 us (36%)
  blocking collectives  71.6 us (33%)
  between operations  24.1 us (11%)
  Pallas kernels  18.2 us (8%)
  starting transfers between devices  16.9 us (8%)
  local copies, waits for them, and re-layouts  8.06 us (4%)
    all_to_all x1, waiting for transfers between devices, per_device(): lax.all_to_all(partial, 'seq', split_axis=0, concat_axis=0, tiled=True)  43.3 us
    all_to_all x1, blocking collectives, per_device(): lax.all_to_all(long_filter.T.reshape(seq_parts, chans, rows), 'seq', spli...  36.3 us
    all_to_all x1, blocking collectives, per_device(): lax.all_to_all(gated, ('tp', 'seq'), split_axis=0, concat_axis=0, tiled=T...  35.2 us
    ppermute x4, waiting for transfers between devices, spread_features(): piece = lax.ppermute(piece, ('seq', 'tp'), pairs)  27.3 us
    ppermute x4, starting transfers between devices, spread_features(): piece = lax.ppermute(piece, ('seq', 'tp'), pairs)  9.27 us
    pallas_call x1, Pallas kernels, project_out(): pl.pallas_call(out_kernel, grid=(ranges,), out_shape=jax.ShapeDtypeStruct...  7.87 us
    all_gather x1, waiting for transfers between devices, per_device(): out_weight = lax.all_gather(out_block, 'seq')  7.57 us
    pallas_call x1, Pallas kernels, project_in(): pl.pallas_call(project_kernel, grid_spec=pltpu.PrefetchScalarGridSpec(num...  7.45 us
  transfers between devices with their start and end apart: 9, of which 4 were waited for; matrix products, arithmetic and copies ran while one was open for 3% of the time, Pallas kernels for 5%

commit v1 on v0

--- a/solution.py
+++ b/solution.py
@@ -11,63 +11,11 @@
 
 HIGHEST = lax.Precision.HIGHEST
 UNROLL = 16
+CHUNKS = 2
 
 
 def outer_factor(seq_parts):
-    outer = 1
-    while 4 * outer * outer <= seq_parts and seq_parts % (2 * outer) == 0:
-        outer *= 2
-    return outer
-
-
-def match_rounds(edges, nodes, degree):
-    left = list(edges)
-    rounds = []
-    for _ in range(degree):
-        by_source = {}
-        for edge in left:
-            by_source.setdefault(edge[0], []).append(edge)
-        taken = {}
-
-        def place(source, seen):
-            for edge in by_source[source]:
-                target = edge[1]
-                if target in seen:
-                    continue
-                seen.add(target)
-                if target not in taken or place(taken[target][0], seen):
-                    taken[target] = edge
-                    return True
-            return False
-
-        for source in range(nodes):
-            place(source, set())
-        chosen = sorted(taken.values())
-        rounds.append(chosen)
-        for edge in chosen:
-            left.remove(edge)
-    return rounds
-
-
-def feature_routes(outer, tp_parts):
-    groups = max(1, outer // tp_parts)
-    shares = max(1, tp_parts // outer)
-    edges = []
-    for src_outer in range(outer):
-        for src_tp in range(tp_parts):
-            for group in range(groups):
-                for dst_tp in range(tp_parts):
-                    dst_outer = src_tp * groups + group if groups > 1 else src_tp // shares
-                    slot = src_outer * shares + (src_tp % shares)
-                    edges.append(
-                        (
-                            src_outer * tp_parts + src_tp,
-                            dst_outer * tp_parts + dst_tp,
-                            group * tp_parts + dst_tp,
-                            slot,
-                        )
-                    )
-    return match_rounds(edges, outer * tp_parts, groups * tp_parts)
+    return 2 if seq_parts % 2 == 0 else 1
 
 
 def spread_features(features, outer, inner_parts, tp_parts):
@@ -75,26 +23,30 @@
     groups = max(1, outer // tp_parts)
     shares = max(1, tp_parts // outer)
     width = cols // (groups * tp_parts)
-    node = (lax.axis_index("seq") // inner_parts) * tp_parts + lax.axis_index("tp")
-    buffer = jnp.zeros((outer * shares, rows, width), features.dtype)
-    for chosen in feature_routes(outer, tp_parts):
-        send = np.zeros(outer * tp_parts, np.int32)
-        fill = np.zeros(outer * tp_parts, np.int32)
-        pairs = []
-        for source, target, block, slot in chosen:
-            send[source] = block
-            fill[target] = slot
-            for inner in range(inner_parts):
-                pairs.append(
-                    (
-                        ((source // tp_parts) * inner_parts + inner) * tp_parts + source % tp_parts,
-                        ((target // tp_parts) * inner_parts + inner) * tp_parts + target % tp_parts,
-                    )
-                )
-        piece = lax.dynamic_slice_in_dim(features, jnp.asarray(send)[node] * width, width, axis=1)
-        piece = lax.ppermute(piece, ("seq", "tp"), pairs)
-        buffer = lax.dynamic_update_slice_in_dim(buffer, piece[None], jnp.asarray(fill)[node], axis=0)
-    return buffer.reshape(outer, shares, rows, width)
+    tp_place = lax.axis_index("tp")
+    outer_place = lax.axis_index("seq") // inner_parts
+    blocks = features.reshape(rows, groups, tp_parts, width)
+    held = []
+    for step in range(tp_parts):
+        which = lax.rem(tp_place + step, tp_parts)
+        piece = lax.dynamic_index_in_dim(blocks, which, axis=2, keepdims=False)
+        if step:
+            piece = lax.ppermute(piece, "tp", [(i, (i + step) % tp_parts) for i in range(tp_parts)])
+        held.append(jnp.transpose(piece, (1, 0, 2)))
+    held = jnp.stack(held)
+    order = lax.rem(tp_place - jnp.arange(tp_parts) + tp_parts, tp_parts)
+    ranges = held[order].reshape(outer, shares, rows, width)
+    seq_parts = outer * inner_parts
+    arrived = []
+    for step in range(outer):
+        which = lax.rem(outer_place + step, outer)
+        piece = lax.dynamic_index_in_dim(ranges, which, axis=0, keepdims=False)
+        if step:
+            far = step * inner_parts
+            piece = lax.ppermute(piece, "seq", [(i, (i + far) % seq_parts) for i in range(seq_parts)])
+        arrived.append(piece)
+    order = lax.rem(outer_place - jnp.arange(outer) + outer, outer)
+    return jnp.stack(arrived)[order]
 
 
 def share_over_tp(part, tp_parts):
@@ -105,40 +57,43 @@
     return pieces
 
 
-def project_kernel(place_ref, *refs):
+def project_kernel(tp_parts, place_ref, *refs):
     *share_refs, weight_ref, out_ref = refs
-    tp_parts = len(share_refs)
-    outer, shares, rows, width = share_refs[0].shape
     seq_parts, _, chans, count = out_ref.shape
-    sums = jnp.zeros((count, seq_parts * chans), jnp.float32)
-    for step, share_ref in enumerate(share_refs):
-        which = lax.rem(place_ref[0] - step + tp_parts, tp_parts)
-        for share in range(shares):
-            sums = sums + jnp.dot(
-                share_ref[:, share].reshape(count, width),
-                weight_ref[0, share, which],
-                preferred_element_type=jnp.float32,
-            )
-    turned = sums.T.astype(out_ref.dtype)
+    done = []
+    for first in range(0, len(share_refs), tp_parts):
+        outer, shares, rows, width = share_refs[first].shape
+        sums = jnp.zeros((outer * rows, seq_parts * chans), jnp.float32)
+        for step in range(tp_parts):
+            which = lax.rem(place_ref[0] - step + tp_parts, tp_parts)
+            for share in range(shares):
+                sums = sums + jnp.dot(
+                    share_refs[first + step][:, share].reshape(outer * rows, width),
+                    weight_ref[0, share, which],
+                    preferred_element_type=jnp.float32,
+                )
+        done.append(sums.reshape(outer, rows, seq_parts * chans))
+    turned = jnp.concatenate(done, 1).reshape(count, seq_parts * chans).T.astype(out_ref.dtype)
     for seq in range(seq_parts):
         out_ref[seq, 0] = turned[seq * chans : (seq + 1) * chans]
 
 
-def project_in(pieces, weight, seq_parts):
-    tp_parts = len(pieces)
-    outer, shares, rows, width = pieces[0].shape
+def project_in(chunks, weight, seq_parts):
+    tp_parts = len(chunks[0])
+    outer, shares, rows, width = chunks[0][0].shape
     streams, _, chan_tp = weight.shape
     weight = weight.reshape(streams, shares, tp_parts, width, chan_tp)
     chans = chan_tp // seq_parts
-    count = outer * rows
+    count = outer * rows * len(chunks)
+    pieces = [piece for chunk in chunks for piece in chunk]
     place = lax.axis_index("tp").astype(jnp.int32)[None]
     whole = pl.BlockSpec((outer, shares, rows, width), lambda i, place: (0, 0, 0, 0))
     return pl.pallas_call(
-        project_kernel,
+        functools.partial(project_kernel, tp_parts),
         grid_spec=pltpu.PrefetchScalarGridSpec(
             num_scalar_prefetch=1,
             grid=(streams,),
-            in_specs=[whole] * tp_parts
+            in_specs=[whole] * len(pieces)
             + [
                 pl.BlockSpec(
                     (1, shares, tp_parts, width, chan_tp), lambda i, place: (i, 0, 0, 0, 0)
@@ -150,7 +105,8 @@
         compiler_params=pltpu.CompilerParams(vmem_limit_bytes=56 * 2**20),
         cost_estimate=pl.CostEstimate(
             flops=2 * count * weight.size,
-            bytes_accessed=2 * (weight.size + tp_parts * pieces[0].size) + 2 * streams * count * chan_tp,
+            bytes_accessed=2 * (weight.size + len(pieces) * pieces[0].size)
+            + 2 * streams * count * chan_tp,
             transcendentals=0,
         ),
     )(place, *pieces, weight)
@@ -347,15 +303,21 @@
     inner_groups = [[a * inner_parts + b for b in range(inner_parts)] for a in range(outer)]
     weight = lax.all_gather(in_proj, "seq", axis=1, tiled=True, axis_index_groups=inner_groups)
 
-    part = spread_features(features, outer, inner_parts, tp_parts)
-    part, out_proj, long_filter = lax.optimization_barrier((part, out_proj, long_filter))
-    pieces = share_over_tp(part, tp_parts)
+    chunk_rows = rows // CHUNKS
+    parts = [
+        spread_features(
+            features[index * chunk_rows : (index + 1) * chunk_rows], outer, inner_parts, tp_parts
+        )
+        for index in range(CHUNKS)
+    ]
+    chunks = [share_over_tp(part, tp_parts) for part in parts]
+    _, out_proj, long_filter = lax.optimization_barrier((parts, out_proj, long_filter))
     out_block = lay_out(out_proj, seq_parts, tp_parts)
     filter_blocks = lax.all_to_all(
         long_filter.T.reshape(seq_parts, chans, rows), "seq", split_axis=0, concat_axis=0, tiled=True
     )
-    pieces, weight, out_block, filter_blocks = lax.optimization_barrier(
-        (pieces, weight, out_block, filter_blocks)
+    chunks, weight, out_block, filter_blocks = lax.optimization_barrier(
+        (chunks, weight, out_block, filter_blocks)
     )
     out_weight = lax.all_gather(out_block, "seq")
     out_weight = out_weight.reshape((tp_parts, seq_parts // tp_parts) + out_proj.shape)
@@ -365,7 +327,7 @@
     skip = lax.dynamic_slice_in_dim(skip_gain, position * chans, chans, axis=0)
     skip = jnp.broadcast_to(skip[:, None], (chans, rows))
 
-    partial = project_in(pieces, weight, seq_parts)
+    partial = project_in(chunks, weight, seq_parts)
     parts = lax.all_to_all(partial, "seq", split_axis=0, concat_axis=0, tiled=True)
 
     gated = convolve(parts, filter_blocks, taps, skip, outer)

time: 219 us -> 213 us (0.973)
  the two profiles are of different devices: /device:TPU:0 before, /device:TPU:12 now
where the time goes in v1:
time: 213 us; the launch traced here: 210 us
  waiting for transfers between devices  97.6 us (46%)
  blocking collectives  53.2 us (25%)
  Pallas kernels  19.3 us (9%)
  starting transfers between devices  16.9 us (8%)
  between operations  13.7 us (6%)
  local copies, waits for them, and re-layouts  9.26 us (4%)
    all_to_all x1, blocking collectives, per_device(): lax.all_to_all(long_filter.T.reshape(seq_parts, chans, rows), 'seq', spli...  33 us
    all_to_all x1, waiting for transfers between devices, per_device(): lax.all_to_all(partial, 'seq', split_axis=0, concat_axis=0, tiled=True)  32.2 us
    all_gather x1, waiting for transfers between devices, per_device(): out_weight = lax.all_gather(out_block, 'seq')  23.6 us
    all_to_all x1, blocking collectives, per_device(): lax.all_to_all(gated, ('tp', 'seq'), split_axis=0, concat_axis=0, tiled=T...  20.2 us
    ppermute x2, waiting for transfers between devices, spread_features(): lax.ppermute(piece, 'seq', [(i, (i + far) % seq_parts) for i in range(seq...  18.1 us
    all_gather x1, waiting for transfers between devices, per_device(): lax.all_gather(in_proj, 'seq', axis=1, tiled=True, axis_index_groups=inne...  15.3 us
    pallas_call x1, Pallas kernels, project_in(): pl.pallas_call(functools.partial(project_kernel, tp_parts), grid_spec=plt...  8.55 us
    pallas_call x1, Pallas kernels, project_out(): pl.pallas_call(out_kernel, grid=(ranges,), out_shape=jax.ShapeDtypeStruct...  7.87 us
  transfers between devices with their start and end apart: 10, of which 7 were waited for; matrix products, arithmetic and copies ran while one was open for 4% of the time, Pallas kernels for 5%

profile of v1, /device:TPU:12, one launch (start us, length us, event | category | flops | bytes accessed | tf_op | source)
XLA Modules:
  0.0 210.2 jit_solution(6554505981323247515)
XLA Ops:
  6.5 0.7 all-gather.4.cloned.1.call-update
  7.3 1.3 fusion.4
  9.4 2.2 %constant_dynamic-slice_fusion.3 = (bf16[64,1,1,2048]{3,2,0,1:T(2,128)(2,1)S(1)}, bf16[64,1,1,2048]{3,2,0,1:T(2,128)(2,1)S(1)}, bf16[64,1,1,2048]{3,2,0,1:T(2,128)(2,1)S(1)}, bf16[64,1,1,2048]{3,2,0,1:T(2,128)(2,1)S(1)}) fusion(bf16[64,1,2,2048]{3,2,0,1:T(2,128)(2,1)S(1)} %reshape.101, s32[]{:T(128)S(6)} %select_n.50, s32[]{:T(128)S(6)} %select_n.51, ...), kind=kLoop, calls=%fused_computation.21 | loop fusion | bytes 2097160 | tf_op jit(solution)/shard_map/jit(dynamic_index_in_dim)/dynamic_slice | solution.py:32
  12.4 1.6 collective-permute-start
  14.4 6.6 %collective-permute-done.3 = bf16[64,1,2048]{2,0,1:T(8,128)(2,1)S(1)} collective-permute-done((bf16[64,1,2048]{2,0,1:T(8,128)(2,1)S(1)}, bf16[64,1,2048]{2,0,1:T(8,128)(2,1)S(1)}, u32[]{:S(2)}, u32[]{:S(2)}) %collective-permute-start.3) | collective-permute-done | bytes 262176 | tf_op jit(solution)/shard_map/ppermute | solution.py:34
  21.0 0.6 gather_fusion.2
  21.7 2.7 %collective-permute-start.4 = (bf16[1,64,2048]{2,1,0:T(8,128)(2,1)S(1)}, bf16[1,64,2048]{2,1,0:T(8,128)(2,1)S(1)}, u32[]{:S(2)}, u32[]{:S(2)}) collective-permute-start(bf16[1,64,2048]{2,1,0:T(8,128)(2,1)S(1)} %get-tuple-element.26), channel_id=1, source_target_pairs={{0,16},{2,18},{4,20},{6,22},{8,24},{10,26},{12,28},{14,30},{16,0},... | collective-permute-start | bytes 786440 | tf_op jit(solution)/shard_map/ppermute | solution.py:46
  24.3 1.1 collective-permute-done
  26.1 2.7 %collective-permute-start.1 = (bf16[1,64,2048]{2,1,0:T(8,128)(2,1)S(1)}, bf16[1,64,2048]{2,1,0:T(8,128)(2,1)S(1)}, u32[]{:S(2)}, u32[]{:S(2)}) collective-permute-start(bf16[1,64,2048]{2,1,0:T(8,128)(2,1)S(1)} %get-tuple-element.30), channel_id=1, source_target_pairs={{0,16},{2,18},{4,20},{6,22},{8,24},{10,26},{12,28},{14,30},{16,0},... | collective-permute-start | bytes 786440 | tf_op jit(solution)/shard_map/ppermute | solution.py:46
  28.8 8.6 %collective-permute-done.4 = bf16[1,64,2048]{2,1,0:T(8,128)(2,1)S(1)} collective-permute-done((bf16[1,64,2048]{2,1,0:T(8,128)(2,1)S(1)}, bf16[1,64,2048]{2,1,0:T(8,128)(2,1)S(1)}, u32[]{:S(2)}, u32[]{:S(2)}) %collective-permute-start.4) | collective-permute-done | bytes 262176 | tf_op jit(solution)/shard_map/ppermute | solution.py:46
  38.0 9.5 %collective-permute-done.1 = bf16[1,64,2048]{2,1,0:T(8,128)(2,1)S(1)} collective-permute-done((bf16[1,64,2048]{2,1,0:T(8,128)(2,1)S(1)}, bf16[1,64,2048]{2,1,0:T(8,128)(2,1)S(1)}, u32[]{:S(2)}, u32[]{:S(2)}) %collective-permute-start.1) | collective-permute-done | bytes 262176 | tf_op jit(solution)/shard_map/ppermute | solution.py:46
  48.2 1.9 collective-permute-start.6
  50.4 1.8 collective-permute-start.2
  52.3 33.0 %all_to_all.15.filter_ref = f32[16,32,128]{2,1,0:T(8,128)S(1)} all-to-all(f32[16,32,128]{2,1,0:T(8,128)S(1)} %bitcast.53), channel_id=1, replica_groups=mesh['seq'=16,'tp'=2] {'seq'}, dimensions={0} | all-to-all | bytes 524288 | tf_op jit(solution)/shard_map/all_to_all | solution.py:316
  85.3 15.3 %all-gather.4.cloned.1.call-done = bf16[3,4096,512]{2,1,0:T(8,128)(2,1)} async-done(((bf16[3,512,512]{2,1,0:T(8,128)(2,1)}), bf16[3,4096,512]{2,1,0:T(8,128)(2,1)}) %all-gather.4.cloned.1.call-update) | async-done | bytes 12582928 | tf_op jit(solution)/shard_map/all_gather | solution.py:304
  100.8 8.5 %shard_map.82 = bf16[16,3,32,256]{3,2,1,0:T(8,128)(2,1)} custom-call(s32[1]{0:T(128)} %bitcast.place_ref, bf16[2,1,64,2048]{3,2,1,0:T(8,128)(2,1)} %bitcast.47, bf16[2,1,64,2048]{3,2,1,0:T(8,128)(2,1)} %copy-done.6, bf16[2,1,64,2048]{3,2,1,0:T(8,128)(2,1)} %bitcast.45, bf16[2,1,64,2048]{3,2,1,0:T(8,128)(2,1)} %copy-done.5, bf16[3,1,2,2048,512]{4,3,2,1,0:T(8,128)(2,1)} %bitcast.42), custom_call_target="tpu_custom_call" | custom-call | flops 3221225472 | bytes 15466496 | tf_op jit(solution)/shard_map/pallas_call | solution.py:91
  109.3 5.4 %all-to-all-start.1 = ((bf16[16,3,32,256]{3,2,1,0:T(8,128)(2,1)}), bf16[16,3,32,256]{3,2,1,0:T(8,128)(2,1)S(1)}, u32[]{:S(2)}, u32[]{:S(2)}) async-start(bf16[16,3,32,256]{3,2,1,0:T(8,128)(2,1)} %shard_map.82), calls=%async_computation.1 | async-start | bytes 1572864 | tf_op jit(solution)/shard_map/all_to_all | solution.py:331
  114.7 0.8 dynamic_slice.41
  115.5 32.2 %all-to-all-done.1.parts_ref = bf16[16,3,32,256]{3,2,1,0:T(8,128)(2,1)S(1)} async-done(((bf16[16,3,32,256]{3,2,1,0:T(8,128)(2,1)}), bf16[16,3,32,256]{3,2,1,0:T(8,128)(2,1)S(1)}, u32[]{:S(2)}, u32[]{:S(2)}) %all-to-all-start.1) | async-done | bytes 786464 | tf_op jit(solution)/shard_map/all_to_all | solution.py:331
  147.9 2.9 %shard_map.83 = bf16[16,32,128]{2,1,0:T(8,128)(2,1)S(1)} custom-call(bf16[16,3,32,256]{3,2,1,0:T(8,128)(2,1)S(1)} %all-to-all-done.1.parts_ref, f32[16,32,128]{2,1,0:T(8,128)S(1)} %all_to_all.15.filter_ref, f32[3,3,32,128]{3,2,1,0:T(8,128)S(1)} %broadcast_in_dim.9.taps_ref, f32[32,128]{1,0:T(8,128)S(1)} %broadcast_in_dim.10.skip_ref, ...), custom_call_target="tpu_custom_call" | custom-call | flops 1000000000 | bytes 4194304 | tf_op jit(solution)/shard_map/pallas_call | solution.py:233
  150.8 20.2 %all_to_all.16 = bf16[32,32,128]{2,1,0:T(8,128)(2,1)S(1)} all-to-all(bf16[32,32,128]{2,1,0:T(8,128)(2,1)S(1)} %bitcast.51), channel_id=1, replica_groups=mesh['seq'=16,'tp'=2] {'tp','seq'}, dimensions={0} | all-to-all | bytes 524288 | tf_op jit(solution)/shard_map/all_to_all | solution.py:335
  171.1 0.8 copy.14
  171.9 23.6 %all-gather.6.cloned.1.call-done = bf16[8192,512]{1,0:T(8,128)(2,1)} async-done(((bf16[512,512]{1,0:T(8,128)(2,1)}), bf16[8192,512]{1,0:T(8,128)(2,1)}) %all-gather.6.cloned.1.call-update) | async-done | bytes 8388624 | tf_op jit(solution)/shard_map/all_gather | solution.py:322
  195.5 7.9 %shard_map.84 = bf16[128,4096]{1,0:T(8,128)(2,1)} custom-call(bf16[128,1024]{1,0:T(8,128)(2,1)} %bitcast.48, bf16[2,8,512,512]{3,2,1,0:T(8,128)(2,1)} %bitcast.43), custom_call_target="tpu_custom_call" | custom-call | flops 1073741824 | bytes 9699328 | tf_op jit(solution)/shard_map/pallas_call | solution.py:275
  (50 shorter events, 4.8 us)
Async XLA Ops:
  6.5 108.9 %copy-start = (f32[3,3,512]{2,1,0:T(4,128)S(1)}, f32[3,3,512]{2,1,0:T(4,128)}, u32[]{:S(2)}) copy-start(f32[3,3,512]{2,1,0:T(4,128)} %param.10) | copy-start | bytes 55300
  6.5 94.1 %all-gather.4.cloned.1.call-start = ((), (), s32[]{:S(2)}) async-start(), calls=%async_computation.3 | async-start | bytes 14155776 | tf_op jit(solution)/shard_map/all_gather | solution.py:304
  7.3 188.3 %all-gather.6.cloned.1.call-start = ((), (), s32[]{:S(2)}) async-start(), calls=%async_computation.4 | async-start | bytes 8912896 | tf_op jit(solution)/shard_map/all_gather | solution.py:322
  9.4 42.8 %copy-start.8 = (f32[128,512]{1,0:T(8,128)S(1)}, f32[128,512]{1,0:T(8,128)}, u32[]{:S(2)}) copy-start(f32[128,512]{1,0:T(8,128)} %param.11) | copy-start | bytes 786436
  11.7 9.3 %collective-permute-start.3 = (bf16[64,1,2048]{2,0,1:T(8,128)(2,1)S(1)}, bf16[64,1,2048]{2,0,1:T(8,128)(2,1)S(1)}, u32[]{:S(2)}, u32[]{:S(2)}) collective-permute-start(bf16[64,1,2048]{2,0,1:T(8,128)(2,1)S(1)} %bitcast.55), channel_id=1, source_target_pairs={{0,1},{1,0},{2,3},{3,2},{4,5},{5,4},{6,7},{7,6},{8,9},{9,8},{10,11... | collective-permute-start | bytes 786440 | tf_op jit(solution)/shard_map/ppermute | solution.py:34
  12.4 13.0 %collective-permute-start = (bf16[64,1,2048]{2,0,1:T(8,128)(2,1)S(1)}, bf16[64,1,2048]{2,0,1:T(8,128)(2,1)S(1)}, u32[]{:S(2)}, u32[]{:S(2)}) collective-permute-start(bf16[64,1,2048]{2,0,1:T(8,128)(2,1)S(1)} %bitcast.54), channel_id=1, source_target_pairs={{0,1},{1,0},{2,3},{3,2},{4,5},{5,4},{6,7},{7,6},{8,9},{9,8},{10,11... | collective-permute-start | bytes 786440 | tf_op jit(solution)/shard_map/ppermute | solution.py:34
  21.7 15.7 %collective-permute-start.4 = (bf16[1,64,2048]{2,1,0:T(8,128)(2,1)S(1)}, bf16[1,64,2048]{2,1,0:T(8,128)(2,1)S(1)}, u32[]{:S(2)}, u32[]{:S(2)}) collective-permute-start(bf16[1,64,2048]{2,1,0:T(8,128)(2,1)S(1)} %get-tuple-element.26), channel_id=1, source_target_pairs={{0,16},{2,18},{4,20},{6,22},{8,24},{10,26},{12,28},{14,30},{16,0},... | collective-permute-start | bytes 786440 | tf_op jit(solution)/shard_map/ppermute | solution.py:46
  26.1 21.4 %collective-permute-start.1 = (bf16[1,64,2048]{2,1,0:T(8,128)(2,1)S(1)}, bf16[1,64,2048]{2,1,0:T(8,128)(2,1)S(1)}, u32[]{:S(2)}, u32[]{:S(2)}) collective-permute-start(bf16[1,64,2048]{2,1,0:T(8,128)(2,1)S(1)} %get-tuple-element.30), channel_id=1, source_target_pairs={{0,16},{2,18},{4,20},{6,22},{8,24},{10,26},{12,28},{14,30},{16,0},... | collective-permute-start | bytes 786440 | tf_op jit(solution)/shard_map/ppermute | solution.py:46
  38.0 62.7 %copy-start.3 = (bf16[2,64,2048]{2,1,0:T(8,128)(2,1)}, bf16[2,64,2048]{2,1,0:T(8,128)(2,1)S(1)}, u32[]{:S(2)}) copy-start(bf16[2,64,2048]{2,1,0:T(8,128)(2,1)S(1)} %gather_fusion.3) | copy-start | bytes 1572868
  48.1 52.6 %copy-start.4 = (bf16[2,64,2048]{2,1,0:T(8,128)(2,1)}, bf16[2,64,2048]{2,1,0:T(8,128)(2,1)S(1)}, u32[]{:S(2)}) copy-start(bf16[2,64,2048]{2,1,0:T(8,128)(2,1)S(1)} %gather_fusion.1) | copy-start | bytes 1572868
  48.2 37.2 %collective-permute-start.6 = (bf16[512,512]{1,0:T(8,128)(2,1)}, bf16[512,512]{1,0:T(8,128)(2,1)S(1)}, u32[]{:S(2)}, u32[]{:S(2)}) collective-permute-start(bf16[512,512]{1,0:T(8,128)(2,1)} %param.13), channel_id=1, source_target_pairs={{0,0},{1,16},{2,2},{3,18},{4,4},{5,20},{6,6},{7,22},{8,8},{9,24},{... | collective-permute-start | bytes 1572872 | tf_op jit(solution)/shard_map/ppermute | solution.py:259
  50.1 35.2 %collective-permute-start.5 = (bf16[2,1,64,2048]{3,2,1,0:T(8,128)(2,1)S(1)}, bf16[2,1,64,2048]{3,2,1,0:T(8,128)(2,1)S(1)}, u32[]{:S(2)}, u32[]{:S(2)}) collective-permute-start(bf16[2,1,64,2048]{3,2,1,0:T(8,128)(2,1)S(1)} %bitcast.44), channel_id=1, source_target_pairs={{0,1},{1,0},{2,3},{3,2},{4,5},{5,4},{6,7},{7,6},{8,9},{9,8},{10,11... | collective-permute-start | bytes 1572872 | tf_op jit(solution)/shard_map/ppermute | solution.py:56
  50.4 35.0 %collective-permute-start.2 = (bf16[2,1,64,2048]{3,2,1,0:T(8,128)(2,1)S(1)}, bf16[2,1,64,2048]{3,2,1,0:T(8,128)(2,1)S(1)}, u32[]{:S(2)}, u32[]{:S(2)}) collective-permute-start(bf16[2,1,64,2048]{3,2,1,0:T(8,128)(2,1)S(1)} %bitcast.46), channel_id=1, source_target_pairs={{0,1},{1,0},{2,3},{3,2},{4,5},{5,4},{6,7},{7,6},{8,9},{9,8},{10,11... | collective-permute-start | bytes 1572872 | tf_op jit(solution)/shard_map/ppermute | solution.py:56
  85.3 15.4 %copy-start.7 = (bf16[512,512]{1,0:T(8,128)(2,1)}, bf16[512,512]{1,0:T(8,128)(2,1)S(1)}, u32[]{:S(2)}) copy-start(bf16[512,512]{1,0:T(8,128)(2,1)S(1)} %collective-permute-done.6) | copy-start | bytes 1572868
  85.3 15.4 %copy-start.5 = (bf16[2,1,64,2048]{3,2,1,0:T(8,128)(2,1)}, bf16[2,1,64,2048]{3,2,1,0:T(8,128)(2,1)S(1)}, u32[]{:S(2)}) copy-start(bf16[2,1,64,2048]{3,2,1,0:T(8,128)(2,1)S(1)} %collective-permute-done.5.refs_3_) | copy-start | bytes 1572868
  85.3 15.4 %copy-start.6 = (bf16[2,1,64,2048]{3,2,1,0:T(8,128)(2,1)}, bf16[2,1,64,2048]{3,2,1,0:T(8,128)(2,1)S(1)}, u32[]{:S(2)}) copy-start(bf16[2,1,64,2048]{3,2,1,0:T(8,128)(2,1)S(1)} %collective-permute-done.2.refs_1_) | copy-start | bytes 1572868
  100.7 47.2 %copy-start.1 = (f32[256,256]{1,0:T(8,128)S(1)}, f32[256,256]{1,0:T(8,128)}, u32[]{:S(2)}) copy-start(f32[256,256]{1,0:T(8,128)} %constant.73.clone.bwd_ref) | copy-start | bytes 786436
  100.7 47.2 %copy-start.2 = (f32[128,256]{1,0:T(8,128)S(1)}, f32[128,256]{1,0:T(8,128)}, u32[]{:S(2)}) copy-start(f32[128,256]{1,0:T(8,128)} %constant.72.clone.fwd_ref) | copy-start | bytes 393220
  109.3 38.4 %all-to-all-start.1 = ((bf16[16,3,32,256]{3,2,1,0:T(8,128)(2,1)}), bf16[16,3,32,256]{3,2,1,0:T(8,128)(2,1)S(1)}, u32[]{:S(2)}, u32[]{:S(2)}) async-start(bf16[16,3,32,256]{3,2,1,0:T(8,128)(2,1)} %shard_map.82), calls=%async_computation.1 | async-start | bytes 1572864 | tf_op jit(solution)/shard_map/all_to_all | solution.py:331
Sparse Core Ops, SparseCore 0:
  9.0 91.6 all-gather.3
  102.8 92.6 all-gather.5

commit v2 on v1

--- a/solution.py
+++ b/solution.py
@@ -14,39 +14,79 @@
 CHUNKS = 2
 
 
-def outer_factor(seq_parts):
-    return 2 if seq_parts % 2 == 0 else 1
-
-
-def spread_features(features, outer, inner_parts, tp_parts):
+def outer_factor(seq_parts, tp_parts):
+    outer = tp_parts
+    while 4 * outer * outer <= seq_parts and seq_parts % (2 * outer) == 0:
+        outer *= 2
+    return outer
+
+
+def match_rounds(edges, nodes, degree):
+    left = list(edges)
+    rounds = []
+    for _ in range(degree):
+        by_source = {}
+        for edge in left:
+            by_source.setdefault(edge[0], []).append(edge)
+        taken = {}
+
+        def place(source, seen):
+            for edge in by_source[source]:
+                target = edge[1]
+                if target in seen:
+                    continue
+                seen.add(target)
+                if target not in taken or place(taken[target][0], seen):
+                    taken[target] = edge
+                    return True
+            return False
+
+        for source in range(nodes):
+            place(source, set())
+        chosen = sorted(taken.values())
+        rounds.append(chosen)
+        for edge in chosen:
+            left.remove(edge)
+    return rounds
+
+
+def return_output(out, outer, inner_parts, tp_parts):
+    _, part_rows, width = out.shape
+    per_tp = outer // tp_parts
+    edges = []
+    for src in range(outer):
+        for tp in range(tp_parts):
+            for dst in range(outer):
+                edges.append((src * tp_parts + tp, dst * tp_parts + src // per_tp, dst, tp, src % per_tp))
+    node = (lax.axis_index("seq") // inner_parts) * tp_parts + lax.axis_index("tp")
+    result = jnp.zeros((tp_parts * part_rows, per_tp * width), out.dtype)
+    for chosen in match_rounds(edges, outer * tp_parts, outer):
+        send, row, column = (np.zeros(outer * tp_parts, np.int32) for _ in range(3))
+        pairs = []
+        for source, target, block, row_part, column_part in chosen:
+            send[source], row[target], column[target] = block, row_part, column_part
+            for inner in range(inner_parts):
+                pairs.append(
+                    tuple(
+                        ((end // tp_parts) * inner_parts + inner) * tp_parts + end % tp_parts
+                        for end in (source, target)
+                    )
+                )
+        piece = lax.dynamic_index_in_dim(out, jnp.asarray(send)[node], axis=0, keepdims=False)
+        piece = lax.ppermute(piece, ("seq", "tp"), pairs)
+        result = lax.dynamic_update_slice(
+            result, piece, (jnp.asarray(row)[node] * part_rows, jnp.asarray(column)[node] * width)
+        )
+    return result
+
+
+def share_columns(features, outer, tp_parts):
     rows, cols = features.shape
-    groups = max(1, outer // tp_parts)
-    shares = max(1, tp_parts // outer)
-    width = cols // (groups * tp_parts)
-    tp_place = lax.axis_index("tp")
-    outer_place = lax.axis_index("seq") // inner_parts
-    blocks = features.reshape(rows, groups, tp_parts, width)
-    held = []
-    for step in range(tp_parts):
-        which = lax.rem(tp_place + step, tp_parts)
-        piece = lax.dynamic_index_in_dim(blocks, which, axis=2, keepdims=False)
-        if step:
-            piece = lax.ppermute(piece, "tp", [(i, (i + step) % tp_parts) for i in range(tp_parts)])
-        held.append(jnp.transpose(piece, (1, 0, 2)))
-    held = jnp.stack(held)
-    order = lax.rem(tp_place - jnp.arange(tp_parts) + tp_parts, tp_parts)
-    ranges = held[order].reshape(outer, shares, rows, width)
-    seq_parts = outer * inner_parts
-    arrived = []
-    for step in range(outer):
-        which = lax.rem(outer_place + step, outer)
-        piece = lax.dynamic_index_in_dim(ranges, which, axis=0, keepdims=False)
-        if step:
-            far = step * inner_parts
-            piece = lax.ppermute(piece, "seq", [(i, (i + far) % seq_parts) for i in range(seq_parts)])
-        arrived.append(piece)
-    order = lax.rem(outer_place - jnp.arange(outer) + outer, outer)
-    return jnp.stack(arrived)[order]
+    groups = outer // tp_parts
+    blocks = features.reshape(rows, groups, tp_parts, cols // outer)
+    blocks = jnp.transpose(blocks, (2, 1, 0, 3))
+    blocks = lax.all_to_all(blocks, "tp", split_axis=0, concat_axis=0, tiled=True)
+    return blocks.reshape(outer, rows, -1)
 
 
 def share_over_tp(part, tp_parts):
@@ -62,16 +102,15 @@
     seq_parts, _, chans, count = out_ref.shape
     done = []
     for first in range(0, len(share_refs), tp_parts):
-        outer, shares, rows, width = share_refs[first].shape
+        outer, rows, width = share_refs[first].shape
         sums = jnp.zeros((outer * rows, seq_parts * chans), jnp.float32)
         for step in range(tp_parts):
             which = lax.rem(place_ref[0] - step + tp_parts, tp_parts)
-            for share in range(shares):
-                sums = sums + jnp.dot(
-                    share_refs[first + step][:, share].reshape(outer * rows, width),
-                    weight_ref[0, share, which],
-                    preferred_element_type=jnp.float32,
-                )
+            sums = sums + jnp.dot(
+                share_refs[first + step][...].reshape(outer * rows, width),
+                weight_ref[0, which],
+                preferred_element_type=jnp.float32,
+            )
         done.append(sums.reshape(outer, rows, seq_parts * chans))
     turned = jnp.concatenate(done, 1).reshape(count, seq_parts * chans).T.astype(out_ref.dtype)
     for seq in range(seq_parts):
@@ -80,25 +119,21 @@
 
 def project_in(chunks, weight, seq_parts):
     tp_parts = len(chunks[0])
-    outer, shares, rows, width = chunks[0][0].shape
+    outer, rows, width = chunks[0][0].shape
     streams, _, chan_tp = weight.shape
-    weight = weight.reshape(streams, shares, tp_parts, width, chan_tp)
+    weight = weight.reshape(streams, tp_parts, width, chan_tp)
     chans = chan_tp // seq_parts
     count = outer * rows * len(chunks)
     pieces = [piece for chunk in chunks for piece in chunk]
     place = lax.axis_index("tp").astype(jnp.int32)[None]
-    whole = pl.BlockSpec((outer, shares, rows, width), lambda i, place: (0, 0, 0, 0))
+    whole = pl.BlockSpec((outer, rows, width), lambda i, place: (0, 0, 0))
     return pl.pallas_call(
         functools.partial(project_kernel, tp_parts),
         grid_spec=pltpu.PrefetchScalarGridSpec(
             num_scalar_prefetch=1,
             grid=(streams,),
             in_specs=[whole] * len(pieces)
-            + [
-                pl.BlockSpec(
-                    (1, shares, tp_parts, width, chan_tp), lambda i, place: (i, 0, 0, 0, 0)
-                )
-            ],
+            + [pl.BlockSpec((1, tp_parts, width, chan_tp), lambda i, place: (i, 0, 0, 0))],
             out_specs=pl.BlockSpec((seq_parts, 1, chans, count), lambda i, place: (0, i, 0, 0)),
         ),
         out_shape=jax.ShapeDtypeStruct((seq_parts, streams, chans, count), jnp.bfloat16),
@@ -216,14 +251,29 @@
 
     def last(index, carried):
         long_mix = back[index, :, :rows] + carried
-        gated = query[index] * (long_mix + skip_ref[...] * inner[index])
-        out_ref[index] = gated.astype(out_ref.dtype)
+        query[index] = query[index] * (long_mix + skip_ref[...] * inner[index])
 
     last(0, jnp.zeros((chans, rows), jnp.float32))
     each(blocks - 1, lambda index: last(index + 1, back[index, :, rows:]))
 
-
-def convolve(parts, filter_blocks, taps, skip, outer):
+    tp_parts = out_ref.shape[0]
+    part_rows = rows // tp_parts
+
+    def spread(inner_index):
+        for part in range(tp_parts):
+            for group in range(outer // tp_parts):
+                packed = jnp.zeros((chans, rows), jnp.float32)
+                for place in range(tp_parts):
+                    block = query[(group * tp_parts + place) * inner_parts + inner_index]
+                    shift = (place - part) * part_rows % rows
+                    block = pltpu.roll(block, shift, 1) if shift else block
+                    packed = jnp.where(lane // part_rows == place, block, packed)
+                out_ref[part, inner_index, :, group * rows : (group + 1) * rows] = packed.astype(out_ref.dtype)
+
+    each(inner_parts, spread)
+
+
+def convolve(parts, filter_blocks, taps, skip, outer, tp_parts):
     blocks, streams, chans, _ = parts.shape
     rows = filter_blocks.shape[2]
     forward, backward = tables(rows)
@@ -232,7 +282,9 @@
     vmem = pl.BlockSpec(memory_space=pltpu.VMEM)
     return pl.pallas_call(
         functools.partial(conv_kernel, outer),
-        out_shape=jax.ShapeDtypeStruct(narrow, jnp.bfloat16),
+        out_shape=jax.ShapeDtypeStruct(
+            (tp_parts, blocks // outer, chans, outer // tp_parts * rows), jnp.bfloat16
+        ),
         in_specs=[vmem] * 6,
         out_specs=vmem,
         scratch_shapes=[
@@ -249,92 +301,93 @@
     )(parts, filter_blocks, taps, skip, jnp.asarray(forward), jnp.asarray(backward))
 
 
-def lay_out(out_proj, seq_parts, tp_parts):
-    ranges = seq_parts // tp_parts
-    pairs = []
-    for seq in range(seq_parts):
-        for tp in range(tp_parts):
-            target = (tp * ranges + seq % ranges) * tp_parts + seq // ranges
-            pairs.append((seq * tp_parts + tp, target))
-    return lax.ppermute(out_proj, ("seq", "tp"), pairs)
-
-
-def out_kernel(gated_ref, weight_ref, out_ref):
-    shares, _, depth, _ = weight_ref.shape
+def out_kernel(place_ref, gated_ref, weight_ref, out_ref):
+    tp_parts = gated_ref.shape[0]
     sums = jnp.zeros(out_ref.shape, jnp.float32)
-    for share in range(shares):
-        left = gated_ref[:, share * depth : (share + 1) * depth]
-        sums = sums + jnp.dot(left, weight_ref[share, 0], preferred_element_type=jnp.float32)
+    for step in range(tp_parts):
+        which = lax.rem(place_ref[0] - step + tp_parts, tp_parts)
+        sums = sums + jnp.dot(gated_ref[which], weight_ref[0, step], preferred_element_type=jnp.float32)
     out_ref[...] = sums.astype(out_ref.dtype)
 
 
 def project_out(gated, weight):
-    rows, depth_all = gated.shape
-    shares, ranges, depth, width = weight.shape
-    columns = ranges * width
+    tp_parts, rows, depth = gated.shape
+    inner_parts, _, _, width = weight.shape
+    columns = inner_parts * width
+    place = lax.axis_index("tp").astype(jnp.int32)[None]
     return pl.pallas_call(
         out_kernel,
-        grid=(ranges,),
+        grid_spec=pltpu.PrefetchScalarGridSpec(
+            num_scalar_prefetch=1,
+            grid=(inner_parts,),
+            in_specs=[
+                pl.BlockSpec((tp_parts, rows, depth), lambda b, place: (0, 0, 0)),
+                pl.BlockSpec((1, tp_parts, depth, width), lambda b, place: (b, 0, 0, 0)),
+            ],
+            out_specs=pl.BlockSpec((rows, width), lambda b, place: (0, b)),
+        ),
         out_shape=jax.ShapeDtypeStruct((rows, columns), jnp.bfloat16),
-        in_specs=[
-            pl.BlockSpec((rows, depth_all), lambda r: (0, 0)),
-            pl.BlockSpec((shares, 1, depth, width), lambda r: (0, r, 0, 0)),
-        ],
-        out_specs=pl.BlockSpec((rows, width), lambda r: (0, r)),
         compiler_params=pltpu.CompilerParams(vmem_limit_bytes=56 * 2**20),
         cost_estimate=pl.CostEstimate(
-            flops=2 * rows * depth_all * columns,
+            flops=2 * gated.size * columns,
             bytes_accessed=2 * (weight.size + gated.size + rows * columns),
             transcendentals=0,
         ),
-    )(gated, weight)
+    )(place, gated, weight)
 
 
 def per_device(features, in_proj, short_taps, long_filter, skip_gain, out_proj):
     rows = features.shape[0]
     seq_parts = lax.axis_size("seq")
     tp_parts = lax.axis_size("tp")
-    outer = outer_factor(seq_parts)
+    outer = outer_factor(seq_parts, tp_parts)
     inner_parts = seq_parts // outer
     streams, _, chan_tp = in_proj.shape
     chans = chan_tp // seq_parts
     position = lax.axis_index("seq")
-
     inner_groups = [[a * inner_parts + b for b in range(inner_parts)] for a in range(outer)]
+    outer_groups = [[a * inner_parts + b for a in range(outer)] for b in range(inner_parts)]
+
     weight = lax.all_gather(in_proj, "seq", axis=1, tiled=True, axis_index_groups=inner_groups)
 
     chunk_rows = rows // CHUNKS
-    parts = [
-        spread_features(
-            features[index * chunk_rows : (index + 1) * chunk_rows], outer, inner_parts, tp_parts
-        )
+    shared = [
+        share_columns(features[index * chunk_rows : (index + 1) * chunk_rows], outer, tp_parts)
         for index in range(CHUNKS)
     ]
-    chunks = [share_over_tp(part, tp_parts) for part in parts]
-    _, out_proj, long_filter = lax.optimization_barrier((parts, out_proj, long_filter))
-    out_block = lay_out(out_proj, seq_parts, tp_parts)
+    crossed = [
+        lax.all_to_all(
+            part, "seq", split_axis=0, concat_axis=0, tiled=True, axis_index_groups=outer_groups
+        )
+        for part in shared
+    ]
+    chunks = [share_over_tp(part, tp_parts) for part in crossed]
+
+    _, out_proj = lax.optimization_barrier((shared, out_proj))
+    out_block = jnp.stack(share_over_tp(out_proj, tp_parts))
+    out_weight = lax.all_gather(out_block, "seq", axis_index_groups=inner_groups)
+
+    _, long_filter = lax.optimization_barrier((crossed, long_filter))
     filter_blocks = lax.all_to_all(
         long_filter.T.reshape(seq_parts, chans, rows), "seq", split_axis=0, concat_axis=0, tiled=True
     )
-    chunks, weight, out_block, filter_blocks = lax.optimization_barrier(
-        (chunks, weight, out_block, filter_blocks)
-    )
-    out_weight = lax.all_gather(out_block, "seq")
-    out_weight = out_weight.reshape((tp_parts, seq_parts // tp_parts) + out_proj.shape)
-
     taps = lax.dynamic_slice_in_dim(short_taps, position * chans, chans, axis=2)
     taps = jnp.broadcast_to(taps[..., None], taps.shape + (rows,))
     skip = lax.dynamic_slice_in_dim(skip_gain, position * chans, chans, axis=0)
     skip = jnp.broadcast_to(skip[:, None], (chans, rows))
+    chunks, filter_blocks, taps, skip = lax.optimization_barrier((chunks, filter_blocks, taps, skip))
 
     partial = project_in(chunks, weight, seq_parts)
     parts = lax.all_to_all(partial, "seq", split_axis=0, concat_axis=0, tiled=True)
 
-    gated = convolve(parts, filter_blocks, taps, skip, outer)
-    gated = jnp.broadcast_to(gated[None], (tp_parts,) + gated.shape).reshape(-1, chans, rows)
-    gated = lax.all_to_all(gated, ("tp", "seq"), split_axis=0, concat_axis=0, tiled=True)
-    gated = gated.reshape(tp_parts * chan_tp, rows).T
-    return project_out(gated, out_weight)
+    gated = convolve(parts, filter_blocks, taps, skip, outer, tp_parts)
+    gated = jnp.broadcast_to(gated[:, None], (tp_parts, outer) + gated.shape[1:])
+    gated = lax.all_to_all(
+        gated.reshape((-1,) + gated.shape[3:]), ("tp", "seq"), split_axis=0, concat_axis=0, tiled=True
+    )
+    gated = jnp.swapaxes(gated.reshape(tp_parts, chan_tp, -1), 1, 2)
+    out = project_out(gated, out_weight)
+    return return_output(out.reshape(outer, rows // tp_parts, -1), outer, inner_parts, tp_parts)
 
 
 def solution(mesh):

time: 213 us -> 204 us (0.958)
  waiting for transfers between devices: 97.6 us -> 36.1 us
  starting transfers between devices: 16.9 us -> 41.6 us
  local copies, waits for them, and re-layouts: 9.26 us -> 27.5 us
  between operations: 13.7 us -> 26.2 us
  Pallas kernels: 19.3 us -> 15.4 us
    ppermute x5 -> x4, waiting for transfers between devices: 25.8 us -> 0.01 us  [return_output(): piece = lax.ppermute(piece, ('seq', 'tp'), pairs)]
    all_gather x1, waiting for transfers between devices: 23.6 us -> 0.01 us  [per_device(): lax.all_gather(out_block, 'seq', axis_index_groups=inner_groups)]
    all_to_all x1 -> x5, starting transfers between devices: 5.41 us -> 27.5 us  [the longest x2 11.6 us: per_device(): lax.all_to_all(part, 'seq', split_axis=0, concat_axis=0, tiled=True, axis...]
    all_gather x1, waiting for transfers between devices: 15.3 us -> 0.01 us  [per_device(): lax.all_gather(in_proj, 'seq', axis=1, tiled=True, axis_index_groups=inne...]
    dynamic_update_slice x0 -> x4, local copies, waits for them, and re-layouts: none -> 13.3 us  [return_output(): lax.dynamic_update_slice(result, piece, (jnp.asarray(row)[node] * part_ro...]
    ppermute x2 -> x3, waiting for transfers between devices: 0.01 us -> 5.1 us  [share_over_tp(): pieces.append(lax.ppermute(part, 'tp', pairs))]
    pallas_call x1, Pallas kernels: 7.87 us -> 4.94 us  [project_out(): pl.pallas_call(out_kernel, grid_spec=pltpu.PrefetchScalarGridSpec(num_sca...]
    dynamic_slice x3 -> x8, local copies, waits for them, and re-layouts: 2.26 us -> 4.87 us  [the longest x4 2.46 us: return_output(): jnp.asarray(send)[node]]
  transfers between devices with their start and end apart: 10 -> 14, of which waited for: 7 -> 6; matrix products, arithmetic and copies ran while one was open for 4% -> 11% of each run, Pallas kernels for 5% -> 5%
where the time goes in v2:
time: 204 us; the launch traced here: 200 us
  blocking collectives  52.4 us (26%)
  starting transfers between devices  41.6 us (20%)
  waiting for transfers between devices  36.1 us (18%)
  local copies, waits for them, and re-layouts  27.5 us (13%)
  between operations  26.2 us (13%)
  Pallas kernels  15.4 us (8%)
    all_to_all x1, blocking collectives, per_device(): lax.all_to_all(partial, 'seq', split_axis=0, concat_axis=0, tiled=True)  41.9 us
    dynamic_update_slice x4, local copies, waits for them, and re-layouts, return_output(): lax.dynamic_update_slice(result, piece, (jnp.asarray(row)[node] * part_ro...  13.3 us
    all_to_all x2, waiting for transfers between devices, per_device(): lax.all_to_all(part, 'seq', split_axis=0, concat_axis=0, tiled=True, axis...  12.3 us
    all_to_all x2, starting transfers between devices, per_device(): lax.all_to_all(part, 'seq', split_axis=0, concat_axis=0, tiled=True, axis...  11.6 us
    ppermute x4, starting transfers between devices, return_output(): piece = lax.ppermute(piece, ('seq', 'tp'), pairs)  11.2 us
    all_to_all x1, blocking collectives, share_columns(): lax.all_to_all(blocks, 'tp', split_axis=0, concat_axis=0, tiled=True)  10.5 us
    pallas_call x1, Pallas kernels, project_in(): pl.pallas_call(functools.partial(project_kernel, tp_parts), grid_spec=plt...  7.5 us
    all_to_all x1, waiting for transfers between devices, per_device(): lax.all_to_all(long_filter.T.reshape(seq_parts, chans, rows), 'seq', spli...  7.32 us
  transfers between devices with their start and end apart: 14, of which 6 were waited for; matrix products, arithmetic and copies ran while one was open for 11% of the time, Pallas kernels for 5%

profile of v2, /device:TPU:12, one launch (start us, length us, event | category | flops | bytes accessed | tf_op | source)
XLA Modules:
  0.0 200.1 jit_solution(3147660681953104582)
XLA Ops:
  9.2 4.7 %all-to-all-start = ((bf16[2,2,64,1024]{3,2,1,0:T(8,128)(2,1)}), bf16[2,2,64,1024]{3,2,1,0:T(8,128)(2,1)}, u32[]{:S(2)}, u32[]{:S(2)}) async-start(bf16[2,2,64,1024]{3,2,1,0:T(8,128)(2,1)} %bitcast.38), calls=%async_computation | async-start | bytes 1048576 | tf_op jit(solution)/shard_map/all_to_all | solution.py:88
  14.5 6.1 %all-to-all-done = bf16[2,2,64,1024]{3,2,1,0:T(8,128)(2,1)} async-done(((bf16[2,2,64,1024]{3,2,1,0:T(8,128)(2,1)}), bf16[2,2,64,1024]{3,2,1,0:T(8,128)(2,1)}, u32[]{:S(2)}, u32[]{:S(2)}) %all-to-all-start) | async-done | bytes 524320 | tf_op jit(solution)/shard_map/all_to_all | solution.py:88
  20.5 10.5 %all_to_all.35 = bf16[2,2,64,1024]{3,2,1,0:T(8,128)(2,1)} all-to-all(bf16[2,2,64,1024]{3,2,1,0:T(8,128)(2,1)S(1)} %bitcast.43), channel_id=1, replica_groups=mesh['seq'=16,'tp'=2] {'tp'}, dimensions={0} | all-to-all | bytes 1048576 | tf_op jit(solution)/shard_map/all_to_all | solution.py:88
  31.0 1.7 collective-permute-start.2
  32.8 5.3 %all-to-all-start.1 = ((bf16[4,64,1024]{2,1,0:T(8,128)(2,1)}), bf16[4,64,1024]{2,1,0:T(8,128)(2,1)S(1)}, u32[]{:S(2)}, u32[]{:S(2)}) async-start(bf16[4,64,1024]{2,1,0:T(8,128)(2,1)} %bitcast.2), calls=%async_computation.1 | async-start | bytes 1048576 | tf_op jit(solution)/shard_map/all_to_all | solution.py:359
  38.1 5.1 %collective-permute-done.2 = bf16[512,512]{1,0:T(8,128)(2,1)S(1)} collective-permute-done((bf16[512,512]{1,0:T(8,128)(2,1)S(1)}, bf16[512,512]{1,0:T(8,128)(2,1)S(1)}, u32[]{:S(2)}, u32[]{:S(2)}) %collective-permute-start.2) | collective-permute-done | bytes 524320 | tf_op jit(solution)/shard_map/ppermute | solution.py:96
  44.3 3.4 %all-to-all-done.1.refs_0_ = bf16[4,64,1024]{2,1,0:T(8,128)(2,1)S(1)} async-done(((bf16[4,64,1024]{2,1,0:T(8,128)(2,1)}), bf16[4,64,1024]{2,1,0:T(8,128)(2,1)S(1)}, u32[]{:S(2)}, u32[]{:S(2)}) %all-to-all-start.1) | async-done | bytes 524320 | tf_op jit(solution)/shard_map/all_to_all | solution.py:359
  47.7 6.3 %all-to-all-start.3 = ((bf16[4,64,1024]{2,1,0:T(8,128)(2,1)}), bf16[4,64,1024]{2,1,0:T(8,128)(2,1)S(1)}, u32[]{:S(2)}, u32[]{:S(2)}) async-start(bf16[4,64,1024]{2,1,0:T(8,128)(2,1)} %bitcast.4), calls=%async_computation.3 | async-start | bytes 1048576 | tf_op jit(solution)/shard_map/all_to_all | solution.py:359
  54.5 8.9 %all-to-all-done.3.refs_2_ = bf16[4,64,1024]{2,1,0:T(8,128)(2,1)S(1)} async-done(((bf16[4,64,1024]{2,1,0:T(8,128)(2,1)}), bf16[4,64,1024]{2,1,0:T(8,128)(2,1)S(1)}, u32[]{:S(2)}, u32[]{:S(2)}) %all-to-all-start.3) | async-done | bytes 524320 | tf_op jit(solution)/shard_map/all_to_all | solution.py:359
  64.8 6.5 %all-to-all-start.4 = ((f32[16,32,128]{2,1,0:T(8,128)}), f32[16,32,128]{2,1,0:T(8,128)S(1)}, u32[]{:S(2)}, u32[]{:S(2)}) async-start(f32[16,32,128]{2,1,0:T(8,128)} %bitcast.6), calls=%async_computation.4 | async-start | bytes 524288 | tf_op jit(solution)/shard_map/all_to_all | solution.py:371
  72.2 7.3 %all-to-all-done.4.filter_ref = f32[16,32,128]{2,1,0:T(8,128)S(1)} async-done(((f32[16,32,128]{2,1,0:T(8,128)}), f32[16,32,128]{2,1,0:T(8,128)S(1)}, u32[]{:S(2)}, u32[]{:S(2)}) %all-to-all-start.4) | async-done | bytes 262176 | tf_op jit(solution)/shard_map/all_to_all | solution.py:371
  80.5 7.5 %shard_map.190 = bf16[16,3,32,512]{3,2,1,0:T(8,128)(2,1)} custom-call(s32[1]{0:T(128)} %bitcast.place_ref, bf16[4,64,1024]{2,1,0:T(8,128)(2,1)} %copy-done.5, bf16[4,64,1024]{2,1,0:T(8,128)(2,1)} %copy-done.9, bf16[4,64,1024]{2,1,0:T(8,128)(2,1)} %copy-done.6, bf16[4,64,1024]{2,1,0:T(8,128)(2,1)} %copy-done.10, bf16[3,2,1024,512]{3,2,1,0:T(8,128)(2,1)} %bitcast.47), custom_call_target="tpu_custom_call" | custom-call | flops 3221225472 | bytes 9961472 | tf_op jit(solution)/shard_map/pallas_call | solution.py:130
  88.0 41.9 %all_to_all.36.parts_ref = bf16[16,3,32,512]{3,2,1,0:T(8,128)(2,1)S(1)} all-to-all(bf16[16,3,32,512]{3,2,1,0:T(8,128)(2,1)} %shard_map.190), channel_id=1, replica_groups=mesh['seq'=16,'tp'=2] {'seq'}, dimensions={0} | all-to-all | bytes 3145728 | tf_op jit(solution)/shard_map/all_to_all | solution.py:381
  129.9 2.9 %shard_map.191 = bf16[2,4,32,256]{3,2,1,0:T(8,128)(2,1)S(1)} custom-call(bf16[16,3,32,512]{3,2,1,0:T(8,128)(2,1)S(1)} %all_to_all.36.parts_ref, f32[16,32,128]{2,1,0:T(8,128)S(1)} %all-to-all-done.4.filter_ref, f32[3,3,32,128]{3,2,1,0:T(8,128)S(1)} %broadcast_in_dim.12.taps_ref, f32[32,128]{1,0:T(8,128)S(1)} %broadcast_in_dim.13.skip_ref, ...), custom_call_target="tpu_custom_call" | custom-call | flops 1000000000 | bytes 4194304 | tf_op jit(solution)/shard_map/pallas_call | solution.py:283
  133.7 4.6 %all-to-all-start.6 = ((bf16[32,32,256]{2,1,0:T(8,128)(2,1)}), bf16[32,32,256]{2,1,0:T(8,128)(2,1)S(1)}, u32[]{:S(2)}, u32[]{:S(2)}) async-start(bf16[32,32,256]{2,1,0:T(8,128)(2,1)} %bitcast.8), calls=%async_computation.6 | async-start | bytes 1048576 | tf_op jit(solution)/shard_map/all_to_all | solution.py:385
  148.3 4.6 %all-to-all-done.6 = bf16[32,32,256]{2,1,0:T(8,128)(2,1)S(1)} async-done(((bf16[32,32,256]{2,1,0:T(8,128)(2,1)}), bf16[32,32,256]{2,1,0:T(8,128)(2,1)S(1)}, u32[]{:S(2)}, u32[]{:S(2)}) %all-to-all-start.6) | async-done | bytes 524320 | tf_op jit(solution)/shard_map/all_to_all | solution.py:385
  153.9 4.9 %shard_map.192 = bf16[256,2048]{1,0:T(8,128)(2,1)} custom-call(s32[1]{0:T(128)} %bitcast.place_ref, bf16[2,256,512]{2,1,0:T(8,128)(2,1)} %bitcast.41, bf16[4,2,512,512]{3,2,1,0:T(8,128)(2,1)} %bitcast.39), custom_call_target="tpu_custom_call" | custom-call | flops 1073741824 | bytes 5767168 | tf_op jit(solution)/shard_map/pallas_call | solution.py:318
  158.8 1.3 dynamic-slice_bitcast_fusion
  160.1 3.5 %collective-permute-start.3 = (bf16[64,2048]{1,0:T(8,128)(2,1)S(1)}, bf16[64,2048]{1,0:T(8,128)(2,1)S(1)}, u32[]{:S(2)}, u32[]{:S(2)}) collective-permute-start(bf16[64,2048]{1,0:T(8,128)(2,1)S(1)} %get-tuple-element.26), channel_id=1, source_target_pairs={{0,24},{2,26},{4,28},{6,30},{1,16},{3,18},{5,20},{7,22},{8,8},{10,... | collective-permute-start | bytes 786440 | tf_op jit(solution)/shard_map/ppermute | solution.py:76
  164.8 6.5 %collective-permute-start.6 = (bf16[64,2048]{1,0:T(8,128)(2,1)S(1)}, bf16[64,2048]{1,0:T(8,128)(2,1)S(1)}, u32[]{:S(2)}, u32[]{:S(2)}) collective-permute-start(bf16[64,2048]{1,0:T(8,128)(2,1)S(1)} %get-tuple-element.23), channel_id=1, source_target_pairs={{0,0},{2,2},{4,4},{6,6},{1,8},{3,10},{5,12},{7,14},{8,16},{10,18},... | collective-permute-start | bytes 786440 | tf_op jit(solution)/shard_map/ppermute | solution.py:76
  178.9 3.0 %dynamic_update_slice.12 = bf16[128,4096]{1,0:T(8,128)(2,1)S(1)} dynamic-update-slice(bf16[128,4096]{1,0:T(8,128)(2,1)S(1)} %broadcast_in_dim.10, bf16[64,2048]{1,0:T(8,128)(2,1)S(1)} %collective-permute-done.3, s32[]{:T(128)S(6)} %select_n.64, s32[]{:T(128)S(6)} %select_n.65) | dynamic-update-slice | bytes 524292 | tf_op jit(solution)/shard_map/dynamic_update_slice | solution.py:77
  181.9 2.5 %dynamic_update_slice.13 = bf16[128,4096]{1,0:T(8,128)(2,1)S(1)} dynamic-update-slice(bf16[128,4096]{1,0:T(8,128)(2,1)S(1)} %dynamic_update_slice.12, bf16[64,2048]{1,0:T(8,128)(2,1)S(1)} %collective-permute-done.4, s32[]{:T(128)S(6)} %select_n.67, s32[]{:T(128)S(6)} %select_n.68) | dynamic-update-slice | bytes 524292 | tf_op jit(solution)/shard_map/dynamic_update_slice | solution.py:77
  184.4 4.3 %dynamic_update_slice.14 = bf16[128,4096]{1,0:T(8,128)(2,1)S(1)} dynamic-update-slice(bf16[128,4096]{1,0:T(8,128)(2,1)S(1)} %dynamic_update_slice.13, bf16[64,2048]{1,0:T(8,128)(2,1)S(1)} %collective-permute-done.5, s32[]{:T(128)S(6)} %select_n.70, s32[]{:T(128)S(6)} %select_n.71) | dynamic-update-slice | bytes 524292 | tf_op jit(solution)/shard_map/dynamic_update_slice | solution.py:77
  189.7 3.5 %dynamic_update_slice.15 = bf16[128,4096]{1,0:T(8,128)(2,1)} dynamic-update-slice(bf16[128,4096]{1,0:T(8,128)(2,1)} %copy-done.4, bf16[64,2048]{1,0:T(8,128)(2,1)S(1)} %collective-permute-done.6, s32[]{:T(128)S(6)} %select_n.73, s32[]{:T(128)S(6)} %select_n.74) | dynamic-update-slice | bytes 524292 | tf_op jit(solution)/shard_map/dynamic_update_slice | solution.py:77
  (76 shorter events, 17.0 us)
Async XLA Ops:
  6.5 65.6 %copy-start = (f32[3,3,512]{2,1,0:T(4,128)S(1)}, f32[3,3,512]{2,1,0:T(4,128)}, u32[]{:S(2)}) copy-start(f32[3,3,512]{2,1,0:T(4,128)} %param.22) | copy-start | bytes 55300
  6.5 73.2 %all-gather.4.cloned.1.call-start = ((), (), s32[]{:S(2)}) async-start(), calls=%async_computation.7 | async-start | bytes 7864320 | tf_op jit(solution)/shard_map/all_gather | solution.py:351
  9.2 11.3 %all-to-all-start = ((bf16[2,2,64,1024]{3,2,1,0:T(8,128)(2,1)}), bf16[2,2,64,1024]{3,2,1,0:T(8,128)(2,1)}, u32[]{:S(2)}, u32[]{:S(2)}) async-start(bf16[2,2,64,1024]{3,2,1,0:T(8,128)(2,1)} %bitcast.38), calls=%async_computation | async-start | bytes 1048576 | tf_op jit(solution)/shard_map/all_to_all | solution.py:88
  13.9 17.1 %copy-start.7 = (bf16[512,512]{1,0:T(8,128)(2,1)S(1)}, bf16[512,512]{1,0:T(8,128)(2,1)}, u32[]{:S(2)}) copy-start(bf16[512,512]{1,0:T(8,128)(2,1)} %param.25) | copy-start | bytes 1572868
  31.0 12.2 %collective-permute-start.2 = (bf16[512,512]{1,0:T(8,128)(2,1)S(1)}, bf16[512,512]{1,0:T(8,128)(2,1)S(1)}, u32[]{:S(2)}, u32[]{:S(2)}) collective-permute-start(bf16[512,512]{1,0:T(8,128)(2,1)S(1)} %copy-done.7), channel_id=1, source_target_pairs={{0,1},{1,0},{2,3},{3,2},{4,5},{5,4},{6,7},{7,6},{8,9},{9,8},{10,11... | collective-permute-start | bytes 1572872 | tf_op jit(solution)/shard_map/ppermute | solution.py:96
  32.8 14.9 %all-to-all-start.1 = ((bf16[4,64,1024]{2,1,0:T(8,128)(2,1)}), bf16[4,64,1024]{2,1,0:T(8,128)(2,1)S(1)}, u32[]{:S(2)}, u32[]{:S(2)}) async-start(bf16[4,64,1024]{2,1,0:T(8,128)(2,1)} %bitcast.2), calls=%async_computation.1 | async-start | bytes 1048576 | tf_op jit(solution)/shard_map/all_to_all | solution.py:359
  38.1 115.8 %all-gather.6.cloned.1.call-start = ((), (), s32[]{:S(2)}) async-start(), calls=%async_computation.8 | async-start | bytes 5242880 | tf_op jit(solution)/shard_map/all_gather | solution.py:368
  44.3 19.7 %copy-start.8 = (f32[128,512]{1,0:T(8,128)S(1)}, f32[128,512]{1,0:T(8,128)}, u32[]{:S(2)}) copy-start(f32[128,512]{1,0:T(8,128)} %param.23) | copy-start | bytes 786436
  47.6 32.0 %copy-start.5 = (bf16[4,64,1024]{2,1,0:T(8,128)(2,1)}, bf16[4,64,1024]{2,1,0:T(8,128)(2,1)S(1)}, u32[]{:S(2)}) copy-start(bf16[4,64,1024]{2,1,0:T(8,128)(2,1)S(1)} %all-to-all-done.1.refs_0_) | copy-start | bytes 1572868
  47.7 15.8 %all-to-all-start.3 = ((bf16[4,64,1024]{2,1,0:T(8,128)(2,1)}), bf16[4,64,1024]{2,1,0:T(8,128)(2,1)S(1)}, u32[]{:S(2)}, u32[]{:S(2)}) async-start(bf16[4,64,1024]{2,1,0:T(8,128)(2,1)} %bitcast.4), calls=%async_computation.3 | async-start | bytes 1048576 | tf_op jit(solution)/shard_map/all_to_all | solution.py:359
  54.0 25.5 %collective-permute-start = (bf16[4,64,1024]{2,1,0:T(8,128)(2,1)S(1)}, bf16[4,64,1024]{2,1,0:T(8,128)(2,1)S(1)}, u32[]{:S(2)}, u32[]{:S(2)}) collective-permute-start(bf16[4,64,1024]{2,1,0:T(8,128)(2,1)S(1)} %all-to-all-done.1.refs_0_), channel_id=1, source_target_pairs={{0,1},{1,0},{2,3},{3,2},{4,5},{5,4},{6,7},{7,6},{8,9},{9,8},{10,11... | collective-permute-start | bytes 1572872 | tf_op jit(solution)/shard_map/ppermute | solution.py:96
  63.4 16.3 %copy-start.6 = (bf16[4,64,1024]{2,1,0:T(8,128)(2,1)}, bf16[4,64,1024]{2,1,0:T(8,128)(2,1)S(1)}, u32[]{:S(2)}) copy-start(bf16[4,64,1024]{2,1,0:T(8,128)(2,1)S(1)} %all-to-all-done.3.refs_2_) | copy-start | bytes 1572868
  63.4 16.1 %collective-permute-start.1 = (bf16[4,64,1024]{2,1,0:T(8,128)(2,1)S(1)}, bf16[4,64,1024]{2,1,0:T(8,128)(2,1)S(1)}, u32[]{:S(2)}, u32[]{:S(2)}) collective-permute-start(bf16[4,64,1024]{2,1,0:T(8,128)(2,1)S(1)} %all-to-all-done.3.refs_2_), channel_id=1, source_target_pairs={{0,1},{1,0},{2,3},{3,2},{4,5},{5,4},{6,7},{7,6},{8,9},{9,8},{10,11... | collective-permute-start | bytes 1572872 | tf_op jit(solution)/shard_map/ppermute | solution.py:96
  64.8 14.7 %all-to-all-start.4 = ((f32[16,32,128]{2,1,0:T(8,128)}), f32[16,32,128]{2,1,0:T(8,128)S(1)}, u32[]{:S(2)}, u32[]{:S(2)}) async-start(f32[16,32,128]{2,1,0:T(8,128)} %bitcast.6), calls=%async_computation.4 | async-start | bytes 524288 | tf_op jit(solution)/shard_map/all_to_all | solution.py:371
  88.0 41.9 %copy-start.1 = (f32[256,256]{1,0:T(8,128)S(1)}, f32[256,256]{1,0:T(8,128)}, u32[]{:S(2)}) copy-start(f32[256,256]{1,0:T(8,128)} %constant.82.clone.bwd_ref) | copy-start | bytes 786436
  88.0 41.9 %copy-start.2 = (f32[128,256]{1,0:T(8,128)S(1)}, f32[128,256]{1,0:T(8,128)}, u32[]{:S(2)}) copy-start(f32[128,256]{1,0:T(8,128)} %constant.81.clone.fwd_ref) | copy-start | bytes 393220
  133.7 19.2 %all-to-all-start.6 = ((bf16[32,32,256]{2,1,0:T(8,128)(2,1)}), bf16[32,32,256]{2,1,0:T(8,128)(2,1)S(1)}, u32[]{:S(2)}, u32[]{:S(2)}) async-start(bf16[32,32,256]{2,1,0:T(8,128)(2,1)} %bitcast.8), calls=%async_computation.6 | async-start | bytes 1048576 | tf_op jit(solution)/shard_map/all_to_all | solution.py:385
  158.8 13.8 %copy-start.13 = (s32[8]{0:T(128)S(1)}, s32[8]{0:T(128)}, u32[]{:S(2)}) copy-start(s32[8]{0:T(128)} %constant.85.clone) | copy-start | bytes 100
  158.8 15.7 %copy-start.12 = (s32[8]{0:T(128)S(1)}, s32[8]{0:T(128)}, u32[]{:S(2)}) copy-start(s32[8]{0:T(128)} %constant.87.clone) | copy-start | bytes 100
  158.8 17.0 %copy-start.11 = (s32[8]{0:T(128)S(1)}, s32[8]{0:T(128)}, u32[]{:S(2)}) copy-start(s32[8]{0:T(128)} %constant.89.clone) | copy-start | bytes 100
  160.1 18.7 %collective-permute-start.3 = (bf16[64,2048]{1,0:T(8,128)(2,1)S(1)}, bf16[64,2048]{1,0:T(8,128)(2,1)S(1)}, u32[]{:S(2)}, u32[]{:S(2)}) collective-permute-start(bf16[64,2048]{1,0:T(8,128)(2,1)S(1)} %get-tuple-element.26), channel_id=1, source_target_pairs={{0,24},{2,26},{4,28},{6,30},{1,16},{3,18},{5,20},{7,22},{8,8},{10,... | collective-permute-start | bytes 786440 | tf_op jit(solution)/shard_map/ppermute | solution.py:76
  163.6 18.3 %collective-permute-start.4 = (bf16[64,2048]{1,0:T(8,128)(2,1)S(1)}, bf16[64,2048]{1,0:T(8,128)(2,1)S(1)}, u32[]{:S(2)}, u32[]{:S(2)}) collective-permute-start(bf16[64,2048]{1,0:T(8,128)(2,1)S(1)} %get-tuple-element.25), channel_id=1, source_target_pairs={{0,16},{2,18},{4,20},{6,22},{1,0},{3,2},{5,4},{7,6},{8,24},{10,26}... | collective-permute-start | bytes 786440 | tf_op jit(solution)/shard_map/ppermute | solution.py:76
  163.7 20.7 %collective-permute-start.5 = (bf16[64,2048]{1,0:T(8,128)(2,1)S(1)}, bf16[64,2048]{1,0:T(8,128)(2,1)S(1)}, u32[]{:S(2)}, u32[]{:S(2)}) collective-permute-start(bf16[64,2048]{1,0:T(8,128)(2,1)S(1)} %get-tuple-element.24), channel_id=1, source_target_pairs={{0,8},{2,10},{4,12},{6,14},{1,24},{3,26},{5,28},{7,30},{8,0},{10,2... | collective-permute-start | bytes 786440 | tf_op jit(solution)/shard_map/ppermute | solution.py:76
  164.8 24.0 %collective-permute-start.6 = (bf16[64,2048]{1,0:T(8,128)(2,1)S(1)}, bf16[64,2048]{1,0:T(8,128)(2,1)S(1)}, u32[]{:S(2)}, u32[]{:S(2)}) collective-permute-start(bf16[64,2048]{1,0:T(8,128)(2,1)S(1)} %get-tuple-element.23), channel_id=1, source_target_pairs={{0,0},{2,2},{4,4},{6,6},{1,8},{3,10},{5,12},{7,14},{8,16},{10,18},... | collective-permute-start | bytes 786440 | tf_op jit(solution)/shard_map/ppermute | solution.py:76
  (9 other events, 50.3 us)
Sparse Core Ops, SparseCore 0:
  8.9 47.4 all-gather.3
  58.0 37.2 all-gather.5

commit v3 on v2

--- a/solution.py
+++ b/solution.py
@@ -21,72 +21,97 @@
     return outer
 
 
-def match_rounds(edges, nodes, degree):
-    left = list(edges)
-    rounds = []
-    for _ in range(degree):
-        by_source = {}
-        for edge in left:
-            by_source.setdefault(edge[0], []).append(edge)
-        taken = {}
-
-        def place(source, seen):
-            for edge in by_source[source]:
-                target = edge[1]
-                if target in seen:
-                    continue
-                seen.add(target)
-                if target not in taken or place(taken[target][0], seen):
-                    taken[target] = edge
-                    return True
-            return False
-
-        for source in range(nodes):
-            place(source, set())
-        chosen = sorted(taken.values())
-        rounds.append(chosen)
-        for edge in chosen:
-            left.remove(edge)
-    return rounds
+def assemble_kernel(place_ref, *refs):
+    *piece_refs, out_ref, sems = refs
+    part_rows, width = piece_refs[0].shape
+    copies = []
+    for index, piece_ref in enumerate(piece_refs):
+        row = pl.multiple_of(place_ref[2 * index] * part_rows, part_rows)
+        column = pl.multiple_of(place_ref[2 * index + 1] * width, width)
+        copies.append(
+            pltpu.make_async_copy(
+                piece_ref,
+                out_ref.at[pl.ds(row, part_rows), pl.ds(column, width)],
+                sems.at[index],
+            )
+        )
+    for copy in copies:
+        copy.start()
+    for copy in copies:
+        copy.wait()
+
+
+def assemble(pieces, places, shape):
+    anywhere = pl.BlockSpec(memory_space=pl.ANY)
+    return pl.pallas_call(
+        assemble_kernel,
+        out_shape=jax.ShapeDtypeStruct(shape, pieces[0].dtype),
+        in_specs=[pl.BlockSpec(memory_space=pltpu.SMEM)] + [anywhere] * len(pieces),
+        out_specs=anywhere,
+        scratch_shapes=[pltpu.SemaphoreType.DMA((len(pieces),))],
+        cost_estimate=pl.CostEstimate(
+            flops=0, bytes_accessed=4 * shape[0] * shape[1], transcendentals=0
+        ),
+    )(jnp.stack(places).astype(jnp.int32), *pieces)
 
 
 def return_output(out, outer, inner_parts, tp_parts):
     _, part_rows, width = out.shape
     per_tp = outer // tp_parts
-    edges = []
-    for src in range(outer):
-        for tp in range(tp_parts):
-            for dst in range(outer):
-                edges.append((src * tp_parts + tp, dst * tp_parts + src // per_tp, dst, tp, src % per_tp))
-    node = (lax.axis_index("seq") // inner_parts) * tp_parts + lax.axis_index("tp")
-    result = jnp.zeros((tp_parts * part_rows, per_tp * width), out.dtype)
-    for chosen in match_rounds(edges, outer * tp_parts, outer):
-        send, row, column = (np.zeros(outer * tp_parts, np.int32) for _ in range(3))
-        pairs = []
-        for source, target, block, row_part, column_part in chosen:
-            send[source], row[target], column[target] = block, row_part, column_part
-            for inner in range(inner_parts):
-                pairs.append(
-                    tuple(
-                        ((end // tp_parts) * inner_parts + inner) * tp_parts + end % tp_parts
-                        for end in (source, target)
-                    )
-                )
-        piece = lax.dynamic_index_in_dim(out, jnp.asarray(send)[node], axis=0, keepdims=False)
-        piece = lax.ppermute(piece, ("seq", "tp"), pairs)
-        result = lax.dynamic_update_slice(
-            result, piece, (jnp.asarray(row)[node] * part_rows, jnp.asarray(column)[node] * width)
-        )
-    return result
+    tp_place = lax.axis_index("tp")
+    outer_place = lax.axis_index("seq") // inner_parts
+    pieces, places = [], []
+    for far in range(tp_parts):
+        for near in range(per_tp):
+
+            def target(seq, tp):
+                src = seq // inner_parts
+                dst = (tp + far) % tp_parts * per_tp + (src % per_tp + near) % per_tp
+                return (dst * inner_parts + seq % inner_parts) * tp_parts + src // per_tp
+
+            pairs = [
+                (seq * tp_parts + tp, target(seq, tp))
+                for seq in range(outer * inner_parts)
+                for tp in range(tp_parts)
+            ]
+            block = (tp_place + far) % tp_parts * per_tp + (outer_place % per_tp + near) % per_tp
+            piece = lax.dynamic_index_in_dim(out, block, axis=0, keepdims=False)
+            pieces.append(lax.ppermute(piece, ("seq", "tp"), pairs))
+            places.append((outer_place // per_tp - far + tp_parts) % tp_parts)
+            places.append((outer_place % per_tp - near + per_tp) % per_tp)
+    return assemble(pieces, places, (tp_parts * part_rows, per_tp * width))
 
 
 def share_columns(features, outer, tp_parts):
     rows, cols = features.shape
-    groups = outer // tp_parts
-    blocks = features.reshape(rows, groups, tp_parts, cols // outer)
-    blocks = jnp.transpose(blocks, (2, 1, 0, 3))
-    blocks = lax.all_to_all(blocks, "tp", split_axis=0, concat_axis=0, tiled=True)
-    return blocks.reshape(outer, rows, -1)
+    per_tp = outer // tp_parts
+    tp_place = lax.axis_index("tp")
+    blocks = features.reshape(rows, per_tp, tp_parts, cols // outer)
+    held = []
+    for step in range(tp_parts):
+        piece = lax.dynamic_index_in_dim(blocks, (tp_place + step) % tp_parts, axis=2, keepdims=False)
+        piece = jnp.swapaxes(piece, 0, 1)
+        if step:
+            piece = lax.ppermute(piece, "tp", [(i, (i + step) % tp_parts) for i in range(tp_parts)])
+        held.append(piece)
+    return jnp.concatenate(held)
+
+
+def cross_outer(held, outer, inner_parts, tp_parts):
+    per_tp = outer // tp_parts
+    seq_parts = outer * inner_parts
+    tp_place = lax.axis_index("tp")
+    outer_place = lax.axis_index("seq") // inner_parts
+    arrived = []
+    for step in range(outer):
+        target = (outer_place + step) % outer
+        which = (tp_place - target // per_tp + tp_parts) % tp_parts * per_tp + target % per_tp
+        piece = lax.dynamic_index_in_dim(held, which, axis=0, keepdims=False)
+        if step:
+            far = step * inner_parts
+            piece = lax.ppermute(piece, "seq", [(i, (i + far) % seq_parts) for i in range(seq_parts)])
+        arrived.append(piece)
+    return jnp.stack(arrived)
 
 
 def share_over_tp(part, tp_parts):
@@ -97,42 +122,38 @@
     return pieces
 
 
-def project_kernel(tp_parts, place_ref, *refs):
+def project_kernel(place_ref, *refs):
     *share_refs, weight_ref, out_ref = refs
+    tp_parts = len(share_refs)
     seq_parts, _, chans, count = out_ref.shape
-    done = []
-    for first in range(0, len(share_refs), tp_parts):
-        outer, rows, width = share_refs[first].shape
-        sums = jnp.zeros((outer * rows, seq_parts * chans), jnp.float32)
-        for step in range(tp_parts):
-            which = lax.rem(place_ref[0] - step + tp_parts, tp_parts)
-            sums = sums + jnp.dot(
-                share_refs[first + step][...].reshape(outer * rows, width),
-                weight_ref[0, which],
-                preferred_element_type=jnp.float32,
-            )
-        done.append(sums.reshape(outer, rows, seq_parts * chans))
-    turned = jnp.concatenate(done, 1).reshape(count, seq_parts * chans).T.astype(out_ref.dtype)
+    outer, rows, width = share_refs[0].shape
+    sums = jnp.zeros((count, seq_parts * chans), jnp.float32)
+    for step, share_ref in enumerate(share_refs):
+        which = lax.rem(place_ref[0] - step + tp_parts, tp_parts)
+        left = [share_ref[lax.rem(place_ref[1] - src + outer, outer)] for src in range(outer)]
+        sums = sums + jnp.dot(
+            jnp.concatenate(left), weight_ref[0, which], preferred_element_type=jnp.float32
+        )
+    turned = sums.T.astype(out_ref.dtype)
     for seq in range(seq_parts):
         out_ref[seq, 0] = turned[seq * chans : (seq + 1) * chans]
 
 
-def project_in(chunks, weight, seq_parts):
-    tp_parts = len(chunks[0])
-    outer, rows, width = chunks[0][0].shape
+def project_in(pieces, weight, outer_place, seq_parts):
+    tp_parts = len(pieces)
+    outer, rows, width = pieces[0].shape
     streams, _, chan_tp = weight.shape
     weight = weight.reshape(streams, tp_parts, width, chan_tp)
     chans = chan_tp // seq_parts
-    count = outer * rows * len(chunks)
-    pieces = [piece for chunk in chunks for piece in chunk]
-    place = lax.axis_index("tp").astype(jnp.int32)[None]
+    count = outer * rows
+    place = jnp.stack([lax.axis_index("tp"), outer_place]).astype(jnp.int32)
     whole = pl.BlockSpec((outer, rows, width), lambda i, place: (0, 0, 0))
     return pl.pallas_call(
-        functools.partial(project_kernel, tp_parts),
+        project_kernel,
         grid_spec=pltpu.PrefetchScalarGridSpec(
             num_scalar_prefetch=1,
             grid=(streams,),
-            in_specs=[whole] * len(pieces)
+            in_specs=[whole] * tp_parts
             + [pl.BlockSpec((1, tp_parts, width, chan_tp), lambda i, place: (i, 0, 0, 0))],
             out_specs=pl.BlockSpec((seq_parts, 1, chans, count), lambda i, place: (0, i, 0, 0)),
         ),
@@ -140,7 +161,7 @@
         compiler_params=pltpu.CompilerParams(vmem_limit_bytes=56 * 2**20),
         cost_estimate=pl.CostEstimate(
             flops=2 * count * weight.size,
-            bytes_accessed=2 * (weight.size + len(pieces) * pieces[0].size)
+            bytes_accessed=2 * (weight.size + tp_parts * pieces[0].size)
             + 2 * streams * count * chan_tp,
             transcendentals=0,
         ),
@@ -177,29 +198,44 @@
 
 
 def conv_kernel(
-    outer, parts_ref, filter_ref, taps_ref, skip_ref, fwd_ref, bwd_ref, out_ref,
-    proj, query, inner, spec, filter_spec, product, back
+    outer, chunks, *refs
 ):
-    blocks, streams, chans, _ = parts_ref.shape
+    part_refs, refs = refs[:chunks], refs[chunks:]
+    filter_ref, taps_ref, skip_ref, fwd_ref, bwd_ref, out_ref, *refs = refs
+    proj, query, inner, spec, filter_spec, product, back = refs
+    blocks, streams, chans, _ = part_refs[0].shape
     rows = filter_ref.shape[2]
     inner_parts = blocks // outer
     taps_count = taps_ref.shape[1]
     lane = lax.broadcasted_iota(jnp.int32, (chans, rows), 1)
 
-    def add_up(index, stream, slot):
-        sums = jnp.zeros((chans, rows), jnp.float32)
-        column = pl.ds(pl.multiple_of(slot * rows, rows), rows)
-        for part in range(outer):
-            sums = sums + parts_ref[part * inner_parts + index % inner_parts, stream, :, column].astype(jnp.float32)
-        return sums
+    chunk_rows = rows // chunks
+
+    def add_up(inner_index, stream, group):
+        column = slice(group * rows, (group + 1) * rows)
+        sums = []
+        for part_ref in part_refs:
+            value = jnp.zeros((chans, rows), jnp.float32)
+            for part in range(outer):
+                value = value + part_ref[part * inner_parts + inner_index, stream, :, column].astype(jnp.float32)
+            sums.append(value)
+        for place in range(chunks):
+            block = sums[0]
+            for chunk, value in enumerate(sums):
+                shift = (chunk - place) * chunk_rows % rows
+                value = pltpu.roll(value, shift, 1) if shift else value
+                block = jnp.where(lane // chunk_rows == chunk, value, block)
+            proj[1 + (group * chunks + place) * inner_parts + inner_index, stream] = block
+
+    for group in range(outer // chunks):
+        for stream in range(streams):
+            each(inner_parts, functools.partial(add_up, stream=stream, group=group))
 
     for stream in range(streams):
         proj[0, stream] = jnp.zeros((chans, rows), jnp.float32)
 
     def first(index):
         filtered = []
-        for stream in range(streams):
-            proj[index + 1, stream] = add_up(index, stream, index // inner_parts)
         for stream in range(streams):
             now, past = proj[index + 1, stream], proj[index, stream]
             value = taps_ref[stream, 0] * now
@@ -274,18 +310,18 @@
 
 
 def convolve(parts, filter_blocks, taps, skip, outer, tp_parts):
-    blocks, streams, chans, _ = parts.shape
+    blocks, streams, chans, _ = parts[0].shape
     rows = filter_blocks.shape[2]
     forward, backward = tables(rows)
     wide = (blocks, chans, 2 * rows)
     narrow = (blocks, chans, rows)
     vmem = pl.BlockSpec(memory_space=pltpu.VMEM)
     return pl.pallas_call(
-        functools.partial(conv_kernel, outer),
+        functools.partial(conv_kernel, outer, len(parts)),
         out_shape=jax.ShapeDtypeStruct(
             (tp_parts, blocks // outer, chans, outer // tp_parts * rows), jnp.bfloat16
         ),
-        in_specs=[vmem] * 6,
+        in_specs=[vmem] * (5 + len(parts)),
         out_specs=vmem,
         scratch_shapes=[
             pltpu.VMEM((blocks + 1, streams, chans, rows), jnp.float32),
@@ -298,7 +334,7 @@
         ],
         compiler_params=pltpu.CompilerParams(vmem_limit_bytes=40 * 2**20),
         cost_estimate=pl.CostEstimate(flops=10**9, bytes_accessed=4 * 2**20, transcendentals=0),
-    )(parts, filter_blocks, taps, skip, jnp.asarray(forward), jnp.asarray(backward))
+    )(*parts, filter_blocks, taps, skip, jnp.asarray(forward), jnp.asarray(backward))
 
 
 def out_kernel(place_ref, gated_ref, weight_ref, out_ref):
@@ -350,24 +386,18 @@
 
     weight = lax.all_gather(in_proj, "seq", axis=1, tiled=True, axis_index_groups=inner_groups)
 
+    outer_place = position // inner_parts
     chunk_rows = rows // CHUNKS
     shared = [
         share_columns(features[index * chunk_rows : (index + 1) * chunk_rows], outer, tp_parts)
         for index in range(CHUNKS)
     ]
-    crossed = [
-        lax.all_to_all(
-            part, "seq", split_axis=0, concat_axis=0, tiled=True, axis_index_groups=outer_groups
-        )
-        for part in shared
-    ]
-    chunks = [share_over_tp(part, tp_parts) for part in crossed]
+    crossed = [cross_outer(part, outer, inner_parts, tp_parts) for part in shared]
 
     _, out_proj = lax.optimization_barrier((shared, out_proj))
     out_block = jnp.stack(share_over_tp(out_proj, tp_parts))
     out_weight = lax.all_gather(out_block, "seq", axis_index_groups=inner_groups)
 
-    _, long_filter = lax.optimization_barrier((crossed, long_filter))
     filter_blocks = lax.all_to_all(
         long_filter.T.reshape(seq_parts, chans, rows), "seq", split_axis=0, concat_axis=0, tiled=True
     )
@@ -375,10 +405,16 @@
     taps = jnp.broadcast_to(taps[..., None], taps.shape + (rows,))
     skip = lax.dynamic_slice_in_dim(skip_gain, position * chans, chans, axis=0)
     skip = jnp.broadcast_to(skip[:, None], (chans, rows))
-    chunks, filter_blocks, taps, skip = lax.optimization_barrier((chunks, filter_blocks, taps, skip))
-
-    partial = project_in(chunks, weight, seq_parts)
-    parts = lax.all_to_all(partial, "seq", split_axis=0, concat_axis=0, tiled=True)
+
+    parts = []
+    for index, part in enumerate(crossed):
+        pieces = share_over_tp(part, tp_parts)
+        if index + 1 == CHUNKS:
+            pieces, filter_blocks, taps, skip = lax.optimization_barrier(
+                (pieces, filter_blocks, taps, skip)
+            )
+        partial = project_in(pieces, weight, outer_place, seq_parts)
+        parts.append(lax.all_to_all(partial, "seq", split_axis=0, concat_axis=0, tiled=True))
 
     gated = convolve(parts, filter_blocks, taps, skip, outer, tp_parts)
     gated = jnp.broadcast_to(gated[:, None], (tp_parts, outer) + gated.shape[1:])

time: 204 us -> 252 us (1.24); the launches traced: 200 us -> 251 us
  waiting for transfers between devices: 36.1 us -> 102 us
  Pallas kernels: 15.4 us -> 55 us
  blocking collectives: 52.4 us -> 26.4 us
  local copies, waits for them, and re-layouts: 27.5 us -> 11.4 us
  between operations: 26.2 us -> 13.7 us
    ppermute x4 -> x12, waiting for transfers between devices: 0.01 us -> 57 us  [the longest x6 21.6 us: cross_outer(): lax.ppermute(piece, 'seq', [(i, (i + far) % seq_parts) for i in range(seq...]
    pallas_call x2 -> x4, Pallas kernels: 10.4 us -> 50.1 us  [the longest x1 33.6 us: assemble(): pl.pallas_call(assemble_kernel, out_shape=jax.ShapeDtypeStruct(shape, pie...]
    ppermute x3, waiting for transfers between devices: 5.1 us -> 30.3 us  [share_over_tp(): pieces.append(lax.ppermute(part, 'tp', pairs))]
    all_to_all x3 -> x1, waiting for transfers between devices: 18.3 us -> 0.01 us  [per_device(): lax.all_to_all(partial, 'seq', split_axis=0, concat_axis=0, tiled=True)]
    all_to_all x1, blocking collectives: 41.9 us -> 26.4 us  [per_device(): lax.all_to_all(partial, 'seq', split_axis=0, concat_axis=0, tiled=True)]
    dynamic_update_slice x4 -> x0, local copies, waits for them, and re-layouts: 13.3 us -> none  [return_output(): lax.dynamic_update_slice(result, piece, (jnp.asarray(row)[node] * part_ro...]
    all_to_all x1 -> x0, blocking collectives: 10.5 us -> none  [share_columns(): lax.all_to_all(blocks, 'tp', split_axis=0, concat_axis=0, tiled=True)]
    all_to_all x3 -> x1, starting transfers between devices: 16.3 us -> 6.31 us  [per_device(): lax.all_to_all(partial, 'seq', split_axis=0, concat_axis=0, tiled=True)]
  transfers between devices with their start and end apart: 14 -> 20, of which waited for: 6 -> 13; matrix products, arithmetic and copies ran while one was open for 11% -> 4% of each run, Pallas kernels for 5% -> 7%
where the time goes in v3:
time: 252 us; the launch traced here: 251 us
  waiting for transfers between devices  102 us (40%)
  Pallas kernels  55 us (22%)
  starting transfers between devices  39.1 us (16%)
  blocking collectives  26.4 us (10%)
  between operations  13.7 us (5%)
  local copies, waits for them, and re-layouts  11.4 us (5%)
  other arithmetic  3.34 us (1%)
    pallas_call x1, Pallas kernels, assemble(): pl.pallas_call(assemble_kernel, out_shape=jax.ShapeDtypeStruct(shape, pie...  33.6 us
    ppermute x3, waiting for transfers between devices, share_over_tp(): pieces.append(lax.ppermute(part, 'tp', pairs))  30.3 us
    all_to_all x1, blocking collectives, per_device(): lax.all_to_all(partial, 'seq', split_axis=0, concat_axis=0, tiled=True)  26.4 us
    ppermute x6, waiting for transfers between devices, cross_outer(): lax.ppermute(piece, 'seq', [(i, (i + far) % seq_parts) for i in range(seq...  21.6 us
    ppermute x4, waiting for transfers between devices, return_output(): pieces.append(lax.ppermute(piece, ('seq', 'tp'), pairs))  21.2 us
    all_to_all x1, waiting for transfers between devices, per_device(): lax.all_to_all(gated.reshape((-1,) + gated.shape[3:]), ('tp', 'seq'), spl...  14.5 us
    ppermute x2, waiting for transfers between devices, share_columns(): lax.ppermute(piece, 'tp', [(i, (i + step) % tp_parts) for i in range(tp_p...  14.2 us
    pallas_call x2, Pallas kernels, project_in(): pl.pallas_call(project_kernel, grid_spec=pltpu.PrefetchScalarGridSpec(num...  13.4 us
  transfers between devices with their start and end apart: 20, of which 13 were waited for; matrix products, arithmetic and copies ran while one was open for 4% of the time, Pallas kernels for 7%

profile of v3, /device:TPU:12, one launch (start us, length us, event | category | flops | bytes accessed | tf_op | source)
XLA Modules:
  0.0 251.4 jit_solution(17479892604153291273)
XLA Ops:
  7.9 13.4 %collective-permute-done.10 = bf16[512,512]{1,0:T(8,128)(2,1)S(1)} collective-permute-done((bf16[512,512]{1,0:T(8,128)(2,1)}, bf16[512,512]{1,0:T(8,128)(2,1)S(1)}, u32[]{:S(2)}, u32[]{:S(2)}) %collective-permute-start.10) | collective-permute-done | bytes 524320 | tf_op jit(solution)/shard_map/ppermute | solution.py:121
  27.4 6.6 %collective-permute-done = bf16[2,64,1024]{2,1,0:T(8,128)(2,1)S(1)} collective-permute-done((bf16[2,64,1024]{2,1,0:T(8,128)(2,1)S(1)}, bf16[2,64,1024]{2,1,0:T(8,128)(2,1)S(1)}, u32[]{:S(2)}, u32[]{:S(2)}) %collective-permute-start) | collective-permute-done | bytes 262176 | tf_op jit(solution)/shard_map/ppermute | solution.py:95
  34.7 2.5 collective-permute-start.2
  37.2 2.5 collective-permute-start.1
  39.7 6.0 %collective-permute-done.3 = bf16[64,1024]{1,0:T(8,128)(2,1)S(1)} collective-permute-done((bf16[64,1024]{1,0:T(8,128)(2,1)S(1)}, bf16[64,1024]{1,0:T(8,128)(2,1)S(1)}, u32[]{:S(2)}, u32[]{:S(2)}) %collective-permute-start.3) | collective-permute-done | bytes 131104 | tf_op jit(solution)/shard_map/ppermute | solution.py:112
  48.0 6.1 %all-to-all-start.1 = ((f32[16,32,128]{2,1,0:T(8,128)}), f32[16,32,128]{2,1,0:T(8,128)S(1)}, u32[]{:S(2)}, u32[]{:S(2)}) async-start(f32[16,32,128]{2,1,0:T(8,128)} %bitcast.28), calls=%async_computation.1 | async-start | bytes 524288 | tf_op jit(solution)/shard_map/all_to_all | solution.py:401
  54.8 4.8 %collective-permute-done.4.refs_1_ = bf16[4,64,1024]{2,1,0:T(8,128)(2,1)S(1)} collective-permute-done((bf16[4,64,1024]{2,1,0:T(8,128)(2,1)S(1)}, bf16[4,64,1024]{2,1,0:T(8,128)(2,1)S(1)}, u32[]{:S(2)}, u32[]{:S(2)}) %collective-permute-start.4) | collective-permute-done | bytes 524320 | tf_op jit(solution)/shard_map/ppermute | solution.py:121
  60.5 6.8 %shard_map.82 = bf16[16,3,32,256]{3,2,1,0:T(8,128)(2,1)} custom-call(s32[2]{0:T(128)} %pad_add_fusion.place_ref, bf16[4,64,1024]{2,1,0:T(8,128)(2,1)} %copy-done.4, bf16[4,64,1024]{2,1,0:T(8,128)(2,1)} %copy-done.7, bf16[3,2,1024,512]{3,2,1,0:T(8,128)(2,1)} %bitcast.62), custom_call_target="tpu_custom_call" | custom-call | flops 1610612736 | bytes 8126464 | tf_op jit(solution)/shard_map/pallas_call | solution.py:151
  67.2 6.3 %all-to-all-start = ((bf16[16,3,32,256]{3,2,1,0:T(8,128)(2,1)}), bf16[16,3,32,256]{3,2,1,0:T(8,128)(2,1)S(1)}, u32[]{:S(2)}, u32[]{:S(2)}) async-start(bf16[16,3,32,256]{3,2,1,0:T(8,128)(2,1)} %shard_map.82), calls=%async_computation | async-start | bytes 1572864 | tf_op jit(solution)/shard_map/all_to_all | solution.py:417
  74.5 7.6 %collective-permute-done.5 = bf16[2,64,1024]{2,1,0:T(8,128)(2,1)S(1)} collective-permute-done((bf16[2,64,1024]{2,1,0:T(8,128)(2,1)S(1)}, bf16[2,64,1024]{2,1,0:T(8,128)(2,1)S(1)}, u32[]{:S(2)}, u32[]{:S(2)}) %collective-permute-start.5) | collective-permute-done | bytes 262176 | tf_op jit(solution)/shard_map/ppermute | solution.py:95
  82.7 2.5 %collective-permute-start.7 = (bf16[64,1024]{1,0:T(8,128)(2,1)S(1)}, bf16[64,1024]{1,0:T(8,128)(2,1)S(1)}, u32[]{:S(2)}, u32[]{:S(2)}) collective-permute-start(bf16[64,1024]{1,0:T(8,128)(2,1)S(1)} %get-tuple-element.25), channel_id=1, source_target_pairs={{0,16},{2,18},{4,20},{6,22},{8,24},{10,26},{12,28},{14,30},{16,0},... | collective-permute-start | bytes 393224 | tf_op jit(solution)/shard_map/ppermute | solution.py:112
  87.7 14.3 %collective-permute-done.8 = bf16[64,1024]{1,0:T(8,128)(2,1)S(1)} collective-permute-done((bf16[64,1024]{1,0:T(8,128)(2,1)S(1)}, bf16[64,1024]{1,0:T(8,128)(2,1)S(1)}, u32[]{:S(2)}, u32[]{:S(2)}) %collective-permute-start.8) | collective-permute-done | bytes 131104 | tf_op jit(solution)/shard_map/ppermute | solution.py:112
  104.0 12.1 %collective-permute-done.9.refs_1_ = bf16[4,64,1024]{2,1,0:T(8,128)(2,1)S(1)} collective-permute-done((bf16[4,64,1024]{2,1,0:T(8,128)(2,1)S(1)}, bf16[4,64,1024]{2,1,0:T(8,128)(2,1)S(1)}, u32[]{:S(2)}, u32[]{:S(2)}) %collective-permute-start.9) | collective-permute-done | bytes 524320 | tf_op jit(solution)/shard_map/ppermute | solution.py:121
  116.9 6.6 %shard_map.83 = bf16[16,3,32,256]{3,2,1,0:T(8,128)(2,1)} custom-call(s32[2]{0:T(128)} %pad_add_fusion.place_ref, bf16[4,64,1024]{2,1,0:T(8,128)(2,1)} %copy-done.3, bf16[4,64,1024]{2,1,0:T(8,128)(2,1)} %copy-done.6, bf16[3,2,1024,512]{3,2,1,0:T(8,128)(2,1)} %bitcast.63), custom_call_target="tpu_custom_call" | custom-call | flops 1610612736 | bytes 8126464 | tf_op jit(solution)/shard_map/pallas_call | solution.py:151
  123.5 26.4 %all_to_all.20.refs_1_ = bf16[16,3,32,256]{3,2,1,0:T(8,128)(2,1)S(1)} all-to-all(bf16[16,3,32,256]{3,2,1,0:T(8,128)(2,1)} %shard_map.83), channel_id=1, replica_groups=mesh['seq'=16,'tp'=2] {'seq'}, dimensions={0} | all-to-all | bytes 1572864 | tf_op jit(solution)/shard_map/all_to_all | solution.py:417
  149.9 3.1 %shard_map.84 = bf16[2,4,32,256]{3,2,1,0:T(8,128)(2,1)S(1)} custom-call(bf16[16,3,32,256]{3,2,1,0:T(8,128)(2,1)S(1)} %all-to-all-done.refs_0_, bf16[16,3,32,256]{3,2,1,0:T(8,128)(2,1)S(1)} %all_to_all.20.refs_1_, f32[16,32,128]{2,1,0:T(8,128)S(1)} %all-to-all-done.1.refs_2_, f32[3,3,32,128]{3,2,1,0:T(8,128)S(1)} %broadcast_in_dim.9.refs_3_, ...), custom_call_target="tpu_custom_call" | custom-call | flops 1000000000 | bytes 4194304 | tf_op jit(solution)/shard_map/pallas_call | solution.py:319
  153.9 4.2 %all-to-all-start.3 = ((bf16[32,32,256]{2,1,0:T(8,128)(2,1)}), bf16[32,32,256]{2,1,0:T(8,128)(2,1)S(1)}, u32[]{:S(2)}, u32[]{:S(2)}) async-start(bf16[32,32,256]{2,1,0:T(8,128)(2,1)} %bitcast.29), calls=%async_computation.3 | async-start | bytes 1048576 | tf_op jit(solution)/shard_map/all_to_all | solution.py:421
  158.2 14.5 %all-to-all-done.3 = bf16[32,32,256]{2,1,0:T(8,128)(2,1)S(1)} async-done(((bf16[32,32,256]{2,1,0:T(8,128)(2,1)}), bf16[32,32,256]{2,1,0:T(8,128)(2,1)S(1)}, u32[]{:S(2)}, u32[]{:S(2)}) %all-to-all-start.3) | async-done | bytes 524320 | tf_op jit(solution)/shard_map/all_to_all | solution.py:421
  173.7 4.9 %shard_map.85 = bf16[256,2048]{1,0:T(8,128)(2,1)} custom-call(s32[1]{0:T(128)} %bitcast.4.place_ref, bf16[2,256,512]{2,1,0:T(8,128)(2,1)} %bitcast.66, bf16[4,2,512,512]{3,2,1,0:T(8,128)(2,1)} %bitcast.64), custom_call_target="tpu_custom_call" | custom-call | flops 1073741824 | bytes 5767168 | tf_op jit(solution)/shard_map/pallas_call | solution.py:354
  179.9 4.0 %collective-permute-start.11 = (bf16[64,2048]{1,0:T(8,128)(2,1)S(1)}, bf16[64,2048]{1,0:T(8,128)(2,1)S(1)}, u32[]{:S(2)}, u32[]{:S(2)}) collective-permute-start(bf16[64,2048]{1,0:T(8,128)(2,1)S(1)} %get-tuple-element.20), channel_id=1, source_target_pairs={{0,0},{1,16},{2,2},{3,18},{4,4},{5,20},{6,6},{7,22},{8,8},{9,24},{... | collective-permute-start | bytes 786440 | tf_op jit(solution)/shard_map/ppermute | solution.py:79
  185.4 3.0 %collective-permute-start.14 = (bf16[64,2048]{1,0:T(8,128)(2,1)S(1)}, bf16[64,2048]{1,0:T(8,128)(2,1)S(1)}, u32[]{:S(2)}, u32[]{:S(2)}) collective-permute-start(bf16[64,2048]{1,0:T(8,128)(2,1)S(1)} %get-tuple-element.17), channel_id=1, source_target_pairs={{0,24},{1,8},{2,26},{3,10},{4,28},{5,12},{6,30},{7,14},{8,16},{9,0... | collective-permute-start | bytes 786440 | tf_op jit(solution)/shard_map/ppermute | solution.py:79
  189.0 11.5 %collective-permute-done.11.refs_0_ = bf16[64,2048]{1,0:T(8,128)(2,1)S(1)} collective-permute-done((bf16[64,2048]{1,0:T(8,128)(2,1)S(1)}, bf16[64,2048]{1,0:T(8,128)(2,1)S(1)}, u32[]{:S(2)}, u32[]{:S(2)}) %collective-permute-start.11) | collective-permute-done | bytes 262176 | tf_op jit(solution)/shard_map/ppermute | solution.py:79
  200.5 7.2 %collective-permute-done.12.refs_1_ = bf16[64,2048]{1,0:T(8,128)(2,1)S(1)} collective-permute-done((bf16[64,2048]{1,0:T(8,128)(2,1)S(1)}, bf16[64,2048]{1,0:T(8,128)(2,1)S(1)}, u32[]{:S(2)}, u32[]{:S(2)}) %collective-permute-start.12) | collective-permute-done | bytes 262176 | tf_op jit(solution)/shard_map/ppermute | solution.py:79
  210.9 33.6 %shard_map.86 = bf16[128,4096]{1,0:T(8,128)(2,1)} custom-call(s32[8]{0:T(128)} %stack.68.place_ref, bf16[64,2048]{1,0:T(8,128)(2,1)} %copy-done.8, bf16[64,2048]{1,0:T(8,128)(2,1)} %copy-done.9, bf16[64,2048]{1,0:T(8,128)(2,1)} %copy-done.10, bf16[64,2048]{1,0:T(8,128)(2,1)} %copy-done.11), custom_call_target="tpu_custom_call" | custom-call | bytes 2097152 | tf_op jit(solution)/shard_map/pallas_call | solution.py:46
  (73 shorter events, 27.0 us)
Async XLA Ops:
  6.5 97.4 %copy-start = (f32[3,3,512]{2,1,0:T(4,128)S(1)}, f32[3,3,512]{2,1,0:T(4,128)}, u32[]{:S(2)}) copy-start(f32[3,3,512]{2,1,0:T(4,128)} %param.10) | copy-start | bytes 55300
  6.5 53.1 %all-gather.4.cloned.1.call-start = ((), (), s32[]{:S(2)}) async-start(), calls=%async_computation.4 | async-start | bytes 7864320 | tf_op jit(solution)/shard_map/all_gather | solution.py:387
  7.3 166.4 %all-gather.6.cloned.1.call-start = ((), (), s32[]{:S(2)}) async-start(), calls=%async_computation.5 | async-start | bytes 5242880 | tf_op jit(solution)/shard_map/all_gather | solution.py:399
  7.3 13.9 %collective-permute-start.10 = (bf16[512,512]{1,0:T(8,128)(2,1)}, bf16[512,512]{1,0:T(8,128)(2,1)S(1)}, u32[]{:S(2)}, u32[]{:S(2)}) collective-permute-start(bf16[512,512]{1,0:T(8,128)(2,1)} %param.13), channel_id=1, source_target_pairs={{0,1},{1,0},{2,3},{3,2},{4,5},{5,4},{6,7},{7,6},{8,9},{9,8},{10,11... | collective-permute-start | bytes 1572872 | tf_op jit(solution)/shard_map/ppermute | solution.py:121
  24.3 22.9 %copy-start.12 = (f32[128,512]{1,0:T(8,128)S(1)}, f32[128,512]{1,0:T(8,128)}, u32[]{:S(2)}) copy-start(f32[128,512]{1,0:T(8,128)} %param.11) | copy-start | bytes 786436
  26.7 7.3 %collective-permute-start = (bf16[2,64,1024]{2,1,0:T(8,128)(2,1)S(1)}, bf16[2,64,1024]{2,1,0:T(8,128)(2,1)S(1)}, u32[]{:S(2)}, u32[]{:S(2)}) collective-permute-start(bf16[2,64,1024]{2,1,0:T(8,128)(2,1)S(1)} %bitcast.72), channel_id=1, source_target_pairs={{0,1},{1,0},{2,3},{3,2},{4,5},{5,4},{6,7},{7,6},{8,9},{9,8},{10,11... | collective-permute-start | bytes 786440 | tf_op jit(solution)/shard_map/ppermute | solution.py:95
  34.2 11.5 %collective-permute-start.3 = (bf16[64,1024]{1,0:T(8,128)(2,1)S(1)}, bf16[64,1024]{1,0:T(8,128)(2,1)S(1)}, u32[]{:S(2)}, u32[]{:S(2)}) collective-permute-start(bf16[64,1024]{1,0:T(8,128)(2,1)S(1)} %get-tuple-element.32), channel_id=1, source_target_pairs={{0,24},{2,26},{4,28},{6,30},{8,0},{10,2},{12,4},{14,6},{16,8},{18,... | collective-permute-start | bytes 393224 | tf_op jit(solution)/shard_map/ppermute | solution.py:112
  34.7 11.0 %collective-permute-start.2 = (bf16[64,1024]{1,0:T(8,128)(2,1)S(1)}, bf16[64,1024]{1,0:T(8,128)(2,1)S(1)}, u32[]{:S(2)}, u32[]{:S(2)}) collective-permute-start(bf16[64,1024]{1,0:T(8,128)(2,1)S(1)} %get-tuple-element.31), channel_id=1, source_target_pairs={{0,16},{2,18},{4,20},{6,22},{8,24},{10,26},{12,28},{14,30},{16,0},... | collective-permute-start | bytes 393224 | tf_op jit(solution)/shard_map/ppermute | solution.py:112
  37.2 9.3 %collective-permute-start.1 = (bf16[64,1024]{1,0:T(8,128)(2,1)S(1)}, bf16[64,1024]{1,0:T(8,128)(2,1)S(1)}, u32[]{:S(2)}, u32[]{:S(2)}) collective-permute-start(bf16[64,1024]{1,0:T(8,128)(2,1)S(1)} %get-tuple-element.30), channel_id=1, source_target_pairs={{0,8},{2,10},{4,12},{6,14},{8,16},{10,18},{12,20},{14,22},{16,24},... | collective-permute-start | bytes 393224 | tf_op jit(solution)/shard_map/ppermute | solution.py:112
  46.5 13.1 %collective-permute-start.4 = (bf16[4,64,1024]{2,1,0:T(8,128)(2,1)S(1)}, bf16[4,64,1024]{2,1,0:T(8,128)(2,1)S(1)}, u32[]{:S(2)}, u32[]{:S(2)}) collective-permute-start(bf16[4,64,1024]{2,1,0:T(8,128)(2,1)S(1)} %pad_maximum_fusion.3.refs_0_), channel_id=1, source_target_pairs={{0,1},{1,0},{2,3},{3,2},{4,5},{5,4},{6,7},{7,6},{8,9},{9,8},{10,11... | collective-permute-start | bytes 1572872 | tf_op jit(solution)/shard_map/ppermute | solution.py:121
  48.0 19.2 %all-to-all-start.1 = ((f32[16,32,128]{2,1,0:T(8,128)}), f32[16,32,128]{2,1,0:T(8,128)S(1)}, u32[]{:S(2)}, u32[]{:S(2)}) async-start(f32[16,32,128]{2,1,0:T(8,128)} %bitcast.28), calls=%async_computation.1 | async-start | bytes 524288 | tf_op jit(solution)/shard_map/all_to_all | solution.py:401
  67.2 56.3 %all-to-all-start = ((bf16[16,3,32,256]{3,2,1,0:T(8,128)(2,1)}), bf16[16,3,32,256]{3,2,1,0:T(8,128)(2,1)S(1)}, u32[]{:S(2)}, u32[]{:S(2)}) async-start(bf16[16,3,32,256]{3,2,1,0:T(8,128)(2,1)} %shard_map.82), calls=%async_computation | async-start | bytes 1572864 | tf_op jit(solution)/shard_map/all_to_all | solution.py:417
  73.7 8.4 %collective-permute-start.5 = (bf16[2,64,1024]{2,1,0:T(8,128)(2,1)S(1)}, bf16[2,64,1024]{2,1,0:T(8,128)(2,1)S(1)}, u32[]{:S(2)}, u32[]{:S(2)}) collective-permute-start(bf16[2,64,1024]{2,1,0:T(8,128)(2,1)S(1)} %bitcast.73), channel_id=1, source_target_pairs={{0,1},{1,0},{2,3},{3,2},{4,5},{5,4},{6,7},{7,6},{8,9},{9,8},{10,11... | collective-permute-start | bytes 786440 | tf_op jit(solution)/shard_map/ppermute | solution.py:95
  82.3 19.7 %collective-permute-start.8 = (bf16[64,1024]{1,0:T(8,128)(2,1)S(1)}, bf16[64,1024]{1,0:T(8,128)(2,1)S(1)}, u32[]{:S(2)}, u32[]{:S(2)}) collective-permute-start(bf16[64,1024]{1,0:T(8,128)(2,1)S(1)} %get-tuple-element.26), channel_id=1, source_target_pairs={{0,24},{2,26},{4,28},{6,30},{8,0},{10,2},{12,4},{14,6},{16,8},{18,... | collective-permute-start | bytes 393224 | tf_op jit(solution)/shard_map/ppermute | solution.py:112
  82.7 19.3 %collective-permute-start.7 = (bf16[64,1024]{1,0:T(8,128)(2,1)S(1)}, bf16[64,1024]{1,0:T(8,128)(2,1)S(1)}, u32[]{:S(2)}, u32[]{:S(2)}) collective-permute-start(bf16[64,1024]{1,0:T(8,128)(2,1)S(1)} %get-tuple-element.25), channel_id=1, source_target_pairs={{0,16},{2,18},{4,20},{6,22},{8,24},{10,26},{12,28},{14,30},{16,0},... | collective-permute-start | bytes 393224 | tf_op jit(solution)/shard_map/ppermute | solution.py:112
  85.3 17.2 %collective-permute-start.6 = (bf16[64,1024]{1,0:T(8,128)(2,1)S(1)}, bf16[64,1024]{1,0:T(8,128)(2,1)S(1)}, u32[]{:S(2)}, u32[]{:S(2)}) collective-permute-start(bf16[64,1024]{1,0:T(8,128)(2,1)S(1)} %get-tuple-element.24), channel_id=1, source_target_pairs={{0,8},{2,10},{4,12},{6,14},{8,16},{10,18},{12,20},{14,22},{16,24},... | collective-permute-start | bytes 393224 | tf_op jit(solution)/shard_map/ppermute | solution.py:112
  102.5 13.5 %collective-permute-start.9 = (bf16[4,64,1024]{2,1,0:T(8,128)(2,1)S(1)}, bf16[4,64,1024]{2,1,0:T(8,128)(2,1)S(1)}, u32[]{:S(2)}, u32[]{:S(2)}) collective-permute-start(bf16[4,64,1024]{2,1,0:T(8,128)(2,1)S(1)} %pad_maximum_fusion.4.refs_0_), channel_id=1, source_target_pairs={{0,1},{1,0},{2,3},{3,2},{4,5},{5,4},{6,7},{7,6},{8,9},{9,8},{10,11... | collective-permute-start | bytes 1572872 | tf_op jit(solution)/shard_map/ppermute | solution.py:121
  116.9 33.1 %copy-start.1 = (f32[256,256]{1,0:T(8,128)S(1)}, f32[256,256]{1,0:T(8,128)}, u32[]{:S(2)}) copy-start(f32[256,256]{1,0:T(8,128)} %constant.290.clone.refs_6_) | copy-start | bytes 786436
  116.9 33.1 %copy-start.2 = (f32[128,256]{1,0:T(8,128)S(1)}, f32[128,256]{1,0:T(8,128)}, u32[]{:S(2)}) copy-start(f32[128,256]{1,0:T(8,128)} %constant.289.clone.refs_5_) | copy-start | bytes 393220
  153.9 18.8 %all-to-all-start.3 = ((bf16[32,32,256]{2,1,0:T(8,128)(2,1)}), bf16[32,32,256]{2,1,0:T(8,128)(2,1)S(1)}, u32[]{:S(2)}, u32[]{:S(2)}) async-start(bf16[32,32,256]{2,1,0:T(8,128)(2,1)} %bitcast.29), calls=%async_computation.3 | async-start | bytes 1048576 | tf_op jit(solution)/shard_map/all_to_all | solution.py:421
  179.9 20.6 %collective-permute-start.11 = (bf16[64,2048]{1,0:T(8,128)(2,1)S(1)}, bf16[64,2048]{1,0:T(8,128)(2,1)S(1)}, u32[]{:S(2)}, u32[]{:S(2)}) collective-permute-start(bf16[64,2048]{1,0:T(8,128)(2,1)S(1)} %get-tuple-element.20), channel_id=1, source_target_pairs={{0,0},{1,16},{2,2},{3,18},{4,4},{5,20},{6,6},{7,22},{8,8},{9,24},{... | collective-permute-start | bytes 786440 | tf_op jit(solution)/shard_map/ppermute | solution.py:79
  183.9 23.8 %collective-permute-start.12 = (bf16[64,2048]{1,0:T(8,128)(2,1)S(1)}, bf16[64,2048]{1,0:T(8,128)(2,1)S(1)}, u32[]{:S(2)}, u32[]{:S(2)}) collective-permute-start(bf16[64,2048]{1,0:T(8,128)(2,1)S(1)} %get-tuple-element.19), channel_id=1, source_target_pairs={{0,8},{1,24},{2,10},{3,26},{4,12},{5,28},{6,14},{7,30},{8,0},{9,16... | collective-permute-start | bytes 786440 | tf_op jit(solution)/shard_map/ppermute | solution.py:79
  185.4 22.4 %collective-permute-start.13 = (bf16[64,2048]{1,0:T(8,128)(2,1)S(1)}, bf16[64,2048]{1,0:T(8,128)(2,1)S(1)}, u32[]{:S(2)}, u32[]{:S(2)}) collective-permute-start(bf16[64,2048]{1,0:T(8,128)(2,1)S(1)} %get-tuple-element.18), channel_id=1, source_target_pairs={{0,16},{1,0},{2,18},{3,2},{4,20},{5,4},{6,22},{7,6},{8,24},{9,8},{... | collective-permute-start | bytes 786440 | tf_op jit(solution)/shard_map/ppermute | solution.py:79
  185.4 24.8 %collective-permute-start.14 = (bf16[64,2048]{1,0:T(8,128)(2,1)S(1)}, bf16[64,2048]{1,0:T(8,128)(2,1)S(1)}, u32[]{:S(2)}, u32[]{:S(2)}) collective-permute-start(bf16[64,2048]{1,0:T(8,128)(2,1)S(1)} %get-tuple-element.17), channel_id=1, source_target_pairs={{0,24},{1,8},{2,26},{3,10},{4,28},{5,12},{6,30},{7,14},{8,16},{9,0... | collective-permute-start | bytes 786440 | tf_op jit(solution)/shard_map/ppermute | solution.py:79
  (9 other events, 60.7 us)
Sparse Core Ops, SparseCore 0:
  8.9 47.4 all-gather.3
  58.0 42.8 all-gather.5

commit v4 on v3

--- a/solution.py
+++ b/solution.py
@@ -22,33 +22,26 @@
 
 
 def assemble_kernel(place_ref, *refs):
-    *piece_refs, out_ref, sems = refs
-    part_rows, width = piece_refs[0].shape
-    copies = []
+    *piece_refs, out_ref = refs
     for index, piece_ref in enumerate(piece_refs):
-        row = pl.multiple_of(place_ref[2 * index] * part_rows, part_rows)
-        column = pl.multiple_of(place_ref[2 * index + 1] * width, width)
-        copies.append(
-            pltpu.make_async_copy(
-                piece_ref,
-                out_ref.at[pl.ds(row, part_rows), pl.ds(column, width)],
-                sems.at[index],
-            )
-        )
-    for copy in copies:
-        copy.start()
-    for copy in copies:
-        copy.wait()
+
+        @pl.when(pl.program_id(0) == index)
+        def _():
+            out_ref[...] = piece_ref[...]
 
 
 def assemble(pieces, places, shape):
-    anywhere = pl.BlockSpec(memory_space=pl.ANY)
     return pl.pallas_call(
         assemble_kernel,
+        grid_spec=pltpu.PrefetchScalarGridSpec(
+            num_scalar_prefetch=1,
+            grid=(len(pieces),),
+            in_specs=[pl.BlockSpec(memory_space=pltpu.VMEM)] * len(pieces),
+            out_specs=pl.BlockSpec(
+                pieces[0].shape, lambda i, place: (place[2 * i], place[2 * i + 1])
+            ),
+        ),
         out_shape=jax.ShapeDtypeStruct(shape, pieces[0].dtype),
-        in_specs=[pl.BlockSpec(memory_space=pltpu.SMEM)] + [anywhere] * len(pieces),
-        out_specs=anywhere,
-        scratch_shapes=[pltpu.SemaphoreType.DMA((len(pieces),))],
         cost_estimate=pl.CostEstimate(
             flops=0, bytes_accessed=4 * shape[0] * shape[1], transcendentals=0
         ),
@@ -111,7 +104,7 @@
             far = step * inner_parts
             piece = lax.ppermute(piece, "seq", [(i, (i + far) % seq_parts) for i in range(seq_parts)])
         arrived.append(piece)
-    return jnp.stack(arrived)
+    return arrived
 
 
 def share_over_tp(part, tp_parts):
@@ -126,27 +119,28 @@
     *share_refs, weight_ref, out_ref = refs
     tp_parts = len(share_refs)
     seq_parts, _, chans, count = out_ref.shape
-    outer, rows, width = share_refs[0].shape
+    width = share_refs[0].shape[2]
     sums = jnp.zeros((count, seq_parts * chans), jnp.float32)
     for step, share_ref in enumerate(share_refs):
         which = lax.rem(place_ref[0] - step + tp_parts, tp_parts)
-        left = [share_ref[lax.rem(place_ref[1] - src + outer, outer)] for src in range(outer)]
         sums = sums + jnp.dot(
-            jnp.concatenate(left), weight_ref[0, which], preferred_element_type=jnp.float32
+            share_ref[...].reshape(count, width),
+            weight_ref[0, which],
+            preferred_element_type=jnp.float32,
         )
     turned = sums.T.astype(out_ref.dtype)
     for seq in range(seq_parts):
         out_ref[seq, 0] = turned[seq * chans : (seq + 1) * chans]
 
 
-def project_in(pieces, weight, outer_place, seq_parts):
+def project_in(pieces, weight, seq_parts):
     tp_parts = len(pieces)
     outer, rows, width = pieces[0].shape
     streams, _, chan_tp = weight.shape
     weight = weight.reshape(streams, tp_parts, width, chan_tp)
     chans = chan_tp // seq_parts
     count = outer * rows
-    place = jnp.stack([lax.axis_index("tp"), outer_place]).astype(jnp.int32)
+    place = lax.axis_index("tp").astype(jnp.int32)[None]
     whole = pl.BlockSpec((outer, rows, width), lambda i, place: (0, 0, 0))
     return pl.pallas_call(
         project_kernel,
@@ -209,25 +203,18 @@
     taps_count = taps_ref.shape[1]
     lane = lax.broadcasted_iota(jnp.int32, (chans, rows), 1)
 
-    chunk_rows = rows // chunks
+    depth = outer // chunks
 
     def add_up(inner_index, stream, group):
-        column = slice(group * rows, (group + 1) * rows)
-        sums = []
-        for part_ref in part_refs:
-            value = jnp.zeros((chans, rows), jnp.float32)
-            for part in range(outer):
-                value = value + part_ref[part * inner_parts + inner_index, stream, :, column].astype(jnp.float32)
-            sums.append(value)
-        for place in range(chunks):
-            block = sums[0]
-            for chunk, value in enumerate(sums):
-                shift = (chunk - place) * chunk_rows % rows
-                value = pltpu.roll(value, shift, 1) if shift else value
-                block = jnp.where(lane // chunk_rows == chunk, value, block)
-            proj[1 + (group * chunks + place) * inner_parts + inner_index, stream] = block
-
-    for group in range(outer // chunks):
+        value = jnp.zeros((chans, rows), jnp.float32)
+        for part in range(outer):
+            slot = (part - group) % outer
+            column = slice(slot % depth * rows, (slot % depth + 1) * rows)
+            source = part_refs[slot // depth]
+            value = value + source[part * inner_parts + inner_index, stream, :, column].astype(jnp.float32)
+        proj[1 + group * inner_parts + inner_index, stream] = value
+
+    for group in range(outer):
         for stream in range(streams):
             each(inner_parts, functools.partial(add_up, stream=stream, group=group))
 
@@ -386,15 +373,12 @@
 
     weight = lax.all_gather(in_proj, "seq", axis=1, tiled=True, axis_index_groups=inner_groups)
 
-    outer_place = position // inner_parts
-    chunk_rows = rows // CHUNKS
-    shared = [
-        share_columns(features[index * chunk_rows : (index + 1) * chunk_rows], outer, tp_parts)
-        for index in range(CHUNKS)
-    ]
-    crossed = [cross_outer(part, outer, inner_parts, tp_parts) for part in shared]
-
-    _, out_proj = lax.optimization_barrier((shared, out_proj))
+    held = share_columns(features, outer, tp_parts)
+    held, out_proj, long_filter = lax.optimization_barrier((held, out_proj, long_filter))
+    arrived = cross_outer(held, outer, inner_parts, tp_parts)
+    depth = outer // CHUNKS
+    crossed = [jnp.stack(arrived[index * depth : (index + 1) * depth]) for index in range(CHUNKS)]
+
     out_block = jnp.stack(share_over_tp(out_proj, tp_parts))
     out_weight = lax.all_gather(out_block, "seq", axis_index_groups=inner_groups)
 
@@ -413,7 +397,7 @@
             pieces, filter_blocks, taps, skip = lax.optimization_barrier(
                 (pieces, filter_blocks, taps, skip)
             )
-        partial = project_in(pieces, weight, outer_place, seq_parts)
+        partial = project_in(pieces, weight, seq_parts)
         parts.append(lax.all_to_all(partial, "seq", split_axis=0, concat_axis=0, tiled=True))
 
     gated = convolve(parts, filter_blocks, taps, skip, outer, tp_parts)

time: 252 us -> 224 us (0.89)
  Pallas kernels: 55 us -> 23 us
  waiting for transfers between devices: 102 us -> 114 us
  starting transfers between devices: 39.1 us -> 32.5 us
    pallas_call x1, Pallas kernels: 33.6 us -> 3.43 us  [assemble(): pl.pallas_call(assemble_kernel, grid_spec=pltpu.PrefetchScalarGridSpec(nu...]
    ppermute x6 -> x3, waiting for transfers between devices: 21.6 us -> 36.4 us  [cross_outer(): lax.ppermute(piece, 'seq', [(i, (i + far) % seq_parts) for i in range(seq...]
    ppermute x6 -> x3, starting transfers between devices: 10.8 us -> 4.56 us  [cross_outer(): lax.ppermute(piece, 'seq', [(i, (i + far) % seq_parts) for i in range(seq...]
    ppermute x2 -> x1, waiting for transfers between devices: 14.2 us -> 12.9 us  [share_columns(): lax.ppermute(piece, 'tp', [(i, (i + step) % tp_parts) for i in range(tp_p...]
  transfers between devices with their start and end apart: 20 -> 16, of which waited for: 13 -> 11; matrix products, arithmetic and copies ran while one was open for 4% -> 5% of each run, Pallas kernels for 7% -> 7%
where the time goes in v4:
time: 224 us; the launch traced here: 223 us
  waiting for transfers between devices  114 us (51%)
  starting transfers between devices  32.5 us (15%)
  blocking collectives  26.7 us (12%)
  Pallas kernels  23 us (10%)
  between operations  13.9 us (6%)
  local copies, waits for them, and re-layouts  12.5 us (6%)
    ppermute x3, waiting for transfers between devices, cross_outer(): lax.ppermute(piece, 'seq', [(i, (i + far) % seq_parts) for i in range(seq...  36.4 us
    ppermute x3, waiting for transfers between devices, share_over_tp(): pieces.append(lax.ppermute(part, 'tp', pairs))  27.8 us
    all_to_all x1, blocking collectives, per_device(): lax.all_to_all(partial, 'seq', split_axis=0, concat_axis=0, tiled=True)  26.7 us
    ppermute x4, waiting for transfers between devices, return_output(): pieces.append(lax.ppermute(piece, ('seq', 'tp'), pairs))  21.2 us
    all_to_all x1, waiting for transfers between devices, per_device(): lax.all_to_all(gated.reshape((-1,) + gated.shape[3:]), ('tp', 'seq'), spl...  14.5 us
    ppermute x1, waiting for transfers between devices, share_columns(): lax.ppermute(piece, 'tp', [(i, (i + step) % tp_parts) for i in range(tp_p...  12.9 us
    pallas_call x2, Pallas kernels, project_in(): pl.pallas_call(project_kernel, grid_spec=pltpu.PrefetchScalarGridSpec(num...  11.7 us
    ppermute x4, starting transfers between devices, return_output(): pieces.append(lax.ppermute(piece, ('seq', 'tp'), pairs))  8.46 us
  transfers between devices with their start and end apart: 16, of which 11 were waited for; matrix products, arithmetic and copies ran while one was open for 5% of the time, Pallas kernels for 7%

profile of v4, /device:TPU:12, one launch (start us, length us, event | category | flops | bytes accessed | tf_op | source)
XLA Modules:
  0.0 223.4 jit_solution(8837197814644067070)
XLA Ops:
  9.2 2.2 constant_dynamic-slice_fusion.3
  12.5 12.9 %collective-permute-done = bf16[2,128,1024]{2,1,0:T(8,128)(2,1)S(1)} collective-permute-done((bf16[2,128,1024]{2,1,0:T(8,128)(2,1)S(1)}, bf16[2,128,1024]{2,1,0:T(8,128)(2,1)S(1)}, u32[]{:S(2)}, u32[]{:S(2)}) %collective-permute-start) | collective-permute-done | bytes 524320 | tf_op jit(solution)/shard_map/ppermute | solution.py:88
  26.1 12.4 %collective-permute-done.6 = bf16[512,512]{1,0:T(8,128)(2,1)S(1)} collective-permute-done((bf16[512,512]{1,0:T(8,128)(2,1)S(1)}, bf16[512,512]{1,0:T(8,128)(2,1)S(1)}, u32[]{:S(2)}, u32[]{:S(2)}) %collective-permute-start.6) | collective-permute-done | bytes 524320 | tf_op jit(solution)/shard_map/ppermute | solution.py:114
  41.6 4.9 %collective-permute-done.1 = bf16[128,1024]{1,0:T(8,128)(2,1)S(1)} collective-permute-done((bf16[128,1024]{1,0:T(8,128)(2,1)S(1)}, bf16[128,1024]{1,0:T(8,128)(2,1)S(1)}, u32[]{:S(2)}, u32[]{:S(2)}) %collective-permute-start.1) | collective-permute-done | bytes 262176 | tf_op jit(solution)/shard_map/ppermute | solution.py:105
  47.9 6.3 %all-to-all-start.1 = ((f32[16,32,128]{2,1,0:T(8,128)}), f32[16,32,128]{2,1,0:T(8,128)S(1)}, u32[]{:S(2)}, u32[]{:S(2)}) async-start(f32[16,32,128]{2,1,0:T(8,128)} %bitcast.17), calls=%async_computation.1 | async-start | bytes 524288 | tf_op jit(solution)/shard_map/all_to_all | solution.py:385
  54.2 3.6 %collective-permute-done.2.refs_1_ = bf16[2,128,1024]{2,1,0:T(8,128)(2,1)S(1)} collective-permute-done((bf16[2,128,1024]{2,1,0:T(8,128)(2,1)S(1)}, bf16[2,128,1024]{2,1,0:T(8,128)(2,1)S(1)}, u32[]{:S(2)}, u32[]{:S(2)}) %collective-permute-start.2) | collective-permute-done | bytes 524320 | tf_op jit(solution)/shard_map/ppermute | solution.py:114
  58.7 5.8 %shard_map.82 = bf16[16,3,32,256]{3,2,1,0:T(8,128)(2,1)} custom-call(s32[1]{0:T(128)} %bitcast.4.place_ref, bf16[2,128,1024]{2,1,0:T(8,128)(2,1)} %copy-done.4, bf16[2,128,1024]{2,1,0:T(8,128)(2,1)} %copy-done.6, bf16[3,2,1024,512]{3,2,1,0:T(8,128)(2,1)} %bitcast.42), custom_call_target="tpu_custom_call" | custom-call | flops 1610612736 | bytes 8126464 | tf_op jit(solution)/shard_map/pallas_call | solution.py:145
  64.5 6.3 %all-to-all-start = ((bf16[16,3,32,256]{3,2,1,0:T(8,128)(2,1)}), bf16[16,3,32,256]{3,2,1,0:T(8,128)(2,1)S(1)}, u32[]{:S(2)}, u32[]{:S(2)}) async-start(bf16[16,3,32,256]{3,2,1,0:T(8,128)(2,1)} %shard_map.82), calls=%async_computation | async-start | bytes 1572864 | tf_op jit(solution)/shard_map/all_to_all | solution.py:401
  70.9 2.8 %collective-permute-start.3 = (bf16[128,1024]{1,0:T(8,128)(2,1)S(1)}, bf16[128,1024]{1,0:T(8,128)(2,1)S(1)}, u32[]{:S(2)}, u32[]{:S(2)}) collective-permute-start(bf16[128,1024]{1,0:T(8,128)(2,1)S(1)} %get-tuple-element.25), channel_id=1, source_target_pairs={{0,16},{2,18},{4,20},{6,22},{8,24},{10,26},{12,28},{14,30},{16,0},... | collective-permute-start | bytes 786440 | tf_op jit(solution)/shard_map/ppermute | solution.py:105
  73.7 28.4 %collective-permute-done.4 = bf16[128,1024]{1,0:T(8,128)(2,1)S(1)} collective-permute-done((bf16[128,1024]{1,0:T(8,128)(2,1)S(1)}, bf16[128,1024]{1,0:T(8,128)(2,1)S(1)}, u32[]{:S(2)}, u32[]{:S(2)}) %collective-permute-start.4) | collective-permute-done | bytes 262176 | tf_op jit(solution)/shard_map/ppermute | solution.py:105
  102.1 3.2 %collective-permute-done.3 = bf16[128,1024]{1,0:T(8,128)(2,1)S(1)} collective-permute-done((bf16[128,1024]{1,0:T(8,128)(2,1)S(1)}, bf16[128,1024]{1,0:T(8,128)(2,1)S(1)}, u32[]{:S(2)}, u32[]{:S(2)}) %collective-permute-start.3) | collective-permute-done | bytes 262176 | tf_op jit(solution)/shard_map/ppermute | solution.py:105
  107.0 11.8 %collective-permute-done.5.refs_1_ = bf16[2,128,1024]{2,1,0:T(8,128)(2,1)S(1)} collective-permute-done((bf16[2,128,1024]{2,1,0:T(8,128)(2,1)S(1)}, bf16[2,128,1024]{2,1,0:T(8,128)(2,1)S(1)}, u32[]{:S(2)}, u32[]{:S(2)}) %collective-permute-start.5) | collective-permute-done | bytes 524320 | tf_op jit(solution)/shard_map/ppermute | solution.py:114
  119.6 5.9 %shard_map.83 = bf16[16,3,32,256]{3,2,1,0:T(8,128)(2,1)} custom-call(s32[1]{0:T(128)} %bitcast.4.place_ref, bf16[2,128,1024]{2,1,0:T(8,128)(2,1)} %copy-done.3, bf16[2,128,1024]{2,1,0:T(8,128)(2,1)} %copy-done.5, bf16[3,2,1024,512]{3,2,1,0:T(8,128)(2,1)} %bitcast.43), custom_call_target="tpu_custom_call" | custom-call | flops 1610612736 | bytes 8126464 | tf_op jit(solution)/shard_map/pallas_call | solution.py:145
  125.5 26.7 %all_to_all.20.refs_1_ = bf16[16,3,32,256]{3,2,1,0:T(8,128)(2,1)S(1)} all-to-all(bf16[16,3,32,256]{3,2,1,0:T(8,128)(2,1)} %shard_map.83), channel_id=1, replica_groups=mesh['seq'=16,'tp'=2] {'seq'}, dimensions={0} | all-to-all | bytes 1572864 | tf_op jit(solution)/shard_map/all_to_all | solution.py:401
  152.2 2.9 %shard_map.84 = bf16[2,4,32,256]{3,2,1,0:T(8,128)(2,1)S(1)} custom-call(bf16[16,3,32,256]{3,2,1,0:T(8,128)(2,1)S(1)} %all-to-all-done.refs_0_, bf16[16,3,32,256]{3,2,1,0:T(8,128)(2,1)S(1)} %all_to_all.20.refs_1_, f32[16,32,128]{2,1,0:T(8,128)S(1)} %all-to-all-done.1.refs_2_, f32[3,3,32,128]{3,2,1,0:T(8,128)S(1)} %broadcast_in_dim.9.refs_3_, ...), custom_call_target="tpu_custom_call" | custom-call | flops 1000000000 | bytes 4194304 | tf_op jit(solution)/shard_map/pallas_call | solution.py:306
  156.0 4.3 %all-to-all-start.3 = ((bf16[32,32,256]{2,1,0:T(8,128)(2,1)}), bf16[32,32,256]{2,1,0:T(8,128)(2,1)S(1)}, u32[]{:S(2)}, u32[]{:S(2)}) async-start(bf16[32,32,256]{2,1,0:T(8,128)(2,1)} %bitcast.18), calls=%async_computation.3 | async-start | bytes 1048576 | tf_op jit(solution)/shard_map/all_to_all | solution.py:405
  160.4 14.5 %all-to-all-done.3 = bf16[32,32,256]{2,1,0:T(8,128)(2,1)S(1)} async-done(((bf16[32,32,256]{2,1,0:T(8,128)(2,1)}), bf16[32,32,256]{2,1,0:T(8,128)(2,1)S(1)}, u32[]{:S(2)}, u32[]{:S(2)}) %all-to-all-start.3) | async-done | bytes 524320 | tf_op jit(solution)/shard_map/all_to_all | solution.py:405
  175.9 4.9 %shard_map.85 = bf16[256,2048]{1,0:T(8,128)(2,1)} custom-call(s32[1]{0:T(128)} %bitcast.4.place_ref, bf16[2,256,512]{2,1,0:T(8,128)(2,1)} %bitcast.46, bf16[4,2,512,512]{3,2,1,0:T(8,128)(2,1)} %bitcast.44), custom_call_target="tpu_custom_call" | custom-call | flops 1073741824 | bytes 5767168 | tf_op jit(solution)/shard_map/pallas_call | solution.py:341
  182.1 4.0 %collective-permute-start.7 = (bf16[64,2048]{1,0:T(8,128)(2,1)S(1)}, bf16[64,2048]{1,0:T(8,128)(2,1)S(1)}, u32[]{:S(2)}, u32[]{:S(2)}) collective-permute-start(bf16[64,2048]{1,0:T(8,128)(2,1)S(1)} %get-tuple-element.24), channel_id=1, source_target_pairs={{0,0},{1,16},{2,2},{3,18},{4,4},{5,20},{6,6},{7,22},{8,8},{9,24},{... | collective-permute-start | bytes 786440 | tf_op jit(solution)/shard_map/ppermute | solution.py:72
  187.6 3.0 %collective-permute-start.10 = (bf16[64,2048]{1,0:T(8,128)(2,1)S(1)}, bf16[64,2048]{1,0:T(8,128)(2,1)S(1)}, u32[]{:S(2)}, u32[]{:S(2)}) collective-permute-start(bf16[64,2048]{1,0:T(8,128)(2,1)S(1)} %get-tuple-element.21), channel_id=1, source_target_pairs={{0,24},{1,8},{2,26},{3,10},{4,28},{5,12},{6,30},{7,14},{8,16},{9,0... | collective-permute-start | bytes 786440 | tf_op jit(solution)/shard_map/ppermute | solution.py:72
  191.2 11.5 %collective-permute-done.7.refs_0_ = bf16[64,2048]{1,0:T(8,128)(2,1)S(1)} collective-permute-done((bf16[64,2048]{1,0:T(8,128)(2,1)S(1)}, bf16[64,2048]{1,0:T(8,128)(2,1)S(1)}, u32[]{:S(2)}, u32[]{:S(2)}) %collective-permute-start.7) | collective-permute-done | bytes 262176 | tf_op jit(solution)/shard_map/ppermute | solution.py:72
  202.7 7.2 %collective-permute-done.8.refs_1_ = bf16[64,2048]{1,0:T(8,128)(2,1)S(1)} collective-permute-done((bf16[64,2048]{1,0:T(8,128)(2,1)S(1)}, bf16[64,2048]{1,0:T(8,128)(2,1)S(1)}, u32[]{:S(2)}, u32[]{:S(2)}) %collective-permute-start.8) | collective-permute-done | bytes 262176 | tf_op jit(solution)/shard_map/ppermute | solution.py:72
  209.9 2.4 %collective-permute-done.10.refs_3_ = bf16[64,2048]{1,0:T(8,128)(2,1)S(1)} collective-permute-done((bf16[64,2048]{1,0:T(8,128)(2,1)S(1)}, bf16[64,2048]{1,0:T(8,128)(2,1)S(1)}, u32[]{:S(2)}, u32[]{:S(2)}) %collective-permute-start.10) | collective-permute-done | bytes 262176 | tf_op jit(solution)/shard_map/ppermute | solution.py:72
  213.1 3.4 %shard_map.86 = bf16[128,4096]{1,0:T(8,128)(2,1)} custom-call(s32[8]{0:T(128)} %stack.48.place_ref, bf16[64,2048]{1,0:T(8,128)(2,1)} %copy-done.8, bf16[64,2048]{1,0:T(8,128)(2,1)} %copy-done.9, bf16[64,2048]{1,0:T(8,128)(2,1)} %copy-done.10, bf16[64,2048]{1,0:T(8,128)(2,1)} %copy-done.11), custom_call_target="tpu_custom_call" | custom-call | bytes 2097152 | tf_op jit(solution)/shard_map/pallas_call | solution.py:34
  (60 shorter events, 18.3 us)
Async XLA Ops:
  6.5 100.4 %copy-start = (f32[3,3,512]{2,1,0:T(4,128)S(1)}, f32[3,3,512]{2,1,0:T(4,128)}, u32[]{:S(2)}) copy-start(f32[3,3,512]{2,1,0:T(4,128)} %param.10) | copy-start | bytes 55300
  6.5 51.3 %all-gather.4.cloned.1.call-start = ((), (), s32[]{:S(2)}) async-start(), calls=%async_computation.4 | async-start | bytes 7864320 | tf_op jit(solution)/shard_map/all_gather | solution.py:374
  7.3 168.6 %all-gather.6.cloned.1.call-start = ((), (), s32[]{:S(2)}) async-start(), calls=%async_computation.5 | async-start | bytes 5242880 | tf_op jit(solution)/shard_map/all_gather | solution.py:383
  9.2 16.3 %copy-start.7 = (bf16[512,512]{1,0:T(8,128)(2,1)S(1)}, bf16[512,512]{1,0:T(8,128)(2,1)}, u32[]{:S(2)}) copy-start(bf16[512,512]{1,0:T(8,128)(2,1)} %param.13) | copy-start | bytes 1572868
  11.7 13.7 %collective-permute-start = (bf16[2,128,1024]{2,1,0:T(8,128)(2,1)S(1)}, bf16[2,128,1024]{2,1,0:T(8,128)(2,1)S(1)}, u32[]{:S(2)}, u32[]{:S(2)}) collective-permute-start(bf16[2,128,1024]{2,1,0:T(8,128)(2,1)S(1)} %bitcast.49), channel_id=1, source_target_pairs={{0,1},{1,0},{2,3},{3,2},{4,5},{5,4},{6,7},{7,6},{8,9},{9,8},{10,11... | collective-permute-start | bytes 1572872 | tf_op jit(solution)/shard_map/ppermute | solution.py:88
  25.4 21.7 %copy-start.12 = (f32[128,512]{1,0:T(8,128)S(1)}, f32[128,512]{1,0:T(8,128)}, u32[]{:S(2)}) copy-start(f32[128,512]{1,0:T(8,128)} %param.11) | copy-start | bytes 786436
  25.5 13.0 %collective-permute-start.6 = (bf16[512,512]{1,0:T(8,128)(2,1)S(1)}, bf16[512,512]{1,0:T(8,128)(2,1)S(1)}, u32[]{:S(2)}, u32[]{:S(2)}) collective-permute-start(bf16[512,512]{1,0:T(8,128)(2,1)S(1)} %copy-done.7), channel_id=1, source_target_pairs={{0,1},{1,0},{2,3},{3,2},{4,5},{5,4},{6,7},{7,6},{8,9},{9,8},{10,11... | collective-permute-start | bytes 1572872 | tf_op jit(solution)/shard_map/ppermute | solution.py:114
  39.9 6.5 %collective-permute-start.1 = (bf16[128,1024]{1,0:T(8,128)(2,1)S(1)}, bf16[128,1024]{1,0:T(8,128)(2,1)S(1)}, u32[]{:S(2)}, u32[]{:S(2)}) collective-permute-start(bf16[128,1024]{1,0:T(8,128)(2,1)S(1)} %get-tuple-element.27), channel_id=1, source_target_pairs={{0,8},{2,10},{4,12},{6,14},{8,16},{10,18},{12,20},{14,22},{16,24},... | collective-permute-start | bytes 786440 | tf_op jit(solution)/shard_map/ppermute | solution.py:105
  46.5 11.3 %copy-start.4 = (bf16[2,128,1024]{2,1,0:T(8,128)(2,1)}, bf16[2,128,1024]{2,1,0:T(8,128)(2,1)S(1)}, u32[]{:S(2)}) copy-start(bf16[2,128,1024]{2,1,0:T(8,128)(2,1)S(1)} %pad_maximum_fusion.2.refs_0_) | copy-start | bytes 1572868
  46.5 11.3 %collective-permute-start.2 = (bf16[2,128,1024]{2,1,0:T(8,128)(2,1)S(1)}, bf16[2,128,1024]{2,1,0:T(8,128)(2,1)S(1)}, u32[]{:S(2)}, u32[]{:S(2)}) collective-permute-start(bf16[2,128,1024]{2,1,0:T(8,128)(2,1)S(1)} %pad_maximum_fusion.2.refs_0_), channel_id=1, source_target_pairs={{0,1},{1,0},{2,3},{3,2},{4,5},{5,4},{6,7},{7,6},{8,9},{9,8},{10,11... | collective-permute-start | bytes 1572872 | tf_op jit(solution)/shard_map/ppermute | solution.py:114
  47.9 16.5 %all-to-all-start.1 = ((f32[16,32,128]{2,1,0:T(8,128)}), f32[16,32,128]{2,1,0:T(8,128)S(1)}, u32[]{:S(2)}, u32[]{:S(2)}) async-start(f32[16,32,128]{2,1,0:T(8,128)} %bitcast.17), calls=%async_computation.1 | async-start | bytes 524288 | tf_op jit(solution)/shard_map/all_to_all | solution.py:385
  64.5 61.1 %all-to-all-start = ((bf16[16,3,32,256]{3,2,1,0:T(8,128)(2,1)}), bf16[16,3,32,256]{3,2,1,0:T(8,128)(2,1)S(1)}, u32[]{:S(2)}, u32[]{:S(2)}) async-start(bf16[16,3,32,256]{3,2,1,0:T(8,128)(2,1)} %shard_map.82), calls=%async_computation | async-start | bytes 1572864 | tf_op jit(solution)/shard_map/all_to_all | solution.py:401
  70.7 31.3 %collective-permute-start.4 = (bf16[128,1024]{1,0:T(8,128)(2,1)S(1)}, bf16[128,1024]{1,0:T(8,128)(2,1)S(1)}, u32[]{:S(2)}, u32[]{:S(2)}) collective-permute-start(bf16[128,1024]{1,0:T(8,128)(2,1)S(1)} %get-tuple-element.26), channel_id=1, source_target_pairs={{0,24},{2,26},{4,28},{6,30},{8,0},{10,2},{12,4},{14,6},{16,8},{18,... | collective-permute-start | bytes 786440 | tf_op jit(solution)/shard_map/ppermute | solution.py:105
  70.9 34.3 %collective-permute-start.3 = (bf16[128,1024]{1,0:T(8,128)(2,1)S(1)}, bf16[128,1024]{1,0:T(8,128)(2,1)S(1)}, u32[]{:S(2)}, u32[]{:S(2)}) collective-permute-start(bf16[128,1024]{1,0:T(8,128)(2,1)S(1)} %get-tuple-element.25), channel_id=1, source_target_pairs={{0,16},{2,18},{4,20},{6,22},{8,24},{10,26},{12,28},{14,30},{16,0},... | collective-permute-start | bytes 786440 | tf_op jit(solution)/shard_map/ppermute | solution.py:105
  105.3 13.7 %copy-start.3 = (bf16[2,128,1024]{2,1,0:T(8,128)(2,1)}, bf16[2,128,1024]{2,1,0:T(8,128)(2,1)S(1)}, u32[]{:S(2)}) copy-start(bf16[2,128,1024]{2,1,0:T(8,128)(2,1)S(1)} %pad_maximum_fusion.3.refs_0_) | copy-start | bytes 1572868
  105.3 13.5 %collective-permute-start.5 = (bf16[2,128,1024]{2,1,0:T(8,128)(2,1)S(1)}, bf16[2,128,1024]{2,1,0:T(8,128)(2,1)S(1)}, u32[]{:S(2)}, u32[]{:S(2)}) collective-permute-start(bf16[2,128,1024]{2,1,0:T(8,128)(2,1)S(1)} %pad_maximum_fusion.3.refs_0_), channel_id=1, source_target_pairs={{0,1},{1,0},{2,3},{3,2},{4,5},{5,4},{6,7},{7,6},{8,9},{9,8},{10,11... | collective-permute-start | bytes 1572872 | tf_op jit(solution)/shard_map/ppermute | solution.py:114
  119.6 32.6 %copy-start.1 = (f32[256,256]{1,0:T(8,128)S(1)}, f32[256,256]{1,0:T(8,128)}, u32[]{:S(2)}) copy-start(f32[256,256]{1,0:T(8,128)} %constant.238.clone.refs_6_) | copy-start | bytes 786436
  119.6 32.6 %copy-start.2 = (f32[128,256]{1,0:T(8,128)S(1)}, f32[128,256]{1,0:T(8,128)}, u32[]{:S(2)}) copy-start(f32[128,256]{1,0:T(8,128)} %constant.237.clone.refs_5_) | copy-start | bytes 393220
  156.0 18.9 %all-to-all-start.3 = ((bf16[32,32,256]{2,1,0:T(8,128)(2,1)}), bf16[32,32,256]{2,1,0:T(8,128)(2,1)S(1)}, u32[]{:S(2)}, u32[]{:S(2)}) async-start(bf16[32,32,256]{2,1,0:T(8,128)(2,1)} %bitcast.18), calls=%async_computation.3 | async-start | bytes 1048576 | tf_op jit(solution)/shard_map/all_to_all | solution.py:405
  182.1 20.6 %collective-permute-start.7 = (bf16[64,2048]{1,0:T(8,128)(2,1)S(1)}, bf16[64,2048]{1,0:T(8,128)(2,1)S(1)}, u32[]{:S(2)}, u32[]{:S(2)}) collective-permute-start(bf16[64,2048]{1,0:T(8,128)(2,1)S(1)} %get-tuple-element.24), channel_id=1, source_target_pairs={{0,0},{1,16},{2,2},{3,18},{4,4},{5,20},{6,6},{7,22},{8,8},{9,24},{... | collective-permute-start | bytes 786440 | tf_op jit(solution)/shard_map/ppermute | solution.py:72
  186.1 23.9 %collective-permute-start.8 = (bf16[64,2048]{1,0:T(8,128)(2,1)S(1)}, bf16[64,2048]{1,0:T(8,128)(2,1)S(1)}, u32[]{:S(2)}, u32[]{:S(2)}) collective-permute-start(bf16[64,2048]{1,0:T(8,128)(2,1)S(1)} %get-tuple-element.23), channel_id=1, source_target_pairs={{0,8},{1,24},{2,10},{3,26},{4,12},{5,28},{6,14},{7,30},{8,0},{9,16... | collective-permute-start | bytes 786440 | tf_op jit(solution)/shard_map/ppermute | solution.py:72
  187.6 22.4 %collective-permute-start.9 = (bf16[64,2048]{1,0:T(8,128)(2,1)S(1)}, bf16[64,2048]{1,0:T(8,128)(2,1)S(1)}, u32[]{:S(2)}, u32[]{:S(2)}) collective-permute-start(bf16[64,2048]{1,0:T(8,128)(2,1)S(1)} %get-tuple-element.22), channel_id=1, source_target_pairs={{0,16},{1,0},{2,18},{3,2},{4,20},{5,4},{6,22},{7,6},{8,24},{9,8},{... | collective-permute-start | bytes 786440 | tf_op jit(solution)/shard_map/ppermute | solution.py:72
  187.6 24.8 %collective-permute-start.10 = (bf16[64,2048]{1,0:T(8,128)(2,1)S(1)}, bf16[64,2048]{1,0:T(8,128)(2,1)S(1)}, u32[]{:S(2)}, u32[]{:S(2)}) collective-permute-start(bf16[64,2048]{1,0:T(8,128)(2,1)S(1)} %get-tuple-element.21), channel_id=1, source_target_pairs={{0,24},{1,8},{2,26},{3,10},{4,28},{5,12},{6,30},{7,14},{8,16},{9,0... | collective-permute-start | bytes 786440 | tf_op jit(solution)/shard_map/ppermute | solution.py:72
  202.7 9.7 %copy-start.8 = (bf16[64,2048]{1,0:T(8,128)(2,1)}, bf16[64,2048]{1,0:T(8,128)(2,1)S(1)}, u32[]{:S(2)}) copy-start(bf16[64,2048]{1,0:T(8,128)(2,1)S(1)} %collective-permute-done.7.refs_0_) | copy-start | bytes 786436
  (5 other events, 7.3 us)
Sparse Core Ops, SparseCore 0:
  8.9 47.4 all-gather.3
  58.0 42.9 all-gather.5

commit v5 on v4

--- a/solution.py
+++ b/solution.py
@@ -12,6 +12,7 @@
 HIGHEST = lax.Precision.HIGHEST
 UNROLL = 16
 CHUNKS = 2
+HEAVY = 30
 
 
 def outer_factor(seq_parts, tp_parts):
@@ -42,6 +43,7 @@
             ),
         ),
         out_shape=jax.ShapeDtypeStruct(shape, pieces[0].dtype),
+        compiler_params=pltpu.CompilerParams(vmem_limit_bytes=4 * 2**20),
         cost_estimate=pl.CostEstimate(
             flops=0, bytes_accessed=4 * shape[0] * shape[1], transcendentals=0
         ),
@@ -79,11 +81,16 @@
     rows, cols = features.shape
     per_tp = outer // tp_parts
     tp_place = lax.axis_index("tp")
-    blocks = features.reshape(rows, per_tp, tp_parts, cols // outer)
+    width = cols // outer
     held = []
     for step in range(tp_parts):
-        piece = lax.dynamic_index_in_dim(blocks, (tp_place + step) % tp_parts, axis=2, keepdims=False)
-        piece = jnp.swapaxes(piece, 0, 1)
+        which = (tp_place + step) % tp_parts
+        piece = jnp.stack(
+            [
+                lax.dynamic_slice_in_dim(features, (group * tp_parts + which) * width, width, axis=1)
+                for group in range(per_tp)
+            ]
+        )
         if step:
             piece = lax.ppermute(piece, "tp", [(i, (i + step) % tp_parts) for i in range(tp_parts)])
         held.append(piece)
@@ -154,7 +161,7 @@
         out_shape=jax.ShapeDtypeStruct((seq_parts, streams, chans, count), jnp.bfloat16),
         compiler_params=pltpu.CompilerParams(vmem_limit_bytes=56 * 2**20),
         cost_estimate=pl.CostEstimate(
-            flops=2 * count * weight.size,
+            flops=HEAVY * 2 * count * weight.size,
             bytes_accessed=2 * (weight.size + tp_parts * pieces[0].size)
             + 2 * streams * count * chan_tp,
             transcendentals=0,
@@ -374,13 +381,10 @@
     weight = lax.all_gather(in_proj, "seq", axis=1, tiled=True, axis_index_groups=inner_groups)
 
     held = share_columns(features, outer, tp_parts)
-    held, out_proj, long_filter = lax.optimization_barrier((held, out_proj, long_filter))
+    held, long_filter = lax.optimization_barrier((held, long_filter))
     arrived = cross_outer(held, outer, inner_parts, tp_parts)
     depth = outer // CHUNKS
     crossed = [jnp.stack(arrived[index * depth : (index + 1) * depth]) for index in range(CHUNKS)]
-
-    out_block = jnp.stack(share_over_tp(out_proj, tp_parts))
-    out_weight = lax.all_gather(out_block, "seq", axis_index_groups=inner_groups)
 
     filter_blocks = lax.all_to_all(
         long_filter.T.reshape(seq_parts, chans, rows), "seq", split_axis=0, concat_axis=0, tiled=True
@@ -394,11 +398,14 @@
     for index, part in enumerate(crossed):
         pieces = share_over_tp(part, tp_parts)
         if index + 1 == CHUNKS:
-            pieces, filter_blocks, taps, skip = lax.optimization_barrier(
-                (pieces, filter_blocks, taps, skip)
+            pieces, out_proj, filter_blocks, taps, skip = lax.optimization_barrier(
+                (pieces, out_proj, filter_blocks, taps, skip)
             )
         partial = project_in(pieces, weight, seq_parts)
         parts.append(lax.all_to_all(partial, "seq", split_axis=0, concat_axis=0, tiled=True))
+
+    out_block = jnp.stack(share_over_tp(out_proj, tp_parts))
+    out_weight = lax.all_gather(out_block, "seq", axis_index_groups=inner_groups)
 
     gated = convolve(parts, filter_blocks, taps, skip, outer, tp_parts)
     gated = jnp.broadcast_to(gated[:, None], (tp_parts, outer) + gated.shape[1:])

time: 224 us -> 210 us (0.938); the launches traced: 223 us -> 206 us
  waiting for transfers between devices: 114 us -> 94.3 us
  starting transfers between devices: 32.5 us -> 44.1 us
  local copies, waits for them, and re-layouts: 12.5 us -> 6.51 us
    ppermute x3, waiting for transfers between devices: 36.4 us -> 17.4 us  [cross_outer(): lax.ppermute(piece, 'seq', [(i, (i + far) % seq_parts) for i in range(seq...]
    ppermute x3, waiting for transfers between devices: 27.8 us -> 14.4 us  [share_over_tp(): pieces.append(lax.ppermute(part, 'tp', pairs))]
    all_to_all x1, waiting for transfers between devices: 0.01 us -> 13.1 us  [per_device(): lax.all_to_all(partial, 'seq', split_axis=0, concat_axis=0, tiled=True)]
    all_to_all x1, starting transfers between devices: 6.27 us -> 14.2 us  [per_device(): lax.all_to_all(partial, 'seq', split_axis=0, concat_axis=0, tiled=True)]
    ppermute x4, waiting for transfers between devices: 21.2 us -> 15.2 us  [return_output(): pieces.append(lax.ppermute(piece, ('seq', 'tp'), pairs))]
    all_to_all x1, waiting for transfers between devices: 0.01 us -> 5.75 us  [per_device(): lax.all_to_all(long_filter.T.reshape(seq_parts, chans, rows), 'seq', spli...]
    unnamed x28 -> x16, local copies, waits for them, and re-layouts: 2.78 us -> 0.04 us
  transfers between devices with their start and end apart: 16 -> 16, of which waited for: 11 -> 11; matrix products, arithmetic and copies ran while one was open for 5% -> 3% of each run, Pallas kernels for 7% -> 7%
where the time goes in v5:
time: 210 us; the launch traced here: 206 us
  waiting for transfers between devices  94.3 us (45%)
  starting transfers between devices  44.1 us (21%)
  blocking collectives  24.9 us (12%)
  Pallas kernels  21.7 us (10%)
  between operations  13.7 us (7%)
  local copies, waits for them, and re-layouts  6.51 us (3%)
    all_to_all x1, blocking collectives, per_device(): lax.all_to_all(partial, 'seq', split_axis=0, concat_axis=0, tiled=True)  24.9 us
    ppermute x3, waiting for transfers between devices, cross_outer(): lax.ppermute(piece, 'seq', [(i, (i + far) % seq_parts) for i in range(seq...  17.4 us
    ppermute x4, waiting for transfers between devices, return_output(): pieces.append(lax.ppermute(piece, ('seq', 'tp'), pairs))  15.2 us
    all_to_all x1, waiting for transfers between devices, per_device(): lax.all_to_all(gated.reshape((-1,) + gated.shape[3:]), ('tp', 'seq'), spl...  14.5 us
    ppermute x3, waiting for transfers between devices, share_over_tp(): pieces.append(lax.ppermute(part, 'tp', pairs))  14.4 us
    all_to_all x1, starting transfers between devices, per_device(): lax.all_to_all(partial, 'seq', split_axis=0, concat_axis=0, tiled=True)  14.2 us
    ppermute x1, waiting for transfers between devices, share_columns(): lax.ppermute(piece, 'tp', [(i, (i + step) % tp_parts) for i in range(tp_p...  13.2 us
    all_to_all x1, waiting for transfers between devices, per_device(): lax.all_to_all(partial, 'seq', split_axis=0, concat_axis=0, tiled=True)  13.1 us
  transfers between devices with their start and end apart: 16, of which 11 were waited for; matrix products, arithmetic and copies ran while one was open for 3% of the time, Pallas kernels for 7%

profile of v5, /device:TPU:12, one launch (start us, length us, event | category | flops | bytes accessed | tf_op | source)
XLA Modules:
  0.0 206.4 jit_solution(15292935159125583851)
XLA Ops:
  9.3 13.2 %collective-permute-done = bf16[2,128,1024]{2,1,0:T(8,128)(2,1)S(1)} collective-permute-done((bf16[2,128,1024]{2,1,0:T(8,128)(2,1)S(1)}, bf16[2,128,1024]{2,1,0:T(8,128)(2,1)S(1)}, u32[]{:S(2)}, u32[]{:S(2)}) %collective-permute-start) | collective-permute-done | bytes 524320 | tf_op jit(solution)/shard_map/ppermute | solution.py:95
  22.6 2.7 %collective-permute-start.3 = (bf16[128,1024]{1,0:T(8,128)(2,1)S(1)}, bf16[128,1024]{1,0:T(8,128)(2,1)S(1)}, u32[]{:S(2)}, u32[]{:S(2)}) collective-permute-start(bf16[128,1024]{1,0:T(8,128)(2,1)S(1)} %get-tuple-element.25), channel_id=1, source_target_pairs={{0,16},{2,18},{4,20},{6,22},{8,24},{10,26},{12,28},{14,30},{16,0},... | collective-permute-start | bytes 786440 | tf_op jit(solution)/shard_map/ppermute | solution.py:112
  25.7 15.4 %collective-permute-done.3 = bf16[128,1024]{1,0:T(8,128)(2,1)S(1)} collective-permute-done((bf16[128,1024]{1,0:T(8,128)(2,1)S(1)}, bf16[128,1024]{1,0:T(8,128)(2,1)S(1)}, u32[]{:S(2)}, u32[]{:S(2)}) %collective-permute-start.3) | collective-permute-done | bytes 262176 | tf_op jit(solution)/shard_map/ppermute | solution.py:112
  42.6 7.1 %all-to-all-start.1 = ((f32[16,32,128]{2,1,0:T(8,128)}), f32[16,32,128]{2,1,0:T(8,128)S(1)}, u32[]{:S(2)}, u32[]{:S(2)}) async-start(f32[16,32,128]{2,1,0:T(8,128)} %bitcast.17), calls=%async_computation.1 | async-start | bytes 524288 | tf_op jit(solution)/shard_map/all_to_all | solution.py:389
  52.1 5.7 %all-to-all-done.1.refs_2_ = f32[16,32,128]{2,1,0:T(8,128)S(1)} async-done(((f32[16,32,128]{2,1,0:T(8,128)}), f32[16,32,128]{2,1,0:T(8,128)S(1)}, u32[]{:S(2)}, u32[]{:S(2)}) %all-to-all-start.1) | async-done | bytes 262176 | tf_op jit(solution)/shard_map/all_to_all | solution.py:389
  59.6 2.1 collective-permute-done.1
  63.4 4.2 %collective-permute-done.6 = bf16[512,512]{1,0:T(8,128)(2,1)S(1)} collective-permute-done((bf16[512,512]{1,0:T(8,128)(2,1)S(1)}, bf16[512,512]{1,0:T(8,128)(2,1)S(1)}, u32[]{:S(2)}, u32[]{:S(2)}) %collective-permute-start.6) | collective-permute-done | bytes 524320 | tf_op jit(solution)/shard_map/ppermute | solution.py:121
  68.6 10.3 %collective-permute-done.2.refs_1_ = bf16[2,128,1024]{2,1,0:T(8,128)(2,1)} collective-permute-done((bf16[2,128,1024]{2,1,0:T(8,128)(2,1)S(1)}, bf16[2,128,1024]{2,1,0:T(8,128)(2,1)}, u32[]{:S(2)}, u32[]{:S(2)}) %collective-permute-start.2) | collective-permute-done | bytes 524320 | tf_op jit(solution)/shard_map/ppermute | solution.py:121
  78.9 5.8 %shard_map.82 = bf16[16,3,32,256]{3,2,1,0:T(8,128)(2,1)} custom-call(s32[1]{0:T(128)} %bitcast.4.place_ref, bf16[2,128,1024]{2,1,0:T(8,128)(2,1)} %copy-done.4, bf16[2,128,1024]{2,1,0:T(8,128)(2,1)} %collective-permute-done.2.refs_1_, bf16[3,2,1024,512]{3,2,1,0:T(8,128)(2,1)} %bitcast.50), custom_call_target="tpu_custom_call" | custom-call | flops 48318382080 | bytes 8126464 | tf_op jit(solution)/shard_map/pallas_call | solution.py:152
  84.7 14.2 %all-to-all-start = ((bf16[16,3,32,256]{3,2,1,0:T(8,128)(2,1)}), bf16[16,3,32,256]{3,2,1,0:T(8,128)(2,1)S(1)}, u32[]{:S(2)}, u32[]{:S(2)}) async-start(bf16[16,3,32,256]{3,2,1,0:T(8,128)(2,1)} %shard_map.82), calls=%async_computation | async-start | bytes 1572864 | tf_op jit(solution)/shard_map/all_to_all | solution.py:405
  98.9 5.9 %shard_map.83 = bf16[16,3,32,256]{3,2,1,0:T(8,128)(2,1)} custom-call(s32[1]{0:T(128)} %bitcast.4.place_ref, bf16[2,128,1024]{2,1,0:T(8,128)(2,1)} %copy-done.3, bf16[2,128,1024]{2,1,0:T(8,128)(2,1)} %copy-done.7, bf16[3,2,1024,512]{3,2,1,0:T(8,128)(2,1)} %bitcast.51), custom_call_target="tpu_custom_call" | custom-call | flops 48318382080 | bytes 8126464 | tf_op jit(solution)/shard_map/pallas_call | solution.py:152
  104.8 13.1 %all-to-all-done.refs_0_ = bf16[16,3,32,256]{3,2,1,0:T(8,128)(2,1)S(1)} async-done(((bf16[16,3,32,256]{3,2,1,0:T(8,128)(2,1)}), bf16[16,3,32,256]{3,2,1,0:T(8,128)(2,1)S(1)}, u32[]{:S(2)}, u32[]{:S(2)}) %all-to-all-start) | async-done | bytes 786464 | tf_op jit(solution)/shard_map/all_to_all | solution.py:405
  118.0 24.9 %all_to_all.20.refs_1_ = bf16[16,3,32,256]{3,2,1,0:T(8,128)(2,1)S(1)} all-to-all(bf16[16,3,32,256]{3,2,1,0:T(8,128)(2,1)} %shard_map.83), channel_id=1, replica_groups=mesh['seq'=16,'tp'=2] {'seq'}, dimensions={0} | all-to-all | bytes 1572864 | tf_op jit(solution)/shard_map/all_to_all | solution.py:405
  142.8 2.9 %shard_map.84 = bf16[2,4,32,256]{3,2,1,0:T(8,128)(2,1)S(1)} custom-call(bf16[16,3,32,256]{3,2,1,0:T(8,128)(2,1)S(1)} %all-to-all-done.refs_0_, bf16[16,3,32,256]{3,2,1,0:T(8,128)(2,1)S(1)} %all_to_all.20.refs_1_, f32[16,32,128]{2,1,0:T(8,128)S(1)} %all-to-all-done.1.refs_2_, f32[3,3,32,128]{3,2,1,0:T(8,128)S(1)} %broadcast_in_dim.9.refs_3_, ...), custom_call_target="tpu_custom_call" | custom-call | flops 1000000000 | bytes 4194304 | tf_op jit(solution)/shard_map/pallas_call | solution.py:313
  146.6 4.4 %all-to-all-start.3 = ((bf16[32,32,256]{2,1,0:T(8,128)(2,1)}), bf16[32,32,256]{2,1,0:T(8,128)(2,1)S(1)}, u32[]{:S(2)}, u32[]{:S(2)}) async-start(bf16[32,32,256]{2,1,0:T(8,128)(2,1)} %bitcast.18), calls=%async_computation.3 | async-start | bytes 1048576 | tf_op jit(solution)/shard_map/all_to_all | solution.py:412
  151.1 14.5 %all-to-all-done.3 = bf16[32,32,256]{2,1,0:T(8,128)(2,1)S(1)} async-done(((bf16[32,32,256]{2,1,0:T(8,128)(2,1)}), bf16[32,32,256]{2,1,0:T(8,128)(2,1)S(1)}, u32[]{:S(2)}, u32[]{:S(2)}) %all-to-all-start.3) | async-done | bytes 524320 | tf_op jit(solution)/shard_map/all_to_all | solution.py:412
  166.6 4.9 %shard_map.85 = bf16[256,2048]{1,0:T(8,128)(2,1)} custom-call(s32[1]{0:T(128)} %bitcast.4.place_ref, bf16[2,256,512]{2,1,0:T(8,128)(2,1)} %bitcast.42, bf16[4,2,512,512]{3,2,1,0:T(8,128)(2,1)} %bitcast.40), custom_call_target="tpu_custom_call" | custom-call | flops 1073741824 | bytes 5767168 | tf_op jit(solution)/shard_map/pallas_call | solution.py:348
  172.8 1.7 collective-permute-start.10
  174.5 1.9 collective-permute-start.8
  176.3 5.8 %collective-permute-start.7 = (bf16[64,2048]{1,0:T(8,128)(2,1)S(1)}, bf16[64,2048]{1,0:T(8,128)(2,1)S(1)}, u32[]{:S(2)}, u32[]{:S(2)}) collective-permute-start(bf16[64,2048]{1,0:T(8,128)(2,1)S(1)} %get-tuple-element.24), channel_id=1, source_target_pairs={{0,0},{1,16},{2,2},{3,18},{4,4},{5,20},{6,6},{7,22},{8,8},{9,24},{... | collective-permute-start | bytes 786440 | tf_op jit(solution)/shard_map/ppermute | solution.py:74
  182.3 11.0 %collective-permute-done.10.refs_3_ = bf16[64,2048]{1,0:T(8,128)(2,1)S(1)} collective-permute-done((bf16[64,2048]{1,0:T(8,128)(2,1)S(1)}, bf16[64,2048]{1,0:T(8,128)(2,1)S(1)}, u32[]{:S(2)}, u32[]{:S(2)}) %collective-permute-start.10) | collective-permute-done | bytes 262176 | tf_op jit(solution)/shard_map/ppermute | solution.py:74
  193.3 1.6 collective-permute-done.8.refs_1_
  194.9 2.5 %collective-permute-done.7.refs_0_ = bf16[64,2048]{1,0:T(8,128)(2,1)S(1)} collective-permute-done((bf16[64,2048]{1,0:T(8,128)(2,1)S(1)}, bf16[64,2048]{1,0:T(8,128)(2,1)S(1)}, u32[]{:S(2)}, u32[]{:S(2)}) %collective-permute-start.7) | collective-permute-done | bytes 262176 | tf_op jit(solution)/shard_map/ppermute | solution.py:74
  197.5 2.1 %shard_map.86 = bf16[128,4096]{1,0:T(8,128)(2,1)} custom-call(s32[8]{0:T(128)S(1)} %stack.63.place_ref, bf16[64,2048]{1,0:T(8,128)(2,1)S(1)} %collective-permute-done.7.refs_0_, bf16[64,2048]{1,0:T(8,128)(2,1)S(1)} %collective-permute-done.8.refs_1_, bf16[64,2048]{1,0:T(8,128)(2,1)S(1)} %collective-permute-done.9.refs_2_, ...), custom_call_target="tpu_custom_call" | custom-call | bytes 2097152 | tf_op jit(solution)/shard_map/pallas_call | solution.py:35
  (48 shorter events, 14.9 us)
Async XLA Ops:
  6.5 45.5 %copy-start = (f32[3,3,512]{2,1,0:T(4,128)S(1)}, f32[3,3,512]{2,1,0:T(4,128)}, u32[]{:S(2)}) copy-start(f32[3,3,512]{2,1,0:T(4,128)} %param.10) | copy-start | bytes 55300
  6.5 72.3 %all-gather.4.cloned.1.call-start = ((), (), s32[]{:S(2)}) async-start(), calls=%async_computation.4 | async-start | bytes 7864320 | tf_op jit(solution)/shard_map/all_gather | solution.py:381
  7.3 34.5 %copy-start.6 = (f32[128,512]{1,0:T(8,128)S(1)}, f32[128,512]{1,0:T(8,128)}, u32[]{:S(2)}) copy-start(f32[128,512]{1,0:T(8,128)} %param.11) | copy-start | bytes 786436
  8.6 49.4 %copy-start.5 = (bf16[512,512]{1,0:T(8,128)(2,1)S(1)}, bf16[512,512]{1,0:T(8,128)(2,1)}, u32[]{:S(2)}) copy-start(bf16[512,512]{1,0:T(8,128)(2,1)} %param.13) | copy-start | bytes 1572868
  8.7 13.7 %collective-permute-start = (bf16[2,128,1024]{2,1,0:T(8,128)(2,1)S(1)}, bf16[2,128,1024]{2,1,0:T(8,128)(2,1)S(1)}, u32[]{:S(2)}, u32[]{:S(2)}) collective-permute-start(bf16[2,128,1024]{2,1,0:T(8,128)(2,1)S(1)} %pad_maximum_fusion.2), channel_id=1, source_target_pairs={{0,1},{1,0},{2,3},{3,2},{4,5},{5,4},{6,7},{7,6},{8,9},{9,8},{10,11... | collective-permute-start | bytes 1572872 | tf_op jit(solution)/shard_map/ppermute | solution.py:95
  22.6 18.5 %collective-permute-start.3 = (bf16[128,1024]{1,0:T(8,128)(2,1)S(1)}, bf16[128,1024]{1,0:T(8,128)(2,1)S(1)}, u32[]{:S(2)}, u32[]{:S(2)}) collective-permute-start(bf16[128,1024]{1,0:T(8,128)(2,1)S(1)} %get-tuple-element.25), channel_id=1, source_target_pairs={{0,16},{2,18},{4,20},{6,22},{8,24},{10,26},{12,28},{14,30},{16,0},... | collective-permute-start | bytes 786440 | tf_op jit(solution)/shard_map/ppermute | solution.py:112
  25.3 15.8 %collective-permute-start.4 = (bf16[128,1024]{1,0:T(8,128)(2,1)S(1)}, bf16[128,1024]{1,0:T(8,128)(2,1)S(1)}, u32[]{:S(2)}, u32[]{:S(2)}) collective-permute-start(bf16[128,1024]{1,0:T(8,128)(2,1)S(1)} %get-tuple-element.26), channel_id=1, source_target_pairs={{0,24},{2,26},{4,28},{6,30},{8,0},{10,2},{12,4},{14,6},{16,8},{18,... | collective-permute-start | bytes 786440 | tf_op jit(solution)/shard_map/ppermute | solution.py:112
  41.1 43.6 %copy-start.3 = (bf16[2,128,1024]{2,1,0:T(8,128)(2,1)}, bf16[2,128,1024]{2,1,0:T(8,128)(2,1)S(1)}, u32[]{:S(2)}) copy-start(bf16[2,128,1024]{2,1,0:T(8,128)(2,1)S(1)} %pad_maximum_fusion.4.refs_0_) | copy-start | bytes 1572868
  41.1 16.7 %collective-permute-start.5 = (bf16[2,128,1024]{2,1,0:T(8,128)(2,1)S(1)}, bf16[2,128,1024]{2,1,0:T(8,128)(2,1)S(1)}, u32[]{:S(2)}, u32[]{:S(2)}) collective-permute-start(bf16[2,128,1024]{2,1,0:T(8,128)(2,1)S(1)} %pad_maximum_fusion.4.refs_0_), channel_id=1, source_target_pairs={{0,1},{1,0},{2,3},{3,2},{4,5},{5,4},{6,7},{7,6},{8,9},{9,8},{10,11... | collective-permute-start | bytes 1572872 | tf_op jit(solution)/shard_map/ppermute | solution.py:121
  42.6 15.3 %all-to-all-start.1 = ((f32[16,32,128]{2,1,0:T(8,128)}), f32[16,32,128]{2,1,0:T(8,128)S(1)}, u32[]{:S(2)}, u32[]{:S(2)}) async-start(f32[16,32,128]{2,1,0:T(8,128)} %bitcast.17), calls=%async_computation.1 | async-start | bytes 524288 | tf_op jit(solution)/shard_map/all_to_all | solution.py:389
  49.7 116.9 %all-gather.6.cloned.1.call-start = ((), (), s32[]{:S(2)}) async-start(), calls=%async_computation.5 | async-start | bytes 5242880 | tf_op jit(solution)/shard_map/all_gather | solution.py:408
  49.8 11.9 %collective-permute-start.1 = (bf16[128,1024]{1,0:T(8,128)(2,1)S(1)}, bf16[128,1024]{1,0:T(8,128)(2,1)S(1)}, u32[]{:S(2)}, u32[]{:S(2)}) collective-permute-start(bf16[128,1024]{1,0:T(8,128)(2,1)S(1)} %get-tuple-element.27), channel_id=1, source_target_pairs={{0,8},{2,10},{4,12},{6,14},{8,16},{10,18},{12,20},{14,22},{16,24},... | collective-permute-start | bytes 786440 | tf_op jit(solution)/shard_map/ppermute | solution.py:112
  57.9 26.8 %copy-start.7 = (bf16[2,128,1024]{2,1,0:T(8,128)(2,1)}, bf16[2,128,1024]{2,1,0:T(8,128)(2,1)S(1)}, u32[]{:S(2)}) copy-start(bf16[2,128,1024]{2,1,0:T(8,128)(2,1)S(1)} %collective-permute-done.5.refs_1_) | copy-start | bytes 1572868
  58.1 9.5 %collective-permute-start.6 = (bf16[512,512]{1,0:T(8,128)(2,1)S(1)}, bf16[512,512]{1,0:T(8,128)(2,1)S(1)}, u32[]{:S(2)}, u32[]{:S(2)}) collective-permute-start(bf16[512,512]{1,0:T(8,128)(2,1)S(1)} %copy-done.5), channel_id=1, source_target_pairs={{0,1},{1,0},{2,3},{3,2},{4,5},{5,4},{6,7},{7,6},{8,9},{9,8},{10,11... | collective-permute-start | bytes 1572872 | tf_op jit(solution)/shard_map/ppermute | solution.py:121
  61.8 17.1 %copy-start.4 = (bf16[2,128,1024]{2,1,0:T(8,128)(2,1)}, bf16[2,128,1024]{2,1,0:T(8,128)(2,1)S(1)}, u32[]{:S(2)}) copy-start(bf16[2,128,1024]{2,1,0:T(8,128)(2,1)S(1)} %pad_maximum_fusion.3.refs_0_) | copy-start | bytes 1572868
  61.8 17.1 %collective-permute-start.2 = (bf16[2,128,1024]{2,1,0:T(8,128)(2,1)S(1)}, bf16[2,128,1024]{2,1,0:T(8,128)(2,1)}, u32[]{:S(2)}, u32[]{:S(2)}) collective-permute-start(bf16[2,128,1024]{2,1,0:T(8,128)(2,1)S(1)} %pad_maximum_fusion.3.refs_0_), channel_id=1, source_target_pairs={{0,1},{1,0},{2,3},{3,2},{4,5},{5,4},{6,7},{7,6},{8,9},{9,8},{10,11... | collective-permute-start | bytes 1572872 | tf_op jit(solution)/shard_map/ppermute | solution.py:121
  84.7 33.3 %all-to-all-start = ((bf16[16,3,32,256]{3,2,1,0:T(8,128)(2,1)}), bf16[16,3,32,256]{3,2,1,0:T(8,128)(2,1)S(1)}, u32[]{:S(2)}, u32[]{:S(2)}) async-start(bf16[16,3,32,256]{3,2,1,0:T(8,128)(2,1)} %shard_map.82), calls=%async_computation | async-start | bytes 1572864 | tf_op jit(solution)/shard_map/all_to_all | solution.py:405
  98.9 43.9 %copy-start.1 = (f32[256,256]{1,0:T(8,128)S(1)}, f32[256,256]{1,0:T(8,128)}, u32[]{:S(2)}) copy-start(f32[256,256]{1,0:T(8,128)} %constant.236.clone.refs_6_) | copy-start | bytes 786436
  98.9 43.9 %copy-start.2 = (f32[128,256]{1,0:T(8,128)S(1)}, f32[128,256]{1,0:T(8,128)}, u32[]{:S(2)}) copy-start(f32[128,256]{1,0:T(8,128)} %constant.235.clone.refs_5_) | copy-start | bytes 393220
  146.6 18.9 %all-to-all-start.3 = ((bf16[32,32,256]{2,1,0:T(8,128)(2,1)}), bf16[32,32,256]{2,1,0:T(8,128)(2,1)S(1)}, u32[]{:S(2)}, u32[]{:S(2)}) async-start(bf16[32,32,256]{2,1,0:T(8,128)(2,1)} %bitcast.18), calls=%async_computation.3 | async-start | bytes 1048576 | tf_op jit(solution)/shard_map/all_to_all | solution.py:412
  172.8 20.5 %collective-permute-start.10 = (bf16[64,2048]{1,0:T(8,128)(2,1)S(1)}, bf16[64,2048]{1,0:T(8,128)(2,1)S(1)}, u32[]{:S(2)}, u32[]{:S(2)}) collective-permute-start(bf16[64,2048]{1,0:T(8,128)(2,1)S(1)} %get-tuple-element.21), channel_id=1, source_target_pairs={{0,24},{1,8},{2,26},{3,10},{4,28},{5,12},{6,30},{7,14},{8,16},{9,0... | collective-permute-start | bytes 786440 | tf_op jit(solution)/shard_map/ppermute | solution.py:74
  174.5 18.9 %collective-permute-start.9 = (bf16[64,2048]{1,0:T(8,128)(2,1)S(1)}, bf16[64,2048]{1,0:T(8,128)(2,1)S(1)}, u32[]{:S(2)}, u32[]{:S(2)}) collective-permute-start(bf16[64,2048]{1,0:T(8,128)(2,1)S(1)} %get-tuple-element.22), channel_id=1, source_target_pairs={{0,16},{1,0},{2,18},{3,2},{4,20},{5,4},{6,22},{7,6},{8,24},{9,8},{... | collective-permute-start | bytes 786440 | tf_op jit(solution)/shard_map/ppermute | solution.py:74
  174.5 20.5 %collective-permute-start.8 = (bf16[64,2048]{1,0:T(8,128)(2,1)S(1)}, bf16[64,2048]{1,0:T(8,128)(2,1)S(1)}, u32[]{:S(2)}, u32[]{:S(2)}) collective-permute-start(bf16[64,2048]{1,0:T(8,128)(2,1)S(1)} %get-tuple-element.23), channel_id=1, source_target_pairs={{0,8},{1,24},{2,10},{3,26},{4,12},{5,28},{6,14},{7,30},{8,0},{9,16... | collective-permute-start | bytes 786440 | tf_op jit(solution)/shard_map/ppermute | solution.py:74
  176.3 21.1 %collective-permute-start.7 = (bf16[64,2048]{1,0:T(8,128)(2,1)S(1)}, bf16[64,2048]{1,0:T(8,128)(2,1)S(1)}, u32[]{:S(2)}, u32[]{:S(2)}) collective-permute-start(bf16[64,2048]{1,0:T(8,128)(2,1)S(1)} %get-tuple-element.24), channel_id=1, source_target_pairs={{0,0},{1,16},{2,2},{3,18},{4,4},{5,20},{6,6},{7,22},{8,8},{9,24},{... | collective-permute-start | bytes 786440 | tf_op jit(solution)/shard_map/ppermute | solution.py:74
Sparse Core Ops, SparseCore 0:
  8.9 49.7 all-gather.3
  68.7 52.6 all-gather.5

commit v6 on v5

--- a/solution.py
+++ b/solution.py
@@ -122,39 +122,43 @@
     return pieces
 
 
-def project_kernel(place_ref, *refs):
+def project_kernel(tp_parts, place_ref, *refs):
     *share_refs, weight_ref, out_ref = refs
-    tp_parts = len(share_refs)
-    seq_parts, _, chans, count = out_ref.shape
-    width = share_refs[0].shape[2]
-    sums = jnp.zeros((count, seq_parts * chans), jnp.float32)
-    for step, share_ref in enumerate(share_refs):
-        which = lax.rem(place_ref[0] - step + tp_parts, tp_parts)
-        sums = sums + jnp.dot(
-            share_ref[...].reshape(count, width),
-            weight_ref[0, which],
-            preferred_element_type=jnp.float32,
-        )
-    turned = sums.T.astype(out_ref.dtype)
-    for seq in range(seq_parts):
-        out_ref[seq, 0] = turned[seq * chans : (seq + 1) * chans]
-
-
-def project_in(pieces, weight, seq_parts):
-    tp_parts = len(pieces)
-    outer, rows, width = pieces[0].shape
+    seq_parts, _, chans, _ = out_ref.shape
+    depth, rows, width = share_refs[0].shape
+    count = depth * rows
+    for chunk in range(len(share_refs) // tp_parts):
+        sums = jnp.zeros((count, seq_parts * chans), jnp.float32)
+        for step in range(tp_parts):
+            which = lax.rem(place_ref[0] - step + tp_parts, tp_parts)
+            sums = sums + jnp.dot(
+                share_refs[chunk * tp_parts + step][...].reshape(count, width),
+                weight_ref[0, which],
+                preferred_element_type=jnp.float32,
+            )
+        turned = sums.T.astype(out_ref.dtype)
+        for seq in range(seq_parts):
+            out_ref[seq, 0, :, chunk * count : (chunk + 1) * count] = turned[
+                seq * chans : (seq + 1) * chans
+            ]
+
+
+def project_in(chunks, weight, seq_parts):
+    tp_parts = len(chunks[0])
+    depth, rows, width = chunks[0][0].shape
     streams, _, chan_tp = weight.shape
     weight = weight.reshape(streams, tp_parts, width, chan_tp)
     chans = chan_tp // seq_parts
-    count = outer * rows
+    count = len(chunks) * depth * rows
+    pieces = [piece for chunk in chunks for piece in chunk]
     place = lax.axis_index("tp").astype(jnp.int32)[None]
-    whole = pl.BlockSpec((outer, rows, width), lambda i, place: (0, 0, 0))
+    whole = pl.BlockSpec((depth, rows, width), lambda i, place: (0, 0, 0))
     return pl.pallas_call(
-        project_kernel,
+        functools.partial(project_kernel, tp_parts),
         grid_spec=pltpu.PrefetchScalarGridSpec(
             num_scalar_prefetch=1,
             grid=(streams,),
-            in_specs=[whole] * tp_parts
+            in_specs=[whole] * len(pieces)
             + [pl.BlockSpec((1, tp_parts, width, chan_tp), lambda i, place: (i, 0, 0, 0))],
             out_specs=pl.BlockSpec((seq_parts, 1, chans, count), lambda i, place: (0, i, 0, 0)),
         ),
@@ -162,7 +166,7 @@
         compiler_params=pltpu.CompilerParams(vmem_limit_bytes=56 * 2**20),
         cost_estimate=pl.CostEstimate(
             flops=HEAVY * 2 * count * weight.size,
-            bytes_accessed=2 * (weight.size + tp_parts * pieces[0].size)
+            bytes_accessed=2 * (weight.size + len(pieces) * pieces[0].size)
             + 2 * streams * count * chan_tp,
             transcendentals=0,
         ),
@@ -380,12 +384,6 @@
 
     weight = lax.all_gather(in_proj, "seq", axis=1, tiled=True, axis_index_groups=inner_groups)
 
-    held = share_columns(features, outer, tp_parts)
-    held, long_filter = lax.optimization_barrier((held, long_filter))
-    arrived = cross_outer(held, outer, inner_parts, tp_parts)
-    depth = outer // CHUNKS
-    crossed = [jnp.stack(arrived[index * depth : (index + 1) * depth]) for index in range(CHUNKS)]
-
     filter_blocks = lax.all_to_all(
         long_filter.T.reshape(seq_parts, chans, rows), "seq", split_axis=0, concat_axis=0, tiled=True
     )
@@ -394,20 +392,22 @@
     skip = lax.dynamic_slice_in_dim(skip_gain, position * chans, chans, axis=0)
     skip = jnp.broadcast_to(skip[:, None], (chans, rows))
 
-    parts = []
-    for index, part in enumerate(crossed):
-        pieces = share_over_tp(part, tp_parts)
-        if index + 1 == CHUNKS:
-            pieces, out_proj, filter_blocks, taps, skip = lax.optimization_barrier(
-                (pieces, out_proj, filter_blocks, taps, skip)
-            )
-        partial = project_in(pieces, weight, seq_parts)
-        parts.append(lax.all_to_all(partial, "seq", split_axis=0, concat_axis=0, tiled=True))
-
+    held = share_columns(features, outer, tp_parts)
+    held, filter_blocks, taps, skip = lax.optimization_barrier((held, filter_blocks, taps, skip))
+    arrived = cross_outer(held, outer, inner_parts, tp_parts)
+    depth = outer // CHUNKS
+    chunks = [
+        share_over_tp(jnp.stack(arrived[index * depth : (index + 1) * depth]), tp_parts)
+        for index in range(CHUNKS)
+    ]
+    chunks, out_proj = lax.optimization_barrier((chunks, out_proj))
+
+    partial = project_in(chunks, weight, seq_parts)
+    parts = lax.all_to_all(partial, "seq", split_axis=0, concat_axis=0, tiled=True)
     out_block = jnp.stack(share_over_tp(out_proj, tp_parts))
     out_weight = lax.all_gather(out_block, "seq", axis_index_groups=inner_groups)
 
-    gated = convolve(parts, filter_blocks, taps, skip, outer, tp_parts)
+    gated = convolve([parts], filter_blocks, taps, skip, outer, tp_parts)
     gated = jnp.broadcast_to(gated[:, None], (tp_parts, outer) + gated.shape[1:])
     gated = lax.all_to_all(
         gated.reshape((-1,) + gated.shape[3:]), ("tp", "seq"), split_axis=0, concat_axis=0, tiled=True

time: 210 us -> 195 us (0.929)
  blocking collectives: 24.9 us -> 40.3 us
  starting transfers between devices: 44.1 us -> 29.4 us
  waiting for transfers between devices: 94.3 us -> 82.6 us
  Pallas kernels: 21.7 us -> 17.5 us
    all_to_all x1, blocking collectives: 24.9 us -> 40.3 us  [per_device(): lax.all_to_all(partial, 'seq', split_axis=0, concat_axis=0, tiled=True)]
    all_to_all x1 -> x0, starting transfers between devices: 14.2 us -> none  [per_device(): lax.all_to_all(partial, 'seq', split_axis=0, concat_axis=0, tiled=True)]
    all_to_all x1 -> x0, waiting for transfers between devices: 13.1 us -> none  [per_device(): lax.all_to_all(partial, 'seq', split_axis=0, concat_axis=0, tiled=True)]
    ppermute x3, waiting for transfers between devices: 14.4 us -> 24.1 us  [share_over_tp(): pieces.append(lax.ppermute(part, 'tp', pairs))]
    ppermute x1, waiting for transfers between devices: 13.2 us -> 4.66 us  [share_columns(): lax.ppermute(piece, 'tp', [(i, (i + step) % tp_parts) for i in range(tp_p...]
    pallas_call x2 -> x1, Pallas kernels: 11.7 us -> 7.45 us  [project_in(): pl.pallas_call(functools.partial(project_kernel, tp_parts), grid_spec=plt...]
    ppermute x3, waiting for transfers between devices: 17.4 us -> 21.3 us  [cross_outer(): lax.ppermute(piece, 'seq', [(i, (i + far) % seq_parts) for i in range(seq...]
    all_to_all x1, waiting for transfers between devices: 5.75 us -> 2.22 us  [per_device(): lax.all_to_all(long_filter.T.reshape(seq_parts, chans, rows), 'seq', spli...]
  transfers between devices with their start and end apart: 16 -> 15, of which waited for: 11 -> 11; matrix products, arithmetic and copies ran while one was open for 3% -> 3% of each run, Pallas kernels for 7% -> 5%
where the time goes in v6:
time: 195 us; the launch traced here: 191 us
  waiting for transfers between devices  82.6 us (42%)
  blocking collectives  40.3 us (21%)
  starting transfers between devices  29.4 us (15%)
  Pallas kernels  17.5 us (9%)
  between operations  14 us (7%)
  local copies, waits for them, and re-layouts  5.93 us (3%)
    all_to_all x1, blocking collectives, per_device(): lax.all_to_all(partial, 'seq', split_axis=0, concat_axis=0, tiled=True)  40.3 us
    ppermute x3, waiting for transfers between devices, share_over_tp(): pieces.append(lax.ppermute(part, 'tp', pairs))  24.1 us
    ppermute x3, waiting for transfers between devices, cross_outer(): lax.ppermute(piece, 'seq', [(i, (i + far) % seq_parts) for i in range(seq...  21.3 us
    ppermute x4, waiting for transfers between devices, return_output(): pieces.append(lax.ppermute(piece, ('seq', 'tp'), pairs))  15.2 us
    all_to_all x1, waiting for transfers between devices, per_device(): lax.all_to_all(gated.reshape((-1,) + gated.shape[3:]), ('tp', 'seq'), spl...  14.5 us
    ppermute x4, starting transfers between devices, return_output(): pieces.append(lax.ppermute(piece, ('seq', 'tp'), pairs))  9.34 us
    pallas_call x1, Pallas kernels, project_in(): pl.pallas_call(functools.partial(project_kernel, tp_parts), grid_spec=plt...  7.45 us
    all_to_all x1, starting transfers between devices, per_device(): lax.all_to_all(long_filter.T.reshape(seq_parts, chans, rows), 'seq', spli...  6.27 us
  transfers between devices with their start and end apart: 15, of which 11 were waited for; matrix products, arithmetic and copies ran while one was open for 3% of the time, Pallas kernels for 5%

profile of v6, /device:TPU:12, one launch (start us, length us, event | category | flops | bytes accessed | tf_op | source)
XLA Modules:
  0.0 191.0 jit_solution(9248040518566198154)
XLA Ops:
  9.6 6.3 %all-to-all-start = ((f32[16,32,128]{2,1,0:T(8,128)}), f32[16,32,128]{2,1,0:T(8,128)S(1)}, u32[]{:S(2)}, u32[]{:S(2)}) async-start(f32[16,32,128]{2,1,0:T(8,128)} %bitcast.10), calls=%async_computation | async-start | bytes 524288 | tf_op jit(solution)/shard_map/all_to_all | solution.py:387
  17.0 4.7 %collective-permute-done = bf16[2,128,1024]{2,1,0:T(8,128)(2,1)S(1)} collective-permute-done((bf16[2,128,1024]{2,1,0:T(8,128)(2,1)S(1)}, bf16[2,128,1024]{2,1,0:T(8,128)(2,1)S(1)}, u32[]{:S(2)}, u32[]{:S(2)}) %collective-permute-start) | collective-permute-done | bytes 524320 | tf_op jit(solution)/shard_map/ppermute | solution.py:95
  21.8 2.2 %all-to-all-done.refs_1_ = f32[16,32,128]{2,1,0:T(8,128)S(1)} async-done(((f32[16,32,128]{2,1,0:T(8,128)}), f32[16,32,128]{2,1,0:T(8,128)S(1)}, u32[]{:S(2)}, u32[]{:S(2)}) %all-to-all-start) | async-done | bytes 262176 | tf_op jit(solution)/shard_map/all_to_all | solution.py:387
  24.2 1.7 collective-permute-start.1
  25.9 2.8 %collective-permute-start.3 = (bf16[128,1024]{1,0:T(8,128)(2,1)S(1)}, bf16[128,1024]{1,0:T(8,128)(2,1)S(1)}, u32[]{:S(2)}, u32[]{:S(2)}) collective-permute-start(bf16[128,1024]{1,0:T(8,128)(2,1)S(1)} %get-tuple-element.27), channel_id=1, source_target_pairs={{0,16},{2,18},{4,20},{6,22},{8,24},{10,26},{12,28},{14,30},{16,0},... | collective-permute-start | bytes 786440 | tf_op jit(solution)/shard_map/ppermute | solution.py:112
  28.7 4.8 %collective-permute-done.1 = bf16[128,1024]{1,0:T(8,128)(2,1)S(1)} collective-permute-done((bf16[128,1024]{1,0:T(8,128)(2,1)S(1)}, bf16[128,1024]{1,0:T(8,128)(2,1)S(1)}, u32[]{:S(2)}, u32[]{:S(2)}) %collective-permute-start.1) | collective-permute-done | bytes 262176 | tf_op jit(solution)/shard_map/ppermute | solution.py:112
  33.5 1.4 collective-permute-start.2
  34.9 13.1 %collective-permute-done.3 = bf16[128,1024]{1,0:T(8,128)(2,1)S(1)} collective-permute-done((bf16[128,1024]{1,0:T(8,128)(2,1)S(1)}, bf16[128,1024]{1,0:T(8,128)(2,1)S(1)}, u32[]{:S(2)}, u32[]{:S(2)}) %collective-permute-start.3) | collective-permute-done | bytes 262176 | tf_op jit(solution)/shard_map/ppermute | solution.py:112
  48.0 3.4 %collective-permute-done.4 = bf16[128,1024]{1,0:T(8,128)(2,1)S(1)} collective-permute-done((bf16[128,1024]{1,0:T(8,128)(2,1)S(1)}, bf16[128,1024]{1,0:T(8,128)(2,1)S(1)}, u32[]{:S(2)}, u32[]{:S(2)}) %collective-permute-start.4) | collective-permute-done | bytes 262176 | tf_op jit(solution)/shard_map/ppermute | solution.py:112
  52.8 12.5 %collective-permute-done.5.refs_3_ = bf16[2,128,1024]{2,1,0:T(8,128)(2,1)S(1)} collective-permute-done((bf16[2,128,1024]{2,1,0:T(8,128)(2,1)S(1)}, bf16[2,128,1024]{2,1,0:T(8,128)(2,1)S(1)}, u32[]{:S(2)}, u32[]{:S(2)}) %collective-permute-start.5) | collective-permute-done | bytes 524320 | tf_op jit(solution)/shard_map/ppermute | solution.py:121
  66.5 11.6 %collective-permute-done.6 = bf16[512,512]{1,0:T(8,128)(2,1)S(1)} collective-permute-done((bf16[512,512]{1,0:T(8,128)(2,1)S(1)}, bf16[512,512]{1,0:T(8,128)(2,1)S(1)}, u32[]{:S(2)}, u32[]{:S(2)}) %collective-permute-start.6) | collective-permute-done | bytes 524320 | tf_op jit(solution)/shard_map/ppermute | solution.py:121
  79.3 7.5 %shard_map.82 = bf16[16,3,32,512]{3,2,1,0:T(8,128)(2,1)} custom-call(s32[1]{0:T(128)} %bitcast.4.place_ref, bf16[2,128,1024]{2,1,0:T(8,128)(2,1)} %copy-done.4, bf16[2,128,1024]{2,1,0:T(8,128)(2,1)} %copy-done.8, bf16[2,128,1024]{2,1,0:T(8,128)(2,1)} %copy-done.5, bf16[2,128,1024]{2,1,0:T(8,128)(2,1)} %copy-done.9, bf16[3,2,1024,512]{3,2,1,0:T(8,128)(2,1)} %bitcast.50), custom_call_target="tpu_custom_call" | custom-call | flops 96636764160 | bytes 9961472 | tf_op jit(solution)/shard_map/pallas_call | solution.py:156
  86.8 40.3 %all_to_all.15.refs_0_ = bf16[16,3,32,512]{3,2,1,0:T(8,128)(2,1)S(1)} all-to-all(bf16[16,3,32,512]{3,2,1,0:T(8,128)(2,1)} %shard_map.82), channel_id=1, replica_groups=mesh['seq'=16,'tp'=2] {'seq'}, dimensions={0} | all-to-all | bytes 3145728 | tf_op jit(solution)/shard_map/all_to_all | solution.py:406
  127.0 3.0 %shard_map.83 = bf16[2,4,32,256]{3,2,1,0:T(8,128)(2,1)S(1)} custom-call(bf16[16,3,32,512]{3,2,1,0:T(8,128)(2,1)S(1)} %all_to_all.15.refs_0_, f32[16,32,128]{2,1,0:T(8,128)S(1)} %all-to-all-done.refs_1_, f32[3,3,32,128]{3,2,1,0:T(8,128)S(1)} %broadcast_in_dim.9.refs_2_, f32[32,128]{1,0:T(8,128)S(1)} %broadcast_in_dim.10.refs_3_, f32[128,256]{1,0:T(8,128)S(1)} %copy-done.2, ...), custom_call_target="tpu_custom_call" | custom-call | flops 1000000000 | bytes 4194304 | tf_op jit(solution)/shard_map/pallas_call | solution.py:317
  130.8 4.8 %all-to-all-start.2 = ((bf16[32,32,256]{2,1,0:T(8,128)(2,1)}), bf16[32,32,256]{2,1,0:T(8,128)(2,1)S(1)}, u32[]{:S(2)}, u32[]{:S(2)}) async-start(bf16[32,32,256]{2,1,0:T(8,128)(2,1)} %bitcast.18), calls=%async_computation.2 | async-start | bytes 1048576 | tf_op jit(solution)/shard_map/all_to_all | solution.py:412
  135.6 14.5 %all-to-all-done.2 = bf16[32,32,256]{2,1,0:T(8,128)(2,1)S(1)} async-done(((bf16[32,32,256]{2,1,0:T(8,128)(2,1)}), bf16[32,32,256]{2,1,0:T(8,128)(2,1)S(1)}, u32[]{:S(2)}, u32[]{:S(2)}) %all-to-all-start.2) | async-done | bytes 524320 | tf_op jit(solution)/shard_map/all_to_all | solution.py:412
  151.1 4.9 %shard_map.84 = bf16[256,2048]{1,0:T(8,128)(2,1)} custom-call(s32[1]{0:T(128)} %bitcast.4.place_ref, bf16[2,256,512]{2,1,0:T(8,128)(2,1)} %bitcast.42, bf16[4,2,512,512]{3,2,1,0:T(8,128)(2,1)} %bitcast.40), custom_call_target="tpu_custom_call" | custom-call | flops 1073741824 | bytes 5767168 | tf_op jit(solution)/shard_map/pallas_call | solution.py:352
  157.3 1.7 collective-permute-start.10
  159.0 1.9 collective-permute-start.8
  160.9 5.8 %collective-permute-start.7 = (bf16[64,2048]{1,0:T(8,128)(2,1)S(1)}, bf16[64,2048]{1,0:T(8,128)(2,1)S(1)}, u32[]{:S(2)}, u32[]{:S(2)}) collective-permute-start(bf16[64,2048]{1,0:T(8,128)(2,1)S(1)} %get-tuple-element.26), channel_id=1, source_target_pairs={{0,0},{1,16},{2,2},{3,18},{4,4},{5,20},{6,6},{7,22},{8,8},{9,24},{... | collective-permute-start | bytes 786440 | tf_op jit(solution)/shard_map/ppermute | solution.py:74
  166.8 11.0 %collective-permute-done.10.refs_3_ = bf16[64,2048]{1,0:T(8,128)(2,1)S(1)} collective-permute-done((bf16[64,2048]{1,0:T(8,128)(2,1)S(1)}, bf16[64,2048]{1,0:T(8,128)(2,1)S(1)}, u32[]{:S(2)}, u32[]{:S(2)}) %collective-permute-start.10) | collective-permute-done | bytes 262176 | tf_op jit(solution)/shard_map/ppermute | solution.py:74
  177.9 1.6 collective-permute-done.8.refs_1_
  179.5 2.5 %collective-permute-done.7.refs_0_ = bf16[64,2048]{1,0:T(8,128)(2,1)S(1)} collective-permute-done((bf16[64,2048]{1,0:T(8,128)(2,1)S(1)}, bf16[64,2048]{1,0:T(8,128)(2,1)S(1)}, u32[]{:S(2)}, u32[]{:S(2)}) %collective-permute-start.7) | collective-permute-done | bytes 262176 | tf_op jit(solution)/shard_map/ppermute | solution.py:74
  182.0 2.1 %shard_map.85 = bf16[128,4096]{1,0:T(8,128)(2,1)} custom-call(s32[8]{0:T(128)S(1)} %stack.63.place_ref, bf16[64,2048]{1,0:T(8,128)(2,1)S(1)} %collective-permute-done.7.refs_0_, bf16[64,2048]{1,0:T(8,128)(2,1)S(1)} %collective-permute-done.8.refs_1_, bf16[64,2048]{1,0:T(8,128)(2,1)S(1)} %collective-permute-done.9.refs_2_, ...), custom_call_target="tpu_custom_call" | custom-call | bytes 2097152 | tf_op jit(solution)/shard_map/pallas_call | solution.py:35
  (49 shorter events, 11.2 us)
Async XLA Ops:
  6.5 10.4 %copy-start = (f32[3,3,512]{2,1,0:T(4,128)S(1)}, f32[3,3,512]{2,1,0:T(4,128)}, u32[]{:S(2)}) copy-start(f32[3,3,512]{2,1,0:T(4,128)} %param.10) | copy-start | bytes 55300
  6.5 1.2 copy-start.3
  6.5 72.7 %all-gather.4.cloned.1.call-start = ((), (), s32[]{:S(2)}) async-start(), calls=%async_computation.3 | async-start | bytes 7864320 | tf_op jit(solution)/shard_map/all_gather | solution.py:385
  7.9 13.7 %collective-permute-start = (bf16[2,128,1024]{2,1,0:T(8,128)(2,1)S(1)}, bf16[2,128,1024]{2,1,0:T(8,128)(2,1)S(1)}, u32[]{:S(2)}, u32[]{:S(2)}) collective-permute-start(bf16[2,128,1024]{2,1,0:T(8,128)(2,1)S(1)} %pad_maximum_fusion.2), channel_id=1, source_target_pairs={{0,1},{1,0},{2,3},{3,2},{4,5},{5,4},{6,7},{7,6},{8,9},{9,8},{10,11... | collective-permute-start | bytes 1572872 | tf_op jit(solution)/shard_map/ppermute | solution.py:95
  9.6 14.4 %all-to-all-start = ((f32[16,32,128]{2,1,0:T(8,128)}), f32[16,32,128]{2,1,0:T(8,128)S(1)}, u32[]{:S(2)}, u32[]{:S(2)}) async-start(f32[16,32,128]{2,1,0:T(8,128)} %bitcast.10), calls=%async_computation | async-start | bytes 524288 | tf_op jit(solution)/shard_map/all_to_all | solution.py:387
  15.8 135.3 %all-gather.6.cloned.1.call-start = ((), (), s32[]{:S(2)}) async-start(), calls=%async_computation.4 | async-start | bytes 5242880 | tf_op jit(solution)/shard_map/all_gather | solution.py:408
  24.2 41.0 %copy-start.6 = (bf16[512,512]{1,0:T(8,128)(2,1)S(1)}, bf16[512,512]{1,0:T(8,128)(2,1)}, u32[]{:S(2)}) copy-start(bf16[512,512]{1,0:T(8,128)(2,1)} %param.13) | copy-start | bytes 1572868
  24.2 9.2 %collective-permute-start.1 = (bf16[128,1024]{1,0:T(8,128)(2,1)S(1)}, bf16[128,1024]{1,0:T(8,128)(2,1)S(1)}, u32[]{:S(2)}, u32[]{:S(2)}) collective-permute-start(bf16[128,1024]{1,0:T(8,128)(2,1)S(1)} %get-tuple-element.29), channel_id=1, source_target_pairs={{0,8},{2,10},{4,12},{6,14},{8,16},{10,18},{12,20},{14,22},{16,24},... | collective-permute-start | bytes 786440 | tf_op jit(solution)/shard_map/ppermute | solution.py:112
  25.9 22.1 %collective-permute-start.3 = (bf16[128,1024]{1,0:T(8,128)(2,1)S(1)}, bf16[128,1024]{1,0:T(8,128)(2,1)S(1)}, u32[]{:S(2)}, u32[]{:S(2)}) collective-permute-start(bf16[128,1024]{1,0:T(8,128)(2,1)S(1)} %get-tuple-element.27), channel_id=1, source_target_pairs={{0,16},{2,18},{4,20},{6,22},{8,24},{10,26},{12,28},{14,30},{16,0},... | collective-permute-start | bytes 786440 | tf_op jit(solution)/shard_map/ppermute | solution.py:112
  28.7 22.7 %collective-permute-start.4 = (bf16[128,1024]{1,0:T(8,128)(2,1)S(1)}, bf16[128,1024]{1,0:T(8,128)(2,1)S(1)}, u32[]{:S(2)}, u32[]{:S(2)}) collective-permute-start(bf16[128,1024]{1,0:T(8,128)(2,1)S(1)} %get-tuple-element.28), channel_id=1, source_target_pairs={{0,24},{2,26},{4,28},{6,30},{8,0},{10,2},{12,4},{14,6},{16,8},{18,... | collective-permute-start | bytes 786440 | tf_op jit(solution)/shard_map/ppermute | solution.py:112
  33.5 45.7 %copy-start.4 = (bf16[2,128,1024]{2,1,0:T(8,128)(2,1)}, bf16[2,128,1024]{2,1,0:T(8,128)(2,1)S(1)}, u32[]{:S(2)}) copy-start(bf16[2,128,1024]{2,1,0:T(8,128)(2,1)S(1)} %pad_maximum_fusion.3.refs_0_) | copy-start | bytes 1572868
  33.5 19.3 %collective-permute-start.2 = (bf16[2,128,1024]{2,1,0:T(8,128)(2,1)S(1)}, bf16[2,128,1024]{2,1,0:T(8,128)(2,1)S(1)}, u32[]{:S(2)}, u32[]{:S(2)}) collective-permute-start(bf16[2,128,1024]{2,1,0:T(8,128)(2,1)S(1)} %pad_maximum_fusion.3.refs_0_), channel_id=1, source_target_pairs={{0,1},{1,0},{2,3},{3,2},{4,5},{5,4},{6,7},{7,6},{8,9},{9,8},{10,11... | collective-permute-start | bytes 1572872 | tf_op jit(solution)/shard_map/ppermute | solution.py:121
  51.4 27.8 %copy-start.5 = (bf16[2,128,1024]{2,1,0:T(8,128)(2,1)}, bf16[2,128,1024]{2,1,0:T(8,128)(2,1)S(1)}, u32[]{:S(2)}) copy-start(bf16[2,128,1024]{2,1,0:T(8,128)(2,1)S(1)} %pad_maximum_fusion.4.refs_2_) | copy-start | bytes 1572868
  51.5 13.8 %collective-permute-start.5 = (bf16[2,128,1024]{2,1,0:T(8,128)(2,1)S(1)}, bf16[2,128,1024]{2,1,0:T(8,128)(2,1)S(1)}, u32[]{:S(2)}, u32[]{:S(2)}) collective-permute-start(bf16[2,128,1024]{2,1,0:T(8,128)(2,1)S(1)} %pad_maximum_fusion.4.refs_2_), channel_id=1, source_target_pairs={{0,1},{1,0},{2,3},{3,2},{4,5},{5,4},{6,7},{7,6},{8,9},{9,8},{10,11... | collective-permute-start | bytes 1572872 | tf_op jit(solution)/shard_map/ppermute | solution.py:121
  52.8 26.4 %copy-start.8 = (bf16[2,128,1024]{2,1,0:T(8,128)(2,1)}, bf16[2,128,1024]{2,1,0:T(8,128)(2,1)S(1)}, u32[]{:S(2)}) copy-start(bf16[2,128,1024]{2,1,0:T(8,128)(2,1)S(1)} %collective-permute-done.2.refs_1_) | copy-start | bytes 1572868
  65.3 14.0 %copy-start.9 = (bf16[2,128,1024]{2,1,0:T(8,128)(2,1)}, bf16[2,128,1024]{2,1,0:T(8,128)(2,1)S(1)}, u32[]{:S(2)}) copy-start(bf16[2,128,1024]{2,1,0:T(8,128)(2,1)S(1)} %collective-permute-done.5.refs_3_) | copy-start | bytes 1572868
  65.3 12.9 %collective-permute-start.6 = (bf16[512,512]{1,0:T(8,128)(2,1)S(1)}, bf16[512,512]{1,0:T(8,128)(2,1)S(1)}, u32[]{:S(2)}, u32[]{:S(2)}) collective-permute-start(bf16[512,512]{1,0:T(8,128)(2,1)S(1)} %copy-done.6), channel_id=1, source_target_pairs={{0,1},{1,0},{2,3},{3,2},{4,5},{5,4},{6,7},{7,6},{8,9},{9,8},{10,11... | collective-permute-start | bytes 1572872 | tf_op jit(solution)/shard_map/ppermute | solution.py:121
  86.7 40.3 %copy-start.1 = (f32[256,256]{1,0:T(8,128)S(1)}, f32[256,256]{1,0:T(8,128)}, u32[]{:S(2)}) copy-start(f32[256,256]{1,0:T(8,128)} %constant.236.clone.refs_5_) | copy-start | bytes 786436
  86.8 40.3 %copy-start.2 = (f32[128,256]{1,0:T(8,128)S(1)}, f32[128,256]{1,0:T(8,128)}, u32[]{:S(2)}) copy-start(f32[128,256]{1,0:T(8,128)} %constant.235.clone.refs_4_) | copy-start | bytes 393220
  130.8 19.3 %all-to-all-start.2 = ((bf16[32,32,256]{2,1,0:T(8,128)(2,1)}), bf16[32,32,256]{2,1,0:T(8,128)(2,1)S(1)}, u32[]{:S(2)}, u32[]{:S(2)}) async-start(bf16[32,32,256]{2,1,0:T(8,128)(2,1)} %bitcast.18), calls=%async_computation.2 | async-start | bytes 1048576 | tf_op jit(solution)/shard_map/all_to_all | solution.py:412
  157.3 20.5 %collective-permute-start.10 = (bf16[64,2048]{1,0:T(8,128)(2,1)S(1)}, bf16[64,2048]{1,0:T(8,128)(2,1)S(1)}, u32[]{:S(2)}, u32[]{:S(2)}) collective-permute-start(bf16[64,2048]{1,0:T(8,128)(2,1)S(1)} %get-tuple-element.23), channel_id=1, source_target_pairs={{0,24},{1,8},{2,26},{3,10},{4,28},{5,12},{6,30},{7,14},{8,16},{9,0... | collective-permute-start | bytes 786440 | tf_op jit(solution)/shard_map/ppermute | solution.py:74
  159.0 18.9 %collective-permute-start.9 = (bf16[64,2048]{1,0:T(8,128)(2,1)S(1)}, bf16[64,2048]{1,0:T(8,128)(2,1)S(1)}, u32[]{:S(2)}, u32[]{:S(2)}) collective-permute-start(bf16[64,2048]{1,0:T(8,128)(2,1)S(1)} %get-tuple-element.24), channel_id=1, source_target_pairs={{0,16},{1,0},{2,18},{3,2},{4,20},{5,4},{6,22},{7,6},{8,24},{9,8},{... | collective-permute-start | bytes 786440 | tf_op jit(solution)/shard_map/ppermute | solution.py:74
  159.0 20.5 %collective-permute-start.8 = (bf16[64,2048]{1,0:T(8,128)(2,1)S(1)}, bf16[64,2048]{1,0:T(8,128)(2,1)S(1)}, u32[]{:S(2)}, u32[]{:S(2)}) collective-permute-start(bf16[64,2048]{1,0:T(8,128)(2,1)S(1)} %get-tuple-element.25), channel_id=1, source_target_pairs={{0,8},{1,24},{2,10},{3,26},{4,12},{5,28},{6,14},{7,30},{8,0},{9,16... | collective-permute-start | bytes 786440 | tf_op jit(solution)/shard_map/ppermute | solution.py:74
  160.9 21.1 %collective-permute-start.7 = (bf16[64,2048]{1,0:T(8,128)(2,1)S(1)}, bf16[64,2048]{1,0:T(8,128)(2,1)S(1)}, u32[]{:S(2)}, u32[]{:S(2)}) collective-permute-start(bf16[64,2048]{1,0:T(8,128)(2,1)S(1)} %get-tuple-element.26), channel_id=1, source_target_pairs={{0,0},{1,16},{2,2},{3,18},{4,4},{5,20},{6,6},{7,22},{8,8},{9,24},{... | collective-permute-start | bytes 786440 | tf_op jit(solution)/shard_map/ppermute | solution.py:74
  (1 other events, 0.9 us)
Sparse Core Ops, SparseCore 0:
  8.9 48.8 all-gather.3
  79.4 50.2 all-gather.5

commit v7 on v6

--- a/solution.py
+++ b/solution.py
@@ -11,7 +11,6 @@
 
 HIGHEST = lax.Precision.HIGHEST
 UNROLL = 16
-CHUNKS = 2
 HEAVY = 30
 
 
@@ -50,31 +49,39 @@
     )(jnp.stack(places).astype(jnp.int32), *pieces)
 
 
-def return_output(out, outer, inner_parts, tp_parts):
-    _, part_rows, width = out.shape
+def return_places(outer, inner_parts, tp_parts):
     per_tp = outer // tp_parts
     tp_place = lax.axis_index("tp")
     outer_place = lax.axis_index("seq") // inner_parts
-    pieces, places = [], []
+    blocks, places = [], []
     for far in range(tp_parts):
         for near in range(per_tp):
-
-            def target(seq, tp):
-                src = seq // inner_parts
-                dst = (tp + far) % tp_parts * per_tp + (src % per_tp + near) % per_tp
-                return (dst * inner_parts + seq % inner_parts) * tp_parts + src // per_tp
-
-            pairs = [
-                (seq * tp_parts + tp, target(seq, tp))
-                for seq in range(outer * inner_parts)
-                for tp in range(tp_parts)
-            ]
-            block = (tp_place + far) % tp_parts * per_tp + (outer_place % per_tp + near) % per_tp
-            piece = lax.dynamic_index_in_dim(out, block, axis=0, keepdims=False)
-            pieces.append(lax.ppermute(piece, ("seq", "tp"), pairs))
+            blocks.append((tp_place + far) % tp_parts * per_tp + (outer_place % per_tp + near) % per_tp)
             places.append((outer_place // per_tp - far + tp_parts) % tp_parts)
             places.append((outer_place % per_tp - near + per_tp) % per_tp)
-    return assemble(pieces, places, (tp_parts * part_rows, per_tp * width))
+    return blocks, places
+
+
+def return_output(pieces, places, inner_parts, tp_parts):
+    outer = len(pieces)
+    part_rows, width = pieces[0].shape
+    per_tp = outer // tp_parts
+    arrived = []
+    for index, piece in enumerate(pieces):
+        far, near = divmod(index, per_tp)
+
+        def target(seq, tp):
+            src = seq // inner_parts
+            dst = (tp + far) % tp_parts * per_tp + (src % per_tp + near) % per_tp
+            return (dst * inner_parts + seq % inner_parts) * tp_parts + src // per_tp
+
+        pairs = [
+            (seq * tp_parts + tp, target(seq, tp))
+            for seq in range(outer * inner_parts)
+            for tp in range(tp_parts)
+        ]
+        arrived.append(lax.ppermute(piece, ("seq", "tp"), pairs))
+    return assemble(arrived, places, (tp_parts * part_rows, per_tp * width))
 
 
 def share_columns(features, outer, tp_parts):
@@ -124,42 +131,39 @@
 
 def project_kernel(tp_parts, place_ref, *refs):
     *share_refs, weight_ref, out_ref = refs
-    seq_parts, _, chans, _ = out_ref.shape
-    depth, rows, width = share_refs[0].shape
-    count = depth * rows
-    for chunk in range(len(share_refs) // tp_parts):
-        sums = jnp.zeros((count, seq_parts * chans), jnp.float32)
-        for step in range(tp_parts):
-            which = lax.rem(place_ref[0] - step + tp_parts, tp_parts)
-            sums = sums + jnp.dot(
-                share_refs[chunk * tp_parts + step][...].reshape(count, width),
-                weight_ref[0, which],
+    seq_parts, _, chans, count = out_ref.shape
+    inner_parts, _, chan_tp, width = weight_ref.shape
+    blocks = inner_parts // tp_parts
+    sums = jnp.zeros((chan_tp, count), jnp.float32)
+    for step in range(tp_parts):
+        which = lax.rem(place_ref[0] - step + tp_parts, tp_parts)
+        right = jnp.concatenate([share_ref[...] for share_ref in share_refs[step::tp_parts]])
+        for block in range(blocks):
+            sums = sums + lax.dot_general(
+                weight_ref[which * blocks + block, 0],
+                right[:, block * width : (block + 1) * width],
+                (((1,), (1,)), ((), ())),
                 preferred_element_type=jnp.float32,
             )
-        turned = sums.T.astype(out_ref.dtype)
-        for seq in range(seq_parts):
-            out_ref[seq, 0, :, chunk * count : (chunk + 1) * count] = turned[
-                seq * chans : (seq + 1) * chans
-            ]
+    done = sums.astype(out_ref.dtype)
+    for seq in range(seq_parts):
+        out_ref[seq, 0] = done[seq * chans : (seq + 1) * chans]
 
 
 def project_in(chunks, weight, seq_parts):
     tp_parts = len(chunks[0])
-    depth, rows, width = chunks[0][0].shape
-    streams, _, chan_tp = weight.shape
-    weight = weight.reshape(streams, tp_parts, width, chan_tp)
+    inner_parts, streams, chan_tp, width = weight.shape
     chans = chan_tp // seq_parts
-    count = len(chunks) * depth * rows
     pieces = [piece for chunk in chunks for piece in chunk]
+    count = len(chunks) * pieces[0].shape[0]
     place = lax.axis_index("tp").astype(jnp.int32)[None]
-    whole = pl.BlockSpec((depth, rows, width), lambda i, place: (0, 0, 0))
     return pl.pallas_call(
         functools.partial(project_kernel, tp_parts),
         grid_spec=pltpu.PrefetchScalarGridSpec(
             num_scalar_prefetch=1,
             grid=(streams,),
-            in_specs=[whole] * len(pieces)
-            + [pl.BlockSpec((1, tp_parts, width, chan_tp), lambda i, place: (i, 0, 0, 0))],
+            in_specs=[pl.BlockSpec(pieces[0].shape, lambda i, place: (0, 0))] * len(pieces)
+            + [pl.BlockSpec((inner_parts, 1, chan_tp, width), lambda i, place: (0, i, 0, 0))],
             out_specs=pl.BlockSpec((seq_parts, 1, chans, count), lambda i, place: (0, i, 0, 0)),
         ),
         out_shape=jax.ShapeDtypeStruct((seq_parts, streams, chans, count), jnp.bfloat16),
@@ -292,6 +296,7 @@
 
     tp_parts = out_ref.shape[0]
     part_rows = rows // tp_parts
+    copies = out_ref.shape[1]
 
     def spread(inner_index):
         for part in range(tp_parts):
@@ -302,7 +307,9 @@
                     shift = (place - part) * part_rows % rows
                     block = pltpu.roll(block, shift, 1) if shift else block
                     packed = jnp.where(lane // part_rows == place, block, packed)
-                out_ref[part, inner_index, :, group * rows : (group + 1) * rows] = packed.astype(out_ref.dtype)
+                packed = packed.astype(out_ref.dtype)
+                for copy in range(copies):
+                    out_ref[part, copy, inner_index, :, group * rows : (group + 1) * rows] = packed
 
     each(inner_parts, spread)
 
@@ -317,7 +324,7 @@
     return pl.pallas_call(
         functools.partial(conv_kernel, outer, len(parts)),
         out_shape=jax.ShapeDtypeStruct(
-            (tp_parts, blocks // outer, chans, outer // tp_parts * rows), jnp.bfloat16
+            (tp_parts, outer, blocks // outer, chans, outer // tp_parts * rows), jnp.bfloat16
         ),
         in_specs=[vmem] * (5 + len(parts)),
         out_specs=vmem,
@@ -335,39 +342,54 @@
     )(*parts, filter_blocks, taps, skip, jnp.asarray(forward), jnp.asarray(backward))
 
 
-def out_kernel(place_ref, gated_ref, weight_ref, out_ref):
+def out_kernel(block_ref, gated_ref, weight_ref, *refs):
+    *out_refs, turned, left = refs
     tp_parts = gated_ref.shape[0]
-    sums = jnp.zeros(out_ref.shape, jnp.float32)
-    for step in range(tp_parts):
-        which = lax.rem(place_ref[0] - step + tp_parts, tp_parts)
-        sums = sums + jnp.dot(gated_ref[which], weight_ref[0, step], preferred_element_type=jnp.float32)
-    out_ref[...] = sums.astype(out_ref.dtype)
-
-
-def project_out(gated, weight):
-    tp_parts, rows, depth = gated.shape
+    part_rows = out_refs[0].shape[0]
+
+    @pl.when(pl.program_id(0) == 0)
+    def _():
+        for part in range(tp_parts):
+            turned[...] = gated_ref[part].T
+            for index in range(len(out_refs)):
+                begin = pl.multiple_of(block_ref[index] * part_rows, part_rows)
+                left[part, index * part_rows : (index + 1) * part_rows] = turned[pl.ds(begin, part_rows)]
+
+    sums = jnp.zeros((left.shape[1], weight_ref.shape[3]), jnp.float32)
+    for part in range(tp_parts):
+        sums = sums + jnp.dot(left[part], weight_ref[0, part], preferred_element_type=jnp.float32)
+    for index, out_ref in enumerate(out_refs):
+        out_ref[...] = sums[index * part_rows : (index + 1) * part_rows].astype(out_ref.dtype)
+
+
+def project_out(gated, weight, blocks):
+    tp_parts, depth, rows = gated.shape
     inner_parts, _, _, width = weight.shape
     columns = inner_parts * width
-    place = lax.axis_index("tp").astype(jnp.int32)[None]
+    part_rows = rows // len(blocks)
     return pl.pallas_call(
         out_kernel,
         grid_spec=pltpu.PrefetchScalarGridSpec(
             num_scalar_prefetch=1,
             grid=(inner_parts,),
             in_specs=[
-                pl.BlockSpec((tp_parts, rows, depth), lambda b, place: (0, 0, 0)),
+                pl.BlockSpec((tp_parts, depth, rows), lambda b, place: (0, 0, 0)),
                 pl.BlockSpec((1, tp_parts, depth, width), lambda b, place: (b, 0, 0, 0)),
             ],
-            out_specs=pl.BlockSpec((rows, width), lambda b, place: (0, b)),
-        ),
-        out_shape=jax.ShapeDtypeStruct((rows, columns), jnp.bfloat16),
+            out_specs=[pl.BlockSpec((part_rows, width), lambda b, place: (0, b))] * len(blocks),
+            scratch_shapes=[
+                pltpu.VMEM((rows, depth), jnp.bfloat16),
+                pltpu.VMEM((tp_parts, rows, depth), jnp.bfloat16),
+            ],
+        ),
+        out_shape=[jax.ShapeDtypeStruct((part_rows, columns), jnp.bfloat16)] * len(blocks),
         compiler_params=pltpu.CompilerParams(vmem_limit_bytes=56 * 2**20),
         cost_estimate=pl.CostEstimate(
             flops=2 * gated.size * columns,
             bytes_accessed=2 * (weight.size + gated.size + rows * columns),
             transcendentals=0,
         ),
-    )(place, gated, weight)
+    )(jnp.stack(blocks).astype(jnp.int32), gated, weight)
 
 
 def per_device(features, in_proj, short_taps, long_filter, skip_gain, out_proj):
@@ -380,9 +402,11 @@
     chans = chan_tp // seq_parts
     position = lax.axis_index("seq")
     inner_groups = [[a * inner_parts + b for b in range(inner_parts)] for a in range(outer)]
-    outer_groups = [[a * inner_parts + b for a in range(outer)] for b in range(inner_parts)]
-
-    weight = lax.all_gather(in_proj, "seq", axis=1, tiled=True, axis_index_groups=inner_groups)
+    tp_groups = [
+        [index * tp_parts + tp for index in group for tp in range(tp_parts)] for group in inner_groups
+    ]
+
+    weight = lax.all_gather(jnp.swapaxes(in_proj, 1, 2), "seq", axis_index_groups=inner_groups)
 
     filter_blocks = lax.all_to_all(
         long_filter.T.reshape(seq_parts, chans, rows), "seq", split_axis=0, concat_axis=0, tiled=True
@@ -395,26 +419,21 @@
     held = share_columns(features, outer, tp_parts)
     held, filter_blocks, taps, skip = lax.optimization_barrier((held, filter_blocks, taps, skip))
     arrived = cross_outer(held, outer, inner_parts, tp_parts)
-    depth = outer // CHUNKS
-    chunks = [
-        share_over_tp(jnp.stack(arrived[index * depth : (index + 1) * depth]), tp_parts)
-        for index in range(CHUNKS)
-    ]
+    chunks = [share_over_tp(piece, tp_parts) for piece in arrived]
     chunks, out_proj = lax.optimization_barrier((chunks, out_proj))
+    out_weight = lax.all_gather(out_proj, ("seq", "tp"), axis_index_groups=tp_groups)
+    out_weight = out_weight.reshape((inner_parts, tp_parts) + out_proj.shape)
 
     partial = project_in(chunks, weight, seq_parts)
     parts = lax.all_to_all(partial, "seq", split_axis=0, concat_axis=0, tiled=True)
-    out_block = jnp.stack(share_over_tp(out_proj, tp_parts))
-    out_weight = lax.all_gather(out_block, "seq", axis_index_groups=inner_groups)
 
     gated = convolve([parts], filter_blocks, taps, skip, outer, tp_parts)
-    gated = jnp.broadcast_to(gated[:, None], (tp_parts, outer) + gated.shape[1:])
     gated = lax.all_to_all(
         gated.reshape((-1,) + gated.shape[3:]), ("tp", "seq"), split_axis=0, concat_axis=0, tiled=True
     )
-    gated = jnp.swapaxes(gated.reshape(tp_parts, chan_tp, -1), 1, 2)
-    out = project_out(gated, out_weight)
-    return return_output(out.reshape(outer, rows // tp_parts, -1), outer, inner_parts, tp_parts)
+    blocks, places = return_places(outer, inner_parts, tp_parts)
+    pieces = project_out(gated.reshape(tp_parts, chan_tp, -1), out_weight, blocks)
+    return return_output(pieces, places, inner_parts, tp_parts)
 
 
 def solution(mesh):

time: 195 us -> 185 us (0.949); the launches traced: 191 us -> 184 us
  waiting for transfers between devices: 82.6 us -> 69.4 us
  blocking collectives: 40.3 us -> 44.2 us
    ppermute x3 -> x4, waiting for transfers between devices: 24.1 us -> 7.78 us  [share_over_tp(): pieces.append(lax.ppermute(part, 'tp', pairs))]
    ppermute x4, waiting for transfers between devices: 15.2 us -> 22 us  [return_output(): arrived.append(lax.ppermute(piece, ('seq', 'tp'), pairs))]
    unnamed x20 -> x29, local copies, waits for them, and re-layouts: 0.74 us -> 5.41 us
    all_to_all x1, blocking collectives: 40.3 us -> 44.2 us  [per_device(): lax.all_to_all(partial, 'seq', split_axis=0, concat_axis=0, tiled=True)]
    ppermute x3, waiting for transfers between devices: 21.3 us -> 18.8 us  [cross_outer(): lax.ppermute(piece, 'seq', [(i, (i + far) % seq_parts) for i in range(seq...]
    ppermute x3 -> x4, starting transfers between devices: 3.97 us -> 5.17 us  [share_over_tp(): pieces.append(lax.ppermute(part, 'tp', pairs))]
  transfers between devices with their start and end apart: 15 -> 16, of which waited for: 11 -> 11; matrix products, arithmetic and copies ran while one was open for 3% -> 2% of each run, Pallas kernels for 5% -> 6%
where the time goes in v7:
time: 185 us; the launch traced here: 184 us
  waiting for transfers between devices  69.4 us (38%)
  blocking collectives  44.2 us (24%)
  starting transfers between devices  29.7 us (16%)
  Pallas kernels  19 us (10%)
  between operations  13.9 us (8%)
  local copies, waits for them, and re-layouts  7.48 us (4%)
    all_to_all x1, blocking collectives, per_device(): lax.all_to_all(partial, 'seq', split_axis=0, concat_axis=0, tiled=True)  44.2 us
    ppermute x4, waiting for transfers between devices, return_output(): arrived.append(lax.ppermute(piece, ('seq', 'tp'), pairs))  22 us
    ppermute x3, waiting for transfers between devices, cross_outer(): lax.ppermute(piece, 'seq', [(i, (i + far) % seq_parts) for i in range(seq...  18.8 us
    all_to_all x1, waiting for transfers between devices, per_device(): lax.all_to_all(gated.reshape((-1,) + gated.shape[3:]), ('tp', 'seq'), spl...  13.9 us
    ppermute x4, starting transfers between devices, return_output(): arrived.append(lax.ppermute(piece, ('seq', 'tp'), pairs))  8.45 us
    ppermute x4, waiting for transfers between devices, share_over_tp(): pieces.append(lax.ppermute(part, 'tp', pairs))  7.78 us
    pallas_call x1, Pallas kernels, project_in(): pl.pallas_call(functools.partial(project_kernel, tp_parts), grid_spec=plt...  7.36 us
    all_to_all x1, starting transfers between devices, per_device(): lax.all_to_all(long_filter.T.reshape(seq_parts, chans, rows), 'seq', spli...  6.27 us
  transfers between devices with their start and end apart: 16, of which 11 were waited for; matrix products, arithmetic and copies ran while one was open for 2% of the time, Pallas kernels for 6%

profile of v7, /device:TPU:12, one launch (start us, length us, event | category | flops | bytes accessed | tf_op | source)
XLA Modules:
  0.0 184.4 jit_solution(6185133931040421573)
XLA Ops:
  6.5 2.6 %copy.12 = bf16[3,512,512]{1,2,0:T(8,128)(2,1)} copy(bf16[3,512,512]{2,1,0:T(8,128)(2,1)} %param.9) | data formatting | bytes 3145728 | tf_op args[1]
  12.2 6.3 %all-to-all-start = ((f32[16,32,128]{2,1,0:T(8,128)}), f32[16,32,128]{2,1,0:T(8,128)S(1)}, u32[]{:S(2)}, u32[]{:S(2)}) async-start(f32[16,32,128]{2,1,0:T(8,128)} %bitcast.14), calls=%async_computation | async-start | bytes 524288 | tf_op jit(solution)/shard_map/all_to_all | solution.py:411
  19.6 4.7 %collective-permute-done = bf16[2,128,1024]{2,1,0:T(8,128)(2,1)S(1)} collective-permute-done((bf16[2,128,1024]{2,1,0:T(8,128)(2,1)S(1)}, bf16[2,128,1024]{2,1,0:T(8,128)(2,1)S(1)}, u32[]{:S(2)}, u32[]{:S(2)}) %collective-permute-start) | collective-permute-done | bytes 524320 | tf_op jit(solution)/shard_map/ppermute | solution.py:102
  24.4 2.2 %all-to-all-done.refs_1_ = f32[16,32,128]{2,1,0:T(8,128)S(1)} async-done(((f32[16,32,128]{2,1,0:T(8,128)}), f32[16,32,128]{2,1,0:T(8,128)S(1)}, u32[]{:S(2)}, u32[]{:S(2)}) %all-to-all-start) | async-done | bytes 262176 | tf_op jit(solution)/shard_map/all_to_all | solution.py:411
  26.8 1.7 collective-permute-start.2
  28.5 2.8 %collective-permute-start.4 = (bf16[128,1024]{1,0:T(8,128)(2,1)S(1)}, bf16[128,1024]{1,0:T(8,128)(2,1)S(1)}, u32[]{:S(2)}, u32[]{:S(2)}) collective-permute-start(bf16[128,1024]{1,0:T(8,128)(2,1)S(1)} %get-tuple-element.40), channel_id=1, source_target_pairs={{0,16},{2,18},{4,20},{6,22},{8,24},{10,26},{12,28},{14,30},{16,0},... | collective-permute-start | bytes 786440 | tf_op jit(solution)/shard_map/ppermute | solution.py:119
  32.6 3.5 %collective-permute-done.2.refs_2_ = bf16[128,1024]{1,0:T(8,128)(2,1)S(1)} collective-permute-done((bf16[128,1024]{1,0:T(8,128)(2,1)S(1)}, bf16[128,1024]{1,0:T(8,128)(2,1)S(1)}, u32[]{:S(2)}, u32[]{:S(2)}) %collective-permute-start.2) | collective-permute-done | bytes 262176 | tf_op jit(solution)/shard_map/ppermute | solution.py:119
  37.4 13.3 %collective-permute-done.4.refs_4_ = bf16[128,1024]{1,0:T(8,128)(2,1)S(1)} collective-permute-done((bf16[128,1024]{1,0:T(8,128)(2,1)S(1)}, bf16[128,1024]{1,0:T(8,128)(2,1)S(1)}, u32[]{:S(2)}, u32[]{:S(2)}) %collective-permute-start.4) | collective-permute-done | bytes 262176 | tf_op jit(solution)/shard_map/ppermute | solution.py:119
  51.9 2.1 %collective-permute-done.6.refs_6_ = bf16[128,1024]{1,0:T(8,128)(2,1)S(1)} collective-permute-done((bf16[128,1024]{1,0:T(8,128)(2,1)S(1)}, bf16[128,1024]{1,0:T(8,128)(2,1)S(1)}, u32[]{:S(2)}, u32[]{:S(2)}) %collective-permute-start.6) | collective-permute-done | bytes 262176 | tf_op jit(solution)/shard_map/ppermute | solution.py:119
  55.3 3.1 %collective-permute-done.5.refs_5_ = bf16[128,1024]{1,0:T(8,128)(2,1)S(1)} collective-permute-done((bf16[128,1024]{1,0:T(8,128)(2,1)S(1)}, bf16[128,1024]{1,0:T(8,128)(2,1)S(1)}, u32[]{:S(2)}, u32[]{:S(2)}) %collective-permute-start.5) | collective-permute-done | bytes 262176 | tf_op jit(solution)/shard_map/ppermute | solution.py:128
  58.4 4.7 %collective-permute-done.7.refs_7_ = bf16[128,1024]{1,0:T(8,128)(2,1)S(1)} collective-permute-done((bf16[128,1024]{1,0:T(8,128)(2,1)S(1)}, bf16[128,1024]{1,0:T(8,128)(2,1)S(1)}, u32[]{:S(2)}, u32[]{:S(2)}) %collective-permute-start.7) | collective-permute-done | bytes 262176 | tf_op jit(solution)/shard_map/ppermute | solution.py:128
  63.8 7.4 %shard_map.82 = bf16[16,3,32,512]{3,2,1,0:T(8,128)(2,1)} custom-call(s32[1]{0:T(128)} %bitcast.8.place_ref, bf16[128,1024]{1,0:T(8,128)(2,1)} %copy-done.5, bf16[128,1024]{1,0:T(8,128)(2,1)} %copy-done.10, bf16[128,1024]{1,0:T(8,128)(2,1)} %copy-done.7, bf16[128,1024]{1,0:T(8,128)(2,1)} %copy-done.11, bf16[128,1024]{1,0:T(8,128)(2,1)} %copy-done.8, ...), custom_call_target="tpu_custom_call" | custom-call | flops 96636764160 | bytes 9961472 | tf_op jit(solution)/shard_map/pallas_call | solution.py:160
  71.1 44.2 %all_to_all.15.refs_0_ = bf16[16,3,32,512]{3,2,1,0:T(8,128)(2,1)S(1)} all-to-all(bf16[16,3,32,512]{3,2,1,0:T(8,128)(2,1)} %shard_map.82), channel_id=1, replica_groups=mesh['seq'=16,'tp'=2] {'seq'}, dimensions={0} | all-to-all | bytes 3145728 | tf_op jit(solution)/shard_map/all_to_all | solution.py:428
  115.3 3.7 %shard_map.83 = bf16[2,4,4,32,256]{4,3,2,1,0:T(8,128)(2,1)} custom-call(bf16[16,3,32,512]{3,2,1,0:T(8,128)(2,1)S(1)} %all_to_all.15.refs_0_, f32[16,32,128]{2,1,0:T(8,128)S(1)} %all-to-all-done.refs_1_, f32[3,3,32,128]{3,2,1,0:T(8,128)S(1)} %broadcast_in_dim.7.refs_2_, f32[32,128]{1,0:T(8,128)S(1)} %broadcast_in_dim.8.refs_3_, f32[128,256]{1,0:T(8,128)S(1)} %copy-done.2, ...), custom_call_target="tpu_custom_call" | custom-call | flops 1000000000 | bytes 4194304 | tf_op jit(solution)/shard_map/pallas_call | solution.py:324
  119.0 4.7 %all-to-all-start.2 = ((bf16[32,32,256]{2,1,0:T(8,128)(2,1)}), bf16[32,32,256]{2,1,0:T(8,128)(2,1)S(1)}, u32[]{:S(2)}, u32[]{:S(2)}) async-start(bf16[32,32,256]{2,1,0:T(8,128)(2,1)} %bitcast.21), calls=%async_computation.2 | async-start | bytes 1048576 | tf_op jit(solution)/shard_map/all_to_all | solution.py:431
  124.4 13.9 %all-to-all-done.2 = bf16[32,32,256]{2,1,0:T(8,128)(2,1)S(1)} async-done(((bf16[32,32,256]{2,1,0:T(8,128)(2,1)}), bf16[32,32,256]{2,1,0:T(8,128)(2,1)S(1)}, u32[]{:S(2)}, u32[]{:S(2)}) %all-to-all-start.2) | async-done | bytes 524320 | tf_op jit(solution)/shard_map/all_to_all | solution.py:431
  139.1 5.7 %shard_map.84 = (bf16[64,2048]{1,0:T(8,128)(2,1)}, bf16[64,2048]{1,0:T(8,128)(2,1)}, bf16[64,2048]{1,0:T(8,128)(2,1)}, bf16[64,2048]{1,0:T(8,128)(2,1)}) custom-call(s32[4]{0:T(128)} %pad_add_fusion.block_ref, bf16[2,512,256]{2,1,0:T(8,128)(2,1)} %bitcast.34, bf16[4,2,512,512]{3,2,1,0:T(8,128)(2,1)} %bitcast.33), custom_call_target="tpu_custom_call" | custom-call | flops 1073741824 | bytes 5767168 | tf_op jit(solution)/shard_map/pallas_call | solution.py:370
  144.9 4.0 %collective-permute-start.8 = (bf16[64,2048]{1,0:T(8,128)(2,1)}, bf16[64,2048]{1,0:T(8,128)(2,1)S(1)}, u32[]{:S(2)}, u32[]{:S(2)}) collective-permute-start(bf16[64,2048]{1,0:T(8,128)(2,1)} %get-tuple-element.35), channel_id=1, source_target_pairs={{0,0},{1,16},{2,2},{3,18},{4,4},{5,20},{6,6},{7,22},{8,8},{9,24},{... | collective-permute-start | bytes 786440 | tf_op jit(solution)/shard_map/ppermute | solution.py:83
  148.9 1.5 collective-permute-start.9
  150.4 3.0 %collective-permute-start.11 = (bf16[64,2048]{1,0:T(8,128)(2,1)}, bf16[64,2048]{1,0:T(8,128)(2,1)S(1)}, u32[]{:S(2)}, u32[]{:S(2)}) collective-permute-start(bf16[64,2048]{1,0:T(8,128)(2,1)} %get-tuple-element.38), channel_id=1, source_target_pairs={{0,24},{1,8},{2,26},{3,10},{4,28},{5,12},{6,30},{7,14},{8,16},{9,0... | collective-permute-start | bytes 786440 | tf_op jit(solution)/shard_map/ppermute | solution.py:83
  153.4 12.4 %collective-permute-done.8.refs_0_ = bf16[64,2048]{1,0:T(8,128)(2,1)S(1)} collective-permute-done((bf16[64,2048]{1,0:T(8,128)(2,1)}, bf16[64,2048]{1,0:T(8,128)(2,1)S(1)}, u32[]{:S(2)}, u32[]{:S(2)}) %collective-permute-start.8) | collective-permute-done | bytes 262176 | tf_op jit(solution)/shard_map/ppermute | solution.py:83
  165.8 7.1 %collective-permute-done.9.refs_1_ = bf16[64,2048]{1,0:T(8,128)(2,1)S(1)} collective-permute-done((bf16[64,2048]{1,0:T(8,128)(2,1)}, bf16[64,2048]{1,0:T(8,128)(2,1)S(1)}, u32[]{:S(2)}, u32[]{:S(2)}) %collective-permute-start.9) | collective-permute-done | bytes 262176 | tf_op jit(solution)/shard_map/ppermute | solution.py:83
  172.9 2.5 %collective-permute-done.11.refs_3_ = bf16[64,2048]{1,0:T(8,128)(2,1)S(1)} collective-permute-done((bf16[64,2048]{1,0:T(8,128)(2,1)}, bf16[64,2048]{1,0:T(8,128)(2,1)S(1)}, u32[]{:S(2)}, u32[]{:S(2)}) %collective-permute-start.11) | collective-permute-done | bytes 262176 | tf_op jit(solution)/shard_map/ppermute | solution.py:83
  175.4 2.1 %shard_map.85 = bf16[128,4096]{1,0:T(8,128)(2,1)} custom-call(s32[8]{0:T(128)S(1)} %stack.53.place_ref, bf16[64,2048]{1,0:T(8,128)(2,1)S(1)} %collective-permute-done.8.refs_0_, bf16[64,2048]{1,0:T(8,128)(2,1)S(1)} %collective-permute-done.9.refs_1_, bf16[64,2048]{1,0:T(8,128)(2,1)S(1)} %collective-permute-done.10.refs_2_, ...), custom_call_target="tpu_custom_call" | custom-call | bytes 2097152 | tf_op jit(solution)/shard_map/pallas_call | solution.py:34
  (55 shorter events, 11.5 us)
Async XLA Ops:
  6.5 13.0 %copy-start = (f32[3,3,512]{2,1,0:T(4,128)S(1)}, f32[3,3,512]{2,1,0:T(4,128)}, u32[]{:S(2)}) copy-start(f32[3,3,512]{2,1,0:T(4,128)} %param.10) | copy-start | bytes 55300
  6.5 56.6 %all-gather.5.cloned.1.call-start = ((), (), s32[]{:S(2)}) async-start(), calls=%async_computation.3 | async-start | bytes 7864320 | tf_op jit(solution)/shard_map/all_gather | solution.py:409
  10.5 13.7 %collective-permute-start = (bf16[2,128,1024]{2,1,0:T(8,128)(2,1)S(1)}, bf16[2,128,1024]{2,1,0:T(8,128)(2,1)S(1)}, u32[]{:S(2)}, u32[]{:S(2)}) collective-permute-start(bf16[2,128,1024]{2,1,0:T(8,128)(2,1)S(1)} %pad_maximum_fusion.1), channel_id=1, source_target_pairs={{0,1},{1,0},{2,3},{3,2},{4,5},{5,4},{6,7},{7,6},{8,9},{9,8},{10,11... | collective-permute-start | bytes 1572872 | tf_op jit(solution)/shard_map/ppermute | solution.py:102
  12.2 14.4 %all-to-all-start = ((f32[16,32,128]{2,1,0:T(8,128)}), f32[16,32,128]{2,1,0:T(8,128)S(1)}, u32[]{:S(2)}, u32[]{:S(2)}) async-start(f32[16,32,128]{2,1,0:T(8,128)} %bitcast.14), calls=%async_computation | async-start | bytes 524288 | tf_op jit(solution)/shard_map/all_to_all | solution.py:411
  18.4 106.0 %all-gather.7.cloned.1.call-start = ((), (), s32[]{:S(2)}) async-start(), calls=%async_computation.4 | async-start | bytes 4718592 | tf_op jit(solution)/shard_map/all_gather | solution.py:424
  26.8 36.3 %copy-start.5 = (bf16[128,1024]{1,0:T(8,128)(2,1)}, bf16[128,1024]{1,0:T(8,128)(2,1)S(1)}, u32[]{:S(2)}) copy-start(bf16[128,1024]{1,0:T(8,128)(2,1)S(1)} %get-tuple-element.23.refs_0_) | copy-start | bytes 786436
  26.8 9.2 %collective-permute-start.2 = (bf16[128,1024]{1,0:T(8,128)(2,1)S(1)}, bf16[128,1024]{1,0:T(8,128)(2,1)S(1)}, u32[]{:S(2)}, u32[]{:S(2)}) collective-permute-start(bf16[128,1024]{1,0:T(8,128)(2,1)S(1)} %get-tuple-element.41), channel_id=1, source_target_pairs={{0,8},{2,10},{4,12},{6,14},{8,16},{10,18},{12,20},{14,22},{16,24},... | collective-permute-start | bytes 786440 | tf_op jit(solution)/shard_map/ppermute | solution.py:119
  28.5 22.1 %collective-permute-start.4 = (bf16[128,1024]{1,0:T(8,128)(2,1)S(1)}, bf16[128,1024]{1,0:T(8,128)(2,1)S(1)}, u32[]{:S(2)}, u32[]{:S(2)}) collective-permute-start(bf16[128,1024]{1,0:T(8,128)(2,1)S(1)} %get-tuple-element.40), channel_id=1, source_target_pairs={{0,16},{2,18},{4,20},{6,22},{8,24},{10,26},{12,28},{14,30},{16,0},... | collective-permute-start | bytes 786440 | tf_op jit(solution)/shard_map/ppermute | solution.py:119
  31.3 22.7 %collective-permute-start.6 = (bf16[128,1024]{1,0:T(8,128)(2,1)S(1)}, bf16[128,1024]{1,0:T(8,128)(2,1)S(1)}, u32[]{:S(2)}, u32[]{:S(2)}) collective-permute-start(bf16[128,1024]{1,0:T(8,128)(2,1)S(1)} %get-tuple-element.39), channel_id=1, source_target_pairs={{0,24},{2,26},{4,28},{6,30},{8,0},{10,2},{12,4},{14,6},{16,8},{18,... | collective-permute-start | bytes 786440 | tf_op jit(solution)/shard_map/ppermute | solution.py:119
  31.3 24.0 %collective-permute-start.1 = (bf16[128,1024]{1,0:T(8,128)(2,1)S(1)}, bf16[128,1024]{1,0:T(8,128)(2,1)S(1)}, u32[]{:S(2)}, u32[]{:S(2)}) collective-permute-start(bf16[128,1024]{1,0:T(8,128)(2,1)S(1)} %get-tuple-element.23.refs_0_), channel_id=1, source_target_pairs={{0,1},{1,0},{2,3},{3,2},{4,5},{5,4},{6,7},{7,6},{8,9},{9,8},{10,11... | collective-permute-start | bytes 786440 | tf_op jit(solution)/shard_map/ppermute | solution.py:128
  36.1 27.1 %copy-start.7 = (bf16[128,1024]{1,0:T(8,128)(2,1)}, bf16[128,1024]{1,0:T(8,128)(2,1)S(1)}, u32[]{:S(2)}) copy-start(bf16[128,1024]{1,0:T(8,128)(2,1)S(1)} %collective-permute-done.2.refs_2_) | copy-start | bytes 786436
  36.1 19.2 %collective-permute-start.3 = (bf16[128,1024]{1,0:T(8,128)(2,1)S(1)}, bf16[128,1024]{1,0:T(8,128)(2,1)S(1)}, u32[]{:S(2)}, u32[]{:S(2)}) collective-permute-start(bf16[128,1024]{1,0:T(8,128)(2,1)S(1)} %collective-permute-done.2.refs_2_), channel_id=1, source_target_pairs={{0,1},{1,0},{2,3},{3,2},{4,5},{5,4},{6,7},{7,6},{8,9},{9,8},{10,11... | collective-permute-start | bytes 786440 | tf_op jit(solution)/shard_map/ppermute | solution.py:128
  50.6 12.5 %copy-start.8 = (bf16[128,1024]{1,0:T(8,128)(2,1)}, bf16[128,1024]{1,0:T(8,128)(2,1)S(1)}, u32[]{:S(2)}) copy-start(bf16[128,1024]{1,0:T(8,128)(2,1)S(1)} %collective-permute-done.4.refs_4_) | copy-start | bytes 786436
  50.6 7.7 %collective-permute-start.5 = (bf16[128,1024]{1,0:T(8,128)(2,1)S(1)}, bf16[128,1024]{1,0:T(8,128)(2,1)S(1)}, u32[]{:S(2)}, u32[]{:S(2)}) collective-permute-start(bf16[128,1024]{1,0:T(8,128)(2,1)S(1)} %collective-permute-done.4.refs_4_), channel_id=1, source_target_pairs={{0,1},{1,0},{2,3},{3,2},{4,5},{5,4},{6,7},{7,6},{8,9},{9,8},{10,11... | collective-permute-start | bytes 786440 | tf_op jit(solution)/shard_map/ppermute | solution.py:128
  54.0 9.2 %copy-start.9 = (bf16[128,1024]{1,0:T(8,128)(2,1)}, bf16[128,1024]{1,0:T(8,128)(2,1)S(1)}, u32[]{:S(2)}) copy-start(bf16[128,1024]{1,0:T(8,128)(2,1)S(1)} %collective-permute-done.6.refs_6_) | copy-start | bytes 786436
  54.0 9.1 %collective-permute-start.7 = (bf16[128,1024]{1,0:T(8,128)(2,1)S(1)}, bf16[128,1024]{1,0:T(8,128)(2,1)S(1)}, u32[]{:S(2)}, u32[]{:S(2)}) collective-permute-start(bf16[128,1024]{1,0:T(8,128)(2,1)S(1)} %collective-permute-done.6.refs_6_), channel_id=1, source_target_pairs={{0,1},{1,0},{2,3},{3,2},{4,5},{5,4},{6,7},{7,6},{8,9},{9,8},{10,11... | collective-permute-start | bytes 786440 | tf_op jit(solution)/shard_map/ppermute | solution.py:128
  55.3 7.9 %copy-start.11 = (bf16[128,1024]{1,0:T(8,128)(2,1)}, bf16[128,1024]{1,0:T(8,128)(2,1)S(1)}, u32[]{:S(2)}) copy-start(bf16[128,1024]{1,0:T(8,128)(2,1)S(1)} %collective-permute-done.3.refs_3_) | copy-start | bytes 786436
  71.1 44.2 %copy-start.1 = (f32[256,256]{1,0:T(8,128)S(1)}, f32[256,256]{1,0:T(8,128)}, u32[]{:S(2)}) copy-start(f32[256,256]{1,0:T(8,128)} %constant.226.clone.refs_5_) | copy-start | bytes 786436
  71.1 44.2 %copy-start.2 = (f32[128,256]{1,0:T(8,128)S(1)}, f32[128,256]{1,0:T(8,128)}, u32[]{:S(2)}) copy-start(f32[128,256]{1,0:T(8,128)} %constant.225.clone.refs_4_) | copy-start | bytes 393220
  119.0 19.3 %all-to-all-start.2 = ((bf16[32,32,256]{2,1,0:T(8,128)(2,1)}), bf16[32,32,256]{2,1,0:T(8,128)(2,1)S(1)}, u32[]{:S(2)}, u32[]{:S(2)}) async-start(bf16[32,32,256]{2,1,0:T(8,128)(2,1)} %bitcast.21), calls=%async_computation.2 | async-start | bytes 1048576 | tf_op jit(solution)/shard_map/all_to_all | solution.py:431
  144.9 20.9 %collective-permute-start.8 = (bf16[64,2048]{1,0:T(8,128)(2,1)}, bf16[64,2048]{1,0:T(8,128)(2,1)S(1)}, u32[]{:S(2)}, u32[]{:S(2)}) collective-permute-start(bf16[64,2048]{1,0:T(8,128)(2,1)} %get-tuple-element.35), channel_id=1, source_target_pairs={{0,0},{1,16},{2,2},{3,18},{4,4},{5,20},{6,6},{7,22},{8,8},{9,24},{... | collective-permute-start | bytes 786440 | tf_op jit(solution)/shard_map/ppermute | solution.py:83
  148.9 24.1 %collective-permute-start.9 = (bf16[64,2048]{1,0:T(8,128)(2,1)}, bf16[64,2048]{1,0:T(8,128)(2,1)S(1)}, u32[]{:S(2)}, u32[]{:S(2)}) collective-permute-start(bf16[64,2048]{1,0:T(8,128)(2,1)} %get-tuple-element.36), channel_id=1, source_target_pairs={{0,8},{1,24},{2,10},{3,26},{4,12},{5,28},{6,14},{7,30},{8,0},{9,16... | collective-permute-start | bytes 786440 | tf_op jit(solution)/shard_map/ppermute | solution.py:83
  150.4 22.6 %collective-permute-start.10 = (bf16[64,2048]{1,0:T(8,128)(2,1)}, bf16[64,2048]{1,0:T(8,128)(2,1)S(1)}, u32[]{:S(2)}, u32[]{:S(2)}) collective-permute-start(bf16[64,2048]{1,0:T(8,128)(2,1)} %get-tuple-element.37), channel_id=1, source_target_pairs={{0,16},{1,0},{2,18},{3,2},{4,20},{5,4},{6,22},{7,6},{8,24},{9,8},{... | collective-permute-start | bytes 786440 | tf_op jit(solution)/shard_map/ppermute | solution.py:83
  150.4 25.1 %collective-permute-start.11 = (bf16[64,2048]{1,0:T(8,128)(2,1)}, bf16[64,2048]{1,0:T(8,128)(2,1)S(1)}, u32[]{:S(2)}, u32[]{:S(2)}) collective-permute-start(bf16[64,2048]{1,0:T(8,128)(2,1)} %get-tuple-element.38), channel_id=1, source_target_pairs={{0,24},{1,8},{2,26},{3,10},{4,28},{5,12},{6,30},{7,14},{8,16},{9,0... | collective-permute-start | bytes 786440 | tf_op jit(solution)/shard_map/ppermute | solution.py:83
  (6 other events, 16.4 us)
Sparse Core Ops, SparseCore 0:
  9.3 49.9 all-gather.4
  63.2 46.8 all-gather.6

commit v8 on v7

--- a/solution.py
+++ b/solution.py
@@ -56,9 +56,11 @@
     blocks, places = [], []
     for far in range(tp_parts):
         for near in range(per_tp):
-            blocks.append((tp_place + far) % tp_parts * per_tp + (outer_place % per_tp + near) % per_tp)
-            places.append((outer_place // per_tp - far + tp_parts) % tp_parts)
-            places.append((outer_place % per_tp - near + per_tp) % per_tp)
+            low = outer_place % per_tp
+            blocks.append((tp_place + low + far) % tp_parts * per_tp + (low + near) % per_tp)
+            low = (low - near + per_tp) % per_tp
+            places.append((outer_place // per_tp - far - low + tp_parts + per_tp * tp_parts) % tp_parts)
+            places.append(low)
     return blocks, places
 
 
@@ -72,7 +74,8 @@
 
         def target(seq, tp):
             src = seq // inner_parts
-            dst = (tp + far) % tp_parts * per_tp + (src % per_tp + near) % per_tp
+            low = src % per_tp
+            dst = (tp + low + far) % tp_parts * per_tp + (low + near) % per_tp
             return (dst * inner_parts + seq % inner_parts) * tp_parts + src // per_tp
 
         pairs = [
@@ -132,38 +135,32 @@
 def project_kernel(tp_parts, place_ref, *refs):
     *share_refs, weight_ref, out_ref = refs
     seq_parts, _, chans, count = out_ref.shape
-    inner_parts, _, chan_tp, width = weight_ref.shape
-    blocks = inner_parts // tp_parts
-    sums = jnp.zeros((chan_tp, count), jnp.float32)
+    sums = jnp.zeros((count, seq_parts * chans), jnp.float32)
     for step in range(tp_parts):
         which = lax.rem(place_ref[0] - step + tp_parts, tp_parts)
-        right = jnp.concatenate([share_ref[...] for share_ref in share_refs[step::tp_parts]])
-        for block in range(blocks):
-            sums = sums + lax.dot_general(
-                weight_ref[which * blocks + block, 0],
-                right[:, block * width : (block + 1) * width],
-                (((1,), (1,)), ((), ())),
-                preferred_element_type=jnp.float32,
-            )
-    done = sums.astype(out_ref.dtype)
+        left = jnp.concatenate([share_ref[...] for share_ref in share_refs[step::tp_parts]])
+        sums = sums + jnp.dot(left, weight_ref[0, which], preferred_element_type=jnp.float32)
+    turned = sums.astype(out_ref.dtype).T
     for seq in range(seq_parts):
-        out_ref[seq, 0] = done[seq * chans : (seq + 1) * chans]
+        out_ref[seq, 0] = turned[seq * chans : (seq + 1) * chans]
 
 
 def project_in(chunks, weight, seq_parts):
     tp_parts = len(chunks[0])
-    inner_parts, streams, chan_tp, width = weight.shape
+    rows, width = chunks[0][0].shape
+    streams, _, chan_tp = weight.shape
+    weight = weight.reshape(streams, tp_parts, width, chan_tp)
     chans = chan_tp // seq_parts
     pieces = [piece for chunk in chunks for piece in chunk]
-    count = len(chunks) * pieces[0].shape[0]
+    count = len(chunks) * rows
     place = lax.axis_index("tp").astype(jnp.int32)[None]
     return pl.pallas_call(
         functools.partial(project_kernel, tp_parts),
         grid_spec=pltpu.PrefetchScalarGridSpec(
             num_scalar_prefetch=1,
             grid=(streams,),
-            in_specs=[pl.BlockSpec(pieces[0].shape, lambda i, place: (0, 0))] * len(pieces)
-            + [pl.BlockSpec((inner_parts, 1, chan_tp, width), lambda i, place: (0, i, 0, 0))],
+            in_specs=[pl.BlockSpec((rows, width), lambda i, place: (0, 0))] * len(pieces)
+            + [pl.BlockSpec((1, tp_parts, width, chan_tp), lambda i, place: (i, 0, 0, 0))],
             out_specs=pl.BlockSpec((seq_parts, 1, chans, count), lambda i, place: (0, i, 0, 0)),
         ),
         out_shape=jax.ShapeDtypeStruct((seq_parts, streams, chans, count), jnp.bfloat16),
@@ -383,7 +380,7 @@
             ],
         ),
         out_shape=[jax.ShapeDtypeStruct((part_rows, columns), jnp.bfloat16)] * len(blocks),
-        compiler_params=pltpu.CompilerParams(vmem_limit_bytes=56 * 2**20),
+        compiler_params=pltpu.CompilerParams(vmem_limit_bytes=16 * 2**20),
         cost_estimate=pl.CostEstimate(
             flops=2 * gated.size * columns,
             bytes_accessed=2 * (weight.size + gated.size + rows * columns),
@@ -406,19 +403,19 @@
         [index * tp_parts + tp for index in group for tp in range(tp_parts)] for group in inner_groups
     ]
 
-    weight = lax.all_gather(jnp.swapaxes(in_proj, 1, 2), "seq", axis_index_groups=inner_groups)
-
-    filter_blocks = lax.all_to_all(
-        long_filter.T.reshape(seq_parts, chans, rows), "seq", split_axis=0, concat_axis=0, tiled=True
-    )
+    weight = lax.all_gather(in_proj, "seq", axis=1, tiled=True, axis_index_groups=inner_groups)
+
     taps = lax.dynamic_slice_in_dim(short_taps, position * chans, chans, axis=2)
     taps = jnp.broadcast_to(taps[..., None], taps.shape + (rows,))
     skip = lax.dynamic_slice_in_dim(skip_gain, position * chans, chans, axis=0)
     skip = jnp.broadcast_to(skip[:, None], (chans, rows))
+    filter_blocks = long_filter.T.reshape(seq_parts, chans, rows)
 
     held = share_columns(features, outer, tp_parts)
-    held, filter_blocks, taps, skip = lax.optimization_barrier((held, filter_blocks, taps, skip))
+    held, taps, skip, filter_blocks = lax.optimization_barrier((held, taps, skip, filter_blocks))
     arrived = cross_outer(held, outer, inner_parts, tp_parts)
+    arrived[-1], filter_blocks = lax.optimization_barrier((arrived[-1], filter_blocks))
+    filter_blocks = lax.all_to_all(filter_blocks, "seq", split_axis=0, concat_axis=0, tiled=True)
     chunks = [share_over_tp(piece, tp_parts) for piece in arrived]
     chunks, out_proj = lax.optimization_barrier((chunks, out_proj))
     out_weight = lax.all_gather(out_proj, ("seq", "tp"), axis_index_groups=tp_groups)
@@ -426,6 +423,8 @@
 
     partial = project_in(chunks, weight, seq_parts)
     parts = lax.all_to_all(partial, "seq", split_axis=0, concat_axis=0, tiled=True)
+
+    parts, out_weight = lax.optimization_barrier((parts, out_weight))
 
     gated = convolve([parts], filter_blocks, taps, skip, outer, tp_parts)
     gated = lax.all_to_all(

time: 185 us -> 187 us (1.011)
  waiting for transfers between devices: 69.4 us -> 80.8 us
  Pallas kernels: 19 us -> 15.9 us
  starting transfers between devices: 29.7 us -> 27.7 us
  local copies, waits for them, and re-layouts: 7.48 us -> 5.57 us
  blocking collectives: 44.2 us -> 42.3 us
    ppermute x1, waiting for transfers between devices: 4.67 us -> 11.3 us  [share_columns(): lax.ppermute(piece, 'tp', [(i, (i + step) % tp_parts) for i in range(tp_p...]
    all_to_all x1, waiting for transfers between devices: 2.22 us -> 8.13 us  [per_device(): lax.all_to_all(filter_blocks, 'seq', split_axis=0, concat_axis=0, tiled=T...]
    pallas_call x1, Pallas kernels: 5.75 us -> 2.63 us  [project_out(): pl.pallas_call(out_kernel, grid_spec=pltpu.PrefetchScalarGridSpec(num_sca...]
    ppermute x4, waiting for transfers between devices: 7.78 us -> 10.4 us  [share_over_tp(): pieces.append(lax.ppermute(part, 'tp', pairs))]
    ppermute x3, waiting for transfers between devices: 18.8 us -> 16.3 us  [cross_outer(): lax.ppermute(piece, 'seq', [(i, (i + far) % seq_parts) for i in range(seq...]
    ppermute x4, waiting for transfers between devices: 22 us -> 19.5 us  [return_output(): arrived.append(lax.ppermute(piece, ('seq', 'tp'), pairs))]
    ppermute x4, starting transfers between devices: 5.17 us -> 3.04 us  [share_over_tp(): pieces.append(lax.ppermute(part, 'tp', pairs))]
    unnamed x29 -> x28, local copies, waits for them, and re-layouts: 5.41 us -> 3.48 us
  transfers between devices with their start and end apart: 16 -> 16, of which waited for: 11 -> 10; matrix products, arithmetic and copies ran while one was open for 2% -> 1% of each run, Pallas kernels for 6% -> 4%
where the time goes in v8:
time: 187 us; the launch traced here: 186 us
  waiting for transfers between devices  80.8 us (43%)
  blocking collectives  42.3 us (23%)
  starting transfers between devices  27.7 us (15%)
  Pallas kernels  15.9 us (9%)
  between operations  13.7 us (7%)
  local copies, waits for them, and re-layouts  5.57 us (3%)
    all_to_all x1, blocking collectives, per_device(): lax.all_to_all(partial, 'seq', split_axis=0, concat_axis=0, tiled=True)  42.3 us
    ppermute x4, waiting for transfers between devices, return_output(): arrived.append(lax.ppermute(piece, ('seq', 'tp'), pairs))  19.5 us
    ppermute x3, waiting for transfers between devices, cross_outer(): lax.ppermute(piece, 'seq', [(i, (i + far) % seq_parts) for i in range(seq...  16.3 us
    all_to_all x1, waiting for transfers between devices, per_device(): lax.all_to_all(gated.reshape((-1,) + gated.shape[3:]), ('tp', 'seq'), spl...  14.4 us
    ppermute x1, waiting for transfers between devices, share_columns(): lax.ppermute(piece, 'tp', [(i, (i + step) % tp_parts) for i in range(tp_p...  11.3 us
    ppermute x4, waiting for transfers between devices, share_over_tp(): pieces.append(lax.ppermute(part, 'tp', pairs))  10.4 us
    ppermute x4, starting transfers between devices, return_output(): arrived.append(lax.ppermute(piece, ('seq', 'tp'), pairs))  8.85 us
    all_to_all x1, waiting for transfers between devices, per_device(): lax.all_to_all(filter_blocks, 'seq', split_axis=0, concat_axis=0, tiled=T...  8.13 us
  transfers between devices with their start and end apart: 16, of which 10 were waited for; matrix products, arithmetic and copies ran while one was open for 1% of the time, Pallas kernels for 4%

profile of v8, /device:TPU:12, one launch (start us, length us, event | category | flops | bytes accessed | tf_op | source)
XLA Modules:
  0.0 186.2 jit_solution(15170482814925311512)
XLA Ops:
  10.4 11.3 %collective-permute-done = bf16[2,128,1024]{2,1,0:T(8,128)(2,1)S(1)} collective-permute-done((bf16[2,128,1024]{2,1,0:T(8,128)(2,1)S(1)}, bf16[2,128,1024]{2,1,0:T(8,128)(2,1)S(1)}, u32[]{:S(2)}, u32[]{:S(2)}) %collective-permute-start) | collective-permute-done | bytes 524320 | tf_op jit(solution)/shard_map/ppermute | solution.py:105
  22.5 2.6 %collective-permute-start.4 = (bf16[128,1024]{1,0:T(8,128)(2,1)S(1)}, bf16[128,1024]{1,0:T(8,128)(2,1)S(1)}, u32[]{:S(2)}, u32[]{:S(2)}) collective-permute-start(bf16[128,1024]{1,0:T(8,128)(2,1)S(1)} %get-tuple-element.48), channel_id=1, source_target_pairs={{0,16},{2,18},{4,20},{6,22},{8,24},{10,26},{12,28},{14,30},{16,0},... | collective-permute-start | bytes 786440 | tf_op jit(solution)/shard_map/ppermute | solution.py:122
  25.1 2.5 %collective-permute-start.2 = (bf16[128,1024]{1,0:T(8,128)(2,1)S(1)}, bf16[128,1024]{1,0:T(8,128)(2,1)S(1)}, u32[]{:S(2)}, u32[]{:S(2)}) collective-permute-start(bf16[128,1024]{1,0:T(8,128)(2,1)S(1)} %get-tuple-element.49), channel_id=1, source_target_pairs={{0,8},{2,10},{4,12},{6,14},{8,16},{10,18},{12,20},{14,22},{16,24},... | collective-permute-start | bytes 786440 | tf_op jit(solution)/shard_map/ppermute | solution.py:122
  28.1 14.5 %collective-permute-done.6.refs_6_ = bf16[128,1024]{1,0:T(8,128)(2,1)S(1)} collective-permute-done((bf16[128,1024]{1,0:T(8,128)(2,1)S(1)}, bf16[128,1024]{1,0:T(8,128)(2,1)S(1)}, u32[]{:S(2)}, u32[]{:S(2)}) %collective-permute-start.6) | collective-permute-done | bytes 262176 | tf_op jit(solution)/shard_map/ppermute | solution.py:122
  43.1 1.5 collective-permute-start.5
  44.6 1.8 collective-permute-done.2.refs_2_
  47.0 2.6 %collective-permute-done.7.refs_7_ = bf16[128,1024]{1,0:T(8,128)(2,1)S(1)} collective-permute-done((bf16[128,1024]{1,0:T(8,128)(2,1)S(1)}, bf16[128,1024]{1,0:T(8,128)(2,1)S(1)}, u32[]{:S(2)}, u32[]{:S(2)}) %collective-permute-start.7) | collective-permute-done | bytes 262176 | tf_op jit(solution)/shard_map/ppermute | solution.py:131
  49.6 5.0 %collective-permute-done.5.refs_5_ = bf16[128,1024]{1,0:T(8,128)(2,1)S(1)} collective-permute-done((bf16[128,1024]{1,0:T(8,128)(2,1)S(1)}, bf16[128,1024]{1,0:T(8,128)(2,1)S(1)}, u32[]{:S(2)}, u32[]{:S(2)}) %collective-permute-start.5) | collective-permute-done | bytes 262176 | tf_op jit(solution)/shard_map/ppermute | solution.py:131
  54.6 2.8 %collective-permute-done.3.refs_3_ = bf16[128,1024]{1,0:T(8,128)(2,1)S(1)} collective-permute-done((bf16[128,1024]{1,0:T(8,128)(2,1)S(1)}, bf16[128,1024]{1,0:T(8,128)(2,1)S(1)}, u32[]{:S(2)}, u32[]{:S(2)}) %collective-permute-start.3) | collective-permute-done | bytes 262176 | tf_op jit(solution)/shard_map/ppermute | solution.py:131
  58.1 7.5 %shard_map.82 = bf16[16,3,32,512]{3,2,1,0:T(8,128)(2,1)} custom-call(s32[1]{0:T(128)} %bitcast.10.place_ref, bf16[128,1024]{1,0:T(8,128)(2,1)} %copy-done.5, bf16[128,1024]{1,0:T(8,128)(2,1)} %copy-done.10, bf16[128,1024]{1,0:T(8,128)(2,1)} %copy-done.9, bf16[128,1024]{1,0:T(8,128)(2,1)} %copy-done.13, bf16[128,1024]{1,0:T(8,128)(2,1)} %copy-done.8, ...), custom_call_target="tpu_custom_call" | custom-call | flops 96636764160 | bytes 9961472 | tf_op jit(solution)/shard_map/pallas_call | solution.py:157
  65.5 42.3 %all_to_all.15.refs_0_ = bf16[16,3,32,512]{3,2,1,0:T(8,128)(2,1)S(1)} all-to-all(bf16[16,3,32,512]{3,2,1,0:T(8,128)(2,1)} %shard_map.82), channel_id=1, replica_groups=mesh['seq'=16,'tp'=2] {'seq'}, dimensions={0} | all-to-all | bytes 3145728 | tf_op jit(solution)/shard_map/all_to_all | solution.py:425
  107.8 5.0 %all-to-all-start.1 = ((f32[16,32,128]{2,1,0:T(8,128)}), f32[16,32,128]{2,1,0:T(8,128)S(1)}, u32[]{:S(2)}, u32[]{:S(2)}) async-start(f32[16,32,128]{2,1,0:T(8,128)} %bitcast.16), calls=%async_computation.1 | async-start | bytes 524288 | tf_op jit(solution)/shard_map/all_to_all | solution.py:418
  112.9 8.1 %all-to-all-done.1.refs_1_ = f32[16,32,128]{2,1,0:T(8,128)S(1)} async-done(((f32[16,32,128]{2,1,0:T(8,128)}), f32[16,32,128]{2,1,0:T(8,128)S(1)}, u32[]{:S(2)}, u32[]{:S(2)}) %all-to-all-start.1) | async-done | bytes 262176 | tf_op jit(solution)/shard_map/all_to_all | solution.py:418
  121.0 3.7 %shard_map.83 = bf16[2,4,4,32,256]{4,3,2,1,0:T(8,128)(2,1)} custom-call(bf16[16,3,32,512]{3,2,1,0:T(8,128)(2,1)S(1)} %all_to_all.15.refs_0_, f32[16,32,128]{2,1,0:T(8,128)S(1)} %all-to-all-done.1.refs_1_, f32[3,3,32,128]{3,2,1,0:T(8,128)S(1)} %broadcast_in_dim.7.refs_2_, f32[32,128]{1,0:T(8,128)S(1)} %broadcast_in_dim.8.refs_3_, f32[128,256]{1,0:T(8,128)S(1)} %copy-done.3, ...), custom_call_target="tpu_custom_call" | custom-call | flops 1000000000 | bytes 4194304 | tf_op jit(solution)/shard_map/pallas_call | solution.py:321
  124.7 4.6 %all-to-all-start.2 = ((bf16[32,32,256]{2,1,0:T(8,128)(2,1)}), bf16[32,32,256]{2,1,0:T(8,128)(2,1)S(1)}, u32[]{:S(2)}, u32[]{:S(2)}) async-start(bf16[32,32,256]{2,1,0:T(8,128)(2,1)} %bitcast.23), calls=%async_computation.2 | async-start | bytes 1048576 | tf_op jit(solution)/shard_map/all_to_all | solution.py:430
  129.5 14.4 %all-to-all-done.2 = bf16[32,32,256]{2,1,0:T(8,128)(2,1)S(1)} async-done(((bf16[32,32,256]{2,1,0:T(8,128)(2,1)}), bf16[32,32,256]{2,1,0:T(8,128)(2,1)S(1)}, u32[]{:S(2)}, u32[]{:S(2)}) %all-to-all-start.2) | async-done | bytes 524320 | tf_op jit(solution)/shard_map/all_to_all | solution.py:430
  143.9 2.2 %copy-done.1 = bf16[4096,512]{1,0:T(8,128)(2,1)S(1)} copy-done((bf16[4096,512]{1,0:T(8,128)(2,1)S(1)}, bf16[4096,512]{1,0:T(8,128)(2,1)}, u32[]{:S(2)}) %copy-start.1) | copy-done | bytes 4194328
  146.1 2.6 %shard_map.84 = (bf16[64,2048]{1,0:T(8,128)(2,1)S(1)}, bf16[64,2048]{1,0:T(8,128)(2,1)S(1)}, bf16[64,2048]{1,0:T(8,128)(2,1)S(1)}, bf16[64,2048]{1,0:T(8,128)(2,1)S(1)}) custom-call(s32[4]{0:T(128)S(1)} %pad_add_fusion.block_ref, bf16[2,512,256]{2,1,0:T(8,128)(2,1)S(1)} %bitcast.34, bf16[4,2,512,512]{3,2,1,0:T(8,128)(2,1)S(1)} %bitcast.33), custom_call_target="tpu_custom_call" | custom-call | flops 1073741824 | bytes 5767168 | tf_op jit(solution)/shard_map/pallas_call | solution.py:367
  148.7 2.6 %collective-permute-start.8 = (bf16[64,2048]{1,0:T(8,128)(2,1)S(1)}, bf16[64,2048]{1,0:T(8,128)(2,1)S(1)}, u32[]{:S(2)}, u32[]{:S(2)}) collective-permute-start(bf16[64,2048]{1,0:T(8,128)(2,1)S(1)} %get-tuple-element.43), channel_id=1, source_target_pairs={{0,0},{1,16},{2,2},{3,18},{4,4},{5,20},{6,6},{7,22},{8,24},{9,8},{... | collective-permute-start | bytes 786440 | tf_op jit(solution)/shard_map/ppermute | solution.py:86
  151.4 3.9 %collective-permute-start.10 = (bf16[64,2048]{1,0:T(8,128)(2,1)S(1)}, bf16[64,2048]{1,0:T(8,128)(2,1)S(1)}, u32[]{:S(2)}, u32[]{:S(2)}) collective-permute-start(bf16[64,2048]{1,0:T(8,128)(2,1)S(1)} %get-tuple-element.45), channel_id=1, source_target_pairs={{0,16},{1,0},{2,18},{3,2},{4,20},{5,4},{6,22},{7,6},{8,8},{9,24},{... | collective-permute-start | bytes 786440 | tf_op jit(solution)/shard_map/ppermute | solution.py:86
  155.3 2.3 %collective-permute-start.11 = (bf16[64,2048]{1,0:T(8,128)(2,1)S(1)}, bf16[64,2048]{1,0:T(8,128)(2,1)S(1)}, u32[]{:S(2)}, u32[]{:S(2)}) collective-permute-start(bf16[64,2048]{1,0:T(8,128)(2,1)S(1)} %get-tuple-element.46), channel_id=1, source_target_pairs={{0,24},{1,8},{2,26},{3,10},{4,28},{5,12},{6,30},{7,14},{8,0},{9,16... | collective-permute-start | bytes 786440 | tf_op jit(solution)/shard_map/ppermute | solution.py:86
  157.7 3.2 %collective-permute-done.8.refs_0_ = bf16[64,2048]{1,0:T(8,128)(2,1)S(1)} collective-permute-done((bf16[64,2048]{1,0:T(8,128)(2,1)S(1)}, bf16[64,2048]{1,0:T(8,128)(2,1)S(1)}, u32[]{:S(2)}, u32[]{:S(2)}) %collective-permute-start.8) | collective-permute-done | bytes 262176 | tf_op jit(solution)/shard_map/ppermute | solution.py:86
  160.8 16.4 %collective-permute-done.9.refs_1_ = bf16[64,2048]{1,0:T(8,128)(2,1)S(1)} collective-permute-done((bf16[64,2048]{1,0:T(8,128)(2,1)S(1)}, bf16[64,2048]{1,0:T(8,128)(2,1)S(1)}, u32[]{:S(2)}, u32[]{:S(2)}) %collective-permute-start.9) | collective-permute-done | bytes 262176 | tf_op jit(solution)/shard_map/ppermute | solution.py:86
  177.2 2.1 %shard_map.85 = bf16[128,4096]{1,0:T(8,128)(2,1)} custom-call(s32[8]{0:T(128)S(1)} %stack.59.place_ref, bf16[64,2048]{1,0:T(8,128)(2,1)S(1)} %collective-permute-done.8.refs_0_, bf16[64,2048]{1,0:T(8,128)(2,1)S(1)} %collective-permute-done.9.refs_1_, bf16[64,2048]{1,0:T(8,128)(2,1)S(1)} %collective-permute-done.10.refs_2_, ...), custom_call_target="tpu_custom_call" | custom-call | bytes 2097152 | tf_op jit(solution)/shard_map/pallas_call | solution.py:34
  (54 shorter events, 7.1 us)
Async XLA Ops:
  6.5 50.9 %all-gather.4.cloned.1.call-start = ((), (), s32[]{:S(2)}) async-start(), calls=%async_computation.3 | async-start | bytes 7864320 | tf_op jit(solution)/shard_map/all_gather | solution.py:406
  7.3 105.6 %all-gather.6.cloned.1.call-start = ((), (), s32[]{:S(2)}) async-start(), calls=%async_computation.4 | async-start | bytes 4718592 | tf_op jit(solution)/shard_map/all_gather | solution.py:421
  7.9 13.7 %collective-permute-start = (bf16[2,128,1024]{2,1,0:T(8,128)(2,1)S(1)}, bf16[2,128,1024]{2,1,0:T(8,128)(2,1)S(1)}, u32[]{:S(2)}, u32[]{:S(2)}) collective-permute-start(bf16[2,128,1024]{2,1,0:T(8,128)(2,1)S(1)} %pad_maximum_fusion.1), channel_id=1, source_target_pairs={{0,1},{1,0},{2,3},{3,2},{4,5},{5,4},{6,7},{7,6},{8,9},{9,8},{10,11... | collective-permute-start | bytes 1572872 | tf_op jit(solution)/shard_map/ppermute | solution.py:105
  22.0 35.4 %copy-start.5 = (bf16[128,1024]{1,0:T(8,128)(2,1)}, bf16[128,1024]{1,0:T(8,128)(2,1)S(1)}, u32[]{:S(2)}) copy-start(bf16[128,1024]{1,0:T(8,128)(2,1)S(1)} %get-tuple-element.29.refs_0_) | copy-start | bytes 786436
  22.0 20.5 %collective-permute-start.6 = (bf16[128,1024]{1,0:T(8,128)(2,1)S(1)}, bf16[128,1024]{1,0:T(8,128)(2,1)S(1)}, u32[]{:S(2)}, u32[]{:S(2)}) collective-permute-start(bf16[128,1024]{1,0:T(8,128)(2,1)S(1)} %get-tuple-element.47), channel_id=1, source_target_pairs={{0,24},{2,26},{4,28},{6,30},{8,0},{10,2},{12,4},{14,6},{16,8},{18,... | collective-permute-start | bytes 786440 | tf_op jit(solution)/shard_map/ppermute | solution.py:122
  22.5 20.5 %collective-permute-start.4 = (bf16[128,1024]{1,0:T(8,128)(2,1)S(1)}, bf16[128,1024]{1,0:T(8,128)(2,1)S(1)}, u32[]{:S(2)}, u32[]{:S(2)}) collective-permute-start(bf16[128,1024]{1,0:T(8,128)(2,1)S(1)} %get-tuple-element.48), channel_id=1, source_target_pairs={{0,16},{2,18},{4,20},{6,22},{8,24},{10,26},{12,28},{14,30},{16,0},... | collective-permute-start | bytes 786440 | tf_op jit(solution)/shard_map/ppermute | solution.py:122
  25.1 21.3 %collective-permute-start.2 = (bf16[128,1024]{1,0:T(8,128)(2,1)S(1)}, bf16[128,1024]{1,0:T(8,128)(2,1)S(1)}, u32[]{:S(2)}, u32[]{:S(2)}) collective-permute-start(bf16[128,1024]{1,0:T(8,128)(2,1)S(1)} %get-tuple-element.49), channel_id=1, source_target_pairs={{0,8},{2,10},{4,12},{6,14},{8,16},{10,18},{12,20},{14,22},{16,24},... | collective-permute-start | bytes 786440 | tf_op jit(solution)/shard_map/ppermute | solution.py:122
  27.6 19.3 %collective-permute-start.1 = (bf16[128,1024]{1,0:T(8,128)(2,1)S(1)}, bf16[128,1024]{1,0:T(8,128)(2,1)S(1)}, u32[]{:S(2)}, u32[]{:S(2)}) collective-permute-start(bf16[128,1024]{1,0:T(8,128)(2,1)S(1)} %get-tuple-element.29.refs_0_), channel_id=1, source_target_pairs={{0,1},{1,0},{2,3},{3,2},{4,5},{5,4},{6,7},{7,6},{8,9},{9,8},{10,11... | collective-permute-start | bytes 786440 | tf_op jit(solution)/shard_map/ppermute | solution.py:131
  42.6 14.9 %copy-start.7 = (bf16[128,1024]{1,0:T(8,128)(2,1)}, bf16[128,1024]{1,0:T(8,128)(2,1)S(1)}, u32[]{:S(2)}) copy-start(bf16[128,1024]{1,0:T(8,128)(2,1)S(1)} %collective-permute-done.6.refs_6_) | copy-start | bytes 786436
  42.6 7.0 %collective-permute-start.7 = (bf16[128,1024]{1,0:T(8,128)(2,1)S(1)}, bf16[128,1024]{1,0:T(8,128)(2,1)S(1)}, u32[]{:S(2)}, u32[]{:S(2)}) collective-permute-start(bf16[128,1024]{1,0:T(8,128)(2,1)S(1)} %collective-permute-done.6.refs_6_), channel_id=1, source_target_pairs={{0,1},{1,0},{2,3},{3,2},{4,5},{5,4},{6,7},{7,6},{8,9},{9,8},{10,11... | collective-permute-start | bytes 786440 | tf_op jit(solution)/shard_map/ppermute | solution.py:131
  43.1 14.4 %copy-start.8 = (bf16[128,1024]{1,0:T(8,128)(2,1)}, bf16[128,1024]{1,0:T(8,128)(2,1)S(1)}, u32[]{:S(2)}) copy-start(bf16[128,1024]{1,0:T(8,128)(2,1)S(1)} %collective-permute-done.4.refs_4_) | copy-start | bytes 786436
  43.1 11.5 %collective-permute-start.5 = (bf16[128,1024]{1,0:T(8,128)(2,1)S(1)}, bf16[128,1024]{1,0:T(8,128)(2,1)S(1)}, u32[]{:S(2)}, u32[]{:S(2)}) collective-permute-start(bf16[128,1024]{1,0:T(8,128)(2,1)S(1)} %collective-permute-done.4.refs_4_), channel_id=1, source_target_pairs={{0,1},{1,0},{2,3},{3,2},{4,5},{5,4},{6,7},{7,6},{8,9},{9,8},{10,11... | collective-permute-start | bytes 786440 | tf_op jit(solution)/shard_map/ppermute | solution.py:131
  46.4 11.0 %copy-start.9 = (bf16[128,1024]{1,0:T(8,128)(2,1)}, bf16[128,1024]{1,0:T(8,128)(2,1)S(1)}, u32[]{:S(2)}) copy-start(bf16[128,1024]{1,0:T(8,128)(2,1)S(1)} %collective-permute-done.2.refs_2_) | copy-start | bytes 786436
  46.4 10.9 %collective-permute-start.3 = (bf16[128,1024]{1,0:T(8,128)(2,1)S(1)}, bf16[128,1024]{1,0:T(8,128)(2,1)S(1)}, u32[]{:S(2)}, u32[]{:S(2)}) collective-permute-start(bf16[128,1024]{1,0:T(8,128)(2,1)S(1)} %collective-permute-done.2.refs_2_), channel_id=1, source_target_pairs={{0,1},{1,0},{2,3},{3,2},{4,5},{5,4},{6,7},{7,6},{8,9},{9,8},{10,11... | collective-permute-start | bytes 786440 | tf_op jit(solution)/shard_map/ppermute | solution.py:131
  47.0 10.5 %copy-start.10 = (bf16[128,1024]{1,0:T(8,128)(2,1)}, bf16[128,1024]{1,0:T(8,128)(2,1)S(1)}, u32[]{:S(2)}) copy-start(bf16[128,1024]{1,0:T(8,128)(2,1)S(1)} %collective-permute-done.1.refs_1_) | copy-start | bytes 786436
  49.6 7.9 %copy-start.11 = (bf16[128,1024]{1,0:T(8,128)(2,1)}, bf16[128,1024]{1,0:T(8,128)(2,1)S(1)}, u32[]{:S(2)}) copy-start(bf16[128,1024]{1,0:T(8,128)(2,1)S(1)} %collective-permute-done.7.refs_7_) | copy-start | bytes 786436
  65.5 55.4 %copy-start.2 = (f32[256,256]{1,0:T(8,128)S(1)}, f32[256,256]{1,0:T(8,128)}, u32[]{:S(2)}) copy-start(f32[256,256]{1,0:T(8,128)} %constant.230.clone.refs_5_) | copy-start | bytes 786436
  65.5 55.4 %copy-start.3 = (f32[128,256]{1,0:T(8,128)S(1)}, f32[128,256]{1,0:T(8,128)}, u32[]{:S(2)}) copy-start(f32[128,256]{1,0:T(8,128)} %constant.229.clone.refs_4_) | copy-start | bytes 393220
  107.8 13.1 %all-to-all-start.1 = ((f32[16,32,128]{2,1,0:T(8,128)}), f32[16,32,128]{2,1,0:T(8,128)S(1)}, u32[]{:S(2)}, u32[]{:S(2)}) async-start(f32[16,32,128]{2,1,0:T(8,128)} %bitcast.16), calls=%async_computation.1 | async-start | bytes 524288 | tf_op jit(solution)/shard_map/all_to_all | solution.py:418
  124.7 19.2 %all-to-all-start.2 = ((bf16[32,32,256]{2,1,0:T(8,128)(2,1)}), bf16[32,32,256]{2,1,0:T(8,128)(2,1)S(1)}, u32[]{:S(2)}, u32[]{:S(2)}) async-start(bf16[32,32,256]{2,1,0:T(8,128)(2,1)} %bitcast.23), calls=%async_computation.2 | async-start | bytes 1048576 | tf_op jit(solution)/shard_map/all_to_all | solution.py:430
  148.7 12.1 %collective-permute-start.8 = (bf16[64,2048]{1,0:T(8,128)(2,1)S(1)}, bf16[64,2048]{1,0:T(8,128)(2,1)S(1)}, u32[]{:S(2)}, u32[]{:S(2)}) collective-permute-start(bf16[64,2048]{1,0:T(8,128)(2,1)S(1)} %get-tuple-element.43), channel_id=1, source_target_pairs={{0,0},{1,16},{2,2},{3,18},{4,4},{5,20},{6,6},{7,22},{8,24},{9,8},{... | collective-permute-start | bytes 786440 | tf_op jit(solution)/shard_map/ppermute | solution.py:86
  151.3 25.9 %collective-permute-start.9 = (bf16[64,2048]{1,0:T(8,128)(2,1)S(1)}, bf16[64,2048]{1,0:T(8,128)(2,1)S(1)}, u32[]{:S(2)}, u32[]{:S(2)}) collective-permute-start(bf16[64,2048]{1,0:T(8,128)(2,1)S(1)} %get-tuple-element.44), channel_id=1, source_target_pairs={{0,8},{1,24},{2,10},{3,26},{4,12},{5,28},{6,14},{7,30},{8,16},{9,0... | collective-permute-start | bytes 786440 | tf_op jit(solution)/shard_map/ppermute | solution.py:86
  151.4 25.8 %collective-permute-start.10 = (bf16[64,2048]{1,0:T(8,128)(2,1)S(1)}, bf16[64,2048]{1,0:T(8,128)(2,1)S(1)}, u32[]{:S(2)}, u32[]{:S(2)}) collective-permute-start(bf16[64,2048]{1,0:T(8,128)(2,1)S(1)} %get-tuple-element.45), channel_id=1, source_target_pairs={{0,16},{1,0},{2,18},{3,2},{4,20},{5,4},{6,22},{7,6},{8,8},{9,24},{... | collective-permute-start | bytes 786440 | tf_op jit(solution)/shard_map/ppermute | solution.py:86
  155.3 22.0 %collective-permute-start.11 = (bf16[64,2048]{1,0:T(8,128)(2,1)S(1)}, bf16[64,2048]{1,0:T(8,128)(2,1)S(1)}, u32[]{:S(2)}, u32[]{:S(2)}) collective-permute-start(bf16[64,2048]{1,0:T(8,128)(2,1)S(1)} %get-tuple-element.46), channel_id=1, source_target_pairs={{0,24},{1,8},{2,26},{3,10},{4,28},{5,12},{6,30},{7,14},{8,0},{9,16... | collective-permute-start | bytes 786440 | tf_op jit(solution)/shard_map/ppermute | solution.py:86
  (6 other events, 11.8 us)
Sparse Core Ops, SparseCore 0:
  8.9 47.4 all-gather.3
  58.3 44.2 all-gather.5

commit v9 on v8

--- a/solution.py
+++ b/solution.py
@@ -132,43 +132,71 @@
     return pieces
 
 
+def fetch_kernel(source_ref, out_ref, sems):
+    copies = [
+        pltpu.make_async_copy(source_ref.at[index], out_ref.at[index], sems.at[index])
+        for index in range(source_ref.shape[0])
+    ]
+    for copy in copies:
+        copy.start()
+    for copy in copies:
+        copy.wait()
+
+
+def fetch(source):
+    return pl.pallas_call(
+        fetch_kernel,
+        out_shape=jax.ShapeDtypeStruct(source.shape, source.dtype),
+        in_specs=[pl.BlockSpec(memory_space=pl.ANY)],
+        out_specs=pl.BlockSpec(memory_space=pltpu.VMEM),
+        scratch_shapes=[pltpu.SemaphoreType.DMA((source.shape[0],))],
+        compiler_params=pltpu.CompilerParams(vmem_limit_bytes=60 * 2**20 - 2 * source.size),
+        cost_estimate=pl.CostEstimate(
+            flops=0, bytes_accessed=4 * source.size, transcendentals=0
+        ),
+    )(source)
+
+
 def project_kernel(tp_parts, place_ref, *refs):
     *share_refs, weight_ref, out_ref = refs
-    seq_parts, _, chans, count = out_ref.shape
-    sums = jnp.zeros((count, seq_parts * chans), jnp.float32)
-    for step in range(tp_parts):
-        which = lax.rem(place_ref[0] - step + tp_parts, tp_parts)
-        left = jnp.concatenate([share_ref[...] for share_ref in share_refs[step::tp_parts]])
-        sums = sums + jnp.dot(left, weight_ref[0, which], preferred_element_type=jnp.float32)
-    turned = sums.astype(out_ref.dtype).T
-    for seq in range(seq_parts):
-        out_ref[seq, 0] = turned[seq * chans : (seq + 1) * chans]
+    seq_parts, streams, chans, count = out_ref.shape
+    left = [
+        jnp.concatenate([share_ref[...] for share_ref in share_refs[step::tp_parts]])
+        for step in range(tp_parts)
+    ]
+    for stream in range(streams):
+        sums = jnp.zeros((count, seq_parts * chans), jnp.float32)
+        for step in range(tp_parts):
+            which = lax.rem(place_ref[0] - step + tp_parts, tp_parts)
+            sums = sums + jnp.dot(
+                left[step],
+                weight_ref[stream * tp_parts + which],
+                preferred_element_type=jnp.float32,
+            )
+        turned = sums.astype(out_ref.dtype).T
+        for seq in range(seq_parts):
+            out_ref[seq, stream] = turned[seq * chans : (seq + 1) * chans]
 
 
 def project_in(chunks, weight, seq_parts):
     tp_parts = len(chunks[0])
     rows, width = chunks[0][0].shape
-    streams, _, chan_tp = weight.shape
-    weight = weight.reshape(streams, tp_parts, width, chan_tp)
-    chans = chan_tp // seq_parts
+    streams = weight.shape[0] // tp_parts
+    chans = weight.shape[2] // seq_parts
     pieces = [piece for chunk in chunks for piece in chunk]
     count = len(chunks) * rows
     place = lax.axis_index("tp").astype(jnp.int32)[None]
+    vmem = pl.BlockSpec(memory_space=pltpu.VMEM)
     return pl.pallas_call(
         functools.partial(project_kernel, tp_parts),
-        grid_spec=pltpu.PrefetchScalarGridSpec(
-            num_scalar_prefetch=1,
-            grid=(streams,),
-            in_specs=[pl.BlockSpec((rows, width), lambda i, place: (0, 0))] * len(pieces)
-            + [pl.BlockSpec((1, tp_parts, width, chan_tp), lambda i, place: (i, 0, 0, 0))],
-            out_specs=pl.BlockSpec((seq_parts, 1, chans, count), lambda i, place: (0, i, 0, 0)),
-        ),
+        in_specs=[pl.BlockSpec(memory_space=pltpu.SMEM)] + [vmem] * (len(pieces) + 1),
+        out_specs=vmem,
         out_shape=jax.ShapeDtypeStruct((seq_parts, streams, chans, count), jnp.bfloat16),
-        compiler_params=pltpu.CompilerParams(vmem_limit_bytes=56 * 2**20),
+        compiler_params=pltpu.CompilerParams(vmem_limit_bytes=32 * 2**20),
         cost_estimate=pl.CostEstimate(
             flops=HEAVY * 2 * count * weight.size,
             bytes_accessed=2 * (weight.size + len(pieces) * pieces[0].size)
-            + 2 * streams * count * chan_tp,
+            + 2 * streams * count * seq_parts * chans,
             transcendentals=0,
         ),
     )(place, *pieces, weight)
@@ -412,19 +440,21 @@
     filter_blocks = long_filter.T.reshape(seq_parts, chans, rows)
 
     held = share_columns(features, outer, tp_parts)
-    held, taps, skip, filter_blocks = lax.optimization_barrier((held, taps, skip, filter_blocks))
+    held, taps, skip = lax.optimization_barrier((held, taps, skip))
     arrived = cross_outer(held, outer, inner_parts, tp_parts)
-    arrived[-1], filter_blocks = lax.optimization_barrier((arrived[-1], filter_blocks))
     filter_blocks = lax.all_to_all(filter_blocks, "seq", split_axis=0, concat_axis=0, tiled=True)
+    arrived[1], filter_blocks = lax.optimization_barrier((arrived[1], filter_blocks))
     chunks = [share_over_tp(piece, tp_parts) for piece in arrived]
     chunks, out_proj = lax.optimization_barrier((chunks, out_proj))
     out_weight = lax.all_gather(out_proj, ("seq", "tp"), axis_index_groups=tp_groups)
     out_weight = out_weight.reshape((inner_parts, tp_parts) + out_proj.shape)
 
+    weight = fetch(weight.reshape(streams * tp_parts, -1, chan_tp))
     partial = project_in(chunks, weight, seq_parts)
     parts = lax.all_to_all(partial, "seq", split_axis=0, concat_axis=0, tiled=True)
 
     parts, out_weight = lax.optimization_barrier((parts, out_weight))
+    out_weight = fetch(out_weight)
 
     gated = convolve([parts], filter_blocks, taps, skip, outer, tp_parts)
     gated = lax.all_to_all(

time: 187 us -> 182 us (0.973)
  blocking collectives: 42.3 us -> 0 us
  waiting for transfers between devices: 80.8 us -> 100 us
  starting transfers between devices: 27.7 us -> 35.6 us
  Pallas kernels: 15.9 us -> 22.8 us
  local copies, waits for them, and re-layouts: 5.57 us -> 8.5 us
    all_to_all x1 -> x0, blocking collectives: 42.3 us -> none  [per_device(): lax.all_to_all(partial, 'seq', split_axis=0, concat_axis=0, tiled=True)]
    all_gather x1, waiting for transfers between devices: 0.01 us -> 30.2 us  [per_device(): lax.all_gather(out_proj, ('seq', 'tp'), axis_index_groups=tp_groups)]
    all_to_all x1, waiting for transfers between devices: 8.13 us -> 0.01 us  [per_device(): lax.all_to_all(filter_blocks, 'seq', split_axis=0, concat_axis=0, tiled=T...]
    pallas_call x1 -> x3, Pallas kernels: 7.45 us -> 14.3 us  [the longest x2 9.65 us: fetch(): pl.pallas_call(fetch_kernel, out_shape=jax.ShapeDtypeStruct(source.shape,...]
    ppermute x1, waiting for transfers between devices: 11.3 us -> 4.89 us  [share_columns(): lax.ppermute(piece, 'tp', [(i, (i + step) % tp_parts) for i in range(tp_p...]
    all_to_all x0 -> x1, starting transfers between devices: none -> 5.93 us  [per_device(): lax.all_to_all(partial, 'seq', split_axis=0, concat_axis=0, tiled=True)]
    all_to_all x0 -> x1, waiting for transfers between devices: none -> 4.72 us  [per_device(): lax.all_to_all(partial, 'seq', split_axis=0, concat_axis=0, tiled=True)]
    all_to_all x1, waiting for transfers between devices: 14.4 us -> 10.2 us  [per_device(): lax.all_to_all(gated.reshape((-1,) + gated.shape[3:]), ('tp', 'seq'), spl...]
  transfers between devices with their start and end apart: 16 -> 17, of which waited for: 10 -> 11; matrix products, arithmetic and copies ran while one was open for 1% -> 2% of each run, Pallas kernels for 4% -> 8%
where the time goes in v9:
time: 182 us; the launch traced here: 181 us
  waiting for transfers between devices  100 us (55%)
  starting transfers between devices  35.6 us (20%)
  Pallas kernels  22.8 us (13%)
  between operations  13.9 us (8%)
  local copies, waits for them, and re-layouts  8.5 us (5%)
    all_gather x1, waiting for transfers between devices, per_device(): lax.all_gather(out_proj, ('seq', 'tp'), axis_index_groups=tp_groups)  30.2 us
    ppermute x4, waiting for transfers between devices, return_output(): arrived.append(lax.ppermute(piece, ('seq', 'tp'), pairs))  19.6 us
    ppermute x3, waiting for transfers between devices, cross_outer(): lax.ppermute(piece, 'seq', [(i, (i + far) % seq_parts) for i in range(seq...  17.2 us
    ppermute x4, waiting for transfers between devices, share_over_tp(): pieces.append(lax.ppermute(part, 'tp', pairs))  12.7 us
    all_to_all x1, waiting for transfers between devices, per_device(): lax.all_to_all(gated.reshape((-1,) + gated.shape[3:]), ('tp', 'seq'), spl...  10.2 us
    pallas_call x2, Pallas kernels, fetch(): pl.pallas_call(fetch_kernel, out_shape=jax.ShapeDtypeStruct(source.shape,...  9.65 us
    ppermute x4, starting transfers between devices, return_output(): arrived.append(lax.ppermute(piece, ('seq', 'tp'), pairs))  8.85 us
    all_to_all x1, starting transfers between devices, per_device(): lax.all_to_all(filter_blocks, 'seq', split_axis=0, concat_axis=0, tiled=T...  6.27 us
  transfers between devices with their start and end apart: 17, of which 11 were waited for; matrix products, arithmetic and copies ran while one was open for 2% of the time, Pallas kernels for 8%

profile of v9, /device:TPU:12, one launch (start us, length us, event | category | flops | bytes accessed | tf_op | source)
XLA Modules:
  0.0 181.3 jit_solution(6970296010634015909)
XLA Ops:
  10.0 6.3 %all-to-all-start = ((f32[16,32,128]{2,1,0:T(8,128)}), f32[16,32,128]{2,1,0:T(8,128)S(1)}, u32[]{:S(2)}, u32[]{:S(2)}) async-start(f32[16,32,128]{2,1,0:T(8,128)} %bitcast.18), calls=%async_computation | async-start | bytes 524288 | tf_op jit(solution)/shard_map/all_to_all | solution.py:445
  17.5 4.9 %collective-permute-done = bf16[2,128,1024]{2,1,0:T(8,128)(2,1)S(1)} collective-permute-done((bf16[2,128,1024]{2,1,0:T(8,128)(2,1)S(1)}, bf16[2,128,1024]{2,1,0:T(8,128)(2,1)S(1)}, u32[]{:S(2)}, u32[]{:S(2)}) %collective-permute-start) | collective-permute-done | bytes 524320 | tf_op jit(solution)/shard_map/ppermute | solution.py:105
  24.8 2.6 %collective-permute-start.4 = (bf16[128,1024]{1,0:T(8,128)(2,1)S(1)}, bf16[128,1024]{1,0:T(8,128)(2,1)S(1)}, u32[]{:S(2)}, u32[]{:S(2)}) collective-permute-start(bf16[128,1024]{1,0:T(8,128)(2,1)S(1)} %get-tuple-element.46), channel_id=1, source_target_pairs={{0,16},{2,18},{4,20},{6,22},{8,24},{10,26},{12,28},{14,30},{16,0},... | collective-permute-start | bytes 786440 | tf_op jit(solution)/shard_map/ppermute | solution.py:122
  27.9 14.4 %collective-permute-done.2.refs_2_ = bf16[128,1024]{1,0:T(8,128)(2,1)S(1)} collective-permute-done((bf16[128,1024]{1,0:T(8,128)(2,1)S(1)}, bf16[128,1024]{1,0:T(8,128)(2,1)S(1)}, u32[]{:S(2)}, u32[]{:S(2)}) %collective-permute-start.2) | collective-permute-done | bytes 262176 | tf_op jit(solution)/shard_map/ppermute | solution.py:122
  43.2 2.7 %collective-permute-done.4.refs_4_ = bf16[128,1024]{1,0:T(8,128)(2,1)S(1)} collective-permute-done((bf16[128,1024]{1,0:T(8,128)(2,1)S(1)}, bf16[128,1024]{1,0:T(8,128)(2,1)S(1)}, u32[]{:S(2)}, u32[]{:S(2)}) %collective-permute-start.4) | collective-permute-done | bytes 262176 | tf_op jit(solution)/shard_map/ppermute | solution.py:122
  47.9 3.7 %collective-permute-done.7.refs_7_ = bf16[128,1024]{1,0:T(8,128)(2,1)S(1)} collective-permute-done((bf16[128,1024]{1,0:T(8,128)(2,1)S(1)}, bf16[128,1024]{1,0:T(8,128)(2,1)S(1)}, u32[]{:S(2)}, u32[]{:S(2)}) %collective-permute-start.7) | collective-permute-done | bytes 262176 | tf_op jit(solution)/shard_map/ppermute | solution.py:131
  51.6 5.6 %collective-permute-done.5.refs_5_ = bf16[128,1024]{1,0:T(8,128)(2,1)S(1)} collective-permute-done((bf16[128,1024]{1,0:T(8,128)(2,1)S(1)}, bf16[128,1024]{1,0:T(8,128)(2,1)S(1)}, u32[]{:S(2)}, u32[]{:S(2)}) %collective-permute-start.5) | collective-permute-done | bytes 262176 | tf_op jit(solution)/shard_map/ppermute | solution.py:131
  57.2 3.4 %collective-permute-done.3.refs_3_ = bf16[128,1024]{1,0:T(8,128)(2,1)S(1)} collective-permute-done((bf16[128,1024]{1,0:T(8,128)(2,1)S(1)}, bf16[128,1024]{1,0:T(8,128)(2,1)S(1)}, u32[]{:S(2)}, u32[]{:S(2)}) %collective-permute-start.3) | collective-permute-done | bytes 262176 | tf_op jit(solution)/shard_map/ppermute | solution.py:131
  60.7 5.5 %shard_map.82.refs_8_ = bf16[6,1024,512]{2,1,0:T(8,128)(2,1)} custom-call(bf16[6,1024,512]{2,1,0:T(8,128)(2,1)} %bitcast.34), custom_call_target="tpu_custom_call" | custom-call | bytes 12582912 | tf_op jit(solution)/shard_map/pallas_call | solution.py:147
  66.2 3.0 %copy-done.2 = bf16[6,1024,512]{2,1,0:T(8,128)(2,1)S(1)} copy-done((bf16[6,1024,512]{2,1,0:T(8,128)(2,1)S(1)}, bf16[6,1024,512]{2,1,0:T(8,128)(2,1)}, u32[]{:S(2)}) %copy-start.2) | copy-done | bytes 6291480
  69.2 4.7 %shard_map.83 = bf16[16,3,32,512]{3,2,1,0:T(8,128)(2,1)} custom-call(s32[1]{0:T(128)} %bitcast.10.place_ref, bf16[128,1024]{1,0:T(8,128)(2,1)S(1)} %get-tuple-element.27.refs_0_, bf16[128,1024]{1,0:T(8,128)(2,1)S(1)} %collective-permute-done.1.refs_1_, bf16[128,1024]{1,0:T(8,128)(2,1)S(1)} %collective-permute-done.2.refs_2_, ...), custom_call_target="tpu_custom_call" | custom-call | flops 96636764160 | bytes 9961472 | tf_op jit(solution)/shard_map/pallas_call | solution.py:190
  73.9 5.9 %all-to-all-start.1 = ((bf16[16,3,32,512]{3,2,1,0:T(8,128)(2,1)}), bf16[16,3,32,512]{3,2,1,0:T(8,128)(2,1)S(1)}, u32[]{:S(2)}, u32[]{:S(2)}) async-start(bf16[16,3,32,512]{3,2,1,0:T(8,128)(2,1)} %shard_map.83), calls=%async_computation.1 | async-start | bytes 3145728 | tf_op jit(solution)/shard_map/all_to_all | solution.py:454
  79.8 30.2 %all-gather.6.cloned.1.call-done = bf16[4096,512]{1,0:T(8,128)(2,1)} async-done(((bf16[512,512]{1,0:T(8,128)(2,1)}), bf16[4096,512]{1,0:T(8,128)(2,1)}) %all-gather.6.cloned.1.call-update) | async-done | bytes 4194320 | tf_op jit(solution)/shard_map/all_gather | solution.py:449
  110.1 4.7 %all-to-all-done.1.refs_0_ = bf16[16,3,32,512]{3,2,1,0:T(8,128)(2,1)S(1)} async-done(((bf16[16,3,32,512]{3,2,1,0:T(8,128)(2,1)}), bf16[16,3,32,512]{3,2,1,0:T(8,128)(2,1)S(1)}, u32[]{:S(2)}, u32[]{:S(2)}) %all-to-all-start.1) | async-done | bytes 1572896 | tf_op jit(solution)/shard_map/all_to_all | solution.py:454
  114.8 3.7 %shard_map.84 = bf16[2,4,4,32,256]{4,3,2,1,0:T(8,128)(2,1)} custom-call(bf16[16,3,32,512]{3,2,1,0:T(8,128)(2,1)S(1)} %all-to-all-done.1.refs_0_, f32[16,32,128]{2,1,0:T(8,128)S(1)} %all-to-all-done.refs_1_, f32[3,3,32,128]{3,2,1,0:T(8,128)S(1)} %broadcast_in_dim.7.refs_2_, f32[32,128]{1,0:T(8,128)S(1)} %broadcast_in_dim.8.refs_3_, f32[128,256]{1,0:T(8,128)S(1)} %copy-done.4, ...), custom_call_target="tpu_custom_call" | custom-call | flops 1000000000 | bytes 4194304 | tf_op jit(solution)/shard_map/pallas_call | solution.py:349
  118.5 5.9 %all-to-all-start.2 = ((bf16[32,32,256]{2,1,0:T(8,128)(2,1)}), bf16[32,32,256]{2,1,0:T(8,128)(2,1)S(1)}, u32[]{:S(2)}, u32[]{:S(2)}) async-start(bf16[32,32,256]{2,1,0:T(8,128)(2,1)} %bitcast.23), calls=%async_computation.2 | async-start | bytes 1048576 | tf_op jit(solution)/shard_map/all_to_all | solution.py:460
  124.6 4.2 %shard_map.85.weight_ref = bf16[4,2,512,512]{3,2,1,0:T(8,128)(2,1)} custom-call(bf16[4,2,512,512]{3,2,1,0:T(8,128)(2,1)} %bitcast.35), custom_call_target="tpu_custom_call" | custom-call | bytes 8388608 | tf_op jit(solution)/shard_map/pallas_call | solution.py:147
  128.8 10.2 %all-to-all-done.2 = bf16[32,32,256]{2,1,0:T(8,128)(2,1)S(1)} async-done(((bf16[32,32,256]{2,1,0:T(8,128)(2,1)}), bf16[32,32,256]{2,1,0:T(8,128)(2,1)S(1)}, u32[]{:S(2)}, u32[]{:S(2)}) %all-to-all-start.2) | async-done | bytes 524320 | tf_op jit(solution)/shard_map/all_to_all | solution.py:460
  141.2 2.6 %shard_map.86 = (bf16[64,2048]{1,0:T(8,128)(2,1)S(1)}, bf16[64,2048]{1,0:T(8,128)(2,1)S(1)}, bf16[64,2048]{1,0:T(8,128)(2,1)S(1)}, bf16[64,2048]{1,0:T(8,128)(2,1)S(1)}) custom-call(s32[4]{0:T(128)S(1)} %pad_add_fusion.block_ref, bf16[2,512,256]{2,1,0:T(8,128)(2,1)S(1)} %bitcast.33, bf16[4,2,512,512]{3,2,1,0:T(8,128)(2,1)S(1)} %copy-done.1), custom_call_target="tpu_custom_call" | custom-call | flops 1073741824 | bytes 5767168 | tf_op jit(solution)/shard_map/pallas_call | solution.py:395
  143.8 2.6 %collective-permute-start.8 = (bf16[64,2048]{1,0:T(8,128)(2,1)S(1)}, bf16[64,2048]{1,0:T(8,128)(2,1)S(1)}, u32[]{:S(2)}, u32[]{:S(2)}) collective-permute-start(bf16[64,2048]{1,0:T(8,128)(2,1)S(1)} %get-tuple-element.41), channel_id=1, source_target_pairs={{0,0},{1,16},{2,2},{3,18},{4,4},{5,20},{6,6},{7,22},{8,24},{9,8},{... | collective-permute-start | bytes 786440 | tf_op jit(solution)/shard_map/ppermute | solution.py:86
  146.5 3.9 %collective-permute-start.10 = (bf16[64,2048]{1,0:T(8,128)(2,1)S(1)}, bf16[64,2048]{1,0:T(8,128)(2,1)S(1)}, u32[]{:S(2)}, u32[]{:S(2)}) collective-permute-start(bf16[64,2048]{1,0:T(8,128)(2,1)S(1)} %get-tuple-element.43), channel_id=1, source_target_pairs={{0,16},{1,0},{2,18},{3,2},{4,20},{5,4},{6,22},{7,6},{8,8},{9,24},{... | collective-permute-start | bytes 786440 | tf_op jit(solution)/shard_map/ppermute | solution.py:86
  150.4 2.3 %collective-permute-start.11 = (bf16[64,2048]{1,0:T(8,128)(2,1)S(1)}, bf16[64,2048]{1,0:T(8,128)(2,1)S(1)}, u32[]{:S(2)}, u32[]{:S(2)}) collective-permute-start(bf16[64,2048]{1,0:T(8,128)(2,1)S(1)} %get-tuple-element.44), channel_id=1, source_target_pairs={{0,24},{1,8},{2,26},{3,10},{4,28},{5,12},{6,30},{7,14},{8,0},{9,16... | collective-permute-start | bytes 786440 | tf_op jit(solution)/shard_map/ppermute | solution.py:86
  152.8 3.2 %collective-permute-done.8.refs_0_ = bf16[64,2048]{1,0:T(8,128)(2,1)S(1)} collective-permute-done((bf16[64,2048]{1,0:T(8,128)(2,1)S(1)}, bf16[64,2048]{1,0:T(8,128)(2,1)S(1)}, u32[]{:S(2)}, u32[]{:S(2)}) %collective-permute-start.8) | collective-permute-done | bytes 262176 | tf_op jit(solution)/shard_map/ppermute | solution.py:86
  156.0 16.4 %collective-permute-done.9.refs_1_ = bf16[64,2048]{1,0:T(8,128)(2,1)S(1)} collective-permute-done((bf16[64,2048]{1,0:T(8,128)(2,1)S(1)}, bf16[64,2048]{1,0:T(8,128)(2,1)S(1)}, u32[]{:S(2)}, u32[]{:S(2)}) %collective-permute-start.9) | collective-permute-done | bytes 262176 | tf_op jit(solution)/shard_map/ppermute | solution.py:86
  (41 shorter events, 14.7 us)
Async XLA Ops:
  6.5 10.9 %copy-start = (f32[3,3,512]{2,1,0:T(4,128)S(1)}, f32[3,3,512]{2,1,0:T(4,128)}, u32[]{:S(2)}) copy-start(f32[3,3,512]{2,1,0:T(4,128)} %param.10) | copy-start | bytes 55300
  6.5 2.7 %copy-start.5 = (f32[128,512]{1,0:T(8,128)S(1)}, f32[128,512]{1,0:T(8,128)}, u32[]{:S(2)}) copy-start(f32[128,512]{1,0:T(8,128)} %param.11) | copy-start | bytes 786436
  6.5 54.2 %all-gather.4.cloned.1.call-start = ((), (), s32[]{:S(2)}) async-start(), calls=%async_computation.3 | async-start | bytes 7864320 | tf_op jit(solution)/shard_map/all_gather | solution.py:434
  8.6 13.7 %collective-permute-start = (bf16[2,128,1024]{2,1,0:T(8,128)(2,1)S(1)}, bf16[2,128,1024]{2,1,0:T(8,128)(2,1)S(1)}, u32[]{:S(2)}, u32[]{:S(2)}) collective-permute-start(bf16[2,128,1024]{2,1,0:T(8,128)(2,1)S(1)} %pad_maximum_fusion.1), channel_id=1, source_target_pairs={{0,1},{1,0},{2,3},{3,2},{4,5},{5,4},{6,7},{7,6},{8,9},{9,8},{10,11... | collective-permute-start | bytes 1572872 | tf_op jit(solution)/shard_map/ppermute | solution.py:105
  10.0 17.9 %all-to-all-start = ((f32[16,32,128]{2,1,0:T(8,128)}), f32[16,32,128]{2,1,0:T(8,128)S(1)}, u32[]{:S(2)}, u32[]{:S(2)}) async-start(f32[16,32,128]{2,1,0:T(8,128)} %bitcast.18), calls=%async_computation | async-start | bytes 524288 | tf_op jit(solution)/shard_map/all_to_all | solution.py:445
  16.3 93.8 %all-gather.6.cloned.1.call-start = ((), (), s32[]{:S(2)}) async-start(), calls=%async_computation.4 | async-start | bytes 4718592 | tf_op jit(solution)/shard_map/all_gather | solution.py:449
  22.7 19.6 %collective-permute-start.2 = (bf16[128,1024]{1,0:T(8,128)(2,1)S(1)}, bf16[128,1024]{1,0:T(8,128)(2,1)S(1)}, u32[]{:S(2)}, u32[]{:S(2)}) collective-permute-start(bf16[128,1024]{1,0:T(8,128)(2,1)S(1)} %get-tuple-element.47), channel_id=1, source_target_pairs={{0,8},{2,10},{4,12},{6,14},{8,16},{10,18},{12,20},{14,22},{16,24},... | collective-permute-start | bytes 786440 | tf_op jit(solution)/shard_map/ppermute | solution.py:122
  24.3 18.0 %collective-permute-start.6 = (bf16[128,1024]{1,0:T(8,128)(2,1)S(1)}, bf16[128,1024]{1,0:T(8,128)(2,1)S(1)}, u32[]{:S(2)}, u32[]{:S(2)}) collective-permute-start(bf16[128,1024]{1,0:T(8,128)(2,1)S(1)} %get-tuple-element.45), channel_id=1, source_target_pairs={{0,24},{2,26},{4,28},{6,30},{8,0},{10,2},{12,4},{14,6},{16,8},{18,... | collective-permute-start | bytes 786440 | tf_op jit(solution)/shard_map/ppermute | solution.py:122
  24.8 21.1 %collective-permute-start.4 = (bf16[128,1024]{1,0:T(8,128)(2,1)S(1)}, bf16[128,1024]{1,0:T(8,128)(2,1)S(1)}, u32[]{:S(2)}, u32[]{:S(2)}) collective-permute-start(bf16[128,1024]{1,0:T(8,128)(2,1)S(1)} %get-tuple-element.46), channel_id=1, source_target_pairs={{0,16},{2,18},{4,20},{6,22},{8,24},{10,26},{12,28},{14,30},{16,0},... | collective-permute-start | bytes 786440 | tf_op jit(solution)/shard_map/ppermute | solution.py:122
  27.4 20.5 %collective-permute-start.1 = (bf16[128,1024]{1,0:T(8,128)(2,1)S(1)}, bf16[128,1024]{1,0:T(8,128)(2,1)S(1)}, u32[]{:S(2)}, u32[]{:S(2)}) collective-permute-start(bf16[128,1024]{1,0:T(8,128)(2,1)S(1)} %get-tuple-element.27.refs_0_), channel_id=1, source_target_pairs={{0,1},{1,0},{2,3},{3,2},{4,5},{5,4},{6,7},{7,6},{8,9},{9,8},{10,11... | collective-permute-start | bytes 786440 | tf_op jit(solution)/shard_map/ppermute | solution.py:131
  42.3 9.2 %collective-permute-start.7 = (bf16[128,1024]{1,0:T(8,128)(2,1)S(1)}, bf16[128,1024]{1,0:T(8,128)(2,1)S(1)}, u32[]{:S(2)}, u32[]{:S(2)}) collective-permute-start(bf16[128,1024]{1,0:T(8,128)(2,1)S(1)} %collective-permute-done.6.refs_6_), channel_id=1, source_target_pairs={{0,1},{1,0},{2,3},{3,2},{4,5},{5,4},{6,7},{7,6},{8,9},{9,8},{10,11... | collective-permute-start | bytes 786440 | tf_op jit(solution)/shard_map/ppermute | solution.py:131
  45.9 11.3 %collective-permute-start.5 = (bf16[128,1024]{1,0:T(8,128)(2,1)S(1)}, bf16[128,1024]{1,0:T(8,128)(2,1)S(1)}, u32[]{:S(2)}, u32[]{:S(2)}) collective-permute-start(bf16[128,1024]{1,0:T(8,128)(2,1)S(1)} %collective-permute-done.4.refs_4_), channel_id=1, source_target_pairs={{0,1},{1,0},{2,3},{3,2},{4,5},{5,4},{6,7},{7,6},{8,9},{9,8},{10,11... | collective-permute-start | bytes 786440 | tf_op jit(solution)/shard_map/ppermute | solution.py:131
  46.7 14.0 %collective-permute-start.3 = (bf16[128,1024]{1,0:T(8,128)(2,1)S(1)}, bf16[128,1024]{1,0:T(8,128)(2,1)S(1)}, u32[]{:S(2)}, u32[]{:S(2)}) collective-permute-start(bf16[128,1024]{1,0:T(8,128)(2,1)S(1)} %collective-permute-done.2.refs_2_), channel_id=1, source_target_pairs={{0,1},{1,0},{2,3},{3,2},{4,5},{5,4},{6,7},{7,6},{8,9},{9,8},{10,11... | collective-permute-start | bytes 786440 | tf_op jit(solution)/shard_map/ppermute | solution.py:131
  66.2 3.0 %copy-start.2 = (bf16[6,1024,512]{2,1,0:T(8,128)(2,1)S(1)}, bf16[6,1024,512]{2,1,0:T(8,128)(2,1)}, u32[]{:S(2)}) copy-start(bf16[6,1024,512]{2,1,0:T(8,128)(2,1)} %shard_map.82.refs_8_) | copy-start | bytes 18874372
  69.2 45.6 %copy-start.3 = (f32[256,256]{1,0:T(8,128)S(1)}, f32[256,256]{1,0:T(8,128)}, u32[]{:S(2)}) copy-start(f32[256,256]{1,0:T(8,128)} %constant.230.clone.refs_5_) | copy-start | bytes 786436
  69.2 45.6 %copy-start.4 = (f32[128,256]{1,0:T(8,128)S(1)}, f32[128,256]{1,0:T(8,128)}, u32[]{:S(2)}) copy-start(f32[128,256]{1,0:T(8,128)} %constant.229.clone.refs_4_) | copy-start | bytes 393220
  73.9 40.9 %all-to-all-start.1 = ((bf16[16,3,32,512]{3,2,1,0:T(8,128)(2,1)}), bf16[16,3,32,512]{3,2,1,0:T(8,128)(2,1)S(1)}, u32[]{:S(2)}, u32[]{:S(2)}) async-start(bf16[16,3,32,512]{3,2,1,0:T(8,128)(2,1)} %shard_map.83), calls=%async_computation.1 | async-start | bytes 3145728 | tf_op jit(solution)/shard_map/all_to_all | solution.py:454
  118.5 20.5 %all-to-all-start.2 = ((bf16[32,32,256]{2,1,0:T(8,128)(2,1)}), bf16[32,32,256]{2,1,0:T(8,128)(2,1)S(1)}, u32[]{:S(2)}, u32[]{:S(2)}) async-start(bf16[32,32,256]{2,1,0:T(8,128)(2,1)} %bitcast.23), calls=%async_computation.2 | async-start | bytes 1048576 | tf_op jit(solution)/shard_map/all_to_all | solution.py:460
  139.0 2.2 %copy-start.1 = (bf16[4,2,512,512]{3,2,1,0:T(8,128)(2,1)S(1)}, bf16[4,2,512,512]{3,2,1,0:T(8,128)(2,1)}, u32[]{:S(2)}) copy-start(bf16[4,2,512,512]{3,2,1,0:T(8,128)(2,1)} %shard_map.85.weight_ref) | copy-start | bytes 12582916
  143.8 12.1 %collective-permute-start.8 = (bf16[64,2048]{1,0:T(8,128)(2,1)S(1)}, bf16[64,2048]{1,0:T(8,128)(2,1)S(1)}, u32[]{:S(2)}, u32[]{:S(2)}) collective-permute-start(bf16[64,2048]{1,0:T(8,128)(2,1)S(1)} %get-tuple-element.41), channel_id=1, source_target_pairs={{0,0},{1,16},{2,2},{3,18},{4,4},{5,20},{6,6},{7,22},{8,24},{9,8},{... | collective-permute-start | bytes 786440 | tf_op jit(solution)/shard_map/ppermute | solution.py:86
  146.4 25.9 %collective-permute-start.9 = (bf16[64,2048]{1,0:T(8,128)(2,1)S(1)}, bf16[64,2048]{1,0:T(8,128)(2,1)S(1)}, u32[]{:S(2)}, u32[]{:S(2)}) collective-permute-start(bf16[64,2048]{1,0:T(8,128)(2,1)S(1)} %get-tuple-element.42), channel_id=1, source_target_pairs={{0,8},{1,24},{2,10},{3,26},{4,12},{5,28},{6,14},{7,30},{8,16},{9,0... | collective-permute-start | bytes 786440 | tf_op jit(solution)/shard_map/ppermute | solution.py:86
  146.5 25.8 %collective-permute-start.10 = (bf16[64,2048]{1,0:T(8,128)(2,1)S(1)}, bf16[64,2048]{1,0:T(8,128)(2,1)S(1)}, u32[]{:S(2)}, u32[]{:S(2)}) collective-permute-start(bf16[64,2048]{1,0:T(8,128)(2,1)S(1)} %get-tuple-element.43), channel_id=1, source_target_pairs={{0,16},{1,0},{2,18},{3,2},{4,20},{5,4},{6,22},{7,6},{8,8},{9,24},{... | collective-permute-start | bytes 786440 | tf_op jit(solution)/shard_map/ppermute | solution.py:86
  150.4 22.0 %collective-permute-start.11 = (bf16[64,2048]{1,0:T(8,128)(2,1)S(1)}, bf16[64,2048]{1,0:T(8,128)(2,1)S(1)}, u32[]{:S(2)}, u32[]{:S(2)}) collective-permute-start(bf16[64,2048]{1,0:T(8,128)(2,1)S(1)} %get-tuple-element.44), channel_id=1, source_target_pairs={{0,24},{1,8},{2,26},{3,10},{4,28},{5,12},{6,30},{7,14},{8,0},{9,16... | collective-permute-start | bytes 786440 | tf_op jit(solution)/shard_map/ppermute | solution.py:86
Sparse Core Ops, SparseCore 0:
  8.9 49.2 all-gather.3
  60.8 49.2 all-gather.5

commit v10 on v9

--- a/solution.py
+++ b/solution.py
@@ -12,6 +12,7 @@
 HIGHEST = lax.Precision.HIGHEST
 UNROLL = 16
 HEAVY = 30
+HALVES = 2
 
 
 def outer_factor(seq_parts, tp_parts):
@@ -150,7 +151,7 @@
         in_specs=[pl.BlockSpec(memory_space=pl.ANY)],
         out_specs=pl.BlockSpec(memory_space=pltpu.VMEM),
         scratch_shapes=[pltpu.SemaphoreType.DMA((source.shape[0],))],
-        compiler_params=pltpu.CompilerParams(vmem_limit_bytes=60 * 2**20 - 2 * source.size),
+        compiler_params=pltpu.CompilerParams(vmem_limit_bytes=16 * 2**20),
         cost_estimate=pl.CostEstimate(
             flops=0, bytes_accessed=4 * source.size, transcendentals=0
         ),
@@ -158,20 +159,25 @@
 
 
 def project_kernel(tp_parts, place_ref, *refs):
-    *share_refs, weight_ref, out_ref = refs
+    *share_refs, weight_ref, out_ref, held, sems = refs
     seq_parts, streams, chans, count = out_ref.shape
+    copies = [
+        pltpu.make_async_copy(weight_ref.at[stream], held.at[stream], sems.at[stream])
+        for stream in range(streams)
+    ]
+    for copy in copies:
+        copy.start()
     left = [
         jnp.concatenate([share_ref[...] for share_ref in share_refs[step::tp_parts]])
         for step in range(tp_parts)
     ]
     for stream in range(streams):
+        copies[stream].wait()
         sums = jnp.zeros((count, seq_parts * chans), jnp.float32)
         for step in range(tp_parts):
             which = lax.rem(place_ref[0] - step + tp_parts, tp_parts)
             sums = sums + jnp.dot(
-                left[step],
-                weight_ref[stream * tp_parts + which],
-                preferred_element_type=jnp.float32,
+                left[step], held[stream, which], preferred_element_type=jnp.float32
             )
         turned = sums.astype(out_ref.dtype).T
         for seq in range(seq_parts):
@@ -181,18 +187,25 @@
 def project_in(chunks, weight, seq_parts):
     tp_parts = len(chunks[0])
     rows, width = chunks[0][0].shape
-    streams = weight.shape[0] // tp_parts
-    chans = weight.shape[2] // seq_parts
+    streams, _, chan_tp = weight.shape
+    weight = weight.reshape(streams, tp_parts, width, chan_tp)
+    chans = chan_tp // seq_parts
     pieces = [piece for chunk in chunks for piece in chunk]
     count = len(chunks) * rows
     place = lax.axis_index("tp").astype(jnp.int32)[None]
     vmem = pl.BlockSpec(memory_space=pltpu.VMEM)
     return pl.pallas_call(
         functools.partial(project_kernel, tp_parts),
-        in_specs=[pl.BlockSpec(memory_space=pltpu.SMEM)] + [vmem] * (len(pieces) + 1),
+        in_specs=[pl.BlockSpec(memory_space=pltpu.SMEM)]
+        + [vmem] * len(pieces)
+        + [pl.BlockSpec(memory_space=pl.ANY)],
         out_specs=vmem,
         out_shape=jax.ShapeDtypeStruct((seq_parts, streams, chans, count), jnp.bfloat16),
-        compiler_params=pltpu.CompilerParams(vmem_limit_bytes=32 * 2**20),
+        scratch_shapes=[
+            pltpu.VMEM(weight.shape, weight.dtype),
+            pltpu.SemaphoreType.DMA((streams,)),
+        ],
+        compiler_params=pltpu.CompilerParams(vmem_limit_bytes=56 * 2**20),
         cost_estimate=pl.CostEstimate(
             flops=HEAVY * 2 * count * weight.size,
             bytes_accessed=2 * (weight.size + len(pieces) * pieces[0].size)
@@ -439,9 +452,14 @@
     skip = jnp.broadcast_to(skip[:, None], (chans, rows))
     filter_blocks = long_filter.T.reshape(seq_parts, chans, rows)
 
-    held = share_columns(features, outer, tp_parts)
-    held, taps, skip = lax.optimization_barrier((held, taps, skip))
-    arrived = cross_outer(held, outer, inner_parts, tp_parts)
+    half = rows // HALVES
+    held = [
+        share_columns(features[index * half : (index + 1) * half], outer, tp_parts)
+        for index in range(HALVES)
+    ]
+    held[-1], taps, skip = lax.optimization_barrier((held[-1], taps, skip))
+    arrived = [cross_outer(part, outer, inner_parts, tp_parts) for part in held]
+    arrived = [jnp.concatenate(parts) for parts in zip(*arrived)]
     filter_blocks = lax.all_to_all(filter_blocks, "seq", split_axis=0, concat_axis=0, tiled=True)
     arrived[1], filter_blocks = lax.optimization_barrier((arrived[1], filter_blocks))
     chunks = [share_over_tp(piece, tp_parts) for piece in arrived]
@@ -449,7 +467,6 @@
     out_weight = lax.all_gather(out_proj, ("seq", "tp"), axis_index_groups=tp_groups)
     out_weight = out_weight.reshape((inner_parts, tp_parts) + out_proj.shape)
 
-    weight = fetch(weight.reshape(streams * tp_parts, -1, chan_tp))
     partial = project_in(chunks, weight, seq_parts)
     parts = lax.all_to_all(partial, "seq", split_axis=0, concat_axis=0, tiled=True)
 

time: 182 us -> 188 us (1.033)
  starting transfers between devices: 35.6 us -> 47.2 us
  Pallas kernels: 22.8 us -> 17.1 us
  local copies, waits for them, and re-layouts: 8.5 us -> 10.4 us
    pallas_call x2 -> x1, Pallas kernels: 9.65 us -> 0.32 us  [fetch(): pl.pallas_call(fetch_kernel, out_shape=jax.ShapeDtypeStruct(source.shape,...]
    ppermute x4, waiting for transfers between devices: 12.7 us -> 20.1 us  [share_over_tp(): pieces.append(lax.ppermute(part, 'tp', pairs))]
    ppermute x3 -> x6, starting transfers between devices: 4.67 us -> 10 us  [cross_outer(): lax.ppermute(piece, 'seq', [(i, (i + far) % seq_parts) for i in range(seq...]
    ppermute x1 -> x2, waiting for transfers between devices: 4.89 us -> 0.34 us  [share_columns(): lax.ppermute(piece, 'tp', [(i, (i + step) % tp_parts) for i in range(tp_p...]
    ppermute x3 -> x6, waiting for transfers between devices: 17.2 us -> 12.9 us  [cross_outer(): lax.ppermute(piece, 'seq', [(i, (i + far) % seq_parts) for i in range(seq...]
    all_to_all x1, starting transfers between devices: 5.93 us -> 9.6 us  [per_device(): lax.all_to_all(partial, 'seq', split_axis=0, concat_axis=0, tiled=True)]
    pallas_call x1, Pallas kernels: 4.68 us -> 8.29 us  [project_in(): pl.pallas_call(functools.partial(project_kernel, tp_parts), in_specs=[pl....]
    unnamed x12 -> x32, local copies, waits for them, and re-layouts: 5.23 us -> 6.97 us
  transfers between devices with their start and end apart: 17 -> 21, of which waited for: 11 -> 12; matrix products, arithmetic and copies ran while one was open for 2% -> 2% of each run, Pallas kernels for 8% -> 5%
where the time goes in v10:
time: 188 us; the launch traced here: 187 us
  waiting for transfers between devices  98.4 us (52%)
  starting transfers between devices  47.2 us (25%)
  Pallas kernels  17.1 us (9%)
  between operations  14 us (7%)
  local copies, waits for them, and re-layouts  10.4 us (6%)
    all_gather x1, waiting for transfers between devices, per_device(): lax.all_gather(out_proj, ('seq', 'tp'), axis_index_groups=tp_groups)  30.5 us
    ppermute x4, waiting for transfers between devices, share_over_tp(): pieces.append(lax.ppermute(part, 'tp', pairs))  20.1 us
    ppermute x4, waiting for transfers between devices, return_output(): arrived.append(lax.ppermute(piece, ('seq', 'tp'), pairs))  19.5 us
    ppermute x6, waiting for transfers between devices, cross_outer(): lax.ppermute(piece, 'seq', [(i, (i + far) % seq_parts) for i in range(seq...  12.9 us
    ppermute x6, starting transfers between devices, cross_outer(): lax.ppermute(piece, 'seq', [(i, (i + far) % seq_parts) for i in range(seq...  10 us
    all_to_all x1, waiting for transfers between devices, per_device(): lax.all_to_all(gated.reshape((-1,) + gated.shape[3:]), ('tp', 'seq'), spl...  9.91 us
    all_to_all x1, starting transfers between devices, per_device(): lax.all_to_all(partial, 'seq', split_axis=0, concat_axis=0, tiled=True)  9.6 us
    ppermute x4, starting transfers between devices, return_output(): arrived.append(lax.ppermute(piece, ('seq', 'tp'), pairs))  8.85 us
  transfers between devices with their start and end apart: 21, of which 12 were waited for; matrix products, arithmetic and copies ran while one was open for 2% of the time, Pallas kernels for 5%

profile of v10, /device:TPU:12, one launch (start us, length us, event | category | flops | bytes accessed | tf_op | source)
XLA Modules:
  0.0 187.4 jit_solution(10643716511126380309)
XLA Ops:
  10.1 6.3 %all-to-all-start = ((f32[16,32,128]{2,1,0:T(8,128)}), f32[16,32,128]{2,1,0:T(8,128)S(1)}, u32[]{:S(2)}, u32[]{:S(2)}) async-start(f32[16,32,128]{2,1,0:T(8,128)} %bitcast.24), calls=%async_computation | async-start | bytes 524288 | tf_op jit(solution)/shard_map/all_to_all | solution.py:463
  19.4 2.8 %collective-permute-start.6 = (bf16[64,1024]{1,0:T(8,128)(2,1)S(1)}, bf16[64,1024]{1,0:T(8,128)(2,1)S(1)}, u32[]{:S(2)}, u32[]{:S(2)}) collective-permute-start(bf16[64,1024]{1,0:T(8,128)(2,1)S(1)} %get-tuple-element.52), channel_id=1, source_target_pairs={{0,16},{2,18},{4,20},{6,22},{8,24},{10,26},{12,28},{14,30},{16,0},... | collective-permute-start | bytes 393224 | tf_op jit(solution)/shard_map/ppermute | solution.py:123
  22.2 2.4 %collective-permute-start.3 = (bf16[64,1024]{1,0:T(8,128)(2,1)S(1)}, bf16[64,1024]{1,0:T(8,128)(2,1)S(1)}, u32[]{:S(2)}, u32[]{:S(2)}) collective-permute-start(bf16[64,1024]{1,0:T(8,128)(2,1)S(1)} %get-tuple-element.53), channel_id=1, source_target_pairs={{0,8},{2,10},{4,12},{6,14},{8,16},{10,18},{12,20},{14,22},{16,24},... | collective-permute-start | bytes 393224 | tf_op jit(solution)/shard_map/ppermute | solution.py:123
  25.6 2.5 %collective-permute-start.7 = (bf16[64,1024]{1,0:T(8,128)(2,1)S(1)}, bf16[64,1024]{1,0:T(8,128)(2,1)S(1)}, u32[]{:S(2)}, u32[]{:S(2)}) collective-permute-start(bf16[64,1024]{1,0:T(8,128)(2,1)S(1)} %get-tuple-element.48), channel_id=1, source_target_pairs={{0,16},{2,18},{4,20},{6,22},{8,24},{10,26},{12,28},{14,30},{16,0},... | collective-permute-start | bytes 393224 | tf_op jit(solution)/shard_map/ppermute | solution.py:123
  28.2 8.8 %collective-permute-done.6 = bf16[64,1024]{1,0:T(8,128)(2,1)S(1)} collective-permute-done((bf16[64,1024]{1,0:T(8,128)(2,1)S(1)}, bf16[64,1024]{1,0:T(8,128)(2,1)S(1)}, u32[]{:S(2)}, u32[]{:S(2)}) %collective-permute-start.6) | collective-permute-done | bytes 131104 | tf_op jit(solution)/shard_map/ppermute | solution.py:123
  38.8 4.0 %collective-permute-done.7 = bf16[64,1024]{1,0:T(8,128)(2,1)S(1)} collective-permute-done((bf16[64,1024]{1,0:T(8,128)(2,1)S(1)}, bf16[64,1024]{1,0:T(8,128)(2,1)S(1)}, u32[]{:S(2)}, u32[]{:S(2)}) %collective-permute-start.7) | collective-permute-done | bytes 131104 | tf_op jit(solution)/shard_map/ppermute | solution.py:123
  47.2 4.9 %collective-permute-done.2.refs_1_ = bf16[128,1024]{1,0:T(8,128)(2,1)S(1)} collective-permute-done((bf16[128,1024]{1,0:T(8,128)(2,1)S(1)}, bf16[128,1024]{1,0:T(8,128)(2,1)S(1)}, u32[]{:S(2)}, u32[]{:S(2)}) %collective-permute-start.2) | collective-permute-done | bytes 262176 | tf_op jit(solution)/shard_map/ppermute | solution.py:132
  52.0 5.6 %collective-permute-done.8.refs_5_ = bf16[128,1024]{1,0:T(8,128)(2,1)S(1)} collective-permute-done((bf16[128,1024]{1,0:T(8,128)(2,1)S(1)}, bf16[128,1024]{1,0:T(8,128)(2,1)S(1)}, u32[]{:S(2)}, u32[]{:S(2)}) %collective-permute-start.8) | collective-permute-done | bytes 262176 | tf_op jit(solution)/shard_map/ppermute | solution.py:132
  57.6 5.6 %collective-permute-done.11.refs_7_ = bf16[128,1024]{1,0:T(8,128)(2,1)S(1)} collective-permute-done((bf16[128,1024]{1,0:T(8,128)(2,1)S(1)}, bf16[128,1024]{1,0:T(8,128)(2,1)S(1)}, u32[]{:S(2)}, u32[]{:S(2)}) %collective-permute-start.11) | collective-permute-done | bytes 262176 | tf_op jit(solution)/shard_map/ppermute | solution.py:132
  63.3 4.0 %collective-permute-done.5.refs_3_ = bf16[128,1024]{1,0:T(8,128)(2,1)S(1)} collective-permute-done((bf16[128,1024]{1,0:T(8,128)(2,1)S(1)}, bf16[128,1024]{1,0:T(8,128)(2,1)S(1)}, u32[]{:S(2)}, u32[]{:S(2)}) %collective-permute-start.5) | collective-permute-done | bytes 262176 | tf_op jit(solution)/shard_map/ppermute | solution.py:132
  67.9 8.3 %shard_map.82 = bf16[16,3,32,512]{3,2,1,0:T(8,128)(2,1)} custom-call(s32[1]{0:T(128)} %bitcast.10.place_ref, bf16[128,1024]{1,0:T(8,128)(2,1)} %copy-done.7, bf16[128,1024]{1,0:T(8,128)(2,1)} %copy-done.11, bf16[128,1024]{1,0:T(8,128)(2,1)} %copy-done.8, bf16[128,1024]{1,0:T(8,128)(2,1)} %copy-done.14, bf16[128,1024]{1,0:T(8,128)(2,1)} %copy-done.9, ...), custom_call_target="tpu_custom_call" | custom-call | flops 96636764160 | bytes 9961472 | tf_op jit(solution)/shard_map/pallas_call | solution.py:197
  76.2 9.6 %all-to-all-start.1 = ((bf16[16,3,32,512]{3,2,1,0:T(8,128)(2,1)}), bf16[16,3,32,512]{3,2,1,0:T(8,128)(2,1)S(1)}, u32[]{:S(2)}, u32[]{:S(2)}) async-start(bf16[16,3,32,512]{3,2,1,0:T(8,128)(2,1)} %shard_map.82), calls=%async_computation.1 | async-start | bytes 3145728 | tf_op jit(solution)/shard_map/all_to_all | solution.py:471
  85.8 30.5 %all-gather.6.cloned.1.call-done = bf16[4096,512]{1,0:T(8,128)(2,1)} async-done(((bf16[512,512]{1,0:T(8,128)(2,1)}), bf16[4096,512]{1,0:T(8,128)(2,1)}) %all-gather.6.cloned.1.call-update) | async-done | bytes 4194320 | tf_op jit(solution)/shard_map/all_gather | solution.py:467
  116.3 4.5 %all-to-all-done.1.refs_0_ = bf16[16,3,32,512]{3,2,1,0:T(8,128)(2,1)S(1)} async-done(((bf16[16,3,32,512]{3,2,1,0:T(8,128)(2,1)}), bf16[16,3,32,512]{3,2,1,0:T(8,128)(2,1)S(1)}, u32[]{:S(2)}, u32[]{:S(2)}) %all-to-all-start.1) | async-done | bytes 1572896 | tf_op jit(solution)/shard_map/all_to_all | solution.py:471
  120.8 3.7 %shard_map.83 = bf16[2,4,4,32,256]{4,3,2,1,0:T(8,128)(2,1)} custom-call(bf16[16,3,32,512]{3,2,1,0:T(8,128)(2,1)S(1)} %all-to-all-done.1.refs_0_, f32[16,32,128]{2,1,0:T(8,128)S(1)} %all-to-all-done.refs_1_, f32[3,3,32,128]{3,2,1,0:T(8,128)S(1)} %broadcast_in_dim.7.refs_2_, f32[32,128]{1,0:T(8,128)S(1)} %broadcast_in_dim.8.refs_3_, f32[128,256]{1,0:T(8,128)S(1)} %copy-done.5, ...), custom_call_target="tpu_custom_call" | custom-call | flops 1000000000 | bytes 4194304 | tf_op jit(solution)/shard_map/pallas_call | solution.py:362
  124.5 6.0 %all-to-all-start.2 = ((bf16[32,32,256]{2,1,0:T(8,128)(2,1)}), bf16[32,32,256]{2,1,0:T(8,128)(2,1)S(1)}, u32[]{:S(2)}, u32[]{:S(2)}) async-start(bf16[32,32,256]{2,1,0:T(8,128)(2,1)} %bitcast.31), calls=%async_computation.2 | async-start | bytes 1048576 | tf_op jit(solution)/shard_map/all_to_all | solution.py:477
  130.7 2.2 %copy-done.3 = bf16[4096,512]{1,0:T(8,128)(2,1)S(1)} copy-done((bf16[4096,512]{1,0:T(8,128)(2,1)S(1)}, bf16[4096,512]{1,0:T(8,128)(2,1)}, u32[]{:S(2)}) %copy-start.3) | copy-done | bytes 4194328
  135.2 9.9 %all-to-all-done.2 = bf16[32,32,256]{2,1,0:T(8,128)(2,1)S(1)} async-done(((bf16[32,32,256]{2,1,0:T(8,128)(2,1)}), bf16[32,32,256]{2,1,0:T(8,128)(2,1)S(1)}, u32[]{:S(2)}, u32[]{:S(2)}) %all-to-all-start.2) | async-done | bytes 524320 | tf_op jit(solution)/shard_map/all_to_all | solution.py:477
  147.2 2.6 %shard_map.85 = (bf16[64,2048]{1,0:T(8,128)(2,1)S(1)}, bf16[64,2048]{1,0:T(8,128)(2,1)S(1)}, bf16[64,2048]{1,0:T(8,128)(2,1)S(1)}, bf16[64,2048]{1,0:T(8,128)(2,1)S(1)}) custom-call(s32[4]{0:T(128)S(1)} %pad_add_fusion.block_ref, bf16[2,512,256]{2,1,0:T(8,128)(2,1)S(1)} %bitcast.50, bf16[4,2,512,512]{3,2,1,0:T(8,128)(2,1)S(1)} %copy-done.2), custom_call_target="tpu_custom_call" | custom-call | flops 1073741824 | bytes 5767168 | tf_op jit(solution)/shard_map/pallas_call | solution.py:408
  149.9 2.6 %collective-permute-start.12 = (bf16[64,2048]{1,0:T(8,128)(2,1)S(1)}, bf16[64,2048]{1,0:T(8,128)(2,1)S(1)}, u32[]{:S(2)}, u32[]{:S(2)}) collective-permute-start(bf16[64,2048]{1,0:T(8,128)(2,1)S(1)} %get-tuple-element.41), channel_id=1, source_target_pairs={{0,0},{1,16},{2,2},{3,18},{4,4},{5,20},{6,6},{7,22},{8,24},{9,8},{... | collective-permute-start | bytes 786440 | tf_op jit(solution)/shard_map/ppermute | solution.py:87
  152.6 3.9 %collective-permute-start.14 = (bf16[64,2048]{1,0:T(8,128)(2,1)S(1)}, bf16[64,2048]{1,0:T(8,128)(2,1)S(1)}, u32[]{:S(2)}, u32[]{:S(2)}) collective-permute-start(bf16[64,2048]{1,0:T(8,128)(2,1)S(1)} %get-tuple-element.43), channel_id=1, source_target_pairs={{0,16},{1,0},{2,18},{3,2},{4,20},{5,4},{6,22},{7,6},{8,8},{9,24},{... | collective-permute-start | bytes 786440 | tf_op jit(solution)/shard_map/ppermute | solution.py:87
  156.5 2.3 %collective-permute-start.15 = (bf16[64,2048]{1,0:T(8,128)(2,1)S(1)}, bf16[64,2048]{1,0:T(8,128)(2,1)S(1)}, u32[]{:S(2)}, u32[]{:S(2)}) collective-permute-start(bf16[64,2048]{1,0:T(8,128)(2,1)S(1)} %get-tuple-element.44), channel_id=1, source_target_pairs={{0,24},{1,8},{2,26},{3,10},{4,28},{5,12},{6,30},{7,14},{8,0},{9,16... | collective-permute-start | bytes 786440 | tf_op jit(solution)/shard_map/ppermute | solution.py:87
  158.9 3.2 %collective-permute-done.12.refs_0_ = bf16[64,2048]{1,0:T(8,128)(2,1)S(1)} collective-permute-done((bf16[64,2048]{1,0:T(8,128)(2,1)S(1)}, bf16[64,2048]{1,0:T(8,128)(2,1)S(1)}, u32[]{:S(2)}, u32[]{:S(2)}) %collective-permute-start.12) | collective-permute-done | bytes 262176 | tf_op jit(solution)/shard_map/ppermute | solution.py:87
  162.0 16.4 %collective-permute-done.13.refs_1_ = bf16[64,2048]{1,0:T(8,128)(2,1)S(1)} collective-permute-done((bf16[64,2048]{1,0:T(8,128)(2,1)S(1)}, bf16[64,2048]{1,0:T(8,128)(2,1)S(1)}, u32[]{:S(2)}, u32[]{:S(2)}) %collective-permute-start.13) | collective-permute-done | bytes 262176 | tf_op jit(solution)/shard_map/ppermute | solution.py:87
  (76 shorter events, 20.8 us)
Async XLA Ops:
  6.5 60.7 %all-gather.4.cloned.1.call-start = ((), (), s32[]{:S(2)}) async-start(), calls=%async_computation.3 | async-start | bytes 7864320 | tf_op jit(solution)/shard_map/all_gather | solution.py:447
  8.7 10.4 %collective-permute-start = (bf16[2,64,1024]{2,1,0:T(8,128)(2,1)S(1)}, bf16[2,64,1024]{2,1,0:T(8,128)(2,1)S(1)}, u32[]{:S(2)}, u32[]{:S(2)}) collective-permute-start(bf16[2,64,1024]{2,1,0:T(8,128)(2,1)S(1)} %pad_maximum_fusion.2), channel_id=1, source_target_pairs={{0,1},{1,0},{2,3},{3,2},{4,5},{5,4},{6,7},{7,6},{8,9},{9,8},{10,11... | collective-permute-start | bytes 786440 | tf_op jit(solution)/shard_map/ppermute | solution.py:106
  10.1 36.5 %all-to-all-start = ((f32[16,32,128]{2,1,0:T(8,128)}), f32[16,32,128]{2,1,0:T(8,128)S(1)}, u32[]{:S(2)}, u32[]{:S(2)}) async-start(f32[16,32,128]{2,1,0:T(8,128)} %bitcast.24), calls=%async_computation | async-start | bytes 524288 | tf_op jit(solution)/shard_map/all_to_all | solution.py:463
  16.4 99.9 %all-gather.6.cloned.1.call-start = ((), (), s32[]{:S(2)}) async-start(), calls=%async_computation.4 | async-start | bytes 4718592 | tf_op jit(solution)/shard_map/all_gather | solution.py:467
  16.5 8.4 %collective-permute-start.1 = (bf16[2,64,1024]{2,1,0:T(8,128)(2,1)S(1)}, bf16[2,64,1024]{2,1,0:T(8,128)(2,1)S(1)}, u32[]{:S(2)}, u32[]{:S(2)}) collective-permute-start(bf16[2,64,1024]{2,1,0:T(8,128)(2,1)S(1)} %pad_maximum_fusion.3), channel_id=1, source_target_pairs={{0,1},{1,0},{2,3},{3,2},{4,5},{5,4},{6,7},{7,6},{8,9},{9,8},{10,11... | collective-permute-start | bytes 786440 | tf_op jit(solution)/shard_map/ppermute | solution.py:106
  19.2 25.1 %collective-permute-start.9 = (bf16[64,1024]{1,0:T(8,128)(2,1)S(1)}, bf16[64,1024]{1,0:T(8,128)(2,1)S(1)}, u32[]{:S(2)}, u32[]{:S(2)}) collective-permute-start(bf16[64,1024]{1,0:T(8,128)(2,1)S(1)} %get-tuple-element.51), channel_id=1, source_target_pairs={{0,24},{2,26},{4,28},{6,30},{8,0},{10,2},{12,4},{14,6},{16,8},{18,... | collective-permute-start | bytes 393224 | tf_op jit(solution)/shard_map/ppermute | solution.py:123
  19.4 17.6 %collective-permute-start.6 = (bf16[64,1024]{1,0:T(8,128)(2,1)S(1)}, bf16[64,1024]{1,0:T(8,128)(2,1)S(1)}, u32[]{:S(2)}, u32[]{:S(2)}) collective-permute-start(bf16[64,1024]{1,0:T(8,128)(2,1)S(1)} %get-tuple-element.52), channel_id=1, source_target_pairs={{0,16},{2,18},{4,20},{6,22},{8,24},{10,26},{12,28},{14,30},{16,0},... | collective-permute-start | bytes 393224 | tf_op jit(solution)/shard_map/ppermute | solution.py:123
  22.2 24.4 %collective-permute-start.3 = (bf16[64,1024]{1,0:T(8,128)(2,1)S(1)}, bf16[64,1024]{1,0:T(8,128)(2,1)S(1)}, u32[]{:S(2)}, u32[]{:S(2)}) collective-permute-start(bf16[64,1024]{1,0:T(8,128)(2,1)S(1)} %get-tuple-element.53), channel_id=1, source_target_pairs={{0,8},{2,10},{4,12},{6,14},{8,16},{10,18},{12,20},{14,22},{16,24},... | collective-permute-start | bytes 393224 | tf_op jit(solution)/shard_map/ppermute | solution.py:123
  25.2 19.7 %collective-permute-start.10 = (bf16[64,1024]{1,0:T(8,128)(2,1)S(1)}, bf16[64,1024]{1,0:T(8,128)(2,1)S(1)}, u32[]{:S(2)}, u32[]{:S(2)}) collective-permute-start(bf16[64,1024]{1,0:T(8,128)(2,1)S(1)} %get-tuple-element.47), channel_id=1, source_target_pairs={{0,24},{2,26},{4,28},{6,30},{8,0},{10,2},{12,4},{14,6},{16,8},{18,... | collective-permute-start | bytes 393224 | tf_op jit(solution)/shard_map/ppermute | solution.py:123
  25.6 17.2 %collective-permute-start.7 = (bf16[64,1024]{1,0:T(8,128)(2,1)S(1)}, bf16[64,1024]{1,0:T(8,128)(2,1)S(1)}, u32[]{:S(2)}, u32[]{:S(2)}) collective-permute-start(bf16[64,1024]{1,0:T(8,128)(2,1)S(1)} %get-tuple-element.48), channel_id=1, source_target_pairs={{0,16},{2,18},{4,20},{6,22},{8,24},{10,26},{12,28},{14,30},{16,0},... | collective-permute-start | bytes 393224 | tf_op jit(solution)/shard_map/ppermute | solution.py:123
  28.2 39.1 %copy-start.7 = (bf16[128,1024]{1,0:T(8,128)(2,1)}, bf16[128,1024]{1,0:T(8,128)(2,1)S(1)}, u32[]{:S(2)}) copy-start(bf16[128,1024]{1,0:T(8,128)(2,1)S(1)} %pad_maximum_fusion.4.refs_0_) | copy-start | bytes 786436
  37.0 9.6 %collective-permute-start.4 = (bf16[64,1024]{1,0:T(8,128)(2,1)S(1)}, bf16[64,1024]{1,0:T(8,128)(2,1)S(1)}, u32[]{:S(2)}, u32[]{:S(2)}) collective-permute-start(bf16[64,1024]{1,0:T(8,128)(2,1)S(1)} %get-tuple-element.49), channel_id=1, source_target_pairs={{0,8},{2,10},{4,12},{6,14},{8,16},{10,18},{12,20},{14,22},{16,24},... | collective-permute-start | bytes 393224 | tf_op jit(solution)/shard_map/ppermute | solution.py:123
  42.8 9.2 %collective-permute-start.2 = (bf16[128,1024]{1,0:T(8,128)(2,1)S(1)}, bf16[128,1024]{1,0:T(8,128)(2,1)S(1)}, u32[]{:S(2)}, u32[]{:S(2)}) collective-permute-start(bf16[128,1024]{1,0:T(8,128)(2,1)S(1)} %pad_maximum_fusion.4.refs_0_), channel_id=1, source_target_pairs={{0,1},{1,0},{2,3},{3,2},{4,5},{5,4},{6,7},{7,6},{8,9},{9,8},{10,11... | collective-permute-start | bytes 786440 | tf_op jit(solution)/shard_map/ppermute | solution.py:132
  44.4 13.3 %collective-permute-start.8 = (bf16[128,1024]{1,0:T(8,128)(2,1)S(1)}, bf16[128,1024]{1,0:T(8,128)(2,1)S(1)}, u32[]{:S(2)}, u32[]{:S(2)}) collective-permute-start(bf16[128,1024]{1,0:T(8,128)(2,1)S(1)} %constant_dynamic-update-slice_fusion.refs_4_), channel_id=1, source_target_pairs={{0,1},{1,0},{2,3},{3,2},{4,5},{5,4},{6,7},{7,6},{8,9},{9,8},{10,11... | collective-permute-start | bytes 786440 | tf_op jit(solution)/shard_map/ppermute | solution.py:132
  45.0 18.3 %collective-permute-start.11 = (bf16[128,1024]{1,0:T(8,128)(2,1)S(1)}, bf16[128,1024]{1,0:T(8,128)(2,1)S(1)}, u32[]{:S(2)}, u32[]{:S(2)}) collective-permute-start(bf16[128,1024]{1,0:T(8,128)(2,1)S(1)} %constant_dynamic-update-slice_fusion.2.refs_6_), channel_id=1, source_target_pairs={{0,1},{1,0},{2,3},{3,2},{4,5},{5,4},{6,7},{7,6},{8,9},{9,8},{10,11... | collective-permute-start | bytes 786440 | tf_op jit(solution)/shard_map/ppermute | solution.py:132
  46.6 20.6 %collective-permute-start.5 = (bf16[128,1024]{1,0:T(8,128)(2,1)S(1)}, bf16[128,1024]{1,0:T(8,128)(2,1)S(1)}, u32[]{:S(2)}, u32[]{:S(2)}) collective-permute-start(bf16[128,1024]{1,0:T(8,128)(2,1)S(1)} %pad_maximum_fusion.5.refs_2_), channel_id=1, source_target_pairs={{0,1},{1,0},{2,3},{3,2},{4,5},{5,4},{6,7},{7,6},{8,9},{9,8},{10,11... | collective-permute-start | bytes 786440 | tf_op jit(solution)/shard_map/ppermute | solution.py:132
  67.9 52.9 %copy-start.4 = (f32[256,256]{1,0:T(8,128)S(1)}, f32[256,256]{1,0:T(8,128)}, u32[]{:S(2)}) copy-start(f32[256,256]{1,0:T(8,128)} %constant.276.clone.refs_5_) | copy-start | bytes 786436
  67.9 52.9 %copy-start.5 = (f32[128,256]{1,0:T(8,128)S(1)}, f32[128,256]{1,0:T(8,128)}, u32[]{:S(2)}) copy-start(f32[128,256]{1,0:T(8,128)} %constant.275.clone.refs_4_) | copy-start | bytes 393220
  76.2 44.6 %all-to-all-start.1 = ((bf16[16,3,32,512]{3,2,1,0:T(8,128)(2,1)}), bf16[16,3,32,512]{3,2,1,0:T(8,128)(2,1)S(1)}, u32[]{:S(2)}, u32[]{:S(2)}) async-start(bf16[16,3,32,512]{3,2,1,0:T(8,128)(2,1)} %shard_map.82), calls=%async_computation.1 | async-start | bytes 3145728 | tf_op jit(solution)/shard_map/all_to_all | solution.py:471
  124.5 20.5 %all-to-all-start.2 = ((bf16[32,32,256]{2,1,0:T(8,128)(2,1)}), bf16[32,32,256]{2,1,0:T(8,128)(2,1)S(1)}, u32[]{:S(2)}, u32[]{:S(2)}) async-start(bf16[32,32,256]{2,1,0:T(8,128)(2,1)} %bitcast.31), calls=%async_computation.2 | async-start | bytes 1048576 | tf_op jit(solution)/shard_map/all_to_all | solution.py:477
  149.9 12.1 %collective-permute-start.12 = (bf16[64,2048]{1,0:T(8,128)(2,1)S(1)}, bf16[64,2048]{1,0:T(8,128)(2,1)S(1)}, u32[]{:S(2)}, u32[]{:S(2)}) collective-permute-start(bf16[64,2048]{1,0:T(8,128)(2,1)S(1)} %get-tuple-element.41), channel_id=1, source_target_pairs={{0,0},{1,16},{2,2},{3,18},{4,4},{5,20},{6,6},{7,22},{8,24},{9,8},{... | collective-permute-start | bytes 786440 | tf_op jit(solution)/shard_map/ppermute | solution.py:87
  152.5 25.9 %collective-permute-start.13 = (bf16[64,2048]{1,0:T(8,128)(2,1)S(1)}, bf16[64,2048]{1,0:T(8,128)(2,1)S(1)}, u32[]{:S(2)}, u32[]{:S(2)}) collective-permute-start(bf16[64,2048]{1,0:T(8,128)(2,1)S(1)} %get-tuple-element.42), channel_id=1, source_target_pairs={{0,8},{1,24},{2,10},{3,26},{4,12},{5,28},{6,14},{7,30},{8,16},{9,0... | collective-permute-start | bytes 786440 | tf_op jit(solution)/shard_map/ppermute | solution.py:87
  152.6 25.8 %collective-permute-start.14 = (bf16[64,2048]{1,0:T(8,128)(2,1)S(1)}, bf16[64,2048]{1,0:T(8,128)(2,1)S(1)}, u32[]{:S(2)}, u32[]{:S(2)}) collective-permute-start(bf16[64,2048]{1,0:T(8,128)(2,1)S(1)} %get-tuple-element.43), channel_id=1, source_target_pairs={{0,16},{1,0},{2,18},{3,2},{4,20},{5,4},{6,22},{7,6},{8,8},{9,24},{... | collective-permute-start | bytes 786440 | tf_op jit(solution)/shard_map/ppermute | solution.py:87
  156.5 22.0 %collective-permute-start.15 = (bf16[64,2048]{1,0:T(8,128)(2,1)S(1)}, bf16[64,2048]{1,0:T(8,128)(2,1)S(1)}, u32[]{:S(2)}, u32[]{:S(2)}) collective-permute-start(bf16[64,2048]{1,0:T(8,128)(2,1)S(1)} %get-tuple-element.44), channel_id=1, source_target_pairs={{0,24},{1,8},{2,26},{3,10},{4,28},{5,12},{6,30},{7,14},{8,0},{9,16... | collective-permute-start | bytes 786440 | tf_op jit(solution)/shard_map/ppermute | solution.py:87
  (12 other events, 116.5 us)
Sparse Core Ops, SparseCore 0:
  8.9 49.2 all-gather.3
  67.4 48.8 all-gather.5

commit v11 on v10

--- a/solution.py
+++ b/solution.py
@@ -12,7 +12,6 @@
 HIGHEST = lax.Precision.HIGHEST
 UNROLL = 16
 HEAVY = 30
-HALVES = 2
 
 
 def outer_factor(seq_parts, tp_parts):
@@ -113,16 +112,18 @@
     seq_parts = outer * inner_parts
     tp_place = lax.axis_index("tp")
     outer_place = lax.axis_index("seq") // inner_parts
-    arrived = []
-    for step in range(outer):
+    arrived = {}
+    for step in sorted(range(outer), key=lambda step: min(step, outer - step)):
+        if step not in (0, 1, outer - 1):
+            arrived[1], held = lax.optimization_barrier((arrived[1], held))
         target = (outer_place + step) % outer
         which = (tp_place - target // per_tp + tp_parts) % tp_parts * per_tp + target % per_tp
         piece = lax.dynamic_index_in_dim(held, which, axis=0, keepdims=False)
         if step:
             far = step * inner_parts
             piece = lax.ppermute(piece, "seq", [(i, (i + far) % seq_parts) for i in range(seq_parts)])
-        arrived.append(piece)
-    return arrived
+        arrived[step] = piece
+    return [arrived[step] for step in range(outer)]
 
 
 def share_over_tp(part, tp_parts):
@@ -131,31 +132,6 @@
         pairs = [(i, (i + step) % tp_parts) for i in range(tp_parts)]
         pieces.append(lax.ppermute(part, "tp", pairs))
     return pieces
-
-
-def fetch_kernel(source_ref, out_ref, sems):
-    copies = [
-        pltpu.make_async_copy(source_ref.at[index], out_ref.at[index], sems.at[index])
-        for index in range(source_ref.shape[0])
-    ]
-    for copy in copies:
-        copy.start()
-    for copy in copies:
-        copy.wait()
-
-
-def fetch(source):
-    return pl.pallas_call(
-        fetch_kernel,
-        out_shape=jax.ShapeDtypeStruct(source.shape, source.dtype),
-        in_specs=[pl.BlockSpec(memory_space=pl.ANY)],
-        out_specs=pl.BlockSpec(memory_space=pltpu.VMEM),
-        scratch_shapes=[pltpu.SemaphoreType.DMA((source.shape[0],))],
-        compiler_params=pltpu.CompilerParams(vmem_limit_bytes=16 * 2**20),
-        cost_estimate=pl.CostEstimate(
-            flops=0, bytes_accessed=4 * source.size, transcendentals=0
-        ),
-    )(source)
 
 
 def project_kernel(tp_parts, place_ref, *refs):
@@ -198,14 +174,14 @@
         functools.partial(project_kernel, tp_parts),
         in_specs=[pl.BlockSpec(memory_space=pltpu.SMEM)]
         + [vmem] * len(pieces)
-        + [pl.BlockSpec(memory_space=pl.ANY)],
+        + [pl.BlockSpec(memory_space=pltpu.HBM)],
         out_specs=vmem,
         out_shape=jax.ShapeDtypeStruct((seq_parts, streams, chans, count), jnp.bfloat16),
         scratch_shapes=[
             pltpu.VMEM(weight.shape, weight.dtype),
             pltpu.SemaphoreType.DMA((streams,)),
         ],
-        compiler_params=pltpu.CompilerParams(vmem_limit_bytes=56 * 2**20),
+        compiler_params=pltpu.CompilerParams(vmem_limit_bytes=32 * 2**20),
         cost_estimate=pl.CostEstimate(
             flops=HEAVY * 2 * count * weight.size,
             bytes_accessed=2 * (weight.size + len(pieces) * pieces[0].size)
@@ -381,23 +357,30 @@
 
 
 def out_kernel(block_ref, gated_ref, weight_ref, *refs):
-    *out_refs, turned, left = refs
+    *out_refs, turned, left, held, sems = refs
     tp_parts = gated_ref.shape[0]
     part_rows = out_refs[0].shape[0]
-
-    @pl.when(pl.program_id(0) == 0)
-    def _():
+    inner_parts, _, _, width = held.shape
+    copies = [
+        pltpu.make_async_copy(weight_ref.at[inner], held.at[inner], sems.at[inner])
+        for inner in range(inner_parts)
+    ]
+    for copy in copies:
+        copy.start()
+    for part in range(tp_parts):
+        turned[...] = gated_ref[part].T
+        for index in range(len(out_refs)):
+            begin = pl.multiple_of(block_ref[index] * part_rows, part_rows)
+            left[part, index * part_rows : (index + 1) * part_rows] = turned[pl.ds(begin, part_rows)]
+    for inner in range(inner_parts):
+        copies[inner].wait()
+        sums = jnp.zeros((left.shape[1], width), jnp.float32)
         for part in range(tp_parts):
-            turned[...] = gated_ref[part].T
-            for index in range(len(out_refs)):
-                begin = pl.multiple_of(block_ref[index] * part_rows, part_rows)
-                left[part, index * part_rows : (index + 1) * part_rows] = turned[pl.ds(begin, part_rows)]
-
-    sums = jnp.zeros((left.shape[1], weight_ref.shape[3]), jnp.float32)
-    for part in range(tp_parts):
-        sums = sums + jnp.dot(left[part], weight_ref[0, part], preferred_element_type=jnp.float32)
-    for index, out_ref in enumerate(out_refs):
-        out_ref[...] = sums[index * part_rows : (index + 1) * part_rows].astype(out_ref.dtype)
+            sums = sums + jnp.dot(left[part], held[inner, part], preferred_element_type=jnp.float32)
+        for index, out_ref in enumerate(out_refs):
+            out_ref[:, inner * width : (inner + 1) * width] = sums[
+                index * part_rows : (index + 1) * part_rows
+            ].astype(out_ref.dtype)
 
 
 def project_out(gated, weight, blocks):
@@ -405,23 +388,23 @@
     inner_parts, _, _, width = weight.shape
     columns = inner_parts * width
     part_rows = rows // len(blocks)
+    vmem = pl.BlockSpec(memory_space=pltpu.VMEM)
     return pl.pallas_call(
         out_kernel,
-        grid_spec=pltpu.PrefetchScalarGridSpec(
-            num_scalar_prefetch=1,
-            grid=(inner_parts,),
-            in_specs=[
-                pl.BlockSpec((tp_parts, depth, rows), lambda b, place: (0, 0, 0)),
-                pl.BlockSpec((1, tp_parts, depth, width), lambda b, place: (b, 0, 0, 0)),
-            ],
-            out_specs=[pl.BlockSpec((part_rows, width), lambda b, place: (0, b))] * len(blocks),
-            scratch_shapes=[
-                pltpu.VMEM((rows, depth), jnp.bfloat16),
-                pltpu.VMEM((tp_parts, rows, depth), jnp.bfloat16),
-            ],
-        ),
+        in_specs=[
+            pl.BlockSpec(memory_space=pltpu.SMEM),
+            vmem,
+            pl.BlockSpec(memory_space=pltpu.HBM),
+        ],
+        out_specs=[vmem] * len(blocks),
+        scratch_shapes=[
+            pltpu.VMEM((rows, depth), jnp.bfloat16),
+            pltpu.VMEM((tp_parts, rows, depth), jnp.bfloat16),
+            pltpu.VMEM(weight.shape, weight.dtype),
+            pltpu.SemaphoreType.DMA((inner_parts,)),
+        ],
         out_shape=[jax.ShapeDtypeStruct((part_rows, columns), jnp.bfloat16)] * len(blocks),
-        compiler_params=pltpu.CompilerParams(vmem_limit_bytes=16 * 2**20),
+        compiler_params=pltpu.CompilerParams(vmem_limit_bytes=24 * 2**20),
         cost_estimate=pl.CostEstimate(
             flops=2 * gated.size * columns,
             bytes_accessed=2 * (weight.size + gated.size + rows * columns),
@@ -452,14 +435,9 @@
     skip = jnp.broadcast_to(skip[:, None], (chans, rows))
     filter_blocks = long_filter.T.reshape(seq_parts, chans, rows)
 
-    half = rows // HALVES
-    held = [
-        share_columns(features[index * half : (index + 1) * half], outer, tp_parts)
-        for index in range(HALVES)
-    ]
-    held[-1], taps, skip = lax.optimization_barrier((held[-1], taps, skip))
-    arrived = [cross_outer(part, outer, inner_parts, tp_parts) for part in held]
-    arrived = [jnp.concatenate(parts) for parts in zip(*arrived)]
+    held = share_columns(features, outer, tp_parts)
+    held, taps, skip = lax.optimization_barrier((held, taps, skip))
+    arrived = cross_outer(held, outer, inner_parts, tp_parts)
     filter_blocks = lax.all_to_all(filter_blocks, "seq", split_axis=0, concat_axis=0, tiled=True)
     arrived[1], filter_blocks = lax.optimization_barrier((arrived[1], filter_blocks))
     chunks = [share_over_tp(piece, tp_parts) for piece in arrived]
@@ -471,7 +449,6 @@
     parts = lax.all_to_all(partial, "seq", split_axis=0, concat_axis=0, tiled=True)
 
     parts, out_weight = lax.optimization_barrier((parts, out_weight))
-    out_weight = fetch(out_weight)
 
     gated = convolve([parts], filter_blocks, taps, skip, outer, tp_parts)
     gated = lax.all_to_all(

time: 188 us -> 185 us (0.984)
  waiting for transfers between devices: 98.4 us -> 113 us
  starting transfers between devices: 47.2 us -> 34.9 us
  Pallas kernels: 17.1 us -> 14.4 us
  local copies, waits for them, and re-layouts: 10.4 us -> 8.25 us
    all_to_all x1, waiting for transfers between devices: 0.01 us -> 13.6 us  [per_device(): lax.all_to_all(filter_blocks, 'seq', split_axis=0, concat_axis=0, tiled=T...]
    ppermute x2 -> x1, waiting for transfers between devices: 0.34 us -> 12.3 us  [share_columns(): lax.ppermute(piece, 'tp', [(i, (i + step) % tp_parts) for i in range(tp_p...]
    ppermute x6 -> x3, waiting for transfers between devices: 12.9 us -> 4.35 us  [cross_outer(): lax.ppermute(piece, 'seq', [(i, (i + far) % seq_parts) for i in range(seq...]
    ppermute x4, waiting for transfers between devices: 20.1 us -> 13 us  [share_over_tp(): pieces.append(lax.ppermute(part, 'tp', pairs))]
    ppermute x6 -> x3, starting transfers between devices: 10 us -> 4.61 us  [cross_outer(): lax.ppermute(piece, 'seq', [(i, (i + far) % seq_parts) for i in range(seq...]
    all_to_all x1, waiting for transfers between devices: 9.91 us -> 14.4 us  [per_device(): lax.all_to_all(gated.reshape((-1,) + gated.shape[3:]), ('tp', 'seq'), spl...]
    pallas_call x1, Pallas kernels: 8.29 us -> 5.74 us  [project_in(): pl.pallas_call(functools.partial(project_kernel, tp_parts), in_specs=[pl....]
    ppermute x4, starting transfers between devices: 4.25 us -> 2.03 us  [share_over_tp(): pieces.append(lax.ppermute(part, 'tp', pairs))]
  transfers between devices with their start and end apart: 21 -> 17, of which waited for: 12 -> 11; matrix products, arithmetic and copies ran while one was open for 2% -> 2% of each run, Pallas kernels for 5% -> 3%
where the time goes in v11:
time: 185 us; the launch traced here: 184 us
  waiting for transfers between devices  113 us (61%)
  starting transfers between devices  34.9 us (19%)
  Pallas kernels  14.4 us (8%)
  between operations  13.7 us (7%)
  local copies, waits for them, and re-layouts  8.25 us (4%)
    all_gather x1, waiting for transfers between devices, per_device(): lax.all_gather(out_proj, ('seq', 'tp'), axis_index_groups=tp_groups)  31.3 us
    ppermute x4, waiting for transfers between devices, return_output(): arrived.append(lax.ppermute(piece, ('seq', 'tp'), pairs))  19.5 us
    all_to_all x1, waiting for transfers between devices, per_device(): lax.all_to_all(gated.reshape((-1,) + gated.shape[3:]), ('tp', 'seq'), spl...  14.4 us
    all_to_all x1, waiting for transfers between devices, per_device(): lax.all_to_all(filter_blocks, 'seq', split_axis=0, concat_axis=0, tiled=T...  13.6 us
    ppermute x4, waiting for transfers between devices, share_over_tp(): pieces.append(lax.ppermute(part, 'tp', pairs))  13 us
    ppermute x1, waiting for transfers between devices, share_columns(): lax.ppermute(piece, 'tp', [(i, (i + step) % tp_parts) for i in range(tp_p...  12.3 us
    ppermute x4, starting transfers between devices, return_output(): arrived.append(lax.ppermute(piece, ('seq', 'tp'), pairs))  8.85 us
    all_to_all x1, starting transfers between devices, per_device(): lax.all_to_all(partial, 'seq', split_axis=0, concat_axis=0, tiled=True)  7.6 us
  transfers between devices with their start and end apart: 17, of which 11 were waited for; matrix products, arithmetic and copies ran while one was open for 2% of the time, Pallas kernels for 3%

profile of v11, /device:TPU:12, one launch (start us, length us, event | category | flops | bytes accessed | tf_op | source)
XLA Modules:
  0.0 184.3 jit_solution(18336976454911475811)
XLA Ops:
  9.3 12.3 %collective-permute-done = bf16[2,128,1024]{2,1,0:T(8,128)(2,1)S(1)} collective-permute-done((bf16[2,128,1024]{2,1,0:T(8,128)(2,1)S(1)}, bf16[2,128,1024]{2,1,0:T(8,128)(2,1)S(1)}, u32[]{:S(2)}, u32[]{:S(2)}) %collective-permute-start) | collective-permute-done | bytes 524320 | tf_op jit(solution)/shard_map/ppermute | solution.py:105
  22.0 1.6 collective-permute-start.2
  24.5 5.3 %all-to-all-start = ((f32[16,32,128]{2,1,0:T(8,128)}), f32[16,32,128]{2,1,0:T(8,128)S(1)}, u32[]{:S(2)}, u32[]{:S(2)}) async-start(f32[16,32,128]{2,1,0:T(8,128)} %bitcast.18), calls=%async_computation | async-start | bytes 524288 | tf_op jit(solution)/shard_map/all_to_all | solution.py:441
  30.7 2.8 %collective-permute-start.4 = (bf16[128,1024]{1,0:T(8,128)(2,1)}, bf16[128,1024]{1,0:T(8,128)(2,1)S(1)}, u32[]{:S(2)}, u32[]{:S(2)}) collective-permute-start(bf16[128,1024]{1,0:T(8,128)(2,1)} %dynamic-slice_bitcast_fusion.1), channel_id=1, source_target_pairs={{0,16},{2,18},{4,20},{6,22},{8,24},{10,26},{12,28},{14,30},{16,0},... | collective-permute-start | bytes 786440 | tf_op jit(solution)/shard_map/ppermute | solution.py:124
  34.1 13.6 %all-to-all-done.refs_1_ = f32[16,32,128]{2,1,0:T(8,128)S(1)} async-done(((f32[16,32,128]{2,1,0:T(8,128)}), f32[16,32,128]{2,1,0:T(8,128)S(1)}, u32[]{:S(2)}, u32[]{:S(2)}) %all-to-all-start) | async-done | bytes 262176 | tf_op jit(solution)/shard_map/all_to_all | solution.py:441
  50.2 2.8 %collective-permute-done.4.refs_4_ = bf16[128,1024]{1,0:T(8,128)(2,1)S(1)} collective-permute-done((bf16[128,1024]{1,0:T(8,128)(2,1)}, bf16[128,1024]{1,0:T(8,128)(2,1)S(1)}, u32[]{:S(2)}, u32[]{:S(2)}) %collective-permute-start.4) | collective-permute-done | bytes 262176 | tf_op jit(solution)/shard_map/ppermute | solution.py:124
  53.6 9.0 %collective-permute-done.7.refs_7_ = bf16[128,1024]{1,0:T(8,128)(2,1)S(1)} collective-permute-done((bf16[128,1024]{1,0:T(8,128)(2,1)S(1)}, bf16[128,1024]{1,0:T(8,128)(2,1)S(1)}, u32[]{:S(2)}, u32[]{:S(2)}) %collective-permute-start.7) | collective-permute-done | bytes 262176 | tf_op jit(solution)/shard_map/ppermute | solution.py:133
  62.5 4.0 %collective-permute-done.5.refs_5_ = bf16[128,1024]{1,0:T(8,128)(2,1)S(1)} collective-permute-done((bf16[128,1024]{1,0:T(8,128)(2,1)S(1)}, bf16[128,1024]{1,0:T(8,128)(2,1)S(1)}, u32[]{:S(2)}, u32[]{:S(2)}) %collective-permute-start.5) | collective-permute-done | bytes 262176 | tf_op jit(solution)/shard_map/ppermute | solution.py:133
  66.6 2.8 %copy-done.2 = bf16[3,2048,512]{2,1,0:T(8,128)(2,1)S(1)} copy-done((bf16[3,2048,512]{2,1,0:T(8,128)(2,1)S(1)}, bf16[3,2048,512]{2,1,0:T(8,128)(2,1)}, u32[]{:S(2)}) %copy-start.2) | copy-done | bytes 6291480
  69.4 5.7 %shard_map.82 = bf16[16,3,32,512]{3,2,1,0:T(8,128)(2,1)} custom-call(s32[1]{0:T(128)} %bitcast.10.place_ref, bf16[128,1024]{1,0:T(8,128)(2,1)S(1)} %get-tuple-element.31.refs_0_, bf16[128,1024]{1,0:T(8,128)(2,1)S(1)} %collective-permute-done.1.refs_1_, bf16[128,1024]{1,0:T(8,128)(2,1)S(1)} %collective-permute-done.2.refs_2_, ...), custom_call_target="tpu_custom_call" | custom-call | flops 96636764160 | bytes 9961472 | tf_op jit(solution)/shard_map/pallas_call | solution.py:173
  75.1 7.6 %all-to-all-start.1 = ((bf16[16,3,32,512]{3,2,1,0:T(8,128)(2,1)}), bf16[16,3,32,512]{3,2,1,0:T(8,128)(2,1)S(1)}, u32[]{:S(2)}, u32[]{:S(2)}) async-start(bf16[16,3,32,512]{3,2,1,0:T(8,128)(2,1)} %shard_map.82), calls=%async_computation.1 | async-start | bytes 3145728 | tf_op jit(solution)/shard_map/all_to_all | solution.py:449
  82.7 31.3 %all-gather.6.cloned.1.call-done = bf16[4096,512]{1,0:T(8,128)(2,1)} async-done(((bf16[512,512]{1,0:T(8,128)(2,1)}), bf16[4096,512]{1,0:T(8,128)(2,1)}) %all-gather.6.cloned.1.call-update) | async-done | bytes 4194320 | tf_op jit(solution)/shard_map/all_gather | solution.py:445
  114.0 3.7 %all-to-all-done.1.refs_0_ = bf16[16,3,32,512]{3,2,1,0:T(8,128)(2,1)S(1)} async-done(((bf16[16,3,32,512]{3,2,1,0:T(8,128)(2,1)}), bf16[16,3,32,512]{3,2,1,0:T(8,128)(2,1)S(1)}, u32[]{:S(2)}, u32[]{:S(2)}) %all-to-all-start.1) | async-done | bytes 1572896 | tf_op jit(solution)/shard_map/all_to_all | solution.py:449
  117.7 3.7 %shard_map.83 = bf16[2,4,4,32,256]{4,3,2,1,0:T(8,128)(2,1)} custom-call(bf16[16,3,32,512]{3,2,1,0:T(8,128)(2,1)S(1)} %all-to-all-done.1.refs_0_, f32[16,32,128]{2,1,0:T(8,128)S(1)} %all-to-all-done.refs_1_, f32[3,3,32,128]{3,2,1,0:T(8,128)S(1)} %broadcast_in_dim.7.refs_2_, f32[32,128]{1,0:T(8,128)S(1)} %broadcast_in_dim.8.refs_3_, f32[128,256]{1,0:T(8,128)S(1)} %copy-done.4, ...), custom_call_target="tpu_custom_call" | custom-call | flops 1000000000 | bytes 4194304 | tf_op jit(solution)/shard_map/pallas_call | solution.py:338
  121.4 5.9 %all-to-all-start.2 = ((bf16[32,32,256]{2,1,0:T(8,128)(2,1)}), bf16[32,32,256]{2,1,0:T(8,128)(2,1)S(1)}, u32[]{:S(2)}, u32[]{:S(2)}) async-start(bf16[32,32,256]{2,1,0:T(8,128)(2,1)} %bitcast.23), calls=%async_computation.2 | async-start | bytes 1048576 | tf_op jit(solution)/shard_map/all_to_all | solution.py:454
  127.5 14.4 %all-to-all-done.2 = bf16[32,32,256]{2,1,0:T(8,128)(2,1)S(1)} async-done(((bf16[32,32,256]{2,1,0:T(8,128)(2,1)}), bf16[32,32,256]{2,1,0:T(8,128)(2,1)S(1)}, u32[]{:S(2)}, u32[]{:S(2)}) %all-to-all-start.2) | async-done | bytes 524320 | tf_op jit(solution)/shard_map/all_to_all | solution.py:454
  141.9 2.2 %copy-done.1 = bf16[4096,512]{1,0:T(8,128)(2,1)S(1)} copy-done((bf16[4096,512]{1,0:T(8,128)(2,1)S(1)}, bf16[4096,512]{1,0:T(8,128)(2,1)}, u32[]{:S(2)}) %copy-start.1) | copy-done | bytes 4194328
  144.0 2.8 %shard_map.84 = (bf16[64,2048]{1,0:T(8,128)(2,1)S(1)}, bf16[64,2048]{1,0:T(8,128)(2,1)S(1)}, bf16[64,2048]{1,0:T(8,128)(2,1)S(1)}, bf16[64,2048]{1,0:T(8,128)(2,1)S(1)}) custom-call(s32[4]{0:T(128)S(1)} %pad_add_fusion.block_ref, bf16[2,512,256]{2,1,0:T(8,128)(2,1)S(1)} %bitcast.34, bf16[4,2,512,512]{3,2,1,0:T(8,128)(2,1)S(1)} %bitcast.33), custom_call_target="tpu_custom_call" | custom-call | flops 1073741824 | bytes 5767168 | tf_op jit(solution)/shard_map/pallas_call | solution.py:392
  146.9 2.6 %collective-permute-start.8 = (bf16[64,2048]{1,0:T(8,128)(2,1)S(1)}, bf16[64,2048]{1,0:T(8,128)(2,1)S(1)}, u32[]{:S(2)}, u32[]{:S(2)}) collective-permute-start(bf16[64,2048]{1,0:T(8,128)(2,1)S(1)} %get-tuple-element.45), channel_id=1, source_target_pairs={{0,0},{1,16},{2,2},{3,18},{4,4},{5,20},{6,6},{7,22},{8,24},{9,8},{... | collective-permute-start | bytes 786440 | tf_op jit(solution)/shard_map/ppermute | solution.py:86
  149.6 3.9 %collective-permute-start.10 = (bf16[64,2048]{1,0:T(8,128)(2,1)S(1)}, bf16[64,2048]{1,0:T(8,128)(2,1)S(1)}, u32[]{:S(2)}, u32[]{:S(2)}) collective-permute-start(bf16[64,2048]{1,0:T(8,128)(2,1)S(1)} %get-tuple-element.47), channel_id=1, source_target_pairs={{0,16},{1,0},{2,18},{3,2},{4,20},{5,4},{6,22},{7,6},{8,8},{9,24},{... | collective-permute-start | bytes 786440 | tf_op jit(solution)/shard_map/ppermute | solution.py:86
  153.4 2.3 %collective-permute-start.11 = (bf16[64,2048]{1,0:T(8,128)(2,1)S(1)}, bf16[64,2048]{1,0:T(8,128)(2,1)S(1)}, u32[]{:S(2)}, u32[]{:S(2)}) collective-permute-start(bf16[64,2048]{1,0:T(8,128)(2,1)S(1)} %get-tuple-element.48), channel_id=1, source_target_pairs={{0,24},{1,8},{2,26},{3,10},{4,28},{5,12},{6,30},{7,14},{8,0},{9,16... | collective-permute-start | bytes 786440 | tf_op jit(solution)/shard_map/ppermute | solution.py:86
  155.8 3.2 %collective-permute-done.8.refs_0_ = bf16[64,2048]{1,0:T(8,128)(2,1)S(1)} collective-permute-done((bf16[64,2048]{1,0:T(8,128)(2,1)S(1)}, bf16[64,2048]{1,0:T(8,128)(2,1)S(1)}, u32[]{:S(2)}, u32[]{:S(2)}) %collective-permute-start.8) | collective-permute-done | bytes 262176 | tf_op jit(solution)/shard_map/ppermute | solution.py:86
  159.0 16.4 %collective-permute-done.9.refs_1_ = bf16[64,2048]{1,0:T(8,128)(2,1)S(1)} collective-permute-done((bf16[64,2048]{1,0:T(8,128)(2,1)S(1)}, bf16[64,2048]{1,0:T(8,128)(2,1)S(1)}, u32[]{:S(2)}, u32[]{:S(2)}) %collective-permute-start.9) | collective-permute-done | bytes 262176 | tf_op jit(solution)/shard_map/ppermute | solution.py:86
  175.4 2.1 %shard_map.85 = bf16[128,4096]{1,0:T(8,128)(2,1)} custom-call(s32[8]{0:T(128)S(1)} %stack.59.place_ref, bf16[64,2048]{1,0:T(8,128)(2,1)S(1)} %collective-permute-done.8.refs_0_, bf16[64,2048]{1,0:T(8,128)(2,1)S(1)} %collective-permute-done.9.refs_1_, bf16[64,2048]{1,0:T(8,128)(2,1)S(1)} %collective-permute-done.10.refs_2_, ...), custom_call_target="tpu_custom_call" | custom-call | bytes 2097152 | tf_op jit(solution)/shard_map/pallas_call | solution.py:34
  (42 shorter events, 8.7 us)
Async XLA Ops:
  6.5 2.7 %copy-start = (f32[3,3,512]{2,1,0:T(4,128)S(1)}, f32[3,3,512]{2,1,0:T(4,128)}, u32[]{:S(2)}) copy-start(f32[3,3,512]{2,1,0:T(4,128)} %param.10) | copy-start | bytes 55300
  6.5 1.2 copy-start.5
  6.5 60.0 %all-gather.4.cloned.1.call-start = ((), (), s32[]{:S(2)}) async-start(), calls=%async_computation.3 | async-start | bytes 7864320 | tf_op jit(solution)/shard_map/all_gather | solution.py:430
  7.9 13.7 %collective-permute-start = (bf16[2,128,1024]{2,1,0:T(8,128)(2,1)S(1)}, bf16[2,128,1024]{2,1,0:T(8,128)(2,1)S(1)}, u32[]{:S(2)}, u32[]{:S(2)}) collective-permute-start(bf16[2,128,1024]{2,1,0:T(8,128)(2,1)S(1)} %pad_maximum_fusion.1), channel_id=1, source_target_pairs={{0,1},{1,0},{2,3},{3,2},{4,5},{5,4},{6,7},{7,6},{8,9},{9,8},{10,11... | collective-permute-start | bytes 1572872 | tf_op jit(solution)/shard_map/ppermute | solution.py:105
  21.6 2.0 %copy-start.6 = (f32[128,512]{1,0:T(8,128)S(1)}, f32[128,512]{1,0:T(8,128)}, u32[]{:S(2)}) copy-start(f32[128,512]{1,0:T(8,128)} %param.11) | copy-start | bytes 786436
  22.0 8.0 %collective-permute-start.2 = (bf16[128,1024]{1,0:T(8,128)(2,1)S(1)}, bf16[128,1024]{1,0:T(8,128)(2,1)S(1)}, u32[]{:S(2)}, u32[]{:S(2)}) collective-permute-start(bf16[128,1024]{1,0:T(8,128)(2,1)S(1)} %get-tuple-element.50), channel_id=1, source_target_pairs={{0,8},{2,10},{4,12},{6,14},{8,16},{10,18},{12,20},{14,22},{16,24},... | collective-permute-start | bytes 786440 | tf_op jit(solution)/shard_map/ppermute | solution.py:124
  24.5 23.2 %all-to-all-start = ((f32[16,32,128]{2,1,0:T(8,128)}), f32[16,32,128]{2,1,0:T(8,128)S(1)}, u32[]{:S(2)}, u32[]{:S(2)}) async-start(f32[16,32,128]{2,1,0:T(8,128)} %bitcast.18), calls=%async_computation | async-start | bytes 524288 | tf_op jit(solution)/shard_map/all_to_all | solution.py:441
  29.7 84.3 %all-gather.6.cloned.1.call-start = ((), (), s32[]{:S(2)}) async-start(), calls=%async_computation.4 | async-start | bytes 4718592 | tf_op jit(solution)/shard_map/all_gather | solution.py:445
  29.8 19.9 %collective-permute-start.6 = (bf16[128,1024]{1,0:T(8,128)(2,1)S(1)}, bf16[128,1024]{1,0:T(8,128)(2,1)S(1)}, u32[]{:S(2)}, u32[]{:S(2)}) collective-permute-start(bf16[128,1024]{1,0:T(8,128)(2,1)S(1)} %get-tuple-element.49), channel_id=1, source_target_pairs={{0,24},{2,26},{4,28},{6,30},{8,0},{10,2},{12,4},{14,6},{16,8},{18,... | collective-permute-start | bytes 786440 | tf_op jit(solution)/shard_map/ppermute | solution.py:124
  30.7 22.3 %collective-permute-start.4 = (bf16[128,1024]{1,0:T(8,128)(2,1)}, bf16[128,1024]{1,0:T(8,128)(2,1)S(1)}, u32[]{:S(2)}, u32[]{:S(2)}) collective-permute-start(bf16[128,1024]{1,0:T(8,128)(2,1)} %dynamic-slice_bitcast_fusion.1), channel_id=1, source_target_pairs={{0,16},{2,18},{4,20},{6,22},{8,24},{10,26},{12,28},{14,30},{16,0},... | collective-permute-start | bytes 786440 | tf_op jit(solution)/shard_map/ppermute | solution.py:124
  33.5 20.0 %collective-permute-start.1 = (bf16[128,1024]{1,0:T(8,128)(2,1)S(1)}, bf16[128,1024]{1,0:T(8,128)(2,1)S(1)}, u32[]{:S(2)}, u32[]{:S(2)}) collective-permute-start(bf16[128,1024]{1,0:T(8,128)(2,1)S(1)} %get-tuple-element.31.refs_0_), channel_id=1, source_target_pairs={{0,1},{1,0},{2,3},{3,2},{4,5},{5,4},{6,7},{7,6},{8,9},{9,8},{10,11... | collective-permute-start | bytes 786440 | tf_op jit(solution)/shard_map/ppermute | solution.py:133
  47.7 14.9 %collective-permute-start.3 = (bf16[128,1024]{1,0:T(8,128)(2,1)S(1)}, bf16[128,1024]{1,0:T(8,128)(2,1)S(1)}, u32[]{:S(2)}, u32[]{:S(2)}) collective-permute-start(bf16[128,1024]{1,0:T(8,128)(2,1)S(1)} %collective-permute-done.2.refs_2_), channel_id=1, source_target_pairs={{0,1},{1,0},{2,3},{3,2},{4,5},{5,4},{6,7},{7,6},{8,9},{9,8},{10,11... | collective-permute-start | bytes 786440 | tf_op jit(solution)/shard_map/ppermute | solution.py:133
  49.7 12.8 %collective-permute-start.7 = (bf16[128,1024]{1,0:T(8,128)(2,1)S(1)}, bf16[128,1024]{1,0:T(8,128)(2,1)S(1)}, u32[]{:S(2)}, u32[]{:S(2)}) collective-permute-start(bf16[128,1024]{1,0:T(8,128)(2,1)S(1)} %collective-permute-done.6.refs_6_), channel_id=1, source_target_pairs={{0,1},{1,0},{2,3},{3,2},{4,5},{5,4},{6,7},{7,6},{8,9},{9,8},{10,11... | collective-permute-start | bytes 786440 | tf_op jit(solution)/shard_map/ppermute | solution.py:133
  53.0 13.5 %collective-permute-start.5 = (bf16[128,1024]{1,0:T(8,128)(2,1)S(1)}, bf16[128,1024]{1,0:T(8,128)(2,1)S(1)}, u32[]{:S(2)}, u32[]{:S(2)}) collective-permute-start(bf16[128,1024]{1,0:T(8,128)(2,1)S(1)} %collective-permute-done.4.refs_4_), channel_id=1, source_target_pairs={{0,1},{1,0},{2,3},{3,2},{4,5},{5,4},{6,7},{7,6},{8,9},{9,8},{10,11... | collective-permute-start | bytes 786440 | tf_op jit(solution)/shard_map/ppermute | solution.py:133
  66.6 2.8 %copy-start.2 = (bf16[3,2048,512]{2,1,0:T(8,128)(2,1)S(1)}, bf16[3,2048,512]{2,1,0:T(8,128)(2,1)}, u32[]{:S(2)}) copy-start(bf16[3,2048,512]{2,1,0:T(8,128)(2,1)} %all-gather.4.cloned.1.call-done) | copy-start | bytes 18874372
  75.1 42.5 %copy-start.3 = (f32[256,256]{1,0:T(8,128)S(1)}, f32[256,256]{1,0:T(8,128)}, u32[]{:S(2)}) copy-start(f32[256,256]{1,0:T(8,128)} %constant.230.clone.refs_5_) | copy-start | bytes 786436
  75.1 42.5 %copy-start.4 = (f32[128,256]{1,0:T(8,128)S(1)}, f32[128,256]{1,0:T(8,128)}, u32[]{:S(2)}) copy-start(f32[128,256]{1,0:T(8,128)} %constant.229.clone.refs_4_) | copy-start | bytes 393220
  75.1 42.5 %all-to-all-start.1 = ((bf16[16,3,32,512]{3,2,1,0:T(8,128)(2,1)}), bf16[16,3,32,512]{3,2,1,0:T(8,128)(2,1)S(1)}, u32[]{:S(2)}, u32[]{:S(2)}) async-start(bf16[16,3,32,512]{3,2,1,0:T(8,128)(2,1)} %shard_map.82), calls=%async_computation.1 | async-start | bytes 3145728 | tf_op jit(solution)/shard_map/all_to_all | solution.py:449
  121.4 20.5 %all-to-all-start.2 = ((bf16[32,32,256]{2,1,0:T(8,128)(2,1)}), bf16[32,32,256]{2,1,0:T(8,128)(2,1)S(1)}, u32[]{:S(2)}, u32[]{:S(2)}) async-start(bf16[32,32,256]{2,1,0:T(8,128)(2,1)} %bitcast.23), calls=%async_computation.2 | async-start | bytes 1048576 | tf_op jit(solution)/shard_map/all_to_all | solution.py:454
  141.9 2.2 %copy-start.1 = (bf16[4096,512]{1,0:T(8,128)(2,1)S(1)}, bf16[4096,512]{1,0:T(8,128)(2,1)}, u32[]{:S(2)}) copy-start(bf16[4096,512]{1,0:T(8,128)(2,1)} %all-gather.6.cloned.1.call-done) | copy-start | bytes 12582916
  146.9 12.1 %collective-permute-start.8 = (bf16[64,2048]{1,0:T(8,128)(2,1)S(1)}, bf16[64,2048]{1,0:T(8,128)(2,1)S(1)}, u32[]{:S(2)}, u32[]{:S(2)}) collective-permute-start(bf16[64,2048]{1,0:T(8,128)(2,1)S(1)} %get-tuple-element.45), channel_id=1, source_target_pairs={{0,0},{1,16},{2,2},{3,18},{4,4},{5,20},{6,6},{7,22},{8,24},{9,8},{... | collective-permute-start | bytes 786440 | tf_op jit(solution)/shard_map/ppermute | solution.py:86
  149.5 25.9 %collective-permute-start.9 = (bf16[64,2048]{1,0:T(8,128)(2,1)S(1)}, bf16[64,2048]{1,0:T(8,128)(2,1)S(1)}, u32[]{:S(2)}, u32[]{:S(2)}) collective-permute-start(bf16[64,2048]{1,0:T(8,128)(2,1)S(1)} %get-tuple-element.46), channel_id=1, source_target_pairs={{0,8},{1,24},{2,10},{3,26},{4,12},{5,28},{6,14},{7,30},{8,16},{9,0... | collective-permute-start | bytes 786440 | tf_op jit(solution)/shard_map/ppermute | solution.py:86
  149.6 25.8 %collective-permute-start.10 = (bf16[64,2048]{1,0:T(8,128)(2,1)S(1)}, bf16[64,2048]{1,0:T(8,128)(2,1)S(1)}, u32[]{:S(2)}, u32[]{:S(2)}) collective-permute-start(bf16[64,2048]{1,0:T(8,128)(2,1)S(1)} %get-tuple-element.47), channel_id=1, source_target_pairs={{0,16},{1,0},{2,18},{3,2},{4,20},{5,4},{6,22},{7,6},{8,8},{9,24},{... | collective-permute-start | bytes 786440 | tf_op jit(solution)/shard_map/ppermute | solution.py:86
  153.4 22.0 %collective-permute-start.11 = (bf16[64,2048]{1,0:T(8,128)(2,1)S(1)}, bf16[64,2048]{1,0:T(8,128)(2,1)S(1)}, u32[]{:S(2)}, u32[]{:S(2)}) collective-permute-start(bf16[64,2048]{1,0:T(8,128)(2,1)S(1)} %get-tuple-element.48), channel_id=1, source_target_pairs={{0,24},{1,8},{2,26},{3,10},{4,28},{5,12},{6,30},{7,14},{8,0},{9,16... | collective-permute-start | bytes 786440 | tf_op jit(solution)/shard_map/ppermute | solution.py:86
Sparse Core Ops, SparseCore 0:
  8.9 50.2 all-gather.3
  66.7 47.2 all-gather.5

commit v12 on v8

--- a/solution.py
+++ b/solution.py
@@ -22,26 +22,28 @@
 
 
 def assemble_kernel(place_ref, *refs):
-    *piece_refs, out_ref = refs
+    *piece_refs, out_ref, sems = refs
+    part_rows, width = piece_refs[0].shape
+    copies = []
     for index, piece_ref in enumerate(piece_refs):
-
-        @pl.when(pl.program_id(0) == index)
-        def _():
-            out_ref[...] = piece_ref[...]
+        row = pl.multiple_of(place_ref[2 * index] * part_rows, part_rows)
+        column = pl.multiple_of(place_ref[2 * index + 1] * width, width)
+        target = out_ref.at[pl.ds(row, part_rows), pl.ds(column, width)]
+        copies.append(pltpu.make_async_copy(piece_ref, target, sems.at[index]))
+    for copy in copies:
+        copy.start()
+    for copy in copies:
+        copy.wait()
 
 
 def assemble(pieces, places, shape):
     return pl.pallas_call(
         assemble_kernel,
-        grid_spec=pltpu.PrefetchScalarGridSpec(
-            num_scalar_prefetch=1,
-            grid=(len(pieces),),
-            in_specs=[pl.BlockSpec(memory_space=pltpu.VMEM)] * len(pieces),
-            out_specs=pl.BlockSpec(
-                pieces[0].shape, lambda i, place: (place[2 * i], place[2 * i + 1])
-            ),
-        ),
+        in_specs=[pl.BlockSpec(memory_space=pltpu.SMEM)]
+        + [pl.BlockSpec(memory_space=pltpu.VMEM)] * len(pieces),
+        out_specs=pl.BlockSpec(memory_space=pl.ANY),
         out_shape=jax.ShapeDtypeStruct(shape, pieces[0].dtype),
+        scratch_shapes=[pltpu.SemaphoreType.DMA((len(pieces),))],
         compiler_params=pltpu.CompilerParams(vmem_limit_bytes=4 * 2**20),
         cost_estimate=pl.CostEstimate(
             flops=0, bytes_accessed=4 * shape[0] * shape[1], transcendentals=0
@@ -132,46 +134,68 @@
     return pieces
 
 
-def project_kernel(tp_parts, place_ref, *refs):
-    *share_refs, weight_ref, out_ref = refs
-    seq_parts, _, chans, count = out_ref.shape
-    sums = jnp.zeros((count, seq_parts * chans), jnp.float32)
-    for step in range(tp_parts):
-        which = lax.rem(place_ref[0] - step + tp_parts, tp_parts)
-        left = jnp.concatenate([share_ref[...] for share_ref in share_refs[step::tp_parts]])
-        sums = sums + jnp.dot(left, weight_ref[0, which], preferred_element_type=jnp.float32)
-    turned = sums.astype(out_ref.dtype).T
-    for seq in range(seq_parts):
-        out_ref[seq, 0] = turned[seq * chans : (seq + 1) * chans]
-
-
-def project_in(chunks, weight, seq_parts):
+def gather_inner(block, inner_parts, settle):
+    held, masks = [block], [0]
+    bit = inner_parts // 2
+    while bit:
+        pairs = [(i, i ^ bit) for i in range(lax.axis_size("seq"))]
+        held += [lax.ppermute(piece, "seq", pairs) for piece in held]
+        masks += [mask ^ bit for mask in masks]
+        if bit == inner_parts // 2:
+            held = settle(held)
+        bit //= 2
+    return held, masks
+
+
+def project_kernel(tp_parts, masks, place_ref, *refs):
+    *refs, out_ref, left = refs
+    share_refs, weight_refs = refs[: -len(masks)], refs[-len(masks) :]
+    seq_parts, streams, chans, count = out_ref.shape
+    blocks, rows, width = len(masks) // tp_parts, share_refs[0].shape[0], left.shape[2]
+    for index, share_ref in enumerate(share_refs):
+        chunk, step = divmod(index, tp_parts)
+        for block in range(blocks):
+            left[step * blocks + block, chunk * rows : (chunk + 1) * rows] = share_ref[
+                :, block * width : (block + 1) * width
+            ]
+    slots = []
+    for mask in masks:
+        inner = jnp.bitwise_xor(place_ref[1], mask)
+        step = lax.rem(place_ref[0] - inner // blocks + tp_parts, tp_parts)
+        slots.append(step * blocks + lax.rem(inner, blocks))
+    for stream in range(streams):
+        sums = jnp.zeros((count, seq_parts * chans), jnp.float32)
+        for slot, weight_ref in zip(slots, weight_refs):
+            sums = sums + jnp.dot(left[slot], weight_ref[stream], preferred_element_type=jnp.float32)
+        turned = sums.astype(out_ref.dtype).T
+        for seq in range(seq_parts):
+            out_ref[seq, stream] = turned[seq * chans : (seq + 1) * chans]
+
+
+def project_in(chunks, weights, masks, inner_parts, seq_parts):
     tp_parts = len(chunks[0])
-    rows, width = chunks[0][0].shape
-    streams, _, chan_tp = weight.shape
-    weight = weight.reshape(streams, tp_parts, width, chan_tp)
+    rows, _ = chunks[0][0].shape
+    streams, width, chan_tp = weights[0].shape
     chans = chan_tp // seq_parts
     pieces = [piece for chunk in chunks for piece in chunk]
     count = len(chunks) * rows
-    place = lax.axis_index("tp").astype(jnp.int32)[None]
+    place = jnp.stack([lax.axis_index("tp"), lax.axis_index("seq") % inner_parts]).astype(jnp.int32)
+    vmem = pl.BlockSpec(memory_space=pltpu.VMEM)
+    size = len(weights) * weights[0].size
     return pl.pallas_call(
-        functools.partial(project_kernel, tp_parts),
-        grid_spec=pltpu.PrefetchScalarGridSpec(
-            num_scalar_prefetch=1,
-            grid=(streams,),
-            in_specs=[pl.BlockSpec((rows, width), lambda i, place: (0, 0))] * len(pieces)
-            + [pl.BlockSpec((1, tp_parts, width, chan_tp), lambda i, place: (i, 0, 0, 0))],
-            out_specs=pl.BlockSpec((seq_parts, 1, chans, count), lambda i, place: (0, i, 0, 0)),
-        ),
+        functools.partial(project_kernel, tp_parts, masks),
+        in_specs=[pl.BlockSpec(memory_space=pltpu.SMEM)] + [vmem] * (len(pieces) + len(weights)),
+        out_specs=vmem,
         out_shape=jax.ShapeDtypeStruct((seq_parts, streams, chans, count), jnp.bfloat16),
-        compiler_params=pltpu.CompilerParams(vmem_limit_bytes=56 * 2**20),
+        scratch_shapes=[pltpu.VMEM((len(masks), count, width), jnp.bfloat16)],
+        compiler_params=pltpu.CompilerParams(vmem_limit_bytes=32 * 2**20),
         cost_estimate=pl.CostEstimate(
-            flops=HEAVY * 2 * count * weight.size,
-            bytes_accessed=2 * (weight.size + len(pieces) * pieces[0].size)
-            + 2 * streams * count * chan_tp,
+            flops=HEAVY * 2 * count * size,
+            bytes_accessed=2 * (size + len(pieces) * pieces[0].size)
+            + 2 * streams * count * seq_parts * chans,
             transcendentals=0,
         ),
-    )(place, *pieces, weight)
+    )(place, *pieces, *weights)
 
 
 def tables(block):
@@ -403,8 +427,6 @@
         [index * tp_parts + tp for index in group for tp in range(tp_parts)] for group in inner_groups
     ]
 
-    weight = lax.all_gather(in_proj, "seq", axis=1, tiled=True, axis_index_groups=inner_groups)
-
     taps = lax.dynamic_slice_in_dim(short_taps, position * chans, chans, axis=2)
     taps = jnp.broadcast_to(taps[..., None], taps.shape + (rows,))
     skip = lax.dynamic_slice_in_dim(skip_gain, position * chans, chans, axis=0)
@@ -412,16 +434,22 @@
     filter_blocks = long_filter.T.reshape(seq_parts, chans, rows)
 
     held = share_columns(features, outer, tp_parts)
-    held, taps, skip, filter_blocks = lax.optimization_barrier((held, taps, skip, filter_blocks))
+    held, taps, skip = lax.optimization_barrier((held, taps, skip))
     arrived = cross_outer(held, outer, inner_parts, tp_parts)
-    arrived[-1], filter_blocks = lax.optimization_barrier((arrived[-1], filter_blocks))
     filter_blocks = lax.all_to_all(filter_blocks, "seq", split_axis=0, concat_axis=0, tiled=True)
+    arrived[1], filter_blocks = lax.optimization_barrier((arrived[1], filter_blocks))
+
+    def settle(held):
+        arrived[2], *held = lax.optimization_barrier((arrived[2], *held))
+        return held
+
+    weights, masks = gather_inner(in_proj, inner_parts, settle)
     chunks = [share_over_tp(piece, tp_parts) for piece in arrived]
     chunks, out_proj = lax.optimization_barrier((chunks, out_proj))
     out_weight = lax.all_gather(out_proj, ("seq", "tp"), axis_index_groups=tp_groups)
     out_weight = out_weight.reshape((inner_parts, tp_parts) + out_proj.shape)
 
-    partial = project_in(chunks, weight, seq_parts)
+    partial = project_in(chunks, weights, masks, inner_parts, seq_parts)
     parts = lax.all_to_all(partial, "seq", split_axis=0, concat_axis=0, tiled=True)
 
     parts, out_weight = lax.optimization_barrier((parts, out_weight))

time: 187 us -> 202 us (1.080)
  waiting for transfers between devices: 80.8 us -> 95.5 us
  starting transfers between devices: 27.7 us -> 29.8 us
    ppermute x0 -> x3, waiting for transfers between devices: none -> 7.18 us  [gather_inner(): held += [lax.ppermute(piece, 'seq', pairs) for piece in held]]
    ppermute x4, waiting for transfers between devices: 10.4 us -> 15.2 us  [share_over_tp(): pieces.append(lax.ppermute(part, 'tp', pairs))]
    ppermute x3, waiting for transfers between devices: 16.3 us -> 20.8 us  [cross_outer(): lax.ppermute(piece, 'seq', [(i, (i + far) % seq_parts) for i in range(seq...]
    all_to_all x1, waiting for transfers between devices: 8.13 us -> 5.52 us  [per_device(): lax.all_to_all(filter_blocks, 'seq', split_axis=0, concat_axis=0, tiled=T...]
  transfers between devices with their start and end apart: 16 -> 18, of which waited for: 10 -> 13; matrix products, arithmetic and copies ran while one was open for 1% -> 2% of each run, Pallas kernels for 4% -> 3%
where the time goes in v12:
time: 202 us; the launch traced here: 201 us
  waiting for transfers between devices  95.5 us (47%)
  blocking collectives  42.3 us (21%)
  starting transfers between devices  29.8 us (15%)
  Pallas kernels  14.3 us (7%)
  between operations  13.6 us (7%)
  local copies, waits for them, and re-layouts  5.45 us (3%)
    all_to_all x1, blocking collectives, per_device(): lax.all_to_all(partial, 'seq', split_axis=0, concat_axis=0, tiled=True)  42.3 us
    ppermute x3, waiting for transfers between devices, cross_outer(): lax.ppermute(piece, 'seq', [(i, (i + far) % seq_parts) for i in range(seq...  20.8 us
    ppermute x4, waiting for transfers between devices, return_output(): arrived.append(lax.ppermute(piece, ('seq', 'tp'), pairs))  19.5 us
    ppermute x4, waiting for transfers between devices, share_over_tp(): pieces.append(lax.ppermute(part, 'tp', pairs))  15.2 us
    all_to_all x1, waiting for transfers between devices, per_device(): lax.all_to_all(gated.reshape((-1,) + gated.shape[3:]), ('tp', 'seq'), spl...  14.4 us
    ppermute x1, waiting for transfers between devices, share_columns(): lax.ppermute(piece, 'tp', [(i, (i + step) % tp_parts) for i in range(tp_p...  12 us
    ppermute x4, starting transfers between devices, return_output(): arrived.append(lax.ppermute(piece, ('seq', 'tp'), pairs))  8.85 us
    ppermute x3, waiting for transfers between devices, gather_inner(): held += [lax.ppermute(piece, 'seq', pairs) for piece in held]  7.18 us
  transfers between devices with their start and end apart: 18, of which 13 were waited for; matrix products, arithmetic and copies ran while one was open for 2% of the time, Pallas kernels for 3%

profile of v12, /device:TPU:12, one launch (start us, length us, event | category | flops | bytes accessed | tf_op | source)
XLA Modules:
  0.0 201.3 jit_solution(6722440853982912767)
XLA Ops:
  10.8 12.0 %collective-permute-done = bf16[2,128,1024]{2,1,0:T(8,128)(2,1)S(1)} collective-permute-done((bf16[2,128,1024]{2,1,0:T(8,128)(2,1)S(1)}, bf16[2,128,1024]{2,1,0:T(8,128)(2,1)S(1)}, u32[]{:S(2)}, u32[]{:S(2)}) %collective-permute-start) | collective-permute-done | bytes 524320 | tf_op jit(solution)/shard_map/ppermute | solution.py:107
  23.2 2.7 %collective-permute-start.4 = (bf16[128,1024]{1,0:T(8,128)(2,1)S(1)}, bf16[128,1024]{1,0:T(8,128)(2,1)S(1)}, u32[]{:S(2)}, u32[]{:S(2)}) collective-permute-start(bf16[128,1024]{1,0:T(8,128)(2,1)S(1)} %get-tuple-element.52), channel_id=1, source_target_pairs={{0,16},{2,18},{4,20},{6,22},{8,24},{10,26},{12,28},{14,30},{16,0},... | collective-permute-start | bytes 786440 | tf_op jit(solution)/shard_map/ppermute | solution.py:124
  25.8 10.0 %collective-permute-done.4.refs_4_ = bf16[128,1024]{1,0:T(8,128)(2,1)S(1)} collective-permute-done((bf16[128,1024]{1,0:T(8,128)(2,1)S(1)}, bf16[128,1024]{1,0:T(8,128)(2,1)S(1)}, u32[]{:S(2)}, u32[]{:S(2)}) %collective-permute-start.4) | collective-permute-done | bytes 262176 | tf_op jit(solution)/shard_map/ppermute | solution.py:124
  35.8 7.2 %collective-permute-done.5.refs_9_ = bf16[3,512,512]{2,1,0:T(8,128)(2,1)} collective-permute-done((bf16[3,512,512]{2,1,0:T(8,128)(2,1)}, bf16[3,512,512]{2,1,0:T(8,128)(2,1)}, u32[]{:S(2)}, u32[]{:S(2)}) %collective-permute-start.5) | collective-permute-done | bytes 1572896 | tf_op jit(solution)/shard_map/ppermute | solution.py:142
  44.3 6.3 %all-to-all-start = ((f32[16,32,128]{2,1,0:T(8,128)}), f32[16,32,128]{2,1,0:T(8,128)S(1)}, u32[]{:S(2)}, u32[]{:S(2)}) async-start(f32[16,32,128]{2,1,0:T(8,128)} %bitcast.19), calls=%async_computation | async-start | bytes 524288 | tf_op jit(solution)/shard_map/all_to_all | solution.py:439
  53.2 5.5 %all-to-all-done.refs_1_ = f32[16,32,128]{2,1,0:T(8,128)S(1)} async-done(((f32[16,32,128]{2,1,0:T(8,128)}), f32[16,32,128]{2,1,0:T(8,128)S(1)}, u32[]{:S(2)}, u32[]{:S(2)}) %all-to-all-start) | async-done | bytes 262176 | tf_op jit(solution)/shard_map/all_to_all | solution.py:439
  58.8 9.5 %collective-permute-done.2.refs_2_ = bf16[128,1024]{1,0:T(8,128)(2,1)S(1)} collective-permute-done((bf16[128,1024]{1,0:T(8,128)(2,1)S(1)}, bf16[128,1024]{1,0:T(8,128)(2,1)S(1)}, u32[]{:S(2)}, u32[]{:S(2)}) %collective-permute-start.2) | collective-permute-done | bytes 262176 | tf_op jit(solution)/shard_map/ppermute | solution.py:124
  70.6 1.5 collective-permute-start.6
  72.2 5.2 %collective-permute-done.3.refs_3_ = bf16[128,1024]{1,0:T(8,128)(2,1)S(1)} collective-permute-done((bf16[128,1024]{1,0:T(8,128)(2,1)S(1)}, bf16[128,1024]{1,0:T(8,128)(2,1)S(1)}, u32[]{:S(2)}, u32[]{:S(2)}) %collective-permute-start.3) | collective-permute-done | bytes 262176 | tf_op jit(solution)/shard_map/ppermute | solution.py:133
  77.4 5.6 %collective-permute-done.8.refs_7_ = bf16[128,1024]{1,0:T(8,128)(2,1)S(1)} collective-permute-done((bf16[128,1024]{1,0:T(8,128)(2,1)S(1)}, bf16[128,1024]{1,0:T(8,128)(2,1)S(1)}, u32[]{:S(2)}, u32[]{:S(2)}) %collective-permute-start.8) | collective-permute-done | bytes 262176 | tf_op jit(solution)/shard_map/ppermute | solution.py:133
  83.0 4.4 %collective-permute-done.6.refs_5_ = bf16[128,1024]{1,0:T(8,128)(2,1)S(1)} collective-permute-done((bf16[128,1024]{1,0:T(8,128)(2,1)S(1)}, bf16[128,1024]{1,0:T(8,128)(2,1)S(1)}, u32[]{:S(2)}, u32[]{:S(2)}) %collective-permute-start.6) | collective-permute-done | bytes 262176 | tf_op jit(solution)/shard_map/ppermute | solution.py:133
  87.5 6.4 %shard_map.82 = bf16[16,3,32,512]{3,2,1,0:T(8,128)(2,1)S(1)} custom-call(s32[2]{0:T(128)S(1)} %pad_add_fusion.1.place_ref, bf16[128,1024]{1,0:T(8,128)(2,1)S(1)} %get-tuple-element.31.refs_0_, bf16[128,1024]{1,0:T(8,128)(2,1)S(1)} %collective-permute-done.1.refs_1_, bf16[128,1024]{1,0:T(8,128)(2,1)S(1)} %collective-permute-done.2.refs_2_, ...), custom_call_target="tpu_custom_call" | custom-call | flops 96636764160 | bytes 9961472 | tf_op jit(solution)/shard_map/pallas_call | solution.py:185
  93.9 42.3 %all_to_all.15.refs_0_ = bf16[16,3,32,512]{3,2,1,0:T(8,128)(2,1)S(1)} all-to-all(bf16[16,3,32,512]{3,2,1,0:T(8,128)(2,1)S(1)} %shard_map.82), channel_id=1, replica_groups=mesh['seq'=16,'tp'=2] {'seq'}, dimensions={0} | all-to-all | bytes 3145728 | tf_op jit(solution)/shard_map/all_to_all | solution.py:453
  136.9 3.7 %shard_map.83 = bf16[2,4,4,32,256]{4,3,2,1,0:T(8,128)(2,1)} custom-call(bf16[16,3,32,512]{3,2,1,0:T(8,128)(2,1)S(1)} %all_to_all.15.refs_0_, f32[16,32,128]{2,1,0:T(8,128)S(1)} %all-to-all-done.refs_1_, f32[3,3,32,128]{3,2,1,0:T(8,128)S(1)} %broadcast_in_dim.4.refs_2_, f32[32,128]{1,0:T(8,128)S(1)} %broadcast_in_dim.5.refs_3_, f32[128,256]{1,0:T(8,128)S(1)} %copy-done.3, ...), custom_call_target="tpu_custom_call" | custom-call | flops 1000000000 | bytes 4194304 | tf_op jit(solution)/shard_map/pallas_call | solution.py:345
  140.7 4.3 %all-to-all-start.2 = ((bf16[32,32,256]{2,1,0:T(8,128)(2,1)}), bf16[32,32,256]{2,1,0:T(8,128)(2,1)S(1)}, u32[]{:S(2)}, u32[]{:S(2)}) async-start(bf16[32,32,256]{2,1,0:T(8,128)(2,1)} %bitcast.23), calls=%async_computation.2 | async-start | bytes 1048576 | tf_op jit(solution)/shard_map/all_to_all | solution.py:458
  145.1 14.4 %all-to-all-done.2 = bf16[32,32,256]{2,1,0:T(8,128)(2,1)S(1)} async-done(((bf16[32,32,256]{2,1,0:T(8,128)(2,1)}), bf16[32,32,256]{2,1,0:T(8,128)(2,1)S(1)}, u32[]{:S(2)}, u32[]{:S(2)}) %all-to-all-start.2) | async-done | bytes 524320 | tf_op jit(solution)/shard_map/all_to_all | solution.py:458
  159.5 2.2 %copy-done.1 = bf16[4096,512]{1,0:T(8,128)(2,1)S(1)} copy-done((bf16[4096,512]{1,0:T(8,128)(2,1)S(1)}, bf16[4096,512]{1,0:T(8,128)(2,1)}, u32[]{:S(2)}) %copy-start.1) | copy-done | bytes 4194328
  161.7 2.6 %shard_map.84 = (bf16[64,2048]{1,0:T(8,128)(2,1)S(1)}, bf16[64,2048]{1,0:T(8,128)(2,1)S(1)}, bf16[64,2048]{1,0:T(8,128)(2,1)S(1)}, bf16[64,2048]{1,0:T(8,128)(2,1)S(1)}) custom-call(s32[4]{0:T(128)S(1)} %pad_add_fusion.block_ref, bf16[2,512,256]{2,1,0:T(8,128)(2,1)S(1)} %bitcast.34, bf16[4,2,512,512]{3,2,1,0:T(8,128)(2,1)S(1)} %bitcast.33), custom_call_target="tpu_custom_call" | custom-call | flops 1073741824 | bytes 5767168 | tf_op jit(solution)/shard_map/pallas_call | solution.py:391
  164.4 2.6 %collective-permute-start.11 = (bf16[64,2048]{1,0:T(8,128)(2,1)S(1)}, bf16[64,2048]{1,0:T(8,128)(2,1)S(1)}, u32[]{:S(2)}, u32[]{:S(2)}) collective-permute-start(bf16[64,2048]{1,0:T(8,128)(2,1)S(1)} %get-tuple-element.47), channel_id=1, source_target_pairs={{0,0},{1,16},{2,2},{3,18},{4,4},{5,20},{6,6},{7,22},{8,24},{9,8},{... | collective-permute-start | bytes 786440 | tf_op jit(solution)/shard_map/ppermute | solution.py:88
  167.0 3.9 %collective-permute-start.13 = (bf16[64,2048]{1,0:T(8,128)(2,1)S(1)}, bf16[64,2048]{1,0:T(8,128)(2,1)S(1)}, u32[]{:S(2)}, u32[]{:S(2)}) collective-permute-start(bf16[64,2048]{1,0:T(8,128)(2,1)S(1)} %get-tuple-element.49), channel_id=1, source_target_pairs={{0,16},{1,0},{2,18},{3,2},{4,20},{5,4},{6,22},{7,6},{8,8},{9,24},{... | collective-permute-start | bytes 786440 | tf_op jit(solution)/shard_map/ppermute | solution.py:88
  170.9 2.3 %collective-permute-start.14 = (bf16[64,2048]{1,0:T(8,128)(2,1)S(1)}, bf16[64,2048]{1,0:T(8,128)(2,1)S(1)}, u32[]{:S(2)}, u32[]{:S(2)}) collective-permute-start(bf16[64,2048]{1,0:T(8,128)(2,1)S(1)} %get-tuple-element.50), channel_id=1, source_target_pairs={{0,24},{1,8},{2,26},{3,10},{4,28},{5,12},{6,30},{7,14},{8,0},{9,16... | collective-permute-start | bytes 786440 | tf_op jit(solution)/shard_map/ppermute | solution.py:88
  173.3 3.2 %collective-permute-done.11.refs_0_ = bf16[64,2048]{1,0:T(8,128)(2,1)S(1)} collective-permute-done((bf16[64,2048]{1,0:T(8,128)(2,1)S(1)}, bf16[64,2048]{1,0:T(8,128)(2,1)S(1)}, u32[]{:S(2)}, u32[]{:S(2)}) %collective-permute-start.11) | collective-permute-done | bytes 262176 | tf_op jit(solution)/shard_map/ppermute | solution.py:88
  176.5 16.4 %collective-permute-done.12.refs_1_ = bf16[64,2048]{1,0:T(8,128)(2,1)S(1)} collective-permute-done((bf16[64,2048]{1,0:T(8,128)(2,1)S(1)}, bf16[64,2048]{1,0:T(8,128)(2,1)S(1)}, u32[]{:S(2)}, u32[]{:S(2)}) %collective-permute-start.12) | collective-permute-done | bytes 262176 | tf_op jit(solution)/shard_map/ppermute | solution.py:88
  192.9 1.5 shard_map.85
  (40 shorter events, 12.1 us)
Async XLA Ops:
  6.5 4.1 %copy-start = (f32[3,3,512]{2,1,0:T(4,128)S(1)}, f32[3,3,512]{2,1,0:T(4,128)}, u32[]{:S(2)}) copy-start(f32[3,3,512]{2,1,0:T(4,128)} %param.10) | copy-start | bytes 55300
  6.5 36.5 %collective-permute-start.5 = (bf16[3,512,512]{2,1,0:T(8,128)(2,1)}, bf16[3,512,512]{2,1,0:T(8,128)(2,1)}, u32[]{:S(2)}, u32[]{:S(2)}) collective-permute-start(bf16[3,512,512]{2,1,0:T(8,128)(2,1)} %refs_8_), channel_id=1, source_target_pairs={{0,4},{2,6},{4,0},{6,2},{8,12},{10,14},{12,8},{14,10},{16,20},{18,... | collective-permute-start | bytes 4718600 | tf_op jit(solution)/shard_map/ppermute | solution.py:142
  9.3 13.4 %collective-permute-start = (bf16[2,128,1024]{2,1,0:T(8,128)(2,1)S(1)}, bf16[2,128,1024]{2,1,0:T(8,128)(2,1)S(1)}, u32[]{:S(2)}, u32[]{:S(2)}) collective-permute-start(bf16[2,128,1024]{2,1,0:T(8,128)(2,1)S(1)} %pad_maximum_fusion.1), channel_id=1, source_target_pairs={{0,1},{1,0},{2,3},{3,2},{4,5},{5,4},{6,7},{7,6},{8,9},{9,8},{10,11... | collective-permute-start | bytes 1572872 | tf_op jit(solution)/shard_map/ppermute | solution.py:107
  22.9 20.6 %copy-start.4 = (f32[128,512]{1,0:T(8,128)S(1)}, f32[128,512]{1,0:T(8,128)}, u32[]{:S(2)}) copy-start(f32[128,512]{1,0:T(8,128)} %param.11) | copy-start | bytes 786436
  23.2 12.6 %collective-permute-start.4 = (bf16[128,1024]{1,0:T(8,128)(2,1)S(1)}, bf16[128,1024]{1,0:T(8,128)(2,1)S(1)}, u32[]{:S(2)}, u32[]{:S(2)}) collective-permute-start(bf16[128,1024]{1,0:T(8,128)(2,1)S(1)} %get-tuple-element.52), channel_id=1, source_target_pairs={{0,16},{2,18},{4,20},{6,22},{8,24},{10,26},{12,28},{14,30},{16,0},... | collective-permute-start | bytes 786440 | tf_op jit(solution)/shard_map/ppermute | solution.py:124
  43.0 44.4 %collective-permute-start.9 = (bf16[3,512,512]{2,1,0:T(8,128)(2,1)}, bf16[3,512,512]{2,1,0:T(8,128)(2,1)}, u32[]{:S(2)}, u32[]{:S(2)}) collective-permute-start(bf16[3,512,512]{2,1,0:T(8,128)(2,1)} %refs_8_), channel_id=1, source_target_pairs={{0,2},{2,0},{4,6},{6,4},{8,10},{10,8},{12,14},{14,12},{16,18},{18,... | collective-permute-start | bytes 4718600 | tf_op jit(solution)/shard_map/ppermute | solution.py:142
  43.0 44.5 %collective-permute-start.10 = (bf16[3,512,512]{2,1,0:T(8,128)(2,1)}, bf16[3,512,512]{2,1,0:T(8,128)(2,1)}, u32[]{:S(2)}, u32[]{:S(2)}) collective-permute-start(bf16[3,512,512]{2,1,0:T(8,128)(2,1)} %collective-permute-done.5.refs_9_), channel_id=1, source_target_pairs={{0,2},{2,0},{4,6},{6,4},{8,10},{10,8},{12,14},{14,12},{16,18},{18,... | collective-permute-start | bytes 4718600 | tf_op jit(solution)/shard_map/ppermute | solution.py:142
  44.3 14.4 %all-to-all-start = ((f32[16,32,128]{2,1,0:T(8,128)}), f32[16,32,128]{2,1,0:T(8,128)S(1)}, u32[]{:S(2)}, u32[]{:S(2)}) async-start(f32[16,32,128]{2,1,0:T(8,128)} %bitcast.19), calls=%async_computation | async-start | bytes 524288 | tf_op jit(solution)/shard_map/all_to_all | solution.py:439
  50.6 86.3 %all-gather.3.cloned.1.call-start = ((), (), s32[]{:S(2)}) async-start(), calls=%async_computation.3 | async-start | bytes 4718592 | tf_op jit(solution)/shard_map/all_gather | solution.py:449
  50.6 17.6 %collective-permute-start.2 = (bf16[128,1024]{1,0:T(8,128)(2,1)S(1)}, bf16[128,1024]{1,0:T(8,128)(2,1)S(1)}, u32[]{:S(2)}, u32[]{:S(2)}) collective-permute-start(bf16[128,1024]{1,0:T(8,128)(2,1)S(1)} %get-tuple-element.53), channel_id=1, source_target_pairs={{0,8},{2,10},{4,12},{6,14},{8,16},{10,18},{12,20},{14,22},{16,24},... | collective-permute-start | bytes 786440 | tf_op jit(solution)/shard_map/ppermute | solution.py:124
  52.2 18.0 %collective-permute-start.7 = (bf16[128,1024]{1,0:T(8,128)(2,1)S(1)}, bf16[128,1024]{1,0:T(8,128)(2,1)S(1)}, u32[]{:S(2)}, u32[]{:S(2)}) collective-permute-start(bf16[128,1024]{1,0:T(8,128)(2,1)S(1)} %get-tuple-element.51), channel_id=1, source_target_pairs={{0,24},{2,26},{4,28},{6,30},{8,0},{10,2},{12,4},{14,6},{16,8},{18,... | collective-permute-start | bytes 786440 | tf_op jit(solution)/shard_map/ppermute | solution.py:124
  52.7 17.9 %collective-permute-start.1 = (bf16[128,1024]{1,0:T(8,128)(2,1)S(1)}, bf16[128,1024]{1,0:T(8,128)(2,1)S(1)}, u32[]{:S(2)}, u32[]{:S(2)}) collective-permute-start(bf16[128,1024]{1,0:T(8,128)(2,1)S(1)} %get-tuple-element.31.refs_0_), channel_id=1, source_target_pairs={{0,1},{1,0},{2,3},{3,2},{4,5},{5,4},{6,7},{7,6},{8,9},{9,8},{10,11... | collective-permute-start | bytes 786440 | tf_op jit(solution)/shard_map/ppermute | solution.py:133
  68.2 9.2 %collective-permute-start.3 = (bf16[128,1024]{1,0:T(8,128)(2,1)S(1)}, bf16[128,1024]{1,0:T(8,128)(2,1)S(1)}, u32[]{:S(2)}, u32[]{:S(2)}) collective-permute-start(bf16[128,1024]{1,0:T(8,128)(2,1)S(1)} %collective-permute-done.2.refs_2_), channel_id=1, source_target_pairs={{0,1},{1,0},{2,3},{3,2},{4,5},{5,4},{6,7},{7,6},{8,9},{9,8},{10,11... | collective-permute-start | bytes 786440 | tf_op jit(solution)/shard_map/ppermute | solution.py:133
  70.1 12.9 %collective-permute-start.8 = (bf16[128,1024]{1,0:T(8,128)(2,1)S(1)}, bf16[128,1024]{1,0:T(8,128)(2,1)S(1)}, u32[]{:S(2)}, u32[]{:S(2)}) collective-permute-start(bf16[128,1024]{1,0:T(8,128)(2,1)S(1)} %collective-permute-done.7.refs_6_), channel_id=1, source_target_pairs={{0,1},{1,0},{2,3},{3,2},{4,5},{5,4},{6,7},{7,6},{8,9},{9,8},{10,11... | collective-permute-start | bytes 786440 | tf_op jit(solution)/shard_map/ppermute | solution.py:133
  70.6 16.8 %collective-permute-start.6 = (bf16[128,1024]{1,0:T(8,128)(2,1)S(1)}, bf16[128,1024]{1,0:T(8,128)(2,1)S(1)}, u32[]{:S(2)}, u32[]{:S(2)}) collective-permute-start(bf16[128,1024]{1,0:T(8,128)(2,1)S(1)} %collective-permute-done.4.refs_4_), channel_id=1, source_target_pairs={{0,1},{1,0},{2,3},{3,2},{4,5},{5,4},{6,7},{7,6},{8,9},{9,8},{10,11... | collective-permute-start | bytes 786440 | tf_op jit(solution)/shard_map/ppermute | solution.py:133
  93.8 43.1 %copy-start.2 = (f32[256,256]{1,0:T(8,128)S(1)}, f32[256,256]{1,0:T(8,128)}, u32[]{:S(2)}) copy-start(f32[256,256]{1,0:T(8,128)} %constant.234.clone.refs_5_) | copy-start | bytes 786436
  93.9 43.1 %copy-start.3 = (f32[128,256]{1,0:T(8,128)S(1)}, f32[128,256]{1,0:T(8,128)}, u32[]{:S(2)}) copy-start(f32[128,256]{1,0:T(8,128)} %constant.233.clone.refs_4_) | copy-start | bytes 393220
  140.7 18.8 %all-to-all-start.2 = ((bf16[32,32,256]{2,1,0:T(8,128)(2,1)}), bf16[32,32,256]{2,1,0:T(8,128)(2,1)S(1)}, u32[]{:S(2)}, u32[]{:S(2)}) async-start(bf16[32,32,256]{2,1,0:T(8,128)(2,1)} %bitcast.23), calls=%async_computation.2 | async-start | bytes 1048576 | tf_op jit(solution)/shard_map/all_to_all | solution.py:458
  159.5 2.2 %copy-start.1 = (bf16[4096,512]{1,0:T(8,128)(2,1)S(1)}, bf16[4096,512]{1,0:T(8,128)(2,1)}, u32[]{:S(2)}) copy-start(bf16[4096,512]{1,0:T(8,128)(2,1)} %all-gather.3.cloned.1.call-done) | copy-start | bytes 12582916
  164.4 12.1 %collective-permute-start.11 = (bf16[64,2048]{1,0:T(8,128)(2,1)S(1)}, bf16[64,2048]{1,0:T(8,128)(2,1)S(1)}, u32[]{:S(2)}, u32[]{:S(2)}) collective-permute-start(bf16[64,2048]{1,0:T(8,128)(2,1)S(1)} %get-tuple-element.47), channel_id=1, source_target_pairs={{0,0},{1,16},{2,2},{3,18},{4,4},{5,20},{6,6},{7,22},{8,24},{9,8},{... | collective-permute-start | bytes 786440 | tf_op jit(solution)/shard_map/ppermute | solution.py:88
  167.0 25.9 %collective-permute-start.12 = (bf16[64,2048]{1,0:T(8,128)(2,1)S(1)}, bf16[64,2048]{1,0:T(8,128)(2,1)S(1)}, u32[]{:S(2)}, u32[]{:S(2)}) collective-permute-start(bf16[64,2048]{1,0:T(8,128)(2,1)S(1)} %get-tuple-element.48), channel_id=1, source_target_pairs={{0,8},{1,24},{2,10},{3,26},{4,12},{5,28},{6,14},{7,30},{8,16},{9,0... | collective-permute-start | bytes 786440 | tf_op jit(solution)/shard_map/ppermute | solution.py:88
  167.0 25.8 %collective-permute-start.13 = (bf16[64,2048]{1,0:T(8,128)(2,1)S(1)}, bf16[64,2048]{1,0:T(8,128)(2,1)S(1)}, u32[]{:S(2)}, u32[]{:S(2)}) collective-permute-start(bf16[64,2048]{1,0:T(8,128)(2,1)S(1)} %get-tuple-element.49), channel_id=1, source_target_pairs={{0,16},{1,0},{2,18},{3,2},{4,20},{5,4},{6,22},{7,6},{8,8},{9,24},{... | collective-permute-start | bytes 786440 | tf_op jit(solution)/shard_map/ppermute | solution.py:88
  170.9 22.0 %collective-permute-start.14 = (bf16[64,2048]{1,0:T(8,128)(2,1)S(1)}, bf16[64,2048]{1,0:T(8,128)(2,1)S(1)}, u32[]{:S(2)}, u32[]{:S(2)}) collective-permute-start(bf16[64,2048]{1,0:T(8,128)(2,1)S(1)} %get-tuple-element.50), channel_id=1, source_target_pairs={{0,24},{1,8},{2,26},{3,10},{4,28},{5,12},{6,30},{7,14},{8,0},{9,16... | collective-permute-start | bytes 786440 | tf_op jit(solution)/shard_map/ppermute | solution.py:88
Sparse Core Ops, SparseCore 0:
  87.5 49.3 all-gather.2

commit v13 on v12

--- a/solution.py
+++ b/solution.py
@@ -134,15 +134,13 @@
     return pieces
 
 
-def gather_inner(block, inner_parts, settle):
+def gather_inner(block, inner_parts):
     held, masks = [block], [0]
     bit = inner_parts // 2
     while bit:
         pairs = [(i, i ^ bit) for i in range(lax.axis_size("seq"))]
         held += [lax.ppermute(piece, "seq", pairs) for piece in held]
         masks += [mask ^ bit for mask in masks]
-        if bit == inner_parts // 2:
-            held = settle(held)
         bit //= 2
     return held, masks
 
@@ -439,11 +437,7 @@
     filter_blocks = lax.all_to_all(filter_blocks, "seq", split_axis=0, concat_axis=0, tiled=True)
     arrived[1], filter_blocks = lax.optimization_barrier((arrived[1], filter_blocks))
 
-    def settle(held):
-        arrived[2], *held = lax.optimization_barrier((arrived[2], *held))
-        return held
-
-    weights, masks = gather_inner(in_proj, inner_parts, settle)
+    weights, masks = gather_inner(in_proj, inner_parts)
     chunks = [share_over_tp(piece, tp_parts) for piece in arrived]
     chunks, out_proj = lax.optimization_barrier((chunks, out_proj))
     out_weight = lax.all_gather(out_proj, ("seq", "tp"), axis_index_groups=tp_groups)

time: 202 us -> 204 us (level)
  waiting for transfers between devices: 95.5 us -> 99.5 us
  starting transfers between devices: 29.8 us -> 27.3 us
    ppermute x3, waiting for transfers between devices: 7.18 us -> 33.1 us  [gather_inner(): held += [lax.ppermute(piece, 'seq', pairs) for piece in held]]
    ppermute x3, waiting for transfers between devices: 20.8 us -> 6.17 us  [cross_outer(): lax.ppermute(piece, 'seq', [(i, (i + far) % seq_parts) for i in range(seq...]
    ppermute x1, waiting for transfers between devices: 12 us -> 0.01 us  [share_columns(): lax.ppermute(piece, 'tp', [(i, (i + step) % tp_parts) for i in range(tp_p...]
    all_to_all x1, waiting for transfers between devices: 5.52 us -> 14.4 us  [per_device(): lax.all_to_all(filter_blocks, 'seq', split_axis=0, concat_axis=0, tiled=T...]
    ppermute x4, waiting for transfers between devices: 15.2 us -> 11.1 us  [share_over_tp(): pieces.append(lax.ppermute(part, 'tp', pairs))]
  transfers between devices with their start and end apart: 18 -> 18, of which waited for: 13 -> 10; matrix products, arithmetic and copies ran while one was open for 2% -> 2% of each run, Pallas kernels for 3% -> 3%
where the time goes in v13:
time: 204 us
  waiting for transfers between devices  99.5 us (49%)
  blocking collectives  43.5 us (21%)
  starting transfers between devices  27.3 us (13%)
  Pallas kernels  14.3 us (7%)
  between operations  13.6 us (7%)
  local copies, waits for them, and re-layouts  5.46 us (3%)
    all_to_all x1, blocking collectives, per_device(): lax.all_to_all(partial, 'seq', split_axis=0, concat_axis=0, tiled=True)  43.5 us
    ppermute x3, waiting for transfers between devices, gather_inner(): held += [lax.ppermute(piece, 'seq', pairs) for piece in held]  33.1 us
    ppermute x4, waiting for transfers between devices, return_output(): arrived.append(lax.ppermute(piece, ('seq', 'tp'), pairs))  19.5 us
    all_to_all x1, waiting for transfers between devices, per_device(): lax.all_to_all(filter_blocks, 'seq', split_axis=0, concat_axis=0, tiled=T...  14.4 us
    all_to_all x1, waiting for transfers between devices, per_device(): lax.all_to_all(gated.reshape((-1,) + gated.shape[3:]), ('tp', 'seq'), spl...  14.4 us
    ppermute x4, waiting for transfers between devices, share_over_tp(): pieces.append(lax.ppermute(part, 'tp', pairs))  11.1 us
    ppermute x4, starting transfers between devices, return_output(): arrived.append(lax.ppermute(piece, ('seq', 'tp'), pairs))  8.85 us
    pallas_call x1, Pallas kernels, project_in(): pl.pallas_call(functools.partial(project_kernel, tp_parts, masks), in_spe...  6.38 us
  transfers between devices with their start and end apart: 18, of which 10 were waited for; matrix products, arithmetic and copies ran while one was open for 2% of the time, Pallas kernels for 3%

profile of v13, /device:TPU:12, one launch (start us, length us, event | category | flops | bytes accessed | tf_op | source)
XLA Modules:
  0.0 204.0 jit_solution(6088705938215622)
XLA Ops:
  6.5 1.5 collective-permute-start.8
  8.0 1.3 dynamic-slice_bitcast_fusion.7
  9.9 33.1 %collective-permute-done.8.refs_9_ = bf16[3,512,512]{2,1,0:T(8,128)(2,1)} collective-permute-done((bf16[3,512,512]{2,1,0:T(8,128)(2,1)}, bf16[3,512,512]{2,1,0:T(8,128)(2,1)}, u32[]{:S(2)}, u32[]{:S(2)}) %collective-permute-start.8) | collective-permute-done | bytes 1572896 | tf_op jit(solution)/shard_map/ppermute | solution.py:142
  44.2 1.6 collective-permute-start.2
  46.7 5.4 %all-to-all-start = ((f32[16,32,128]{2,1,0:T(8,128)}), f32[16,32,128]{2,1,0:T(8,128)S(1)}, u32[]{:S(2)}, u32[]{:S(2)}) async-start(f32[16,32,128]{2,1,0:T(8,128)} %bitcast.19), calls=%async_computation | async-start | bytes 524288 | tf_op jit(solution)/shard_map/all_to_all | solution.py:437
  52.7 2.4 %collective-permute-start.4 = (bf16[128,1024]{1,0:T(8,128)(2,1)S(1)}, bf16[128,1024]{1,0:T(8,128)(2,1)S(1)}, u32[]{:S(2)}, u32[]{:S(2)}) collective-permute-start(bf16[128,1024]{1,0:T(8,128)(2,1)S(1)} %get-tuple-element.46), channel_id=1, source_target_pairs={{0,16},{2,18},{4,20},{6,22},{8,24},{10,26},{12,28},{14,30},{16,0},... | collective-permute-start | bytes 786440 | tf_op jit(solution)/shard_map/ppermute | solution.py:124
  55.7 14.4 %all-to-all-done.refs_1_ = f32[16,32,128]{2,1,0:T(8,128)S(1)} async-done(((f32[16,32,128]{2,1,0:T(8,128)}), f32[16,32,128]{2,1,0:T(8,128)S(1)}, u32[]{:S(2)}, u32[]{:S(2)}) %all-to-all-start) | async-done | bytes 262176 | tf_op jit(solution)/shard_map/all_to_all | solution.py:437
  70.6 4.8 %collective-permute-done.4.refs_4_ = bf16[128,1024]{1,0:T(8,128)(2,1)S(1)} collective-permute-done((bf16[128,1024]{1,0:T(8,128)(2,1)S(1)}, bf16[128,1024]{1,0:T(8,128)(2,1)S(1)}, u32[]{:S(2)}, u32[]{:S(2)}) %collective-permute-start.4) | collective-permute-done | bytes 262176 | tf_op jit(solution)/shard_map/ppermute | solution.py:124
  75.8 1.4 collective-permute-done.6.refs_6_
  77.8 6.7 %collective-permute-done.5.refs_5_ = bf16[128,1024]{1,0:T(8,128)(2,1)S(1)} collective-permute-done((bf16[128,1024]{1,0:T(8,128)(2,1)S(1)}, bf16[128,1024]{1,0:T(8,128)(2,1)S(1)}, u32[]{:S(2)}, u32[]{:S(2)}) %collective-permute-start.5) | collective-permute-done | bytes 262176 | tf_op jit(solution)/shard_map/ppermute | solution.py:133
  84.5 4.4 %collective-permute-done.7.refs_7_ = bf16[128,1024]{1,0:T(8,128)(2,1)S(1)} collective-permute-done((bf16[128,1024]{1,0:T(8,128)(2,1)S(1)}, bf16[128,1024]{1,0:T(8,128)(2,1)S(1)}, u32[]{:S(2)}, u32[]{:S(2)}) %collective-permute-start.7) | collective-permute-done | bytes 262176 | tf_op jit(solution)/shard_map/ppermute | solution.py:133
  89.0 6.4 %shard_map.82 = bf16[16,3,32,512]{3,2,1,0:T(8,128)(2,1)S(1)} custom-call(s32[2]{0:T(128)S(1)} %pad_add_fusion.1.place_ref, bf16[128,1024]{1,0:T(8,128)(2,1)S(1)} %get-tuple-element.27.refs_0_, bf16[128,1024]{1,0:T(8,128)(2,1)S(1)} %collective-permute-done.1.refs_1_, bf16[128,1024]{1,0:T(8,128)(2,1)S(1)} %collective-permute-done.2.refs_2_, ...), custom_call_target="tpu_custom_call" | custom-call | flops 96636764160 | bytes 9961472 | tf_op jit(solution)/shard_map/pallas_call | solution.py:183
  95.4 43.5 %all_to_all.15.refs_0_ = bf16[16,3,32,512]{3,2,1,0:T(8,128)(2,1)S(1)} all-to-all(bf16[16,3,32,512]{3,2,1,0:T(8,128)(2,1)S(1)} %shard_map.82), channel_id=1, replica_groups=mesh['seq'=16,'tp'=2] {'seq'}, dimensions={0} | all-to-all | bytes 3145728 | tf_op jit(solution)/shard_map/all_to_all | solution.py:447
  139.7 3.7 %shard_map.83 = bf16[2,4,4,32,256]{4,3,2,1,0:T(8,128)(2,1)} custom-call(bf16[16,3,32,512]{3,2,1,0:T(8,128)(2,1)S(1)} %all_to_all.15.refs_0_, f32[16,32,128]{2,1,0:T(8,128)S(1)} %all-to-all-done.refs_1_, f32[3,3,32,128]{3,2,1,0:T(8,128)S(1)} %broadcast_in_dim.4.refs_2_, f32[32,128]{1,0:T(8,128)S(1)} %broadcast_in_dim.5.refs_3_, f32[128,256]{1,0:T(8,128)S(1)} %copy-done.3, ...), custom_call_target="tpu_custom_call" | custom-call | flops 1000000000 | bytes 4194304 | tf_op jit(solution)/shard_map/pallas_call | solution.py:343
  143.4 4.3 %all-to-all-start.2 = ((bf16[32,32,256]{2,1,0:T(8,128)(2,1)}), bf16[32,32,256]{2,1,0:T(8,128)(2,1)S(1)}, u32[]{:S(2)}, u32[]{:S(2)}) async-start(bf16[32,32,256]{2,1,0:T(8,128)(2,1)} %bitcast.23), calls=%async_computation.2 | async-start | bytes 1048576 | tf_op jit(solution)/shard_map/all_to_all | solution.py:452
  147.9 14.4 %all-to-all-done.2 = bf16[32,32,256]{2,1,0:T(8,128)(2,1)S(1)} async-done(((bf16[32,32,256]{2,1,0:T(8,128)(2,1)}), bf16[32,32,256]{2,1,0:T(8,128)(2,1)S(1)}, u32[]{:S(2)}, u32[]{:S(2)}) %all-to-all-start.2) | async-done | bytes 524320 | tf_op jit(solution)/shard_map/all_to_all | solution.py:452
  162.3 2.2 %copy-done.1 = bf16[4096,512]{1,0:T(8,128)(2,1)S(1)} copy-done((bf16[4096,512]{1,0:T(8,128)(2,1)S(1)}, bf16[4096,512]{1,0:T(8,128)(2,1)}, u32[]{:S(2)}) %copy-start.1) | copy-done | bytes 4194328
  164.4 2.6 %shard_map.84 = (bf16[64,2048]{1,0:T(8,128)(2,1)S(1)}, bf16[64,2048]{1,0:T(8,128)(2,1)S(1)}, bf16[64,2048]{1,0:T(8,128)(2,1)S(1)}, bf16[64,2048]{1,0:T(8,128)(2,1)S(1)}) custom-call(s32[4]{0:T(128)S(1)} %pad_add_fusion.block_ref, bf16[2,512,256]{2,1,0:T(8,128)(2,1)S(1)} %bitcast.34, bf16[4,2,512,512]{3,2,1,0:T(8,128)(2,1)S(1)} %bitcast.33), custom_call_target="tpu_custom_call" | custom-call | flops 1073741824 | bytes 5767168 | tf_op jit(solution)/shard_map/pallas_call | solution.py:389
  167.1 2.6 %collective-permute-start.11 = (bf16[64,2048]{1,0:T(8,128)(2,1)S(1)}, bf16[64,2048]{1,0:T(8,128)(2,1)S(1)}, u32[]{:S(2)}, u32[]{:S(2)}) collective-permute-start(bf16[64,2048]{1,0:T(8,128)(2,1)S(1)} %get-tuple-element.41), channel_id=1, source_target_pairs={{0,0},{1,16},{2,2},{3,18},{4,4},{5,20},{6,6},{7,22},{8,24},{9,8},{... | collective-permute-start | bytes 786440 | tf_op jit(solution)/shard_map/ppermute | solution.py:88
  169.8 3.9 %collective-permute-start.13 = (bf16[64,2048]{1,0:T(8,128)(2,1)S(1)}, bf16[64,2048]{1,0:T(8,128)(2,1)S(1)}, u32[]{:S(2)}, u32[]{:S(2)}) collective-permute-start(bf16[64,2048]{1,0:T(8,128)(2,1)S(1)} %get-tuple-element.43), channel_id=1, source_target_pairs={{0,16},{1,0},{2,18},{3,2},{4,20},{5,4},{6,22},{7,6},{8,8},{9,24},{... | collective-permute-start | bytes 786440 | tf_op jit(solution)/shard_map/ppermute | solution.py:88
  173.7 2.3 %collective-permute-start.14 = (bf16[64,2048]{1,0:T(8,128)(2,1)S(1)}, bf16[64,2048]{1,0:T(8,128)(2,1)S(1)}, u32[]{:S(2)}, u32[]{:S(2)}) collective-permute-start(bf16[64,2048]{1,0:T(8,128)(2,1)S(1)} %get-tuple-element.44), channel_id=1, source_target_pairs={{0,24},{1,8},{2,26},{3,10},{4,28},{5,12},{6,30},{7,14},{8,0},{9,16... | collective-permute-start | bytes 786440 | tf_op jit(solution)/shard_map/ppermute | solution.py:88
  176.1 3.2 %collective-permute-done.11.refs_0_ = bf16[64,2048]{1,0:T(8,128)(2,1)S(1)} collective-permute-done((bf16[64,2048]{1,0:T(8,128)(2,1)S(1)}, bf16[64,2048]{1,0:T(8,128)(2,1)S(1)}, u32[]{:S(2)}, u32[]{:S(2)}) %collective-permute-start.11) | collective-permute-done | bytes 262176 | tf_op jit(solution)/shard_map/ppermute | solution.py:88
  179.2 16.4 %collective-permute-done.12.refs_1_ = bf16[64,2048]{1,0:T(8,128)(2,1)S(1)} collective-permute-done((bf16[64,2048]{1,0:T(8,128)(2,1)S(1)}, bf16[64,2048]{1,0:T(8,128)(2,1)S(1)}, u32[]{:S(2)}, u32[]{:S(2)}) %collective-permute-start.12) | collective-permute-done | bytes 262176 | tf_op jit(solution)/shard_map/ppermute | solution.py:88
  195.6 1.5 shard_map.85
  (40 shorter events, 6.5 us)
Async XLA Ops:
  6.5 37.2 %copy-start = (f32[3,3,512]{2,1,0:T(4,128)S(1)}, f32[3,3,512]{2,1,0:T(4,128)}, u32[]{:S(2)}) copy-start(f32[3,3,512]{2,1,0:T(4,128)} %param.10) | copy-start | bytes 55300
  6.5 36.5 %collective-permute-start.8 = (bf16[3,512,512]{2,1,0:T(8,128)(2,1)}, bf16[3,512,512]{2,1,0:T(8,128)(2,1)}, u32[]{:S(2)}, u32[]{:S(2)}) collective-permute-start(bf16[3,512,512]{2,1,0:T(8,128)(2,1)} %refs_8_.1), channel_id=1, source_target_pairs={{0,4},{2,6},{4,0},{6,2},{8,12},{10,14},{12,8},{14,10},{16,20},{18,... | collective-permute-start | bytes 4718600 | tf_op jit(solution)/shard_map/ppermute | solution.py:142
  9.3 34.5 %collective-permute-start = (bf16[2,128,1024]{2,1,0:T(8,128)(2,1)S(1)}, bf16[2,128,1024]{2,1,0:T(8,128)(2,1)S(1)}, u32[]{:S(2)}, u32[]{:S(2)}) collective-permute-start(bf16[2,128,1024]{2,1,0:T(8,128)(2,1)S(1)} %pad_maximum_fusion.1), channel_id=1, source_target_pairs={{0,1},{1,0},{2,3},{3,2},{4,5},{5,4},{6,7},{7,6},{8,9},{9,8},{10,11... | collective-permute-start | bytes 1572872 | tf_op jit(solution)/shard_map/ppermute | solution.py:107
  9.9 79.0 %collective-permute-start.9 = (bf16[3,512,512]{2,1,0:T(8,128)(2,1)}, bf16[3,512,512]{2,1,0:T(8,128)(2,1)}, u32[]{:S(2)}, u32[]{:S(2)}) collective-permute-start(bf16[3,512,512]{2,1,0:T(8,128)(2,1)} %refs_8_.1), channel_id=1, source_target_pairs={{0,2},{2,0},{4,6},{6,4},{8,10},{10,8},{12,14},{14,12},{16,18},{18,... | collective-permute-start | bytes 4718600 | tf_op jit(solution)/shard_map/ppermute | solution.py:142
  43.0 46.0 %collective-permute-start.10 = (bf16[3,512,512]{2,1,0:T(8,128)(2,1)}, bf16[3,512,512]{2,1,0:T(8,128)(2,1)}, u32[]{:S(2)}, u32[]{:S(2)}) collective-permute-start(bf16[3,512,512]{2,1,0:T(8,128)(2,1)} %collective-permute-done.8.refs_9_), channel_id=1, source_target_pairs={{0,2},{2,0},{4,6},{6,4},{8,10},{10,8},{12,14},{14,12},{16,18},{18,... | collective-permute-start | bytes 4718600 | tf_op jit(solution)/shard_map/ppermute | solution.py:142
  43.9 1.9 copy-start.4
  44.2 10.9 %collective-permute-start.2 = (bf16[128,1024]{1,0:T(8,128)(2,1)S(1)}, bf16[128,1024]{1,0:T(8,128)(2,1)S(1)}, u32[]{:S(2)}, u32[]{:S(2)}) collective-permute-start(bf16[128,1024]{1,0:T(8,128)(2,1)S(1)} %get-tuple-element.47), channel_id=1, source_target_pairs={{0,8},{2,10},{4,12},{6,14},{8,16},{10,18},{12,20},{14,22},{16,24},... | collective-permute-start | bytes 786440 | tf_op jit(solution)/shard_map/ppermute | solution.py:124
  46.7 23.4 %all-to-all-start = ((f32[16,32,128]{2,1,0:T(8,128)}), f32[16,32,128]{2,1,0:T(8,128)S(1)}, u32[]{:S(2)}, u32[]{:S(2)}) async-start(f32[16,32,128]{2,1,0:T(8,128)} %bitcast.19), calls=%async_computation | async-start | bytes 524288 | tf_op jit(solution)/shard_map/all_to_all | solution.py:437
  52.1 87.6 %all-gather.3.cloned.1.call-start = ((), (), s32[]{:S(2)}) async-start(), calls=%async_computation.3 | async-start | bytes 4718592 | tf_op jit(solution)/shard_map/all_gather | solution.py:443
  52.1 17.9 %collective-permute-start.1 = (bf16[128,1024]{1,0:T(8,128)(2,1)S(1)}, bf16[128,1024]{1,0:T(8,128)(2,1)S(1)}, u32[]{:S(2)}, u32[]{:S(2)}) collective-permute-start(bf16[128,1024]{1,0:T(8,128)(2,1)S(1)} %get-tuple-element.27.refs_0_), channel_id=1, source_target_pairs={{0,1},{1,0},{2,3},{3,2},{4,5},{5,4},{6,7},{7,6},{8,9},{9,8},{10,11... | collective-permute-start | bytes 786440 | tf_op jit(solution)/shard_map/ppermute | solution.py:133
  52.7 22.6 %collective-permute-start.4 = (bf16[128,1024]{1,0:T(8,128)(2,1)S(1)}, bf16[128,1024]{1,0:T(8,128)(2,1)S(1)}, u32[]{:S(2)}, u32[]{:S(2)}) collective-permute-start(bf16[128,1024]{1,0:T(8,128)(2,1)S(1)} %get-tuple-element.46), channel_id=1, source_target_pairs={{0,16},{2,18},{4,20},{6,22},{8,24},{10,26},{12,28},{14,30},{16,0},... | collective-permute-start | bytes 786440 | tf_op jit(solution)/shard_map/ppermute | solution.py:124
  55.1 22.2 %collective-permute-start.6 = (bf16[128,1024]{1,0:T(8,128)(2,1)S(1)}, bf16[128,1024]{1,0:T(8,128)(2,1)S(1)}, u32[]{:S(2)}, u32[]{:S(2)}) collective-permute-start(bf16[128,1024]{1,0:T(8,128)(2,1)S(1)} %get-tuple-element.45), channel_id=1, source_target_pairs={{0,24},{2,26},{4,28},{6,30},{8,0},{10,2},{12,4},{14,6},{16,8},{18,... | collective-permute-start | bytes 786440 | tf_op jit(solution)/shard_map/ppermute | solution.py:124
  70.1 7.8 %collective-permute-start.3 = (bf16[128,1024]{1,0:T(8,128)(2,1)S(1)}, bf16[128,1024]{1,0:T(8,128)(2,1)S(1)}, u32[]{:S(2)}, u32[]{:S(2)}) collective-permute-start(bf16[128,1024]{1,0:T(8,128)(2,1)S(1)} %collective-permute-done.2.refs_2_), channel_id=1, source_target_pairs={{0,1},{1,0},{2,3},{3,2},{4,5},{5,4},{6,7},{7,6},{8,9},{9,8},{10,11... | collective-permute-start | bytes 786440 | tf_op jit(solution)/shard_map/ppermute | solution.py:133
  75.3 9.2 %collective-permute-start.5 = (bf16[128,1024]{1,0:T(8,128)(2,1)S(1)}, bf16[128,1024]{1,0:T(8,128)(2,1)S(1)}, u32[]{:S(2)}, u32[]{:S(2)}) collective-permute-start(bf16[128,1024]{1,0:T(8,128)(2,1)S(1)} %collective-permute-done.4.refs_4_), channel_id=1, source_target_pairs={{0,1},{1,0},{2,3},{3,2},{4,5},{5,4},{6,7},{7,6},{8,9},{9,8},{10,11... | collective-permute-start | bytes 786440 | tf_op jit(solution)/shard_map/ppermute | solution.py:133
  77.2 11.7 %collective-permute-start.7 = (bf16[128,1024]{1,0:T(8,128)(2,1)S(1)}, bf16[128,1024]{1,0:T(8,128)(2,1)S(1)}, u32[]{:S(2)}, u32[]{:S(2)}) collective-permute-start(bf16[128,1024]{1,0:T(8,128)(2,1)S(1)} %collective-permute-done.6.refs_6_), channel_id=1, source_target_pairs={{0,1},{1,0},{2,3},{3,2},{4,5},{5,4},{6,7},{7,6},{8,9},{9,8},{10,11... | collective-permute-start | bytes 786440 | tf_op jit(solution)/shard_map/ppermute | solution.py:133
  95.3 44.3 %copy-start.2 = (f32[256,256]{1,0:T(8,128)S(1)}, f32[256,256]{1,0:T(8,128)}, u32[]{:S(2)}) copy-start(f32[256,256]{1,0:T(8,128)} %constant.234.clone.refs_5_) | copy-start | bytes 786436
  95.4 44.3 %copy-start.3 = (f32[128,256]{1,0:T(8,128)S(1)}, f32[128,256]{1,0:T(8,128)}, u32[]{:S(2)}) copy-start(f32[128,256]{1,0:T(8,128)} %constant.233.clone.refs_4_) | copy-start | bytes 393220
  143.4 18.8 %all-to-all-start.2 = ((bf16[32,32,256]{2,1,0:T(8,128)(2,1)}), bf16[32,32,256]{2,1,0:T(8,128)(2,1)S(1)}, u32[]{:S(2)}, u32[]{:S(2)}) async-start(bf16[32,32,256]{2,1,0:T(8,128)(2,1)} %bitcast.23), calls=%async_computation.2 | async-start | bytes 1048576 | tf_op jit(solution)/shard_map/all_to_all | solution.py:452
  162.3 2.2 %copy-start.1 = (bf16[4096,512]{1,0:T(8,128)(2,1)S(1)}, bf16[4096,512]{1,0:T(8,128)(2,1)}, u32[]{:S(2)}) copy-start(bf16[4096,512]{1,0:T(8,128)(2,1)} %all-gather.3.cloned.1.call-done) | copy-start | bytes 12582916
  167.1 12.1 %collective-permute-start.11 = (bf16[64,2048]{1,0:T(8,128)(2,1)S(1)}, bf16[64,2048]{1,0:T(8,128)(2,1)S(1)}, u32[]{:S(2)}, u32[]{:S(2)}) collective-permute-start(bf16[64,2048]{1,0:T(8,128)(2,1)S(1)} %get-tuple-element.41), channel_id=1, source_target_pairs={{0,0},{1,16},{2,2},{3,18},{4,4},{5,20},{6,6},{7,22},{8,24},{9,8},{... | collective-permute-start | bytes 786440 | tf_op jit(solution)/shard_map/ppermute | solution.py:88
  169.7 25.9 %collective-permute-start.12 = (bf16[64,2048]{1,0:T(8,128)(2,1)S(1)}, bf16[64,2048]{1,0:T(8,128)(2,1)S(1)}, u32[]{:S(2)}, u32[]{:S(2)}) collective-permute-start(bf16[64,2048]{1,0:T(8,128)(2,1)S(1)} %get-tuple-element.42), channel_id=1, source_target_pairs={{0,8},{1,24},{2,10},{3,26},{4,12},{5,28},{6,14},{7,30},{8,16},{9,0... | collective-permute-start | bytes 786440 | tf_op jit(solution)/shard_map/ppermute | solution.py:88
  169.8 25.8 %collective-permute-start.13 = (bf16[64,2048]{1,0:T(8,128)(2,1)S(1)}, bf16[64,2048]{1,0:T(8,128)(2,1)S(1)}, u32[]{:S(2)}, u32[]{:S(2)}) collective-permute-start(bf16[64,2048]{1,0:T(8,128)(2,1)S(1)} %get-tuple-element.43), channel_id=1, source_target_pairs={{0,16},{1,0},{2,18},{3,2},{4,20},{5,4},{6,22},{7,6},{8,8},{9,24},{... | collective-permute-start | bytes 786440 | tf_op jit(solution)/shard_map/ppermute | solution.py:88
  173.7 22.0 %collective-permute-start.14 = (bf16[64,2048]{1,0:T(8,128)(2,1)S(1)}, bf16[64,2048]{1,0:T(8,128)(2,1)S(1)}, u32[]{:S(2)}, u32[]{:S(2)}) collective-permute-start(bf16[64,2048]{1,0:T(8,128)(2,1)S(1)} %get-tuple-element.44), channel_id=1, source_target_pairs={{0,24},{1,8},{2,26},{3,10},{4,28},{5,12},{6,30},{7,14},{8,0},{9,16... | collective-permute-start | bytes 786440 | tf_op jit(solution)/shard_map/ppermute | solution.py:88
Sparse Core Ops, SparseCore 0:
  89.1 50.5 all-gather.2

commit v14 on v8

--- a/solution.py
+++ b/solution.py
@@ -22,26 +22,28 @@
 
 
 def assemble_kernel(place_ref, *refs):
-    *piece_refs, out_ref = refs
+    *piece_refs, out_ref, sems = refs
+    part_rows, width = piece_refs[0].shape
+    copies = []
     for index, piece_ref in enumerate(piece_refs):
-
-        @pl.when(pl.program_id(0) == index)
-        def _():
-            out_ref[...] = piece_ref[...]
+        row = pl.multiple_of(place_ref[2 * index] * part_rows, part_rows)
+        column = pl.multiple_of(place_ref[2 * index + 1] * width, width)
+        target = out_ref.at[pl.ds(row, part_rows), pl.ds(column, width)]
+        copies.append(pltpu.make_async_copy(piece_ref, target, sems.at[index]))
+    for copy in copies:
+        copy.start()
+    for copy in copies:
+        copy.wait()
 
 
 def assemble(pieces, places, shape):
     return pl.pallas_call(
         assemble_kernel,
-        grid_spec=pltpu.PrefetchScalarGridSpec(
-            num_scalar_prefetch=1,
-            grid=(len(pieces),),
-            in_specs=[pl.BlockSpec(memory_space=pltpu.VMEM)] * len(pieces),
-            out_specs=pl.BlockSpec(
-                pieces[0].shape, lambda i, place: (place[2 * i], place[2 * i + 1])
-            ),
-        ),
+        in_specs=[pl.BlockSpec(memory_space=pltpu.SMEM)]
+        + [pl.BlockSpec(memory_space=pltpu.VMEM)] * len(pieces),
+        out_specs=pl.BlockSpec(memory_space=pl.ANY),
         out_shape=jax.ShapeDtypeStruct(shape, pieces[0].dtype),
+        scratch_shapes=[pltpu.SemaphoreType.DMA((len(pieces),))],
         compiler_params=pltpu.CompilerParams(vmem_limit_bytes=4 * 2**20),
         cost_estimate=pl.CostEstimate(
             flops=0, bytes_accessed=4 * shape[0] * shape[1], transcendentals=0
@@ -112,16 +114,18 @@
     seq_parts = outer * inner_parts
     tp_place = lax.axis_index("tp")
     outer_place = lax.axis_index("seq") // inner_parts
-    arrived = []
-    for step in range(outer):
+    arrived = {}
+    for step in sorted(range(outer), key=lambda step: min(step, outer - step)):
+        if step not in (0, 1, outer - 1):
+            arrived[1], held = lax.optimization_barrier((arrived[1], held))
         target = (outer_place + step) % outer
         which = (tp_place - target // per_tp + tp_parts) % tp_parts * per_tp + target % per_tp
         piece = lax.dynamic_index_in_dim(held, which, axis=0, keepdims=False)
         if step:
             far = step * inner_parts
             piece = lax.ppermute(piece, "seq", [(i, (i + far) % seq_parts) for i in range(seq_parts)])
-        arrived.append(piece)
-    return arrived
+        arrived[step] = piece
+    return [arrived[step] for step in range(outer)]
 
 
 def share_over_tp(part, tp_parts):
@@ -409,13 +413,13 @@
     taps = jnp.broadcast_to(taps[..., None], taps.shape + (rows,))
     skip = lax.dynamic_slice_in_dim(skip_gain, position * chans, chans, axis=0)
     skip = jnp.broadcast_to(skip[:, None], (chans, rows))
-    filter_blocks = long_filter.T.reshape(seq_parts, chans, rows)
+    filter_blocks = lax.all_to_all(
+        long_filter.T.reshape(seq_parts, chans, rows), "seq", split_axis=0, concat_axis=0, tiled=True
+    )
 
     held = share_columns(features, outer, tp_parts)
     held, taps, skip, filter_blocks = lax.optimization_barrier((held, taps, skip, filter_blocks))
     arrived = cross_outer(held, outer, inner_parts, tp_parts)
-    arrived[-1], filter_blocks = lax.optimization_barrier((arrived[-1], filter_blocks))
-    filter_blocks = lax.all_to_all(filter_blocks, "seq", split_axis=0, concat_axis=0, tiled=True)
     chunks = [share_over_tp(piece, tp_parts) for piece in arrived]
     chunks, out_proj = lax.optimization_barrier((chunks, out_proj))
     out_weight = lax.all_gather(out_proj, ("seq", "tp"), axis_index_groups=tp_groups)

time: 187 us -> 175 us (0.936)
  blocking collectives: 42.3 us -> 0 us
  waiting for transfers between devices: 80.8 us -> 102 us
  starting transfers between devices: 27.7 us -> 37 us
    all_to_all x1 -> x0, blocking collectives: 42.3 us -> none  [per_device(): lax.all_to_all(partial, 'seq', split_axis=0, concat_axis=0, tiled=True)]
    all_gather x1, waiting for transfers between devices: 0.01 us -> 31.8 us  [per_device(): lax.all_gather(out_proj, ('seq', 'tp'), axis_index_groups=tp_groups)]
    all_to_all x1 -> x2, starting transfers between devices: 5 us -> 12.8 us  [the longest x1 6.56 us: per_device(): lax.all_to_all(partial, 'seq', split_axis=0, concat_axis=0, tiled=True)]
    ppermute x1, waiting for transfers between devices: 11.3 us -> 4.73 us  [share_columns(): lax.ppermute(piece, 'tp', [(i, (i + step) % tp_parts) for i in range(tp_p...]
    all_to_all x1 -> x2, waiting for transfers between devices: 8.13 us -> 5.38 us  [the longest x1 3.16 us: per_device(): lax.all_to_all(partial, 'seq', split_axis=0, concat_axis=0, tiled=True)]
    ppermute x4, waiting for transfers between devices: 10.4 us -> 8.48 us  [share_over_tp(): pieces.append(lax.ppermute(part, 'tp', pairs))]
  transfers between devices with their start and end apart: 16 -> 17, of which waited for: 10 -> 12; matrix products, arithmetic and copies ran while one was open for 1% -> 1% of each run, Pallas kernels for 4% -> 4%
where the time goes in v14:
time: 175 us; the launch traced here: 174 us
  waiting for transfers between devices  102 us (58%)
  starting transfers between devices  37 us (21%)
  Pallas kernels  15.3 us (9%)
  between operations  13.9 us (8%)
  local copies, waits for them, and re-layouts  5.6 us (3%)
    all_gather x1, waiting for transfers between devices, per_device(): lax.all_gather(out_proj, ('seq', 'tp'), axis_index_groups=tp_groups)  31.8 us
    ppermute x4, waiting for transfers between devices, return_output(): arrived.append(lax.ppermute(piece, ('seq', 'tp'), pairs))  19.5 us
    ppermute x3, waiting for transfers between devices, cross_outer(): lax.ppermute(piece, 'seq', [(i, (i + far) % seq_parts) for i in range(seq...  17.3 us
    all_to_all x1, waiting for transfers between devices, per_device(): lax.all_to_all(gated.reshape((-1,) + gated.shape[3:]), ('tp', 'seq'), spl...  14.4 us
    ppermute x4, starting transfers between devices, return_output(): arrived.append(lax.ppermute(piece, ('seq', 'tp'), pairs))  8.85 us
    ppermute x4, waiting for transfers between devices, share_over_tp(): pieces.append(lax.ppermute(part, 'tp', pairs))  8.48 us
    pallas_call x1, Pallas kernels, project_in(): pl.pallas_call(functools.partial(project_kernel, tp_parts), grid_spec=plt...  7.41 us
    all_to_all x1, starting transfers between devices, per_device(): lax.all_to_all(partial, 'seq', split_axis=0, concat_axis=0, tiled=True)  6.56 us
  transfers between devices with their start and end apart: 17, of which 12 were waited for; matrix products, arithmetic and copies ran while one was open for 1% of the time, Pallas kernels for 4%

profile of v14, /device:TPU:12, one launch (start us, length us, event | category | flops | bytes accessed | tf_op | source)
XLA Modules:
  0.0 174.4 jit_solution(14064356289907269229)
XLA Ops:
  9.6 6.3 %all-to-all-start = ((f32[16,32,128]{2,1,0:T(8,128)}), f32[16,32,128]{2,1,0:T(8,128)S(1)}, u32[]{:S(2)}, u32[]{:S(2)}) async-start(f32[16,32,128]{2,1,0:T(8,128)} %bitcast.16), calls=%async_computation | async-start | bytes 524288 | tf_op jit(solution)/shard_map/all_to_all | solution.py:416
  16.9 4.7 %collective-permute-done = bf16[2,128,1024]{2,1,0:T(8,128)(2,1)S(1)} collective-permute-done((bf16[2,128,1024]{2,1,0:T(8,128)(2,1)S(1)}, bf16[2,128,1024]{2,1,0:T(8,128)(2,1)S(1)}, u32[]{:S(2)}, u32[]{:S(2)}) %collective-permute-start) | collective-permute-done | bytes 524320 | tf_op jit(solution)/shard_map/ppermute | solution.py:107
  21.8 2.2 %all-to-all-done.refs_1_ = f32[16,32,128]{2,1,0:T(8,128)S(1)} async-done(((f32[16,32,128]{2,1,0:T(8,128)}), f32[16,32,128]{2,1,0:T(8,128)S(1)}, u32[]{:S(2)}, u32[]{:S(2)}) %all-to-all-start) | async-done | bytes 262176 | tf_op jit(solution)/shard_map/all_to_all | solution.py:416
  24.2 1.7 collective-permute-start.2
  26.5 7.0 %collective-permute-done.2.refs_2_ = bf16[128,1024]{1,0:T(8,128)(2,1)S(1)} collective-permute-done((bf16[128,1024]{1,0:T(8,128)(2,1)S(1)}, bf16[128,1024]{1,0:T(8,128)(2,1)S(1)}, u32[]{:S(2)}, u32[]{:S(2)}) %collective-permute-start.2) | collective-permute-done | bytes 262176 | tf_op jit(solution)/shard_map/ppermute | solution.py:126
  33.5 2.0 %collective-permute-start.4 = (bf16[128,1024]{1,0:T(8,128)(2,1)S(1)}, bf16[128,1024]{1,0:T(8,128)(2,1)S(1)}, u32[]{:S(2)}, u32[]{:S(2)}) collective-permute-start(bf16[128,1024]{1,0:T(8,128)(2,1)S(1)} %dynamic-slice_bitcast_fusion.1), channel_id=1, source_target_pairs={{0,16},{2,18},{4,20},{6,22},{8,24},{10,26},{12,28},{14,30},{16,0},... | collective-permute-start | bytes 786440 | tf_op jit(solution)/shard_map/ppermute | solution.py:126
  37.5 8.6 %collective-permute-done.6.refs_6_ = bf16[128,1024]{1,0:T(8,128)(2,1)S(1)} collective-permute-done((bf16[128,1024]{1,0:T(8,128)(2,1)S(1)}, bf16[128,1024]{1,0:T(8,128)(2,1)S(1)}, u32[]{:S(2)}, u32[]{:S(2)}) %collective-permute-start.6) | collective-permute-done | bytes 262176 | tf_op jit(solution)/shard_map/ppermute | solution.py:126
  47.4 1.7 collective-permute-done.4.refs_4_
  50.4 4.4 %collective-permute-done.7.refs_7_ = bf16[128,1024]{1,0:T(8,128)(2,1)S(1)} collective-permute-done((bf16[128,1024]{1,0:T(8,128)(2,1)S(1)}, bf16[128,1024]{1,0:T(8,128)(2,1)S(1)}, u32[]{:S(2)}, u32[]{:S(2)}) %collective-permute-start.7) | collective-permute-done | bytes 262176 | tf_op jit(solution)/shard_map/ppermute | solution.py:135
  54.8 4.1 %collective-permute-done.5.refs_5_ = bf16[128,1024]{1,0:T(8,128)(2,1)S(1)} collective-permute-done((bf16[128,1024]{1,0:T(8,128)(2,1)S(1)}, bf16[128,1024]{1,0:T(8,128)(2,1)S(1)}, u32[]{:S(2)}, u32[]{:S(2)}) %collective-permute-start.5) | collective-permute-done | bytes 262176 | tf_op jit(solution)/shard_map/ppermute | solution.py:135
  59.6 7.4 %shard_map.82 = bf16[16,3,32,512]{3,2,1,0:T(8,128)(2,1)} custom-call(s32[1]{0:T(128)} %bitcast.10.place_ref, bf16[128,1024]{1,0:T(8,128)(2,1)} %copy-done.5, bf16[128,1024]{1,0:T(8,128)(2,1)} %copy-done.10, bf16[128,1024]{1,0:T(8,128)(2,1)} %copy-done.7, bf16[128,1024]{1,0:T(8,128)(2,1)} %copy-done.11, bf16[128,1024]{1,0:T(8,128)(2,1)} %copy-done.9, ...), custom_call_target="tpu_custom_call" | custom-call | flops 96636764160 | bytes 9961472 | tf_op jit(solution)/shard_map/pallas_call | solution.py:161
  67.0 6.6 %all-to-all-start.1 = ((bf16[16,3,32,512]{3,2,1,0:T(8,128)(2,1)}), bf16[16,3,32,512]{3,2,1,0:T(8,128)(2,1)S(1)}, u32[]{:S(2)}, u32[]{:S(2)}) async-start(bf16[16,3,32,512]{3,2,1,0:T(8,128)(2,1)} %shard_map.82), calls=%async_computation.1 | async-start | bytes 3145728 | tf_op jit(solution)/shard_map/all_to_all | solution.py:429
  73.6 31.8 %all-gather.6.cloned.1.call-done = bf16[4096,512]{1,0:T(8,128)(2,1)} async-done(((bf16[512,512]{1,0:T(8,128)(2,1)}), bf16[4096,512]{1,0:T(8,128)(2,1)}) %all-gather.6.cloned.1.call-update) | async-done | bytes 4194320 | tf_op jit(solution)/shard_map/all_gather | solution.py:425
  105.3 3.2 %all-to-all-done.1.refs_0_ = bf16[16,3,32,512]{3,2,1,0:T(8,128)(2,1)S(1)} async-done(((bf16[16,3,32,512]{3,2,1,0:T(8,128)(2,1)}), bf16[16,3,32,512]{3,2,1,0:T(8,128)(2,1)S(1)}, u32[]{:S(2)}, u32[]{:S(2)}) %all-to-all-start.1) | async-done | bytes 1572896 | tf_op jit(solution)/shard_map/all_to_all | solution.py:429
  108.5 3.7 %shard_map.83 = bf16[2,4,4,32,256]{4,3,2,1,0:T(8,128)(2,1)} custom-call(bf16[16,3,32,512]{3,2,1,0:T(8,128)(2,1)S(1)} %all-to-all-done.1.refs_0_, f32[16,32,128]{2,1,0:T(8,128)S(1)} %all-to-all-done.refs_1_, f32[3,3,32,128]{3,2,1,0:T(8,128)S(1)} %broadcast_in_dim.7.refs_2_, f32[32,128]{1,0:T(8,128)S(1)} %broadcast_in_dim.8.refs_3_, f32[128,256]{1,0:T(8,128)S(1)} %copy-done.3, ...), custom_call_target="tpu_custom_call" | custom-call | flops 1000000000 | bytes 4194304 | tf_op jit(solution)/shard_map/pallas_call | solution.py:325
  112.2 5.9 %all-to-all-start.2 = ((bf16[32,32,256]{2,1,0:T(8,128)(2,1)}), bf16[32,32,256]{2,1,0:T(8,128)(2,1)S(1)}, u32[]{:S(2)}, u32[]{:S(2)}) async-start(bf16[32,32,256]{2,1,0:T(8,128)(2,1)} %bitcast.23), calls=%async_computation.2 | async-start | bytes 1048576 | tf_op jit(solution)/shard_map/all_to_all | solution.py:434
  118.3 14.4 %all-to-all-done.2 = bf16[32,32,256]{2,1,0:T(8,128)(2,1)S(1)} async-done(((bf16[32,32,256]{2,1,0:T(8,128)(2,1)}), bf16[32,32,256]{2,1,0:T(8,128)(2,1)S(1)}, u32[]{:S(2)}, u32[]{:S(2)}) %all-to-all-start.2) | async-done | bytes 524320 | tf_op jit(solution)/shard_map/all_to_all | solution.py:434
  132.7 2.2 %copy-done.1 = bf16[4096,512]{1,0:T(8,128)(2,1)S(1)} copy-done((bf16[4096,512]{1,0:T(8,128)(2,1)S(1)}, bf16[4096,512]{1,0:T(8,128)(2,1)}, u32[]{:S(2)}) %copy-start.1) | copy-done | bytes 4194328
  134.9 2.6 %shard_map.84 = (bf16[64,2048]{1,0:T(8,128)(2,1)S(1)}, bf16[64,2048]{1,0:T(8,128)(2,1)S(1)}, bf16[64,2048]{1,0:T(8,128)(2,1)S(1)}, bf16[64,2048]{1,0:T(8,128)(2,1)S(1)}) custom-call(s32[4]{0:T(128)S(1)} %pad_add_fusion.block_ref, bf16[2,512,256]{2,1,0:T(8,128)(2,1)S(1)} %bitcast.34, bf16[4,2,512,512]{3,2,1,0:T(8,128)(2,1)S(1)} %bitcast.33), custom_call_target="tpu_custom_call" | custom-call | flops 1073741824 | bytes 5767168 | tf_op jit(solution)/shard_map/pallas_call | solution.py:371
  137.5 2.6 %collective-permute-start.8 = (bf16[64,2048]{1,0:T(8,128)(2,1)S(1)}, bf16[64,2048]{1,0:T(8,128)(2,1)S(1)}, u32[]{:S(2)}, u32[]{:S(2)}) collective-permute-start(bf16[64,2048]{1,0:T(8,128)(2,1)S(1)} %get-tuple-element.43), channel_id=1, source_target_pairs={{0,0},{1,16},{2,2},{3,18},{4,4},{5,20},{6,6},{7,22},{8,24},{9,8},{... | collective-permute-start | bytes 786440 | tf_op jit(solution)/shard_map/ppermute | solution.py:88
  140.2 3.9 %collective-permute-start.10 = (bf16[64,2048]{1,0:T(8,128)(2,1)S(1)}, bf16[64,2048]{1,0:T(8,128)(2,1)S(1)}, u32[]{:S(2)}, u32[]{:S(2)}) collective-permute-start(bf16[64,2048]{1,0:T(8,128)(2,1)S(1)} %get-tuple-element.45), channel_id=1, source_target_pairs={{0,16},{1,0},{2,18},{3,2},{4,20},{5,4},{6,22},{7,6},{8,8},{9,24},{... | collective-permute-start | bytes 786440 | tf_op jit(solution)/shard_map/ppermute | solution.py:88
  144.1 2.3 %collective-permute-start.11 = (bf16[64,2048]{1,0:T(8,128)(2,1)S(1)}, bf16[64,2048]{1,0:T(8,128)(2,1)S(1)}, u32[]{:S(2)}, u32[]{:S(2)}) collective-permute-start(bf16[64,2048]{1,0:T(8,128)(2,1)S(1)} %get-tuple-element.46), channel_id=1, source_target_pairs={{0,24},{1,8},{2,26},{3,10},{4,28},{5,12},{6,30},{7,14},{8,0},{9,16... | collective-permute-start | bytes 786440 | tf_op jit(solution)/shard_map/ppermute | solution.py:88
  146.5 3.2 %collective-permute-done.8.refs_0_ = bf16[64,2048]{1,0:T(8,128)(2,1)S(1)} collective-permute-done((bf16[64,2048]{1,0:T(8,128)(2,1)S(1)}, bf16[64,2048]{1,0:T(8,128)(2,1)S(1)}, u32[]{:S(2)}, u32[]{:S(2)}) %collective-permute-start.8) | collective-permute-done | bytes 262176 | tf_op jit(solution)/shard_map/ppermute | solution.py:88
  149.6 16.4 %collective-permute-done.9.refs_1_ = bf16[64,2048]{1,0:T(8,128)(2,1)S(1)} collective-permute-done((bf16[64,2048]{1,0:T(8,128)(2,1)S(1)}, bf16[64,2048]{1,0:T(8,128)(2,1)S(1)}, u32[]{:S(2)}, u32[]{:S(2)}) %collective-permute-start.9) | collective-permute-done | bytes 262176 | tf_op jit(solution)/shard_map/ppermute | solution.py:88
  (56 shorter events, 11.8 us)
Async XLA Ops:
  6.5 10.3 %copy-start = (f32[3,3,512]{2,1,0:T(4,128)S(1)}, f32[3,3,512]{2,1,0:T(4,128)}, u32[]{:S(2)}) copy-start(f32[3,3,512]{2,1,0:T(4,128)} %param.10) | copy-start | bytes 55300
  6.5 52.4 %all-gather.4.cloned.1.call-start = ((), (), s32[]{:S(2)}) async-start(), calls=%async_computation.3 | async-start | bytes 7864320 | tf_op jit(solution)/shard_map/all_gather | solution.py:410
  7.9 13.7 %collective-permute-start = (bf16[2,128,1024]{2,1,0:T(8,128)(2,1)S(1)}, bf16[2,128,1024]{2,1,0:T(8,128)(2,1)S(1)}, u32[]{:S(2)}, u32[]{:S(2)}) collective-permute-start(bf16[2,128,1024]{2,1,0:T(8,128)(2,1)S(1)} %pad_maximum_fusion.1), channel_id=1, source_target_pairs={{0,1},{1,0},{2,3},{3,2},{4,5},{5,4},{6,7},{7,6},{8,9},{9,8},{10,11... | collective-permute-start | bytes 1572872 | tf_op jit(solution)/shard_map/ppermute | solution.py:107
  9.6 14.4 %all-to-all-start = ((f32[16,32,128]{2,1,0:T(8,128)}), f32[16,32,128]{2,1,0:T(8,128)S(1)}, u32[]{:S(2)}, u32[]{:S(2)}) async-start(f32[16,32,128]{2,1,0:T(8,128)} %bitcast.16), calls=%async_computation | async-start | bytes 524288 | tf_op jit(solution)/shard_map/all_to_all | solution.py:416
  15.8 89.5 %all-gather.6.cloned.1.call-start = ((), (), s32[]{:S(2)}) async-start(), calls=%async_computation.4 | async-start | bytes 4718592 | tf_op jit(solution)/shard_map/all_gather | solution.py:425
  24.2 34.7 %copy-start.5 = (bf16[128,1024]{1,0:T(8,128)(2,1)}, bf16[128,1024]{1,0:T(8,128)(2,1)S(1)}, u32[]{:S(2)}) copy-start(bf16[128,1024]{1,0:T(8,128)(2,1)S(1)} %get-tuple-element.29.refs_0_) | copy-start | bytes 786436
  24.2 9.2 %collective-permute-start.2 = (bf16[128,1024]{1,0:T(8,128)(2,1)S(1)}, bf16[128,1024]{1,0:T(8,128)(2,1)S(1)}, u32[]{:S(2)}, u32[]{:S(2)}) collective-permute-start(bf16[128,1024]{1,0:T(8,128)(2,1)S(1)} %get-tuple-element.48), channel_id=1, source_target_pairs={{0,8},{2,10},{4,12},{6,14},{8,16},{10,18},{12,20},{14,22},{16,24},... | collective-permute-start | bytes 786440 | tf_op jit(solution)/shard_map/ppermute | solution.py:126
  25.9 20.2 %collective-permute-start.6 = (bf16[128,1024]{1,0:T(8,128)(2,1)S(1)}, bf16[128,1024]{1,0:T(8,128)(2,1)S(1)}, u32[]{:S(2)}, u32[]{:S(2)}) collective-permute-start(bf16[128,1024]{1,0:T(8,128)(2,1)S(1)} %get-tuple-element.47), channel_id=1, source_target_pairs={{0,24},{2,26},{4,28},{6,30},{8,0},{10,2},{12,4},{14,6},{16,8},{18,... | collective-permute-start | bytes 786440 | tf_op jit(solution)/shard_map/ppermute | solution.py:126
  33.5 25.5 %copy-start.7 = (bf16[128,1024]{1,0:T(8,128)(2,1)}, bf16[128,1024]{1,0:T(8,128)(2,1)S(1)}, u32[]{:S(2)}) copy-start(bf16[128,1024]{1,0:T(8,128)(2,1)S(1)} %collective-permute-done.2.refs_2_) | copy-start | bytes 786436
  33.5 15.6 %collective-permute-start.4 = (bf16[128,1024]{1,0:T(8,128)(2,1)S(1)}, bf16[128,1024]{1,0:T(8,128)(2,1)S(1)}, u32[]{:S(2)}, u32[]{:S(2)}) collective-permute-start(bf16[128,1024]{1,0:T(8,128)(2,1)S(1)} %dynamic-slice_bitcast_fusion.1), channel_id=1, source_target_pairs={{0,16},{2,18},{4,20},{6,22},{8,24},{10,26},{12,28},{14,30},{16,0},... | collective-permute-start | bytes 786440 | tf_op jit(solution)/shard_map/ppermute | solution.py:126
  35.5 14.9 %collective-permute-start.1 = (bf16[128,1024]{1,0:T(8,128)(2,1)S(1)}, bf16[128,1024]{1,0:T(8,128)(2,1)S(1)}, u32[]{:S(2)}, u32[]{:S(2)}) collective-permute-start(bf16[128,1024]{1,0:T(8,128)(2,1)S(1)} %get-tuple-element.29.refs_0_), channel_id=1, source_target_pairs={{0,1},{1,0},{2,3},{3,2},{4,5},{5,4},{6,7},{7,6},{8,9},{9,8},{10,11... | collective-permute-start | bytes 786440 | tf_op jit(solution)/shard_map/ppermute | solution.py:135
  36.8 18.0 %collective-permute-start.3 = (bf16[128,1024]{1,0:T(8,128)(2,1)S(1)}, bf16[128,1024]{1,0:T(8,128)(2,1)S(1)}, u32[]{:S(2)}, u32[]{:S(2)}) collective-permute-start(bf16[128,1024]{1,0:T(8,128)(2,1)S(1)} %collective-permute-done.2.refs_2_), channel_id=1, source_target_pairs={{0,1},{1,0},{2,3},{3,2},{4,5},{5,4},{6,7},{7,6},{8,9},{9,8},{10,11... | collective-permute-start | bytes 786440 | tf_op jit(solution)/shard_map/ppermute | solution.py:135
  46.1 12.9 %copy-start.8 = (bf16[128,1024]{1,0:T(8,128)(2,1)}, bf16[128,1024]{1,0:T(8,128)(2,1)S(1)}, u32[]{:S(2)}) copy-start(bf16[128,1024]{1,0:T(8,128)(2,1)S(1)} %collective-permute-done.6.refs_6_) | copy-start | bytes 786436
  46.1 8.7 %collective-permute-start.7 = (bf16[128,1024]{1,0:T(8,128)(2,1)S(1)}, bf16[128,1024]{1,0:T(8,128)(2,1)S(1)}, u32[]{:S(2)}, u32[]{:S(2)}) collective-permute-start(bf16[128,1024]{1,0:T(8,128)(2,1)S(1)} %collective-permute-done.6.refs_6_), channel_id=1, source_target_pairs={{0,1},{1,0},{2,3},{3,2},{4,5},{5,4},{6,7},{7,6},{8,9},{9,8},{10,11... | collective-permute-start | bytes 786440 | tf_op jit(solution)/shard_map/ppermute | solution.py:135
  49.1 9.9 %copy-start.9 = (bf16[128,1024]{1,0:T(8,128)(2,1)}, bf16[128,1024]{1,0:T(8,128)(2,1)S(1)}, u32[]{:S(2)}) copy-start(bf16[128,1024]{1,0:T(8,128)(2,1)S(1)} %collective-permute-done.4.refs_4_) | copy-start | bytes 786436
  49.1 9.8 %collective-permute-start.5 = (bf16[128,1024]{1,0:T(8,128)(2,1)S(1)}, bf16[128,1024]{1,0:T(8,128)(2,1)S(1)}, u32[]{:S(2)}, u32[]{:S(2)}) collective-permute-start(bf16[128,1024]{1,0:T(8,128)(2,1)S(1)} %collective-permute-done.4.refs_4_), channel_id=1, source_target_pairs={{0,1},{1,0},{2,3},{3,2},{4,5},{5,4},{6,7},{7,6},{8,9},{9,8},{10,11... | collective-permute-start | bytes 786440 | tf_op jit(solution)/shard_map/ppermute | solution.py:135
  67.0 41.5 %copy-start.2 = (f32[256,256]{1,0:T(8,128)S(1)}, f32[256,256]{1,0:T(8,128)}, u32[]{:S(2)}) copy-start(f32[256,256]{1,0:T(8,128)} %constant.230.clone.refs_5_) | copy-start | bytes 786436
  67.0 41.5 %copy-start.3 = (f32[128,256]{1,0:T(8,128)S(1)}, f32[128,256]{1,0:T(8,128)}, u32[]{:S(2)}) copy-start(f32[128,256]{1,0:T(8,128)} %constant.229.clone.refs_4_) | copy-start | bytes 393220
  67.0 41.5 %all-to-all-start.1 = ((bf16[16,3,32,512]{3,2,1,0:T(8,128)(2,1)}), bf16[16,3,32,512]{3,2,1,0:T(8,128)(2,1)S(1)}, u32[]{:S(2)}, u32[]{:S(2)}) async-start(bf16[16,3,32,512]{3,2,1,0:T(8,128)(2,1)} %shard_map.82), calls=%async_computation.1 | async-start | bytes 3145728 | tf_op jit(solution)/shard_map/all_to_all | solution.py:429
  112.2 20.4 %all-to-all-start.2 = ((bf16[32,32,256]{2,1,0:T(8,128)(2,1)}), bf16[32,32,256]{2,1,0:T(8,128)(2,1)S(1)}, u32[]{:S(2)}, u32[]{:S(2)}) async-start(bf16[32,32,256]{2,1,0:T(8,128)(2,1)} %bitcast.23), calls=%async_computation.2 | async-start | bytes 1048576 | tf_op jit(solution)/shard_map/all_to_all | solution.py:434
  137.5 12.1 %collective-permute-start.8 = (bf16[64,2048]{1,0:T(8,128)(2,1)S(1)}, bf16[64,2048]{1,0:T(8,128)(2,1)S(1)}, u32[]{:S(2)}, u32[]{:S(2)}) collective-permute-start(bf16[64,2048]{1,0:T(8,128)(2,1)S(1)} %get-tuple-element.43), channel_id=1, source_target_pairs={{0,0},{1,16},{2,2},{3,18},{4,4},{5,20},{6,6},{7,22},{8,24},{9,8},{... | collective-permute-start | bytes 786440 | tf_op jit(solution)/shard_map/ppermute | solution.py:88
  140.1 25.9 %collective-permute-start.9 = (bf16[64,2048]{1,0:T(8,128)(2,1)S(1)}, bf16[64,2048]{1,0:T(8,128)(2,1)S(1)}, u32[]{:S(2)}, u32[]{:S(2)}) collective-permute-start(bf16[64,2048]{1,0:T(8,128)(2,1)S(1)} %get-tuple-element.44), channel_id=1, source_target_pairs={{0,8},{1,24},{2,10},{3,26},{4,12},{5,28},{6,14},{7,30},{8,16},{9,0... | collective-permute-start | bytes 786440 | tf_op jit(solution)/shard_map/ppermute | solution.py:88
  140.2 25.8 %collective-permute-start.10 = (bf16[64,2048]{1,0:T(8,128)(2,1)S(1)}, bf16[64,2048]{1,0:T(8,128)(2,1)S(1)}, u32[]{:S(2)}, u32[]{:S(2)}) collective-permute-start(bf16[64,2048]{1,0:T(8,128)(2,1)S(1)} %get-tuple-element.45), channel_id=1, source_target_pairs={{0,16},{1,0},{2,18},{3,2},{4,20},{5,4},{6,22},{7,6},{8,8},{9,24},{... | collective-permute-start | bytes 786440 | tf_op jit(solution)/shard_map/ppermute | solution.py:88
  144.1 22.0 %collective-permute-start.11 = (bf16[64,2048]{1,0:T(8,128)(2,1)S(1)}, bf16[64,2048]{1,0:T(8,128)(2,1)S(1)}, u32[]{:S(2)}, u32[]{:S(2)}) collective-permute-start(bf16[64,2048]{1,0:T(8,128)(2,1)S(1)} %get-tuple-element.46), channel_id=1, source_target_pairs={{0,24},{1,8},{2,26},{3,10},{4,28},{5,12},{6,30},{7,14},{8,0},{9,16... | collective-permute-start | bytes 786440 | tf_op jit(solution)/shard_map/ppermute | solution.py:88
  (7 other events, 22.1 us)
Sparse Core Ops, SparseCore 0:
  8.9 48.8 all-gather.3
  59.7 45.5 all-gather.5

commit v15 on v14

--- a/solution.py
+++ b/solution.py
@@ -109,15 +109,13 @@
     return jnp.concatenate(held)
 
 
-def cross_outer(held, outer, inner_parts, tp_parts):
+def cross_outer(held, steps, outer, inner_parts, tp_parts):
     per_tp = outer // tp_parts
     seq_parts = outer * inner_parts
     tp_place = lax.axis_index("tp")
     outer_place = lax.axis_index("seq") // inner_parts
     arrived = {}
-    for step in sorted(range(outer), key=lambda step: min(step, outer - step)):
-        if step not in (0, 1, outer - 1):
-            arrived[1], held = lax.optimization_barrier((arrived[1], held))
+    for step in steps:
         target = (outer_place + step) % outer
         which = (tp_place - target // per_tp + tp_parts) % tp_parts * per_tp + target % per_tp
         piece = lax.dynamic_index_in_dim(held, which, axis=0, keepdims=False)
@@ -125,7 +123,7 @@
             far = step * inner_parts
             piece = lax.ppermute(piece, "seq", [(i, (i + far) % seq_parts) for i in range(seq_parts)])
         arrived[step] = piece
-    return [arrived[step] for step in range(outer)]
+    return arrived
 
 
 def share_over_tp(part, tp_parts):
@@ -419,8 +417,11 @@
 
     held = share_columns(features, outer, tp_parts)
     held, taps, skip, filter_blocks = lax.optimization_barrier((held, taps, skip, filter_blocks))
-    arrived = cross_outer(held, outer, inner_parts, tp_parts)
-    chunks = [share_over_tp(piece, tp_parts) for piece in arrived]
+    arrived = cross_outer(held, sorted({0, 1, outer - 1}), outer, inner_parts, tp_parts)
+    own = share_over_tp(arrived[0], tp_parts)
+    held, arrived[1], own = lax.optimization_barrier((held, arrived[1], own))
+    arrived |= cross_outer(held, range(2, outer - 1), outer, inner_parts, tp_parts)
+    chunks = [own] + [share_over_tp(arrived[step], tp_parts) for step in range(1, outer)]
     chunks, out_proj = lax.optimization_barrier((chunks, out_proj))
     out_weight = lax.all_gather(out_proj, ("seq", "tp"), axis_index_groups=tp_groups)
     out_weight = out_weight.reshape((inner_parts, tp_parts) + out_proj.shape)

time: 175 us -> 174 us (level)
  waiting for transfers between devices: 102 us -> 100 us
where the time goes in v15:
time: 174 us; the launch traced here: 173 us
  waiting for transfers between devices  100 us (57%)
  starting transfers between devices  38.1 us (22%)
  Pallas kernels  15.3 us (9%)
  between operations  13.9 us (8%)
  local copies, waits for them, and re-layouts  5.6 us (3%)
    all_gather x1, waiting for transfers between devices, per_device(): lax.all_gather(out_proj, ('seq', 'tp'), axis_index_groups=tp_groups)  31.9 us
    ppermute x4, waiting for transfers between devices, return_output(): arrived.append(lax.ppermute(piece, ('seq', 'tp'), pairs))  19.5 us
    ppermute x3, waiting for transfers between devices, cross_outer(): lax.ppermute(piece, 'seq', [(i, (i + far) % seq_parts) for i in range(seq...  15.8 us
    all_to_all x1, waiting for transfers between devices, per_device(): lax.all_to_all(gated.reshape((-1,) + gated.shape[3:]), ('tp', 'seq'), spl...  14.4 us
    ppermute x4, starting transfers between devices, return_output(): arrived.append(lax.ppermute(piece, ('seq', 'tp'), pairs))  8.85 us
    ppermute x4, waiting for transfers between devices, share_over_tp(): pieces.append(lax.ppermute(part, 'tp', pairs))  7.66 us
    pallas_call x1, Pallas kernels, project_in(): pl.pallas_call(functools.partial(project_kernel, tp_parts), grid_spec=plt...  7.41 us
    all_to_all x1, starting transfers between devices, per_device(): lax.all_to_all(long_filter.T.reshape(seq_parts, chans, rows), 'seq', spli...  6.27 us
  transfers between devices with their start and end apart: 17, of which 12 were waited for; matrix products, arithmetic and copies ran while one was open for 1% of the time, Pallas kernels for 4%

profile of v15, /device:TPU:12, one launch (start us, length us, event | category | flops | bytes accessed | tf_op | source)
XLA Modules:
  0.0 173.2 jit_solution(2030406552012799894)
XLA Ops:
  9.6 6.3 %all-to-all-start = ((f32[16,32,128]{2,1,0:T(8,128)}), f32[16,32,128]{2,1,0:T(8,128)S(1)}, u32[]{:S(2)}, u32[]{:S(2)}) async-start(f32[16,32,128]{2,1,0:T(8,128)} %bitcast.16), calls=%async_computation | async-start | bytes 524288 | tf_op jit(solution)/shard_map/all_to_all | solution.py:414
  16.9 4.7 %collective-permute-done = bf16[2,128,1024]{2,1,0:T(8,128)(2,1)S(1)} collective-permute-done((bf16[2,128,1024]{2,1,0:T(8,128)(2,1)S(1)}, bf16[2,128,1024]{2,1,0:T(8,128)(2,1)S(1)}, u32[]{:S(2)}, u32[]{:S(2)}) %collective-permute-start) | collective-permute-done | bytes 524320 | tf_op jit(solution)/shard_map/ppermute | solution.py:107
  21.8 2.2 %all-to-all-done.refs_1_ = f32[16,32,128]{2,1,0:T(8,128)S(1)} async-done(((f32[16,32,128]{2,1,0:T(8,128)}), f32[16,32,128]{2,1,0:T(8,128)S(1)}, u32[]{:S(2)}, u32[]{:S(2)}) %all-to-all-start) | async-done | bytes 262176 | tf_op jit(solution)/shard_map/all_to_all | solution.py:414
  24.2 1.7 collective-permute-start.1
  27.7 5.8 %collective-permute-done.1.refs_2_ = bf16[128,1024]{1,0:T(8,128)(2,1)S(1)} collective-permute-done((bf16[128,1024]{1,0:T(8,128)(2,1)S(1)}, bf16[128,1024]{1,0:T(8,128)(2,1)S(1)}, u32[]{:S(2)}, u32[]{:S(2)}) %collective-permute-start.1) | collective-permute-done | bytes 262176 | tf_op jit(solution)/shard_map/ppermute | solution.py:124
  33.5 3.0 %collective-permute-start.4 = (bf16[128,1024]{1,0:T(8,128)(2,1)S(1)}, bf16[128,1024]{1,0:T(8,128)(2,1)S(1)}, u32[]{:S(2)}, u32[]{:S(2)}) collective-permute-start(bf16[128,1024]{1,0:T(8,128)(2,1)S(1)} %dynamic-slice_bitcast_fusion.1), channel_id=1, source_target_pairs={{0,16},{2,18},{4,20},{6,22},{8,24},{10,26},{12,28},{14,30},{16,0},... | collective-permute-start | bytes 786440 | tf_op jit(solution)/shard_map/ppermute | solution.py:124
  37.8 8.3 %collective-permute-done.6.refs_6_ = bf16[128,1024]{1,0:T(8,128)(2,1)S(1)} collective-permute-done((bf16[128,1024]{1,0:T(8,128)(2,1)S(1)}, bf16[128,1024]{1,0:T(8,128)(2,1)S(1)}, u32[]{:S(2)}, u32[]{:S(2)}) %collective-permute-start.6) | collective-permute-done | bytes 262176 | tf_op jit(solution)/shard_map/ppermute | solution.py:124
  47.4 1.7 %collective-permute-done.4.refs_4_ = bf16[128,1024]{1,0:T(8,128)(2,1)S(1)} collective-permute-done((bf16[128,1024]{1,0:T(8,128)(2,1)S(1)}, bf16[128,1024]{1,0:T(8,128)(2,1)S(1)}, u32[]{:S(2)}, u32[]{:S(2)}) %collective-permute-start.4) | collective-permute-done | bytes 262176 | tf_op jit(solution)/shard_map/ppermute | solution.py:124
  50.4 2.7 %collective-permute-done.7.refs_7_ = bf16[128,1024]{1,0:T(8,128)(2,1)S(1)} collective-permute-done((bf16[128,1024]{1,0:T(8,128)(2,1)S(1)}, bf16[128,1024]{1,0:T(8,128)(2,1)S(1)}, u32[]{:S(2)}, u32[]{:S(2)}) %collective-permute-start.7) | collective-permute-done | bytes 262176 | tf_op jit(solution)/shard_map/ppermute | solution.py:133
  53.1 4.9 %collective-permute-done.5.refs_5_ = bf16[128,1024]{1,0:T(8,128)(2,1)S(1)} collective-permute-done((bf16[128,1024]{1,0:T(8,128)(2,1)S(1)}, bf16[128,1024]{1,0:T(8,128)(2,1)S(1)}, u32[]{:S(2)}, u32[]{:S(2)}) %collective-permute-start.5) | collective-permute-done | bytes 262176 | tf_op jit(solution)/shard_map/ppermute | solution.py:133
  58.8 7.4 %shard_map.82 = bf16[16,3,32,512]{3,2,1,0:T(8,128)(2,1)} custom-call(s32[1]{0:T(128)} %bitcast.10.place_ref, bf16[128,1024]{1,0:T(8,128)(2,1)} %copy-done.5, bf16[128,1024]{1,0:T(8,128)(2,1)} %copy-done.8, bf16[128,1024]{1,0:T(8,128)(2,1)} %copy-done.7, bf16[128,1024]{1,0:T(8,128)(2,1)} %copy-done.11, bf16[128,1024]{1,0:T(8,128)(2,1)} %copy-done.10, ...), custom_call_target="tpu_custom_call" | custom-call | flops 96636764160 | bytes 9961472 | tf_op jit(solution)/shard_map/pallas_call | solution.py:159
  66.2 6.1 %all-to-all-start.1 = ((bf16[16,3,32,512]{3,2,1,0:T(8,128)(2,1)}), bf16[16,3,32,512]{3,2,1,0:T(8,128)(2,1)S(1)}, u32[]{:S(2)}, u32[]{:S(2)}) async-start(bf16[16,3,32,512]{3,2,1,0:T(8,128)(2,1)} %shard_map.82), calls=%async_computation.1 | async-start | bytes 3145728 | tf_op jit(solution)/shard_map/all_to_all | solution.py:430
  72.3 31.9 %all-gather.6.cloned.1.call-done = bf16[4096,512]{1,0:T(8,128)(2,1)} async-done(((bf16[512,512]{1,0:T(8,128)(2,1)}), bf16[4096,512]{1,0:T(8,128)(2,1)}) %all-gather.6.cloned.1.call-update) | async-done | bytes 4194320 | tf_op jit(solution)/shard_map/all_gather | solution.py:426
  104.2 3.0 %all-to-all-done.1.refs_0_ = bf16[16,3,32,512]{3,2,1,0:T(8,128)(2,1)S(1)} async-done(((bf16[16,3,32,512]{3,2,1,0:T(8,128)(2,1)}), bf16[16,3,32,512]{3,2,1,0:T(8,128)(2,1)S(1)}, u32[]{:S(2)}, u32[]{:S(2)}) %all-to-all-start.1) | async-done | bytes 1572896 | tf_op jit(solution)/shard_map/all_to_all | solution.py:430
  107.3 3.7 %shard_map.83 = bf16[2,4,4,32,256]{4,3,2,1,0:T(8,128)(2,1)} custom-call(bf16[16,3,32,512]{3,2,1,0:T(8,128)(2,1)S(1)} %all-to-all-done.1.refs_0_, f32[16,32,128]{2,1,0:T(8,128)S(1)} %all-to-all-done.refs_1_, f32[3,3,32,128]{3,2,1,0:T(8,128)S(1)} %broadcast_in_dim.7.refs_2_, f32[32,128]{1,0:T(8,128)S(1)} %broadcast_in_dim.8.refs_3_, f32[128,256]{1,0:T(8,128)S(1)} %copy-done.3, ...), custom_call_target="tpu_custom_call" | custom-call | flops 1000000000 | bytes 4194304 | tf_op jit(solution)/shard_map/pallas_call | solution.py:323
  111.0 5.9 %all-to-all-start.2 = ((bf16[32,32,256]{2,1,0:T(8,128)(2,1)}), bf16[32,32,256]{2,1,0:T(8,128)(2,1)S(1)}, u32[]{:S(2)}, u32[]{:S(2)}) async-start(bf16[32,32,256]{2,1,0:T(8,128)(2,1)} %bitcast.23), calls=%async_computation.2 | async-start | bytes 1048576 | tf_op jit(solution)/shard_map/all_to_all | solution.py:435
  117.0 14.4 %all-to-all-done.2 = bf16[32,32,256]{2,1,0:T(8,128)(2,1)S(1)} async-done(((bf16[32,32,256]{2,1,0:T(8,128)(2,1)}), bf16[32,32,256]{2,1,0:T(8,128)(2,1)S(1)}, u32[]{:S(2)}, u32[]{:S(2)}) %all-to-all-start.2) | async-done | bytes 524320 | tf_op jit(solution)/shard_map/all_to_all | solution.py:435
  131.4 2.2 %copy-done.1 = bf16[4096,512]{1,0:T(8,128)(2,1)S(1)} copy-done((bf16[4096,512]{1,0:T(8,128)(2,1)S(1)}, bf16[4096,512]{1,0:T(8,128)(2,1)}, u32[]{:S(2)}) %copy-start.1) | copy-done | bytes 4194328
  133.6 2.6 %shard_map.84 = (bf16[64,2048]{1,0:T(8,128)(2,1)S(1)}, bf16[64,2048]{1,0:T(8,128)(2,1)S(1)}, bf16[64,2048]{1,0:T(8,128)(2,1)S(1)}, bf16[64,2048]{1,0:T(8,128)(2,1)S(1)}) custom-call(s32[4]{0:T(128)S(1)} %pad_add_fusion.block_ref, bf16[2,512,256]{2,1,0:T(8,128)(2,1)S(1)} %bitcast.34, bf16[4,2,512,512]{3,2,1,0:T(8,128)(2,1)S(1)} %bitcast.33), custom_call_target="tpu_custom_call" | custom-call | flops 1073741824 | bytes 5767168 | tf_op jit(solution)/shard_map/pallas_call | solution.py:369
  136.3 2.6 %collective-permute-start.8 = (bf16[64,2048]{1,0:T(8,128)(2,1)S(1)}, bf16[64,2048]{1,0:T(8,128)(2,1)S(1)}, u32[]{:S(2)}, u32[]{:S(2)}) collective-permute-start(bf16[64,2048]{1,0:T(8,128)(2,1)S(1)} %get-tuple-element.47), channel_id=1, source_target_pairs={{0,0},{1,16},{2,2},{3,18},{4,4},{5,20},{6,6},{7,22},{8,24},{9,8},{... | collective-permute-start | bytes 786440 | tf_op jit(solution)/shard_map/ppermute | solution.py:88
  138.9 3.9 %collective-permute-start.10 = (bf16[64,2048]{1,0:T(8,128)(2,1)S(1)}, bf16[64,2048]{1,0:T(8,128)(2,1)S(1)}, u32[]{:S(2)}, u32[]{:S(2)}) collective-permute-start(bf16[64,2048]{1,0:T(8,128)(2,1)S(1)} %get-tuple-element.49), channel_id=1, source_target_pairs={{0,16},{1,0},{2,18},{3,2},{4,20},{5,4},{6,22},{7,6},{8,8},{9,24},{... | collective-permute-start | bytes 786440 | tf_op jit(solution)/shard_map/ppermute | solution.py:88
  142.8 2.3 %collective-permute-start.11 = (bf16[64,2048]{1,0:T(8,128)(2,1)S(1)}, bf16[64,2048]{1,0:T(8,128)(2,1)S(1)}, u32[]{:S(2)}, u32[]{:S(2)}) collective-permute-start(bf16[64,2048]{1,0:T(8,128)(2,1)S(1)} %get-tuple-element.50), channel_id=1, source_target_pairs={{0,24},{1,8},{2,26},{3,10},{4,28},{5,12},{6,30},{7,14},{8,0},{9,16... | collective-permute-start | bytes 786440 | tf_op jit(solution)/shard_map/ppermute | solution.py:88
  145.2 3.2 %collective-permute-done.8.refs_0_ = bf16[64,2048]{1,0:T(8,128)(2,1)S(1)} collective-permute-done((bf16[64,2048]{1,0:T(8,128)(2,1)S(1)}, bf16[64,2048]{1,0:T(8,128)(2,1)S(1)}, u32[]{:S(2)}, u32[]{:S(2)}) %collective-permute-start.8) | collective-permute-done | bytes 262176 | tf_op jit(solution)/shard_map/ppermute | solution.py:88
  148.4 16.4 %collective-permute-done.9.refs_1_ = bf16[64,2048]{1,0:T(8,128)(2,1)S(1)} collective-permute-done((bf16[64,2048]{1,0:T(8,128)(2,1)S(1)}, bf16[64,2048]{1,0:T(8,128)(2,1)S(1)}, u32[]{:S(2)}, u32[]{:S(2)}) %collective-permute-start.9) | collective-permute-done | bytes 262176 | tf_op jit(solution)/shard_map/ppermute | solution.py:88
  (56 shorter events, 12.3 us)
Async XLA Ops:
  6.5 10.3 %copy-start = (f32[3,3,512]{2,1,0:T(4,128)S(1)}, f32[3,3,512]{2,1,0:T(4,128)}, u32[]{:S(2)}) copy-start(f32[3,3,512]{2,1,0:T(4,128)} %param.10) | copy-start | bytes 55300
  6.5 51.6 %all-gather.4.cloned.1.call-start = ((), (), s32[]{:S(2)}) async-start(), calls=%async_computation.3 | async-start | bytes 7864320 | tf_op jit(solution)/shard_map/all_gather | solution.py:408
  7.9 13.7 %collective-permute-start = (bf16[2,128,1024]{2,1,0:T(8,128)(2,1)S(1)}, bf16[2,128,1024]{2,1,0:T(8,128)(2,1)S(1)}, u32[]{:S(2)}, u32[]{:S(2)}) collective-permute-start(bf16[2,128,1024]{2,1,0:T(8,128)(2,1)S(1)} %pad_maximum_fusion.1), channel_id=1, source_target_pairs={{0,1},{1,0},{2,3},{3,2},{4,5},{5,4},{6,7},{7,6},{8,9},{9,8},{10,11... | collective-permute-start | bytes 1572872 | tf_op jit(solution)/shard_map/ppermute | solution.py:107
  9.6 14.4 %all-to-all-start = ((f32[16,32,128]{2,1,0:T(8,128)}), f32[16,32,128]{2,1,0:T(8,128)S(1)}, u32[]{:S(2)}, u32[]{:S(2)}) async-start(f32[16,32,128]{2,1,0:T(8,128)} %bitcast.16), calls=%async_computation | async-start | bytes 524288 | tf_op jit(solution)/shard_map/all_to_all | solution.py:414
  15.8 88.4 %all-gather.6.cloned.1.call-start = ((), (), s32[]{:S(2)}) async-start(), calls=%async_computation.4 | async-start | bytes 4718592 | tf_op jit(solution)/shard_map/all_gather | solution.py:426
  24.2 33.9 %copy-start.5 = (bf16[128,1024]{1,0:T(8,128)(2,1)}, bf16[128,1024]{1,0:T(8,128)(2,1)S(1)}, u32[]{:S(2)}) copy-start(bf16[128,1024]{1,0:T(8,128)(2,1)S(1)} %get-tuple-element.33.refs_0_) | copy-start | bytes 786436
  24.2 9.2 %collective-permute-start.1 = (bf16[128,1024]{1,0:T(8,128)(2,1)S(1)}, bf16[128,1024]{1,0:T(8,128)(2,1)S(1)}, u32[]{:S(2)}, u32[]{:S(2)}) collective-permute-start(bf16[128,1024]{1,0:T(8,128)(2,1)S(1)} %get-tuple-element.53), channel_id=1, source_target_pairs={{0,8},{2,10},{4,12},{6,14},{8,16},{10,18},{12,20},{14,22},{16,24},... | collective-permute-start | bytes 786440 | tf_op jit(solution)/shard_map/ppermute | solution.py:124
  25.9 7.6 %collective-permute-start.2 = (bf16[128,1024]{1,0:T(8,128)(2,1)S(1)}, bf16[128,1024]{1,0:T(8,128)(2,1)S(1)}, u32[]{:S(2)}, u32[]{:S(2)}) collective-permute-start(bf16[128,1024]{1,0:T(8,128)(2,1)S(1)} %get-tuple-element.33.refs_0_), channel_id=1, source_target_pairs={{0,1},{1,0},{2,3},{3,2},{4,5},{5,4},{6,7},{7,6},{8,9},{9,8},{10,11... | collective-permute-start | bytes 786440 | tf_op jit(solution)/shard_map/ppermute | solution.py:133
  27.2 18.9 %collective-permute-start.6 = (bf16[128,1024]{1,0:T(8,128)(2,1)S(1)}, bf16[128,1024]{1,0:T(8,128)(2,1)S(1)}, u32[]{:S(2)}, u32[]{:S(2)}) collective-permute-start(bf16[128,1024]{1,0:T(8,128)(2,1)S(1)} %get-tuple-element.51), channel_id=1, source_target_pairs={{0,24},{2,26},{4,28},{6,30},{8,0},{10,2},{12,4},{14,6},{16,8},{18,... | collective-permute-start | bytes 786440 | tf_op jit(solution)/shard_map/ppermute | solution.py:124
  33.5 24.7 %copy-start.7 = (bf16[128,1024]{1,0:T(8,128)(2,1)}, bf16[128,1024]{1,0:T(8,128)(2,1)S(1)}, u32[]{:S(2)}) copy-start(bf16[128,1024]{1,0:T(8,128)(2,1)S(1)} %collective-permute-done.1.refs_2_) | copy-start | bytes 786436
  33.5 24.7 %copy-start.8 = (bf16[128,1024]{1,0:T(8,128)(2,1)}, bf16[128,1024]{1,0:T(8,128)(2,1)S(1)}, u32[]{:S(2)}) copy-start(bf16[128,1024]{1,0:T(8,128)(2,1)S(1)} %collective-permute-done.2.refs_1_) | copy-start | bytes 786436
  33.5 15.6 %collective-permute-start.4 = (bf16[128,1024]{1,0:T(8,128)(2,1)S(1)}, bf16[128,1024]{1,0:T(8,128)(2,1)S(1)}, u32[]{:S(2)}, u32[]{:S(2)}) collective-permute-start(bf16[128,1024]{1,0:T(8,128)(2,1)S(1)} %dynamic-slice_bitcast_fusion.1), channel_id=1, source_target_pairs={{0,16},{2,18},{4,20},{6,22},{8,24},{10,26},{12,28},{14,30},{16,0},... | collective-permute-start | bytes 786440 | tf_op jit(solution)/shard_map/ppermute | solution.py:124
  36.5 16.6 %collective-permute-start.3 = (bf16[128,1024]{1,0:T(8,128)(2,1)S(1)}, bf16[128,1024]{1,0:T(8,128)(2,1)S(1)}, u32[]{:S(2)}, u32[]{:S(2)}) collective-permute-start(bf16[128,1024]{1,0:T(8,128)(2,1)S(1)} %collective-permute-done.1.refs_2_), channel_id=1, source_target_pairs={{0,1},{1,0},{2,3},{3,2},{4,5},{5,4},{6,7},{7,6},{8,9},{9,8},{10,11... | collective-permute-start | bytes 786440 | tf_op jit(solution)/shard_map/ppermute | solution.py:133
  46.1 12.1 %copy-start.9 = (bf16[128,1024]{1,0:T(8,128)(2,1)}, bf16[128,1024]{1,0:T(8,128)(2,1)S(1)}, u32[]{:S(2)}) copy-start(bf16[128,1024]{1,0:T(8,128)(2,1)S(1)} %collective-permute-done.6.refs_6_) | copy-start | bytes 786436
  46.1 7.0 %collective-permute-start.7 = (bf16[128,1024]{1,0:T(8,128)(2,1)S(1)}, bf16[128,1024]{1,0:T(8,128)(2,1)S(1)}, u32[]{:S(2)}, u32[]{:S(2)}) collective-permute-start(bf16[128,1024]{1,0:T(8,128)(2,1)S(1)} %collective-permute-done.6.refs_6_), channel_id=1, source_target_pairs={{0,1},{1,0},{2,3},{3,2},{4,5},{5,4},{6,7},{7,6},{8,9},{9,8},{10,11... | collective-permute-start | bytes 786440 | tf_op jit(solution)/shard_map/ppermute | solution.py:133
  49.1 9.0 %collective-permute-start.5 = (bf16[128,1024]{1,0:T(8,128)(2,1)S(1)}, bf16[128,1024]{1,0:T(8,128)(2,1)S(1)}, u32[]{:S(2)}, u32[]{:S(2)}) collective-permute-start(bf16[128,1024]{1,0:T(8,128)(2,1)S(1)} %collective-permute-done.4.refs_4_), channel_id=1, source_target_pairs={{0,1},{1,0},{2,3},{3,2},{4,5},{5,4},{6,7},{7,6},{8,9},{9,8},{10,11... | collective-permute-start | bytes 786440 | tf_op jit(solution)/shard_map/ppermute | solution.py:133
  66.2 41.1 %copy-start.2 = (f32[256,256]{1,0:T(8,128)S(1)}, f32[256,256]{1,0:T(8,128)}, u32[]{:S(2)}) copy-start(f32[256,256]{1,0:T(8,128)} %constant.232.clone.refs_5_) | copy-start | bytes 786436
  66.2 41.1 %copy-start.3 = (f32[128,256]{1,0:T(8,128)S(1)}, f32[128,256]{1,0:T(8,128)}, u32[]{:S(2)}) copy-start(f32[128,256]{1,0:T(8,128)} %constant.231.clone.refs_4_) | copy-start | bytes 393220
  66.2 41.1 %all-to-all-start.1 = ((bf16[16,3,32,512]{3,2,1,0:T(8,128)(2,1)}), bf16[16,3,32,512]{3,2,1,0:T(8,128)(2,1)S(1)}, u32[]{:S(2)}, u32[]{:S(2)}) async-start(bf16[16,3,32,512]{3,2,1,0:T(8,128)(2,1)} %shard_map.82), calls=%async_computation.1 | async-start | bytes 3145728 | tf_op jit(solution)/shard_map/all_to_all | solution.py:430
  111.0 20.4 %all-to-all-start.2 = ((bf16[32,32,256]{2,1,0:T(8,128)(2,1)}), bf16[32,32,256]{2,1,0:T(8,128)(2,1)S(1)}, u32[]{:S(2)}, u32[]{:S(2)}) async-start(bf16[32,32,256]{2,1,0:T(8,128)(2,1)} %bitcast.23), calls=%async_computation.2 | async-start | bytes 1048576 | tf_op jit(solution)/shard_map/all_to_all | solution.py:435
  136.3 12.1 %collective-permute-start.8 = (bf16[64,2048]{1,0:T(8,128)(2,1)S(1)}, bf16[64,2048]{1,0:T(8,128)(2,1)S(1)}, u32[]{:S(2)}, u32[]{:S(2)}) collective-permute-start(bf16[64,2048]{1,0:T(8,128)(2,1)S(1)} %get-tuple-element.47), channel_id=1, source_target_pairs={{0,0},{1,16},{2,2},{3,18},{4,4},{5,20},{6,6},{7,22},{8,24},{9,8},{... | collective-permute-start | bytes 786440 | tf_op jit(solution)/shard_map/ppermute | solution.py:88
  138.9 25.9 %collective-permute-start.9 = (bf16[64,2048]{1,0:T(8,128)(2,1)S(1)}, bf16[64,2048]{1,0:T(8,128)(2,1)S(1)}, u32[]{:S(2)}, u32[]{:S(2)}) collective-permute-start(bf16[64,2048]{1,0:T(8,128)(2,1)S(1)} %get-tuple-element.48), channel_id=1, source_target_pairs={{0,8},{1,24},{2,10},{3,26},{4,12},{5,28},{6,14},{7,30},{8,16},{9,0... | collective-permute-start | bytes 786440 | tf_op jit(solution)/shard_map/ppermute | solution.py:88
  138.9 25.8 %collective-permute-start.10 = (bf16[64,2048]{1,0:T(8,128)(2,1)S(1)}, bf16[64,2048]{1,0:T(8,128)(2,1)S(1)}, u32[]{:S(2)}, u32[]{:S(2)}) collective-permute-start(bf16[64,2048]{1,0:T(8,128)(2,1)S(1)} %get-tuple-element.49), channel_id=1, source_target_pairs={{0,16},{1,0},{2,18},{3,2},{4,20},{5,4},{6,22},{7,6},{8,8},{9,24},{... | collective-permute-start | bytes 786440 | tf_op jit(solution)/shard_map/ppermute | solution.py:88
  142.8 22.0 %collective-permute-start.11 = (bf16[64,2048]{1,0:T(8,128)(2,1)S(1)}, bf16[64,2048]{1,0:T(8,128)(2,1)S(1)}, u32[]{:S(2)}, u32[]{:S(2)}) collective-permute-start(bf16[64,2048]{1,0:T(8,128)(2,1)S(1)} %get-tuple-element.50), channel_id=1, source_target_pairs={{0,24},{1,8},{2,26},{3,10},{4,28},{5,12},{6,30},{7,14},{8,0},{9,16... | collective-permute-start | bytes 786440 | tf_op jit(solution)/shard_map/ppermute | solution.py:88
  (7 other events, 24.3 us)
Sparse Core Ops, SparseCore 0:
  8.9 48.8 all-gather.3
  59.7 44.4 all-gather.5

commit v16 on v11

--- a/solution.py
+++ b/solution.py
@@ -22,26 +22,28 @@
 
 
 def assemble_kernel(place_ref, *refs):
-    *piece_refs, out_ref = refs
+    *piece_refs, out_ref, sems = refs
+    part_rows, width = piece_refs[0].shape
+    copies = []
     for index, piece_ref in enumerate(piece_refs):
-
-        @pl.when(pl.program_id(0) == index)
-        def _():
-            out_ref[...] = piece_ref[...]
+        row = pl.multiple_of(place_ref[2 * index] * part_rows, part_rows)
+        column = pl.multiple_of(place_ref[2 * index + 1] * width, width)
+        target = out_ref.at[pl.ds(row, part_rows), pl.ds(column, width)]
+        copies.append(pltpu.make_async_copy(piece_ref, target, sems.at[index]))
+    for copy in copies:
+        copy.start()
+    for copy in copies:
+        copy.wait()
 
 
 def assemble(pieces, places, shape):
     return pl.pallas_call(
         assemble_kernel,
-        grid_spec=pltpu.PrefetchScalarGridSpec(
-            num_scalar_prefetch=1,
-            grid=(len(pieces),),
-            in_specs=[pl.BlockSpec(memory_space=pltpu.VMEM)] * len(pieces),
-            out_specs=pl.BlockSpec(
-                pieces[0].shape, lambda i, place: (place[2 * i], place[2 * i + 1])
-            ),
-        ),
+        in_specs=[pl.BlockSpec(memory_space=pltpu.SMEM)]
+        + [pl.BlockSpec(memory_space=pltpu.VMEM)] * len(pieces),
+        out_specs=pl.BlockSpec(memory_space=pl.ANY),
         out_shape=jax.ShapeDtypeStruct(shape, pieces[0].dtype),
+        scratch_shapes=[pltpu.SemaphoreType.DMA((len(pieces),))],
         compiler_params=pltpu.CompilerParams(vmem_limit_bytes=4 * 2**20),
         cost_estimate=pl.CostEstimate(
             flops=0, bytes_accessed=4 * shape[0] * shape[1], transcendentals=0
@@ -107,15 +109,13 @@
     return jnp.concatenate(held)
 
 
-def cross_outer(held, outer, inner_parts, tp_parts):
+def cross_outer(held, steps, outer, inner_parts, tp_parts):
     per_tp = outer // tp_parts
     seq_parts = outer * inner_parts
     tp_place = lax.axis_index("tp")
     outer_place = lax.axis_index("seq") // inner_parts
     arrived = {}
-    for step in sorted(range(outer), key=lambda step: min(step, outer - step)):
-        if step not in (0, 1, outer - 1):
-            arrived[1], held = lax.optimization_barrier((arrived[1], held))
+    for step in steps:
         target = (outer_place + step) % outer
         which = (tp_place - target // per_tp + tp_parts) % tp_parts * per_tp + target % per_tp
         piece = lax.dynamic_index_in_dim(held, which, axis=0, keepdims=False)
@@ -123,7 +123,7 @@
             far = step * inner_parts
             piece = lax.ppermute(piece, "seq", [(i, (i + far) % seq_parts) for i in range(seq_parts)])
         arrived[step] = piece
-    return [arrived[step] for step in range(outer)]
+    return arrived
 
 
 def share_over_tp(part, tp_parts):
@@ -137,23 +137,26 @@
 def project_kernel(tp_parts, place_ref, *refs):
     *share_refs, weight_ref, out_ref, held, sems = refs
     seq_parts, streams, chans, count = out_ref.shape
-    copies = [
-        pltpu.make_async_copy(weight_ref.at[stream], held.at[stream], sems.at[stream])
-        for stream in range(streams)
-    ]
-    for copy in copies:
-        copy.start()
+    copies = []
+    for stream in range(streams):
+        for step in range(tp_parts):
+            which = lax.rem(place_ref[0] - step + tp_parts, tp_parts)
+            copies.append(
+                pltpu.make_async_copy(
+                    weight_ref.at[stream, which], held.at[stream, step], sems.at[len(copies)]
+                )
+            )
+            copies[-1].start()
     left = [
         jnp.concatenate([share_ref[...] for share_ref in share_refs[step::tp_parts]])
         for step in range(tp_parts)
     ]
     for stream in range(streams):
-        copies[stream].wait()
         sums = jnp.zeros((count, seq_parts * chans), jnp.float32)
         for step in range(tp_parts):
-            which = lax.rem(place_ref[0] - step + tp_parts, tp_parts)
+            copies[stream * tp_parts + step].wait()
             sums = sums + jnp.dot(
-                left[step], held[stream, which], preferred_element_type=jnp.float32
+                left[step], held[stream, step], preferred_element_type=jnp.float32
             )
         turned = sums.astype(out_ref.dtype).T
         for seq in range(seq_parts):
@@ -174,14 +177,14 @@
         functools.partial(project_kernel, tp_parts),
         in_specs=[pl.BlockSpec(memory_space=pltpu.SMEM)]
         + [vmem] * len(pieces)
-        + [pl.BlockSpec(memory_space=pltpu.HBM)],
+        + [pl.BlockSpec(memory_space=pl.ANY)],
         out_specs=vmem,
         out_shape=jax.ShapeDtypeStruct((seq_parts, streams, chans, count), jnp.bfloat16),
         scratch_shapes=[
             pltpu.VMEM(weight.shape, weight.dtype),
-            pltpu.SemaphoreType.DMA((streams,)),
+            pltpu.SemaphoreType.DMA((streams * tp_parts,)),
         ],
-        compiler_params=pltpu.CompilerParams(vmem_limit_bytes=32 * 2**20),
+        compiler_params=pltpu.CompilerParams(vmem_limit_bytes=48 * 2**20),
         cost_estimate=pl.CostEstimate(
             flops=HEAVY * 2 * count * weight.size,
             bytes_accessed=2 * (weight.size + len(pieces) * pieces[0].size)
@@ -394,7 +397,7 @@
         in_specs=[
             pl.BlockSpec(memory_space=pltpu.SMEM),
             vmem,
-            pl.BlockSpec(memory_space=pltpu.HBM),
+            pl.BlockSpec(memory_space=pl.ANY),
         ],
         out_specs=[vmem] * len(blocks),
         scratch_shapes=[
@@ -404,7 +407,7 @@
             pltpu.SemaphoreType.DMA((inner_parts,)),
         ],
         out_shape=[jax.ShapeDtypeStruct((part_rows, columns), jnp.bfloat16)] * len(blocks),
-        compiler_params=pltpu.CompilerParams(vmem_limit_bytes=24 * 2**20),
+        compiler_params=pltpu.CompilerParams(vmem_limit_bytes=52 * 2**20),
         cost_estimate=pl.CostEstimate(
             flops=2 * gated.size * columns,
             bytes_accessed=2 * (weight.size + gated.size + rows * columns),
@@ -433,14 +436,19 @@
     taps = jnp.broadcast_to(taps[..., None], taps.shape + (rows,))
     skip = lax.dynamic_slice_in_dim(skip_gain, position * chans, chans, axis=0)
     skip = jnp.broadcast_to(skip[:, None], (chans, rows))
-    filter_blocks = long_filter.T.reshape(seq_parts, chans, rows)
+    filter_blocks = lax.all_to_all(
+        long_filter.T.reshape(seq_parts, chans, rows), "seq", split_axis=0, concat_axis=0, tiled=True
+    )
 
     held = share_columns(features, outer, tp_parts)
-    held, taps, skip = lax.optimization_barrier((held, taps, skip))
-    arrived = cross_outer(held, outer, inner_parts, tp_parts)
-    filter_blocks = lax.all_to_all(filter_blocks, "seq", split_axis=0, concat_axis=0, tiled=True)
-    arrived[1], filter_blocks = lax.optimization_barrier((arrived[1], filter_blocks))
-    chunks = [share_over_tp(piece, tp_parts) for piece in arrived]
+    arrived = cross_outer(held, (0, 1), outer, inner_parts, tp_parts)
+    held, taps, skip, filter_blocks = lax.optimization_barrier((held, taps, skip, filter_blocks))
+    if outer > 2:
+        arrived |= cross_outer(held, (outer - 1,), outer, inner_parts, tp_parts)
+    own = share_over_tp(arrived[0], tp_parts)
+    held, arrived[1], own = lax.optimization_barrier((held, arrived[1], own))
+    arrived |= cross_outer(held, range(2, outer - 1), outer, inner_parts, tp_parts)
+    chunks = [own] + [share_over_tp(arrived[step], tp_parts) for step in range(1, outer)]
     chunks, out_proj = lax.optimization_barrier((chunks, out_proj))
     out_weight = lax.all_gather(out_proj, ("seq", "tp"), axis_index_groups=tp_groups)
     out_weight = out_weight.reshape((inner_parts, tp_parts) + out_proj.shape)

time: 185 us -> 173 us (0.935)
  waiting for transfers between devices: 113 us -> 103 us
  local copies, waits for them, and re-layouts: 8.25 us -> 2.81 us
  starting transfers between devices: 34.9 us -> 37.2 us
    all_to_all x1, waiting for transfers between devices: 13.6 us -> 0.01 us  [per_device(): lax.all_to_all(long_filter.T.reshape(seq_parts, chans, rows), 'seq', spli...]
    all_gather x1, waiting for transfers between devices: 31.3 us -> 39.7 us  [per_device(): lax.all_gather(out_proj, ('seq', 'tp'), axis_index_groups=tp_groups)]
    ppermute x1, waiting for transfers between devices: 12.3 us -> 5.62 us  [share_columns(): lax.ppermute(piece, 'tp', [(i, (i + step) % tp_parts) for i in range(tp_p...]
    ppermute x3, waiting for transfers between devices: 4.35 us -> 10.5 us  [cross_outer(): lax.ppermute(piece, 'seq', [(i, (i + far) % seq_parts) for i in range(seq...]
    unnamed x14 -> x10, local copies, waits for them, and re-layouts: 5.47 us -> 0.74 us
    ppermute x3, starting transfers between devices: 4.61 us -> 9.2 us  [cross_outer(): lax.ppermute(piece, 'seq', [(i, (i + far) % seq_parts) for i in range(seq...]
    ppermute x4, waiting for transfers between devices: 13 us -> 8.77 us  [share_over_tp(): pieces.append(lax.ppermute(part, 'tp', pairs))]
    all_to_all x1, waiting for transfers between devices: 3.65 us -> 0.01 us  [per_device(): lax.all_to_all(partial, 'seq', split_axis=0, concat_axis=0, tiled=True)]
  transfers between devices with their start and end apart: 17 -> 17, of which waited for: 11 -> 12; matrix products, arithmetic and copies ran while one was open for 2% -> 1% of each run, Pallas kernels for 3% -> 4%
where the time goes in v16:
time: 173 us
  waiting for transfers between devices  103 us (60%)
  starting transfers between devices  37.2 us (22%)
  Pallas kernels  15.7 us (9%)
  between operations  13.8 us (8%)
  local copies, waits for them, and re-layouts  2.81 us (2%)
    all_gather x1, waiting for transfers between devices, per_device(): lax.all_gather(out_proj, ('seq', 'tp'), axis_index_groups=tp_groups)  39.7 us
    ppermute x4, waiting for transfers between devices, return_output(): arrived.append(lax.ppermute(piece, ('seq', 'tp'), pairs))  19.5 us
    all_to_all x1, waiting for transfers between devices, per_device(): lax.all_to_all(gated.reshape((-1,) + gated.shape[3:]), ('tp', 'seq'), spl...  14.4 us
    ppermute x3, waiting for transfers between devices, cross_outer(): lax.ppermute(piece, 'seq', [(i, (i + far) % seq_parts) for i in range(seq...  10.5 us
    ppermute x3, starting transfers between devices, cross_outer(): lax.ppermute(piece, 'seq', [(i, (i + far) % seq_parts) for i in range(seq...  9.2 us
    ppermute x4, starting transfers between devices, return_output(): arrived.append(lax.ppermute(piece, ('seq', 'tp'), pairs))  8.85 us
    ppermute x4, waiting for transfers between devices, share_over_tp(): pieces.append(lax.ppermute(part, 'tp', pairs))  8.77 us
    pallas_call x1, Pallas kernels, project_in(): pl.pallas_call(functools.partial(project_kernel, tp_parts), in_specs=[pl....  6.82 us
  transfers between devices with their start and end apart: 17, of which 12 were waited for; matrix products, arithmetic and copies ran while one was open for 1% of the time, Pallas kernels for 4%

profile of v16, /device:TPU:12, one launch (start us, length us, event | category | flops | bytes accessed | tf_op | source)
XLA Modules:
  0.0 172.6 jit_solution(6959764708844620754)
XLA Ops:
  9.6 6.3 %all-to-all-start = ((f32[16,32,128]{2,1,0:T(8,128)}), f32[16,32,128]{2,1,0:T(8,128)S(1)}, u32[]{:S(2)}, u32[]{:S(2)}) async-start(f32[16,32,128]{2,1,0:T(8,128)} %bitcast.16), calls=%async_computation | async-start | bytes 524288 | tf_op jit(solution)/shard_map/all_to_all | solution.py:439
  16.0 5.6 %collective-permute-done = bf16[2,128,1024]{2,1,0:T(8,128)(2,1)S(1)} collective-permute-done((bf16[2,128,1024]{2,1,0:T(8,128)(2,1)S(1)}, bf16[2,128,1024]{2,1,0:T(8,128)(2,1)S(1)}, u32[]{:S(2)}, u32[]{:S(2)}) %collective-permute-start) | collective-permute-done | bytes 524320 | tf_op jit(solution)/shard_map/ppermute | solution.py:107
  21.8 1.6 collective-permute-start.1
  26.2 3.6 %collective-permute-done.1.refs_2_ = bf16[128,1024]{1,0:T(8,128)(2,1)S(1)} collective-permute-done((bf16[128,1024]{1,0:T(8,128)(2,1)S(1)}, bf16[128,1024]{1,0:T(8,128)(2,1)S(1)}, u32[]{:S(2)}, u32[]{:S(2)}) %collective-permute-start.1) | collective-permute-done | bytes 262176 | tf_op jit(solution)/shard_map/ppermute | solution.py:124
  30.3 6.3 %collective-permute-start.4 = (bf16[128,1024]{1,0:T(8,128)(2,1)S(1)}, bf16[128,1024]{1,0:T(8,128)(2,1)S(1)}, u32[]{:S(2)}, u32[]{:S(2)}) collective-permute-start(bf16[128,1024]{1,0:T(8,128)(2,1)S(1)} %dynamic-slice_bitcast_fusion.1), channel_id=1, source_target_pairs={{0,16},{2,18},{4,20},{6,22},{8,24},{10,26},{12,28},{14,30},{16,0},... | collective-permute-start | bytes 786440 | tf_op jit(solution)/shard_map/ppermute | solution.py:124
  36.6 1.5 collective-permute-start.3
  38.1 3.4 %collective-permute-done.6.refs_6_ = bf16[128,1024]{1,0:T(8,128)(2,1)S(1)} collective-permute-done((bf16[128,1024]{1,0:T(8,128)(2,1)S(1)}, bf16[128,1024]{1,0:T(8,128)(2,1)S(1)}, u32[]{:S(2)}, u32[]{:S(2)}) %collective-permute-start.6) | collective-permute-done | bytes 262176 | tf_op jit(solution)/shard_map/ppermute | solution.py:124
  41.5 3.5 %collective-permute-done.4.refs_4_ = bf16[128,1024]{1,0:T(8,128)(2,1)S(1)} collective-permute-done((bf16[128,1024]{1,0:T(8,128)(2,1)S(1)}, bf16[128,1024]{1,0:T(8,128)(2,1)S(1)}, u32[]{:S(2)}, u32[]{:S(2)}) %collective-permute-start.4) | collective-permute-done | bytes 262176 | tf_op jit(solution)/shard_map/ppermute | solution.py:124
  46.0 4.7 %collective-permute-done.7.refs_7_ = bf16[128,1024]{1,0:T(8,128)(2,1)S(1)} collective-permute-done((bf16[128,1024]{1,0:T(8,128)(2,1)S(1)}, bf16[128,1024]{1,0:T(8,128)(2,1)S(1)}, u32[]{:S(2)}, u32[]{:S(2)}) %collective-permute-start.7) | collective-permute-done | bytes 262176 | tf_op jit(solution)/shard_map/ppermute | solution.py:133
  50.7 3.5 %collective-permute-done.5.refs_5_ = bf16[128,1024]{1,0:T(8,128)(2,1)S(1)} collective-permute-done((bf16[128,1024]{1,0:T(8,128)(2,1)S(1)}, bf16[128,1024]{1,0:T(8,128)(2,1)S(1)}, u32[]{:S(2)}, u32[]{:S(2)}) %collective-permute-start.5) | collective-permute-done | bytes 262176 | tf_op jit(solution)/shard_map/ppermute | solution.py:133
  54.3 3.6 %all-gather.4.cloned.1.call-done = bf16[3,2048,512]{2,1,0:T(8,128)(2,1)} async-done(((bf16[3,512,512]{2,1,0:T(8,128)(2,1)}), bf16[3,2048,512]{2,1,0:T(8,128)(2,1)}) %all-gather.4.cloned.1.call-update) | async-done | bytes 6291472 | tf_op jit(solution)/shard_map/all_gather | solution.py:433
  57.9 6.8 %shard_map.82 = bf16[16,3,32,512]{3,2,1,0:T(8,128)(2,1)} custom-call(s32[1]{0:T(128)} %bitcast.10.place_ref, bf16[128,1024]{1,0:T(8,128)(2,1)S(1)} %get-tuple-element.33.refs_0_, bf16[128,1024]{1,0:T(8,128)(2,1)S(1)} %collective-permute-done.2.refs_1_, bf16[128,1024]{1,0:T(8,128)(2,1)S(1)} %collective-permute-done.1.refs_2_, ...), custom_call_target="tpu_custom_call" | custom-call | flops 96636764160 | bytes 9961472 | tf_op jit(solution)/shard_map/pallas_call | solution.py:176
  64.7 4.8 %all-to-all-start.1 = ((bf16[16,3,32,512]{3,2,1,0:T(8,128)(2,1)}), bf16[16,3,32,512]{3,2,1,0:T(8,128)(2,1)S(1)}, u32[]{:S(2)}, u32[]{:S(2)}) async-start(bf16[16,3,32,512]{3,2,1,0:T(8,128)(2,1)} %shard_map.82), calls=%async_computation.1 | async-start | bytes 3145728 | tf_op jit(solution)/shard_map/all_to_all | solution.py:457
  69.5 39.7 %all-gather.6.cloned.1.call-done = bf16[4096,512]{1,0:T(8,128)(2,1)} async-done(((bf16[512,512]{1,0:T(8,128)(2,1)}), bf16[4096,512]{1,0:T(8,128)(2,1)}) %all-gather.6.cloned.1.call-update) | async-done | bytes 4194320 | tf_op jit(solution)/shard_map/all_gather | solution.py:453
  109.2 3.7 %shard_map.83 = bf16[2,4,4,32,256]{4,3,2,1,0:T(8,128)(2,1)} custom-call(bf16[16,3,32,512]{3,2,1,0:T(8,128)(2,1)S(1)} %all-to-all-done.1.refs_0_, f32[16,32,128]{2,1,0:T(8,128)S(1)} %all-to-all-done.refs_1_, f32[3,3,32,128]{3,2,1,0:T(8,128)S(1)} %broadcast_in_dim.7.refs_2_, f32[32,128]{1,0:T(8,128)S(1)} %broadcast_in_dim.8.refs_3_, f32[128,256]{1,0:T(8,128)S(1)} %copy-done.2, ...), custom_call_target="tpu_custom_call" | custom-call | flops 1000000000 | bytes 4194304 | tf_op jit(solution)/shard_map/pallas_call | solution.py:341
  113.0 4.6 %all-to-all-start.2 = ((bf16[32,32,256]{2,1,0:T(8,128)(2,1)}), bf16[32,32,256]{2,1,0:T(8,128)(2,1)S(1)}, u32[]{:S(2)}, u32[]{:S(2)}) async-start(bf16[32,32,256]{2,1,0:T(8,128)(2,1)} %bitcast.23), calls=%async_computation.2 | async-start | bytes 1048576 | tf_op jit(solution)/shard_map/all_to_all | solution.py:462
  117.7 14.4 %all-to-all-done.2 = bf16[32,32,256]{2,1,0:T(8,128)(2,1)S(1)} async-done(((bf16[32,32,256]{2,1,0:T(8,128)(2,1)}), bf16[32,32,256]{2,1,0:T(8,128)(2,1)S(1)}, u32[]{:S(2)}, u32[]{:S(2)}) %all-to-all-start.2) | async-done | bytes 524320 | tf_op jit(solution)/shard_map/all_to_all | solution.py:462
  132.1 3.6 %shard_map.84 = (bf16[64,2048]{1,0:T(8,128)(2,1)S(1)}, bf16[64,2048]{1,0:T(8,128)(2,1)S(1)}, bf16[64,2048]{1,0:T(8,128)(2,1)S(1)}, bf16[64,2048]{1,0:T(8,128)(2,1)S(1)}) custom-call(s32[4]{0:T(128)S(1)} %pad_add_fusion.block_ref, bf16[2,512,256]{2,1,0:T(8,128)(2,1)S(1)} %bitcast.33, bf16[4,2,512,512]{3,2,1,0:T(8,128)(2,1)} %bitcast.34), custom_call_target="tpu_custom_call" | custom-call | flops 1073741824 | bytes 5767168 | tf_op jit(solution)/shard_map/pallas_call | solution.py:395
  135.7 2.6 %collective-permute-start.8 = (bf16[64,2048]{1,0:T(8,128)(2,1)S(1)}, bf16[64,2048]{1,0:T(8,128)(2,1)S(1)}, u32[]{:S(2)}, u32[]{:S(2)}) collective-permute-start(bf16[64,2048]{1,0:T(8,128)(2,1)S(1)} %get-tuple-element.47), channel_id=1, source_target_pairs={{0,0},{1,16},{2,2},{3,18},{4,4},{5,20},{6,6},{7,22},{8,24},{9,8},{... | collective-permute-start | bytes 786440 | tf_op jit(solution)/shard_map/ppermute | solution.py:88
  138.3 3.9 %collective-permute-start.10 = (bf16[64,2048]{1,0:T(8,128)(2,1)S(1)}, bf16[64,2048]{1,0:T(8,128)(2,1)S(1)}, u32[]{:S(2)}, u32[]{:S(2)}) collective-permute-start(bf16[64,2048]{1,0:T(8,128)(2,1)S(1)} %get-tuple-element.49), channel_id=1, source_target_pairs={{0,16},{1,0},{2,18},{3,2},{4,20},{5,4},{6,22},{7,6},{8,8},{9,24},{... | collective-permute-start | bytes 786440 | tf_op jit(solution)/shard_map/ppermute | solution.py:88
  142.2 2.3 %collective-permute-start.11 = (bf16[64,2048]{1,0:T(8,128)(2,1)S(1)}, bf16[64,2048]{1,0:T(8,128)(2,1)S(1)}, u32[]{:S(2)}, u32[]{:S(2)}) collective-permute-start(bf16[64,2048]{1,0:T(8,128)(2,1)S(1)} %get-tuple-element.50), channel_id=1, source_target_pairs={{0,24},{1,8},{2,26},{3,10},{4,28},{5,12},{6,30},{7,14},{8,0},{9,16... | collective-permute-start | bytes 786440 | tf_op jit(solution)/shard_map/ppermute | solution.py:88
  144.6 3.2 %collective-permute-done.8.refs_0_ = bf16[64,2048]{1,0:T(8,128)(2,1)S(1)} collective-permute-done((bf16[64,2048]{1,0:T(8,128)(2,1)S(1)}, bf16[64,2048]{1,0:T(8,128)(2,1)S(1)}, u32[]{:S(2)}, u32[]{:S(2)}) %collective-permute-start.8) | collective-permute-done | bytes 262176 | tf_op jit(solution)/shard_map/ppermute | solution.py:88
  147.8 16.4 %collective-permute-done.9.refs_1_ = bf16[64,2048]{1,0:T(8,128)(2,1)S(1)} collective-permute-done((bf16[64,2048]{1,0:T(8,128)(2,1)S(1)}, bf16[64,2048]{1,0:T(8,128)(2,1)S(1)}, u32[]{:S(2)}, u32[]{:S(2)}) %collective-permute-start.9) | collective-permute-done | bytes 262176 | tf_op jit(solution)/shard_map/ppermute | solution.py:88
  164.2 1.5 shard_map.85
  (39 shorter events, 7.7 us)
Async XLA Ops:
  6.5 18.1 %copy-start = (f32[3,3,512]{2,1,0:T(4,128)S(1)}, f32[3,3,512]{2,1,0:T(4,128)}, u32[]{:S(2)}) copy-start(f32[3,3,512]{2,1,0:T(4,128)} %param.10) | copy-start | bytes 55300
  6.5 1.2 copy-start.3
  6.5 51.3 %all-gather.4.cloned.1.call-start = ((), (), s32[]{:S(2)}) async-start(), calls=%async_computation.3 | async-start | bytes 7864320 | tf_op jit(solution)/shard_map/all_gather | solution.py:433
  7.8 0.9 copy-start.4
  7.9 13.7 %collective-permute-start = (bf16[2,128,1024]{2,1,0:T(8,128)(2,1)S(1)}, bf16[2,128,1024]{2,1,0:T(8,128)(2,1)S(1)}, u32[]{:S(2)}, u32[]{:S(2)}) collective-permute-start(bf16[2,128,1024]{2,1,0:T(8,128)(2,1)S(1)} %pad_maximum_fusion.1), channel_id=1, source_target_pairs={{0,1},{1,0},{2,3},{3,2},{4,5},{5,4},{6,7},{7,6},{8,9},{9,8},{10,11... | collective-permute-start | bytes 1572872 | tf_op jit(solution)/shard_map/ppermute | solution.py:107
  9.6 15.2 %all-to-all-start = ((f32[16,32,128]{2,1,0:T(8,128)}), f32[16,32,128]{2,1,0:T(8,128)S(1)}, u32[]{:S(2)}, u32[]{:S(2)}) async-start(f32[16,32,128]{2,1,0:T(8,128)} %bitcast.16), calls=%async_computation | async-start | bytes 524288 | tf_op jit(solution)/shard_map/all_to_all | solution.py:439
  15.8 93.4 %all-gather.6.cloned.1.call-start = ((), (), s32[]{:S(2)}) async-start(), calls=%async_computation.4 | async-start | bytes 4718592 | tf_op jit(solution)/shard_map/all_gather | solution.py:453
  21.8 8.0 %collective-permute-start.1 = (bf16[128,1024]{1,0:T(8,128)(2,1)S(1)}, bf16[128,1024]{1,0:T(8,128)(2,1)S(1)}, u32[]{:S(2)}, u32[]{:S(2)}) collective-permute-start(bf16[128,1024]{1,0:T(8,128)(2,1)S(1)} %get-tuple-element.52), channel_id=1, source_target_pairs={{0,8},{2,10},{4,12},{6,14},{8,16},{10,18},{12,20},{14,22},{16,24},... | collective-permute-start | bytes 786440 | tf_op jit(solution)/shard_map/ppermute | solution.py:124
  23.4 6.9 %collective-permute-start.2 = (bf16[128,1024]{1,0:T(8,128)(2,1)S(1)}, bf16[128,1024]{1,0:T(8,128)(2,1)S(1)}, u32[]{:S(2)}, u32[]{:S(2)}) collective-permute-start(bf16[128,1024]{1,0:T(8,128)(2,1)S(1)} %get-tuple-element.33.refs_0_), channel_id=1, source_target_pairs={{0,1},{1,0},{2,3},{3,2},{4,5},{5,4},{6,7},{7,6},{8,9},{9,8},{10,11... | collective-permute-start | bytes 786440 | tf_op jit(solution)/shard_map/ppermute | solution.py:133
  25.0 16.5 %collective-permute-start.6 = (bf16[128,1024]{1,0:T(8,128)(2,1)S(1)}, bf16[128,1024]{1,0:T(8,128)(2,1)S(1)}, u32[]{:S(2)}, u32[]{:S(2)}) collective-permute-start(bf16[128,1024]{1,0:T(8,128)(2,1)S(1)} %dynamic-slice_bitcast_fusion), channel_id=1, source_target_pairs={{0,24},{2,26},{4,28},{6,30},{8,0},{10,2},{12,4},{14,6},{16,8},{18,... | collective-permute-start | bytes 786440 | tf_op jit(solution)/shard_map/ppermute | solution.py:124
  30.3 14.6 %collective-permute-start.4 = (bf16[128,1024]{1,0:T(8,128)(2,1)S(1)}, bf16[128,1024]{1,0:T(8,128)(2,1)S(1)}, u32[]{:S(2)}, u32[]{:S(2)}) collective-permute-start(bf16[128,1024]{1,0:T(8,128)(2,1)S(1)} %dynamic-slice_bitcast_fusion.1), channel_id=1, source_target_pairs={{0,16},{2,18},{4,20},{6,22},{8,24},{10,26},{12,28},{14,30},{16,0},... | collective-permute-start | bytes 786440 | tf_op jit(solution)/shard_map/ppermute | solution.py:124
  36.6 14.1 %collective-permute-start.3 = (bf16[128,1024]{1,0:T(8,128)(2,1)S(1)}, bf16[128,1024]{1,0:T(8,128)(2,1)S(1)}, u32[]{:S(2)}, u32[]{:S(2)}) collective-permute-start(bf16[128,1024]{1,0:T(8,128)(2,1)S(1)} %collective-permute-done.1.refs_2_), channel_id=1, source_target_pairs={{0,1},{1,0},{2,3},{3,2},{4,5},{5,4},{6,7},{7,6},{8,9},{9,8},{10,11... | collective-permute-start | bytes 786440 | tf_op jit(solution)/shard_map/ppermute | solution.py:133
  41.5 9.2 %collective-permute-start.7 = (bf16[128,1024]{1,0:T(8,128)(2,1)S(1)}, bf16[128,1024]{1,0:T(8,128)(2,1)S(1)}, u32[]{:S(2)}, u32[]{:S(2)}) collective-permute-start(bf16[128,1024]{1,0:T(8,128)(2,1)S(1)} %collective-permute-done.6.refs_6_), channel_id=1, source_target_pairs={{0,1},{1,0},{2,3},{3,2},{4,5},{5,4},{6,7},{7,6},{8,9},{9,8},{10,11... | collective-permute-start | bytes 786440 | tf_op jit(solution)/shard_map/ppermute | solution.py:133
  45.0 9.3 %collective-permute-start.5 = (bf16[128,1024]{1,0:T(8,128)(2,1)S(1)}, bf16[128,1024]{1,0:T(8,128)(2,1)S(1)}, u32[]{:S(2)}, u32[]{:S(2)}) collective-permute-start(bf16[128,1024]{1,0:T(8,128)(2,1)S(1)} %collective-permute-done.4.refs_4_), channel_id=1, source_target_pairs={{0,1},{1,0},{2,3},{3,2},{4,5},{5,4},{6,7},{7,6},{8,9},{9,8},{10,11... | collective-permute-start | bytes 786440 | tf_op jit(solution)/shard_map/ppermute | solution.py:133
  64.7 44.5 %copy-start.1 = (f32[256,256]{1,0:T(8,128)S(1)}, f32[256,256]{1,0:T(8,128)}, u32[]{:S(2)}) copy-start(f32[256,256]{1,0:T(8,128)} %constant.234.clone.refs_5_) | copy-start | bytes 786436
  64.7 44.5 %copy-start.2 = (f32[128,256]{1,0:T(8,128)S(1)}, f32[128,256]{1,0:T(8,128)}, u32[]{:S(2)}) copy-start(f32[128,256]{1,0:T(8,128)} %constant.233.clone.refs_4_) | copy-start | bytes 393220
  64.7 44.5 %all-to-all-start.1 = ((bf16[16,3,32,512]{3,2,1,0:T(8,128)(2,1)}), bf16[16,3,32,512]{3,2,1,0:T(8,128)(2,1)S(1)}, u32[]{:S(2)}, u32[]{:S(2)}) async-start(bf16[16,3,32,512]{3,2,1,0:T(8,128)(2,1)} %shard_map.82), calls=%async_computation.1 | async-start | bytes 3145728 | tf_op jit(solution)/shard_map/all_to_all | solution.py:457
  113.0 19.1 %all-to-all-start.2 = ((bf16[32,32,256]{2,1,0:T(8,128)(2,1)}), bf16[32,32,256]{2,1,0:T(8,128)(2,1)S(1)}, u32[]{:S(2)}, u32[]{:S(2)}) async-start(bf16[32,32,256]{2,1,0:T(8,128)(2,1)} %bitcast.23), calls=%async_computation.2 | async-start | bytes 1048576 | tf_op jit(solution)/shard_map/all_to_all | solution.py:462
  135.7 12.1 %collective-permute-start.8 = (bf16[64,2048]{1,0:T(8,128)(2,1)S(1)}, bf16[64,2048]{1,0:T(8,128)(2,1)S(1)}, u32[]{:S(2)}, u32[]{:S(2)}) collective-permute-start(bf16[64,2048]{1,0:T(8,128)(2,1)S(1)} %get-tuple-element.47), channel_id=1, source_target_pairs={{0,0},{1,16},{2,2},{3,18},{4,4},{5,20},{6,6},{7,22},{8,24},{9,8},{... | collective-permute-start | bytes 786440 | tf_op jit(solution)/shard_map/ppermute | solution.py:88
  138.3 25.9 %collective-permute-start.9 = (bf16[64,2048]{1,0:T(8,128)(2,1)S(1)}, bf16[64,2048]{1,0:T(8,128)(2,1)S(1)}, u32[]{:S(2)}, u32[]{:S(2)}) collective-permute-start(bf16[64,2048]{1,0:T(8,128)(2,1)S(1)} %get-tuple-element.48), channel_id=1, source_target_pairs={{0,8},{1,24},{2,10},{3,26},{4,12},{5,28},{6,14},{7,30},{8,16},{9,0... | collective-permute-start | bytes 786440 | tf_op jit(solution)/shard_map/ppermute | solution.py:88
  138.3 25.8 %collective-permute-start.10 = (bf16[64,2048]{1,0:T(8,128)(2,1)S(1)}, bf16[64,2048]{1,0:T(8,128)(2,1)S(1)}, u32[]{:S(2)}, u32[]{:S(2)}) collective-permute-start(bf16[64,2048]{1,0:T(8,128)(2,1)S(1)} %get-tuple-element.49), channel_id=1, source_target_pairs={{0,16},{1,0},{2,18},{3,2},{4,20},{5,4},{6,22},{7,6},{8,8},{9,24},{... | collective-permute-start | bytes 786440 | tf_op jit(solution)/shard_map/ppermute | solution.py:88
  142.2 22.0 %collective-permute-start.11 = (bf16[64,2048]{1,0:T(8,128)(2,1)S(1)}, bf16[64,2048]{1,0:T(8,128)(2,1)S(1)}, u32[]{:S(2)}, u32[]{:S(2)}) collective-permute-start(bf16[64,2048]{1,0:T(8,128)(2,1)S(1)} %get-tuple-element.50), channel_id=1, source_target_pairs={{0,24},{1,8},{2,26},{3,10},{4,28},{5,12},{6,30},{7,14},{8,0},{9,16... | collective-permute-start | bytes 786440 | tf_op jit(solution)/shard_map/ppermute | solution.py:88
Sparse Core Ops, SparseCore 0:
  8.9 48.8 all-gather.3
  59.7 49.4 all-gather.5

commit v17 on v16

--- a/solution.py
+++ b/solution.py
@@ -456,8 +456,6 @@
     partial = project_in(chunks, weight, seq_parts)
     parts = lax.all_to_all(partial, "seq", split_axis=0, concat_axis=0, tiled=True)
 
-    parts, out_weight = lax.optimization_barrier((parts, out_weight))
-
     gated = convolve([parts], filter_blocks, taps, skip, outer, tp_parts)
     gated = lax.all_to_all(
         gated.reshape((-1,) + gated.shape[3:]), ("tp", "seq"), split_axis=0, concat_axis=0, tiled=True

time: 173 us -> 168 us (0.971)
  blocking collectives: 0 us -> 40.7 us
  waiting for transfers between devices: 103 us -> 63.1 us
  starting transfers between devices: 37.2 us -> 32.6 us
    all_to_all x0 -> x1, blocking collectives: none -> 40.7 us  [per_device(): lax.all_to_all(partial, 'seq', split_axis=0, concat_axis=0, tiled=True)]
    all_gather x1, waiting for transfers between devices: 39.7 us -> 0.01 us  [per_device(): lax.all_gather(out_proj, ('seq', 'tp'), axis_index_groups=tp_groups)]
    all_to_all x1 -> x0, starting transfers between devices: 4.76 us -> none  [per_device(): lax.all_to_all(partial, 'seq', split_axis=0, concat_axis=0, tiled=True)]
  transfers between devices with their start and end apart: 17 -> 16, of which waited for: 12 -> 11; matrix products, arithmetic and copies ran while one was open for 1% -> 1% of each run, Pallas kernels for 4% -> 6%
where the time goes in v17:
time: 168 us
  waiting for transfers between devices  63.1 us (38%)
  blocking collectives  40.7 us (24%)
  starting transfers between devices  32.6 us (19%)
  Pallas kernels  14.5 us (9%)
  between operations  13.8 us (8%)
  local copies, waits for them, and re-layouts  2.81 us (2%)
    all_to_all x1, blocking collectives, per_device(): lax.all_to_all(partial, 'seq', split_axis=0, concat_axis=0, tiled=True)  40.7 us
    ppermute x4, waiting for transfers between devices, return_output(): arrived.append(lax.ppermute(piece, ('seq', 'tp'), pairs))  19.5 us
    all_to_all x1, waiting for transfers between devices, per_device(): lax.all_to_all(gated.reshape((-1,) + gated.shape[3:]), ('tp', 'seq'), spl...  14.4 us
    ppermute x3, waiting for transfers between devices, cross_outer(): lax.ppermute(piece, 'seq', [(i, (i + far) % seq_parts) for i in range(seq...  10.5 us
    ppermute x3, starting transfers between devices, cross_outer(): lax.ppermute(piece, 'seq', [(i, (i + far) % seq_parts) for i in range(seq...  9.2 us
    ppermute x4, starting transfers between devices, return_output(): arrived.append(lax.ppermute(piece, ('seq', 'tp'), pairs))  8.85 us
    ppermute x4, waiting for transfers between devices, share_over_tp(): pieces.append(lax.ppermute(part, 'tp', pairs))  8.77 us
    all_to_all x1, starting transfers between devices, per_device(): lax.all_to_all(long_filter.T.reshape(seq_parts, chans, rows), 'seq', spli...  6.27 us
  transfers between devices with their start and end apart: 16, of which 11 were waited for; matrix products, arithmetic and copies ran while one was open for 1% of the time, Pallas kernels for 6%

profile of v17, /device:TPU:12, one launch (start us, length us, event | category | flops | bytes accessed | tf_op | source)
XLA Modules:
  0.0 167.8 jit_solution(8003088453791103069)
XLA Ops:
  9.6 6.3 %all-to-all-start = ((f32[16,32,128]{2,1,0:T(8,128)}), f32[16,32,128]{2,1,0:T(8,128)S(1)}, u32[]{:S(2)}, u32[]{:S(2)}) async-start(f32[16,32,128]{2,1,0:T(8,128)} %bitcast.16), calls=%async_computation | async-start | bytes 524288 | tf_op jit(solution)/shard_map/all_to_all | solution.py:439
  16.0 5.6 %collective-permute-done = bf16[2,128,1024]{2,1,0:T(8,128)(2,1)S(1)} collective-permute-done((bf16[2,128,1024]{2,1,0:T(8,128)(2,1)S(1)}, bf16[2,128,1024]{2,1,0:T(8,128)(2,1)S(1)}, u32[]{:S(2)}, u32[]{:S(2)}) %collective-permute-start) | collective-permute-done | bytes 524320 | tf_op jit(solution)/shard_map/ppermute | solution.py:107
  21.8 1.6 collective-permute-start.1
  25.0 1.3 collective-permute-start.6
  26.2 3.6 %collective-permute-done.1.refs_2_ = bf16[128,1024]{1,0:T(8,128)(2,1)S(1)} collective-permute-done((bf16[128,1024]{1,0:T(8,128)(2,1)S(1)}, bf16[128,1024]{1,0:T(8,128)(2,1)S(1)}, u32[]{:S(2)}, u32[]{:S(2)}) %collective-permute-start.1) | collective-permute-done | bytes 262176 | tf_op jit(solution)/shard_map/ppermute | solution.py:124
  30.3 6.3 %collective-permute-start.4 = (bf16[128,1024]{1,0:T(8,128)(2,1)S(1)}, bf16[128,1024]{1,0:T(8,128)(2,1)S(1)}, u32[]{:S(2)}, u32[]{:S(2)}) collective-permute-start(bf16[128,1024]{1,0:T(8,128)(2,1)S(1)} %dynamic-slice_bitcast_fusion.1), channel_id=1, source_target_pairs={{0,16},{2,18},{4,20},{6,22},{8,24},{10,26},{12,28},{14,30},{16,0},... | collective-permute-start | bytes 786440 | tf_op jit(solution)/shard_map/ppermute | solution.py:124
  36.6 1.5 collective-permute-start.3
  38.1 3.4 %collective-permute-done.6.refs_6_ = bf16[128,1024]{1,0:T(8,128)(2,1)S(1)} collective-permute-done((bf16[128,1024]{1,0:T(8,128)(2,1)S(1)}, bf16[128,1024]{1,0:T(8,128)(2,1)S(1)}, u32[]{:S(2)}, u32[]{:S(2)}) %collective-permute-start.6) | collective-permute-done | bytes 262176 | tf_op jit(solution)/shard_map/ppermute | solution.py:124
  41.5 3.5 %collective-permute-done.4.refs_4_ = bf16[128,1024]{1,0:T(8,128)(2,1)S(1)} collective-permute-done((bf16[128,1024]{1,0:T(8,128)(2,1)S(1)}, bf16[128,1024]{1,0:T(8,128)(2,1)S(1)}, u32[]{:S(2)}, u32[]{:S(2)}) %collective-permute-start.4) | collective-permute-done | bytes 262176 | tf_op jit(solution)/shard_map/ppermute | solution.py:124
  46.0 4.7 %collective-permute-done.7.refs_7_ = bf16[128,1024]{1,0:T(8,128)(2,1)S(1)} collective-permute-done((bf16[128,1024]{1,0:T(8,128)(2,1)S(1)}, bf16[128,1024]{1,0:T(8,128)(2,1)S(1)}, u32[]{:S(2)}, u32[]{:S(2)}) %collective-permute-start.7) | collective-permute-done | bytes 262176 | tf_op jit(solution)/shard_map/ppermute | solution.py:133
  50.7 3.5 %collective-permute-done.5.refs_5_ = bf16[128,1024]{1,0:T(8,128)(2,1)S(1)} collective-permute-done((bf16[128,1024]{1,0:T(8,128)(2,1)S(1)}, bf16[128,1024]{1,0:T(8,128)(2,1)S(1)}, u32[]{:S(2)}, u32[]{:S(2)}) %collective-permute-start.5) | collective-permute-done | bytes 262176 | tf_op jit(solution)/shard_map/ppermute | solution.py:133
  54.3 3.6 %all-gather.4.cloned.1.call-done = bf16[3,2048,512]{2,1,0:T(8,128)(2,1)} async-done(((bf16[3,512,512]{2,1,0:T(8,128)(2,1)}), bf16[3,2048,512]{2,1,0:T(8,128)(2,1)}) %all-gather.4.cloned.1.call-update) | async-done | bytes 6291472 | tf_op jit(solution)/shard_map/all_gather | solution.py:433
  57.9 5.7 %shard_map.82 = bf16[16,3,32,512]{3,2,1,0:T(8,128)(2,1)S(1)} custom-call(s32[1]{0:T(128)} %bitcast.10.place_ref, bf16[128,1024]{1,0:T(8,128)(2,1)S(1)} %get-tuple-element.31.refs_0_, bf16[128,1024]{1,0:T(8,128)(2,1)S(1)} %collective-permute-done.2.refs_1_, bf16[128,1024]{1,0:T(8,128)(2,1)S(1)} %collective-permute-done.1.refs_2_, ...), custom_call_target="tpu_custom_call" | custom-call | flops 96636764160 | bytes 9961472 | tf_op jit(solution)/shard_map/pallas_call | solution.py:176
  63.6 40.7 %all_to_all.15.refs_0_ = bf16[16,3,32,512]{3,2,1,0:T(8,128)(2,1)S(1)} all-to-all(bf16[16,3,32,512]{3,2,1,0:T(8,128)(2,1)S(1)} %shard_map.82), channel_id=1, replica_groups=mesh['seq'=16,'tp'=2] {'seq'}, dimensions={0} | all-to-all | bytes 3145728 | tf_op jit(solution)/shard_map/all_to_all | solution.py:457
  104.3 3.7 %shard_map.83 = bf16[2,4,4,32,256]{4,3,2,1,0:T(8,128)(2,1)} custom-call(bf16[16,3,32,512]{3,2,1,0:T(8,128)(2,1)S(1)} %all_to_all.15.refs_0_, f32[16,32,128]{2,1,0:T(8,128)S(1)} %all-to-all-done.refs_1_, f32[3,3,32,128]{3,2,1,0:T(8,128)S(1)} %broadcast_in_dim.7.refs_2_, f32[32,128]{1,0:T(8,128)S(1)} %broadcast_in_dim.8.refs_3_, f32[128,256]{1,0:T(8,128)S(1)} %copy-done.2, ...), custom_call_target="tpu_custom_call" | custom-call | flops 1000000000 | bytes 4194304 | tf_op jit(solution)/shard_map/pallas_call | solution.py:341
  108.0 4.7 %all-to-all-start.2 = ((bf16[32,32,256]{2,1,0:T(8,128)(2,1)}), bf16[32,32,256]{2,1,0:T(8,128)(2,1)S(1)}, u32[]{:S(2)}, u32[]{:S(2)}) async-start(bf16[32,32,256]{2,1,0:T(8,128)(2,1)} %bitcast.22), calls=%async_computation.2 | async-start | bytes 1048576 | tf_op jit(solution)/shard_map/all_to_all | solution.py:460
  112.9 14.4 %all-to-all-done.2 = bf16[32,32,256]{2,1,0:T(8,128)(2,1)S(1)} async-done(((bf16[32,32,256]{2,1,0:T(8,128)(2,1)}), bf16[32,32,256]{2,1,0:T(8,128)(2,1)S(1)}, u32[]{:S(2)}, u32[]{:S(2)}) %all-to-all-start.2) | async-done | bytes 524320 | tf_op jit(solution)/shard_map/all_to_all | solution.py:460
  127.3 3.6 %shard_map.84 = (bf16[64,2048]{1,0:T(8,128)(2,1)S(1)}, bf16[64,2048]{1,0:T(8,128)(2,1)S(1)}, bf16[64,2048]{1,0:T(8,128)(2,1)S(1)}, bf16[64,2048]{1,0:T(8,128)(2,1)S(1)}) custom-call(s32[4]{0:T(128)S(1)} %pad_add_fusion.block_ref, bf16[2,512,256]{2,1,0:T(8,128)(2,1)S(1)} %bitcast.33, bf16[4,2,512,512]{3,2,1,0:T(8,128)(2,1)} %bitcast.34), custom_call_target="tpu_custom_call" | custom-call | flops 1073741824 | bytes 5767168 | tf_op jit(solution)/shard_map/pallas_call | solution.py:395
  130.8 2.6 %collective-permute-start.8 = (bf16[64,2048]{1,0:T(8,128)(2,1)S(1)}, bf16[64,2048]{1,0:T(8,128)(2,1)S(1)}, u32[]{:S(2)}, u32[]{:S(2)}) collective-permute-start(bf16[64,2048]{1,0:T(8,128)(2,1)S(1)} %get-tuple-element.43), channel_id=1, source_target_pairs={{0,0},{1,16},{2,2},{3,18},{4,4},{5,20},{6,6},{7,22},{8,24},{9,8},{... | collective-permute-start | bytes 786440 | tf_op jit(solution)/shard_map/ppermute | solution.py:88
  133.5 3.9 %collective-permute-start.10 = (bf16[64,2048]{1,0:T(8,128)(2,1)S(1)}, bf16[64,2048]{1,0:T(8,128)(2,1)S(1)}, u32[]{:S(2)}, u32[]{:S(2)}) collective-permute-start(bf16[64,2048]{1,0:T(8,128)(2,1)S(1)} %get-tuple-element.45), channel_id=1, source_target_pairs={{0,16},{1,0},{2,18},{3,2},{4,20},{5,4},{6,22},{7,6},{8,8},{9,24},{... | collective-permute-start | bytes 786440 | tf_op jit(solution)/shard_map/ppermute | solution.py:88
  137.4 2.3 %collective-permute-start.11 = (bf16[64,2048]{1,0:T(8,128)(2,1)S(1)}, bf16[64,2048]{1,0:T(8,128)(2,1)S(1)}, u32[]{:S(2)}, u32[]{:S(2)}) collective-permute-start(bf16[64,2048]{1,0:T(8,128)(2,1)S(1)} %get-tuple-element.46), channel_id=1, source_target_pairs={{0,24},{1,8},{2,26},{3,10},{4,28},{5,12},{6,30},{7,14},{8,0},{9,16... | collective-permute-start | bytes 786440 | tf_op jit(solution)/shard_map/ppermute | solution.py:88
  139.8 3.2 %collective-permute-done.8.refs_0_ = bf16[64,2048]{1,0:T(8,128)(2,1)S(1)} collective-permute-done((bf16[64,2048]{1,0:T(8,128)(2,1)S(1)}, bf16[64,2048]{1,0:T(8,128)(2,1)S(1)}, u32[]{:S(2)}, u32[]{:S(2)}) %collective-permute-start.8) | collective-permute-done | bytes 262176 | tf_op jit(solution)/shard_map/ppermute | solution.py:88
  143.0 16.4 %collective-permute-done.9.refs_1_ = bf16[64,2048]{1,0:T(8,128)(2,1)S(1)} collective-permute-done((bf16[64,2048]{1,0:T(8,128)(2,1)S(1)}, bf16[64,2048]{1,0:T(8,128)(2,1)S(1)}, u32[]{:S(2)}, u32[]{:S(2)}) %collective-permute-start.9) | collective-permute-done | bytes 262176 | tf_op jit(solution)/shard_map/ppermute | solution.py:88
  159.4 1.5 shard_map.85
  (38 shorter events, 6.5 us)
Async XLA Ops:
  6.5 18.1 %copy-start = (f32[3,3,512]{2,1,0:T(4,128)S(1)}, f32[3,3,512]{2,1,0:T(4,128)}, u32[]{:S(2)}) copy-start(f32[3,3,512]{2,1,0:T(4,128)} %param.10) | copy-start | bytes 55300
  6.5 1.2 copy-start.3
  6.5 51.3 %all-gather.4.cloned.1.call-start = ((), (), s32[]{:S(2)}) async-start(), calls=%async_computation.3 | async-start | bytes 7864320 | tf_op jit(solution)/shard_map/all_gather | solution.py:433
  7.8 0.9 copy-start.4
  7.9 13.7 %collective-permute-start = (bf16[2,128,1024]{2,1,0:T(8,128)(2,1)S(1)}, bf16[2,128,1024]{2,1,0:T(8,128)(2,1)S(1)}, u32[]{:S(2)}, u32[]{:S(2)}) collective-permute-start(bf16[2,128,1024]{2,1,0:T(8,128)(2,1)S(1)} %pad_maximum_fusion.1), channel_id=1, source_target_pairs={{0,1},{1,0},{2,3},{3,2},{4,5},{5,4},{6,7},{7,6},{8,9},{9,8},{10,11... | collective-permute-start | bytes 1572872 | tf_op jit(solution)/shard_map/ppermute | solution.py:107
  9.6 15.2 %all-to-all-start = ((f32[16,32,128]{2,1,0:T(8,128)}), f32[16,32,128]{2,1,0:T(8,128)S(1)}, u32[]{:S(2)}, u32[]{:S(2)}) async-start(f32[16,32,128]{2,1,0:T(8,128)} %bitcast.16), calls=%async_computation | async-start | bytes 524288 | tf_op jit(solution)/shard_map/all_to_all | solution.py:439
  15.8 97.0 %all-gather.6.cloned.1.call-start = ((), (), s32[]{:S(2)}) async-start(), calls=%async_computation.4 | async-start | bytes 4718592 | tf_op jit(solution)/shard_map/all_gather | solution.py:453
  21.8 8.0 %collective-permute-start.1 = (bf16[128,1024]{1,0:T(8,128)(2,1)S(1)}, bf16[128,1024]{1,0:T(8,128)(2,1)S(1)}, u32[]{:S(2)}, u32[]{:S(2)}) collective-permute-start(bf16[128,1024]{1,0:T(8,128)(2,1)S(1)} %get-tuple-element.48), channel_id=1, source_target_pairs={{0,8},{2,10},{4,12},{6,14},{8,16},{10,18},{12,20},{14,22},{16,24},... | collective-permute-start | bytes 786440 | tf_op jit(solution)/shard_map/ppermute | solution.py:124
  23.4 6.9 %collective-permute-start.2 = (bf16[128,1024]{1,0:T(8,128)(2,1)S(1)}, bf16[128,1024]{1,0:T(8,128)(2,1)S(1)}, u32[]{:S(2)}, u32[]{:S(2)}) collective-permute-start(bf16[128,1024]{1,0:T(8,128)(2,1)S(1)} %get-tuple-element.31.refs_0_), channel_id=1, source_target_pairs={{0,1},{1,0},{2,3},{3,2},{4,5},{5,4},{6,7},{7,6},{8,9},{9,8},{10,11... | collective-permute-start | bytes 786440 | tf_op jit(solution)/shard_map/ppermute | solution.py:133
  25.0 16.5 %collective-permute-start.6 = (bf16[128,1024]{1,0:T(8,128)(2,1)S(1)}, bf16[128,1024]{1,0:T(8,128)(2,1)S(1)}, u32[]{:S(2)}, u32[]{:S(2)}) collective-permute-start(bf16[128,1024]{1,0:T(8,128)(2,1)S(1)} %dynamic-slice_bitcast_fusion), channel_id=1, source_target_pairs={{0,24},{2,26},{4,28},{6,30},{8,0},{10,2},{12,4},{14,6},{16,8},{18,... | collective-permute-start | bytes 786440 | tf_op jit(solution)/shard_map/ppermute | solution.py:124
  30.3 14.6 %collective-permute-start.4 = (bf16[128,1024]{1,0:T(8,128)(2,1)S(1)}, bf16[128,1024]{1,0:T(8,128)(2,1)S(1)}, u32[]{:S(2)}, u32[]{:S(2)}) collective-permute-start(bf16[128,1024]{1,0:T(8,128)(2,1)S(1)} %dynamic-slice_bitcast_fusion.1), channel_id=1, source_target_pairs={{0,16},{2,18},{4,20},{6,22},{8,24},{10,26},{12,28},{14,30},{16,0},... | collective-permute-start | bytes 786440 | tf_op jit(solution)/shard_map/ppermute | solution.py:124
  36.6 14.1 %collective-permute-start.3 = (bf16[128,1024]{1,0:T(8,128)(2,1)S(1)}, bf16[128,1024]{1,0:T(8,128)(2,1)S(1)}, u32[]{:S(2)}, u32[]{:S(2)}) collective-permute-start(bf16[128,1024]{1,0:T(8,128)(2,1)S(1)} %collective-permute-done.1.refs_2_), channel_id=1, source_target_pairs={{0,1},{1,0},{2,3},{3,2},{4,5},{5,4},{6,7},{7,6},{8,9},{9,8},{10,11... | collective-permute-start | bytes 786440 | tf_op jit(solution)/shard_map/ppermute | solution.py:133
  41.5 9.2 %collective-permute-start.7 = (bf16[128,1024]{1,0:T(8,128)(2,1)S(1)}, bf16[128,1024]{1,0:T(8,128)(2,1)S(1)}, u32[]{:S(2)}, u32[]{:S(2)}) collective-permute-start(bf16[128,1024]{1,0:T(8,128)(2,1)S(1)} %collective-permute-done.6.refs_6_), channel_id=1, source_target_pairs={{0,1},{1,0},{2,3},{3,2},{4,5},{5,4},{6,7},{7,6},{8,9},{9,8},{10,11... | collective-permute-start | bytes 786440 | tf_op jit(solution)/shard_map/ppermute | solution.py:133
  45.0 9.3 %collective-permute-start.5 = (bf16[128,1024]{1,0:T(8,128)(2,1)S(1)}, bf16[128,1024]{1,0:T(8,128)(2,1)S(1)}, u32[]{:S(2)}, u32[]{:S(2)}) collective-permute-start(bf16[128,1024]{1,0:T(8,128)(2,1)S(1)} %collective-permute-done.4.refs_4_), channel_id=1, source_target_pairs={{0,1},{1,0},{2,3},{3,2},{4,5},{5,4},{6,7},{7,6},{8,9},{9,8},{10,11... | collective-permute-start | bytes 786440 | tf_op jit(solution)/shard_map/ppermute | solution.py:133
  63.6 40.7 %copy-start.1 = (f32[256,256]{1,0:T(8,128)S(1)}, f32[256,256]{1,0:T(8,128)}, u32[]{:S(2)}) copy-start(f32[256,256]{1,0:T(8,128)} %constant.234.clone.refs_5_) | copy-start | bytes 786436
  63.6 40.7 %copy-start.2 = (f32[128,256]{1,0:T(8,128)S(1)}, f32[128,256]{1,0:T(8,128)}, u32[]{:S(2)}) copy-start(f32[128,256]{1,0:T(8,128)} %constant.233.clone.refs_4_) | copy-start | bytes 393220
  108.0 19.3 %all-to-all-start.2 = ((bf16[32,32,256]{2,1,0:T(8,128)(2,1)}), bf16[32,32,256]{2,1,0:T(8,128)(2,1)S(1)}, u32[]{:S(2)}, u32[]{:S(2)}) async-start(bf16[32,32,256]{2,1,0:T(8,128)(2,1)} %bitcast.22), calls=%async_computation.2 | async-start | bytes 1048576 | tf_op jit(solution)/shard_map/all_to_all | solution.py:460
  130.8 12.1 %collective-permute-start.8 = (bf16[64,2048]{1,0:T(8,128)(2,1)S(1)}, bf16[64,2048]{1,0:T(8,128)(2,1)S(1)}, u32[]{:S(2)}, u32[]{:S(2)}) collective-permute-start(bf16[64,2048]{1,0:T(8,128)(2,1)S(1)} %get-tuple-element.43), channel_id=1, source_target_pairs={{0,0},{1,16},{2,2},{3,18},{4,4},{5,20},{6,6},{7,22},{8,24},{9,8},{... | collective-permute-start | bytes 786440 | tf_op jit(solution)/shard_map/ppermute | solution.py:88
  133.5 25.9 %collective-permute-start.9 = (bf16[64,2048]{1,0:T(8,128)(2,1)S(1)}, bf16[64,2048]{1,0:T(8,128)(2,1)S(1)}, u32[]{:S(2)}, u32[]{:S(2)}) collective-permute-start(bf16[64,2048]{1,0:T(8,128)(2,1)S(1)} %get-tuple-element.44), channel_id=1, source_target_pairs={{0,8},{1,24},{2,10},{3,26},{4,12},{5,28},{6,14},{7,30},{8,16},{9,0... | collective-permute-start | bytes 786440 | tf_op jit(solution)/shard_map/ppermute | solution.py:88
  133.5 25.8 %collective-permute-start.10 = (bf16[64,2048]{1,0:T(8,128)(2,1)S(1)}, bf16[64,2048]{1,0:T(8,128)(2,1)S(1)}, u32[]{:S(2)}, u32[]{:S(2)}) collective-permute-start(bf16[64,2048]{1,0:T(8,128)(2,1)S(1)} %get-tuple-element.45), channel_id=1, source_target_pairs={{0,16},{1,0},{2,18},{3,2},{4,20},{5,4},{6,22},{7,6},{8,8},{9,24},{... | collective-permute-start | bytes 786440 | tf_op jit(solution)/shard_map/ppermute | solution.py:88
  137.4 22.0 %collective-permute-start.11 = (bf16[64,2048]{1,0:T(8,128)(2,1)S(1)}, bf16[64,2048]{1,0:T(8,128)(2,1)S(1)}, u32[]{:S(2)}, u32[]{:S(2)}) collective-permute-start(bf16[64,2048]{1,0:T(8,128)(2,1)S(1)} %get-tuple-element.46), channel_id=1, source_target_pairs={{0,24},{1,8},{2,26},{3,10},{4,28},{5,12},{6,30},{7,14},{8,0},{9,16... | collective-permute-start | bytes 786440 | tf_op jit(solution)/shard_map/ppermute | solution.py:88
Sparse Core Ops, SparseCore 0:
  8.9 48.8 all-gather.3
  59.7 51.3 all-gather.5

commit v18 on v17

--- a/solution.py
+++ b/solution.py
@@ -89,24 +89,25 @@
     return assemble(arrived, places, (tp_parts * part_rows, per_tp * width))
 
 
-def share_columns(features, outer, tp_parts):
-    rows, cols = features.shape
+def share_columns(features, outer, inner_parts, tp_parts):
+    _, cols = features.shape
     per_tp = outer // tp_parts
+    width = cols // outer
     tp_place = lax.axis_index("tp")
-    width = cols // outer
+    outer_place = lax.axis_index("seq") // inner_parts
     held = []
-    for step in range(tp_parts):
-        which = (tp_place + step) % tp_parts
-        piece = jnp.stack(
-            [
-                lax.dynamic_slice_in_dim(features, (group * tp_parts + which) * width, width, axis=1)
-                for group in range(per_tp)
-            ]
-        )
-        if step:
-            piece = lax.ppermute(piece, "tp", [(i, (i + step) % tp_parts) for i in range(tp_parts)])
-        held.append(piece)
-    return jnp.concatenate(held)
+    for after in range(per_tp):
+        group = (outer_place + 1 + after) % per_tp
+        pieces = []
+        for step in range(tp_parts):
+            column = (group * tp_parts + (tp_place + step) % tp_parts) * width
+            piece = lax.dynamic_slice_in_dim(features, column, width, axis=1)
+            if step:
+                pairs = [(i, (i + step) % tp_parts) for i in range(tp_parts)]
+                piece = lax.ppermute(piece, "tp", pairs)
+            pieces.append(piece)
+        held.append(jnp.stack(pieces))
+    return held
 
 
 def cross_outer(held, steps, outer, inner_parts, tp_parts):
@@ -117,8 +118,8 @@
     arrived = {}
     for step in steps:
         target = (outer_place + step) % outer
-        which = (tp_place - target // per_tp + tp_parts) % tp_parts * per_tp + target % per_tp
-        piece = lax.dynamic_index_in_dim(held, which, axis=0, keepdims=False)
+        which = (tp_place - target // per_tp + tp_parts) % tp_parts
+        piece = lax.dynamic_index_in_dim(held[(step - 1) % per_tp], which, axis=0, keepdims=False)
         if step:
             far = step * inner_parts
             piece = lax.ppermute(piece, "seq", [(i, (i + far) % seq_parts) for i in range(seq_parts)])
@@ -134,64 +135,68 @@
     return pieces
 
 
-def project_kernel(tp_parts, place_ref, *refs):
-    *share_refs, weight_ref, out_ref, held, sems = refs
+def gather_inner(block, inner_parts, settle):
+    held, masks = [block], [0]
+    bit = inner_parts // 2
+    while bit:
+        pairs = [(i, i ^ bit) for i in range(lax.axis_size("seq"))]
+        held += [lax.ppermute(piece, "seq", pairs) for piece in held]
+        masks += [mask ^ bit for mask in masks]
+        if bit == inner_parts // 2:
+            held = settle(held)
+        bit //= 2
+    return held, masks
+
+
+def project_kernel(tp_parts, masks, place_ref, *refs):
+    *refs, out_ref, left = refs
+    share_refs, weight_refs = refs[: -len(masks)], refs[-len(masks) :]
     seq_parts, streams, chans, count = out_ref.shape
-    copies = []
-    for stream in range(streams):
-        for step in range(tp_parts):
-            which = lax.rem(place_ref[0] - step + tp_parts, tp_parts)
-            copies.append(
-                pltpu.make_async_copy(
-                    weight_ref.at[stream, which], held.at[stream, step], sems.at[len(copies)]
-                )
-            )
-            copies[-1].start()
-    left = [
-        jnp.concatenate([share_ref[...] for share_ref in share_refs[step::tp_parts]])
-        for step in range(tp_parts)
-    ]
+    blocks, rows, width = len(masks) // tp_parts, share_refs[0].shape[0], left.shape[2]
+    for index, share_ref in enumerate(share_refs):
+        chunk, step = divmod(index, tp_parts)
+        for block in range(blocks):
+            left[step * blocks + block, chunk * rows : (chunk + 1) * rows] = share_ref[
+                :, block * width : (block + 1) * width
+            ]
+    slots = []
+    for mask in masks:
+        inner = jnp.bitwise_xor(place_ref[1], mask)
+        step = lax.rem(place_ref[0] - inner // blocks + tp_parts, tp_parts)
+        slots.append(step * blocks + lax.rem(inner, blocks))
     for stream in range(streams):
         sums = jnp.zeros((count, seq_parts * chans), jnp.float32)
-        for step in range(tp_parts):
-            copies[stream * tp_parts + step].wait()
-            sums = sums + jnp.dot(
-                left[step], held[stream, step], preferred_element_type=jnp.float32
-            )
+        for slot, weight_ref in zip(slots, weight_refs):
+            sums = sums + jnp.dot(left[slot], weight_ref[stream], preferred_element_type=jnp.float32)
         turned = sums.astype(out_ref.dtype).T
         for seq in range(seq_parts):
             out_ref[seq, stream] = turned[seq * chans : (seq + 1) * chans]
 
 
-def project_in(chunks, weight, seq_parts):
+def project_in(chunks, weights, masks, inner_parts, seq_parts):
     tp_parts = len(chunks[0])
-    rows, width = chunks[0][0].shape
-    streams, _, chan_tp = weight.shape
-    weight = weight.reshape(streams, tp_parts, width, chan_tp)
+    rows, _ = chunks[0][0].shape
+    streams, width, chan_tp = weights[0].shape
     chans = chan_tp // seq_parts
     pieces = [piece for chunk in chunks for piece in chunk]
     count = len(chunks) * rows
-    place = lax.axis_index("tp").astype(jnp.int32)[None]
+    place = jnp.stack([lax.axis_index("tp"), lax.axis_index("seq") % inner_parts]).astype(jnp.int32)
     vmem = pl.BlockSpec(memory_space=pltpu.VMEM)
+    size = len(weights) * weights[0].size
     return pl.pallas_call(
-        functools.partial(project_kernel, tp_parts),
-        in_specs=[pl.BlockSpec(memory_space=pltpu.SMEM)]
-        + [vmem] * len(pieces)
-        + [pl.BlockSpec(memory_space=pl.ANY)],
+        functools.partial(project_kernel, tp_parts, masks),
+        in_specs=[pl.BlockSpec(memory_space=pltpu.SMEM)] + [vmem] * (len(pieces) + len(weights)),
         out_specs=vmem,
         out_shape=jax.ShapeDtypeStruct((seq_parts, streams, chans, count), jnp.bfloat16),
-        scratch_shapes=[
-            pltpu.VMEM(weight.shape, weight.dtype),
-            pltpu.SemaphoreType.DMA((streams * tp_parts,)),
-        ],
-        compiler_params=pltpu.CompilerParams(vmem_limit_bytes=48 * 2**20),
+        scratch_shapes=[pltpu.VMEM((len(masks), count, width), jnp.bfloat16)],
+        compiler_params=pltpu.CompilerParams(vmem_limit_bytes=32 * 2**20),
         cost_estimate=pl.CostEstimate(
-            flops=HEAVY * 2 * count * weight.size,
-            bytes_accessed=2 * (weight.size + len(pieces) * pieces[0].size)
+            flops=HEAVY * 2 * count * size,
+            bytes_accessed=2 * (size + len(pieces) * pieces[0].size)
             + 2 * streams * count * seq_parts * chans,
             transcendentals=0,
         ),
-    )(place, *pieces, weight)
+    )(place, *pieces, *weights)
 
 
 def tables(block):
@@ -430,8 +435,6 @@
         [index * tp_parts + tp for index in group for tp in range(tp_parts)] for group in inner_groups
     ]
 
-    weight = lax.all_gather(in_proj, "seq", axis=1, tiled=True, axis_index_groups=inner_groups)
-
     taps = lax.dynamic_slice_in_dim(short_taps, position * chans, chans, axis=2)
     taps = jnp.broadcast_to(taps[..., None], taps.shape + (rows,))
     skip = lax.dynamic_slice_in_dim(skip_gain, position * chans, chans, axis=0)
@@ -440,20 +443,26 @@
         long_filter.T.reshape(seq_parts, chans, rows), "seq", split_axis=0, concat_axis=0, tiled=True
     )
 
-    held = share_columns(features, outer, tp_parts)
+    held = share_columns(features, outer, inner_parts, tp_parts)
     arrived = cross_outer(held, (0, 1), outer, inner_parts, tp_parts)
-    held, taps, skip, filter_blocks = lax.optimization_barrier((held, taps, skip, filter_blocks))
+    held[0], taps, skip, filter_blocks = lax.optimization_barrier((held[0], taps, skip, filter_blocks))
     if outer > 2:
         arrived |= cross_outer(held, (outer - 1,), outer, inner_parts, tp_parts)
     own = share_over_tp(arrived[0], tp_parts)
     held, arrived[1], own = lax.optimization_barrier((held, arrived[1], own))
     arrived |= cross_outer(held, range(2, outer - 1), outer, inner_parts, tp_parts)
     chunks = [own] + [share_over_tp(arrived[step], tp_parts) for step in range(1, outer)]
+
+    def settle(shards):
+        chunks[outer // 2][0], *shards = lax.optimization_barrier((chunks[outer // 2][0], *shards))
+        return shards
+
+    weights, masks = gather_inner(in_proj, inner_parts, settle)
     chunks, out_proj = lax.optimization_barrier((chunks, out_proj))
     out_weight = lax.all_gather(out_proj, ("seq", "tp"), axis_index_groups=tp_groups)
     out_weight = out_weight.reshape((inner_parts, tp_parts) + out_proj.shape)
 
-    partial = project_in(chunks, weight, seq_parts)
+    partial = project_in(chunks, weights, masks, inner_parts, seq_parts)
     parts = lax.all_to_all(partial, "seq", split_axis=0, concat_axis=0, tiled=True)
 
     gated = convolve([parts], filter_blocks, taps, skip, outer, tp_parts)

time: 168 us -> 199 us (1.18)
  waiting for transfers between devices: 63.1 us -> 83.4 us
  blocking collectives: 40.7 us -> 44.7 us
  other arithmetic: 0.23 us -> 3.73 us
  local copies, waits for them, and re-layouts: 2.81 us -> 5.87 us
    all_to_all x1, waiting for transfers between devices: 0.01 us -> 17.9 us  [per_device(): lax.all_to_all(long_filter.T.reshape(seq_parts, chans, rows), 'seq', spli...]
    ppermute x3, waiting for transfers between devices: 10.5 us -> 17.8 us  [cross_outer(): lax.ppermute(piece, 'seq', [(i, (i + far) % seq_parts) for i in range(seq...]
    all_to_all x1, blocking collectives: 40.7 us -> 44.7 us  [per_device(): lax.all_to_all(partial, 'seq', split_axis=0, concat_axis=0, tiled=True)]
    all_gather x1 -> x0, waiting for transfers between devices: 3.59 us -> none  [per_device(): lax.all_gather(in_proj, 'seq', axis=1, tiled=True, axis_index_groups=inne...]
    ppermute x3, starting transfers between devices: 9.2 us -> 5.64 us  [cross_outer(): lax.ppermute(piece, 'seq', [(i, (i + far) % seq_parts) for i in range(seq...]
    ppermute x1 -> x5, starting transfers between devices: 0.57 us -> 4.09 us  [the longest x2 2.09 us: share_columns(): piece = lax.ppermute(piece, 'tp', pairs)]
    ppermute x1 -> x5, waiting for transfers between devices: 5.62 us -> 2.6 us  [the longest x2 2.59 us: share_columns(): piece = lax.ppermute(piece, 'tp', pairs)]
    another operation x1 -> x3, other arithmetic: 0.05 us -> 2.74 us  [the longest x2 2.66 us: share_columns(): held.append(jnp.stack(pieces))]
  transfers between devices with their start and end apart: 16 -> 19, of which waited for: 11 -> 10; matrix products, arithmetic and copies ran while one was open for 1% -> 4% of each run, Pallas kernels for 6% -> 5%
where the time goes in v18:
time: 199 us; the launch traced here: 198 us
  waiting for transfers between devices  83.4 us (42%)
  blocking collectives  44.7 us (22%)
  starting transfers between devices  31.7 us (16%)
  Pallas kernels  15 us (8%)
  between operations  13.7 us (7%)
  local copies, waits for them, and re-layouts  5.87 us (3%)
  other arithmetic  3.73 us (2%)
    all_to_all x1, blocking collectives, per_device(): lax.all_to_all(partial, 'seq', split_axis=0, concat_axis=0, tiled=True)  44.7 us
    ppermute x4, waiting for transfers between devices, return_output(): arrived.append(lax.ppermute(piece, ('seq', 'tp'), pairs))  19.6 us
    all_to_all x1, waiting for transfers between devices, per_device(): lax.all_to_all(long_filter.T.reshape(seq_parts, chans, rows), 'seq', spli...  17.9 us
    ppermute x3, waiting for transfers between devices, cross_outer(): lax.ppermute(piece, 'seq', [(i, (i + far) % seq_parts) for i in range(seq...  17.8 us
    all_to_all x1, waiting for transfers between devices, per_device(): lax.all_to_all(gated.reshape((-1,) + gated.shape[3:]), ('tp', 'seq'), spl...  14.4 us
    ppermute x4, waiting for transfers between devices, share_over_tp(): pieces.append(lax.ppermute(part, 'tp', pairs))  11.2 us
    ppermute x4, starting transfers between devices, return_output(): arrived.append(lax.ppermute(piece, ('seq', 'tp'), pairs))  8.85 us
    pallas_call x1, Pallas kernels, project_in(): pl.pallas_call(functools.partial(project_kernel, tp_parts, masks), in_spe...  6.19 us
  transfers between devices with their start and end apart: 19, of which 10 were waited for; matrix products, arithmetic and copies ran while one was open for 4% of the time, Pallas kernels for 5%

profile of v18, /device:TPU:12, one launch (start us, length us, event | category | flops | bytes accessed | tf_op | source)
XLA Modules:
  0.0 198.3 jit_solution(2714630551594773216)
XLA Ops:
  9.9 1.5 collective-permute-start.1
  12.2 5.3 %all-to-all-start = ((f32[16,32,128]{2,1,0:T(8,128)}), f32[16,32,128]{2,1,0:T(8,128)S(1)}, u32[]{:S(2)}, u32[]{:S(2)}) async-start(f32[16,32,128]{2,1,0:T(8,128)} %bitcast.15), calls=%async_computation | async-start | bytes 524288 | tf_op jit(solution)/shard_map/all_to_all | solution.py:442
  19.4 1.6 collective-permute-start.2
  21.0 1.8 collective-permute-done.1
  25.8 1.8 pad_maximum_fusion.1
  27.6 17.9 %all-to-all-done.refs_1_ = f32[16,32,128]{2,1,0:T(8,128)S(1)} async-done(((f32[16,32,128]{2,1,0:T(8,128)}), f32[16,32,128]{2,1,0:T(8,128)S(1)}, u32[]{:S(2)}, u32[]{:S(2)}) %all-to-all-start) | async-done | bytes 262176 | tf_op jit(solution)/shard_map/all_to_all | solution.py:442
  46.7 2.7 %collective-permute-start.5 = (bf16[128,1024]{1,0:T(8,128)(2,1)S(1)}, bf16[128,1024]{1,0:T(8,128)(2,1)S(1)}, u32[]{:S(2)}, u32[]{:S(2)}) collective-permute-start(bf16[128,1024]{1,0:T(8,128)(2,1)S(1)} %dynamic-slice_bitcast_fusion.1), channel_id=1, source_target_pairs={{0,16},{2,18},{4,20},{6,22},{8,24},{10,26},{12,28},{14,30},{16,0},... | collective-permute-start | bytes 786440 | tf_op jit(solution)/shard_map/ppermute | solution.py:125
  49.3 11.3 %collective-permute-done.5.refs_4_ = bf16[128,1024]{1,0:T(8,128)(2,1)S(1)} collective-permute-done((bf16[128,1024]{1,0:T(8,128)(2,1)S(1)}, bf16[128,1024]{1,0:T(8,128)(2,1)S(1)}, u32[]{:S(2)}, u32[]{:S(2)}) %collective-permute-start.5) | collective-permute-done | bytes 262176 | tf_op jit(solution)/shard_map/ppermute | solution.py:125
  64.0 6.5 %collective-permute-done.8.refs_6_ = bf16[128,1024]{1,0:T(8,128)(2,1)S(1)} collective-permute-done((bf16[128,1024]{1,0:T(8,128)(2,1)S(1)}, bf16[128,1024]{1,0:T(8,128)(2,1)S(1)}, u32[]{:S(2)}, u32[]{:S(2)}) %collective-permute-start.8) | collective-permute-done | bytes 262176 | tf_op jit(solution)/shard_map/ppermute | solution.py:125
  71.0 1.5 collective-permute-start.7
  72.6 7.2 %collective-permute-done.9.refs_7_ = bf16[128,1024]{1,0:T(8,128)(2,1)} collective-permute-done((bf16[128,1024]{1,0:T(8,128)(2,1)S(1)}, bf16[128,1024]{1,0:T(8,128)(2,1)}, u32[]{:S(2)}, u32[]{:S(2)}) %collective-permute-start.9) | collective-permute-done | bytes 262176 | tf_op jit(solution)/shard_map/ppermute | solution.py:134
  79.8 3.9 %collective-permute-done.7.refs_5_ = bf16[128,1024]{1,0:T(8,128)(2,1)} collective-permute-done((bf16[128,1024]{1,0:T(8,128)(2,1)S(1)}, bf16[128,1024]{1,0:T(8,128)(2,1)}, u32[]{:S(2)}, u32[]{:S(2)}) %collective-permute-start.7) | collective-permute-done | bytes 262176 | tf_op jit(solution)/shard_map/ppermute | solution.py:134
  83.8 6.2 %shard_map.82 = bf16[16,3,32,512]{3,2,1,0:T(8,128)(2,1)S(1)} custom-call(s32[2]{0:T(128)S(1)} %pad_add_fusion.1.place_ref, bf16[128,1024]{1,0:T(8,128)(2,1)S(1)} %fusion.1.refs_0_, bf16[128,1024]{1,0:T(8,128)(2,1)S(1)} %collective-permute-done.3.refs_1_, bf16[128,1024]{1,0:T(8,128)(2,1)S(1)} %collective-permute-done.2.refs_2_, ...), custom_call_target="tpu_custom_call" | custom-call | flops 96636764160 | bytes 9961472 | tf_op jit(solution)/shard_map/pallas_call | solution.py:186
  90.0 44.7 %all_to_all.15.refs_0_ = bf16[16,3,32,512]{3,2,1,0:T(8,128)(2,1)S(1)} all-to-all(bf16[16,3,32,512]{3,2,1,0:T(8,128)(2,1)S(1)} %shard_map.82), channel_id=1, replica_groups=mesh['seq'=16,'tp'=2] {'seq'}, dimensions={0} | all-to-all | bytes 3145728 | tf_op jit(solution)/shard_map/all_to_all | solution.py:466
  134.8 3.7 %shard_map.83 = bf16[2,4,4,32,256]{4,3,2,1,0:T(8,128)(2,1)} custom-call(bf16[16,3,32,512]{3,2,1,0:T(8,128)(2,1)S(1)} %all_to_all.15.refs_0_, f32[16,32,128]{2,1,0:T(8,128)S(1)} %all-to-all-done.refs_1_, f32[3,3,32,128]{3,2,1,0:T(8,128)S(1)} %broadcast_in_dim.4.refs_2_, f32[32,128]{1,0:T(8,128)S(1)} %broadcast_in_dim.5.refs_3_, f32[128,256]{1,0:T(8,128)S(1)} %copy-done.3, ...), custom_call_target="tpu_custom_call" | custom-call | flops 1000000000 | bytes 4194304 | tf_op jit(solution)/shard_map/pallas_call | solution.py:346
  138.5 4.7 %all-to-all-start.2 = ((bf16[32,32,256]{2,1,0:T(8,128)(2,1)}), bf16[32,32,256]{2,1,0:T(8,128)(2,1)S(1)}, u32[]{:S(2)}, u32[]{:S(2)}) async-start(bf16[32,32,256]{2,1,0:T(8,128)(2,1)} %bitcast.22), calls=%async_computation.2 | async-start | bytes 1048576 | tf_op jit(solution)/shard_map/all_to_all | solution.py:469
  143.4 14.4 %all-to-all-done.2 = bf16[32,32,256]{2,1,0:T(8,128)(2,1)S(1)} async-done(((bf16[32,32,256]{2,1,0:T(8,128)(2,1)}), bf16[32,32,256]{2,1,0:T(8,128)(2,1)S(1)}, u32[]{:S(2)}, u32[]{:S(2)}) %all-to-all-start.2) | async-done | bytes 524320 | tf_op jit(solution)/shard_map/all_to_all | solution.py:469
  157.8 3.6 %shard_map.84 = (bf16[64,2048]{1,0:T(8,128)(2,1)S(1)}, bf16[64,2048]{1,0:T(8,128)(2,1)S(1)}, bf16[64,2048]{1,0:T(8,128)(2,1)S(1)}, bf16[64,2048]{1,0:T(8,128)(2,1)S(1)}) custom-call(s32[4]{0:T(128)S(1)} %pad_add_fusion.block_ref, bf16[2,512,256]{2,1,0:T(8,128)(2,1)S(1)} %bitcast.31, bf16[4,2,512,512]{3,2,1,0:T(8,128)(2,1)} %bitcast.32), custom_call_target="tpu_custom_call" | custom-call | flops 1073741824 | bytes 5767168 | tf_op jit(solution)/shard_map/pallas_call | solution.py:400
  161.4 2.6 %collective-permute-start.12 = (bf16[64,2048]{1,0:T(8,128)(2,1)S(1)}, bf16[64,2048]{1,0:T(8,128)(2,1)S(1)}, u32[]{:S(2)}, u32[]{:S(2)}) collective-permute-start(bf16[64,2048]{1,0:T(8,128)(2,1)S(1)} %get-tuple-element.49), channel_id=1, source_target_pairs={{0,0},{1,16},{2,2},{3,18},{4,4},{5,20},{6,6},{7,22},{8,24},{9,8},{... | collective-permute-start | bytes 786440 | tf_op jit(solution)/shard_map/ppermute | solution.py:88
  164.1 3.9 %collective-permute-start.14 = (bf16[64,2048]{1,0:T(8,128)(2,1)S(1)}, bf16[64,2048]{1,0:T(8,128)(2,1)S(1)}, u32[]{:S(2)}, u32[]{:S(2)}) collective-permute-start(bf16[64,2048]{1,0:T(8,128)(2,1)S(1)} %get-tuple-element.51), channel_id=1, source_target_pairs={{0,16},{1,0},{2,18},{3,2},{4,20},{5,4},{6,22},{7,6},{8,8},{9,24},{... | collective-permute-start | bytes 786440 | tf_op jit(solution)/shard_map/ppermute | solution.py:88
  167.9 2.3 %collective-permute-start.15 = (bf16[64,2048]{1,0:T(8,128)(2,1)S(1)}, bf16[64,2048]{1,0:T(8,128)(2,1)S(1)}, u32[]{:S(2)}, u32[]{:S(2)}) collective-permute-start(bf16[64,2048]{1,0:T(8,128)(2,1)S(1)} %get-tuple-element.52), channel_id=1, source_target_pairs={{0,24},{1,8},{2,26},{3,10},{4,28},{5,12},{6,30},{7,14},{8,0},{9,16... | collective-permute-start | bytes 786440 | tf_op jit(solution)/shard_map/ppermute | solution.py:88
  170.3 3.2 %collective-permute-done.12.refs_0_ = bf16[64,2048]{1,0:T(8,128)(2,1)S(1)} collective-permute-done((bf16[64,2048]{1,0:T(8,128)(2,1)S(1)}, bf16[64,2048]{1,0:T(8,128)(2,1)S(1)}, u32[]{:S(2)}, u32[]{:S(2)}) %collective-permute-start.12) | collective-permute-done | bytes 262176 | tf_op jit(solution)/shard_map/ppermute | solution.py:88
  173.5 16.4 %collective-permute-done.13.refs_1_ = bf16[64,2048]{1,0:T(8,128)(2,1)S(1)} collective-permute-done((bf16[64,2048]{1,0:T(8,128)(2,1)S(1)}, bf16[64,2048]{1,0:T(8,128)(2,1)S(1)}, u32[]{:S(2)}, u32[]{:S(2)}) %collective-permute-start.13) | collective-permute-done | bytes 262176 | tf_op jit(solution)/shard_map/ppermute | solution.py:88
  189.9 1.5 shard_map.85
  (47 shorter events, 14.3 us)
Async XLA Ops:
  6.5 17.6 %copy-start = (f32[3,3,512]{2,1,0:T(4,128)S(1)}, f32[3,3,512]{2,1,0:T(4,128)}, u32[]{:S(2)}) copy-start(f32[3,3,512]{2,1,0:T(4,128)} %param.10) | copy-start | bytes 55300
  6.5 4.8 %copy-start.5 = (f32[128,512]{1,0:T(8,128)S(1)}, f32[128,512]{1,0:T(8,128)}, u32[]{:S(2)}) copy-start(f32[128,512]{1,0:T(8,128)} %param.11) | copy-start | bytes 786436
  6.5 54.1 %collective-permute-start.6 = (bf16[3,512,512]{2,1,0:T(8,128)(2,1)}, bf16[3,512,512]{2,1,0:T(8,128)(2,1)}, u32[]{:S(2)}, u32[]{:S(2)}) collective-permute-start(bf16[3,512,512]{2,1,0:T(8,128)(2,1)} %refs_8_), channel_id=1, source_target_pairs={{0,4},{2,6},{4,0},{6,2},{8,12},{10,14},{12,8},{14,10},{16,20},{18,... | collective-permute-start | bytes 4718600 | tf_op jit(solution)/shard_map/ppermute | solution.py:143
  9.3 9.3 %collective-permute-start = (bf16[128,1024]{1,0:T(8,128)(2,1)S(1)}, bf16[128,1024]{1,0:T(8,128)(2,1)S(1)}, u32[]{:S(2)}, u32[]{:S(2)}) collective-permute-start(bf16[128,1024]{1,0:T(8,128)(2,1)S(1)} %get-tuple-element.54), channel_id=1, source_target_pairs={{0,1},{1,0},{2,3},{3,2},{4,5},{5,4},{6,7},{7,6},{8,9},{9,8},{10,11... | collective-permute-start | bytes 786440 | tf_op jit(solution)/shard_map/ppermute | solution.py:107
  9.9 12.9 %collective-permute-start.1 = (bf16[128,1024]{1,0:T(8,128)(2,1)S(1)}, bf16[128,1024]{1,0:T(8,128)(2,1)S(1)}, u32[]{:S(2)}, u32[]{:S(2)}) collective-permute-start(bf16[128,1024]{1,0:T(8,128)(2,1)S(1)} %get-tuple-element.56), channel_id=1, source_target_pairs={{0,1},{1,0},{2,3},{3,2},{4,5},{5,4},{6,7},{7,6},{8,9},{9,8},{10,11... | collective-permute-start | bytes 786440 | tf_op jit(solution)/shard_map/ppermute | solution.py:107
  12.2 33.3 %all-to-all-start = ((f32[16,32,128]{2,1,0:T(8,128)}), f32[16,32,128]{2,1,0:T(8,128)S(1)}, u32[]{:S(2)}, u32[]{:S(2)}) async-start(f32[16,32,128]{2,1,0:T(8,128)} %bitcast.15), calls=%async_computation | async-start | bytes 524288 | tf_op jit(solution)/shard_map/all_to_all | solution.py:442
  17.6 140.2 %all-gather.3.cloned.1.call-start = ((), (), s32[]{:S(2)}) async-start(), calls=%async_computation.3 | async-start | bytes 4718592 | tf_op jit(solution)/shard_map/all_gather | solution.py:462
  19.4 26.3 %collective-permute-start.2 = (bf16[128,1024]{1,0:T(8,128)(2,1)}, bf16[128,1024]{1,0:T(8,128)(2,1)S(1)}, u32[]{:S(2)}, u32[]{:S(2)}) collective-permute-start(bf16[128,1024]{1,0:T(8,128)(2,1)} %fusion.3), channel_id=1, source_target_pairs={{0,8},{2,10},{4,12},{6,14},{8,16},{10,18},{12,20},{14,22},{16,24},... | collective-permute-start | bytes 786440 | tf_op jit(solution)/shard_map/ppermute | solution.py:125
  23.6 37.1 %copy-start.1 = (bf16[3,512,512]{2,1,0:T(8,128)(2,1)S(1)}, bf16[3,512,512]{2,1,0:T(8,128)(2,1)}, u32[]{:S(2)}) copy-start(bf16[3,512,512]{2,1,0:T(8,128)(2,1)} %refs_8_) | copy-start | bytes 4718596
  23.6 22.1 %collective-permute-start.3 = (bf16[128,1024]{1,0:T(8,128)(2,1)S(1)}, bf16[128,1024]{1,0:T(8,128)(2,1)S(1)}, u32[]{:S(2)}, u32[]{:S(2)}) collective-permute-start(bf16[128,1024]{1,0:T(8,128)(2,1)S(1)} %fusion.1.refs_0_), channel_id=1, source_target_pairs={{0,1},{1,0},{2,3},{3,2},{4,5},{5,4},{6,7},{7,6},{8,9},{9,8},{10,11... | collective-permute-start | bytes 786440 | tf_op jit(solution)/shard_map/ppermute | solution.py:134
  46.7 14.0 %collective-permute-start.5 = (bf16[128,1024]{1,0:T(8,128)(2,1)S(1)}, bf16[128,1024]{1,0:T(8,128)(2,1)S(1)}, u32[]{:S(2)}, u32[]{:S(2)}) collective-permute-start(bf16[128,1024]{1,0:T(8,128)(2,1)S(1)} %dynamic-slice_bitcast_fusion.1), channel_id=1, source_target_pairs={{0,16},{2,18},{4,20},{6,22},{8,24},{10,26},{12,28},{14,30},{16,0},... | collective-permute-start | bytes 786440 | tf_op jit(solution)/shard_map/ppermute | solution.py:125
  60.7 23.1 %collective-permute-start.10 = (bf16[3,512,512]{2,1,0:T(8,128)(2,1)S(1)}, bf16[3,512,512]{2,1,0:T(8,128)(2,1)}, u32[]{:S(2)}, u32[]{:S(2)}) collective-permute-start(bf16[3,512,512]{2,1,0:T(8,128)(2,1)S(1)} %copy-done.1), channel_id=1, source_target_pairs={{0,2},{2,0},{4,6},{6,4},{8,10},{10,8},{12,14},{14,12},{16,18},{18,... | collective-permute-start | bytes 4718600 | tf_op jit(solution)/shard_map/ppermute | solution.py:143
  60.7 23.1 %collective-permute-start.11 = (bf16[3,512,512]{2,1,0:T(8,128)(2,1)}, bf16[3,512,512]{2,1,0:T(8,128)(2,1)}, u32[]{:S(2)}, u32[]{:S(2)}) collective-permute-start(bf16[3,512,512]{2,1,0:T(8,128)(2,1)} %collective-permute-done.6.refs_9_), channel_id=1, source_target_pairs={{0,2},{2,0},{4,6},{6,4},{8,10},{10,8},{12,14},{14,12},{16,18},{18,... | collective-permute-start | bytes 4718600 | tf_op jit(solution)/shard_map/ppermute | solution.py:143
  62.2 8.3 %collective-permute-start.8 = (bf16[128,1024]{1,0:T(8,128)(2,1)S(1)}, bf16[128,1024]{1,0:T(8,128)(2,1)S(1)}, u32[]{:S(2)}, u32[]{:S(2)}) collective-permute-start(bf16[128,1024]{1,0:T(8,128)(2,1)S(1)} %dynamic-slice_bitcast_fusion), channel_id=1, source_target_pairs={{0,24},{2,26},{4,28},{6,30},{8,0},{10,2},{12,4},{14,6},{16,8},{18,... | collective-permute-start | bytes 786440 | tf_op jit(solution)/shard_map/ppermute | solution.py:125
  63.6 9.0 %collective-permute-start.4 = (bf16[128,1024]{1,0:T(8,128)(2,1)S(1)}, bf16[128,1024]{1,0:T(8,128)(2,1)}, u32[]{:S(2)}, u32[]{:S(2)}) collective-permute-start(bf16[128,1024]{1,0:T(8,128)(2,1)S(1)} %collective-permute-done.2.refs_2_), channel_id=1, source_target_pairs={{0,1},{1,0},{2,3},{3,2},{4,5},{5,4},{6,7},{7,6},{8,9},{9,8},{10,11... | collective-permute-start | bytes 786440 | tf_op jit(solution)/shard_map/ppermute | solution.py:134
  70.5 9.3 %collective-permute-start.9 = (bf16[128,1024]{1,0:T(8,128)(2,1)S(1)}, bf16[128,1024]{1,0:T(8,128)(2,1)}, u32[]{:S(2)}, u32[]{:S(2)}) collective-permute-start(bf16[128,1024]{1,0:T(8,128)(2,1)S(1)} %collective-permute-done.8.refs_6_), channel_id=1, source_target_pairs={{0,1},{1,0},{2,3},{3,2},{4,5},{5,4},{6,7},{7,6},{8,9},{9,8},{10,11... | collective-permute-start | bytes 786440 | tf_op jit(solution)/shard_map/ppermute | solution.py:134
  71.0 12.8 %collective-permute-start.7 = (bf16[128,1024]{1,0:T(8,128)(2,1)S(1)}, bf16[128,1024]{1,0:T(8,128)(2,1)}, u32[]{:S(2)}, u32[]{:S(2)}) collective-permute-start(bf16[128,1024]{1,0:T(8,128)(2,1)S(1)} %collective-permute-done.5.refs_4_), channel_id=1, source_target_pairs={{0,1},{1,0},{2,3},{3,2},{4,5},{5,4},{6,7},{7,6},{8,9},{9,8},{10,11... | collective-permute-start | bytes 786440 | tf_op jit(solution)/shard_map/ppermute | solution.py:134
  90.0 44.8 %copy-start.2 = (f32[256,256]{1,0:T(8,128)S(1)}, f32[256,256]{1,0:T(8,128)}, u32[]{:S(2)}) copy-start(f32[256,256]{1,0:T(8,128)} %constant.237.clone.refs_5_) | copy-start | bytes 786436
  90.0 44.8 %copy-start.3 = (f32[128,256]{1,0:T(8,128)S(1)}, f32[128,256]{1,0:T(8,128)}, u32[]{:S(2)}) copy-start(f32[128,256]{1,0:T(8,128)} %constant.236.clone.refs_4_) | copy-start | bytes 393220
  138.5 19.3 %all-to-all-start.2 = ((bf16[32,32,256]{2,1,0:T(8,128)(2,1)}), bf16[32,32,256]{2,1,0:T(8,128)(2,1)S(1)}, u32[]{:S(2)}, u32[]{:S(2)}) async-start(bf16[32,32,256]{2,1,0:T(8,128)(2,1)} %bitcast.22), calls=%async_computation.2 | async-start | bytes 1048576 | tf_op jit(solution)/shard_map/all_to_all | solution.py:469
  161.4 12.1 %collective-permute-start.12 = (bf16[64,2048]{1,0:T(8,128)(2,1)S(1)}, bf16[64,2048]{1,0:T(8,128)(2,1)S(1)}, u32[]{:S(2)}, u32[]{:S(2)}) collective-permute-start(bf16[64,2048]{1,0:T(8,128)(2,1)S(1)} %get-tuple-element.49), channel_id=1, source_target_pairs={{0,0},{1,16},{2,2},{3,18},{4,4},{5,20},{6,6},{7,22},{8,24},{9,8},{... | collective-permute-start | bytes 786440 | tf_op jit(solution)/shard_map/ppermute | solution.py:88
  164.0 25.9 %collective-permute-start.13 = (bf16[64,2048]{1,0:T(8,128)(2,1)S(1)}, bf16[64,2048]{1,0:T(8,128)(2,1)S(1)}, u32[]{:S(2)}, u32[]{:S(2)}) collective-permute-start(bf16[64,2048]{1,0:T(8,128)(2,1)S(1)} %get-tuple-element.50), channel_id=1, source_target_pairs={{0,8},{1,24},{2,10},{3,26},{4,12},{5,28},{6,14},{7,30},{8,16},{9,0... | collective-permute-start | bytes 786440 | tf_op jit(solution)/shard_map/ppermute | solution.py:88
  164.1 25.8 %collective-permute-start.14 = (bf16[64,2048]{1,0:T(8,128)(2,1)S(1)}, bf16[64,2048]{1,0:T(8,128)(2,1)S(1)}, u32[]{:S(2)}, u32[]{:S(2)}) collective-permute-start(bf16[64,2048]{1,0:T(8,128)(2,1)S(1)} %get-tuple-element.51), channel_id=1, source_target_pairs={{0,16},{1,0},{2,18},{3,2},{4,20},{5,4},{6,22},{7,6},{8,8},{9,24},{... | collective-permute-start | bytes 786440 | tf_op jit(solution)/shard_map/ppermute | solution.py:88
  167.9 22.0 %collective-permute-start.15 = (bf16[64,2048]{1,0:T(8,128)(2,1)S(1)}, bf16[64,2048]{1,0:T(8,128)(2,1)S(1)}, u32[]{:S(2)}, u32[]{:S(2)}) collective-permute-start(bf16[64,2048]{1,0:T(8,128)(2,1)S(1)} %get-tuple-element.52), channel_id=1, source_target_pairs={{0,24},{1,8},{2,26},{3,10},{4,28},{5,12},{6,30},{7,14},{8,0},{9,16... | collective-permute-start | bytes 786440 | tf_op jit(solution)/shard_map/ppermute | solution.py:88
  (1 other events, 0.7 us)
Sparse Core Ops, SparseCore 0:
  83.9 51.9 all-gather.2

commit v19 on v18

--- a/solution.py
+++ b/solution.py
@@ -445,7 +445,7 @@
 
     held = share_columns(features, outer, inner_parts, tp_parts)
     arrived = cross_outer(held, (0, 1), outer, inner_parts, tp_parts)
-    held[0], taps, skip, filter_blocks = lax.optimization_barrier((held[0], taps, skip, filter_blocks))
+    held[0], taps, skip = lax.optimization_barrier((held[0], taps, skip))
     if outer > 2:
         arrived |= cross_outer(held, (outer - 1,), outer, inner_parts, tp_parts)
     own = share_over_tp(arrived[0], tp_parts)
@@ -458,7 +458,7 @@
         return shards
 
     weights, masks = gather_inner(in_proj, inner_parts, settle)
-    chunks, out_proj = lax.optimization_barrier((chunks, out_proj))
+    chunks, out_proj, filter_blocks = lax.optimization_barrier((chunks, out_proj, filter_blocks))
     out_weight = lax.all_gather(out_proj, ("seq", "tp"), axis_index_groups=tp_groups)
     out_weight = out_weight.reshape((inner_parts, tp_parts) + out_proj.shape)
 

time: 199 us -> 186 us (0.935)
  waiting for transfers between devices: 83.4 us -> 72.5 us
  blocking collectives: 44.7 us -> 42.1 us
    all_to_all x1, waiting for transfers between devices: 17.9 us -> 5.19 us  [per_device(): lax.all_to_all(long_filter.T.reshape(seq_parts, chans, rows), 'seq', spli...]
    ppermute x3, waiting for transfers between devices: 17.8 us -> 9.17 us  [cross_outer(): lax.ppermute(piece, 'seq', [(i, (i + far) % seq_parts) for i in range(seq...]
    ppermute x2, waiting for transfers between devices: 2.59 us -> 8.26 us  [share_columns(): piece = lax.ppermute(piece, 'tp', pairs)]
    ppermute x4, waiting for transfers between devices: 11.2 us -> 15.3 us  [share_over_tp(): pieces.append(lax.ppermute(part, 'tp', pairs))]
    all_to_all x1, blocking collectives: 44.7 us -> 42.1 us  [per_device(): lax.all_to_all(partial, 'seq', split_axis=0, concat_axis=0, tiled=True)]
  transfers between devices with their start and end apart: 19 -> 19, of which waited for: 10 -> 12; matrix products, arithmetic and copies ran while one was open for 4% -> 4% of each run, Pallas kernels for 5% -> 5%
where the time goes in v19:
time: 186 us; the launch traced here: 185 us
  waiting for transfers between devices  72.5 us (39%)
  blocking collectives  42.1 us (23%)
  starting transfers between devices  32.7 us (18%)
  Pallas kernels  15 us (8%)
  between operations  13.6 us (7%)
  local copies, waits for them, and re-layouts  6.31 us (3%)
  other arithmetic  3.05 us (2%)
    all_to_all x1, blocking collectives, per_device(): lax.all_to_all(partial, 'seq', split_axis=0, concat_axis=0, tiled=True)  42.1 us
    ppermute x4, waiting for transfers between devices, return_output(): arrived.append(lax.ppermute(piece, ('seq', 'tp'), pairs))  19.6 us
    ppermute x4, waiting for transfers between devices, share_over_tp(): pieces.append(lax.ppermute(part, 'tp', pairs))  15.3 us
    all_to_all x1, waiting for transfers between devices, per_device(): lax.all_to_all(gated.reshape((-1,) + gated.shape[3:]), ('tp', 'seq'), spl...  14.4 us
    ppermute x3, waiting for transfers between devices, cross_outer(): lax.ppermute(piece, 'seq', [(i, (i + far) % seq_parts) for i in range(seq...  9.17 us
    ppermute x4, starting transfers between devices, return_output(): arrived.append(lax.ppermute(piece, ('seq', 'tp'), pairs))  8.85 us
    ppermute x2, waiting for transfers between devices, share_columns(): piece = lax.ppermute(piece, 'tp', pairs)  8.26 us
    all_to_all x1, starting transfers between devices, per_device(): lax.all_to_all(long_filter.T.reshape(seq_parts, chans, rows), 'seq', spli...  6.83 us
  transfers between devices with their start and end apart: 19, of which 12 were waited for; matrix products, arithmetic and copies ran while one was open for 4% of the time, Pallas kernels for 5%

profile of v19, /device:TPU:12, one launch (start us, length us, event | category | flops | bytes accessed | tf_op | source)
XLA Modules:
  0.0 185.4 jit_solution(15672707217349277912)
XLA Ops:
  9.9 1.5 collective-permute-start.1
  11.4 7.2 %collective-permute-done = bf16[128,1024]{1,0:T(8,128)(2,1)S(1)} collective-permute-done((bf16[128,1024]{1,0:T(8,128)(2,1)S(1)}, bf16[128,1024]{1,0:T(8,128)(2,1)S(1)}, u32[]{:S(2)}, u32[]{:S(2)}) %collective-permute-start) | collective-permute-done | bytes 262176 | tf_op jit(solution)/shard_map/ppermute | solution.py:107
  20.1 1.6 collective-permute-start.2
  27.2 3.4 %collective-permute-done.3.refs_1_ = bf16[128,1024]{1,0:T(8,128)(2,1)S(1)} collective-permute-done((bf16[128,1024]{1,0:T(8,128)(2,1)S(1)}, bf16[128,1024]{1,0:T(8,128)(2,1)S(1)}, u32[]{:S(2)}, u32[]{:S(2)}) %collective-permute-start.3) | collective-permute-done | bytes 262176 | tf_op jit(solution)/shard_map/ppermute | solution.py:134
  30.6 2.7 %collective-permute-start.5 = (bf16[128,1024]{1,0:T(8,128)(2,1)S(1)}, bf16[128,1024]{1,0:T(8,128)(2,1)S(1)}, u32[]{:S(2)}, u32[]{:S(2)}) collective-permute-start(bf16[128,1024]{1,0:T(8,128)(2,1)S(1)} %dynamic-slice_bitcast_fusion.1), channel_id=1, source_target_pairs={{0,16},{2,18},{4,20},{6,22},{8,24},{10,26},{12,28},{14,30},{16,0},... | collective-permute-start | bytes 786440 | tf_op jit(solution)/shard_map/ppermute | solution.py:125
  33.3 9.2 %collective-permute-done.5.refs_4_ = bf16[128,1024]{1,0:T(8,128)(2,1)S(1)} collective-permute-done((bf16[128,1024]{1,0:T(8,128)(2,1)S(1)}, bf16[128,1024]{1,0:T(8,128)(2,1)S(1)}, u32[]{:S(2)}, u32[]{:S(2)}) %collective-permute-start.5) | collective-permute-done | bytes 262176 | tf_op jit(solution)/shard_map/ppermute | solution.py:125
  45.0 1.8 copy.9
  46.8 6.8 %all-to-all-start = ((f32[16,32,128]{2,1,0:T(8,128)}), f32[16,32,128]{2,1,0:T(8,128)S(1)}, u32[]{:S(2)}, u32[]{:S(2)}) async-start(f32[16,32,128]{2,1,0:T(8,128)} %bitcast.33), calls=%async_computation | async-start | bytes 524288 | tf_op jit(solution)/shard_map/all_to_all | solution.py:442
  54.3 1.5 collective-permute-start.9
  56.4 5.2 %all-to-all-done.refs_1_ = f32[16,32,128]{2,1,0:T(8,128)S(1)} async-done(((f32[16,32,128]{2,1,0:T(8,128)}), f32[16,32,128]{2,1,0:T(8,128)S(1)}, u32[]{:S(2)}, u32[]{:S(2)}) %all-to-all-start) | async-done | bytes 262176 | tf_op jit(solution)/shard_map/all_to_all | solution.py:442
  63.0 5.6 %collective-permute-done.9.refs_7_ = bf16[128,1024]{1,0:T(8,128)(2,1)} collective-permute-done((bf16[128,1024]{1,0:T(8,128)(2,1)S(1)}, bf16[128,1024]{1,0:T(8,128)(2,1)}, u32[]{:S(2)}, u32[]{:S(2)}) %collective-permute-start.9) | collective-permute-done | bytes 262176 | tf_op jit(solution)/shard_map/ppermute | solution.py:134
  68.6 4.8 %collective-permute-done.7.refs_5_ = bf16[128,1024]{1,0:T(8,128)(2,1)} collective-permute-done((bf16[128,1024]{1,0:T(8,128)(2,1)S(1)}, bf16[128,1024]{1,0:T(8,128)(2,1)}, u32[]{:S(2)}, u32[]{:S(2)}) %collective-permute-start.7) | collective-permute-done | bytes 262176 | tf_op jit(solution)/shard_map/ppermute | solution.py:134
  73.5 6.2 %shard_map.82 = bf16[16,3,32,512]{3,2,1,0:T(8,128)(2,1)S(1)} custom-call(s32[2]{0:T(128)S(1)} %pad_add_fusion.1.place_ref, bf16[128,1024]{1,0:T(8,128)(2,1)S(1)} %fusion.1.refs_0_, bf16[128,1024]{1,0:T(8,128)(2,1)S(1)} %collective-permute-done.3.refs_1_, bf16[128,1024]{1,0:T(8,128)(2,1)S(1)} %collective-permute-done.2.refs_2_, ...), custom_call_target="tpu_custom_call" | custom-call | flops 96636764160 | bytes 9961472 | tf_op jit(solution)/shard_map/pallas_call | solution.py:186
  79.7 42.1 %all_to_all.15.refs_0_ = bf16[16,3,32,512]{3,2,1,0:T(8,128)(2,1)S(1)} all-to-all(bf16[16,3,32,512]{3,2,1,0:T(8,128)(2,1)S(1)} %shard_map.82), channel_id=1, replica_groups=mesh['seq'=16,'tp'=2] {'seq'}, dimensions={0} | all-to-all | bytes 3145728 | tf_op jit(solution)/shard_map/all_to_all | solution.py:466
  121.8 3.7 %shard_map.83 = bf16[2,4,4,32,256]{4,3,2,1,0:T(8,128)(2,1)} custom-call(bf16[16,3,32,512]{3,2,1,0:T(8,128)(2,1)S(1)} %all_to_all.15.refs_0_, f32[16,32,128]{2,1,0:T(8,128)S(1)} %all-to-all-done.refs_1_, f32[3,3,32,128]{3,2,1,0:T(8,128)S(1)} %broadcast_in_dim.4.refs_2_, f32[32,128]{1,0:T(8,128)S(1)} %broadcast_in_dim.5.refs_3_, f32[128,256]{1,0:T(8,128)S(1)} %copy-done.3, ...), custom_call_target="tpu_custom_call" | custom-call | flops 1000000000 | bytes 4194304 | tf_op jit(solution)/shard_map/pallas_call | solution.py:346
  125.6 4.7 %all-to-all-start.2 = ((bf16[32,32,256]{2,1,0:T(8,128)(2,1)}), bf16[32,32,256]{2,1,0:T(8,128)(2,1)S(1)}, u32[]{:S(2)}, u32[]{:S(2)}) async-start(bf16[32,32,256]{2,1,0:T(8,128)(2,1)} %bitcast.22), calls=%async_computation.2 | async-start | bytes 1048576 | tf_op jit(solution)/shard_map/all_to_all | solution.py:469
  130.5 14.4 %all-to-all-done.2 = bf16[32,32,256]{2,1,0:T(8,128)(2,1)S(1)} async-done(((bf16[32,32,256]{2,1,0:T(8,128)(2,1)}), bf16[32,32,256]{2,1,0:T(8,128)(2,1)S(1)}, u32[]{:S(2)}, u32[]{:S(2)}) %all-to-all-start.2) | async-done | bytes 524320 | tf_op jit(solution)/shard_map/all_to_all | solution.py:469
  144.9 3.6 %shard_map.84 = (bf16[64,2048]{1,0:T(8,128)(2,1)S(1)}, bf16[64,2048]{1,0:T(8,128)(2,1)S(1)}, bf16[64,2048]{1,0:T(8,128)(2,1)S(1)}, bf16[64,2048]{1,0:T(8,128)(2,1)S(1)}) custom-call(s32[4]{0:T(128)S(1)} %pad_add_fusion.block_ref, bf16[2,512,256]{2,1,0:T(8,128)(2,1)S(1)} %bitcast.31, bf16[4,2,512,512]{3,2,1,0:T(8,128)(2,1)} %bitcast.32), custom_call_target="tpu_custom_call" | custom-call | flops 1073741824 | bytes 5767168 | tf_op jit(solution)/shard_map/pallas_call | solution.py:400
  148.4 2.6 %collective-permute-start.12 = (bf16[64,2048]{1,0:T(8,128)(2,1)S(1)}, bf16[64,2048]{1,0:T(8,128)(2,1)S(1)}, u32[]{:S(2)}, u32[]{:S(2)}) collective-permute-start(bf16[64,2048]{1,0:T(8,128)(2,1)S(1)} %get-tuple-element.49), channel_id=1, source_target_pairs={{0,0},{1,16},{2,2},{3,18},{4,4},{5,20},{6,6},{7,22},{8,24},{9,8},{... | collective-permute-start | bytes 786440 | tf_op jit(solution)/shard_map/ppermute | solution.py:88
  151.1 3.9 %collective-permute-start.14 = (bf16[64,2048]{1,0:T(8,128)(2,1)S(1)}, bf16[64,2048]{1,0:T(8,128)(2,1)S(1)}, u32[]{:S(2)}, u32[]{:S(2)}) collective-permute-start(bf16[64,2048]{1,0:T(8,128)(2,1)S(1)} %get-tuple-element.51), channel_id=1, source_target_pairs={{0,16},{1,0},{2,18},{3,2},{4,20},{5,4},{6,22},{7,6},{8,8},{9,24},{... | collective-permute-start | bytes 786440 | tf_op jit(solution)/shard_map/ppermute | solution.py:88
  155.0 2.3 %collective-permute-start.15 = (bf16[64,2048]{1,0:T(8,128)(2,1)S(1)}, bf16[64,2048]{1,0:T(8,128)(2,1)S(1)}, u32[]{:S(2)}, u32[]{:S(2)}) collective-permute-start(bf16[64,2048]{1,0:T(8,128)(2,1)S(1)} %get-tuple-element.52), channel_id=1, source_target_pairs={{0,24},{1,8},{2,26},{3,10},{4,28},{5,12},{6,30},{7,14},{8,0},{9,16... | collective-permute-start | bytes 786440 | tf_op jit(solution)/shard_map/ppermute | solution.py:88
  157.4 3.2 %collective-permute-done.12.refs_0_ = bf16[64,2048]{1,0:T(8,128)(2,1)S(1)} collective-permute-done((bf16[64,2048]{1,0:T(8,128)(2,1)S(1)}, bf16[64,2048]{1,0:T(8,128)(2,1)S(1)}, u32[]{:S(2)}, u32[]{:S(2)}) %collective-permute-start.12) | collective-permute-done | bytes 262176 | tf_op jit(solution)/shard_map/ppermute | solution.py:88
  160.6 16.4 %collective-permute-done.13.refs_1_ = bf16[64,2048]{1,0:T(8,128)(2,1)S(1)} collective-permute-done((bf16[64,2048]{1,0:T(8,128)(2,1)S(1)}, bf16[64,2048]{1,0:T(8,128)(2,1)S(1)}, u32[]{:S(2)}, u32[]{:S(2)}) %collective-permute-start.13) | collective-permute-done | bytes 262176 | tf_op jit(solution)/shard_map/ppermute | solution.py:88
  176.9 1.5 shard_map.85
  (47 shorter events, 15.8 us)
Async XLA Ops:
  6.5 17.6 %copy-start = (f32[3,3,512]{2,1,0:T(4,128)S(1)}, f32[3,3,512]{2,1,0:T(4,128)}, u32[]{:S(2)}) copy-start(f32[3,3,512]{2,1,0:T(4,128)} %param.10) | copy-start | bytes 55300
  6.5 36.5 %collective-permute-start.6 = (bf16[3,512,512]{2,1,0:T(8,128)(2,1)}, bf16[3,512,512]{2,1,0:T(8,128)(2,1)}, u32[]{:S(2)}, u32[]{:S(2)}) collective-permute-start(bf16[3,512,512]{2,1,0:T(8,128)(2,1)} %refs_8_), channel_id=1, source_target_pairs={{0,4},{2,6},{4,0},{6,2},{8,12},{10,14},{12,8},{14,10},{16,20},{18,... | collective-permute-start | bytes 4718600 | tf_op jit(solution)/shard_map/ppermute | solution.py:143
  9.3 9.3 %collective-permute-start = (bf16[128,1024]{1,0:T(8,128)(2,1)S(1)}, bf16[128,1024]{1,0:T(8,128)(2,1)S(1)}, u32[]{:S(2)}, u32[]{:S(2)}) collective-permute-start(bf16[128,1024]{1,0:T(8,128)(2,1)S(1)} %get-tuple-element.54), channel_id=1, source_target_pairs={{0,1},{1,0},{2,3},{3,2},{4,5},{5,4},{6,7},{7,6},{8,9},{9,8},{10,11... | collective-permute-start | bytes 786440 | tf_op jit(solution)/shard_map/ppermute | solution.py:107
  9.9 12.9 %collective-permute-start.1 = (bf16[128,1024]{1,0:T(8,128)(2,1)S(1)}, bf16[128,1024]{1,0:T(8,128)(2,1)S(1)}, u32[]{:S(2)}, u32[]{:S(2)}) collective-permute-start(bf16[128,1024]{1,0:T(8,128)(2,1)S(1)} %get-tuple-element.56), channel_id=1, source_target_pairs={{0,1},{1,0},{2,3},{3,2},{4,5},{5,4},{6,7},{7,6},{8,9},{9,8},{10,11... | collective-permute-start | bytes 786440 | tf_op jit(solution)/shard_map/ppermute | solution.py:107
  18.6 0.7 copy-start.5
  20.1 7.0 %collective-permute-start.2 = (bf16[128,1024]{1,0:T(8,128)(2,1)}, bf16[128,1024]{1,0:T(8,128)(2,1)S(1)}, u32[]{:S(2)}, u32[]{:S(2)}) collective-permute-start(bf16[128,1024]{1,0:T(8,128)(2,1)} %fusion.3), channel_id=1, source_target_pairs={{0,8},{2,10},{4,12},{6,14},{8,16},{10,18},{12,20},{14,22},{16,24},... | collective-permute-start | bytes 786440 | tf_op jit(solution)/shard_map/ppermute | solution.py:125
  23.5 19.4 %copy-start.1 = (bf16[3,512,512]{2,1,0:T(8,128)(2,1)S(1)}, bf16[3,512,512]{2,1,0:T(8,128)(2,1)}, u32[]{:S(2)}) copy-start(bf16[3,512,512]{2,1,0:T(8,128)(2,1)} %refs_8_) | copy-start | bytes 4718596
  23.6 7.0 %collective-permute-start.3 = (bf16[128,1024]{1,0:T(8,128)(2,1)S(1)}, bf16[128,1024]{1,0:T(8,128)(2,1)S(1)}, u32[]{:S(2)}, u32[]{:S(2)}) collective-permute-start(bf16[128,1024]{1,0:T(8,128)(2,1)S(1)} %fusion.1.refs_0_), channel_id=1, source_target_pairs={{0,1},{1,0},{2,3},{3,2},{4,5},{5,4},{6,7},{7,6},{8,9},{9,8},{10,11... | collective-permute-start | bytes 786440 | tf_op jit(solution)/shard_map/ppermute | solution.py:134
  30.6 11.8 %collective-permute-start.5 = (bf16[128,1024]{1,0:T(8,128)(2,1)S(1)}, bf16[128,1024]{1,0:T(8,128)(2,1)S(1)}, u32[]{:S(2)}, u32[]{:S(2)}) collective-permute-start(bf16[128,1024]{1,0:T(8,128)(2,1)S(1)} %dynamic-slice_bitcast_fusion.1), channel_id=1, source_target_pairs={{0,16},{2,18},{4,20},{6,22},{8,24},{10,26},{12,28},{14,30},{16,0},... | collective-permute-start | bytes 786440 | tf_op jit(solution)/shard_map/ppermute | solution.py:125
  43.0 30.5 %collective-permute-start.10 = (bf16[3,512,512]{2,1,0:T(8,128)(2,1)S(1)}, bf16[3,512,512]{2,1,0:T(8,128)(2,1)}, u32[]{:S(2)}, u32[]{:S(2)}) collective-permute-start(bf16[3,512,512]{2,1,0:T(8,128)(2,1)S(1)} %copy-done.1), channel_id=1, source_target_pairs={{0,2},{2,0},{4,6},{6,4},{8,10},{10,8},{12,14},{14,12},{16,18},{18,... | collective-permute-start | bytes 4718600 | tf_op jit(solution)/shard_map/ppermute | solution.py:143
  43.0 30.5 %collective-permute-start.11 = (bf16[3,512,512]{2,1,0:T(8,128)(2,1)}, bf16[3,512,512]{2,1,0:T(8,128)(2,1)}, u32[]{:S(2)}, u32[]{:S(2)}) collective-permute-start(bf16[3,512,512]{2,1,0:T(8,128)(2,1)} %collective-permute-done.6.refs_9_), channel_id=1, source_target_pairs={{0,2},{2,0},{4,6},{6,4},{8,10},{10,8},{12,14},{14,12},{16,18},{18,... | collective-permute-start | bytes 4718600 | tf_op jit(solution)/shard_map/ppermute | solution.py:143
  44.2 10.0 %collective-permute-start.8 = (bf16[128,1024]{1,0:T(8,128)(2,1)}, bf16[128,1024]{1,0:T(8,128)(2,1)S(1)}, u32[]{:S(2)}, u32[]{:S(2)}) collective-permute-start(bf16[128,1024]{1,0:T(8,128)(2,1)} %dynamic-slice_bitcast_fusion), channel_id=1, source_target_pairs={{0,24},{2,26},{4,28},{6,30},{8,0},{10,2},{12,4},{14,6},{16,8},{18,... | collective-permute-start | bytes 786440 | tf_op jit(solution)/shard_map/ppermute | solution.py:125
  46.8 14.7 %all-to-all-start = ((f32[16,32,128]{2,1,0:T(8,128)}), f32[16,32,128]{2,1,0:T(8,128)S(1)}, u32[]{:S(2)}, u32[]{:S(2)}) async-start(f32[16,32,128]{2,1,0:T(8,128)} %bitcast.33), calls=%async_computation | async-start | bytes 524288 | tf_op jit(solution)/shard_map/all_to_all | solution.py:442
  53.6 91.2 %all-gather.3.cloned.1.call-start = ((), (), s32[]{:S(2)}) async-start(), calls=%async_computation.3 | async-start | bytes 4718592 | tf_op jit(solution)/shard_map/all_gather | solution.py:462
  53.7 9.3 %collective-permute-start.4 = (bf16[128,1024]{1,0:T(8,128)(2,1)S(1)}, bf16[128,1024]{1,0:T(8,128)(2,1)}, u32[]{:S(2)}, u32[]{:S(2)}) collective-permute-start(bf16[128,1024]{1,0:T(8,128)(2,1)S(1)} %collective-permute-done.2.refs_2_), channel_id=1, source_target_pairs={{0,1},{1,0},{2,3},{3,2},{4,5},{5,4},{6,7},{7,6},{8,9},{9,8},{10,11... | collective-permute-start | bytes 786440 | tf_op jit(solution)/shard_map/ppermute | solution.py:134
  54.3 14.4 %collective-permute-start.9 = (bf16[128,1024]{1,0:T(8,128)(2,1)S(1)}, bf16[128,1024]{1,0:T(8,128)(2,1)}, u32[]{:S(2)}, u32[]{:S(2)}) collective-permute-start(bf16[128,1024]{1,0:T(8,128)(2,1)S(1)} %collective-permute-done.8.refs_6_), channel_id=1, source_target_pairs={{0,1},{1,0},{2,3},{3,2},{4,5},{5,4},{6,7},{7,6},{8,9},{9,8},{10,11... | collective-permute-start | bytes 786440 | tf_op jit(solution)/shard_map/ppermute | solution.py:134
  55.8 17.7 %collective-permute-start.7 = (bf16[128,1024]{1,0:T(8,128)(2,1)S(1)}, bf16[128,1024]{1,0:T(8,128)(2,1)}, u32[]{:S(2)}, u32[]{:S(2)}) collective-permute-start(bf16[128,1024]{1,0:T(8,128)(2,1)S(1)} %collective-permute-done.5.refs_4_), channel_id=1, source_target_pairs={{0,1},{1,0},{2,3},{3,2},{4,5},{5,4},{6,7},{7,6},{8,9},{9,8},{10,11... | collective-permute-start | bytes 786440 | tf_op jit(solution)/shard_map/ppermute | solution.py:134
  79.7 42.2 %copy-start.2 = (f32[256,256]{1,0:T(8,128)S(1)}, f32[256,256]{1,0:T(8,128)}, u32[]{:S(2)}) copy-start(f32[256,256]{1,0:T(8,128)} %constant.237.clone.refs_5_) | copy-start | bytes 786436
  79.7 42.1 %copy-start.3 = (f32[128,256]{1,0:T(8,128)S(1)}, f32[128,256]{1,0:T(8,128)}, u32[]{:S(2)}) copy-start(f32[128,256]{1,0:T(8,128)} %constant.236.clone.refs_4_) | copy-start | bytes 393220
  125.6 19.3 %all-to-all-start.2 = ((bf16[32,32,256]{2,1,0:T(8,128)(2,1)}), bf16[32,32,256]{2,1,0:T(8,128)(2,1)S(1)}, u32[]{:S(2)}, u32[]{:S(2)}) async-start(bf16[32,32,256]{2,1,0:T(8,128)(2,1)} %bitcast.22), calls=%async_computation.2 | async-start | bytes 1048576 | tf_op jit(solution)/shard_map/all_to_all | solution.py:469
  148.4 12.1 %collective-permute-start.12 = (bf16[64,2048]{1,0:T(8,128)(2,1)S(1)}, bf16[64,2048]{1,0:T(8,128)(2,1)S(1)}, u32[]{:S(2)}, u32[]{:S(2)}) collective-permute-start(bf16[64,2048]{1,0:T(8,128)(2,1)S(1)} %get-tuple-element.49), channel_id=1, source_target_pairs={{0,0},{1,16},{2,2},{3,18},{4,4},{5,20},{6,6},{7,22},{8,24},{9,8},{... | collective-permute-start | bytes 786440 | tf_op jit(solution)/shard_map/ppermute | solution.py:88
  151.1 25.9 %collective-permute-start.13 = (bf16[64,2048]{1,0:T(8,128)(2,1)S(1)}, bf16[64,2048]{1,0:T(8,128)(2,1)S(1)}, u32[]{:S(2)}, u32[]{:S(2)}) collective-permute-start(bf16[64,2048]{1,0:T(8,128)(2,1)S(1)} %get-tuple-element.50), channel_id=1, source_target_pairs={{0,8},{1,24},{2,10},{3,26},{4,12},{5,28},{6,14},{7,30},{8,16},{9,0... | collective-permute-start | bytes 786440 | tf_op jit(solution)/shard_map/ppermute | solution.py:88
  151.1 25.8 %collective-permute-start.14 = (bf16[64,2048]{1,0:T(8,128)(2,1)S(1)}, bf16[64,2048]{1,0:T(8,128)(2,1)S(1)}, u32[]{:S(2)}, u32[]{:S(2)}) collective-permute-start(bf16[64,2048]{1,0:T(8,128)(2,1)S(1)} %get-tuple-element.51), channel_id=1, source_target_pairs={{0,16},{1,0},{2,18},{3,2},{4,20},{5,4},{6,22},{7,6},{8,8},{9,24},{... | collective-permute-start | bytes 786440 | tf_op jit(solution)/shard_map/ppermute | solution.py:88
  155.0 22.0 %collective-permute-start.15 = (bf16[64,2048]{1,0:T(8,128)(2,1)S(1)}, bf16[64,2048]{1,0:T(8,128)(2,1)S(1)}, u32[]{:S(2)}, u32[]{:S(2)}) collective-permute-start(bf16[64,2048]{1,0:T(8,128)(2,1)S(1)} %get-tuple-element.52), channel_id=1, source_target_pairs={{0,24},{1,8},{2,26},{3,10},{4,28},{5,12},{6,30},{7,14},{8,0},{9,16... | collective-permute-start | bytes 786440 | tf_op jit(solution)/shard_map/ppermute | solution.py:88
  (1 other events, 0.7 us)
Sparse Core Ops, SparseCore 0:
  73.6 49.3 all-gather.2

commit v20 on v17

--- a/solution.py
+++ b/solution.py
@@ -3,13 +3,13 @@
 
 import jax
 import jax.numpy as jnp
+import ml_dtypes
 import numpy as np
 from jax import lax
 from jax.experimental import pallas as pl
 from jax.experimental.pallas import tpu as pltpu
 from jax.sharding import PartitionSpec as P
 
-HIGHEST = lax.Precision.HIGHEST
 UNROLL = 16
 HEAVY = 30
 
@@ -201,7 +201,13 @@
     place = np.arange(2 * block)
     angle = 2.0 * math.pi * np.outer(np.arange(block) + 0.5, place) / (2 * block)
     backward = np.concatenate([np.cos(angle), -np.sin(angle)], 0) / block
-    return forward.astype(np.float32), backward.astype(np.float32)
+    return halves(forward), halves(backward)
+
+
+def halves(table):
+    high = table.astype(ml_dtypes.bfloat16)
+    low = (table - high.astype(np.float64)).astype(ml_dtypes.bfloat16)
+    return np.stack([high, low])
 
 
 def each(count, body):
@@ -259,9 +265,7 @@
             now, past = proj[index + 1, stream], proj[index, stream]
             value = taps_ref[stream, 0] * now
             for offset in range(1, taps_count):
-                moved = jnp.where(
-                    lane < offset, pltpu.roll(past, offset, 1), pltpu.roll(now, offset, 1)
-                )
+                moved = pltpu.roll(jnp.where(lane < rows - offset, now, past), offset, 1)
                 value = value + taps_ref[stream, offset] * moved
             filtered.append(value)
         query[index] = filtered[0]
@@ -269,17 +273,23 @@
 
     each(blocks, first)
 
+    def product_of(value, table_ref):
+        high = value.astype(jnp.bfloat16)
+        low = (value - high.astype(jnp.float32)).astype(jnp.bfloat16)
+        return (
+            jnp.dot(high, table_ref[0], preferred_element_type=jnp.float32)
+            + jnp.dot(low, table_ref[0], preferred_element_type=jnp.float32)
+            + jnp.dot(high, table_ref[1], preferred_element_type=jnp.float32)
+        )
+
     def apply(source, table_ref, target):
         if chans % 8 == 0:
             flat = source[...].reshape(blocks * chans, source.shape[2])
-            done = jnp.dot(flat, table_ref[...], precision=HIGHEST, preferred_element_type=jnp.float32)
-            target[...] = done.reshape(target.shape)
+            target[...] = product_of(flat, table_ref).reshape(target.shape)
         else:
 
             def one(index):
-                target[index] = jnp.dot(
-                    source[index], table_ref[...], precision=HIGHEST, preferred_element_type=jnp.float32
-                )
+                target[index] = product_of(source[index], table_ref)
 
             each(blocks, one)
 

time: 168 us -> 167 us (level)
  transfers between devices with their start and end apart: 16 -> 16, of which waited for: 11 -> 11; matrix products, arithmetic and copies ran while one was open for 1% -> 1% of each run, Pallas kernels for 6% -> 5%
where the time goes in v20:
time: 167 us
  waiting for transfers between devices  63.1 us (38%)
  blocking collectives  40.7 us (24%)
  starting transfers between devices  32.7 us (20%)
  between operations  13.8 us (8%)
  Pallas kernels  13.4 us (8%)
  local copies, waits for them, and re-layouts  2.81 us (2%)
    all_to_all x1, blocking collectives, per_device(): lax.all_to_all(partial, 'seq', split_axis=0, concat_axis=0, tiled=True)  40.7 us
    ppermute x4, waiting for transfers between devices, return_output(): arrived.append(lax.ppermute(piece, ('seq', 'tp'), pairs))  19.6 us
    all_to_all x1, waiting for transfers between devices, per_device(): lax.all_to_all(gated.reshape((-1,) + gated.shape[3:]), ('tp', 'seq'), spl...  14.4 us
    ppermute x3, waiting for transfers between devices, cross_outer(): lax.ppermute(piece, 'seq', [(i, (i + far) % seq_parts) for i in range(seq...  10.5 us
    ppermute x3, starting transfers between devices, cross_outer(): lax.ppermute(piece, 'seq', [(i, (i + far) % seq_parts) for i in range(seq...  9.2 us
    ppermute x4, starting transfers between devices, return_output(): arrived.append(lax.ppermute(piece, ('seq', 'tp'), pairs))  8.85 us
    ppermute x4, waiting for transfers between devices, share_over_tp(): pieces.append(lax.ppermute(part, 'tp', pairs))  8.77 us
    all_to_all x1, starting transfers between devices, per_device(): lax.all_to_all(long_filter.T.reshape(seq_parts, chans, rows), 'seq', spli...  6.27 us
  transfers between devices with their start and end apart: 16, of which 11 were waited for; matrix products, arithmetic and copies ran while one was open for 1% of the time, Pallas kernels for 5%

profile of v20, /device:TPU:12, one launch (start us, length us, event | category | flops | bytes accessed | tf_op | source)
XLA Modules:
  0.0 166.7 jit_solution(12168659869536956046)
XLA Ops:
  9.6 6.3 %all-to-all-start = ((f32[16,32,128]{2,1,0:T(8,128)}), f32[16,32,128]{2,1,0:T(8,128)S(1)}, u32[]{:S(2)}, u32[]{:S(2)}) async-start(f32[16,32,128]{2,1,0:T(8,128)} %bitcast.16), calls=%async_computation | async-start | bytes 524288 | tf_op jit(solution)/shard_map/all_to_all | solution.py:449
  16.0 5.6 %collective-permute-done = bf16[2,128,1024]{2,1,0:T(8,128)(2,1)S(1)} collective-permute-done((bf16[2,128,1024]{2,1,0:T(8,128)(2,1)S(1)}, bf16[2,128,1024]{2,1,0:T(8,128)(2,1)S(1)}, u32[]{:S(2)}, u32[]{:S(2)}) %collective-permute-start) | collective-permute-done | bytes 524320 | tf_op jit(solution)/shard_map/ppermute | solution.py:107
  21.8 1.6 collective-permute-start.1
  25.0 1.3 collective-permute-start.6
  26.2 3.6 %collective-permute-done.1.refs_2_ = bf16[128,1024]{1,0:T(8,128)(2,1)S(1)} collective-permute-done((bf16[128,1024]{1,0:T(8,128)(2,1)S(1)}, bf16[128,1024]{1,0:T(8,128)(2,1)S(1)}, u32[]{:S(2)}, u32[]{:S(2)}) %collective-permute-start.1) | collective-permute-done | bytes 262176 | tf_op jit(solution)/shard_map/ppermute | solution.py:124
  30.3 6.3 %collective-permute-start.4 = (bf16[128,1024]{1,0:T(8,128)(2,1)S(1)}, bf16[128,1024]{1,0:T(8,128)(2,1)S(1)}, u32[]{:S(2)}, u32[]{:S(2)}) collective-permute-start(bf16[128,1024]{1,0:T(8,128)(2,1)S(1)} %dynamic-slice_bitcast_fusion.1), channel_id=1, source_target_pairs={{0,16},{2,18},{4,20},{6,22},{8,24},{10,26},{12,28},{14,30},{16,0},... | collective-permute-start | bytes 786440 | tf_op jit(solution)/shard_map/ppermute | solution.py:124
  36.6 1.5 collective-permute-start.3
  38.1 3.4 %collective-permute-done.6.refs_6_ = bf16[128,1024]{1,0:T(8,128)(2,1)S(1)} collective-permute-done((bf16[128,1024]{1,0:T(8,128)(2,1)S(1)}, bf16[128,1024]{1,0:T(8,128)(2,1)S(1)}, u32[]{:S(2)}, u32[]{:S(2)}) %collective-permute-start.6) | collective-permute-done | bytes 262176 | tf_op jit(solution)/shard_map/ppermute | solution.py:124
  41.5 3.5 %collective-permute-done.4.refs_4_ = bf16[128,1024]{1,0:T(8,128)(2,1)S(1)} collective-permute-done((bf16[128,1024]{1,0:T(8,128)(2,1)S(1)}, bf16[128,1024]{1,0:T(8,128)(2,1)S(1)}, u32[]{:S(2)}, u32[]{:S(2)}) %collective-permute-start.4) | collective-permute-done | bytes 262176 | tf_op jit(solution)/shard_map/ppermute | solution.py:124
  46.0 4.7 %collective-permute-done.7.refs_7_ = bf16[128,1024]{1,0:T(8,128)(2,1)S(1)} collective-permute-done((bf16[128,1024]{1,0:T(8,128)(2,1)S(1)}, bf16[128,1024]{1,0:T(8,128)(2,1)S(1)}, u32[]{:S(2)}, u32[]{:S(2)}) %collective-permute-start.7) | collective-permute-done | bytes 262176 | tf_op jit(solution)/shard_map/ppermute | solution.py:133
  50.7 3.5 %collective-permute-done.5.refs_5_ = bf16[128,1024]{1,0:T(8,128)(2,1)S(1)} collective-permute-done((bf16[128,1024]{1,0:T(8,128)(2,1)S(1)}, bf16[128,1024]{1,0:T(8,128)(2,1)S(1)}, u32[]{:S(2)}, u32[]{:S(2)}) %collective-permute-start.5) | collective-permute-done | bytes 262176 | tf_op jit(solution)/shard_map/ppermute | solution.py:133
  54.3 3.6 %all-gather.4.cloned.1.call-done = bf16[3,2048,512]{2,1,0:T(8,128)(2,1)} async-done(((bf16[3,512,512]{2,1,0:T(8,128)(2,1)}), bf16[3,2048,512]{2,1,0:T(8,128)(2,1)}) %all-gather.4.cloned.1.call-update) | async-done | bytes 6291472 | tf_op jit(solution)/shard_map/all_gather | solution.py:443
  57.9 5.7 %shard_map.82 = bf16[16,3,32,512]{3,2,1,0:T(8,128)(2,1)S(1)} custom-call(s32[1]{0:T(128)} %bitcast.10.place_ref, bf16[128,1024]{1,0:T(8,128)(2,1)S(1)} %get-tuple-element.31.refs_0_, bf16[128,1024]{1,0:T(8,128)(2,1)S(1)} %collective-permute-done.2.refs_1_, bf16[128,1024]{1,0:T(8,128)(2,1)S(1)} %collective-permute-done.1.refs_2_, ...), custom_call_target="tpu_custom_call" | custom-call | flops 96636764160 | bytes 9961472 | tf_op jit(solution)/shard_map/pallas_call | solution.py:176
  63.6 40.7 %all_to_all.15.refs_0_ = bf16[16,3,32,512]{3,2,1,0:T(8,128)(2,1)S(1)} all-to-all(bf16[16,3,32,512]{3,2,1,0:T(8,128)(2,1)S(1)} %shard_map.82), channel_id=1, replica_groups=mesh['seq'=16,'tp'=2] {'seq'}, dimensions={0} | all-to-all | bytes 3145728 | tf_op jit(solution)/shard_map/all_to_all | solution.py:467
  104.3 2.6 %shard_map.83 = bf16[2,4,4,32,256]{4,3,2,1,0:T(8,128)(2,1)} custom-call(bf16[16,3,32,512]{3,2,1,0:T(8,128)(2,1)S(1)} %all_to_all.15.refs_0_, f32[16,32,128]{2,1,0:T(8,128)S(1)} %all-to-all-done.refs_1_, f32[3,3,32,128]{3,2,1,0:T(8,128)S(1)} %broadcast_in_dim.7.refs_2_, f32[32,128]{1,0:T(8,128)S(1)} %broadcast_in_dim.8.refs_3_, ...), custom_call_target="tpu_custom_call" | custom-call | flops 1000000000 | bytes 4194304 | tf_op jit(solution)/shard_map/pallas_call | solution.py:351
  106.9 4.8 %all-to-all-start.2 = ((bf16[32,32,256]{2,1,0:T(8,128)(2,1)}), bf16[32,32,256]{2,1,0:T(8,128)(2,1)S(1)}, u32[]{:S(2)}, u32[]{:S(2)}) async-start(bf16[32,32,256]{2,1,0:T(8,128)(2,1)} %bitcast.22), calls=%async_computation.2 | async-start | bytes 1048576 | tf_op jit(solution)/shard_map/all_to_all | solution.py:470
  111.8 14.4 %all-to-all-done.2 = bf16[32,32,256]{2,1,0:T(8,128)(2,1)S(1)} async-done(((bf16[32,32,256]{2,1,0:T(8,128)(2,1)}), bf16[32,32,256]{2,1,0:T(8,128)(2,1)S(1)}, u32[]{:S(2)}, u32[]{:S(2)}) %all-to-all-start.2) | async-done | bytes 524320 | tf_op jit(solution)/shard_map/all_to_all | solution.py:470
  126.2 3.6 %shard_map.84 = (bf16[64,2048]{1,0:T(8,128)(2,1)S(1)}, bf16[64,2048]{1,0:T(8,128)(2,1)S(1)}, bf16[64,2048]{1,0:T(8,128)(2,1)S(1)}, bf16[64,2048]{1,0:T(8,128)(2,1)S(1)}) custom-call(s32[4]{0:T(128)S(1)} %pad_add_fusion.block_ref, bf16[2,512,256]{2,1,0:T(8,128)(2,1)S(1)} %bitcast.33, bf16[4,2,512,512]{3,2,1,0:T(8,128)(2,1)} %bitcast.34), custom_call_target="tpu_custom_call" | custom-call | flops 1073741824 | bytes 5767168 | tf_op jit(solution)/shard_map/pallas_call | solution.py:405
  129.8 2.6 %collective-permute-start.8 = (bf16[64,2048]{1,0:T(8,128)(2,1)S(1)}, bf16[64,2048]{1,0:T(8,128)(2,1)S(1)}, u32[]{:S(2)}, u32[]{:S(2)}) collective-permute-start(bf16[64,2048]{1,0:T(8,128)(2,1)S(1)} %get-tuple-element.43), channel_id=1, source_target_pairs={{0,0},{1,16},{2,2},{3,18},{4,4},{5,20},{6,6},{7,22},{8,24},{9,8},{... | collective-permute-start | bytes 786440 | tf_op jit(solution)/shard_map/ppermute | solution.py:88
  132.4 3.9 %collective-permute-start.10 = (bf16[64,2048]{1,0:T(8,128)(2,1)S(1)}, bf16[64,2048]{1,0:T(8,128)(2,1)S(1)}, u32[]{:S(2)}, u32[]{:S(2)}) collective-permute-start(bf16[64,2048]{1,0:T(8,128)(2,1)S(1)} %get-tuple-element.45), channel_id=1, source_target_pairs={{0,16},{1,0},{2,18},{3,2},{4,20},{5,4},{6,22},{7,6},{8,8},{9,24},{... | collective-permute-start | bytes 786440 | tf_op jit(solution)/shard_map/ppermute | solution.py:88
  136.3 2.3 %collective-permute-start.11 = (bf16[64,2048]{1,0:T(8,128)(2,1)S(1)}, bf16[64,2048]{1,0:T(8,128)(2,1)S(1)}, u32[]{:S(2)}, u32[]{:S(2)}) collective-permute-start(bf16[64,2048]{1,0:T(8,128)(2,1)S(1)} %get-tuple-element.46), channel_id=1, source_target_pairs={{0,24},{1,8},{2,26},{3,10},{4,28},{5,12},{6,30},{7,14},{8,0},{9,16... | collective-permute-start | bytes 786440 | tf_op jit(solution)/shard_map/ppermute | solution.py:88
  138.7 3.2 %collective-permute-done.8.refs_0_ = bf16[64,2048]{1,0:T(8,128)(2,1)S(1)} collective-permute-done((bf16[64,2048]{1,0:T(8,128)(2,1)S(1)}, bf16[64,2048]{1,0:T(8,128)(2,1)S(1)}, u32[]{:S(2)}, u32[]{:S(2)}) %collective-permute-start.8) | collective-permute-done | bytes 262176 | tf_op jit(solution)/shard_map/ppermute | solution.py:88
  141.9 16.4 %collective-permute-done.9.refs_1_ = bf16[64,2048]{1,0:T(8,128)(2,1)S(1)} collective-permute-done((bf16[64,2048]{1,0:T(8,128)(2,1)S(1)}, bf16[64,2048]{1,0:T(8,128)(2,1)S(1)}, u32[]{:S(2)}, u32[]{:S(2)}) %collective-permute-start.9) | collective-permute-done | bytes 262176 | tf_op jit(solution)/shard_map/ppermute | solution.py:88
  158.3 1.5 shard_map.85
  (38 shorter events, 6.5 us)
Async XLA Ops:
  6.5 18.1 %copy-start = (f32[3,3,512]{2,1,0:T(4,128)S(1)}, f32[3,3,512]{2,1,0:T(4,128)}, u32[]{:S(2)}) copy-start(f32[3,3,512]{2,1,0:T(4,128)} %param.10) | copy-start | bytes 55300
  6.5 1.2 copy-start.3
  6.5 51.3 %all-gather.4.cloned.1.call-start = ((), (), s32[]{:S(2)}) async-start(), calls=%async_computation.3 | async-start | bytes 7864320 | tf_op jit(solution)/shard_map/all_gather | solution.py:443
  7.8 0.9 copy-start.4
  7.9 13.7 %collective-permute-start = (bf16[2,128,1024]{2,1,0:T(8,128)(2,1)S(1)}, bf16[2,128,1024]{2,1,0:T(8,128)(2,1)S(1)}, u32[]{:S(2)}, u32[]{:S(2)}) collective-permute-start(bf16[2,128,1024]{2,1,0:T(8,128)(2,1)S(1)} %pad_maximum_fusion.1), channel_id=1, source_target_pairs={{0,1},{1,0},{2,3},{3,2},{4,5},{5,4},{6,7},{7,6},{8,9},{9,8},{10,11... | collective-permute-start | bytes 1572872 | tf_op jit(solution)/shard_map/ppermute | solution.py:107
  9.6 15.2 %all-to-all-start = ((f32[16,32,128]{2,1,0:T(8,128)}), f32[16,32,128]{2,1,0:T(8,128)S(1)}, u32[]{:S(2)}, u32[]{:S(2)}) async-start(f32[16,32,128]{2,1,0:T(8,128)} %bitcast.16), calls=%async_computation | async-start | bytes 524288 | tf_op jit(solution)/shard_map/all_to_all | solution.py:449
  15.8 96.0 %all-gather.6.cloned.1.call-start = ((), (), s32[]{:S(2)}) async-start(), calls=%async_computation.4 | async-start | bytes 4718592 | tf_op jit(solution)/shard_map/all_gather | solution.py:463
  21.8 8.0 %collective-permute-start.1 = (bf16[128,1024]{1,0:T(8,128)(2,1)S(1)}, bf16[128,1024]{1,0:T(8,128)(2,1)S(1)}, u32[]{:S(2)}, u32[]{:S(2)}) collective-permute-start(bf16[128,1024]{1,0:T(8,128)(2,1)S(1)} %get-tuple-element.48), channel_id=1, source_target_pairs={{0,8},{2,10},{4,12},{6,14},{8,16},{10,18},{12,20},{14,22},{16,24},... | collective-permute-start | bytes 786440 | tf_op jit(solution)/shard_map/ppermute | solution.py:124
  23.4 6.9 %collective-permute-start.2 = (bf16[128,1024]{1,0:T(8,128)(2,1)S(1)}, bf16[128,1024]{1,0:T(8,128)(2,1)S(1)}, u32[]{:S(2)}, u32[]{:S(2)}) collective-permute-start(bf16[128,1024]{1,0:T(8,128)(2,1)S(1)} %get-tuple-element.31.refs_0_), channel_id=1, source_target_pairs={{0,1},{1,0},{2,3},{3,2},{4,5},{5,4},{6,7},{7,6},{8,9},{9,8},{10,11... | collective-permute-start | bytes 786440 | tf_op jit(solution)/shard_map/ppermute | solution.py:133
  25.0 16.5 %collective-permute-start.6 = (bf16[128,1024]{1,0:T(8,128)(2,1)S(1)}, bf16[128,1024]{1,0:T(8,128)(2,1)S(1)}, u32[]{:S(2)}, u32[]{:S(2)}) collective-permute-start(bf16[128,1024]{1,0:T(8,128)(2,1)S(1)} %dynamic-slice_bitcast_fusion), channel_id=1, source_target_pairs={{0,24},{2,26},{4,28},{6,30},{8,0},{10,2},{12,4},{14,6},{16,8},{18,... | collective-permute-start | bytes 786440 | tf_op jit(solution)/shard_map/ppermute | solution.py:124
  30.3 14.6 %collective-permute-start.4 = (bf16[128,1024]{1,0:T(8,128)(2,1)S(1)}, bf16[128,1024]{1,0:T(8,128)(2,1)S(1)}, u32[]{:S(2)}, u32[]{:S(2)}) collective-permute-start(bf16[128,1024]{1,0:T(8,128)(2,1)S(1)} %dynamic-slice_bitcast_fusion.1), channel_id=1, source_target_pairs={{0,16},{2,18},{4,20},{6,22},{8,24},{10,26},{12,28},{14,30},{16,0},... | collective-permute-start | bytes 786440 | tf_op jit(solution)/shard_map/ppermute | solution.py:124
  36.6 14.1 %collective-permute-start.3 = (bf16[128,1024]{1,0:T(8,128)(2,1)S(1)}, bf16[128,1024]{1,0:T(8,128)(2,1)S(1)}, u32[]{:S(2)}, u32[]{:S(2)}) collective-permute-start(bf16[128,1024]{1,0:T(8,128)(2,1)S(1)} %collective-permute-done.1.refs_2_), channel_id=1, source_target_pairs={{0,1},{1,0},{2,3},{3,2},{4,5},{5,4},{6,7},{7,6},{8,9},{9,8},{10,11... | collective-permute-start | bytes 786440 | tf_op jit(solution)/shard_map/ppermute | solution.py:133
  41.5 9.2 %collective-permute-start.7 = (bf16[128,1024]{1,0:T(8,128)(2,1)S(1)}, bf16[128,1024]{1,0:T(8,128)(2,1)S(1)}, u32[]{:S(2)}, u32[]{:S(2)}) collective-permute-start(bf16[128,1024]{1,0:T(8,128)(2,1)S(1)} %collective-permute-done.6.refs_6_), channel_id=1, source_target_pairs={{0,1},{1,0},{2,3},{3,2},{4,5},{5,4},{6,7},{7,6},{8,9},{9,8},{10,11... | collective-permute-start | bytes 786440 | tf_op jit(solution)/shard_map/ppermute | solution.py:133
  45.0 9.3 %collective-permute-start.5 = (bf16[128,1024]{1,0:T(8,128)(2,1)S(1)}, bf16[128,1024]{1,0:T(8,128)(2,1)S(1)}, u32[]{:S(2)}, u32[]{:S(2)}) collective-permute-start(bf16[128,1024]{1,0:T(8,128)(2,1)S(1)} %collective-permute-done.4.refs_4_), channel_id=1, source_target_pairs={{0,1},{1,0},{2,3},{3,2},{4,5},{5,4},{6,7},{7,6},{8,9},{9,8},{10,11... | collective-permute-start | bytes 786440 | tf_op jit(solution)/shard_map/ppermute | solution.py:133
  63.6 40.7 %copy-start.1 = (bf16[2,256,256]{2,1,0:T(8,128)(2,1)S(1)}, bf16[2,256,256]{2,1,0:T(8,128)(2,1)}, u32[]{:S(2)}) copy-start(bf16[2,256,256]{2,1,0:T(8,128)(2,1)} %constant.234.clone.refs_5_) | copy-start | bytes 786436
  63.6 40.7 %copy-start.2 = (bf16[2,128,256]{2,1,0:T(8,128)(2,1)S(1)}, bf16[2,128,256]{2,1,0:T(8,128)(2,1)}, u32[]{:S(2)}) copy-start(bf16[2,128,256]{2,1,0:T(8,128)(2,1)} %constant.233.clone.refs_4_) | copy-start | bytes 393220
  106.9 19.3 %all-to-all-start.2 = ((bf16[32,32,256]{2,1,0:T(8,128)(2,1)}), bf16[32,32,256]{2,1,0:T(8,128)(2,1)S(1)}, u32[]{:S(2)}, u32[]{:S(2)}) async-start(bf16[32,32,256]{2,1,0:T(8,128)(2,1)} %bitcast.22), calls=%async_computation.2 | async-start | bytes 1048576 | tf_op jit(solution)/shard_map/all_to_all | solution.py:470
  129.8 12.1 %collective-permute-start.8 = (bf16[64,2048]{1,0:T(8,128)(2,1)S(1)}, bf16[64,2048]{1,0:T(8,128)(2,1)S(1)}, u32[]{:S(2)}, u32[]{:S(2)}) collective-permute-start(bf16[64,2048]{1,0:T(8,128)(2,1)S(1)} %get-tuple-element.43), channel_id=1, source_target_pairs={{0,0},{1,16},{2,2},{3,18},{4,4},{5,20},{6,6},{7,22},{8,24},{9,8},{... | collective-permute-start | bytes 786440 | tf_op jit(solution)/shard_map/ppermute | solution.py:88
  132.4 25.9 %collective-permute-start.9 = (bf16[64,2048]{1,0:T(8,128)(2,1)S(1)}, bf16[64,2048]{1,0:T(8,128)(2,1)S(1)}, u32[]{:S(2)}, u32[]{:S(2)}) collective-permute-start(bf16[64,2048]{1,0:T(8,128)(2,1)S(1)} %get-tuple-element.44), channel_id=1, source_target_pairs={{0,8},{1,24},{2,10},{3,26},{4,12},{5,28},{6,14},{7,30},{8,16},{9,0... | collective-permute-start | bytes 786440 | tf_op jit(solution)/shard_map/ppermute | solution.py:88
  132.4 25.8 %collective-permute-start.10 = (bf16[64,2048]{1,0:T(8,128)(2,1)S(1)}, bf16[64,2048]{1,0:T(8,128)(2,1)S(1)}, u32[]{:S(2)}, u32[]{:S(2)}) collective-permute-start(bf16[64,2048]{1,0:T(8,128)(2,1)S(1)} %get-tuple-element.45), channel_id=1, source_target_pairs={{0,16},{1,0},{2,18},{3,2},{4,20},{5,4},{6,22},{7,6},{8,8},{9,24},{... | collective-permute-start | bytes 786440 | tf_op jit(solution)/shard_map/ppermute | solution.py:88
  136.3 22.0 %collective-permute-start.11 = (bf16[64,2048]{1,0:T(8,128)(2,1)S(1)}, bf16[64,2048]{1,0:T(8,128)(2,1)S(1)}, u32[]{:S(2)}, u32[]{:S(2)}) collective-permute-start(bf16[64,2048]{1,0:T(8,128)(2,1)S(1)} %get-tuple-element.46), channel_id=1, source_target_pairs={{0,24},{1,8},{2,26},{3,10},{4,28},{5,12},{6,30},{7,14},{8,0},{9,16... | collective-permute-start | bytes 786440 | tf_op jit(solution)/shard_map/ppermute | solution.py:88
Sparse Core Ops, SparseCore 0:
  8.9 48.8 all-gather.3
  59.7 51.3 all-gather.5

commit v21 on v20

--- a/solution.py
+++ b/solution.py
@@ -89,24 +89,25 @@
     return assemble(arrived, places, (tp_parts * part_rows, per_tp * width))
 
 
-def share_columns(features, outer, tp_parts):
-    rows, cols = features.shape
+def share_columns(features, outer, inner_parts, tp_parts):
+    _, cols = features.shape
     per_tp = outer // tp_parts
+    width = cols // outer
     tp_place = lax.axis_index("tp")
-    width = cols // outer
+    outer_place = lax.axis_index("seq") // inner_parts
     held = []
-    for step in range(tp_parts):
-        which = (tp_place + step) % tp_parts
-        piece = jnp.stack(
-            [
-                lax.dynamic_slice_in_dim(features, (group * tp_parts + which) * width, width, axis=1)
-                for group in range(per_tp)
-            ]
-        )
-        if step:
-            piece = lax.ppermute(piece, "tp", [(i, (i + step) % tp_parts) for i in range(tp_parts)])
-        held.append(piece)
-    return jnp.concatenate(held)
+    for after in range(per_tp):
+        group = (outer_place + 1 + after) % per_tp
+        pieces = []
+        for step in range(tp_parts):
+            column = (group * tp_parts + (tp_place + step) % tp_parts) * width
+            piece = lax.dynamic_slice_in_dim(features, column, width, axis=1)
+            if step:
+                pairs = [(i, (i + step) % tp_parts) for i in range(tp_parts)]
+                piece = lax.ppermute(piece, "tp", pairs)
+            pieces.append(piece)
+        held.append(jnp.stack(pieces))
+    return held
 
 
 def cross_outer(held, steps, outer, inner_parts, tp_parts):
@@ -117,8 +118,8 @@
     arrived = {}
     for step in steps:
         target = (outer_place + step) % outer
-        which = (tp_place - target // per_tp + tp_parts) % tp_parts * per_tp + target % per_tp
-        piece = lax.dynamic_index_in_dim(held, which, axis=0, keepdims=False)
+        which = (tp_place - target // per_tp + tp_parts) % tp_parts
+        piece = lax.dynamic_index_in_dim(held[(step - 1) % per_tp], which, axis=0, keepdims=False)
         if step:
             far = step * inner_parts
             piece = lax.ppermute(piece, "seq", [(i, (i + far) % seq_parts) for i in range(seq_parts)])
@@ -137,16 +138,20 @@
 def project_kernel(tp_parts, place_ref, *refs):
     *share_refs, weight_ref, out_ref, held, sems = refs
     seq_parts, streams, chans, count = out_ref.shape
+    near_parts, far_parts = weight_ref.shape[:2]
+    blocks = near_parts * far_parts // tp_parts
     copies = []
     for stream in range(streams):
         for step in range(tp_parts):
             which = lax.rem(place_ref[0] - step + tp_parts, tp_parts)
-            copies.append(
-                pltpu.make_async_copy(
-                    weight_ref.at[stream, which], held.at[stream, step], sems.at[len(copies)]
+            for block in range(blocks):
+                inner = which * blocks + block
+                source = weight_ref.at[lax.rem(inner, near_parts), inner // near_parts, stream]
+                slot = len(copies)
+                copies.append(
+                    pltpu.make_async_copy(source, held.at[stream, step, block], sems.at[slot])
                 )
-            )
-            copies[-1].start()
+                copies[-1].start()
     left = [
         jnp.concatenate([share_ref[...] for share_ref in share_refs[step::tp_parts]])
         for step in range(tp_parts)
@@ -154,9 +159,13 @@
     for stream in range(streams):
         sums = jnp.zeros((count, seq_parts * chans), jnp.float32)
         for step in range(tp_parts):
-            copies[stream * tp_parts + step].wait()
+            first = (stream * tp_parts + step) * blocks
+            for copy in copies[first : first + blocks]:
+                copy.wait()
             sums = sums + jnp.dot(
-                left[step], held[stream, step], preferred_element_type=jnp.float32
+                left[step],
+                held[stream, step].reshape(left[step].shape[1], -1),
+                preferred_element_type=jnp.float32,
             )
         turned = sums.astype(out_ref.dtype).T
         for seq in range(seq_parts):
@@ -166,8 +175,8 @@
 def project_in(chunks, weight, seq_parts):
     tp_parts = len(chunks[0])
     rows, width = chunks[0][0].shape
-    streams, _, chan_tp = weight.shape
-    weight = weight.reshape(streams, tp_parts, width, chan_tp)
+    near_parts, far_parts, streams, depth, chan_tp = weight.shape
+    blocks = near_parts * far_parts // tp_parts
     chans = chan_tp // seq_parts
     pieces = [piece for chunk in chunks for piece in chunk]
     count = len(chunks) * rows
@@ -181,8 +190,8 @@
         out_specs=vmem,
         out_shape=jax.ShapeDtypeStruct((seq_parts, streams, chans, count), jnp.bfloat16),
         scratch_shapes=[
-            pltpu.VMEM(weight.shape, weight.dtype),
-            pltpu.SemaphoreType.DMA((streams * tp_parts,)),
+            pltpu.VMEM((streams, tp_parts, blocks, depth, chan_tp), weight.dtype),
+            pltpu.SemaphoreType.DMA((streams * tp_parts * blocks,)),
         ],
         compiler_params=pltpu.CompilerParams(vmem_limit_bytes=48 * 2**20),
         cost_estimate=pl.CostEstimate(
@@ -440,7 +449,12 @@
         [index * tp_parts + tp for index in group for tp in range(tp_parts)] for group in inner_groups
     ]
 
-    weight = lax.all_gather(in_proj, "seq", axis=1, tiled=True, axis_index_groups=inner_groups)
+    near = 2 if inner_parts % 2 == 0 else 1
+    far_groups = [group[index::near] for group in inner_groups for index in range(near)]
+    near_groups = [
+        group[index : index + near] for group in inner_groups for index in range(0, inner_parts, near)
+    ]
+    weight = lax.all_gather(in_proj, "seq", axis_index_groups=far_groups)
 
     taps = lax.dynamic_slice_in_dim(short_taps, position * chans, chans, axis=2)
     taps = jnp.broadcast_to(taps[..., None], taps.shape + (rows,))
@@ -450,15 +464,19 @@
         long_filter.T.reshape(seq_parts, chans, rows), "seq", split_axis=0, concat_axis=0, tiled=True
     )
 
-    held = share_columns(features, outer, tp_parts)
+    held = share_columns(features, outer, inner_parts, tp_parts)
     arrived = cross_outer(held, (0, 1), outer, inner_parts, tp_parts)
-    held, taps, skip, filter_blocks = lax.optimization_barrier((held, taps, skip, filter_blocks))
+    held[0], taps, skip, filter_blocks = lax.optimization_barrier((held[0], taps, skip, filter_blocks))
     if outer > 2:
         arrived |= cross_outer(held, (outer - 1,), outer, inner_parts, tp_parts)
     own = share_over_tp(arrived[0], tp_parts)
     held, arrived[1], own = lax.optimization_barrier((held, arrived[1], own))
     arrived |= cross_outer(held, range(2, outer - 1), outer, inner_parts, tp_parts)
     chunks = [own] + [share_over_tp(arrived[step], tp_parts) for step in range(1, outer)]
+    last = chunks[outer // 2]
+    last[0], weight = lax.optimization_barrier((last[0], weight))
+    weight = lax.all_gather(weight, "seq", axis_index_groups=near_groups)
+
     chunks, out_proj = lax.optimization_barrier((chunks, out_proj))
     out_weight = lax.all_gather(out_proj, ("seq", "tp"), axis_index_groups=tp_groups)
     out_weight = out_weight.reshape((inner_parts, tp_parts) + out_proj.shape)

time: 167 us -> 190 us (1.14)
  waiting for transfers between devices: 63.1 us -> 86.3 us
  starting transfers between devices: 32.7 us -> 29.8 us
  blocking collectives: 40.7 us -> 42.8 us
    ppermute x3, waiting for transfers between devices: 10.5 us -> 22.8 us  [cross_outer(): lax.ppermute(piece, 'seq', [(i, (i + far) % seq_parts) for i in range(seq...]
    all_gather x1 -> x2, waiting for transfers between devices: 3.59 us -> 13.2 us  [the longest x1 13.1 us: per_device(): weight = lax.all_gather(in_proj, 'seq', axis_index_groups=far_groups)]
    ppermute x3, starting transfers between devices: 9.2 us -> 4.65 us  [cross_outer(): lax.ppermute(piece, 'seq', [(i, (i + far) % seq_parts) for i in range(seq...]
    ppermute x1 -> x2, waiting for transfers between devices: 5.62 us -> 2.72 us  [share_columns(): piece = lax.ppermute(piece, 'tp', pairs)]
    ppermute x4, waiting for transfers between devices: 8.77 us -> 11 us  [share_over_tp(): pieces.append(lax.ppermute(part, 'tp', pairs))]
    all_to_all x1, blocking collectives: 40.7 us -> 42.8 us  [per_device(): lax.all_to_all(partial, 'seq', split_axis=0, concat_axis=0, tiled=True)]
    all_to_all x1, waiting for transfers between devices: 0.01 us -> 2 us  [per_device(): lax.all_to_all(long_filter.T.reshape(seq_parts, chans, rows), 'seq', spli...]
  transfers between devices with their start and end apart: 16 -> 18, of which waited for: 11 -> 11; matrix products, arithmetic and copies ran while one was open for 1% -> 2% of each run, Pallas kernels for 5% -> 4%
where the time goes in v21:
time: 190 us
  waiting for transfers between devices  86.3 us (45%)
  blocking collectives  42.8 us (23%)
  starting transfers between devices  29.8 us (16%)
  between operations  13.6 us (7%)
  Pallas kernels  13.5 us (7%)
  local copies, waits for them, and re-layouts  3.25 us (2%)
    all_to_all x1, blocking collectives, per_device(): lax.all_to_all(partial, 'seq', split_axis=0, concat_axis=0, tiled=True)  42.8 us
    ppermute x3, waiting for transfers between devices, cross_outer(): lax.ppermute(piece, 'seq', [(i, (i + far) % seq_parts) for i in range(seq...  22.8 us
    ppermute x4, waiting for transfers between devices, return_output(): arrived.append(lax.ppermute(piece, ('seq', 'tp'), pairs))  19.5 us
    all_to_all x1, waiting for transfers between devices, per_device(): lax.all_to_all(gated.reshape((-1,) + gated.shape[3:]), ('tp', 'seq'), spl...  14.4 us
    all_gather x1, waiting for transfers between devices, per_device(): weight = lax.all_gather(in_proj, 'seq', axis_index_groups=far_groups)  13.1 us
    ppermute x4, waiting for transfers between devices, share_over_tp(): pieces.append(lax.ppermute(part, 'tp', pairs))  11 us
    ppermute x4, starting transfers between devices, return_output(): arrived.append(lax.ppermute(piece, ('seq', 'tp'), pairs))  8.85 us
    all_to_all x1, starting transfers between devices, per_device(): lax.all_to_all(long_filter.T.reshape(seq_parts, chans, rows), 'seq', spli...  6.27 us
  transfers between devices with their start and end apart: 18, of which 11 were waited for; matrix products, arithmetic and copies ran while one was open for 2% of the time, Pallas kernels for 4%

profile of v21, /device:TPU:12, one launch (start us, length us, event | category | flops | bytes accessed | tf_op | source)
XLA Modules:
  0.0 189.7 jit_solution(10961769839270511884)
XLA Ops:
  9.2 1.5 collective-permute-start.1
  11.6 6.3 %all-to-all-start = ((f32[16,32,128]{2,1,0:T(8,128)}), f32[16,32,128]{2,1,0:T(8,128)S(1)}, u32[]{:S(2)}, u32[]{:S(2)}) async-start(f32[16,32,128]{2,1,0:T(8,128)} %bitcast.14), calls=%async_computation | async-start | bytes 524288 | tf_op jit(solution)/shard_map/all_to_all | solution.py:463
  19.6 2.7 %collective-permute-done.1 = bf16[128,1024]{1,0:T(8,128)(2,1)S(1)} collective-permute-done((bf16[128,1024]{1,0:T(8,128)(2,1)S(1)}, bf16[128,1024]{1,0:T(8,128)(2,1)S(1)}, u32[]{:S(2)}, u32[]{:S(2)}) %collective-permute-start.1) | collective-permute-done | bytes 262176 | tf_op jit(solution)/shard_map/ppermute | solution.py:107
  24.0 2.0 %all-to-all-done.refs_1_ = f32[16,32,128]{2,1,0:T(8,128)S(1)} async-done(((f32[16,32,128]{2,1,0:T(8,128)}), f32[16,32,128]{2,1,0:T(8,128)S(1)}, u32[]{:S(2)}, u32[]{:S(2)}) %all-to-all-start) | async-done | bytes 262176 | tf_op jit(solution)/shard_map/all_to_all | solution.py:463
  26.1 3.7 %collective-permute-done.2.refs_2_ = bf16[128,1024]{1,0:T(8,128)(2,1)S(1)} collective-permute-done((bf16[128,1024]{1,0:T(8,128)(2,1)S(1)}, bf16[128,1024]{1,0:T(8,128)(2,1)S(1)}, u32[]{:S(2)}, u32[]{:S(2)}) %collective-permute-start.2) | collective-permute-done | bytes 262176 | tf_op jit(solution)/shard_map/ppermute | solution.py:125
  29.8 2.5 %collective-permute-start.5 = (bf16[128,1024]{1,0:T(8,128)(2,1)S(1)}, bf16[128,1024]{1,0:T(8,128)(2,1)S(1)}, u32[]{:S(2)}, u32[]{:S(2)}) collective-permute-start(bf16[128,1024]{1,0:T(8,128)(2,1)S(1)} %dynamic-slice_bitcast_fusion.1), channel_id=1, source_target_pairs={{0,16},{2,18},{4,20},{6,22},{8,24},{10,26},{12,28},{14,30},{16,0},... | collective-permute-start | bytes 786440 | tf_op jit(solution)/shard_map/ppermute | solution.py:125
  32.4 11.9 %collective-permute-done.5.refs_4_ = bf16[128,1024]{1,0:T(8,128)(2,1)S(1)} collective-permute-done((bf16[128,1024]{1,0:T(8,128)(2,1)S(1)}, bf16[128,1024]{1,0:T(8,128)(2,1)S(1)}, u32[]{:S(2)}, u32[]{:S(2)}) %collective-permute-start.5) | collective-permute-done | bytes 262176 | tf_op jit(solution)/shard_map/ppermute | solution.py:125
  44.3 13.1 %all-gather.7.cloned.1.call-done = bf16[6,512,512]{2,1,0:T(8,128)(2,1)} async-done(((bf16[3,512,512]{2,1,0:T(8,128)(2,1)}), bf16[6,512,512]{2,1,0:T(8,128)(2,1)}) %all-gather.7.cloned.1.call-update) | async-done | bytes 3145744 | tf_op jit(solution)/shard_map/all_gather | solution.py:457
  58.7 7.2 %collective-permute-done.7.refs_6_ = bf16[128,1024]{1,0:T(8,128)(2,1)S(1)} collective-permute-done((bf16[128,1024]{1,0:T(8,128)(2,1)S(1)}, bf16[128,1024]{1,0:T(8,128)(2,1)S(1)}, u32[]{:S(2)}, u32[]{:S(2)}) %collective-permute-start.7) | collective-permute-done | bytes 262176 | tf_op jit(solution)/shard_map/ppermute | solution.py:125
  66.4 1.5 collective-permute-start.6
  67.9 7.2 %collective-permute-done.8.refs_7_ = bf16[128,1024]{1,0:T(8,128)(2,1)S(1)} collective-permute-done((bf16[128,1024]{1,0:T(8,128)(2,1)S(1)}, bf16[128,1024]{1,0:T(8,128)(2,1)S(1)}, u32[]{:S(2)}, u32[]{:S(2)}) %collective-permute-start.8) | collective-permute-done | bytes 262176 | tf_op jit(solution)/shard_map/ppermute | solution.py:134
  75.2 3.8 %collective-permute-done.6.refs_5_ = bf16[128,1024]{1,0:T(8,128)(2,1)S(1)} collective-permute-done((bf16[128,1024]{1,0:T(8,128)(2,1)S(1)}, bf16[128,1024]{1,0:T(8,128)(2,1)S(1)}, u32[]{:S(2)}, u32[]{:S(2)}) %collective-permute-start.6) | collective-permute-done | bytes 262176 | tf_op jit(solution)/shard_map/ppermute | solution.py:134
  79.0 5.7 %shard_map.82 = bf16[16,3,32,512]{3,2,1,0:T(8,128)(2,1)S(1)} custom-call(s32[1]{0:T(128)} %bitcast.10.place_ref, bf16[128,1024]{1,0:T(8,128)(2,1)S(1)} %fusion.1.refs_0_, bf16[128,1024]{1,0:T(8,128)(2,1)S(1)} %collective-permute-done.3.refs_1_, bf16[128,1024]{1,0:T(8,128)(2,1)S(1)} %collective-permute-done.2.refs_2_, ...), custom_call_target="tpu_custom_call" | custom-call | flops 96636764160 | bytes 9961472 | tf_op jit(solution)/shard_map/pallas_call | solution.py:185
  84.8 42.8 %all_to_all.15.refs_0_ = bf16[16,3,32,512]{3,2,1,0:T(8,128)(2,1)S(1)} all-to-all(bf16[16,3,32,512]{3,2,1,0:T(8,128)(2,1)S(1)} %shard_map.82), channel_id=1, replica_groups=mesh['seq'=16,'tp'=2] {'seq'}, dimensions={0} | all-to-all | bytes 3145728 | tf_op jit(solution)/shard_map/all_to_all | solution.py:485
  127.6 2.6 %shard_map.83 = bf16[2,4,4,32,256]{4,3,2,1,0:T(8,128)(2,1)} custom-call(bf16[16,3,32,512]{3,2,1,0:T(8,128)(2,1)S(1)} %all_to_all.15.refs_0_, f32[16,32,128]{2,1,0:T(8,128)S(1)} %all-to-all-done.refs_1_, f32[3,3,32,128]{3,2,1,0:T(8,128)S(1)} %broadcast_in_dim.7.refs_2_, f32[32,128]{1,0:T(8,128)S(1)} %broadcast_in_dim.8.refs_3_, ...), custom_call_target="tpu_custom_call" | custom-call | flops 1000000000 | bytes 4194304 | tf_op jit(solution)/shard_map/pallas_call | solution.py:360
  130.2 4.7 %all-to-all-start.2 = ((bf16[32,32,256]{2,1,0:T(8,128)(2,1)}), bf16[32,32,256]{2,1,0:T(8,128)(2,1)S(1)}, u32[]{:S(2)}, u32[]{:S(2)}) async-start(bf16[32,32,256]{2,1,0:T(8,128)(2,1)} %bitcast.23), calls=%async_computation.2 | async-start | bytes 1048576 | tf_op jit(solution)/shard_map/all_to_all | solution.py:488
  135.1 14.4 %all-to-all-done.2 = bf16[32,32,256]{2,1,0:T(8,128)(2,1)S(1)} async-done(((bf16[32,32,256]{2,1,0:T(8,128)(2,1)}), bf16[32,32,256]{2,1,0:T(8,128)(2,1)S(1)}, u32[]{:S(2)}, u32[]{:S(2)}) %all-to-all-start.2) | async-done | bytes 524320 | tf_op jit(solution)/shard_map/all_to_all | solution.py:488
  149.5 3.6 %shard_map.84 = (bf16[64,2048]{1,0:T(8,128)(2,1)S(1)}, bf16[64,2048]{1,0:T(8,128)(2,1)S(1)}, bf16[64,2048]{1,0:T(8,128)(2,1)S(1)}, bf16[64,2048]{1,0:T(8,128)(2,1)S(1)}) custom-call(s32[4]{0:T(128)S(1)} %pad_add_fusion.block_ref, bf16[2,512,256]{2,1,0:T(8,128)(2,1)S(1)} %bitcast.32, bf16[4,2,512,512]{3,2,1,0:T(8,128)(2,1)} %bitcast.33), custom_call_target="tpu_custom_call" | custom-call | flops 1073741824 | bytes 5767168 | tf_op jit(solution)/shard_map/pallas_call | solution.py:414
  153.1 2.6 %collective-permute-start.9 = (bf16[64,2048]{1,0:T(8,128)(2,1)S(1)}, bf16[64,2048]{1,0:T(8,128)(2,1)S(1)}, u32[]{:S(2)}, u32[]{:S(2)}) collective-permute-start(bf16[64,2048]{1,0:T(8,128)(2,1)S(1)} %get-tuple-element.47), channel_id=1, source_target_pairs={{0,0},{1,16},{2,2},{3,18},{4,4},{5,20},{6,6},{7,22},{8,24},{9,8},{... | collective-permute-start | bytes 786440 | tf_op jit(solution)/shard_map/ppermute | solution.py:88
  155.8 3.9 %collective-permute-start.11 = (bf16[64,2048]{1,0:T(8,128)(2,1)S(1)}, bf16[64,2048]{1,0:T(8,128)(2,1)S(1)}, u32[]{:S(2)}, u32[]{:S(2)}) collective-permute-start(bf16[64,2048]{1,0:T(8,128)(2,1)S(1)} %get-tuple-element.49), channel_id=1, source_target_pairs={{0,16},{1,0},{2,18},{3,2},{4,20},{5,4},{6,22},{7,6},{8,8},{9,24},{... | collective-permute-start | bytes 786440 | tf_op jit(solution)/shard_map/ppermute | solution.py:88
  159.6 2.3 %collective-permute-start.12 = (bf16[64,2048]{1,0:T(8,128)(2,1)S(1)}, bf16[64,2048]{1,0:T(8,128)(2,1)S(1)}, u32[]{:S(2)}, u32[]{:S(2)}) collective-permute-start(bf16[64,2048]{1,0:T(8,128)(2,1)S(1)} %get-tuple-element.50), channel_id=1, source_target_pairs={{0,24},{1,8},{2,26},{3,10},{4,28},{5,12},{6,30},{7,14},{8,0},{9,16... | collective-permute-start | bytes 786440 | tf_op jit(solution)/shard_map/ppermute | solution.py:88
  162.0 3.2 %collective-permute-done.9.refs_0_ = bf16[64,2048]{1,0:T(8,128)(2,1)S(1)} collective-permute-done((bf16[64,2048]{1,0:T(8,128)(2,1)S(1)}, bf16[64,2048]{1,0:T(8,128)(2,1)S(1)}, u32[]{:S(2)}, u32[]{:S(2)}) %collective-permute-start.9) | collective-permute-done | bytes 262176 | tf_op jit(solution)/shard_map/ppermute | solution.py:88
  165.2 16.4 %collective-permute-done.10.refs_1_ = bf16[64,2048]{1,0:T(8,128)(2,1)S(1)} collective-permute-done((bf16[64,2048]{1,0:T(8,128)(2,1)S(1)}, bf16[64,2048]{1,0:T(8,128)(2,1)S(1)}, u32[]{:S(2)}, u32[]{:S(2)}) %collective-permute-start.10) | collective-permute-done | bytes 262176 | tf_op jit(solution)/shard_map/ppermute | solution.py:88
  181.6 1.5 shard_map.85
  (42 shorter events, 8.8 us)
Async XLA Ops:
  6.5 16.5 %copy-start = (f32[3,3,512]{2,1,0:T(4,128)S(1)}, f32[3,3,512]{2,1,0:T(4,128)}, u32[]{:S(2)}) copy-start(f32[3,3,512]{2,1,0:T(4,128)} %param.10) | copy-start | bytes 55300
  6.5 4.2 %copy-start.3 = (f32[128,512]{1,0:T(8,128)S(1)}, f32[128,512]{1,0:T(8,128)}, u32[]{:S(2)}) copy-start(f32[128,512]{1,0:T(8,128)} %param.11) | copy-start | bytes 786436
  6.5 50.9 %all-gather.7.cloned.1.call-start = ((), (), s32[]{:S(2)}) async-start(), calls=%async_computation.3 | async-start | bytes 4718592 | tf_op jit(solution)/shard_map/all_gather | solution.py:457
  8.6 9.4 %collective-permute-start = (bf16[128,1024]{1,0:T(8,128)(2,1)S(1)}, bf16[128,1024]{1,0:T(8,128)(2,1)S(1)}, u32[]{:S(2)}, u32[]{:S(2)}) collective-permute-start(bf16[128,1024]{1,0:T(8,128)(2,1)S(1)} %get-tuple-element.52), channel_id=1, source_target_pairs={{0,1},{1,0},{2,3},{3,2},{4,5},{5,4},{6,7},{7,6},{8,9},{9,8},{10,11... | collective-permute-start | bytes 786440 | tf_op jit(solution)/shard_map/ppermute | solution.py:107
  9.2 13.2 %collective-permute-start.1 = (bf16[128,1024]{1,0:T(8,128)(2,1)S(1)}, bf16[128,1024]{1,0:T(8,128)(2,1)S(1)}, u32[]{:S(2)}, u32[]{:S(2)}) collective-permute-start(bf16[128,1024]{1,0:T(8,128)(2,1)S(1)} %get-tuple-element.54), channel_id=1, source_target_pairs={{0,1},{1,0},{2,3},{3,2},{4,5},{5,4},{6,7},{7,6},{8,9},{9,8},{10,11... | collective-permute-start | bytes 786440 | tf_op jit(solution)/shard_map/ppermute | solution.py:107
  11.6 14.4 %all-to-all-start = ((f32[16,32,128]{2,1,0:T(8,128)}), f32[16,32,128]{2,1,0:T(8,128)S(1)}, u32[]{:S(2)}, u32[]{:S(2)}) async-start(f32[16,32,128]{2,1,0:T(8,128)} %bitcast.14), calls=%async_computation | async-start | bytes 524288 | tf_op jit(solution)/shard_map/all_to_all | solution.py:463
  17.8 61.2 %all-gather.9.cloned.1.call-start = ((), (), s32[]{:S(2)}) async-start(), calls=%async_computation.4 | async-start | bytes 9437184 | tf_op jit(solution)/shard_map/all_gather | solution.py:478
  18.1 11.7 %collective-permute-start.2 = (bf16[128,1024]{1,0:T(8,128)(2,1)S(1)}, bf16[128,1024]{1,0:T(8,128)(2,1)S(1)}, u32[]{:S(2)}, u32[]{:S(2)}) collective-permute-start(bf16[128,1024]{1,0:T(8,128)(2,1)S(1)} %fusion.3), channel_id=1, source_target_pairs={{0,8},{2,10},{4,12},{6,14},{8,16},{10,18},{12,20},{14,22},{16,24},... | collective-permute-start | bytes 786440 | tf_op jit(solution)/shard_map/ppermute | solution.py:125
  22.5 7.4 %collective-permute-start.3 = (bf16[128,1024]{1,0:T(8,128)(2,1)S(1)}, bf16[128,1024]{1,0:T(8,128)(2,1)S(1)}, u32[]{:S(2)}, u32[]{:S(2)}) collective-permute-start(bf16[128,1024]{1,0:T(8,128)(2,1)S(1)} %fusion.1.refs_0_), channel_id=1, source_target_pairs={{0,1},{1,0},{2,3},{3,2},{4,5},{5,4},{6,7},{7,6},{8,9},{9,8},{10,11... | collective-permute-start | bytes 786440 | tf_op jit(solution)/shard_map/ppermute | solution.py:134
  29.8 14.5 %collective-permute-start.5 = (bf16[128,1024]{1,0:T(8,128)(2,1)S(1)}, bf16[128,1024]{1,0:T(8,128)(2,1)S(1)}, u32[]{:S(2)}, u32[]{:S(2)}) collective-permute-start(bf16[128,1024]{1,0:T(8,128)(2,1)S(1)} %dynamic-slice_bitcast_fusion.1), channel_id=1, source_target_pairs={{0,16},{2,18},{4,20},{6,22},{8,24},{10,26},{12,28},{14,30},{16,0},... | collective-permute-start | bytes 786440 | tf_op jit(solution)/shard_map/ppermute | solution.py:125
  57.5 77.6 %all-gather.11.cloned.1.call-start = ((), (), s32[]{:S(2)}) async-start(), calls=%async_computation.5 | async-start | bytes 4718592 | tf_op jit(solution)/shard_map/all_gather | solution.py:481
  57.6 8.3 %collective-permute-start.7 = (bf16[128,1024]{1,0:T(8,128)(2,1)S(1)}, bf16[128,1024]{1,0:T(8,128)(2,1)S(1)}, u32[]{:S(2)}, u32[]{:S(2)}) collective-permute-start(bf16[128,1024]{1,0:T(8,128)(2,1)S(1)} %dynamic-slice_bitcast_fusion), channel_id=1, source_target_pairs={{0,24},{2,26},{4,28},{6,30},{8,0},{10,2},{12,4},{14,6},{16,8},{18,... | collective-permute-start | bytes 786440 | tf_op jit(solution)/shard_map/ppermute | solution.py:125
  58.2 9.7 %collective-permute-start.4 = (bf16[128,1024]{1,0:T(8,128)(2,1)S(1)}, bf16[128,1024]{1,0:T(8,128)(2,1)S(1)}, u32[]{:S(2)}, u32[]{:S(2)}) collective-permute-start(bf16[128,1024]{1,0:T(8,128)(2,1)S(1)} %collective-permute-done.2.refs_2_), channel_id=1, source_target_pairs={{0,1},{1,0},{2,3},{3,2},{4,5},{5,4},{6,7},{7,6},{8,9},{9,8},{10,11... | collective-permute-start | bytes 786440 | tf_op jit(solution)/shard_map/ppermute | solution.py:134
  65.9 9.2 %collective-permute-start.8 = (bf16[128,1024]{1,0:T(8,128)(2,1)S(1)}, bf16[128,1024]{1,0:T(8,128)(2,1)S(1)}, u32[]{:S(2)}, u32[]{:S(2)}) collective-permute-start(bf16[128,1024]{1,0:T(8,128)(2,1)S(1)} %collective-permute-done.7.refs_6_), channel_id=1, source_target_pairs={{0,1},{1,0},{2,3},{3,2},{4,5},{5,4},{6,7},{7,6},{8,9},{9,8},{10,11... | collective-permute-start | bytes 786440 | tf_op jit(solution)/shard_map/ppermute | solution.py:134
  66.4 12.5 %collective-permute-start.6 = (bf16[128,1024]{1,0:T(8,128)(2,1)S(1)}, bf16[128,1024]{1,0:T(8,128)(2,1)S(1)}, u32[]{:S(2)}, u32[]{:S(2)}) collective-permute-start(bf16[128,1024]{1,0:T(8,128)(2,1)S(1)} %collective-permute-done.5.refs_4_), channel_id=1, source_target_pairs={{0,1},{1,0},{2,3},{3,2},{4,5},{5,4},{6,7},{7,6},{8,9},{9,8},{10,11... | collective-permute-start | bytes 786440 | tf_op jit(solution)/shard_map/ppermute | solution.py:134
  84.7 42.9 %copy-start.1 = (bf16[2,256,256]{2,1,0:T(8,128)(2,1)S(1)}, bf16[2,256,256]{2,1,0:T(8,128)(2,1)}, u32[]{:S(2)}) copy-start(bf16[2,256,256]{2,1,0:T(8,128)(2,1)} %constant.233.clone.refs_5_) | copy-start | bytes 786436
  84.7 42.9 %copy-start.2 = (bf16[2,128,256]{2,1,0:T(8,128)(2,1)S(1)}, bf16[2,128,256]{2,1,0:T(8,128)(2,1)}, u32[]{:S(2)}) copy-start(bf16[2,128,256]{2,1,0:T(8,128)(2,1)} %constant.232.clone.refs_4_) | copy-start | bytes 393220
  130.2 19.3 %all-to-all-start.2 = ((bf16[32,32,256]{2,1,0:T(8,128)(2,1)}), bf16[32,32,256]{2,1,0:T(8,128)(2,1)S(1)}, u32[]{:S(2)}, u32[]{:S(2)}) async-start(bf16[32,32,256]{2,1,0:T(8,128)(2,1)} %bitcast.23), calls=%async_computation.2 | async-start | bytes 1048576 | tf_op jit(solution)/shard_map/all_to_all | solution.py:488
  153.1 12.1 %collective-permute-start.9 = (bf16[64,2048]{1,0:T(8,128)(2,1)S(1)}, bf16[64,2048]{1,0:T(8,128)(2,1)S(1)}, u32[]{:S(2)}, u32[]{:S(2)}) collective-permute-start(bf16[64,2048]{1,0:T(8,128)(2,1)S(1)} %get-tuple-element.47), channel_id=1, source_target_pairs={{0,0},{1,16},{2,2},{3,18},{4,4},{5,20},{6,6},{7,22},{8,24},{9,8},{... | collective-permute-start | bytes 786440 | tf_op jit(solution)/shard_map/ppermute | solution.py:88
  155.7 25.9 %collective-permute-start.10 = (bf16[64,2048]{1,0:T(8,128)(2,1)S(1)}, bf16[64,2048]{1,0:T(8,128)(2,1)S(1)}, u32[]{:S(2)}, u32[]{:S(2)}) collective-permute-start(bf16[64,2048]{1,0:T(8,128)(2,1)S(1)} %get-tuple-element.48), channel_id=1, source_target_pairs={{0,8},{1,24},{2,10},{3,26},{4,12},{5,28},{6,14},{7,30},{8,16},{9,0... | collective-permute-start | bytes 786440 | tf_op jit(solution)/shard_map/ppermute | solution.py:88
  155.8 25.8 %collective-permute-start.11 = (bf16[64,2048]{1,0:T(8,128)(2,1)S(1)}, bf16[64,2048]{1,0:T(8,128)(2,1)S(1)}, u32[]{:S(2)}, u32[]{:S(2)}) collective-permute-start(bf16[64,2048]{1,0:T(8,128)(2,1)S(1)} %get-tuple-element.49), channel_id=1, source_target_pairs={{0,16},{1,0},{2,18},{3,2},{4,20},{5,4},{6,22},{7,6},{8,8},{9,24},{... | collective-permute-start | bytes 786440 | tf_op jit(solution)/shard_map/ppermute | solution.py:88
  159.6 22.0 %collective-permute-start.12 = (bf16[64,2048]{1,0:T(8,128)(2,1)S(1)}, bf16[64,2048]{1,0:T(8,128)(2,1)S(1)}, u32[]{:S(2)}, u32[]{:S(2)}) collective-permute-start(bf16[64,2048]{1,0:T(8,128)(2,1)S(1)} %get-tuple-element.50), channel_id=1, source_target_pairs={{0,24},{1,8},{2,26},{3,10},{4,28},{5,12},{6,30},{7,14},{8,0},{9,16... | collective-permute-start | bytes 786440 | tf_op jit(solution)/shard_map/ppermute | solution.py:88
Sparse Core Ops, SparseCore 0:
  8.9 48.4 all-gather.6
  59.0 16.7 all-gather.8
  79.1 50.9 all-gather.10

commit v22 on v21

--- a/solution.py
+++ b/solution.py
@@ -135,63 +135,89 @@
     return pieces
 
 
-def project_kernel(tp_parts, place_ref, *refs):
-    *share_refs, weight_ref, out_ref, held, sems = refs
+def gather_inner(block, inner_parts):
+    held, masks = [block], [0]
+    bit = inner_parts // 2
+    while bit:
+        pairs = [(i, i ^ bit) for i in range(lax.axis_size("seq"))]
+        held += [lax.ppermute(piece, "seq", pairs) for piece in held]
+        masks += [mask ^ bit for mask in masks]
+        bit //= 2
+    return held, masks
+
+
+def project_kernel(tp_parts, masks, place_ref, *refs):
+    *refs, weight_ref, out_ref, held, weight_sems, shard_sems = refs
+    share_refs, shard_refs = refs[: -len(masks)], refs[-len(masks) :]
     seq_parts, streams, chans, count = out_ref.shape
-    near_parts, far_parts = weight_ref.shape[:2]
-    blocks = near_parts * far_parts // tp_parts
-    copies = []
-    for stream in range(streams):
+    gathered = weight_ref.shape[0]
+    depth = shard_refs[0].shape[1]
+    blocks = len(masks) // tp_parts
+    copies = {stream: [] for stream in range(streams)}
+    for stream in range(gathered):
         for step in range(tp_parts):
             which = lax.rem(place_ref[0] - step + tp_parts, tp_parts)
-            for block in range(blocks):
-                inner = which * blocks + block
-                source = weight_ref.at[lax.rem(inner, near_parts), inner // near_parts, stream]
-                slot = len(copies)
-                copies.append(
-                    pltpu.make_async_copy(source, held.at[stream, step, block], sems.at[slot])
+            copies[stream].append(
+                pltpu.make_async_copy(
+                    weight_ref.at[stream, which], held.at[stream, step], weight_sems.at[stream, step]
                 )
-                copies[-1].start()
+            )
+    for slot, mask in enumerate(masks):
+        inner = jnp.bitwise_xor(place_ref[1], mask)
+        step = lax.rem(place_ref[0] - inner // blocks + tp_parts, tp_parts)
+        row = pl.multiple_of(lax.rem(inner, blocks) * depth, depth)
+        for stream in range(gathered, streams):
+            copies[stream].append(
+                pltpu.make_async_copy(
+                    shard_refs[slot].at[stream - gathered],
+                    held.at[stream, step, pl.ds(row, depth)],
+                    shard_sems.at[stream - gathered, slot],
+                )
+            )
+    order = [*range(gathered, streams), *range(gathered)]
+    for stream in order:
+        for copy in copies[stream]:
+            copy.start()
     left = [
         jnp.concatenate([share_ref[...] for share_ref in share_refs[step::tp_parts]])
         for step in range(tp_parts)
     ]
-    for stream in range(streams):
+    for stream in order:
+        for copy in copies[stream]:
+            copy.wait()
         sums = jnp.zeros((count, seq_parts * chans), jnp.float32)
         for step in range(tp_parts):
-            first = (stream * tp_parts + step) * blocks
-            for copy in copies[first : first + blocks]:
-                copy.wait()
             sums = sums + jnp.dot(
-                left[step],
-                held[stream, step].reshape(left[step].shape[1], -1),
-                preferred_element_type=jnp.float32,
+                left[step], held[stream, step], preferred_element_type=jnp.float32
             )
         turned = sums.astype(out_ref.dtype).T
         for seq in range(seq_parts):
             out_ref[seq, stream] = turned[seq * chans : (seq + 1) * chans]
 
 
-def project_in(chunks, weight, seq_parts):
+def project_in(chunks, weight, shards, masks, inner_parts, seq_parts):
     tp_parts = len(chunks[0])
     rows, width = chunks[0][0].shape
-    near_parts, far_parts, streams, depth, chan_tp = weight.shape
-    blocks = near_parts * far_parts // tp_parts
+    gathered, _, chan_tp = weight.shape
+    weight = weight.reshape(gathered, tp_parts, width, chan_tp)
+    sent = shards[0].shape[0]
+    streams = gathered + sent
     chans = chan_tp // seq_parts
     pieces = [piece for chunk in chunks for piece in chunk]
     count = len(chunks) * rows
-    place = lax.axis_index("tp").astype(jnp.int32)[None]
+    place = jnp.stack([lax.axis_index("tp"), lax.axis_index("seq") % inner_parts]).astype(jnp.int32)
     vmem = pl.BlockSpec(memory_space=pltpu.VMEM)
     return pl.pallas_call(
-        functools.partial(project_kernel, tp_parts),
+        functools.partial(project_kernel, tp_parts, masks),
         in_specs=[pl.BlockSpec(memory_space=pltpu.SMEM)]
-        + [vmem] * len(pieces)
+        + [vmem] * (len(pieces) + len(shards))
         + [pl.BlockSpec(memory_space=pl.ANY)],
         out_specs=vmem,
         out_shape=jax.ShapeDtypeStruct((seq_parts, streams, chans, count), jnp.bfloat16),
         scratch_shapes=[
-            pltpu.VMEM((streams, tp_parts, blocks, depth, chan_tp), weight.dtype),
-            pltpu.SemaphoreType.DMA((streams * tp_parts * blocks,)),
+            pltpu.VMEM((streams, tp_parts, width, chan_tp), weight.dtype),
+            pltpu.SemaphoreType.DMA((gathered, tp_parts)),
+            pltpu.SemaphoreType.DMA((sent, len(shards))),
         ],
         compiler_params=pltpu.CompilerParams(vmem_limit_bytes=48 * 2**20),
         cost_estimate=pl.CostEstimate(
@@ -200,7 +226,7 @@
             + 2 * streams * count * seq_parts * chans,
             transcendentals=0,
         ),
-    )(place, *pieces, weight)
+    )(place, *pieces, *shards, weight)
 
 
 def tables(block):
@@ -449,12 +475,10 @@
         [index * tp_parts + tp for index in group for tp in range(tp_parts)] for group in inner_groups
     ]
 
-    near = 2 if inner_parts % 2 == 0 else 1
-    far_groups = [group[index::near] for group in inner_groups for index in range(near)]
-    near_groups = [
-        group[index : index + near] for group in inner_groups for index in range(0, inner_parts, near)
-    ]
-    weight = lax.all_gather(in_proj, "seq", axis_index_groups=far_groups)
+    weight = lax.all_gather(
+        in_proj[: streams - 1], "seq", axis=1, tiled=True, axis_index_groups=inner_groups
+    )
+    shards, masks = gather_inner(in_proj[streams - 1 :], inner_parts)
 
     taps = lax.dynamic_slice_in_dim(short_taps, position * chans, chans, axis=2)
     taps = jnp.broadcast_to(taps[..., None], taps.shape + (rows,))
@@ -465,23 +489,20 @@
     )
 
     held = share_columns(features, outer, inner_parts, tp_parts)
-    arrived = cross_outer(held, (0, 1), outer, inner_parts, tp_parts)
-    held[0], taps, skip, filter_blocks = lax.optimization_barrier((held[0], taps, skip, filter_blocks))
-    if outer > 2:
-        arrived |= cross_outer(held, (outer - 1,), outer, inner_parts, tp_parts)
+    arrived = cross_outer(held, sorted({0, 1, outer - 1}), outer, inner_parts, tp_parts)
     own = share_over_tp(arrived[0], tp_parts)
-    held, arrived[1], own = lax.optimization_barrier((held, arrived[1], own))
+    first = [arrived[step] for step in sorted({1, outer - 1})]
+    held, first, own, taps, skip, filter_blocks = lax.optimization_barrier(
+        (held, first, own, taps, skip, filter_blocks)
+    )
+    arrived |= dict(zip(sorted({1, outer - 1}), first))
     arrived |= cross_outer(held, range(2, outer - 1), outer, inner_parts, tp_parts)
     chunks = [own] + [share_over_tp(arrived[step], tp_parts) for step in range(1, outer)]
-    last = chunks[outer // 2]
-    last[0], weight = lax.optimization_barrier((last[0], weight))
-    weight = lax.all_gather(weight, "seq", axis_index_groups=near_groups)
-
     chunks, out_proj = lax.optimization_barrier((chunks, out_proj))
     out_weight = lax.all_gather(out_proj, ("seq", "tp"), axis_index_groups=tp_groups)
     out_weight = out_weight.reshape((inner_parts, tp_parts) + out_proj.shape)
 
-    partial = project_in(chunks, weight, seq_parts)
+    partial = project_in(chunks, weight, shards, masks, inner_parts, seq_parts)
     parts = lax.all_to_all(partial, "seq", split_axis=0, concat_axis=0, tiled=True)
 
     gated = convolve([parts], filter_blocks, taps, skip, outer, tp_parts)

time: 190 us -> 178 us (0.937)
  waiting for transfers between devices: 86.3 us -> 71 us
  local copies, waits for them, and re-layouts: 3.25 us -> 6.97 us
    all_gather x2 -> x1, waiting for transfers between devices: 13.2 us -> 0.02 us  [per_device(): lax.all_gather(in_proj[:streams - 1], 'seq', axis=1, tiled=True, axis_ind...]
    ppermute x3, waiting for transfers between devices: 22.8 us -> 12.2 us  [cross_outer(): lax.ppermute(piece, 'seq', [(i, (i + far) % seq_parts) for i in range(seq...]
    ppermute x0 -> x3, waiting for transfers between devices: none -> 7.39 us  [gather_inner(): held += [lax.ppermute(piece, 'seq', pairs) for piece in held]]
    ppermute x4, waiting for transfers between devices: 11 us -> 16.7 us  [share_over_tp(): pieces.append(lax.ppermute(part, 'tp', pairs))]
    slice x0 -> x2, local copies, waits for them, and re-layouts: none -> 3.48 us  [the longest x1 2.35 us: per_device(): in_proj[:streams - 1]]
    ppermute x2, waiting for transfers between devices: 2.72 us -> 0.01 us  [share_columns(): piece = lax.ppermute(piece, 'tp', pairs)]
  transfers between devices with their start and end apart: 18 -> 20, of which waited for: 11 -> 11; matrix products, arithmetic and copies ran while one was open for 2% -> 3% of each run, Pallas kernels for 4% -> 5%
where the time goes in v22:
time: 178 us; the launch traced here: 177 us
  waiting for transfers between devices  71 us (40%)
  blocking collectives  41.2 us (23%)
  starting transfers between devices  29.8 us (17%)
  between operations  13.7 us (8%)
  Pallas kernels  13.4 us (8%)
  local copies, waits for them, and re-layouts  6.97 us (4%)
    all_to_all x1, blocking collectives, per_device(): lax.all_to_all(partial, 'seq', split_axis=0, concat_axis=0, tiled=True)  41.2 us
    ppermute x4, waiting for transfers between devices, return_output(): arrived.append(lax.ppermute(piece, ('seq', 'tp'), pairs))  19.6 us
    ppermute x4, waiting for transfers between devices, share_over_tp(): pieces.append(lax.ppermute(part, 'tp', pairs))  16.7 us
    all_to_all x1, waiting for transfers between devices, per_device(): lax.all_to_all(gated.reshape((-1,) + gated.shape[3:]), ('tp', 'seq'), spl...  14.4 us
    ppermute x3, waiting for transfers between devices, cross_outer(): lax.ppermute(piece, 'seq', [(i, (i + far) % seq_parts) for i in range(seq...  12.2 us
    ppermute x4, starting transfers between devices, return_output(): arrived.append(lax.ppermute(piece, ('seq', 'tp'), pairs))  8.85 us
    ppermute x3, waiting for transfers between devices, gather_inner(): held += [lax.ppermute(piece, 'seq', pairs) for piece in held]  7.39 us
    all_to_all x1, starting transfers between devices, per_device(): lax.all_to_all(long_filter.T.reshape(seq_parts, chans, rows), 'seq', spli...  6.27 us
  transfers between devices with their start and end apart: 20, of which 11 were waited for; matrix products, arithmetic and copies ran while one was open for 3% of the time, Pallas kernels for 5%

profile of v22, /device:TPU:12, one launch (start us, length us, event | category | flops | bytes accessed | tf_op | source)
XLA Modules:
  0.0 177.5 jit_solution(5642282121920810387)
XLA Ops:
  6.5 2.4 %slice.7 = bf16[2,512,512]{2,1,0:T(8,128)(2,1)} slice(bf16[3,512,512]{2,1,0:T(8,128)(2,1)} %param.9), slice={[0:2], [0:512], [0:512]} | slice | bytes 2097152 | tf_op jit(solution)/shard_map/slice | solution.py:479
  9.7 1.5 collective-permute-start.1
  12.0 6.3 %all-to-all-start = ((f32[16,32,128]{2,1,0:T(8,128)}), f32[16,32,128]{2,1,0:T(8,128)S(1)}, u32[]{:S(2)}, u32[]{:S(2)}) async-start(f32[16,32,128]{2,1,0:T(8,128)} %bitcast.20), calls=%async_computation | async-start | bytes 524288 | tf_op jit(solution)/shard_map/all_to_all | solution.py:487
  19.5 1.5 collective-permute-start.9
  22.0 1.5 collective-permute-start.2
  26.5 9.6 %collective-permute-done.2.refs_2_ = bf16[128,1024]{1,0:T(8,128)(2,1)S(1)} collective-permute-done((bf16[128,1024]{1,0:T(8,128)(2,1)}, bf16[128,1024]{1,0:T(8,128)(2,1)S(1)}, u32[]{:S(2)}, u32[]{:S(2)}) %collective-permute-start.2) | collective-permute-done | bytes 262176 | tf_op jit(solution)/shard_map/ppermute | solution.py:125
  36.0 1.8 %collective-permute-done.3.refs_6_ = bf16[128,1024]{1,0:T(8,128)(2,1)S(1)} collective-permute-done((bf16[128,1024]{1,0:T(8,128)(2,1)}, bf16[128,1024]{1,0:T(8,128)(2,1)S(1)}, u32[]{:S(2)}, u32[]{:S(2)}) %collective-permute-start.3) | collective-permute-done | bytes 262176 | tf_op jit(solution)/shard_map/ppermute | solution.py:125
  39.7 7.4 %collective-permute-done.9.refs_9_ = bf16[1,512,512]{2,1,0:T(8,128)(2,1)S(1)} collective-permute-done((bf16[1,512,512]{2,1,0:T(8,128)(2,1)S(1)}, bf16[1,512,512]{2,1,0:T(8,128)(2,1)S(1)}, u32[]{:S(2)}, u32[]{:S(2)}) %collective-permute-start.9) | collective-permute-done | bytes 524320 | tf_op jit(solution)/shard_map/ppermute | solution.py:143
  47.6 1.5 collective-permute-start.8
  50.5 5.8 %collective-permute-done.5.refs_3_ = bf16[128,1024]{1,0:T(8,128)(2,1)} collective-permute-done((bf16[128,1024]{1,0:T(8,128)(2,1)S(1)}, bf16[128,1024]{1,0:T(8,128)(2,1)}, u32[]{:S(2)}, u32[]{:S(2)}) %collective-permute-start.5) | collective-permute-done | bytes 262176 | tf_op jit(solution)/shard_map/ppermute | solution.py:134
  56.3 5.6 %collective-permute-done.8.refs_7_ = bf16[128,1024]{1,0:T(8,128)(2,1)} collective-permute-done((bf16[128,1024]{1,0:T(8,128)(2,1)S(1)}, bf16[128,1024]{1,0:T(8,128)(2,1)}, u32[]{:S(2)}, u32[]{:S(2)}) %collective-permute-start.8) | collective-permute-done | bytes 262176 | tf_op jit(solution)/shard_map/ppermute | solution.py:134
  61.9 5.2 %collective-permute-done.7.refs_5_ = bf16[128,1024]{1,0:T(8,128)(2,1)} collective-permute-done((bf16[128,1024]{1,0:T(8,128)(2,1)}, bf16[128,1024]{1,0:T(8,128)(2,1)}, u32[]{:S(2)}, u32[]{:S(2)}) %collective-permute-start.7) | collective-permute-done | bytes 262176 | tf_op jit(solution)/shard_map/ppermute | solution.py:134
  68.2 5.6 %shard_map.82 = bf16[16,3,32,512]{3,2,1,0:T(8,128)(2,1)S(1)} custom-call(s32[2]{0:T(128)S(1)} %pad_add_fusion.1.place_ref, bf16[128,1024]{1,0:T(8,128)(2,1)S(1)} %fusion.1.refs_0_, bf16[128,1024]{1,0:T(8,128)(2,1)S(1)} %copy-done.2, bf16[128,1024]{1,0:T(8,128)(2,1)S(1)} %collective-permute-done.2.refs_2_, bf16[128,1024]{1,0:T(8,128)(2,1)} %collective-permute-done.5.refs_3_, ...), custom_call_target="tpu_custom_call" | custom-call | flops 64424509440 | bytes 7864320 | tf_op jit(solution)/shard_map/pallas_call | solution.py:210
  73.8 41.2 %all_to_all.15.refs_0_ = bf16[16,3,32,512]{3,2,1,0:T(8,128)(2,1)S(1)} all-to-all(bf16[16,3,32,512]{3,2,1,0:T(8,128)(2,1)S(1)} %shard_map.82), channel_id=1, replica_groups=mesh['seq'=16,'tp'=2] {'seq'}, dimensions={0} | all-to-all | bytes 3145728 | tf_op jit(solution)/shard_map/all_to_all | solution.py:506
  115.1 2.6 %shard_map.83 = bf16[2,4,4,32,256]{4,3,2,1,0:T(8,128)(2,1)} custom-call(bf16[16,3,32,512]{3,2,1,0:T(8,128)(2,1)S(1)} %all_to_all.15.refs_0_, f32[16,32,128]{2,1,0:T(8,128)S(1)} %all-to-all-done.refs_1_, f32[3,3,32,128]{3,2,1,0:T(8,128)S(1)} %broadcast_in_dim.4.refs_2_, f32[32,128]{1,0:T(8,128)S(1)} %broadcast_in_dim.5.refs_3_, ...), custom_call_target="tpu_custom_call" | custom-call | flops 1000000000 | bytes 4194304 | tf_op jit(solution)/shard_map/pallas_call | solution.py:386
  117.7 4.7 %all-to-all-start.2 = ((bf16[32,32,256]{2,1,0:T(8,128)(2,1)}), bf16[32,32,256]{2,1,0:T(8,128)(2,1)S(1)}, u32[]{:S(2)}, u32[]{:S(2)}) async-start(bf16[32,32,256]{2,1,0:T(8,128)(2,1)} %bitcast.23), calls=%async_computation.2 | async-start | bytes 1048576 | tf_op jit(solution)/shard_map/all_to_all | solution.py:509
  122.6 14.4 %all-to-all-done.2 = bf16[32,32,256]{2,1,0:T(8,128)(2,1)S(1)} async-done(((bf16[32,32,256]{2,1,0:T(8,128)(2,1)}), bf16[32,32,256]{2,1,0:T(8,128)(2,1)S(1)}, u32[]{:S(2)}, u32[]{:S(2)}) %all-to-all-start.2) | async-done | bytes 524320 | tf_op jit(solution)/shard_map/all_to_all | solution.py:509
  137.0 3.6 %shard_map.84 = (bf16[64,2048]{1,0:T(8,128)(2,1)S(1)}, bf16[64,2048]{1,0:T(8,128)(2,1)S(1)}, bf16[64,2048]{1,0:T(8,128)(2,1)S(1)}, bf16[64,2048]{1,0:T(8,128)(2,1)S(1)}) custom-call(s32[4]{0:T(128)S(1)} %pad_add_fusion.block_ref, bf16[2,512,256]{2,1,0:T(8,128)(2,1)S(1)} %bitcast.32, bf16[4,2,512,512]{3,2,1,0:T(8,128)(2,1)} %bitcast.33), custom_call_target="tpu_custom_call" | custom-call | flops 1073741824 | bytes 5767168 | tf_op jit(solution)/shard_map/pallas_call | solution.py:440
  140.5 2.6 %collective-permute-start.12 = (bf16[64,2048]{1,0:T(8,128)(2,1)S(1)}, bf16[64,2048]{1,0:T(8,128)(2,1)S(1)}, u32[]{:S(2)}, u32[]{:S(2)}) collective-permute-start(bf16[64,2048]{1,0:T(8,128)(2,1)S(1)} %get-tuple-element.43), channel_id=1, source_target_pairs={{0,0},{1,16},{2,2},{3,18},{4,4},{5,20},{6,6},{7,22},{8,24},{9,8},{... | collective-permute-start | bytes 786440 | tf_op jit(solution)/shard_map/ppermute | solution.py:88
  143.2 3.9 %collective-permute-start.14 = (bf16[64,2048]{1,0:T(8,128)(2,1)S(1)}, bf16[64,2048]{1,0:T(8,128)(2,1)S(1)}, u32[]{:S(2)}, u32[]{:S(2)}) collective-permute-start(bf16[64,2048]{1,0:T(8,128)(2,1)S(1)} %get-tuple-element.45), channel_id=1, source_target_pairs={{0,16},{1,0},{2,18},{3,2},{4,20},{5,4},{6,22},{7,6},{8,8},{9,24},{... | collective-permute-start | bytes 786440 | tf_op jit(solution)/shard_map/ppermute | solution.py:88
  147.1 2.3 %collective-permute-start.15 = (bf16[64,2048]{1,0:T(8,128)(2,1)S(1)}, bf16[64,2048]{1,0:T(8,128)(2,1)S(1)}, u32[]{:S(2)}, u32[]{:S(2)}) collective-permute-start(bf16[64,2048]{1,0:T(8,128)(2,1)S(1)} %get-tuple-element.46), channel_id=1, source_target_pairs={{0,24},{1,8},{2,26},{3,10},{4,28},{5,12},{6,30},{7,14},{8,0},{9,16... | collective-permute-start | bytes 786440 | tf_op jit(solution)/shard_map/ppermute | solution.py:88
  149.5 3.2 %collective-permute-done.12.refs_0_ = bf16[64,2048]{1,0:T(8,128)(2,1)S(1)} collective-permute-done((bf16[64,2048]{1,0:T(8,128)(2,1)S(1)}, bf16[64,2048]{1,0:T(8,128)(2,1)S(1)}, u32[]{:S(2)}, u32[]{:S(2)}) %collective-permute-start.12) | collective-permute-done | bytes 262176 | tf_op jit(solution)/shard_map/ppermute | solution.py:88
  152.7 16.4 %collective-permute-done.13.refs_1_ = bf16[64,2048]{1,0:T(8,128)(2,1)S(1)} collective-permute-done((bf16[64,2048]{1,0:T(8,128)(2,1)S(1)}, bf16[64,2048]{1,0:T(8,128)(2,1)S(1)}, u32[]{:S(2)}, u32[]{:S(2)}) %collective-permute-start.13) | collective-permute-done | bytes 262176 | tf_op jit(solution)/shard_map/ppermute | solution.py:88
  169.1 1.5 shard_map.85
  (52 shorter events, 11.6 us)
Async XLA Ops:
  6.5 19.0 %copy-start = (f32[3,3,512]{2,1,0:T(4,128)S(1)}, f32[3,3,512]{2,1,0:T(4,128)}, u32[]{:S(2)}) copy-start(f32[3,3,512]{2,1,0:T(4,128)} %param.10) | copy-start | bytes 55300
  6.5 60.7 %all-gather.4.cloned.1.call-start = ((), (), s32[]{:S(2)}) async-start(), calls=%async_computation.3 | async-start | bytes 5242880 | tf_op jit(solution)/shard_map/all_gather | solution.py:478
  6.5 2.5 %copy-start.5 = (bf16[128,4096]{1,0:T(8,128)(2,1)S(1)}, bf16[128,4096]{1,0:T(8,128)(2,1)}, u32[]{:S(2)}) copy-start(bf16[128,4096]{1,0:T(8,128)(2,1)} %param.8) | copy-start | bytes 3145732
  9.1 11.9 %collective-permute-start = (bf16[128,1024]{1,0:T(8,128)(2,1)S(1)}, bf16[128,1024]{1,0:T(8,128)(2,1)S(1)}, u32[]{:S(2)}, u32[]{:S(2)}) collective-permute-start(bf16[128,1024]{1,0:T(8,128)(2,1)S(1)} %get-tuple-element.47), channel_id=1, source_target_pairs={{0,1},{1,0},{2,3},{3,2},{4,5},{5,4},{6,7},{7,6},{8,9},{9,8},{10,11... | collective-permute-start | bytes 786440 | tf_op jit(solution)/shard_map/ppermute | solution.py:107
  9.7 14.4 %collective-permute-start.1 = (bf16[128,1024]{1,0:T(8,128)(2,1)S(1)}, bf16[128,1024]{1,0:T(8,128)(2,1)S(1)}, u32[]{:S(2)}, u32[]{:S(2)}) collective-permute-start(bf16[128,1024]{1,0:T(8,128)(2,1)S(1)} %get-tuple-element.49), channel_id=1, source_target_pairs={{0,1},{1,0},{2,3},{3,2},{4,5},{5,4},{6,7},{7,6},{8,9},{9,8},{10,11... | collective-permute-start | bytes 786440 | tf_op jit(solution)/shard_map/ppermute | solution.py:107
  12.0 14.4 %all-to-all-start = ((f32[16,32,128]{2,1,0:T(8,128)}), f32[16,32,128]{2,1,0:T(8,128)S(1)}, u32[]{:S(2)}, u32[]{:S(2)}) async-start(f32[16,32,128]{2,1,0:T(8,128)} %bitcast.20), calls=%async_computation | async-start | bytes 524288 | tf_op jit(solution)/shard_map/all_to_all | solution.py:487
  18.3 104.3 %all-gather.6.cloned.1.call-start = ((), (), s32[]{:S(2)}) async-start(), calls=%async_computation.4 | async-start | bytes 4718592 | tf_op jit(solution)/shard_map/all_gather | solution.py:502
  19.5 27.6 %collective-permute-start.9 = (bf16[1,512,512]{2,1,0:T(8,128)(2,1)S(1)}, bf16[1,512,512]{2,1,0:T(8,128)(2,1)S(1)}, u32[]{:S(2)}, u32[]{:S(2)}) collective-permute-start(bf16[1,512,512]{2,1,0:T(8,128)(2,1)S(1)} %slice.6.refs_8_), channel_id=1, source_target_pairs={{0,4},{2,6},{4,0},{6,2},{8,12},{10,14},{12,8},{14,10},{16,20},{18,... | collective-permute-start | bytes 1572872 | tf_op jit(solution)/shard_map/ppermute | solution.py:143
  22.0 14.0 %collective-permute-start.2 = (bf16[128,1024]{1,0:T(8,128)(2,1)}, bf16[128,1024]{1,0:T(8,128)(2,1)S(1)}, u32[]{:S(2)}, u32[]{:S(2)}) collective-permute-start(bf16[128,1024]{1,0:T(8,128)(2,1)} %get-tuple-element.52), channel_id=1, source_target_pairs={{0,8},{2,10},{4,12},{6,14},{8,16},{10,18},{12,20},{14,22},{16,24},... | collective-permute-start | bytes 786440 | tf_op jit(solution)/shard_map/ppermute | solution.py:125
  23.5 14.3 %collective-permute-start.3 = (bf16[128,1024]{1,0:T(8,128)(2,1)}, bf16[128,1024]{1,0:T(8,128)(2,1)S(1)}, u32[]{:S(2)}, u32[]{:S(2)}) collective-permute-start(bf16[128,1024]{1,0:T(8,128)(2,1)} %get-tuple-element.51), channel_id=1, source_target_pairs={{0,24},{2,26},{4,28},{6,30},{8,0},{10,2},{12,4},{14,6},{16,8},{18,... | collective-permute-start | bytes 786440 | tf_op jit(solution)/shard_map/ppermute | solution.py:125
  24.2 13.7 %collective-permute-start.4 = (bf16[128,1024]{1,0:T(8,128)(2,1)S(1)}, bf16[128,1024]{1,0:T(8,128)(2,1)S(1)}, u32[]{:S(2)}, u32[]{:S(2)}) collective-permute-start(bf16[128,1024]{1,0:T(8,128)(2,1)S(1)} %fusion.1.refs_0_), channel_id=1, source_target_pairs={{0,1},{1,0},{2,3},{3,2},{4,5},{5,4},{6,7},{7,6},{8,9},{9,8},{10,11... | collective-permute-start | bytes 786440 | tf_op jit(solution)/shard_map/ppermute | solution.py:134
  38.5 11.4 %collective-permute-start.6 = (bf16[128,1024]{1,0:T(8,128)(2,1)S(1)}, bf16[128,1024]{1,0:T(8,128)(2,1)}, u32[]{:S(2)}, u32[]{:S(2)}) collective-permute-start(bf16[128,1024]{1,0:T(8,128)(2,1)S(1)} %dynamic-slice_bitcast_fusion), channel_id=1, source_target_pairs={{0,16},{2,18},{4,20},{6,22},{8,24},{10,26},{12,28},{14,30},{16,0},... | collective-permute-start | bytes 786440 | tf_op jit(solution)/shard_map/ppermute | solution.py:125
  39.7 27.5 %collective-permute-start.10 = (bf16[1,512,512]{2,1,0:T(8,128)(2,1)S(1)}, bf16[1,512,512]{2,1,0:T(8,128)(2,1)S(1)}, u32[]{:S(2)}, u32[]{:S(2)}) collective-permute-start(bf16[1,512,512]{2,1,0:T(8,128)(2,1)S(1)} %slice.6.refs_8_), channel_id=1, source_target_pairs={{0,2},{2,0},{4,6},{6,4},{8,10},{10,8},{12,14},{14,12},{16,18},{18,... | collective-permute-start | bytes 1572872 | tf_op jit(solution)/shard_map/ppermute | solution.py:143
  47.1 20.1 %collective-permute-start.11 = (bf16[1,512,512]{2,1,0:T(8,128)(2,1)S(1)}, bf16[1,512,512]{2,1,0:T(8,128)(2,1)S(1)}, u32[]{:S(2)}, u32[]{:S(2)}) collective-permute-start(bf16[1,512,512]{2,1,0:T(8,128)(2,1)S(1)} %collective-permute-done.9.refs_9_), channel_id=1, source_target_pairs={{0,2},{2,0},{4,6},{6,4},{8,10},{10,8},{12,14},{14,12},{16,18},{18,... | collective-permute-start | bytes 1572872 | tf_op jit(solution)/shard_map/ppermute | solution.py:143
  47.1 9.2 %collective-permute-start.5 = (bf16[128,1024]{1,0:T(8,128)(2,1)S(1)}, bf16[128,1024]{1,0:T(8,128)(2,1)}, u32[]{:S(2)}, u32[]{:S(2)}) collective-permute-start(bf16[128,1024]{1,0:T(8,128)(2,1)S(1)} %collective-permute-done.2.refs_2_), channel_id=1, source_target_pairs={{0,1},{1,0},{2,3},{3,2},{4,5},{5,4},{6,7},{7,6},{8,9},{9,8},{10,11... | collective-permute-start | bytes 786440 | tf_op jit(solution)/shard_map/ppermute | solution.py:134
  47.6 14.3 %collective-permute-start.8 = (bf16[128,1024]{1,0:T(8,128)(2,1)S(1)}, bf16[128,1024]{1,0:T(8,128)(2,1)}, u32[]{:S(2)}, u32[]{:S(2)}) collective-permute-start(bf16[128,1024]{1,0:T(8,128)(2,1)S(1)} %collective-permute-done.3.refs_6_), channel_id=1, source_target_pairs={{0,1},{1,0},{2,3},{3,2},{4,5},{5,4},{6,7},{7,6},{8,9},{9,8},{10,11... | collective-permute-start | bytes 786440 | tf_op jit(solution)/shard_map/ppermute | solution.py:134
  49.9 17.2 %collective-permute-start.7 = (bf16[128,1024]{1,0:T(8,128)(2,1)}, bf16[128,1024]{1,0:T(8,128)(2,1)}, u32[]{:S(2)}, u32[]{:S(2)}) collective-permute-start(bf16[128,1024]{1,0:T(8,128)(2,1)} %collective-permute-done.6.refs_4_), channel_id=1, source_target_pairs={{0,1},{1,0},{2,3},{3,2},{4,5},{5,4},{6,7},{7,6},{8,9},{9,8},{10,11... | collective-permute-start | bytes 786440 | tf_op jit(solution)/shard_map/ppermute | solution.py:134
  73.8 41.3 %copy-start.3 = (bf16[2,256,256]{2,1,0:T(8,128)(2,1)S(1)}, bf16[2,256,256]{2,1,0:T(8,128)(2,1)}, u32[]{:S(2)}) copy-start(bf16[2,256,256]{2,1,0:T(8,128)(2,1)} %constant.235.clone.refs_5_) | copy-start | bytes 786436
  73.8 41.2 %copy-start.4 = (bf16[2,128,256]{2,1,0:T(8,128)(2,1)S(1)}, bf16[2,128,256]{2,1,0:T(8,128)(2,1)}, u32[]{:S(2)}) copy-start(bf16[2,128,256]{2,1,0:T(8,128)(2,1)} %constant.234.clone.refs_4_) | copy-start | bytes 393220
  117.7 19.3 %all-to-all-start.2 = ((bf16[32,32,256]{2,1,0:T(8,128)(2,1)}), bf16[32,32,256]{2,1,0:T(8,128)(2,1)S(1)}, u32[]{:S(2)}, u32[]{:S(2)}) async-start(bf16[32,32,256]{2,1,0:T(8,128)(2,1)} %bitcast.23), calls=%async_computation.2 | async-start | bytes 1048576 | tf_op jit(solution)/shard_map/all_to_all | solution.py:509
  140.5 12.1 %collective-permute-start.12 = (bf16[64,2048]{1,0:T(8,128)(2,1)S(1)}, bf16[64,2048]{1,0:T(8,128)(2,1)S(1)}, u32[]{:S(2)}, u32[]{:S(2)}) collective-permute-start(bf16[64,2048]{1,0:T(8,128)(2,1)S(1)} %get-tuple-element.43), channel_id=1, source_target_pairs={{0,0},{1,16},{2,2},{3,18},{4,4},{5,20},{6,6},{7,22},{8,24},{9,8},{... | collective-permute-start | bytes 786440 | tf_op jit(solution)/shard_map/ppermute | solution.py:88
  143.2 25.9 %collective-permute-start.13 = (bf16[64,2048]{1,0:T(8,128)(2,1)S(1)}, bf16[64,2048]{1,0:T(8,128)(2,1)S(1)}, u32[]{:S(2)}, u32[]{:S(2)}) collective-permute-start(bf16[64,2048]{1,0:T(8,128)(2,1)S(1)} %get-tuple-element.44), channel_id=1, source_target_pairs={{0,8},{1,24},{2,10},{3,26},{4,12},{5,28},{6,14},{7,30},{8,16},{9,0... | collective-permute-start | bytes 786440 | tf_op jit(solution)/shard_map/ppermute | solution.py:88
  143.2 25.8 %collective-permute-start.14 = (bf16[64,2048]{1,0:T(8,128)(2,1)S(1)}, bf16[64,2048]{1,0:T(8,128)(2,1)S(1)}, u32[]{:S(2)}, u32[]{:S(2)}) collective-permute-start(bf16[64,2048]{1,0:T(8,128)(2,1)S(1)} %get-tuple-element.45), channel_id=1, source_target_pairs={{0,16},{1,0},{2,18},{3,2},{4,20},{5,4},{6,22},{7,6},{8,8},{9,24},{... | collective-permute-start | bytes 786440 | tf_op jit(solution)/shard_map/ppermute | solution.py:88
  147.1 22.0 %collective-permute-start.15 = (bf16[64,2048]{1,0:T(8,128)(2,1)S(1)}, bf16[64,2048]{1,0:T(8,128)(2,1)S(1)}, u32[]{:S(2)}, u32[]{:S(2)}) collective-permute-start(bf16[64,2048]{1,0:T(8,128)(2,1)S(1)} %get-tuple-element.46), channel_id=1, source_target_pairs={{0,24},{1,8},{2,26},{3,10},{4,28},{5,12},{6,30},{7,14},{8,0},{9,16... | collective-permute-start | bytes 786440 | tf_op jit(solution)/shard_map/ppermute | solution.py:88
  (3 other events, 4.0 us)
Sparse Core Ops, SparseCore 0:
  9.0 49.6 all-gather.3
  67.3 47.8 all-gather.5

commit v23 on v20

--- a/solution.py
+++ b/solution.py
@@ -89,24 +89,25 @@
     return assemble(arrived, places, (tp_parts * part_rows, per_tp * width))
 
 
-def share_columns(features, outer, tp_parts):
-    rows, cols = features.shape
+def share_columns(features, outer, inner_parts, tp_parts):
+    _, cols = features.shape
     per_tp = outer // tp_parts
+    width = cols // outer
     tp_place = lax.axis_index("tp")
-    width = cols // outer
+    outer_place = lax.axis_index("seq") // inner_parts
     held = []
-    for step in range(tp_parts):
-        which = (tp_place + step) % tp_parts
-        piece = jnp.stack(
-            [
-                lax.dynamic_slice_in_dim(features, (group * tp_parts + which) * width, width, axis=1)
-                for group in range(per_tp)
-            ]
-        )
-        if step:
-            piece = lax.ppermute(piece, "tp", [(i, (i + step) % tp_parts) for i in range(tp_parts)])
-        held.append(piece)
-    return jnp.concatenate(held)
+    for after in range(per_tp):
+        group = (outer_place + 1 + after) % per_tp
+        pieces = []
+        for step in range(tp_parts):
+            column = (group * tp_parts + (tp_place + step) % tp_parts) * width
+            piece = lax.dynamic_slice_in_dim(features, column, width, axis=1)
+            if step:
+                pairs = [(i, (i + step) % tp_parts) for i in range(tp_parts)]
+                piece = lax.ppermute(piece, "tp", pairs)
+            pieces.append(piece)
+        held.append(jnp.stack(pieces))
+    return held
 
 
 def cross_outer(held, steps, outer, inner_parts, tp_parts):
@@ -117,8 +118,8 @@
     arrived = {}
     for step in steps:
         target = (outer_place + step) % outer
-        which = (tp_place - target // per_tp + tp_parts) % tp_parts * per_tp + target % per_tp
-        piece = lax.dynamic_index_in_dim(held, which, axis=0, keepdims=False)
+        which = (tp_place - target // per_tp + tp_parts) % tp_parts
+        piece = lax.dynamic_index_in_dim(held[(step - 1) % per_tp], which, axis=0, keepdims=False)
         if step:
             far = step * inner_parts
             piece = lax.ppermute(piece, "seq", [(i, (i + far) % seq_parts) for i in range(seq_parts)])
@@ -450,9 +451,9 @@
         long_filter.T.reshape(seq_parts, chans, rows), "seq", split_axis=0, concat_axis=0, tiled=True
     )
 
-    held = share_columns(features, outer, tp_parts)
+    held = share_columns(features, outer, inner_parts, tp_parts)
     arrived = cross_outer(held, (0, 1), outer, inner_parts, tp_parts)
-    held, taps, skip, filter_blocks = lax.optimization_barrier((held, taps, skip, filter_blocks))
+    held[0], taps, skip, filter_blocks = lax.optimization_barrier((held[0], taps, skip, filter_blocks))
     if outer > 2:
         arrived |= cross_outer(held, (outer - 1,), outer, inner_parts, tp_parts)
     own = share_over_tp(arrived[0], tp_parts)

time: 167 us -> 168 us (level)
  waiting for transfers between devices: 63.1 us -> 67.5 us
  starting transfers between devices: 32.7 us -> 28.9 us
    ppermute x3, waiting for transfers between devices: 10.5 us -> 16.2 us  [cross_outer(): lax.ppermute(piece, 'seq', [(i, (i + far) % seq_parts) for i in range(seq...]
    ppermute x3, starting transfers between devices: 9.2 us -> 4.11 us  [cross_outer(): lax.ppermute(piece, 'seq', [(i, (i + far) % seq_parts) for i in range(seq...]
    ppermute x1 -> x2, waiting for transfers between devices: 5.62 us -> 1.81 us  [share_columns(): piece = lax.ppermute(piece, 'tp', pairs)]
    all_to_all x1, waiting for transfers between devices: 0.01 us -> 2.83 us  [per_device(): lax.all_to_all(long_filter.T.reshape(seq_parts, chans, rows), 'seq', spli...]
  transfers between devices with their start and end apart: 16 -> 17, of which waited for: 11 -> 10; matrix products, arithmetic and copies ran while one was open for 1% -> 1% of each run, Pallas kernels for 5% -> 5%
where the time goes in v23:
time: 168 us
  waiting for transfers between devices  67.5 us (40%)
  blocking collectives  41.2 us (25%)
  starting transfers between devices  28.9 us (17%)
  between operations  13.9 us (8%)
  Pallas kernels  13.4 us (8%)
  local copies, waits for them, and re-layouts  2.5 us (1%)
    all_to_all x1, blocking collectives, per_device(): lax.all_to_all(partial, 'seq', split_axis=0, concat_axis=0, tiled=True)  41.2 us
    ppermute x4, waiting for transfers between devices, return_output(): arrived.append(lax.ppermute(piece, ('seq', 'tp'), pairs))  19.5 us
    ppermute x3, waiting for transfers between devices, cross_outer(): lax.ppermute(piece, 'seq', [(i, (i + far) % seq_parts) for i in range(seq...  16.2 us
    all_to_all x1, waiting for transfers between devices, per_device(): lax.all_to_all(gated.reshape((-1,) + gated.shape[3:]), ('tp', 'seq'), spl...  14.4 us
    ppermute x4, starting transfers between devices, return_output(): arrived.append(lax.ppermute(piece, ('seq', 'tp'), pairs))  8.85 us
    ppermute x4, waiting for transfers between devices, share_over_tp(): pieces.append(lax.ppermute(part, 'tp', pairs))  8.74 us
    all_to_all x1, starting transfers between devices, per_device(): lax.all_to_all(long_filter.T.reshape(seq_parts, chans, rows), 'seq', spli...  6.27 us
    pallas_call x1, Pallas kernels, project_in(): pl.pallas_call(functools.partial(project_kernel, tp_parts), in_specs=[pl....  5.69 us
  transfers between devices with their start and end apart: 17, of which 10 were waited for; matrix products, arithmetic and copies ran while one was open for 1% of the time, Pallas kernels for 5%

profile of v23, /device:TPU:12, one launch (start us, length us, event | category | flops | bytes accessed | tf_op | source)
XLA Modules:
  0.0 167.8 jit_solution(3656585555549880798)
XLA Ops:
  8.4 1.5 collective-permute-start.1
  9.9 0.8 copy.9
  10.8 6.3 %all-to-all-start = ((f32[16,32,128]{2,1,0:T(8,128)}), f32[16,32,128]{2,1,0:T(8,128)S(1)}, u32[]{:S(2)}, u32[]{:S(2)}) async-start(f32[16,32,128]{2,1,0:T(8,128)} %bitcast.14), calls=%async_computation | async-start | bytes 524288 | tf_op jit(solution)/shard_map/all_to_all | solution.py:450
  18.3 1.5 collective-permute-start.2
  19.8 1.8 %collective-permute-done.1 = bf16[128,1024]{1,0:T(8,128)(2,1)S(1)} collective-permute-done((bf16[128,1024]{1,0:T(8,128)(2,1)S(1)}, bf16[128,1024]{1,0:T(8,128)(2,1)S(1)}, u32[]{:S(2)}, u32[]{:S(2)}) %collective-permute-start.1) | collective-permute-done | bytes 262176 | tf_op jit(solution)/shard_map/ppermute | solution.py:107
  22.4 2.8 %all-to-all-done.refs_1_ = f32[16,32,128]{2,1,0:T(8,128)S(1)} async-done(((f32[16,32,128]{2,1,0:T(8,128)}), f32[16,32,128]{2,1,0:T(8,128)S(1)}, u32[]{:S(2)}, u32[]{:S(2)}) %all-to-all-start) | async-done | bytes 262176 | tf_op jit(solution)/shard_map/all_to_all | solution.py:450
  25.4 2.5 %collective-permute-start.7 = (bf16[128,1024]{1,0:T(8,128)(2,1)S(1)}, bf16[128,1024]{1,0:T(8,128)(2,1)S(1)}, u32[]{:S(2)}, u32[]{:S(2)}) collective-permute-start(bf16[128,1024]{1,0:T(8,128)(2,1)S(1)} %dynamic-slice_bitcast_fusion), channel_id=1, source_target_pairs={{0,24},{2,26},{4,28},{6,30},{8,0},{10,2},{12,4},{14,6},{16,8},{18,... | collective-permute-start | bytes 786440 | tf_op jit(solution)/shard_map/ppermute | solution.py:125
  27.9 7.1 %collective-permute-done.2.refs_2_ = bf16[128,1024]{1,0:T(8,128)(2,1)S(1)} collective-permute-done((bf16[128,1024]{1,0:T(8,128)(2,1)S(1)}, bf16[128,1024]{1,0:T(8,128)(2,1)S(1)}, u32[]{:S(2)}, u32[]{:S(2)}) %collective-permute-start.2) | collective-permute-done | bytes 262176 | tf_op jit(solution)/shard_map/ppermute | solution.py:125
  36.1 1.1 collective-permute-start.8
  37.2 8.7 %collective-permute-done.5.refs_4_ = bf16[128,1024]{1,0:T(8,128)(2,1)S(1)} collective-permute-done((bf16[128,1024]{1,0:T(8,128)(2,1)S(1)}, bf16[128,1024]{1,0:T(8,128)(2,1)S(1)}, u32[]{:S(2)}, u32[]{:S(2)}) %collective-permute-start.5) | collective-permute-done | bytes 262176 | tf_op jit(solution)/shard_map/ppermute | solution.py:125
  46.4 8.7 %collective-permute-done.6.refs_5_ = bf16[128,1024]{1,0:T(8,128)(2,1)S(1)} collective-permute-done((bf16[128,1024]{1,0:T(8,128)(2,1)S(1)}, bf16[128,1024]{1,0:T(8,128)(2,1)S(1)}, u32[]{:S(2)}, u32[]{:S(2)}) %collective-permute-start.6) | collective-permute-done | bytes 262176 | tf_op jit(solution)/shard_map/ppermute | solution.py:134
  55.2 3.3 %all-gather.4.cloned.1.call-done = bf16[3,2048,512]{2,1,0:T(8,128)(2,1)} async-done(((bf16[3,512,512]{2,1,0:T(8,128)(2,1)}), bf16[3,2048,512]{2,1,0:T(8,128)(2,1)}) %all-gather.4.cloned.1.call-update) | async-done | bytes 6291472 | tf_op jit(solution)/shard_map/all_gather | solution.py:444
  58.5 5.7 %shard_map.82 = bf16[16,3,32,512]{3,2,1,0:T(8,128)(2,1)S(1)} custom-call(s32[1]{0:T(128)} %bitcast.10.place_ref, bf16[128,1024]{1,0:T(8,128)(2,1)S(1)} %fusion.1.refs_0_, bf16[128,1024]{1,0:T(8,128)(2,1)S(1)} %collective-permute-done.3.refs_1_, bf16[128,1024]{1,0:T(8,128)(2,1)S(1)} %collective-permute-done.2.refs_2_, ...), custom_call_target="tpu_custom_call" | custom-call | flops 96636764160 | bytes 9961472 | tf_op jit(solution)/shard_map/pallas_call | solution.py:177
  64.2 41.2 %all_to_all.15.refs_0_ = bf16[16,3,32,512]{3,2,1,0:T(8,128)(2,1)S(1)} all-to-all(bf16[16,3,32,512]{3,2,1,0:T(8,128)(2,1)S(1)} %shard_map.82), channel_id=1, replica_groups=mesh['seq'=16,'tp'=2] {'seq'}, dimensions={0} | all-to-all | bytes 3145728 | tf_op jit(solution)/shard_map/all_to_all | solution.py:468
  105.4 2.6 %shard_map.83 = bf16[2,4,4,32,256]{4,3,2,1,0:T(8,128)(2,1)} custom-call(bf16[16,3,32,512]{3,2,1,0:T(8,128)(2,1)S(1)} %all_to_all.15.refs_0_, f32[16,32,128]{2,1,0:T(8,128)S(1)} %all-to-all-done.refs_1_, f32[3,3,32,128]{3,2,1,0:T(8,128)S(1)} %broadcast_in_dim.7.refs_2_, f32[32,128]{1,0:T(8,128)S(1)} %broadcast_in_dim.8.refs_3_, ...), custom_call_target="tpu_custom_call" | custom-call | flops 1000000000 | bytes 4194304 | tf_op jit(solution)/shard_map/pallas_call | solution.py:352
  108.0 4.8 %all-to-all-start.2 = ((bf16[32,32,256]{2,1,0:T(8,128)(2,1)}), bf16[32,32,256]{2,1,0:T(8,128)(2,1)S(1)}, u32[]{:S(2)}, u32[]{:S(2)}) async-start(bf16[32,32,256]{2,1,0:T(8,128)(2,1)} %bitcast.22), calls=%async_computation.2 | async-start | bytes 1048576 | tf_op jit(solution)/shard_map/all_to_all | solution.py:471
  112.9 14.4 %all-to-all-done.2 = bf16[32,32,256]{2,1,0:T(8,128)(2,1)S(1)} async-done(((bf16[32,32,256]{2,1,0:T(8,128)(2,1)}), bf16[32,32,256]{2,1,0:T(8,128)(2,1)S(1)}, u32[]{:S(2)}, u32[]{:S(2)}) %all-to-all-start.2) | async-done | bytes 524320 | tf_op jit(solution)/shard_map/all_to_all | solution.py:471
  127.3 3.6 %shard_map.84 = (bf16[64,2048]{1,0:T(8,128)(2,1)S(1)}, bf16[64,2048]{1,0:T(8,128)(2,1)S(1)}, bf16[64,2048]{1,0:T(8,128)(2,1)S(1)}, bf16[64,2048]{1,0:T(8,128)(2,1)S(1)}) custom-call(s32[4]{0:T(128)S(1)} %pad_add_fusion.block_ref, bf16[2,512,256]{2,1,0:T(8,128)(2,1)S(1)} %bitcast.31, bf16[4,2,512,512]{3,2,1,0:T(8,128)(2,1)} %bitcast.32), custom_call_target="tpu_custom_call" | custom-call | flops 1073741824 | bytes 5767168 | tf_op jit(solution)/shard_map/pallas_call | solution.py:406
  130.9 2.6 %collective-permute-start.9 = (bf16[64,2048]{1,0:T(8,128)(2,1)S(1)}, bf16[64,2048]{1,0:T(8,128)(2,1)S(1)}, u32[]{:S(2)}, u32[]{:S(2)}) collective-permute-start(bf16[64,2048]{1,0:T(8,128)(2,1)S(1)} %get-tuple-element.43), channel_id=1, source_target_pairs={{0,0},{1,16},{2,2},{3,18},{4,4},{5,20},{6,6},{7,22},{8,24},{9,8},{... | collective-permute-start | bytes 786440 | tf_op jit(solution)/shard_map/ppermute | solution.py:88
  133.5 3.9 %collective-permute-start.11 = (bf16[64,2048]{1,0:T(8,128)(2,1)S(1)}, bf16[64,2048]{1,0:T(8,128)(2,1)S(1)}, u32[]{:S(2)}, u32[]{:S(2)}) collective-permute-start(bf16[64,2048]{1,0:T(8,128)(2,1)S(1)} %get-tuple-element.45), channel_id=1, source_target_pairs={{0,16},{1,0},{2,18},{3,2},{4,20},{5,4},{6,22},{7,6},{8,8},{9,24},{... | collective-permute-start | bytes 786440 | tf_op jit(solution)/shard_map/ppermute | solution.py:88
  137.4 2.3 %collective-permute-start.12 = (bf16[64,2048]{1,0:T(8,128)(2,1)S(1)}, bf16[64,2048]{1,0:T(8,128)(2,1)S(1)}, u32[]{:S(2)}, u32[]{:S(2)}) collective-permute-start(bf16[64,2048]{1,0:T(8,128)(2,1)S(1)} %get-tuple-element.46), channel_id=1, source_target_pairs={{0,24},{1,8},{2,26},{3,10},{4,28},{5,12},{6,30},{7,14},{8,0},{9,16... | collective-permute-start | bytes 786440 | tf_op jit(solution)/shard_map/ppermute | solution.py:88
  139.8 3.2 %collective-permute-done.9.refs_0_ = bf16[64,2048]{1,0:T(8,128)(2,1)S(1)} collective-permute-done((bf16[64,2048]{1,0:T(8,128)(2,1)S(1)}, bf16[64,2048]{1,0:T(8,128)(2,1)S(1)}, u32[]{:S(2)}, u32[]{:S(2)}) %collective-permute-start.9) | collective-permute-done | bytes 262176 | tf_op jit(solution)/shard_map/ppermute | solution.py:88
  143.0 16.4 %collective-permute-done.10.refs_1_ = bf16[64,2048]{1,0:T(8,128)(2,1)S(1)} collective-permute-done((bf16[64,2048]{1,0:T(8,128)(2,1)S(1)}, bf16[64,2048]{1,0:T(8,128)(2,1)S(1)}, u32[]{:S(2)}, u32[]{:S(2)}) %collective-permute-start.10) | collective-permute-done | bytes 262176 | tf_op jit(solution)/shard_map/ppermute | solution.py:88
  159.4 1.5 shard_map.85
  (41 shorter events, 5.6 us)
Async XLA Ops:
  6.5 10.7 %copy-start = (f32[3,3,512]{2,1,0:T(4,128)S(1)}, f32[3,3,512]{2,1,0:T(4,128)}, u32[]{:S(2)}) copy-start(f32[3,3,512]{2,1,0:T(4,128)} %param.10) | copy-start | bytes 55300
  6.5 1.2 copy-start.3
  6.5 51.9 %all-gather.4.cloned.1.call-start = ((), (), s32[]{:S(2)}) async-start(), calls=%async_computation.3 | async-start | bytes 7864320 | tf_op jit(solution)/shard_map/all_gather | solution.py:444
  6.5 3.4 %copy-start.4 = (f32[128,512]{1,0:T(8,128)S(1)}, f32[128,512]{1,0:T(8,128)}, u32[]{:S(2)}) copy-start(f32[128,512]{1,0:T(8,128)} %param.11) | copy-start | bytes 786436
  7.9 10.3 %collective-permute-start = (bf16[128,1024]{1,0:T(8,128)(2,1)S(1)}, bf16[128,1024]{1,0:T(8,128)(2,1)S(1)}, u32[]{:S(2)}, u32[]{:S(2)}) collective-permute-start(bf16[128,1024]{1,0:T(8,128)(2,1)S(1)} %get-tuple-element.48), channel_id=1, source_target_pairs={{0,1},{1,0},{2,3},{3,2},{4,5},{5,4},{6,7},{7,6},{8,9},{9,8},{10,11... | collective-permute-start | bytes 786440 | tf_op jit(solution)/shard_map/ppermute | solution.py:107
  8.4 13.2 %collective-permute-start.1 = (bf16[128,1024]{1,0:T(8,128)(2,1)S(1)}, bf16[128,1024]{1,0:T(8,128)(2,1)S(1)}, u32[]{:S(2)}, u32[]{:S(2)}) collective-permute-start(bf16[128,1024]{1,0:T(8,128)(2,1)S(1)} %get-tuple-element.50), channel_id=1, source_target_pairs={{0,1},{1,0},{2,3},{3,2},{4,5},{5,4},{6,7},{7,6},{8,9},{9,8},{10,11... | collective-permute-start | bytes 786440 | tf_op jit(solution)/shard_map/ppermute | solution.py:107
  10.8 14.4 %all-to-all-start = ((f32[16,32,128]{2,1,0:T(8,128)}), f32[16,32,128]{2,1,0:T(8,128)S(1)}, u32[]{:S(2)}, u32[]{:S(2)}) async-start(f32[16,32,128]{2,1,0:T(8,128)} %bitcast.14), calls=%async_computation | async-start | bytes 524288 | tf_op jit(solution)/shard_map/all_to_all | solution.py:450
  17.1 95.8 %all-gather.6.cloned.1.call-start = ((), (), s32[]{:S(2)}) async-start(), calls=%async_computation.4 | async-start | bytes 4718592 | tf_op jit(solution)/shard_map/all_gather | solution.py:464
  18.3 16.7 %collective-permute-start.2 = (bf16[128,1024]{1,0:T(8,128)(2,1)S(1)}, bf16[128,1024]{1,0:T(8,128)(2,1)S(1)}, u32[]{:S(2)}, u32[]{:S(2)}) collective-permute-start(bf16[128,1024]{1,0:T(8,128)(2,1)S(1)} %fusion.3), channel_id=1, source_target_pairs={{0,8},{2,10},{4,12},{6,14},{8,16},{10,18},{12,20},{14,22},{16,24},... | collective-permute-start | bytes 786440 | tf_op jit(solution)/shard_map/ppermute | solution.py:125
  21.7 13.3 %collective-permute-start.3 = (bf16[128,1024]{1,0:T(8,128)(2,1)S(1)}, bf16[128,1024]{1,0:T(8,128)(2,1)S(1)}, u32[]{:S(2)}, u32[]{:S(2)}) collective-permute-start(bf16[128,1024]{1,0:T(8,128)(2,1)S(1)} %fusion.1.refs_0_), channel_id=1, source_target_pairs={{0,1},{1,0},{2,3},{3,2},{4,5},{5,4},{6,7},{7,6},{8,9},{9,8},{10,11... | collective-permute-start | bytes 786440 | tf_op jit(solution)/shard_map/ppermute | solution.py:134
  25.4 10.7 %collective-permute-start.7 = (bf16[128,1024]{1,0:T(8,128)(2,1)S(1)}, bf16[128,1024]{1,0:T(8,128)(2,1)S(1)}, u32[]{:S(2)}, u32[]{:S(2)}) collective-permute-start(bf16[128,1024]{1,0:T(8,128)(2,1)S(1)} %dynamic-slice_bitcast_fusion), channel_id=1, source_target_pairs={{0,24},{2,26},{4,28},{6,30},{8,0},{10,2},{12,4},{14,6},{16,8},{18,... | collective-permute-start | bytes 786440 | tf_op jit(solution)/shard_map/ppermute | solution.py:125
  35.0 10.9 %collective-permute-start.5 = (bf16[128,1024]{1,0:T(8,128)(2,1)S(1)}, bf16[128,1024]{1,0:T(8,128)(2,1)S(1)}, u32[]{:S(2)}, u32[]{:S(2)}) collective-permute-start(bf16[128,1024]{1,0:T(8,128)(2,1)S(1)} %dynamic-slice_bitcast_fusion.1), channel_id=1, source_target_pairs={{0,16},{2,18},{4,20},{6,22},{8,24},{10,26},{12,28},{14,30},{16,0},... | collective-permute-start | bytes 786440 | tf_op jit(solution)/shard_map/ppermute | solution.py:125
  35.1 11.3 %collective-permute-start.4 = (bf16[128,1024]{1,0:T(8,128)(2,1)S(1)}, bf16[128,1024]{1,0:T(8,128)(2,1)S(1)}, u32[]{:S(2)}, u32[]{:S(2)}) collective-permute-start(bf16[128,1024]{1,0:T(8,128)(2,1)S(1)} %collective-permute-done.2.refs_2_), channel_id=1, source_target_pairs={{0,1},{1,0},{2,3},{3,2},{4,5},{5,4},{6,7},{7,6},{8,9},{9,8},{10,11... | collective-permute-start | bytes 786440 | tf_op jit(solution)/shard_map/ppermute | solution.py:134
  36.1 10.3 %collective-permute-start.8 = (bf16[128,1024]{1,0:T(8,128)(2,1)S(1)}, bf16[128,1024]{1,0:T(8,128)(2,1)S(1)}, u32[]{:S(2)}, u32[]{:S(2)}) collective-permute-start(bf16[128,1024]{1,0:T(8,128)(2,1)S(1)} %collective-permute-done.7.refs_6_), channel_id=1, source_target_pairs={{0,1},{1,0},{2,3},{3,2},{4,5},{5,4},{6,7},{7,6},{8,9},{9,8},{10,11... | collective-permute-start | bytes 786440 | tf_op jit(solution)/shard_map/ppermute | solution.py:134
  45.9 9.2 %collective-permute-start.6 = (bf16[128,1024]{1,0:T(8,128)(2,1)S(1)}, bf16[128,1024]{1,0:T(8,128)(2,1)S(1)}, u32[]{:S(2)}, u32[]{:S(2)}) collective-permute-start(bf16[128,1024]{1,0:T(8,128)(2,1)S(1)} %collective-permute-done.5.refs_4_), channel_id=1, source_target_pairs={{0,1},{1,0},{2,3},{3,2},{4,5},{5,4},{6,7},{7,6},{8,9},{9,8},{10,11... | collective-permute-start | bytes 786440 | tf_op jit(solution)/shard_map/ppermute | solution.py:134
  64.2 41.2 %copy-start.1 = (bf16[2,256,256]{2,1,0:T(8,128)(2,1)S(1)}, bf16[2,256,256]{2,1,0:T(8,128)(2,1)}, u32[]{:S(2)}) copy-start(bf16[2,256,256]{2,1,0:T(8,128)(2,1)} %constant.233.clone.refs_5_) | copy-start | bytes 786436
  64.2 41.2 %copy-start.2 = (bf16[2,128,256]{2,1,0:T(8,128)(2,1)S(1)}, bf16[2,128,256]{2,1,0:T(8,128)(2,1)}, u32[]{:S(2)}) copy-start(bf16[2,128,256]{2,1,0:T(8,128)(2,1)} %constant.232.clone.refs_4_) | copy-start | bytes 393220
  108.0 19.3 %all-to-all-start.2 = ((bf16[32,32,256]{2,1,0:T(8,128)(2,1)}), bf16[32,32,256]{2,1,0:T(8,128)(2,1)S(1)}, u32[]{:S(2)}, u32[]{:S(2)}) async-start(bf16[32,32,256]{2,1,0:T(8,128)(2,1)} %bitcast.22), calls=%async_computation.2 | async-start | bytes 1048576 | tf_op jit(solution)/shard_map/all_to_all | solution.py:471
  130.9 12.1 %collective-permute-start.9 = (bf16[64,2048]{1,0:T(8,128)(2,1)S(1)}, bf16[64,2048]{1,0:T(8,128)(2,1)S(1)}, u32[]{:S(2)}, u32[]{:S(2)}) collective-permute-start(bf16[64,2048]{1,0:T(8,128)(2,1)S(1)} %get-tuple-element.43), channel_id=1, source_target_pairs={{0,0},{1,16},{2,2},{3,18},{4,4},{5,20},{6,6},{7,22},{8,24},{9,8},{... | collective-permute-start | bytes 786440 | tf_op jit(solution)/shard_map/ppermute | solution.py:88
  133.5 25.9 %collective-permute-start.10 = (bf16[64,2048]{1,0:T(8,128)(2,1)S(1)}, bf16[64,2048]{1,0:T(8,128)(2,1)S(1)}, u32[]{:S(2)}, u32[]{:S(2)}) collective-permute-start(bf16[64,2048]{1,0:T(8,128)(2,1)S(1)} %get-tuple-element.44), channel_id=1, source_target_pairs={{0,8},{1,24},{2,10},{3,26},{4,12},{5,28},{6,14},{7,30},{8,16},{9,0... | collective-permute-start | bytes 786440 | tf_op jit(solution)/shard_map/ppermute | solution.py:88
  133.5 25.8 %collective-permute-start.11 = (bf16[64,2048]{1,0:T(8,128)(2,1)S(1)}, bf16[64,2048]{1,0:T(8,128)(2,1)S(1)}, u32[]{:S(2)}, u32[]{:S(2)}) collective-permute-start(bf16[64,2048]{1,0:T(8,128)(2,1)S(1)} %get-tuple-element.45), channel_id=1, source_target_pairs={{0,16},{1,0},{2,18},{3,2},{4,20},{5,4},{6,22},{7,6},{8,8},{9,24},{... | collective-permute-start | bytes 786440 | tf_op jit(solution)/shard_map/ppermute | solution.py:88
  137.4 22.0 %collective-permute-start.12 = (bf16[64,2048]{1,0:T(8,128)(2,1)S(1)}, bf16[64,2048]{1,0:T(8,128)(2,1)S(1)}, u32[]{:S(2)}, u32[]{:S(2)}) collective-permute-start(bf16[64,2048]{1,0:T(8,128)(2,1)S(1)} %get-tuple-element.46), channel_id=1, source_target_pairs={{0,24},{1,8},{2,26},{3,10},{4,28},{5,12},{6,30},{7,14},{8,0},{9,16... | collective-permute-start | bytes 786440 | tf_op jit(solution)/shard_map/ppermute | solution.py:88
Sparse Core Ops, SparseCore 0:
  8.9 49.5 all-gather.3
  60.4 51.3 all-gather.5

commit v24 on v20

--- a/solution.py
+++ b/solution.py
@@ -135,8 +135,9 @@
 
 
 def project_kernel(tp_parts, place_ref, *refs):
-    *share_refs, weight_ref, out_ref, held, sems = refs
+    *share_refs, weight_ref, out_ref, held, left, sems = refs
     seq_parts, streams, chans, count = out_ref.shape
+    rows, width = share_refs[0].shape
     copies = []
     for stream in range(streams):
         for step in range(tp_parts):
@@ -147,17 +148,17 @@
                 )
             )
             copies[-1].start()
-    left = [
-        jnp.concatenate([share_ref[...] for share_ref in share_refs[step::tp_parts]])
-        for step in range(tp_parts)
-    ]
+    for index, share_ref in enumerate(share_refs):
+        chunk, step = divmod(index, tp_parts)
+        left[chunk * rows : (chunk + 1) * rows, step * width : (step + 1) * width] = share_ref[...]
     for stream in range(streams):
-        sums = jnp.zeros((count, seq_parts * chans), jnp.float32)
-        for step in range(tp_parts):
-            copies[stream * tp_parts + step].wait()
-            sums = sums + jnp.dot(
-                left[step], held[stream, step], preferred_element_type=jnp.float32
-            )
+        for copy in copies[stream * tp_parts : (stream + 1) * tp_parts]:
+            copy.wait()
+        sums = jnp.dot(
+            left[...],
+            held[stream].reshape(tp_parts * width, seq_parts * chans),
+            preferred_element_type=jnp.float32,
+        )
         turned = sums.astype(out_ref.dtype).T
         for seq in range(seq_parts):
             out_ref[seq, stream] = turned[seq * chans : (seq + 1) * chans]
@@ -182,6 +183,7 @@
         out_shape=jax.ShapeDtypeStruct((seq_parts, streams, chans, count), jnp.bfloat16),
         scratch_shapes=[
             pltpu.VMEM(weight.shape, weight.dtype),
+            pltpu.VMEM((count, tp_parts * width), jnp.bfloat16),
             pltpu.SemaphoreType.DMA((streams * tp_parts,)),
         ],
         compiler_params=pltpu.CompilerParams(vmem_limit_bytes=48 * 2**20),
@@ -373,7 +375,7 @@
     *out_refs, turned, left, held, sems = refs
     tp_parts = gated_ref.shape[0]
     part_rows = out_refs[0].shape[0]
-    inner_parts, _, _, width = held.shape
+    inner_parts, _, depth, width = held.shape
     copies = [
         pltpu.make_async_copy(weight_ref.at[inner], held.at[inner], sems.at[inner])
         for inner in range(inner_parts)
@@ -384,12 +386,16 @@
         turned[...] = gated_ref[part].T
         for index in range(len(out_refs)):
             begin = pl.multiple_of(block_ref[index] * part_rows, part_rows)
-            left[part, index * part_rows : (index + 1) * part_rows] = turned[pl.ds(begin, part_rows)]
+            left[
+                index * part_rows : (index + 1) * part_rows, part * depth : (part + 1) * depth
+            ] = turned[pl.ds(begin, part_rows)]
     for inner in range(inner_parts):
         copies[inner].wait()
-        sums = jnp.zeros((left.shape[1], width), jnp.float32)
-        for part in range(tp_parts):
-            sums = sums + jnp.dot(left[part], held[inner, part], preferred_element_type=jnp.float32)
+        sums = jnp.dot(
+            left[...],
+            held[inner].reshape(tp_parts * depth, width),
+            preferred_element_type=jnp.float32,
+        )
         for index, out_ref in enumerate(out_refs):
             out_ref[:, inner * width : (inner + 1) * width] = sums[
                 index * part_rows : (index + 1) * part_rows
@@ -412,7 +418,7 @@
         out_specs=[vmem] * len(blocks),
         scratch_shapes=[
             pltpu.VMEM((rows, depth), jnp.bfloat16),
-            pltpu.VMEM((tp_parts, rows, depth), jnp.bfloat16),
+            pltpu.VMEM((rows, tp_parts * depth), jnp.bfloat16),
             pltpu.VMEM(weight.shape, weight.dtype),
             pltpu.SemaphoreType.DMA((inner_parts,)),
         ],

time: 167 us -> 167 us (level)
  no operation moved by 1% of the time
where the time goes in v24:
time: 167 us
  waiting for transfers between devices  63.1 us (38%)
  blocking collectives  40.7 us (24%)
  starting transfers between devices  32.6 us (20%)
  between operations  13.8 us (8%)
  Pallas kernels  13.3 us (8%)
  local copies, waits for them, and re-layouts  2.81 us (2%)
    all_to_all x1, blocking collectives, per_device(): lax.all_to_all(partial, 'seq', split_axis=0, concat_axis=0, tiled=True)  40.7 us
    ppermute x4, waiting for transfers between devices, return_output(): arrived.append(lax.ppermute(piece, ('seq', 'tp'), pairs))  19.5 us
    all_to_all x1, waiting for transfers between devices, per_device(): lax.all_to_all(gated.reshape((-1,) + gated.shape[3:]), ('tp', 'seq'), spl...  14.4 us
    ppermute x3, waiting for transfers between devices, cross_outer(): lax.ppermute(piece, 'seq', [(i, (i + far) % seq_parts) for i in range(seq...  10.5 us
    ppermute x3, starting transfers between devices, cross_outer(): lax.ppermute(piece, 'seq', [(i, (i + far) % seq_parts) for i in range(seq...  9.2 us
    ppermute x4, starting transfers between devices, return_output(): arrived.append(lax.ppermute(piece, ('seq', 'tp'), pairs))  8.85 us
    ppermute x4, waiting for transfers between devices, share_over_tp(): pieces.append(lax.ppermute(part, 'tp', pairs))  8.77 us
    all_to_all x1, starting transfers between devices, per_device(): lax.all_to_all(long_filter.T.reshape(seq_parts, chans, rows), 'seq', spli...  6.27 us
  transfers between devices with their start and end apart: 16, of which 11 were waited for; matrix products, arithmetic and copies ran while one was open for 1% of the time, Pallas kernels for 5%

profile of v24, /device:TPU:12, one launch (start us, length us, event | category | flops | bytes accessed | tf_op | source)
XLA Modules:
  0.0 166.5 jit_solution(1544967992308888987)
XLA Ops:
  9.6 6.3 %all-to-all-start = ((f32[16,32,128]{2,1,0:T(8,128)}), f32[16,32,128]{2,1,0:T(8,128)S(1)}, u32[]{:S(2)}, u32[]{:S(2)}) async-start(f32[16,32,128]{2,1,0:T(8,128)} %bitcast.16), calls=%async_computation | async-start | bytes 524288 | tf_op jit(solution)/shard_map/all_to_all | solution.py:455
  16.0 5.6 %collective-permute-done = bf16[2,128,1024]{2,1,0:T(8,128)(2,1)S(1)} collective-permute-done((bf16[2,128,1024]{2,1,0:T(8,128)(2,1)S(1)}, bf16[2,128,1024]{2,1,0:T(8,128)(2,1)S(1)}, u32[]{:S(2)}, u32[]{:S(2)}) %collective-permute-start) | collective-permute-done | bytes 524320 | tf_op jit(solution)/shard_map/ppermute | solution.py:107
  21.8 1.6 collective-permute-start.1
  25.0 1.3 collective-permute-start.6
  26.2 3.6 %collective-permute-done.1.refs_2_ = bf16[128,1024]{1,0:T(8,128)(2,1)S(1)} collective-permute-done((bf16[128,1024]{1,0:T(8,128)(2,1)S(1)}, bf16[128,1024]{1,0:T(8,128)(2,1)S(1)}, u32[]{:S(2)}, u32[]{:S(2)}) %collective-permute-start.1) | collective-permute-done | bytes 262176 | tf_op jit(solution)/shard_map/ppermute | solution.py:124
  30.3 6.3 %collective-permute-start.4 = (bf16[128,1024]{1,0:T(8,128)(2,1)S(1)}, bf16[128,1024]{1,0:T(8,128)(2,1)S(1)}, u32[]{:S(2)}, u32[]{:S(2)}) collective-permute-start(bf16[128,1024]{1,0:T(8,128)(2,1)S(1)} %dynamic-slice_bitcast_fusion.1), channel_id=1, source_target_pairs={{0,16},{2,18},{4,20},{6,22},{8,24},{10,26},{12,28},{14,30},{16,0},... | collective-permute-start | bytes 786440 | tf_op jit(solution)/shard_map/ppermute | solution.py:124
  36.6 1.5 collective-permute-start.3
  38.1 3.4 %collective-permute-done.6.refs_6_ = bf16[128,1024]{1,0:T(8,128)(2,1)S(1)} collective-permute-done((bf16[128,1024]{1,0:T(8,128)(2,1)S(1)}, bf16[128,1024]{1,0:T(8,128)(2,1)S(1)}, u32[]{:S(2)}, u32[]{:S(2)}) %collective-permute-start.6) | collective-permute-done | bytes 262176 | tf_op jit(solution)/shard_map/ppermute | solution.py:124
  41.5 3.5 %collective-permute-done.4.refs_4_ = bf16[128,1024]{1,0:T(8,128)(2,1)S(1)} collective-permute-done((bf16[128,1024]{1,0:T(8,128)(2,1)S(1)}, bf16[128,1024]{1,0:T(8,128)(2,1)S(1)}, u32[]{:S(2)}, u32[]{:S(2)}) %collective-permute-start.4) | collective-permute-done | bytes 262176 | tf_op jit(solution)/shard_map/ppermute | solution.py:124
  46.0 4.7 %collective-permute-done.7.refs_7_ = bf16[128,1024]{1,0:T(8,128)(2,1)S(1)} collective-permute-done((bf16[128,1024]{1,0:T(8,128)(2,1)S(1)}, bf16[128,1024]{1,0:T(8,128)(2,1)S(1)}, u32[]{:S(2)}, u32[]{:S(2)}) %collective-permute-start.7) | collective-permute-done | bytes 262176 | tf_op jit(solution)/shard_map/ppermute | solution.py:133
  50.7 3.5 %collective-permute-done.5.refs_5_ = bf16[128,1024]{1,0:T(8,128)(2,1)S(1)} collective-permute-done((bf16[128,1024]{1,0:T(8,128)(2,1)S(1)}, bf16[128,1024]{1,0:T(8,128)(2,1)S(1)}, u32[]{:S(2)}, u32[]{:S(2)}) %collective-permute-start.5) | collective-permute-done | bytes 262176 | tf_op jit(solution)/shard_map/ppermute | solution.py:133
  54.3 3.6 %all-gather.4.cloned.1.call-done = bf16[3,2048,512]{2,1,0:T(8,128)(2,1)} async-done(((bf16[3,512,512]{2,1,0:T(8,128)(2,1)}), bf16[3,2048,512]{2,1,0:T(8,128)(2,1)}) %all-gather.4.cloned.1.call-update) | async-done | bytes 6291472 | tf_op jit(solution)/shard_map/all_gather | solution.py:449
  57.9 5.6 %shard_map.82 = bf16[16,3,32,512]{3,2,1,0:T(8,128)(2,1)S(1)} custom-call(s32[1]{0:T(128)} %bitcast.10.place_ref, bf16[128,1024]{1,0:T(8,128)(2,1)S(1)} %get-tuple-element.31.refs_0_, bf16[128,1024]{1,0:T(8,128)(2,1)S(1)} %collective-permute-done.2.refs_1_, bf16[128,1024]{1,0:T(8,128)(2,1)S(1)} %collective-permute-done.1.refs_2_, ...), custom_call_target="tpu_custom_call" | custom-call | flops 96636764160 | bytes 9961472 | tf_op jit(solution)/shard_map/pallas_call | solution.py:177
  63.5 40.7 %all_to_all.15.refs_0_ = bf16[16,3,32,512]{3,2,1,0:T(8,128)(2,1)S(1)} all-to-all(bf16[16,3,32,512]{3,2,1,0:T(8,128)(2,1)S(1)} %shard_map.82), channel_id=1, replica_groups=mesh['seq'=16,'tp'=2] {'seq'}, dimensions={0} | all-to-all | bytes 3145728 | tf_op jit(solution)/shard_map/all_to_all | solution.py:473
  104.1 2.6 %shard_map.83 = bf16[2,4,4,32,256]{4,3,2,1,0:T(8,128)(2,1)} custom-call(bf16[16,3,32,512]{3,2,1,0:T(8,128)(2,1)S(1)} %all_to_all.15.refs_0_, f32[16,32,128]{2,1,0:T(8,128)S(1)} %all-to-all-done.refs_1_, f32[3,3,32,128]{3,2,1,0:T(8,128)S(1)} %broadcast_in_dim.7.refs_2_, f32[32,128]{1,0:T(8,128)S(1)} %broadcast_in_dim.8.refs_3_, ...), custom_call_target="tpu_custom_call" | custom-call | flops 1000000000 | bytes 4194304 | tf_op jit(solution)/shard_map/pallas_call | solution.py:353
  106.7 4.8 %all-to-all-start.2 = ((bf16[32,32,256]{2,1,0:T(8,128)(2,1)}), bf16[32,32,256]{2,1,0:T(8,128)(2,1)S(1)}, u32[]{:S(2)}, u32[]{:S(2)}) async-start(bf16[32,32,256]{2,1,0:T(8,128)(2,1)} %bitcast.22), calls=%async_computation.2 | async-start | bytes 1048576 | tf_op jit(solution)/shard_map/all_to_all | solution.py:476
  111.7 14.4 %all-to-all-done.2 = bf16[32,32,256]{2,1,0:T(8,128)(2,1)S(1)} async-done(((bf16[32,32,256]{2,1,0:T(8,128)(2,1)}), bf16[32,32,256]{2,1,0:T(8,128)(2,1)S(1)}, u32[]{:S(2)}, u32[]{:S(2)}) %all-to-all-start.2) | async-done | bytes 524320 | tf_op jit(solution)/shard_map/all_to_all | solution.py:476
  126.1 3.6 %shard_map.84 = (bf16[64,2048]{1,0:T(8,128)(2,1)S(1)}, bf16[64,2048]{1,0:T(8,128)(2,1)S(1)}, bf16[64,2048]{1,0:T(8,128)(2,1)S(1)}, bf16[64,2048]{1,0:T(8,128)(2,1)S(1)}) custom-call(s32[4]{0:T(128)S(1)} %pad_add_fusion.block_ref, bf16[2,512,256]{2,1,0:T(8,128)(2,1)S(1)} %bitcast.33, bf16[4,2,512,512]{3,2,1,0:T(8,128)(2,1)} %bitcast.34), custom_call_target="tpu_custom_call" | custom-call | flops 1073741824 | bytes 5767168 | tf_op jit(solution)/shard_map/pallas_call | solution.py:411
  129.6 2.6 %collective-permute-start.8 = (bf16[64,2048]{1,0:T(8,128)(2,1)S(1)}, bf16[64,2048]{1,0:T(8,128)(2,1)S(1)}, u32[]{:S(2)}, u32[]{:S(2)}) collective-permute-start(bf16[64,2048]{1,0:T(8,128)(2,1)S(1)} %get-tuple-element.43), channel_id=1, source_target_pairs={{0,0},{1,16},{2,2},{3,18},{4,4},{5,20},{6,6},{7,22},{8,24},{9,8},{... | collective-permute-start | bytes 786440 | tf_op jit(solution)/shard_map/ppermute | solution.py:88
  132.3 3.9 %collective-permute-start.10 = (bf16[64,2048]{1,0:T(8,128)(2,1)S(1)}, bf16[64,2048]{1,0:T(8,128)(2,1)S(1)}, u32[]{:S(2)}, u32[]{:S(2)}) collective-permute-start(bf16[64,2048]{1,0:T(8,128)(2,1)S(1)} %get-tuple-element.45), channel_id=1, source_target_pairs={{0,16},{1,0},{2,18},{3,2},{4,20},{5,4},{6,22},{7,6},{8,8},{9,24},{... | collective-permute-start | bytes 786440 | tf_op jit(solution)/shard_map/ppermute | solution.py:88
  136.2 2.3 %collective-permute-start.11 = (bf16[64,2048]{1,0:T(8,128)(2,1)S(1)}, bf16[64,2048]{1,0:T(8,128)(2,1)S(1)}, u32[]{:S(2)}, u32[]{:S(2)}) collective-permute-start(bf16[64,2048]{1,0:T(8,128)(2,1)S(1)} %get-tuple-element.46), channel_id=1, source_target_pairs={{0,24},{1,8},{2,26},{3,10},{4,28},{5,12},{6,30},{7,14},{8,0},{9,16... | collective-permute-start | bytes 786440 | tf_op jit(solution)/shard_map/ppermute | solution.py:88
  138.6 3.2 %collective-permute-done.8.refs_0_ = bf16[64,2048]{1,0:T(8,128)(2,1)S(1)} collective-permute-done((bf16[64,2048]{1,0:T(8,128)(2,1)S(1)}, bf16[64,2048]{1,0:T(8,128)(2,1)S(1)}, u32[]{:S(2)}, u32[]{:S(2)}) %collective-permute-start.8) | collective-permute-done | bytes 262176 | tf_op jit(solution)/shard_map/ppermute | solution.py:88
  141.8 16.4 %collective-permute-done.9.refs_1_ = bf16[64,2048]{1,0:T(8,128)(2,1)S(1)} collective-permute-done((bf16[64,2048]{1,0:T(8,128)(2,1)S(1)}, bf16[64,2048]{1,0:T(8,128)(2,1)S(1)}, u32[]{:S(2)}, u32[]{:S(2)}) %collective-permute-start.9) | collective-permute-done | bytes 262176 | tf_op jit(solution)/shard_map/ppermute | solution.py:88
  158.1 1.5 shard_map.85
  (38 shorter events, 6.5 us)
Async XLA Ops:
  6.5 18.1 %copy-start = (f32[3,3,512]{2,1,0:T(4,128)S(1)}, f32[3,3,512]{2,1,0:T(4,128)}, u32[]{:S(2)}) copy-start(f32[3,3,512]{2,1,0:T(4,128)} %param.10) | copy-start | bytes 55300
  6.5 1.2 copy-start.3
  6.5 51.3 %all-gather.4.cloned.1.call-start = ((), (), s32[]{:S(2)}) async-start(), calls=%async_computation.3 | async-start | bytes 7864320 | tf_op jit(solution)/shard_map/all_gather | solution.py:449
  7.8 0.9 copy-start.4
  7.9 13.7 %collective-permute-start = (bf16[2,128,1024]{2,1,0:T(8,128)(2,1)S(1)}, bf16[2,128,1024]{2,1,0:T(8,128)(2,1)S(1)}, u32[]{:S(2)}, u32[]{:S(2)}) collective-permute-start(bf16[2,128,1024]{2,1,0:T(8,128)(2,1)S(1)} %pad_maximum_fusion.1), channel_id=1, source_target_pairs={{0,1},{1,0},{2,3},{3,2},{4,5},{5,4},{6,7},{7,6},{8,9},{9,8},{10,11... | collective-permute-start | bytes 1572872 | tf_op jit(solution)/shard_map/ppermute | solution.py:107
  9.6 15.2 %all-to-all-start = ((f32[16,32,128]{2,1,0:T(8,128)}), f32[16,32,128]{2,1,0:T(8,128)S(1)}, u32[]{:S(2)}, u32[]{:S(2)}) async-start(f32[16,32,128]{2,1,0:T(8,128)} %bitcast.16), calls=%async_computation | async-start | bytes 524288 | tf_op jit(solution)/shard_map/all_to_all | solution.py:455
  15.8 95.8 %all-gather.6.cloned.1.call-start = ((), (), s32[]{:S(2)}) async-start(), calls=%async_computation.4 | async-start | bytes 4718592 | tf_op jit(solution)/shard_map/all_gather | solution.py:469
  21.8 8.0 %collective-permute-start.1 = (bf16[128,1024]{1,0:T(8,128)(2,1)S(1)}, bf16[128,1024]{1,0:T(8,128)(2,1)S(1)}, u32[]{:S(2)}, u32[]{:S(2)}) collective-permute-start(bf16[128,1024]{1,0:T(8,128)(2,1)S(1)} %get-tuple-element.48), channel_id=1, source_target_pairs={{0,8},{2,10},{4,12},{6,14},{8,16},{10,18},{12,20},{14,22},{16,24},... | collective-permute-start | bytes 786440 | tf_op jit(solution)/shard_map/ppermute | solution.py:124
  23.4 6.9 %collective-permute-start.2 = (bf16[128,1024]{1,0:T(8,128)(2,1)S(1)}, bf16[128,1024]{1,0:T(8,128)(2,1)S(1)}, u32[]{:S(2)}, u32[]{:S(2)}) collective-permute-start(bf16[128,1024]{1,0:T(8,128)(2,1)S(1)} %get-tuple-element.31.refs_0_), channel_id=1, source_target_pairs={{0,1},{1,0},{2,3},{3,2},{4,5},{5,4},{6,7},{7,6},{8,9},{9,8},{10,11... | collective-permute-start | bytes 786440 | tf_op jit(solution)/shard_map/ppermute | solution.py:133
  25.0 16.5 %collective-permute-start.6 = (bf16[128,1024]{1,0:T(8,128)(2,1)S(1)}, bf16[128,1024]{1,0:T(8,128)(2,1)S(1)}, u32[]{:S(2)}, u32[]{:S(2)}) collective-permute-start(bf16[128,1024]{1,0:T(8,128)(2,1)S(1)} %dynamic-slice_bitcast_fusion), channel_id=1, source_target_pairs={{0,24},{2,26},{4,28},{6,30},{8,0},{10,2},{12,4},{14,6},{16,8},{18,... | collective-permute-start | bytes 786440 | tf_op jit(solution)/shard_map/ppermute | solution.py:124
  30.3 14.6 %collective-permute-start.4 = (bf16[128,1024]{1,0:T(8,128)(2,1)S(1)}, bf16[128,1024]{1,0:T(8,128)(2,1)S(1)}, u32[]{:S(2)}, u32[]{:S(2)}) collective-permute-start(bf16[128,1024]{1,0:T(8,128)(2,1)S(1)} %dynamic-slice_bitcast_fusion.1), channel_id=1, source_target_pairs={{0,16},{2,18},{4,20},{6,22},{8,24},{10,26},{12,28},{14,30},{16,0},... | collective-permute-start | bytes 786440 | tf_op jit(solution)/shard_map/ppermute | solution.py:124
  36.6 14.1 %collective-permute-start.3 = (bf16[128,1024]{1,0:T(8,128)(2,1)S(1)}, bf16[128,1024]{1,0:T(8,128)(2,1)S(1)}, u32[]{:S(2)}, u32[]{:S(2)}) collective-permute-start(bf16[128,1024]{1,0:T(8,128)(2,1)S(1)} %collective-permute-done.1.refs_2_), channel_id=1, source_target_pairs={{0,1},{1,0},{2,3},{3,2},{4,5},{5,4},{6,7},{7,6},{8,9},{9,8},{10,11... | collective-permute-start | bytes 786440 | tf_op jit(solution)/shard_map/ppermute | solution.py:133
  41.5 9.2 %collective-permute-start.7 = (bf16[128,1024]{1,0:T(8,128)(2,1)S(1)}, bf16[128,1024]{1,0:T(8,128)(2,1)S(1)}, u32[]{:S(2)}, u32[]{:S(2)}) collective-permute-start(bf16[128,1024]{1,0:T(8,128)(2,1)S(1)} %collective-permute-done.6.refs_6_), channel_id=1, source_target_pairs={{0,1},{1,0},{2,3},{3,2},{4,5},{5,4},{6,7},{7,6},{8,9},{9,8},{10,11... | collective-permute-start | bytes 786440 | tf_op jit(solution)/shard_map/ppermute | solution.py:133
  45.0 9.3 %collective-permute-start.5 = (bf16[128,1024]{1,0:T(8,128)(2,1)S(1)}, bf16[128,1024]{1,0:T(8,128)(2,1)S(1)}, u32[]{:S(2)}, u32[]{:S(2)}) collective-permute-start(bf16[128,1024]{1,0:T(8,128)(2,1)S(1)} %collective-permute-done.4.refs_4_), channel_id=1, source_target_pairs={{0,1},{1,0},{2,3},{3,2},{4,5},{5,4},{6,7},{7,6},{8,9},{9,8},{10,11... | collective-permute-start | bytes 786440 | tf_op jit(solution)/shard_map/ppermute | solution.py:133
  63.4 40.7 %copy-start.1 = (bf16[2,256,256]{2,1,0:T(8,128)(2,1)S(1)}, bf16[2,256,256]{2,1,0:T(8,128)(2,1)}, u32[]{:S(2)}) copy-start(bf16[2,256,256]{2,1,0:T(8,128)(2,1)} %constant.234.clone.refs_5_) | copy-start | bytes 786436
  63.4 40.7 %copy-start.2 = (bf16[2,128,256]{2,1,0:T(8,128)(2,1)S(1)}, bf16[2,128,256]{2,1,0:T(8,128)(2,1)}, u32[]{:S(2)}) copy-start(bf16[2,128,256]{2,1,0:T(8,128)(2,1)} %constant.233.clone.refs_4_) | copy-start | bytes 393220
  106.7 19.3 %all-to-all-start.2 = ((bf16[32,32,256]{2,1,0:T(8,128)(2,1)}), bf16[32,32,256]{2,1,0:T(8,128)(2,1)S(1)}, u32[]{:S(2)}, u32[]{:S(2)}) async-start(bf16[32,32,256]{2,1,0:T(8,128)(2,1)} %bitcast.22), calls=%async_computation.2 | async-start | bytes 1048576 | tf_op jit(solution)/shard_map/all_to_all | solution.py:476
  129.6 12.1 %collective-permute-start.8 = (bf16[64,2048]{1,0:T(8,128)(2,1)S(1)}, bf16[64,2048]{1,0:T(8,128)(2,1)S(1)}, u32[]{:S(2)}, u32[]{:S(2)}) collective-permute-start(bf16[64,2048]{1,0:T(8,128)(2,1)S(1)} %get-tuple-element.43), channel_id=1, source_target_pairs={{0,0},{1,16},{2,2},{3,18},{4,4},{5,20},{6,6},{7,22},{8,24},{9,8},{... | collective-permute-start | bytes 786440 | tf_op jit(solution)/shard_map/ppermute | solution.py:88
  132.2 25.9 %collective-permute-start.9 = (bf16[64,2048]{1,0:T(8,128)(2,1)S(1)}, bf16[64,2048]{1,0:T(8,128)(2,1)S(1)}, u32[]{:S(2)}, u32[]{:S(2)}) collective-permute-start(bf16[64,2048]{1,0:T(8,128)(2,1)S(1)} %get-tuple-element.44), channel_id=1, source_target_pairs={{0,8},{1,24},{2,10},{3,26},{4,12},{5,28},{6,14},{7,30},{8,16},{9,0... | collective-permute-start | bytes 786440 | tf_op jit(solution)/shard_map/ppermute | solution.py:88
  132.3 25.8 %collective-permute-start.10 = (bf16[64,2048]{1,0:T(8,128)(2,1)S(1)}, bf16[64,2048]{1,0:T(8,128)(2,1)S(1)}, u32[]{:S(2)}, u32[]{:S(2)}) collective-permute-start(bf16[64,2048]{1,0:T(8,128)(2,1)S(1)} %get-tuple-element.45), channel_id=1, source_target_pairs={{0,16},{1,0},{2,18},{3,2},{4,20},{5,4},{6,22},{7,6},{8,8},{9,24},{... | collective-permute-start | bytes 786440 | tf_op jit(solution)/shard_map/ppermute | solution.py:88
  136.2 22.0 %collective-permute-start.11 = (bf16[64,2048]{1,0:T(8,128)(2,1)S(1)}, bf16[64,2048]{1,0:T(8,128)(2,1)S(1)}, u32[]{:S(2)}, u32[]{:S(2)}) collective-permute-start(bf16[64,2048]{1,0:T(8,128)(2,1)S(1)} %get-tuple-element.46), channel_id=1, source_target_pairs={{0,24},{1,8},{2,26},{3,10},{4,28},{5,12},{6,30},{7,14},{8,0},{9,16... | collective-permute-start | bytes 786440 | tf_op jit(solution)/shard_map/ppermute | solution.py:88
Sparse Core Ops, SparseCore 0:
  8.9 48.8 all-gather.3
  59.7 51.2 all-gather.5

commit v25 on v24

--- a/solution.py
+++ b/solution.py
@@ -402,11 +402,10 @@
             ].astype(out_ref.dtype)
 
 
-def project_out(gated, weight, blocks):
+def project_out(gated, weight, blocks, part_rows):
     tp_parts, depth, rows = gated.shape
     inner_parts, _, _, width = weight.shape
     columns = inner_parts * width
-    part_rows = rows // len(blocks)
     vmem = pl.BlockSpec(memory_space=pltpu.VMEM)
     return pl.pallas_call(
         out_kernel,
@@ -418,15 +417,15 @@
         out_specs=[vmem] * len(blocks),
         scratch_shapes=[
             pltpu.VMEM((rows, depth), jnp.bfloat16),
-            pltpu.VMEM((rows, tp_parts * depth), jnp.bfloat16),
+            pltpu.VMEM((len(blocks) * part_rows, tp_parts * depth), jnp.bfloat16),
             pltpu.VMEM(weight.shape, weight.dtype),
             pltpu.SemaphoreType.DMA((inner_parts,)),
         ],
         out_shape=[jax.ShapeDtypeStruct((part_rows, columns), jnp.bfloat16)] * len(blocks),
         compiler_params=pltpu.CompilerParams(vmem_limit_bytes=52 * 2**20),
         cost_estimate=pl.CostEstimate(
-            flops=2 * gated.size * columns,
-            bytes_accessed=2 * (weight.size + gated.size + rows * columns),
+            flops=2 * tp_parts * depth * len(blocks) * part_rows * columns,
+            bytes_accessed=2 * (weight.size + gated.size + len(blocks) * part_rows * columns),
             transcendentals=0,
         ),
     )(jnp.stack(blocks).astype(jnp.int32), gated, weight)
@@ -477,7 +476,11 @@
         gated.reshape((-1,) + gated.shape[3:]), ("tp", "seq"), split_axis=0, concat_axis=0, tiled=True
     )
     blocks, places = return_places(outer, inner_parts, tp_parts)
-    pieces = project_out(gated.reshape(tp_parts, chan_tp, -1), out_weight, blocks)
+    gated = gated.reshape(tp_parts, chan_tp, -1)
+    half = (outer + 1) // 2
+    pieces = []
+    for some in (blocks[:half], blocks[half:]):
+        pieces += project_out(gated, out_weight, some, rows // tp_parts)
     return return_output(pieces, places, inner_parts, tp_parts)
 
 

time: 167 us -> 169 us (1.012)
  Pallas kernels: 13.3 us -> 15.8 us
    pallas_call x1 -> x2, Pallas kernels: 3.57 us -> 6.13 us  [project_out(): pl.pallas_call(out_kernel, in_specs=[pl.BlockSpec(memory_space=pltpu.SMEM...]
  transfers between devices with their start and end apart: 16 -> 16, of which waited for: 11 -> 12; matrix products, arithmetic and copies ran while one was open for 1% -> 1% of each run, Pallas kernels for 5% -> 5%
where the time goes in v25:
time: 169 us; the launch traced here: 168 us
  waiting for transfers between devices  63.4 us (38%)
  blocking collectives  40.7 us (24%)
  starting transfers between devices  31.8 us (19%)
  Pallas kernels  15.8 us (9%)
  between operations  13.8 us (8%)
  local copies, waits for them, and re-layouts  2.81 us (2%)
    all_to_all x1, blocking collectives, per_device(): lax.all_to_all(partial, 'seq', split_axis=0, concat_axis=0, tiled=True)  40.7 us
    ppermute x4, waiting for transfers between devices, return_output(): arrived.append(lax.ppermute(piece, ('seq', 'tp'), pairs))  19.8 us
    all_to_all x1, waiting for transfers between devices, per_device(): lax.all_to_all(gated.reshape((-1,) + gated.shape[3:]), ('tp', 'seq'), spl...  14.4 us
    ppermute x3, waiting for transfers between devices, cross_outer(): lax.ppermute(piece, 'seq', [(i, (i + far) % seq_parts) for i in range(seq...  10.5 us
    ppermute x3, starting transfers between devices, cross_outer(): lax.ppermute(piece, 'seq', [(i, (i + far) % seq_parts) for i in range(seq...  9.2 us
    ppermute x4, waiting for transfers between devices, share_over_tp(): pieces.append(lax.ppermute(part, 'tp', pairs))  8.77 us
    ppermute x4, starting transfers between devices, return_output(): arrived.append(lax.ppermute(piece, ('seq', 'tp'), pairs))  7.96 us
    all_to_all x1, starting transfers between devices, per_device(): lax.all_to_all(long_filter.T.reshape(seq_parts, chans, rows), 'seq', spli...  6.27 us
  transfers between devices with their start and end apart: 16, of which 12 were waited for; matrix products, arithmetic and copies ran while one was open for 1% of the time, Pallas kernels for 5%

profile of v25, /device:TPU:12, one launch (start us, length us, event | category | flops | bytes accessed | tf_op | source)
XLA Modules:
  0.0 168.5 jit_solution(12133883844892192605)
XLA Ops:
  9.6 6.3 %all-to-all-start = ((f32[16,32,128]{2,1,0:T(8,128)}), f32[16,32,128]{2,1,0:T(8,128)S(1)}, u32[]{:S(2)}, u32[]{:S(2)}) async-start(f32[16,32,128]{2,1,0:T(8,128)} %bitcast.14), calls=%async_computation | async-start | bytes 524288 | tf_op jit(solution)/shard_map/all_to_all | solution.py:454
  16.0 5.6 %collective-permute-done = bf16[2,128,1024]{2,1,0:T(8,128)(2,1)S(1)} collective-permute-done((bf16[2,128,1024]{2,1,0:T(8,128)(2,1)S(1)}, bf16[2,128,1024]{2,1,0:T(8,128)(2,1)S(1)}, u32[]{:S(2)}, u32[]{:S(2)}) %collective-permute-start) | collective-permute-done | bytes 524320 | tf_op jit(solution)/shard_map/ppermute | solution.py:107
  21.8 1.6 collective-permute-start.1
  26.2 3.6 %collective-permute-done.1.refs_2_ = bf16[128,1024]{1,0:T(8,128)(2,1)S(1)} collective-permute-done((bf16[128,1024]{1,0:T(8,128)(2,1)S(1)}, bf16[128,1024]{1,0:T(8,128)(2,1)S(1)}, u32[]{:S(2)}, u32[]{:S(2)}) %collective-permute-start.1) | collective-permute-done | bytes 262176 | tf_op jit(solution)/shard_map/ppermute | solution.py:124
  30.3 6.3 %collective-permute-start.4 = (bf16[128,1024]{1,0:T(8,128)(2,1)S(1)}, bf16[128,1024]{1,0:T(8,128)(2,1)S(1)}, u32[]{:S(2)}, u32[]{:S(2)}) collective-permute-start(bf16[128,1024]{1,0:T(8,128)(2,1)S(1)} %dynamic-slice_bitcast_fusion.1), channel_id=1, source_target_pairs={{0,16},{2,18},{4,20},{6,22},{8,24},{10,26},{12,28},{14,30},{16,0},... | collective-permute-start | bytes 786440 | tf_op jit(solution)/shard_map/ppermute | solution.py:124
  36.6 1.5 collective-permute-start.3
  38.1 3.4 %collective-permute-done.6.refs_6_ = bf16[128,1024]{1,0:T(8,128)(2,1)S(1)} collective-permute-done((bf16[128,1024]{1,0:T(8,128)(2,1)S(1)}, bf16[128,1024]{1,0:T(8,128)(2,1)S(1)}, u32[]{:S(2)}, u32[]{:S(2)}) %collective-permute-start.6) | collective-permute-done | bytes 262176 | tf_op jit(solution)/shard_map/ppermute | solution.py:124
  41.5 3.5 %collective-permute-done.4.refs_4_ = bf16[128,1024]{1,0:T(8,128)(2,1)S(1)} collective-permute-done((bf16[128,1024]{1,0:T(8,128)(2,1)S(1)}, bf16[128,1024]{1,0:T(8,128)(2,1)S(1)}, u32[]{:S(2)}, u32[]{:S(2)}) %collective-permute-start.4) | collective-permute-done | bytes 262176 | tf_op jit(solution)/shard_map/ppermute | solution.py:124
  46.0 4.7 %collective-permute-done.7.refs_7_ = bf16[128,1024]{1,0:T(8,128)(2,1)S(1)} collective-permute-done((bf16[128,1024]{1,0:T(8,128)(2,1)S(1)}, bf16[128,1024]{1,0:T(8,128)(2,1)S(1)}, u32[]{:S(2)}, u32[]{:S(2)}) %collective-permute-start.7) | collective-permute-done | bytes 262176 | tf_op jit(solution)/shard_map/ppermute | solution.py:133
  50.7 3.5 %collective-permute-done.5.refs_5_ = bf16[128,1024]{1,0:T(8,128)(2,1)S(1)} collective-permute-done((bf16[128,1024]{1,0:T(8,128)(2,1)S(1)}, bf16[128,1024]{1,0:T(8,128)(2,1)S(1)}, u32[]{:S(2)}, u32[]{:S(2)}) %collective-permute-start.5) | collective-permute-done | bytes 262176 | tf_op jit(solution)/shard_map/ppermute | solution.py:133
  54.3 3.6 %all-gather.4.cloned.1.call-done = bf16[3,2048,512]{2,1,0:T(8,128)(2,1)} async-done(((bf16[3,512,512]{2,1,0:T(8,128)(2,1)}), bf16[3,2048,512]{2,1,0:T(8,128)(2,1)}) %all-gather.4.cloned.1.call-update) | async-done | bytes 6291472 | tf_op jit(solution)/shard_map/all_gather | solution.py:448
  57.9 5.6 %shard_map.82 = bf16[16,3,32,512]{3,2,1,0:T(8,128)(2,1)S(1)} custom-call(s32[1]{0:T(128)} %bitcast.8.place_ref, bf16[128,1024]{1,0:T(8,128)(2,1)S(1)} %get-tuple-element.31.refs_0_, bf16[128,1024]{1,0:T(8,128)(2,1)S(1)} %collective-permute-done.2.refs_1_, bf16[128,1024]{1,0:T(8,128)(2,1)S(1)} %collective-permute-done.1.refs_2_, ...), custom_call_target="tpu_custom_call" | custom-call | flops 96636764160 | bytes 9961472 | tf_op jit(solution)/shard_map/pallas_call | solution.py:177
  63.5 40.7 %all_to_all.15.refs_0_ = bf16[16,3,32,512]{3,2,1,0:T(8,128)(2,1)S(1)} all-to-all(bf16[16,3,32,512]{3,2,1,0:T(8,128)(2,1)S(1)} %shard_map.82), channel_id=1, replica_groups=mesh['seq'=16,'tp'=2] {'seq'}, dimensions={0} | all-to-all | bytes 3145728 | tf_op jit(solution)/shard_map/all_to_all | solution.py:472
  104.1 2.6 %shard_map.83 = bf16[2,4,4,32,256]{4,3,2,1,0:T(8,128)(2,1)} custom-call(bf16[16,3,32,512]{3,2,1,0:T(8,128)(2,1)S(1)} %all_to_all.15.refs_0_, f32[16,32,128]{2,1,0:T(8,128)S(1)} %all-to-all-done.refs_1_, f32[3,3,32,128]{3,2,1,0:T(8,128)S(1)} %broadcast_in_dim.7.refs_2_, f32[32,128]{1,0:T(8,128)S(1)} %broadcast_in_dim.8.refs_3_, ...), custom_call_target="tpu_custom_call" | custom-call | flops 1000000000 | bytes 4194304 | tf_op jit(solution)/shard_map/pallas_call | solution.py:353
  106.7 4.8 %all-to-all-start.2 = ((bf16[32,32,256]{2,1,0:T(8,128)(2,1)}), bf16[32,32,256]{2,1,0:T(8,128)(2,1)S(1)}, u32[]{:S(2)}, u32[]{:S(2)}) async-start(bf16[32,32,256]{2,1,0:T(8,128)(2,1)} %bitcast.20), calls=%async_computation.2 | async-start | bytes 1048576 | tf_op jit(solution)/shard_map/all_to_all | solution.py:475
  111.7 14.4 %all-to-all-done.2 = bf16[32,32,256]{2,1,0:T(8,128)(2,1)S(1)} async-done(((bf16[32,32,256]{2,1,0:T(8,128)(2,1)}), bf16[32,32,256]{2,1,0:T(8,128)(2,1)S(1)}, u32[]{:S(2)}, u32[]{:S(2)}) %all-to-all-start.2) | async-done | bytes 524320 | tf_op jit(solution)/shard_map/all_to_all | solution.py:475
  126.1 3.1 %shard_map.85 = (bf16[64,2048]{1,0:T(8,128)(2,1)S(1)}, bf16[64,2048]{1,0:T(8,128)(2,1)S(1)}) custom-call(s32[2]{0:T(128)S(1)} %get-tuple-element.54.block_ref, bf16[2,512,256]{2,1,0:T(8,128)(2,1)S(1)} %bitcast.33, bf16[4,2,512,512]{3,2,1,0:T(8,128)(2,1)} %bitcast.35), custom_call_target="tpu_custom_call" | custom-call | flops 536870912 | bytes 5242880 | tf_op jit(solution)/shard_map/pallas_call | solution.py:410
  129.1 3.1 %shard_map.84 = (bf16[64,2048]{1,0:T(8,128)(2,1)S(1)}, bf16[64,2048]{1,0:T(8,128)(2,1)S(1)}) custom-call(s32[2]{0:T(128)S(1)} %get-tuple-element.53.block_ref, bf16[2,512,256]{2,1,0:T(8,128)(2,1)S(1)} %bitcast.34, bf16[4,2,512,512]{3,2,1,0:T(8,128)(2,1)} %bitcast.36), custom_call_target="tpu_custom_call" | custom-call | flops 536870912 | bytes 5242880 | tf_op jit(solution)/shard_map/pallas_call | solution.py:410
  132.2 4.0 %collective-permute-start.10 = (bf16[64,2048]{1,0:T(8,128)(2,1)S(1)}, bf16[64,2048]{1,0:T(8,128)(2,1)S(1)}, u32[]{:S(2)}, u32[]{:S(2)}) collective-permute-start(bf16[64,2048]{1,0:T(8,128)(2,1)S(1)} %get-tuple-element.45), channel_id=1, source_target_pairs={{0,16},{1,0},{2,18},{3,2},{4,20},{5,4},{6,22},{7,6},{8,8},{9,24},{... | collective-permute-start | bytes 786440 | tf_op jit(solution)/shard_map/ppermute | solution.py:88
  136.3 2.5 %collective-permute-start.8 = (bf16[64,2048]{1,0:T(8,128)(2,1)S(1)}, bf16[64,2048]{1,0:T(8,128)(2,1)S(1)}, u32[]{:S(2)}, u32[]{:S(2)}) collective-permute-start(bf16[64,2048]{1,0:T(8,128)(2,1)S(1)} %get-tuple-element.43), channel_id=1, source_target_pairs={{0,0},{1,16},{2,2},{3,18},{4,4},{5,20},{6,6},{7,22},{8,24},{9,8},{... | collective-permute-start | bytes 786440 | tf_op jit(solution)/shard_map/ppermute | solution.py:88
  138.8 1.4 collective-permute-start.9
  140.3 13.9 %collective-permute-done.10.refs_2_ = bf16[64,2048]{1,0:T(8,128)(2,1)S(1)} collective-permute-done((bf16[64,2048]{1,0:T(8,128)(2,1)S(1)}, bf16[64,2048]{1,0:T(8,128)(2,1)S(1)}, u32[]{:S(2)}, u32[]{:S(2)}) %collective-permute-start.10) | collective-permute-done | bytes 262176 | tf_op jit(solution)/shard_map/ppermute | solution.py:88
  154.2 5.6 %collective-permute-done.11.refs_3_ = bf16[64,2048]{1,0:T(8,128)(2,1)S(1)} collective-permute-done((bf16[64,2048]{1,0:T(8,128)(2,1)S(1)}, bf16[64,2048]{1,0:T(8,128)(2,1)S(1)}, u32[]{:S(2)}, u32[]{:S(2)}) %collective-permute-start.11) | collective-permute-done | bytes 262176 | tf_op jit(solution)/shard_map/ppermute | solution.py:88
  160.1 1.5 shard_map.86
  (39 shorter events, 8.0 us)
Async XLA Ops:
  6.5 18.1 %copy-start = (f32[3,3,512]{2,1,0:T(4,128)S(1)}, f32[3,3,512]{2,1,0:T(4,128)}, u32[]{:S(2)}) copy-start(f32[3,3,512]{2,1,0:T(4,128)} %param.10) | copy-start | bytes 55300
  6.5 1.2 copy-start.3
  6.5 51.3 %all-gather.4.cloned.1.call-start = ((), (), s32[]{:S(2)}) async-start(), calls=%async_computation.3 | async-start | bytes 7864320 | tf_op jit(solution)/shard_map/all_gather | solution.py:448
  7.8 0.9 copy-start.4
  7.9 13.7 %collective-permute-start = (bf16[2,128,1024]{2,1,0:T(8,128)(2,1)S(1)}, bf16[2,128,1024]{2,1,0:T(8,128)(2,1)S(1)}, u32[]{:S(2)}, u32[]{:S(2)}) collective-permute-start(bf16[2,128,1024]{2,1,0:T(8,128)(2,1)S(1)} %pad_maximum_fusion.1), channel_id=1, source_target_pairs={{0,1},{1,0},{2,3},{3,2},{4,5},{5,4},{6,7},{7,6},{8,9},{9,8},{10,11... | collective-permute-start | bytes 1572872 | tf_op jit(solution)/shard_map/ppermute | solution.py:107
  9.6 15.2 %all-to-all-start = ((f32[16,32,128]{2,1,0:T(8,128)}), f32[16,32,128]{2,1,0:T(8,128)S(1)}, u32[]{:S(2)}, u32[]{:S(2)}) async-start(f32[16,32,128]{2,1,0:T(8,128)} %bitcast.14), calls=%async_computation | async-start | bytes 524288 | tf_op jit(solution)/shard_map/all_to_all | solution.py:454
  15.8 95.8 %all-gather.6.cloned.1.call-start = ((), (), s32[]{:S(2)}) async-start(), calls=%async_computation.4 | async-start | bytes 4718592 | tf_op jit(solution)/shard_map/all_gather | solution.py:468
  21.8 8.0 %collective-permute-start.1 = (bf16[128,1024]{1,0:T(8,128)(2,1)S(1)}, bf16[128,1024]{1,0:T(8,128)(2,1)S(1)}, u32[]{:S(2)}, u32[]{:S(2)}) collective-permute-start(bf16[128,1024]{1,0:T(8,128)(2,1)S(1)} %get-tuple-element.48), channel_id=1, source_target_pairs={{0,8},{2,10},{4,12},{6,14},{8,16},{10,18},{12,20},{14,22},{16,24},... | collective-permute-start | bytes 786440 | tf_op jit(solution)/shard_map/ppermute | solution.py:124
  23.4 6.9 %collective-permute-start.2 = (bf16[128,1024]{1,0:T(8,128)(2,1)S(1)}, bf16[128,1024]{1,0:T(8,128)(2,1)S(1)}, u32[]{:S(2)}, u32[]{:S(2)}) collective-permute-start(bf16[128,1024]{1,0:T(8,128)(2,1)S(1)} %get-tuple-element.31.refs_0_), channel_id=1, source_target_pairs={{0,1},{1,0},{2,3},{3,2},{4,5},{5,4},{6,7},{7,6},{8,9},{9,8},{10,11... | collective-permute-start | bytes 786440 | tf_op jit(solution)/shard_map/ppermute | solution.py:133
  25.0 16.5 %collective-permute-start.6 = (bf16[128,1024]{1,0:T(8,128)(2,1)S(1)}, bf16[128,1024]{1,0:T(8,128)(2,1)S(1)}, u32[]{:S(2)}, u32[]{:S(2)}) collective-permute-start(bf16[128,1024]{1,0:T(8,128)(2,1)S(1)} %dynamic-slice_bitcast_fusion), channel_id=1, source_target_pairs={{0,24},{2,26},{4,28},{6,30},{8,0},{10,2},{12,4},{14,6},{16,8},{18,... | collective-permute-start | bytes 786440 | tf_op jit(solution)/shard_map/ppermute | solution.py:124
  30.3 14.6 %collective-permute-start.4 = (bf16[128,1024]{1,0:T(8,128)(2,1)S(1)}, bf16[128,1024]{1,0:T(8,128)(2,1)S(1)}, u32[]{:S(2)}, u32[]{:S(2)}) collective-permute-start(bf16[128,1024]{1,0:T(8,128)(2,1)S(1)} %dynamic-slice_bitcast_fusion.1), channel_id=1, source_target_pairs={{0,16},{2,18},{4,20},{6,22},{8,24},{10,26},{12,28},{14,30},{16,0},... | collective-permute-start | bytes 786440 | tf_op jit(solution)/shard_map/ppermute | solution.py:124
  36.6 14.1 %collective-permute-start.3 = (bf16[128,1024]{1,0:T(8,128)(2,1)S(1)}, bf16[128,1024]{1,0:T(8,128)(2,1)S(1)}, u32[]{:S(2)}, u32[]{:S(2)}) collective-permute-start(bf16[128,1024]{1,0:T(8,128)(2,1)S(1)} %collective-permute-done.1.refs_2_), channel_id=1, source_target_pairs={{0,1},{1,0},{2,3},{3,2},{4,5},{5,4},{6,7},{7,6},{8,9},{9,8},{10,11... | collective-permute-start | bytes 786440 | tf_op jit(solution)/shard_map/ppermute | solution.py:133
  41.5 9.2 %collective-permute-start.7 = (bf16[128,1024]{1,0:T(8,128)(2,1)S(1)}, bf16[128,1024]{1,0:T(8,128)(2,1)S(1)}, u32[]{:S(2)}, u32[]{:S(2)}) collective-permute-start(bf16[128,1024]{1,0:T(8,128)(2,1)S(1)} %collective-permute-done.6.refs_6_), channel_id=1, source_target_pairs={{0,1},{1,0},{2,3},{3,2},{4,5},{5,4},{6,7},{7,6},{8,9},{9,8},{10,11... | collective-permute-start | bytes 786440 | tf_op jit(solution)/shard_map/ppermute | solution.py:133
  45.0 9.3 %collective-permute-start.5 = (bf16[128,1024]{1,0:T(8,128)(2,1)S(1)}, bf16[128,1024]{1,0:T(8,128)(2,1)S(1)}, u32[]{:S(2)}, u32[]{:S(2)}) collective-permute-start(bf16[128,1024]{1,0:T(8,128)(2,1)S(1)} %collective-permute-done.4.refs_4_), channel_id=1, source_target_pairs={{0,1},{1,0},{2,3},{3,2},{4,5},{5,4},{6,7},{7,6},{8,9},{9,8},{10,11... | collective-permute-start | bytes 786440 | tf_op jit(solution)/shard_map/ppermute | solution.py:133
  63.4 40.7 %copy-start.1 = (bf16[2,256,256]{2,1,0:T(8,128)(2,1)S(1)}, bf16[2,256,256]{2,1,0:T(8,128)(2,1)}, u32[]{:S(2)}) copy-start(bf16[2,256,256]{2,1,0:T(8,128)(2,1)} %constant.234.clone.refs_5_) | copy-start | bytes 786436
  63.4 40.7 %copy-start.2 = (bf16[2,128,256]{2,1,0:T(8,128)(2,1)S(1)}, bf16[2,128,256]{2,1,0:T(8,128)(2,1)}, u32[]{:S(2)}) copy-start(bf16[2,128,256]{2,1,0:T(8,128)(2,1)} %constant.233.clone.refs_4_) | copy-start | bytes 393220
  106.7 19.3 %all-to-all-start.2 = ((bf16[32,32,256]{2,1,0:T(8,128)(2,1)}), bf16[32,32,256]{2,1,0:T(8,128)(2,1)S(1)}, u32[]{:S(2)}, u32[]{:S(2)}) async-start(bf16[32,32,256]{2,1,0:T(8,128)(2,1)} %bitcast.20), calls=%async_computation.2 | async-start | bytes 1048576 | tf_op jit(solution)/shard_map/all_to_all | solution.py:475
  132.2 22.0 %collective-permute-start.10 = (bf16[64,2048]{1,0:T(8,128)(2,1)S(1)}, bf16[64,2048]{1,0:T(8,128)(2,1)S(1)}, u32[]{:S(2)}, u32[]{:S(2)}) collective-permute-start(bf16[64,2048]{1,0:T(8,128)(2,1)S(1)} %get-tuple-element.45), channel_id=1, source_target_pairs={{0,16},{1,0},{2,18},{3,2},{4,20},{5,4},{6,22},{7,6},{8,8},{9,24},{... | collective-permute-start | bytes 786440 | tf_op jit(solution)/shard_map/ppermute | solution.py:88
  136.2 23.6 %collective-permute-start.11 = (bf16[64,2048]{1,0:T(8,128)(2,1)S(1)}, bf16[64,2048]{1,0:T(8,128)(2,1)S(1)}, u32[]{:S(2)}, u32[]{:S(2)}) collective-permute-start(bf16[64,2048]{1,0:T(8,128)(2,1)S(1)} %get-tuple-element.46), channel_id=1, source_target_pairs={{0,24},{1,8},{2,26},{3,10},{4,28},{5,12},{6,30},{7,14},{8,0},{9,16... | collective-permute-start | bytes 786440 | tf_op jit(solution)/shard_map/ppermute | solution.py:88
  136.3 23.5 %collective-permute-start.8 = (bf16[64,2048]{1,0:T(8,128)(2,1)S(1)}, bf16[64,2048]{1,0:T(8,128)(2,1)S(1)}, u32[]{:S(2)}, u32[]{:S(2)}) collective-permute-start(bf16[64,2048]{1,0:T(8,128)(2,1)S(1)} %get-tuple-element.43), channel_id=1, source_target_pairs={{0,0},{1,16},{2,2},{3,18},{4,4},{5,20},{6,6},{7,22},{8,24},{9,8},{... | collective-permute-start | bytes 786440 | tf_op jit(solution)/shard_map/ppermute | solution.py:88
  138.8 21.3 %collective-permute-start.9 = (bf16[64,2048]{1,0:T(8,128)(2,1)S(1)}, bf16[64,2048]{1,0:T(8,128)(2,1)S(1)}, u32[]{:S(2)}, u32[]{:S(2)}) collective-permute-start(bf16[64,2048]{1,0:T(8,128)(2,1)S(1)} %get-tuple-element.44), channel_id=1, source_target_pairs={{0,8},{1,24},{2,10},{3,26},{4,12},{5,28},{6,14},{7,30},{8,16},{9,0... | collective-permute-start | bytes 786440 | tf_op jit(solution)/shard_map/ppermute | solution.py:88
Sparse Core Ops, SparseCore 0:
  8.9 48.8 all-gather.3
  59.7 51.2 all-gather.5

commit v26 on v24

--- a/solution.py
+++ b/solution.py
@@ -458,11 +458,13 @@
 
     held = share_columns(features, outer, tp_parts)
     arrived = cross_outer(held, (0, 1), outer, inner_parts, tp_parts)
-    held, taps, skip, filter_blocks = lax.optimization_barrier((held, taps, skip, filter_blocks))
+    held, taps, skip = lax.optimization_barrier((held, taps, skip))
     if outer > 2:
         arrived |= cross_outer(held, (outer - 1,), outer, inner_parts, tp_parts)
     own = share_over_tp(arrived[0], tp_parts)
-    held, arrived[1], own = lax.optimization_barrier((held, arrived[1], own))
+    held, arrived[1], own, filter_blocks = lax.optimization_barrier(
+        (held, arrived[1], own, filter_blocks)
+    )
     arrived |= cross_outer(held, range(2, outer - 1), outer, inner_parts, tp_parts)
     chunks = [own] + [share_over_tp(arrived[step], tp_parts) for step in range(1, outer)]
     chunks, out_proj = lax.optimization_barrier((chunks, out_proj))

time: 167 us -> 167 us (level)
    ppermute x3, starting transfers between devices: 9.2 us -> 6.38 us  [cross_outer(): lax.ppermute(piece, 'seq', [(i, (i + far) % seq_parts) for i in range(seq...]
    ppermute x3, waiting for transfers between devices: 10.5 us -> 12.4 us  [cross_outer(): lax.ppermute(piece, 'seq', [(i, (i + far) % seq_parts) for i in range(seq...]
  transfers between devices with their start and end apart: 16 -> 16, of which waited for: 11 -> 10; matrix products, arithmetic and copies ran while one was open for 1% -> 1% of each run, Pallas kernels for 5% -> 5%
where the time goes in v26:
time: 167 us
  waiting for transfers between devices  64.6 us (39%)
  blocking collectives  40.7 us (24%)
  starting transfers between devices  31.1 us (19%)
  between operations  13.8 us (8%)
  Pallas kernels  13.3 us (8%)
  local copies, waits for them, and re-layouts  2.81 us (2%)
    all_to_all x1, blocking collectives, per_device(): lax.all_to_all(partial, 'seq', split_axis=0, concat_axis=0, tiled=True)  40.7 us
    ppermute x4, waiting for transfers between devices, return_output(): arrived.append(lax.ppermute(piece, ('seq', 'tp'), pairs))  19.5 us
    all_to_all x1, waiting for transfers between devices, per_device(): lax.all_to_all(gated.reshape((-1,) + gated.shape[3:]), ('tp', 'seq'), spl...  14.4 us
    ppermute x3, waiting for transfers between devices, cross_outer(): lax.ppermute(piece, 'seq', [(i, (i + far) % seq_parts) for i in range(seq...  12.4 us
    ppermute x4, starting transfers between devices, return_output(): arrived.append(lax.ppermute(piece, ('seq', 'tp'), pairs))  8.85 us
    ppermute x4, waiting for transfers between devices, share_over_tp(): pieces.append(lax.ppermute(part, 'tp', pairs))  7.57 us
    ppermute x3, starting transfers between devices, cross_outer(): lax.ppermute(piece, 'seq', [(i, (i + far) % seq_parts) for i in range(seq...  6.38 us
    all_to_all x1, starting transfers between devices, per_device(): lax.all_to_all(long_filter.T.reshape(seq_parts, chans, rows), 'seq', spli...  6.27 us
  transfers between devices with their start and end apart: 16, of which 10 were waited for; matrix products, arithmetic and copies ran while one was open for 1% of the time, Pallas kernels for 5%

profile of v26, /device:TPU:12, one launch (start us, length us, event | category | flops | bytes accessed | tf_op | source)
XLA Modules:
  0.0 166.5 jit_solution(5608048785473069039)
XLA Ops:
  9.6 6.3 %all-to-all-start = ((f32[16,32,128]{2,1,0:T(8,128)}), f32[16,32,128]{2,1,0:T(8,128)S(1)}, u32[]{:S(2)}, u32[]{:S(2)}) async-start(f32[16,32,128]{2,1,0:T(8,128)} %bitcast.18), calls=%async_computation | async-start | bytes 524288 | tf_op jit(solution)/shard_map/all_to_all | solution.py:455
  16.0 5.6 %collective-permute-done = bf16[2,128,1024]{2,1,0:T(8,128)(2,1)S(1)} collective-permute-done((bf16[2,128,1024]{2,1,0:T(8,128)(2,1)S(1)}, bf16[2,128,1024]{2,1,0:T(8,128)(2,1)S(1)}, u32[]{:S(2)}, u32[]{:S(2)}) %collective-permute-start) | collective-permute-done | bytes 524320 | tf_op jit(solution)/shard_map/ppermute | solution.py:107
  21.8 1.6 collective-permute-start.1
  25.5 5.6 %collective-permute-done.1.refs_2_ = bf16[128,1024]{1,0:T(8,128)(2,1)S(1)} collective-permute-done((bf16[128,1024]{1,0:T(8,128)(2,1)S(1)}, bf16[128,1024]{1,0:T(8,128)(2,1)S(1)}, u32[]{:S(2)}, u32[]{:S(2)}) %collective-permute-start.1) | collective-permute-done | bytes 262176 | tf_op jit(solution)/shard_map/ppermute | solution.py:124
  31.1 4.3 %collective-permute-start.4 = (bf16[128,1024]{1,0:T(8,128)(2,1)S(1)}, bf16[128,1024]{1,0:T(8,128)(2,1)S(1)}, u32[]{:S(2)}, u32[]{:S(2)}) collective-permute-start(bf16[128,1024]{1,0:T(8,128)(2,1)S(1)} %dynamic-slice_bitcast_fusion.1), channel_id=1, source_target_pairs={{0,16},{2,18},{4,20},{6,22},{8,24},{10,26},{12,28},{14,30},{16,0},... | collective-permute-start | bytes 786440 | tf_op jit(solution)/shard_map/ppermute | solution.py:124
  35.4 2.7 %collective-permute-start.3 = (bf16[128,1024]{1,0:T(8,128)(2,1)S(1)}, bf16[128,1024]{1,0:T(8,128)(2,1)S(1)}, u32[]{:S(2)}, u32[]{:S(2)}) collective-permute-start(bf16[128,1024]{1,0:T(8,128)(2,1)S(1)} %collective-permute-done.1.refs_2_), channel_id=1, source_target_pairs={{0,1},{1,0},{2,3},{3,2},{4,5},{5,4},{6,7},{7,6},{8,9},{9,8},{10,11... | collective-permute-start | bytes 786440 | tf_op jit(solution)/shard_map/ppermute | solution.py:133
  38.1 3.5 %collective-permute-done.6.refs_6_ = bf16[128,1024]{1,0:T(8,128)(2,1)S(1)} collective-permute-done((bf16[128,1024]{1,0:T(8,128)(2,1)S(1)}, bf16[128,1024]{1,0:T(8,128)(2,1)S(1)}, u32[]{:S(2)}, u32[]{:S(2)}) %collective-permute-start.6) | collective-permute-done | bytes 262176 | tf_op jit(solution)/shard_map/ppermute | solution.py:124
  41.6 3.4 %collective-permute-done.4.refs_4_ = bf16[128,1024]{1,0:T(8,128)(2,1)S(1)} collective-permute-done((bf16[128,1024]{1,0:T(8,128)(2,1)S(1)}, bf16[128,1024]{1,0:T(8,128)(2,1)S(1)}, u32[]{:S(2)}, u32[]{:S(2)}) %collective-permute-start.4) | collective-permute-done | bytes 262176 | tf_op jit(solution)/shard_map/ppermute | solution.py:124
  44.9 1.1 collective-permute-start.5
  46.0 2.1 %collective-permute-done.7.refs_7_ = bf16[128,1024]{1,0:T(8,128)(2,1)S(1)} collective-permute-done((bf16[128,1024]{1,0:T(8,128)(2,1)S(1)}, bf16[128,1024]{1,0:T(8,128)(2,1)S(1)}, u32[]{:S(2)}, u32[]{:S(2)}) %collective-permute-start.7) | collective-permute-done | bytes 262176 | tf_op jit(solution)/shard_map/ppermute | solution.py:133
  48.1 5.5 %collective-permute-done.5.refs_5_ = bf16[128,1024]{1,0:T(8,128)(2,1)S(1)} collective-permute-done((bf16[128,1024]{1,0:T(8,128)(2,1)S(1)}, bf16[128,1024]{1,0:T(8,128)(2,1)S(1)}, u32[]{:S(2)}, u32[]{:S(2)}) %collective-permute-start.5) | collective-permute-done | bytes 262176 | tf_op jit(solution)/shard_map/ppermute | solution.py:133
  53.6 4.3 %all-gather.4.cloned.1.call-done = bf16[3,2048,512]{2,1,0:T(8,128)(2,1)} async-done(((bf16[3,512,512]{2,1,0:T(8,128)(2,1)}), bf16[3,2048,512]{2,1,0:T(8,128)(2,1)}) %all-gather.4.cloned.1.call-update) | async-done | bytes 6291472 | tf_op jit(solution)/shard_map/all_gather | solution.py:449
  57.9 5.6 %shard_map.82 = bf16[16,3,32,512]{3,2,1,0:T(8,128)(2,1)S(1)} custom-call(s32[1]{0:T(128)} %bitcast.10.place_ref, bf16[128,1024]{1,0:T(8,128)(2,1)S(1)} %get-tuple-element.31.refs_0_, bf16[128,1024]{1,0:T(8,128)(2,1)S(1)} %collective-permute-done.2.refs_1_, bf16[128,1024]{1,0:T(8,128)(2,1)S(1)} %collective-permute-done.1.refs_2_, ...), custom_call_target="tpu_custom_call" | custom-call | flops 96636764160 | bytes 9961472 | tf_op jit(solution)/shard_map/pallas_call | solution.py:177
  63.5 40.7 %all_to_all.15.refs_0_ = bf16[16,3,32,512]{3,2,1,0:T(8,128)(2,1)S(1)} all-to-all(bf16[16,3,32,512]{3,2,1,0:T(8,128)(2,1)S(1)} %shard_map.82), channel_id=1, replica_groups=mesh['seq'=16,'tp'=2] {'seq'}, dimensions={0} | all-to-all | bytes 3145728 | tf_op jit(solution)/shard_map/all_to_all | solution.py:475
  104.1 2.6 %shard_map.83 = bf16[2,4,4,32,256]{4,3,2,1,0:T(8,128)(2,1)} custom-call(bf16[16,3,32,512]{3,2,1,0:T(8,128)(2,1)S(1)} %all_to_all.15.refs_0_, f32[16,32,128]{2,1,0:T(8,128)S(1)} %all-to-all-done.refs_1_, f32[3,3,32,128]{3,2,1,0:T(8,128)S(1)} %broadcast_in_dim.7.refs_2_, f32[32,128]{1,0:T(8,128)S(1)} %broadcast_in_dim.8.refs_3_, ...), custom_call_target="tpu_custom_call" | custom-call | flops 1000000000 | bytes 4194304 | tf_op jit(solution)/shard_map/pallas_call | solution.py:353
  106.7 4.8 %all-to-all-start.2 = ((bf16[32,32,256]{2,1,0:T(8,128)(2,1)}), bf16[32,32,256]{2,1,0:T(8,128)(2,1)S(1)}, u32[]{:S(2)}, u32[]{:S(2)}) async-start(bf16[32,32,256]{2,1,0:T(8,128)(2,1)} %bitcast.22), calls=%async_computation.2 | async-start | bytes 1048576 | tf_op jit(solution)/shard_map/all_to_all | solution.py:478
  111.7 14.4 %all-to-all-done.2 = bf16[32,32,256]{2,1,0:T(8,128)(2,1)S(1)} async-done(((bf16[32,32,256]{2,1,0:T(8,128)(2,1)}), bf16[32,32,256]{2,1,0:T(8,128)(2,1)S(1)}, u32[]{:S(2)}, u32[]{:S(2)}) %all-to-all-start.2) | async-done | bytes 524320 | tf_op jit(solution)/shard_map/all_to_all | solution.py:478
  126.1 3.6 %shard_map.84 = (bf16[64,2048]{1,0:T(8,128)(2,1)S(1)}, bf16[64,2048]{1,0:T(8,128)(2,1)S(1)}, bf16[64,2048]{1,0:T(8,128)(2,1)S(1)}, bf16[64,2048]{1,0:T(8,128)(2,1)S(1)}) custom-call(s32[4]{0:T(128)S(1)} %pad_add_fusion.block_ref, bf16[2,512,256]{2,1,0:T(8,128)(2,1)S(1)} %bitcast.33, bf16[4,2,512,512]{3,2,1,0:T(8,128)(2,1)} %bitcast.34), custom_call_target="tpu_custom_call" | custom-call | flops 1073741824 | bytes 5767168 | tf_op jit(solution)/shard_map/pallas_call | solution.py:411
  129.6 2.6 %collective-permute-start.8 = (bf16[64,2048]{1,0:T(8,128)(2,1)S(1)}, bf16[64,2048]{1,0:T(8,128)(2,1)S(1)}, u32[]{:S(2)}, u32[]{:S(2)}) collective-permute-start(bf16[64,2048]{1,0:T(8,128)(2,1)S(1)} %get-tuple-element.43), channel_id=1, source_target_pairs={{0,0},{1,16},{2,2},{3,18},{4,4},{5,20},{6,6},{7,22},{8,24},{9,8},{... | collective-permute-start | bytes 786440 | tf_op jit(solution)/shard_map/ppermute | solution.py:88
  132.3 3.9 %collective-permute-start.10 = (bf16[64,2048]{1,0:T(8,128)(2,1)S(1)}, bf16[64,2048]{1,0:T(8,128)(2,1)S(1)}, u32[]{:S(2)}, u32[]{:S(2)}) collective-permute-start(bf16[64,2048]{1,0:T(8,128)(2,1)S(1)} %get-tuple-element.45), channel_id=1, source_target_pairs={{0,16},{1,0},{2,18},{3,2},{4,20},{5,4},{6,22},{7,6},{8,8},{9,24},{... | collective-permute-start | bytes 786440 | tf_op jit(solution)/shard_map/ppermute | solution.py:88
  136.2 2.3 %collective-permute-start.11 = (bf16[64,2048]{1,0:T(8,128)(2,1)S(1)}, bf16[64,2048]{1,0:T(8,128)(2,1)S(1)}, u32[]{:S(2)}, u32[]{:S(2)}) collective-permute-start(bf16[64,2048]{1,0:T(8,128)(2,1)S(1)} %get-tuple-element.46), channel_id=1, source_target_pairs={{0,24},{1,8},{2,26},{3,10},{4,28},{5,12},{6,30},{7,14},{8,0},{9,16... | collective-permute-start | bytes 786440 | tf_op jit(solution)/shard_map/ppermute | solution.py:88
  138.6 3.2 %collective-permute-done.8.refs_0_ = bf16[64,2048]{1,0:T(8,128)(2,1)S(1)} collective-permute-done((bf16[64,2048]{1,0:T(8,128)(2,1)S(1)}, bf16[64,2048]{1,0:T(8,128)(2,1)S(1)}, u32[]{:S(2)}, u32[]{:S(2)}) %collective-permute-start.8) | collective-permute-done | bytes 262176 | tf_op jit(solution)/shard_map/ppermute | solution.py:88
  141.8 16.4 %collective-permute-done.9.refs_1_ = bf16[64,2048]{1,0:T(8,128)(2,1)S(1)} collective-permute-done((bf16[64,2048]{1,0:T(8,128)(2,1)S(1)}, bf16[64,2048]{1,0:T(8,128)(2,1)S(1)}, u32[]{:S(2)}, u32[]{:S(2)}) %collective-permute-start.9) | collective-permute-done | bytes 262176 | tf_op jit(solution)/shard_map/ppermute | solution.py:88
  158.1 1.5 shard_map.85
  (38 shorter events, 5.5 us)
Async XLA Ops:
  6.5 18.1 %copy-start = (f32[3,3,512]{2,1,0:T(4,128)S(1)}, f32[3,3,512]{2,1,0:T(4,128)}, u32[]{:S(2)}) copy-start(f32[3,3,512]{2,1,0:T(4,128)} %param.10) | copy-start | bytes 55300
  6.5 1.2 copy-start.3
  6.5 51.3 %all-gather.4.cloned.1.call-start = ((), (), s32[]{:S(2)}) async-start(), calls=%async_computation.3 | async-start | bytes 7864320 | tf_op jit(solution)/shard_map/all_gather | solution.py:449
  7.8 0.9 copy-start.4
  7.9 13.7 %collective-permute-start = (bf16[2,128,1024]{2,1,0:T(8,128)(2,1)S(1)}, bf16[2,128,1024]{2,1,0:T(8,128)(2,1)S(1)}, u32[]{:S(2)}, u32[]{:S(2)}) collective-permute-start(bf16[2,128,1024]{2,1,0:T(8,128)(2,1)S(1)} %pad_maximum_fusion.1), channel_id=1, source_target_pairs={{0,1},{1,0},{2,3},{3,2},{4,5},{5,4},{6,7},{7,6},{8,9},{9,8},{10,11... | collective-permute-start | bytes 1572872 | tf_op jit(solution)/shard_map/ppermute | solution.py:107
  9.6 15.9 %all-to-all-start = ((f32[16,32,128]{2,1,0:T(8,128)}), f32[16,32,128]{2,1,0:T(8,128)S(1)}, u32[]{:S(2)}, u32[]{:S(2)}) async-start(f32[16,32,128]{2,1,0:T(8,128)} %bitcast.18), calls=%async_computation | async-start | bytes 524288 | tf_op jit(solution)/shard_map/all_to_all | solution.py:455
  15.8 95.8 %all-gather.6.cloned.1.call-start = ((), (), s32[]{:S(2)}) async-start(), calls=%async_computation.4 | async-start | bytes 4718592 | tf_op jit(solution)/shard_map/all_gather | solution.py:471
  21.8 9.3 %collective-permute-start.1 = (bf16[128,1024]{1,0:T(8,128)(2,1)S(1)}, bf16[128,1024]{1,0:T(8,128)(2,1)S(1)}, u32[]{:S(2)}, u32[]{:S(2)}) collective-permute-start(bf16[128,1024]{1,0:T(8,128)(2,1)S(1)} %get-tuple-element.48), channel_id=1, source_target_pairs={{0,8},{2,10},{4,12},{6,14},{8,16},{10,18},{12,20},{14,22},{16,24},... | collective-permute-start | bytes 786440 | tf_op jit(solution)/shard_map/ppermute | solution.py:124
  23.4 7.7 %collective-permute-start.2 = (bf16[128,1024]{1,0:T(8,128)(2,1)S(1)}, bf16[128,1024]{1,0:T(8,128)(2,1)S(1)}, u32[]{:S(2)}, u32[]{:S(2)}) collective-permute-start(bf16[128,1024]{1,0:T(8,128)(2,1)S(1)} %get-tuple-element.31.refs_0_), channel_id=1, source_target_pairs={{0,1},{1,0},{2,3},{3,2},{4,5},{5,4},{6,7},{7,6},{8,9},{9,8},{10,11... | collective-permute-start | bytes 786440 | tf_op jit(solution)/shard_map/ppermute | solution.py:133
  25.0 16.6 %collective-permute-start.6 = (bf16[128,1024]{1,0:T(8,128)(2,1)S(1)}, bf16[128,1024]{1,0:T(8,128)(2,1)S(1)}, u32[]{:S(2)}, u32[]{:S(2)}) collective-permute-start(bf16[128,1024]{1,0:T(8,128)(2,1)S(1)} %dynamic-slice_bitcast_fusion), channel_id=1, source_target_pairs={{0,24},{2,26},{4,28},{6,30},{8,0},{10,2},{12,4},{14,6},{16,8},{18,... | collective-permute-start | bytes 786440 | tf_op jit(solution)/shard_map/ppermute | solution.py:124
  31.1 13.8 %collective-permute-start.4 = (bf16[128,1024]{1,0:T(8,128)(2,1)S(1)}, bf16[128,1024]{1,0:T(8,128)(2,1)S(1)}, u32[]{:S(2)}, u32[]{:S(2)}) collective-permute-start(bf16[128,1024]{1,0:T(8,128)(2,1)S(1)} %dynamic-slice_bitcast_fusion.1), channel_id=1, source_target_pairs={{0,16},{2,18},{4,20},{6,22},{8,24},{10,26},{12,28},{14,30},{16,0},... | collective-permute-start | bytes 786440 | tf_op jit(solution)/shard_map/ppermute | solution.py:124
  35.4 12.7 %collective-permute-start.3 = (bf16[128,1024]{1,0:T(8,128)(2,1)S(1)}, bf16[128,1024]{1,0:T(8,128)(2,1)S(1)}, u32[]{:S(2)}, u32[]{:S(2)}) collective-permute-start(bf16[128,1024]{1,0:T(8,128)(2,1)S(1)} %collective-permute-done.1.refs_2_), channel_id=1, source_target_pairs={{0,1},{1,0},{2,3},{3,2},{4,5},{5,4},{6,7},{7,6},{8,9},{9,8},{10,11... | collective-permute-start | bytes 786440 | tf_op jit(solution)/shard_map/ppermute | solution.py:133
  41.5 6.5 %collective-permute-start.7 = (bf16[128,1024]{1,0:T(8,128)(2,1)S(1)}, bf16[128,1024]{1,0:T(8,128)(2,1)S(1)}, u32[]{:S(2)}, u32[]{:S(2)}) collective-permute-start(bf16[128,1024]{1,0:T(8,128)(2,1)S(1)} %collective-permute-done.6.refs_6_), channel_id=1, source_target_pairs={{0,1},{1,0},{2,3},{3,2},{4,5},{5,4},{6,7},{7,6},{8,9},{9,8},{10,11... | collective-permute-start | bytes 786440 | tf_op jit(solution)/shard_map/ppermute | solution.py:133
  44.9 8.6 %collective-permute-start.5 = (bf16[128,1024]{1,0:T(8,128)(2,1)S(1)}, bf16[128,1024]{1,0:T(8,128)(2,1)S(1)}, u32[]{:S(2)}, u32[]{:S(2)}) collective-permute-start(bf16[128,1024]{1,0:T(8,128)(2,1)S(1)} %collective-permute-done.4.refs_4_), channel_id=1, source_target_pairs={{0,1},{1,0},{2,3},{3,2},{4,5},{5,4},{6,7},{7,6},{8,9},{9,8},{10,11... | collective-permute-start | bytes 786440 | tf_op jit(solution)/shard_map/ppermute | solution.py:133
  63.4 40.7 %copy-start.1 = (bf16[2,256,256]{2,1,0:T(8,128)(2,1)S(1)}, bf16[2,256,256]{2,1,0:T(8,128)(2,1)}, u32[]{:S(2)}) copy-start(bf16[2,256,256]{2,1,0:T(8,128)(2,1)} %constant.234.clone.refs_5_) | copy-start | bytes 786436
  63.4 40.7 %copy-start.2 = (bf16[2,128,256]{2,1,0:T(8,128)(2,1)S(1)}, bf16[2,128,256]{2,1,0:T(8,128)(2,1)}, u32[]{:S(2)}) copy-start(bf16[2,128,256]{2,1,0:T(8,128)(2,1)} %constant.233.clone.refs_4_) | copy-start | bytes 393220
  106.7 19.3 %all-to-all-start.2 = ((bf16[32,32,256]{2,1,0:T(8,128)(2,1)}), bf16[32,32,256]{2,1,0:T(8,128)(2,1)S(1)}, u32[]{:S(2)}, u32[]{:S(2)}) async-start(bf16[32,32,256]{2,1,0:T(8,128)(2,1)} %bitcast.22), calls=%async_computation.2 | async-start | bytes 1048576 | tf_op jit(solution)/shard_map/all_to_all | solution.py:478
  129.6 12.1 %collective-permute-start.8 = (bf16[64,2048]{1,0:T(8,128)(2,1)S(1)}, bf16[64,2048]{1,0:T(8,128)(2,1)S(1)}, u32[]{:S(2)}, u32[]{:S(2)}) collective-permute-start(bf16[64,2048]{1,0:T(8,128)(2,1)S(1)} %get-tuple-element.43), channel_id=1, source_target_pairs={{0,0},{1,16},{2,2},{3,18},{4,4},{5,20},{6,6},{7,22},{8,24},{9,8},{... | collective-permute-start | bytes 786440 | tf_op jit(solution)/shard_map/ppermute | solution.py:88
  132.2 25.9 %collective-permute-start.9 = (bf16[64,2048]{1,0:T(8,128)(2,1)S(1)}, bf16[64,2048]{1,0:T(8,128)(2,1)S(1)}, u32[]{:S(2)}, u32[]{:S(2)}) collective-permute-start(bf16[64,2048]{1,0:T(8,128)(2,1)S(1)} %get-tuple-element.44), channel_id=1, source_target_pairs={{0,8},{1,24},{2,10},{3,26},{4,12},{5,28},{6,14},{7,30},{8,16},{9,0... | collective-permute-start | bytes 786440 | tf_op jit(solution)/shard_map/ppermute | solution.py:88
  132.3 25.8 %collective-permute-start.10 = (bf16[64,2048]{1,0:T(8,128)(2,1)S(1)}, bf16[64,2048]{1,0:T(8,128)(2,1)S(1)}, u32[]{:S(2)}, u32[]{:S(2)}) collective-permute-start(bf16[64,2048]{1,0:T(8,128)(2,1)S(1)} %get-tuple-element.45), channel_id=1, source_target_pairs={{0,16},{1,0},{2,18},{3,2},{4,20},{5,4},{6,22},{7,6},{8,8},{9,24},{... | collective-permute-start | bytes 786440 | tf_op jit(solution)/shard_map/ppermute | solution.py:88
  136.2 22.0 %collective-permute-start.11 = (bf16[64,2048]{1,0:T(8,128)(2,1)S(1)}, bf16[64,2048]{1,0:T(8,128)(2,1)S(1)}, u32[]{:S(2)}, u32[]{:S(2)}) collective-permute-start(bf16[64,2048]{1,0:T(8,128)(2,1)S(1)} %get-tuple-element.46), channel_id=1, source_target_pairs={{0,24},{1,8},{2,26},{3,10},{4,28},{5,12},{6,30},{7,14},{8,0},{9,16... | collective-permute-start | bytes 786440 | tf_op jit(solution)/shard_map/ppermute | solution.py:88
Sparse Core Ops, SparseCore 0:
  8.9 48.8 all-gather.3
  59.7 51.2 all-gather.5

commit v27 on v26

--- a/solution.py
+++ b/solution.py
@@ -453,7 +453,7 @@
     skip = lax.dynamic_slice_in_dim(skip_gain, position * chans, chans, axis=0)
     skip = jnp.broadcast_to(skip[:, None], (chans, rows))
     filter_blocks = lax.all_to_all(
-        long_filter.T.reshape(seq_parts, chans, rows), "seq", split_axis=0, concat_axis=0, tiled=True
+        long_filter.T.astype(jnp.bfloat16).reshape(seq_parts, chans, rows), "seq", split_axis=0, concat_axis=0, tiled=True
     )
 
     held = share_columns(features, outer, tp_parts)

time: 167 us -> 171 us (1.024)
  waiting for transfers between devices: 64.6 us -> 69.8 us
  starting transfers between devices: 31.1 us -> 28.3 us
  blocking collectives: 40.7 us -> 43.1 us
    ppermute x1, waiting for transfers between devices: 5.62 us -> 13.2 us  [share_columns(): lax.ppermute(piece, 'tp', [(i, (i + step) % tp_parts) for i in range(tp_p...]
    all_gather x1, waiting for transfers between devices: 4.3 us -> 0.02 us  [per_device(): lax.all_gather(in_proj, 'seq', axis=1, tiled=True, axis_index_groups=inne...]
    all_to_all x1, waiting for transfers between devices: 0.01 us -> 4.02 us  [per_device(): lax.all_to_all(long_filter.T.astype(jnp.bfloat16).reshape(seq_parts, chan...]
    ppermute x3, starting transfers between devices: 6.38 us -> 3.74 us  [cross_outer(): lax.ppermute(piece, 'seq', [(i, (i + far) % seq_parts) for i in range(seq...]
    all_to_all x1, blocking collectives: 40.7 us -> 43.1 us  [per_device(): lax.all_to_all(partial, 'seq', split_axis=0, concat_axis=0, tiled=True)]
  transfers between devices with their start and end apart: 16 -> 16, of which waited for: 10 -> 9; matrix products, arithmetic and copies ran while one was open for 1% -> 1% of each run, Pallas kernels for 5% -> 5%
where the time goes in v27:
time: 171 us
  waiting for transfers between devices  69.8 us (41%)
  blocking collectives  43.1 us (25%)
  starting transfers between devices  28.3 us (17%)
  between operations  13.8 us (8%)
  Pallas kernels  13.3 us (8%)
  local copies, waits for them, and re-layouts  2.5 us (1%)
    all_to_all x1, blocking collectives, per_device(): lax.all_to_all(partial, 'seq', split_axis=0, concat_axis=0, tiled=True)  43.1 us
    ppermute x4, waiting for transfers between devices, return_output(): arrived.append(lax.ppermute(piece, ('seq', 'tp'), pairs))  19.6 us
    all_to_all x1, waiting for transfers between devices, per_device(): lax.all_to_all(gated.reshape((-1,) + gated.shape[3:]), ('tp', 'seq'), spl...  14.4 us
    ppermute x1, waiting for transfers between devices, share_columns(): lax.ppermute(piece, 'tp', [(i, (i + step) % tp_parts) for i in range(tp_p...  13.2 us
    ppermute x3, waiting for transfers between devices, cross_outer(): lax.ppermute(piece, 'seq', [(i, (i + far) % seq_parts) for i in range(seq...  11.2 us
    ppermute x4, starting transfers between devices, return_output(): arrived.append(lax.ppermute(piece, ('seq', 'tp'), pairs))  8.85 us
    ppermute x4, waiting for transfers between devices, share_over_tp(): pieces.append(lax.ppermute(part, 'tp', pairs))  6.72 us
    pallas_call x1, Pallas kernels, project_in(): pl.pallas_call(functools.partial(project_kernel, tp_parts), in_specs=[pl....  5.57 us
  transfers between devices with their start and end apart: 16, of which 9 were waited for; matrix products, arithmetic and copies ran while one was open for 1% of the time, Pallas kernels for 5%

profile of v27, /device:TPU:12, one launch (start us, length us, event | category | flops | bytes accessed | tf_op | source)
XLA Modules:
  0.0 171.0 jit_solution(4830624856511043361)
XLA Ops:
  8.5 13.2 %collective-permute-done = bf16[2,128,1024]{2,1,0:T(8,128)(2,1)S(1)} collective-permute-done((bf16[2,128,1024]{2,1,0:T(8,128)(2,1)S(1)}, bf16[2,128,1024]{2,1,0:T(8,128)(2,1)S(1)}, u32[]{:S(2)}, u32[]{:S(2)}) %collective-permute-start) | collective-permute-done | bytes 524320 | tf_op jit(solution)/shard_map/ppermute | solution.py:107
  21.8 1.6 collective-permute-start.1
  24.7 5.3 %all-to-all-start = ((bf16[16,32,128]{2,1,0:T(8,128)(2,1)}), bf16[16,32,128]{2,1,0:T(8,128)(2,1)S(1)}, u32[]{:S(2)}, u32[]{:S(2)}) async-start(bf16[16,32,128]{2,1,0:T(8,128)(2,1)} %bitcast.18), calls=%async_computation | async-start | bytes 262144 | tf_op jit(solution)/shard_map/all_to_all | solution.py:455
  30.1 0.8 dynamic_slice.36
  31.3 4.0 %all-to-all-done.refs_1_ = bf16[16,32,128]{2,1,0:T(8,128)(2,1)S(1)} async-done(((bf16[16,32,128]{2,1,0:T(8,128)(2,1)}), bf16[16,32,128]{2,1,0:T(8,128)(2,1)S(1)}, u32[]{:S(2)}, u32[]{:S(2)}) %all-to-all-start) | async-done | bytes 131104 | tf_op jit(solution)/shard_map/all_to_all | solution.py:455
  35.4 2.0 %collective-permute-start.4 = (bf16[128,1024]{1,0:T(8,128)(2,1)S(1)}, bf16[128,1024]{1,0:T(8,128)(2,1)S(1)}, u32[]{:S(2)}, u32[]{:S(2)}) collective-permute-start(bf16[128,1024]{1,0:T(8,128)(2,1)S(1)} %dynamic-slice_bitcast_fusion.1), channel_id=1, source_target_pairs={{0,16},{2,18},{4,20},{6,22},{8,24},{10,26},{12,28},{14,30},{16,0},... | collective-permute-start | bytes 786440 | tf_op jit(solution)/shard_map/ppermute | solution.py:124
  37.4 1.5 collective-permute-start.3
  38.9 8.2 %collective-permute-done.6.refs_6_ = bf16[128,1024]{1,0:T(8,128)(2,1)S(1)} collective-permute-done((bf16[128,1024]{1,0:T(8,128)(2,1)S(1)}, bf16[128,1024]{1,0:T(8,128)(2,1)S(1)}, u32[]{:S(2)}, u32[]{:S(2)}) %collective-permute-start.6) | collective-permute-done | bytes 262176 | tf_op jit(solution)/shard_map/ppermute | solution.py:124
  47.1 1.5 collective-permute-start.7
  48.6 3.0 %collective-permute-done.4.refs_4_ = bf16[128,1024]{1,0:T(8,128)(2,1)S(1)} collective-permute-done((bf16[128,1024]{1,0:T(8,128)(2,1)S(1)}, bf16[128,1024]{1,0:T(8,128)(2,1)S(1)}, u32[]{:S(2)}, u32[]{:S(2)}) %collective-permute-start.4) | collective-permute-done | bytes 262176 | tf_op jit(solution)/shard_map/ppermute | solution.py:124
  51.6 1.5 collective-permute-start.5
  53.5 6.4 %collective-permute-done.5.refs_5_ = bf16[128,1024]{1,0:T(8,128)(2,1)S(1)} collective-permute-done((bf16[128,1024]{1,0:T(8,128)(2,1)S(1)}, bf16[128,1024]{1,0:T(8,128)(2,1)S(1)}, u32[]{:S(2)}, u32[]{:S(2)}) %collective-permute-start.5) | collective-permute-done | bytes 262176 | tf_op jit(solution)/shard_map/ppermute | solution.py:133
  59.9 5.6 %shard_map.82 = bf16[16,3,32,512]{3,2,1,0:T(8,128)(2,1)S(1)} custom-call(s32[1]{0:T(128)} %bitcast.10.place_ref, bf16[128,1024]{1,0:T(8,128)(2,1)S(1)} %get-tuple-element.31.refs_0_, bf16[128,1024]{1,0:T(8,128)(2,1)S(1)} %collective-permute-done.2.refs_1_, bf16[128,1024]{1,0:T(8,128)(2,1)S(1)} %collective-permute-done.1.refs_2_, ...), custom_call_target="tpu_custom_call" | custom-call | flops 96636764160 | bytes 9961472 | tf_op jit(solution)/shard_map/pallas_call | solution.py:177
  65.5 43.1 %all_to_all.15.refs_0_ = bf16[16,3,32,512]{3,2,1,0:T(8,128)(2,1)S(1)} all-to-all(bf16[16,3,32,512]{3,2,1,0:T(8,128)(2,1)S(1)} %shard_map.82), channel_id=1, replica_groups=mesh['seq'=16,'tp'=2] {'seq'}, dimensions={0} | all-to-all | bytes 3145728 | tf_op jit(solution)/shard_map/all_to_all | solution.py:475
  108.6 2.6 %shard_map.83 = bf16[2,4,4,32,256]{4,3,2,1,0:T(8,128)(2,1)} custom-call(bf16[16,3,32,512]{3,2,1,0:T(8,128)(2,1)S(1)} %all_to_all.15.refs_0_, bf16[16,32,128]{2,1,0:T(8,128)(2,1)S(1)} %all-to-all-done.refs_1_, f32[3,3,32,128]{3,2,1,0:T(8,128)S(1)} %broadcast_in_dim.7.refs_2_, f32[32,128]{1,0:T(8,128)S(1)} %broadcast_in_dim.8.refs_3_, ...), custom_call_target="tpu_custom_call" | custom-call | flops 1000000000 | bytes 4194304 | tf_op jit(solution)/shard_map/pallas_call | solution.py:353
  111.2 4.8 %all-to-all-start.2 = ((bf16[32,32,256]{2,1,0:T(8,128)(2,1)}), bf16[32,32,256]{2,1,0:T(8,128)(2,1)S(1)}, u32[]{:S(2)}, u32[]{:S(2)}) async-start(bf16[32,32,256]{2,1,0:T(8,128)(2,1)} %bitcast.22), calls=%async_computation.2 | async-start | bytes 1048576 | tf_op jit(solution)/shard_map/all_to_all | solution.py:478
  116.1 14.4 %all-to-all-done.2 = bf16[32,32,256]{2,1,0:T(8,128)(2,1)S(1)} async-done(((bf16[32,32,256]{2,1,0:T(8,128)(2,1)}), bf16[32,32,256]{2,1,0:T(8,128)(2,1)S(1)}, u32[]{:S(2)}, u32[]{:S(2)}) %all-to-all-start.2) | async-done | bytes 524320 | tf_op jit(solution)/shard_map/all_to_all | solution.py:478
  130.5 3.6 %shard_map.84 = (bf16[64,2048]{1,0:T(8,128)(2,1)S(1)}, bf16[64,2048]{1,0:T(8,128)(2,1)S(1)}, bf16[64,2048]{1,0:T(8,128)(2,1)S(1)}, bf16[64,2048]{1,0:T(8,128)(2,1)S(1)}) custom-call(s32[4]{0:T(128)S(1)} %pad_add_fusion.block_ref, bf16[2,512,256]{2,1,0:T(8,128)(2,1)S(1)} %bitcast.34, bf16[4,2,512,512]{3,2,1,0:T(8,128)(2,1)} %bitcast.35), custom_call_target="tpu_custom_call" | custom-call | flops 1073741824 | bytes 5767168 | tf_op jit(solution)/shard_map/pallas_call | solution.py:411
  134.1 2.6 %collective-permute-start.8 = (bf16[64,2048]{1,0:T(8,128)(2,1)S(1)}, bf16[64,2048]{1,0:T(8,128)(2,1)S(1)}, u32[]{:S(2)}, u32[]{:S(2)}) collective-permute-start(bf16[64,2048]{1,0:T(8,128)(2,1)S(1)} %get-tuple-element.43), channel_id=1, source_target_pairs={{0,0},{1,16},{2,2},{3,18},{4,4},{5,20},{6,6},{7,22},{8,24},{9,8},{... | collective-permute-start | bytes 786440 | tf_op jit(solution)/shard_map/ppermute | solution.py:88
  136.8 3.9 %collective-permute-start.10 = (bf16[64,2048]{1,0:T(8,128)(2,1)S(1)}, bf16[64,2048]{1,0:T(8,128)(2,1)S(1)}, u32[]{:S(2)}, u32[]{:S(2)}) collective-permute-start(bf16[64,2048]{1,0:T(8,128)(2,1)S(1)} %get-tuple-element.45), channel_id=1, source_target_pairs={{0,16},{1,0},{2,18},{3,2},{4,20},{5,4},{6,22},{7,6},{8,8},{9,24},{... | collective-permute-start | bytes 786440 | tf_op jit(solution)/shard_map/ppermute | solution.py:88
  140.7 2.3 %collective-permute-start.11 = (bf16[64,2048]{1,0:T(8,128)(2,1)S(1)}, bf16[64,2048]{1,0:T(8,128)(2,1)S(1)}, u32[]{:S(2)}, u32[]{:S(2)}) collective-permute-start(bf16[64,2048]{1,0:T(8,128)(2,1)S(1)} %get-tuple-element.46), channel_id=1, source_target_pairs={{0,24},{1,8},{2,26},{3,10},{4,28},{5,12},{6,30},{7,14},{8,0},{9,16... | collective-permute-start | bytes 786440 | tf_op jit(solution)/shard_map/ppermute | solution.py:88
  143.1 3.2 %collective-permute-done.8.refs_0_ = bf16[64,2048]{1,0:T(8,128)(2,1)S(1)} collective-permute-done((bf16[64,2048]{1,0:T(8,128)(2,1)S(1)}, bf16[64,2048]{1,0:T(8,128)(2,1)S(1)}, u32[]{:S(2)}, u32[]{:S(2)}) %collective-permute-start.8) | collective-permute-done | bytes 262176 | tf_op jit(solution)/shard_map/ppermute | solution.py:88
  146.3 16.4 %collective-permute-done.9.refs_1_ = bf16[64,2048]{1,0:T(8,128)(2,1)S(1)} collective-permute-done((bf16[64,2048]{1,0:T(8,128)(2,1)S(1)}, bf16[64,2048]{1,0:T(8,128)(2,1)S(1)}, u32[]{:S(2)}, u32[]{:S(2)}) %collective-permute-start.9) | collective-permute-done | bytes 262176 | tf_op jit(solution)/shard_map/ppermute | solution.py:88
  162.6 1.5 shard_map.85
  (39 shorter events, 4.4 us)
Async XLA Ops:
  6.5 24.4 %copy-start = (f32[3,3,512]{2,1,0:T(4,128)S(1)}, f32[3,3,512]{2,1,0:T(4,128)}, u32[]{:S(2)}) copy-start(f32[3,3,512]{2,1,0:T(4,128)} %param.10) | copy-start | bytes 55300
  6.5 1.2 copy-start.3
  6.5 53.4 %all-gather.4.cloned.1.call-start = ((), (), s32[]{:S(2)}) async-start(), calls=%async_computation.3 | async-start | bytes 7864320 | tf_op jit(solution)/shard_map/all_gather | solution.py:449
  7.9 13.7 %collective-permute-start = (bf16[2,128,1024]{2,1,0:T(8,128)(2,1)S(1)}, bf16[2,128,1024]{2,1,0:T(8,128)(2,1)S(1)}, u32[]{:S(2)}, u32[]{:S(2)}) collective-permute-start(bf16[2,128,1024]{2,1,0:T(8,128)(2,1)S(1)} %pad_maximum_fusion.1), channel_id=1, source_target_pairs={{0,1},{1,0},{2,3},{3,2},{4,5},{5,4},{6,7},{7,6},{8,9},{9,8},{10,11... | collective-permute-start | bytes 1572872 | tf_op jit(solution)/shard_map/ppermute | solution.py:107
  21.6 2.3 %copy-start.4 = (f32[128,512]{1,0:T(8,128)S(1)}, f32[128,512]{1,0:T(8,128)}, u32[]{:S(2)}) copy-start(f32[128,512]{1,0:T(8,128)} %param.11) | copy-start | bytes 786436
  21.8 13.6 %collective-permute-start.1 = (bf16[128,1024]{1,0:T(8,128)(2,1)S(1)}, bf16[128,1024]{1,0:T(8,128)(2,1)S(1)}, u32[]{:S(2)}, u32[]{:S(2)}) collective-permute-start(bf16[128,1024]{1,0:T(8,128)(2,1)S(1)} %get-tuple-element.48), channel_id=1, source_target_pairs={{0,8},{2,10},{4,12},{6,14},{8,16},{10,18},{12,20},{14,22},{16,24},... | collective-permute-start | bytes 786440 | tf_op jit(solution)/shard_map/ppermute | solution.py:124
  23.4 12.0 %collective-permute-start.2 = (bf16[128,1024]{1,0:T(8,128)(2,1)S(1)}, bf16[128,1024]{1,0:T(8,128)(2,1)S(1)}, u32[]{:S(2)}, u32[]{:S(2)}) collective-permute-start(bf16[128,1024]{1,0:T(8,128)(2,1)S(1)} %get-tuple-element.31.refs_0_), channel_id=1, source_target_pairs={{0,1},{1,0},{2,3},{3,2},{4,5},{5,4},{6,7},{7,6},{8,9},{9,8},{10,11... | collective-permute-start | bytes 786440 | tf_op jit(solution)/shard_map/ppermute | solution.py:133
  24.7 10.7 %all-to-all-start = ((bf16[16,32,128]{2,1,0:T(8,128)(2,1)}), bf16[16,32,128]{2,1,0:T(8,128)(2,1)S(1)}, u32[]{:S(2)}, u32[]{:S(2)}) async-start(bf16[16,32,128]{2,1,0:T(8,128)(2,1)} %bitcast.18), calls=%async_computation | async-start | bytes 262144 | tf_op jit(solution)/shard_map/all_to_all | solution.py:455
  30.0 86.2 %all-gather.6.cloned.1.call-start = ((), (), s32[]{:S(2)}) async-start(), calls=%async_computation.4 | async-start | bytes 4718592 | tf_op jit(solution)/shard_map/all_gather | solution.py:471
  31.2 15.9 %collective-permute-start.6 = (bf16[128,1024]{1,0:T(8,128)(2,1)S(1)}, bf16[128,1024]{1,0:T(8,128)(2,1)S(1)}, u32[]{:S(2)}, u32[]{:S(2)}) collective-permute-start(bf16[128,1024]{1,0:T(8,128)(2,1)S(1)} %dynamic-slice_bitcast_fusion), channel_id=1, source_target_pairs={{0,24},{2,26},{4,28},{6,30},{8,0},{10,2},{12,4},{14,6},{16,8},{18,... | collective-permute-start | bytes 786440 | tf_op jit(solution)/shard_map/ppermute | solution.py:124
  35.4 16.2 %collective-permute-start.4 = (bf16[128,1024]{1,0:T(8,128)(2,1)S(1)}, bf16[128,1024]{1,0:T(8,128)(2,1)S(1)}, u32[]{:S(2)}, u32[]{:S(2)}) collective-permute-start(bf16[128,1024]{1,0:T(8,128)(2,1)S(1)} %dynamic-slice_bitcast_fusion.1), channel_id=1, source_target_pairs={{0,16},{2,18},{4,20},{6,22},{8,24},{10,26},{12,28},{14,30},{16,0},... | collective-permute-start | bytes 786440 | tf_op jit(solution)/shard_map/ppermute | solution.py:124
  37.4 16.1 %collective-permute-start.3 = (bf16[128,1024]{1,0:T(8,128)(2,1)S(1)}, bf16[128,1024]{1,0:T(8,128)(2,1)S(1)}, u32[]{:S(2)}, u32[]{:S(2)}) collective-permute-start(bf16[128,1024]{1,0:T(8,128)(2,1)S(1)} %collective-permute-done.1.refs_2_), channel_id=1, source_target_pairs={{0,1},{1,0},{2,3},{3,2},{4,5},{5,4},{6,7},{7,6},{8,9},{9,8},{10,11... | collective-permute-start | bytes 786440 | tf_op jit(solution)/shard_map/ppermute | solution.py:133
  47.1 6.4 %collective-permute-start.7 = (bf16[128,1024]{1,0:T(8,128)(2,1)S(1)}, bf16[128,1024]{1,0:T(8,128)(2,1)S(1)}, u32[]{:S(2)}, u32[]{:S(2)}) collective-permute-start(bf16[128,1024]{1,0:T(8,128)(2,1)S(1)} %collective-permute-done.6.refs_6_), channel_id=1, source_target_pairs={{0,1},{1,0},{2,3},{3,2},{4,5},{5,4},{6,7},{7,6},{8,9},{9,8},{10,11... | collective-permute-start | bytes 786440 | tf_op jit(solution)/shard_map/ppermute | solution.py:133
  51.6 8.2 %collective-permute-start.5 = (bf16[128,1024]{1,0:T(8,128)(2,1)S(1)}, bf16[128,1024]{1,0:T(8,128)(2,1)S(1)}, u32[]{:S(2)}, u32[]{:S(2)}) collective-permute-start(bf16[128,1024]{1,0:T(8,128)(2,1)S(1)} %collective-permute-done.4.refs_4_), channel_id=1, source_target_pairs={{0,1},{1,0},{2,3},{3,2},{4,5},{5,4},{6,7},{7,6},{8,9},{9,8},{10,11... | collective-permute-start | bytes 786440 | tf_op jit(solution)/shard_map/ppermute | solution.py:133
  65.5 43.1 %copy-start.1 = (bf16[2,256,256]{2,1,0:T(8,128)(2,1)S(1)}, bf16[2,256,256]{2,1,0:T(8,128)(2,1)}, u32[]{:S(2)}) copy-start(bf16[2,256,256]{2,1,0:T(8,128)(2,1)} %constant.234.clone.refs_5_) | copy-start | bytes 786436
  65.5 43.1 %copy-start.2 = (bf16[2,128,256]{2,1,0:T(8,128)(2,1)S(1)}, bf16[2,128,256]{2,1,0:T(8,128)(2,1)}, u32[]{:S(2)}) copy-start(bf16[2,128,256]{2,1,0:T(8,128)(2,1)} %constant.233.clone.refs_4_) | copy-start | bytes 393220
  111.2 19.3 %all-to-all-start.2 = ((bf16[32,32,256]{2,1,0:T(8,128)(2,1)}), bf16[32,32,256]{2,1,0:T(8,128)(2,1)S(1)}, u32[]{:S(2)}, u32[]{:S(2)}) async-start(bf16[32,32,256]{2,1,0:T(8,128)(2,1)} %bitcast.22), calls=%async_computation.2 | async-start | bytes 1048576 | tf_op jit(solution)/shard_map/all_to_all | solution.py:478
  134.1 12.1 %collective-permute-start.8 = (bf16[64,2048]{1,0:T(8,128)(2,1)S(1)}, bf16[64,2048]{1,0:T(8,128)(2,1)S(1)}, u32[]{:S(2)}, u32[]{:S(2)}) collective-permute-start(bf16[64,2048]{1,0:T(8,128)(2,1)S(1)} %get-tuple-element.43), channel_id=1, source_target_pairs={{0,0},{1,16},{2,2},{3,18},{4,4},{5,20},{6,6},{7,22},{8,24},{9,8},{... | collective-permute-start | bytes 786440 | tf_op jit(solution)/shard_map/ppermute | solution.py:88
  136.7 25.9 %collective-permute-start.9 = (bf16[64,2048]{1,0:T(8,128)(2,1)S(1)}, bf16[64,2048]{1,0:T(8,128)(2,1)S(1)}, u32[]{:S(2)}, u32[]{:S(2)}) collective-permute-start(bf16[64,2048]{1,0:T(8,128)(2,1)S(1)} %get-tuple-element.44), channel_id=1, source_target_pairs={{0,8},{1,24},{2,10},{3,26},{4,12},{5,28},{6,14},{7,30},{8,16},{9,0... | collective-permute-start | bytes 786440 | tf_op jit(solution)/shard_map/ppermute | solution.py:88
  136.8 25.8 %collective-permute-start.10 = (bf16[64,2048]{1,0:T(8,128)(2,1)S(1)}, bf16[64,2048]{1,0:T(8,128)(2,1)S(1)}, u32[]{:S(2)}, u32[]{:S(2)}) collective-permute-start(bf16[64,2048]{1,0:T(8,128)(2,1)S(1)} %get-tuple-element.45), channel_id=1, source_target_pairs={{0,16},{1,0},{2,18},{3,2},{4,20},{5,4},{6,22},{7,6},{8,8},{9,24},{... | collective-permute-start | bytes 786440 | tf_op jit(solution)/shard_map/ppermute | solution.py:88
  140.7 22.0 %collective-permute-start.11 = (bf16[64,2048]{1,0:T(8,128)(2,1)S(1)}, bf16[64,2048]{1,0:T(8,128)(2,1)S(1)}, u32[]{:S(2)}, u32[]{:S(2)}) collective-permute-start(bf16[64,2048]{1,0:T(8,128)(2,1)S(1)} %get-tuple-element.46), channel_id=1, source_target_pairs={{0,24},{1,8},{2,26},{3,10},{4,28},{5,12},{6,30},{7,14},{8,0},{9,16... | collective-permute-start | bytes 786440 | tf_op jit(solution)/shard_map/ppermute | solution.py:88
Sparse Core Ops, SparseCore 0:
  8.9 48.8 all-gather.3
  60.0 52.1 all-gather.5
